TPU v7x, 32 devices: a whole 2x2x4 slice. The times are simulated.
32 devices in a mesh: subj: 2 (over x), row: 8 (over z, y), col: 2 (over core).
Axes of the slice: x: 2, y: 2, z: 4, core: 2. Of those that a mesh axis runs over, the one named last changes fastest.
Arguments:
- bold: bfloat16 [4, 256, 16, 16, 128], P('subj', None, 'row', 'col'), parts along dimension 0, may hold values from -6 to 6
- gm_index: int32 [16384], P(('row', 'col')), may hold values from -1 to 2047, as said below
- partners: int32 [128, 16], P(('row', 'col')), may hold values from -1 to 127, as said below
Outputs:
- connectome: bfloat16 [128, 16, 4, 128, 128], P(('row', 'col'), None, 'subj'), parts along dimension 2
There are 2 independent parts, one for each index of `subj`. A program takes and returns all parts, laid end to end along the dimension named above; an argument that names none is the same for every part. Nothing has to cross between parts.
Inputs may be any that keep to these rules, and one draw needn't show every extreme that they name: `gm_index`: entries of one slab's 1024 rows are distinct voxel numbers, the last few of them -1; every slab has some -1 rows. `partners`: block g lies in slab g // 8, slabs numbered row-major over slab rows and columns. Slot 0 of block i names i, slot 1 names (i + 1) mod 128, slot 2 names (i - 1) mod 128; every named block lies in a slab whose slab row is within 2 of block i's slab row, counted cyclically. -1 marks an empty slot.
All inputs are finite; a program needn't handle non-finite values.
Results may differ from a plain program's by a relative error of at most 0.0053.
Values may be sent and summed in bfloat16 or wider, within the bound.
No kernel may reach another device: no remote copies, remote signals or barrier semaphores. Data moves between devices by JAX's collectives and lax.ppermute only.
A program may use at most 128 MiB of HBM per device.

v0:
```python
import math

import jax
import jax.numpy as jnp
from jax import lax
from jax.sharding import PartitionSpec as P

HOP = 2


side_weight = math.exp(-0.5) / (1.0 + 2.0 * math.exp(-0.5))
centre_weight = 1.0 / (1.0 + 2.0 * math.exp(-0.5))


def from_behind(value, axis, steps):
    count = lax.axis_size(axis)
    pairs = [(source, (source + steps) % count) for source in range(count)]
    return lax.ppermute(value, axis, pairs)


def padded_2(block, sides, width):
    for axis, dim in sides:
        count = lax.axis_size(axis)
        forward = [(i, i + 1) for i in range(count - 1)]
        backward = [(target, source) for source, target in forward]
        low = lax.ppermute(
            lax.slice_in_dim(block, block.shape[dim] - width, None, axis=dim), axis, forward
        )
        high = lax.ppermute(lax.slice_in_dim(block, 0, width, axis=dim), axis, backward)
        block = jnp.concatenate([low, block, high], axis=dim)
    return block


def gaussian_blur(padded):
    first = (
        side_weight * padded[:, :, :-2]
        + centre_weight * padded[:, :, 1:-1]
        + side_weight * padded[:, :, 2:]
    )
    second = (
        side_weight * first[:, :, :, :-2]
        + centre_weight * first[:, :, :, 1:-1]
        + side_weight * first[:, :, :, 2:]
    )
    return (
        side_weight * second[..., :-2]
        + centre_weight * second[..., 1:-1]
        + side_weight * second[..., 2:]
    )


def standardize(smooth):
    windows, frames = (smooth.shape[0], smooth.shape[1])
    series = smooth.reshape(windows, frames, -1)
    centred = series - jnp.mean(series, axis=1, keepdims=True)
    spread = jnp.mean(centred * centred, axis=1, keepdims=True)
    scored = centred * lax.rsqrt((spread + 1e-05) * frames)
    return jnp.transpose(scored, (2, 0, 1)).astype(jnp.bfloat16)


def nearby_rows(source):
    lower_rows = []
    current = source
    for hop_step in range(HOP):
        current = from_behind(current, "row", 1)
        lower_rows.append(current)
    upper_rows = []
    current = source
    for hop_step in range(HOP):
        current = from_behind(current, "row", -1)
        upper_rows.append(current)
    ordered = lower_rows[::-1] + [source] + upper_rows
    return jnp.stack(ordered, 0)


def on_device(bold, gm_index, partners):
    padded = padded_2(bold, (("row", 2), ("col", 3)), 1)
    widened = jnp.pad(padded.astype(jnp.float32), ((0, 0), (0, 0), (0, 0), (0, 0), (1, 1)))
    scored = standardize(gaussian_blur(widened))
    picked = jnp.take(scored, jnp.maximum(gm_index, 0), axis=0)
    panel = jnp.where((gm_index >= 0)[:, None, None], picked, jnp.zeros_like(picked))
    row_count, windows, frames = panel.shape
    block_count = partners.shape[0]
    block_rows = row_count // block_count
    flat_panel = panel.reshape(row_count, windows * frames)
    col_count = lax.axis_size("col")
    own_column = nearby_rows(flat_panel)
    collected = lax.all_gather(own_column, "col", axis=1, tiled=True)
    candidates = collected.reshape(
        (2 * HOP + 1) * col_count * block_count, block_rows, windows, frames
    )
    row_here = lax.axis_index("row")
    row_total = lax.axis_size("row")
    partner_ids = jnp.maximum(partners, 0)
    source_slab = partner_ids // block_count
    distance_slot = (source_slab // col_count - row_here + HOP + row_total) % row_total
    position = (
        distance_slot * col_count + source_slab % col_count
    ) * block_count + partner_ids % block_count
    local_blocks = panel.reshape(block_count, block_rows, windows, frames)

    def block_tiles(inputs):
        local_block, where_from, present = inputs
        partner_rows = jnp.take(candidates, where_from, axis=0)
        tiles_out = jnp.einsum(
            "awf,kbwf->kwab", local_block, partner_rows, preferred_element_type=jnp.float32
        )
        tiles_out = jnp.where(present[:, None, None, None], tiles_out, jnp.zeros_like(tiles_out))
        return tiles_out.astype(jnp.bfloat16)

    return lax.map(block_tiles, (local_blocks, position, partners >= 0))


def solution(mesh):
    in_specs = (P("subj", None, "row", "col", None), P(("row", "col")), P(("row", "col"), None))
    out_specs = P(("row", "col"), None, "subj", None, None)
    return jax.shard_map(
        on_device, mesh=mesh, in_specs=in_specs, out_specs=out_specs, check_vma=False
    )
```

profile of v0, /device:TPU:0, one launch (start us, length us, event | category | flops | bytes accessed | tf_op | source)
XLA Modules:
  0.0 383.1 jit_solution(14022659666264512104)
XLA Ops:
  8.6 4.9 %collective-permute-start = (bf16[2,256,1,8,128]{4,1,3,2,0:T(8,128)(2,1)S(1)}, bf16[2,256,1,8,128]{4,1,3,2,0:T(8,128)(2,1)S(1)}, u32[]{:S(2)}, u32[]{:S(2)}) collective-permute-start(bf16[2,256,1,8,128]{4,1,3,2,0:T(8,128)(2,1)S(1)} %copy.38), channel_id=1, source_target_pairs={{0,2},{2,4},{4,6},{6,8},{8,10},{10,12},{12,14},{1,3},{3,5},{5,7},{... | collective-permute-start | bytes 3145736 | tf_op jit(solution)/shard_map/ppermute | solution.py:26
  15.0 43.3 %collective-permute-done = bf16[2,256,1,8,128]{4,1,3,2,0:T(8,128)(2,1)S(1)} collective-permute-done((bf16[2,256,1,8,128]{4,1,3,2,0:T(8,128)(2,1)S(1)}, bf16[2,256,1,8,128]{4,1,3,2,0:T(8,128)(2,1)S(1)}, u32[]{:S(2)}, u32[]{:S(2)}) %collective-permute-start) | collective-permute-done | bytes 1048608 | tf_op jit(solution)/shard_map/ppermute | solution.py:26
  64.5 6.6 %fusion.17 = f32[2,256,4,10,130]{4,1,3,2,0:T(8,128)S(1)} fusion(bf16[2,256,4,1,128]{4,1,3,2,0:T(8,128)(2,1)S(1)} %collective-permute-done.3, bf16[2,256,4,8,128]{4,1,3,2,0:T(8,128)(2,1)S(1)} %constant_dynamic-update-slice_fusion.1, bf16[2,256,4,1,128]{4,1,3,2,0:T(8,128)(2,1)S(1)} %collective-permute-done.2), kind=kLoop, calls=%fused_computation.26 | loop fusion | flops 31948800 | bytes 15892480 | tf_op jit(solution)/shard_map/jit(_pad)/pad | solution.py:78
  71.1 6.1 %fusion.18 = f32[2,256,2,10,130]{4,1,3,2,0:T(8,128)} fusion(f32[2,256,4,10,130]{4,1,3,2,0:T(8,128)S(1)} %fusion.17), kind=kLoop, calls=%fused_computation.28 | loop fusion | flops 6656000 | bytes 21299200 | tf_op jit(solution)/shard_map/add | solution.py:36
  77.2 9.6 %fusion.20 = f32[2,256,2,8,130]{4,1,3,2,0:T(8,128)S(1)} fusion(f32[2,256,2,10,130]{4,1,3,2,0:T(8,128)} %fusion.18), kind=kLoop, calls=%fused_computation.33 | loop fusion | flops 5324800 | bytes 17039360 | tf_op jit(solution)/shard_map/add | solution.py:41
  86.8 3.7 fusion.35
  90.5 7.3 %copy.19 = f32[2,256,2,8,128]{1,0,4,3,2:T(2,128)} copy(f32[2,256,2,8,128]{4,1,3,2,0:T(8,128)} %get-tuple-element.63) | data formatting | bytes 8388608 | tf_op jit(solution)/shard_map/add | solution.py:46
  97.8 2.8 multiply_reduce_fusion
  102.3 10.4 %fusion.25 = bf16[2,256,2048]{1,0,2:T(2,128)(2,1)S(1)} fusion(f32[2,256,2,8,128]{1,0,4,3,2:T(2,128)} %copy.19, f32[2,2048]{0,1:T(8,128)} %bitcast.59, f32[2,2048]{0,1:T(8,128)S(1)} %bitcast.58), kind=kLoop, calls=%fused_computation.44 | loop fusion | flops 3145728 | bytes 6324224 | tf_op jit(solution)/shard_map/convert_element_type | solution.py:58
  112.7 4.2 %gather_fusion.1 = bf16[1024,2,256]{2,1,0:T(2,128)(2,1)S(1)} fusion(bf16[2048,2,256]{2,1,0:T(2,128)(2,1)S(1)} %bitcast.55, s32[1024]{0:T(1024)S(1)} %maximum_clamp_fusion), kind=kCustom, calls=%fused_computation.1 | custom fusion | bytes 2101248 | tf_op jit(solution)/shard_map/jit(_take)/gather | solution.py:80
  122.7 42.9 %collective-permute-done.4 = bf16[1024,512]{1,0:T(8,128)(2,1)} collective-permute-done((bf16[1024,512]{1,0:T(8,128)(2,1)S(1)}, bf16[1024,512]{1,0:T(8,128)(2,1)}, u32[]{:S(2)}, u32[]{:S(2)}) %collective-permute-start.4) | collective-permute-done | bytes 1048608 | tf_op jit(solution)/shard_map/ppermute | solution.py:18
  168.9 2.8 collective-permute-start.7
  171.7 41.2 %collective-permute-done.5 = bf16[1024,512]{1,0:T(8,128)(2,1)} collective-permute-done((bf16[1024,512]{1,0:T(8,128)(2,1)}, bf16[1024,512]{1,0:T(8,128)(2,1)}, u32[]{:S(2)}, u32[]{:S(2)}) %collective-permute-start.5) | collective-permute-done | bytes 1048608 | tf_op jit(solution)/shard_map/ppermute | solution.py:18
  223.1 24.4 %all-gather.2.cloned.1.call-done = bf16[5,2048,512]{2,1,0:T(8,128)(2,1)} async-done(((bf16[5,1024,512]{2,1,0:T(8,128)(2,1)}), bf16[5,2048,512]{2,1,0:T(8,128)(2,1)}) %all-gather.2.cloned.1.call-update) | async-done | bytes 10485776 | tf_op jit(solution)/shard_map/all_gather | solution.py:88
  247.5 15.3 %reshape.127 = bf16[80,128,2,256]{3,2,1,0:T(2,128)(2,1)} reshape(bf16[5,2048,512]{2,1,0:T(8,128)(2,1)} %all-gather.2.cloned.1.call-done) | data formatting | bytes 20971520 | tf_op jit(solution)/shard_map/reshape | solution.py:89
  262.9 113.4 %while.10 = (s32[]{:T(128)}, bf16[8,16,2,128,128]{4,3,2,1,0:T(8,128)(2,1)}, pred[8,16]{1,0:T(8,128)(4,1)S(1)}, s32[8,16]{1,0:T(8,128)S(1)}, bf16[80,128,2,256]{3...) while((s32[]{:T(128)}, bf16[8,16,2,128,128]{4,3,2,1,0:T(8,128)(2,1)}, ...), condition=%wide.region_3.4_spmd, body=%wide.region_2.3_spmd.sunk | while | flops 270533792 | bytes 15865309 | solution.py:111
  262.9 9.8 %gather_fusion = bf16[16,128,2,256]{3,2,1,0:T(2,128)(2,1)S(1)} fusion(bf16[80,128,2,256]{3,2,1,0:T(2,128)(2,1)} %get-tuple-element.125, s32[1024]{0:T(1024)S(1)} %pad_clamp_fusion.2), kind=kCustom, calls=%fused_computation.clone.1 | custom fusion | bytes 4194368 | tf_op jit(solution)/shard_map/while/body/eval_jaxpr/jit(_take)/gather | solution.py:104
  277.0 9.8 %gather_fusion = bf16[16,128,2,256]{3,2,1,0:T(2,128)(2,1)S(1)} fusion(bf16[80,128,2,256]{3,2,1,0:T(2,128)(2,1)} %get-tuple-element.125, s32[1024]{0:T(1024)S(1)} %pad_clamp_fusion.2), kind=kCustom, calls=%fused_computation.clone.1 | custom fusion | bytes 4194368 | tf_op jit(solution)/shard_map/while/body/eval_jaxpr/jit(_take)/gather | solution.py:104
  291.2 9.8 %gather_fusion = bf16[16,128,2,256]{3,2,1,0:T(2,128)(2,1)S(1)} fusion(bf16[80,128,2,256]{3,2,1,0:T(2,128)(2,1)} %get-tuple-element.125, s32[1024]{0:T(1024)S(1)} %pad_clamp_fusion.2), kind=kCustom, calls=%fused_computation.clone.1 | custom fusion | bytes 4194368 | tf_op jit(solution)/shard_map/while/body/eval_jaxpr/jit(_take)/gather | solution.py:104
  305.4 9.8 %gather_fusion = bf16[16,128,2,256]{3,2,1,0:T(2,128)(2,1)S(1)} fusion(bf16[80,128,2,256]{3,2,1,0:T(2,128)(2,1)} %get-tuple-element.125, s32[1024]{0:T(1024)S(1)} %pad_clamp_fusion.2), kind=kCustom, calls=%fused_computation.clone.1 | custom fusion | bytes 4194368 | tf_op jit(solution)/shard_map/while/body/eval_jaxpr/jit(_take)/gather | solution.py:104
  319.6 9.8 %gather_fusion = bf16[16,128,2,256]{3,2,1,0:T(2,128)(2,1)S(1)} fusion(bf16[80,128,2,256]{3,2,1,0:T(2,128)(2,1)} %get-tuple-element.125, s32[1024]{0:T(1024)S(1)} %pad_clamp_fusion.2), kind=kCustom, calls=%fused_computation.clone.1 | custom fusion | bytes 4194368 | tf_op jit(solution)/shard_map/while/body/eval_jaxpr/jit(_take)/gather | solution.py:104
  333.8 9.8 %gather_fusion = bf16[16,128,2,256]{3,2,1,0:T(2,128)(2,1)S(1)} fusion(bf16[80,128,2,256]{3,2,1,0:T(2,128)(2,1)} %get-tuple-element.125, s32[1024]{0:T(1024)S(1)} %pad_clamp_fusion.2), kind=kCustom, calls=%fused_computation.clone.1 | custom fusion | bytes 4194368 | tf_op jit(solution)/shard_map/while/body/eval_jaxpr/jit(_take)/gather | solution.py:104
  347.9 9.8 %gather_fusion = bf16[16,128,2,256]{3,2,1,0:T(2,128)(2,1)S(1)} fusion(bf16[80,128,2,256]{3,2,1,0:T(2,128)(2,1)} %get-tuple-element.125, s32[1024]{0:T(1024)S(1)} %pad_clamp_fusion.2), kind=kCustom, calls=%fused_computation.clone.1 | custom fusion | bytes 4194368 | tf_op jit(solution)/shard_map/while/body/eval_jaxpr/jit(_take)/gather | solution.py:104
  362.1 9.8 %gather_fusion = bf16[16,128,2,256]{3,2,1,0:T(2,128)(2,1)S(1)} fusion(bf16[80,128,2,256]{3,2,1,0:T(2,128)(2,1)} %get-tuple-element.125, s32[1024]{0:T(1024)S(1)} %pad_clamp_fusion.2), kind=kCustom, calls=%fused_computation.clone.1 | custom fusion | bytes 4194368 | tf_op jit(solution)/shard_map/while/body/eval_jaxpr/jit(_take)/gather | solution.py:104
  (109 shorter events, 65.4 us)
Async XLA Ops:
  6.5 51.9 %copy-start = (bf16[2,256,2,8,128]{4,3,2,1,0:T(8,128)(2,1)S(1)}, bf16[2,256,2,8,128]{4,3,2,1,0:T(8,128)(2,1)}, u32[]{:S(2)}) copy-start(bf16[2,256,2,8,128]{4,3,2,1,0:T(8,128)(2,1)} %param.5) | copy-start | bytes 6291460
  6.5 241.0 %all-gather.2.cloned.1.call-start = ((), (), s32[]{:S(2)}) async-start(), calls=%async_computation | async-start | bytes 15728640 | tf_op jit(solution)/shard_map/all_gather | solution.py:88
  8.6 49.7 %collective-permute-start = (bf16[2,256,1,8,128]{4,1,3,2,0:T(8,128)(2,1)S(1)}, bf16[2,256,1,8,128]{4,1,3,2,0:T(8,128)(2,1)S(1)}, u32[]{:S(2)}, u32[]{:S(2)}) collective-permute-start(bf16[2,256,1,8,128]{4,1,3,2,0:T(8,128)(2,1)S(1)} %copy.38), channel_id=1, source_target_pairs={{0,2},{2,4},{4,6},{6,8},{8,10},{10,12},{12,14},{1,3},{3,5},{5,7},{... | collective-permute-start | bytes 3145736 | tf_op jit(solution)/shard_map/ppermute | solution.py:26
  13.7 48.3 %copy-start.2 = (s32[1024]{0:T(1024)S(1)}, s32[1024]{0:T(1024)}, u32[]{:S(2)}) copy-start(s32[1024]{0:T(1024)} %param.6) | copy-start | bytes 12292
  13.7 45.4 %collective-permute-start.1 = (bf16[2,256,1,8,128]{4,1,3,2,0:T(8,128)(2,1)S(1)}, bf16[2,256,1,8,128]{4,1,3,2,0:T(8,128)(2,1)S(1)}, u32[]{:S(2)}, u32[]{:S(2)}) collective-permute-start(bf16[2,256,1,8,128]{4,1,3,2,0:T(8,128)(2,1)S(1)} %copy.39), channel_id=1, source_target_pairs={{2,0},{4,2},{6,4},{8,6},{10,8},{12,10},{14,12},{3,1},{5,3},{7,5},{... | collective-permute-start | bytes 3145736 | tf_op jit(solution)/shard_map/ppermute | solution.py:29
  59.3 2.8 collective-permute-start.2
  60.7 3.8 collective-permute-start.3
  117.9 47.7 %collective-permute-start.4 = (bf16[1024,512]{1,0:T(8,128)(2,1)S(1)}, bf16[1024,512]{1,0:T(8,128)(2,1)}, u32[]{:S(2)}, u32[]{:S(2)}) collective-permute-start(bf16[1024,512]{1,0:T(8,128)(2,1)S(1)} %select_select_fusion.1), channel_id=1, source_target_pairs={{0,2},{2,4},{4,6},{6,8},{8,10},{10,12},{12,14},{14,0},{1,3},{3,5},... | collective-permute-start | bytes 3145736 | tf_op jit(solution)/shard_map/ppermute | solution.py:18
  120.5 48.5 %collective-permute-start.6 = (bf16[1024,512]{1,0:T(8,128)(2,1)S(1)}, bf16[1024,512]{1,0:T(8,128)(2,1)}, u32[]{:S(2)}, u32[]{:S(2)}) collective-permute-start(bf16[1024,512]{1,0:T(8,128)(2,1)S(1)} %select_select_fusion.1), channel_id=1, source_target_pairs={{0,14},{2,0},{4,2},{6,4},{8,6},{10,8},{12,10},{14,12},{1,15},{3,1}... | collective-permute-start | bytes 3145736 | tf_op jit(solution)/shard_map/ppermute | solution.py:18
  165.6 47.3 %collective-permute-start.5 = (bf16[1024,512]{1,0:T(8,128)(2,1)}, bf16[1024,512]{1,0:T(8,128)(2,1)}, u32[]{:S(2)}, u32[]{:S(2)}) collective-permute-start(bf16[1024,512]{1,0:T(8,128)(2,1)} %collective-permute-done.4), channel_id=1, source_target_pairs={{0,2},{2,4},{4,6},{6,8},{8,10},{10,12},{12,14},{14,0},{1,3},{3,5},... | collective-permute-start | bytes 3145736 | tf_op jit(solution)/shard_map/ppermute | solution.py:18
  168.9 52.5 %collective-permute-start.7 = (bf16[1024,512]{1,0:T(8,128)(2,1)}, bf16[1024,512]{1,0:T(8,128)(2,1)S(1)}, u32[]{:S(2)}, u32[]{:S(2)}) collective-permute-start(bf16[1024,512]{1,0:T(8,128)(2,1)} %collective-permute-done.6), channel_id=1, source_target_pairs={{0,14},{2,0},{4,2},{6,4},{8,6},{10,8},{12,10},{14,12},{1,15},{3,1}... | collective-permute-start | bytes 3145736 | tf_op jit(solution)/shard_map/ppermute | solution.py:18
  219.1 3.4 copy-start.1
Sparse Core Ops, SparseCore 0:
  222.6 24.9 all-gather.1
where the time goes:
time: 384 us; the launch traced here: 383 us
  waiting for transfers between devices  154 us (40%)
  local copies, waits for them, and re-layouts  133 us (35%)
  other arithmetic  57.5 us (15%)
  starting transfers between devices  19 us (5%)
  between operations  13.7 us (4%)
  matrix products  5.71 us (1%)
    ppermute x4, waiting for transfers between devices, from_behind(): return lax.ppermute(value, axis, pairs)  84.1 us
    gather x8, local copies, waits for them, and re-layouts, block_tiles(): partner_rows = jnp.take(candidates, where_from, axis=0)  78.3 us
    ppermute x2, waiting for transfers between devices, padded_2(): lax.ppermute(lax.slice_in_dim(block, block.shape[dim] - width, None, axis...  43.4 us
    all_gather x1, waiting for transfers between devices, on_device(): collected = lax.all_gather(own_column, 'col', axis=1, tiled=True)  24.4 us
    reshape x1, local copies, waits for them, and re-layouts, on_device(): collected.reshape((2 * HOP + 1) * col_count * block_count, block_rows, wi...  15.3 us
    select_n x16, other arithmetic, block_tiles(): partner_rows = jnp.take(candidates, where_from, axis=0)  15.1 us
    dynamic_update_slice x16, local copies, waits for them, and re-layouts, on_device(): return lax.map(block_tiles, (local_blocks, position, partners >= 0))  13.7 us
    convert_element_type x1, other arithmetic, standardize(): return jnp.transpose(scored, (2, 0, 1)).astype(jnp.bfloat16)  10.4 us
  transfers between devices with their start and end apart: 9, of which 6 were waited for; matrix products, arithmetic and copies ran while one was open for 3% of the time, Pallas kernels for 0%

commit v1 on v0

v1 whole, which is shorter than its diff:
```python
import functools
import math

import jax
import jax.numpy as jnp
from jax import lax
from jax.experimental import pallas as pl
from jax.experimental.pallas import tpu as pltpu
from jax.sharding import PartitionSpec as P

BLOCK = 128
SIDE = math.exp(-0.5) / (1.0 + 2.0 * math.exp(-0.5))
CENTRE = 1.0 / (1.0 + 2.0 * math.exp(-0.5))
VMEM_BYTES = 48 * 1024 * 1024


def panel_kernel(
    col_ref, bold_ref, low_ref, high_ref, edge_ref, corner_ref, gm_ref, out_ref,
    wide, wide_low, wide_high, planes, scored,
):
    frames, slab_x, slab_y, slab_z = bold_ref.shape[1:]
    per_frame = slab_x * slab_y
    wide[...] = bold_ref[0].reshape(frames * per_frame, slab_z).astype(jnp.float32)
    wide_low[...] = low_ref[...].reshape(frames * slab_y, slab_z).astype(jnp.float32)
    wide_high[...] = high_ref[...].reshape(frames * slab_y, slab_z).astype(jnp.float32)

    def along_x(before, here, after):
        return SIDE * before + CENTRE * here + SIDE * after

    for y in range(slab_y):
        layers = [wide_low[pl.ds(y, frames, stride=slab_y), :]]
        for x in range(slab_x):
            layers.append(wide[pl.ds(x * slab_y + y, frames, stride=per_frame), :])
        layers.append(wide_high[pl.ds(y, frames, stride=slab_y), :])
        for x in range(slab_x):
            planes[x, y + 1] = along_x(*layers[x : x + 3])
    edges = [corner_ref[0].astype(jnp.float32)]
    for x in range(slab_x):
        edges.append(edge_ref[x].astype(jnp.float32))
    edges.append(corner_ref[1].astype(jnp.float32))
    for x in range(slab_x):
        edge = along_x(*edges[x : x + 3])
        planes[x, 0] = jnp.where(col_ref[0] == 0, 0.0, edge)
        planes[x, slab_y + 1] = jnp.where(col_ref[0] == 0, edge, 0.0)

    lane = lax.broadcasted_iota(jnp.int32, (frames, slab_z), 1)
    for x in range(slab_x):
        for y in range(slab_y):
            part = along_x(planes[x, y], planes[x, y + 1], planes[x, y + 2])
            before = jnp.where(lane == 0, 0.0, pltpu.roll(part, 1, 1))
            after = jnp.where(lane == slab_z - 1, 0.0, pltpu.roll(part, slab_z - 1, 1))
            smooth = along_x(before, part, after)
            centred = smooth - jnp.mean(smooth, axis=0, keepdims=True)
            spread = jnp.mean(centred * centred, axis=0, keepdims=True)
            value = centred * lax.rsqrt((spread + 1e-05) * frames)
            start = (x * slab_y + y) * slab_z
            scored[:, start : start + slab_z] = value.astype(jnp.bfloat16)

    voxels = per_frame * slab_z
    rows = gm_ref.shape[1]
    step = 2 * BLOCK
    for start in range(0, rows, step):
        wanted = gm_ref[:, start : start + step]
        voxel = lax.broadcasted_iota(jnp.int32, (voxels, step), 0)
        chosen = jnp.where(voxel == wanted, 1.0, 0.0).astype(jnp.bfloat16)
        picked = jnp.dot(scored[...], chosen, preferred_element_type=jnp.float32)
        out_ref[:, start : start + step] = picked.astype(jnp.bfloat16)


def make_panel(window, col, bold, low, high, edge, corner, gm):
    _, frames, slab_x, slab_y, slab_z = bold.shape
    rows = gm.shape[1]
    whole = lambda array: pl.BlockSpec(array.shape, lambda *_: (0,) * array.ndim)
    f32 = jnp.float32
    return pl.pallas_call(
        panel_kernel,
        grid=(1,),
        in_specs=[
            pl.BlockSpec(memory_space=pltpu.SMEM),
            pl.BlockSpec((1, frames, slab_x, slab_y, slab_z), lambda _: (window, 0, 0, 0, 0)),
            whole(low), whole(high), whole(edge), whole(corner), whole(gm),
        ],
        out_specs=pl.BlockSpec((frames, rows), lambda _: (0, 0)),
        out_shape=jax.ShapeDtypeStruct((frames, rows), jnp.bfloat16),
        scratch_shapes=[
            pltpu.VMEM((frames * slab_x * slab_y, slab_z), f32),
            pltpu.VMEM((frames * slab_y, slab_z), f32),
            pltpu.VMEM((frames * slab_y, slab_z), f32),
            pltpu.VMEM((slab_x, slab_y + 2, frames, slab_z), f32),
            pltpu.VMEM((frames, slab_x * slab_y * slab_z), jnp.bfloat16),
        ],
        compiler_params=pltpu.CompilerParams(vmem_limit_bytes=VMEM_BYTES),
        cost_estimate=pl.CostEstimate(
            flops=2 * frames * rows * slab_x * slab_y * slab_z,
            bytes_accessed=4 * 1024 * 1024, transcendentals=0,
        ),
        name="blur_score_pick",
    )(col, bold, low, high, edge, corner, gm)


def tiles_kernel(place_ref, present_ref, *refs, sources):
    parts = refs[:sources]
    out_ref, held, sems = refs[-3:]
    block = pl.program_id(0)
    slots = out_ref.shape[1]
    blocks_each = held.shape[2] // BLOCK

    @pl.when(block == 0)
    def _():
        for n, part in enumerate(parts):
            pltpu.make_async_copy(part, held.at[n], sems.at[n]).start()
        for n, part in enumerate(parts):
            pltpu.make_async_copy(part, held.at[n], sems.at[n]).wait()

    own = held[0, :, pl.ds(pl.multiple_of(block * BLOCK, BLOCK), BLOCK)].T

    def partner(slot):
        place = place_ref[block * slots + slot]
        start = pl.multiple_of(lax.rem(place, blocks_each) * BLOCK, BLOCK)
        return held[place // blocks_each, :, pl.ds(start, BLOCK)]

    for slot in range(0, slots, 2):
        pair = jnp.concatenate([partner(slot), partner(slot + 1)], axis=1)
        both = jnp.dot(own, pair, preferred_element_type=jnp.float32)
        for n in range(2):
            keep = present_ref[block * slots + slot + n] != 0
            tile = both[:, n * BLOCK : (n + 1) * BLOCK]
            out_ref[0, slot + n, 0] = jnp.where(keep, tile, 0.0).astype(jnp.bfloat16)


def make_tiles(window, windows, place, present, sources, earlier):
    frames, rows = sources[0].shape
    blocks = rows // BLOCK
    slots = place.shape[0] // blocks
    count = len(sources)
    anywhere = pl.BlockSpec(memory_space=pl.ANY)
    operands = list(sources) + ([] if earlier is None else [earlier])
    return pl.pallas_call(
        functools.partial(tiles_kernel, sources=count),
        grid_spec=pltpu.PrefetchScalarGridSpec(
            num_scalar_prefetch=2,
            grid=(blocks,),
            in_specs=[anywhere] * len(operands),
            out_specs=pl.BlockSpec(
                (1, slots, 1, BLOCK, BLOCK), lambda i, *_: (i, 0, window, 0, 0)
            ),
            scratch_shapes=[
                pltpu.VMEM((count, frames, rows), jnp.bfloat16),
                pltpu.SemaphoreType.DMA((count,)),
            ],
        ),
        out_shape=jax.ShapeDtypeStruct((blocks, slots, windows, BLOCK, BLOCK), jnp.bfloat16),
        input_output_aliases={} if earlier is None else {2 + count: 0},
        compiler_params=pltpu.CompilerParams(vmem_limit_bytes=VMEM_BYTES),
        cost_estimate=pl.CostEstimate(
            flops=2 * blocks * slots * BLOCK * BLOCK * frames,
            bytes_accessed=10 * 1024 * 1024, transcendentals=0,
        ),
        name="tiles",
    )(place, present, *operands)


def on_device(bold, gm_index, partners):
    windows, frames, slab_x, slab_y, slab_z = bold.shape
    row_total = lax.axis_size("row")
    col_total = lax.axis_size("col")
    row = lax.axis_index("row")
    col = lax.axis_index("col")
    even = row % 2 == 0

    def shift_row(value, pairs):
        return lax.ppermute(value, "row", pairs)

    def other_col(value):
        return lax.ppermute(value, "col", [(0, 1), (1, 0)])

    up = [(i, i + 1) for i in range(row_total - 1)]
    down = [(i + 1, i) for i in range(row_total - 1)]
    up_two = [(i, (i + 2) % row_total) for i in range(row_total)]
    down_two = [((i + 2) % row_total, i) for i in range(row_total)]
    pairs = [(i, i ^ 1) for i in range(row_total)]

    gm = gm_index.reshape(1, -1)
    col_arg = col.reshape(1).astype(jnp.int32)

    face = jnp.where(col == 0, bold[:, :, :, -1], bold[:, :, :, 0])
    edge = other_col(jnp.transpose(face, (0, 2, 1, 3)))

    blocks = partners.shape[0]
    ids = jnp.maximum(partners, 0)
    slab = ids // blocks
    distance = (slab // col_total - row + 2 + row_total) % row_total
    kind = jnp.where(
        even,
        jnp.array([1, 4, 0, 3, 2], jnp.int32)[jnp.minimum(distance, 4)],
        jnp.array([1, 3, 0, 4, 2], jnp.int32)[jnp.minimum(distance, 4)],
    )
    away = (slab % col_total != col).astype(jnp.int32)
    place = ((away * 5 + kind) * blocks + ids % blocks).astype(jnp.int32).reshape(-1)
    present = (partners >= 0).astype(jnp.int32).reshape(-1)

    halos = []
    for window in range(windows):
        low = shift_row(bold[window, :, -1], up)
        high = shift_row(bold[window, :, 0], down)
        halos.append((low, high))
    out = None
    for window in range(windows):
        low, high = halos[window]
        ends = jnp.stack(
            [jnp.where(col == 0, layer[:, -1], layer[:, 0]) for layer in (low, high)], 0
        )
        corner = other_col(ends)
        own = make_panel(window, col_arg, bold, low, high, edge[window], corner, gm)
        lower = shift_row(own, up_two)
        upper = shift_row(own, down_two)
        pair = shift_row(own, pairs)
        rest = shift_row(jnp.where(even, upper, lower), pairs)
        mine = [own, lower, upper, pair, rest]
        sources = mine + [other_col(part) for part in mine]
        out = make_tiles(window, windows, place, present, sources, out)
    return out


def solution(mesh):
    in_specs = (P("subj", None, "row", "col", None), P(("row", "col")), P(("row", "col"), None))
    out_specs = P(("row", "col"), None, "subj", None, None)
    return jax.shard_map(
        on_device, mesh=mesh, in_specs=in_specs, out_specs=out_specs, check_vma=False
    )
```

time: 384 us -> 146 us (0.38)
  local copies, waits for them, and re-layouts: 133 us -> 12.8 us
  waiting for transfers between devices: 154 us -> 76.9 us
  other arithmetic: 57.5 us -> 1.98 us
  Pallas kernels: 0 us -> 26 us
  between operations: 13.7 us -> 0.54 us
  starting transfers between devices: 19 us -> 25.1 us
  matrix products: 5.71 us -> 0 us
    gather x11 -> x2, local copies, waits for them, and re-layouts: 83.3 us -> 2.45 us  [the longest x1 1.23 us: on_device(): jnp.array([1, 4, 0, 3, 2], jnp.int32)[jnp.minimum(distance, 4)]]
    ppermute x8 -> x25, waiting for transfers between devices: 130 us -> 76.9 us  [the longest x12 76.2 us: shift_row(): return lax.ppermute(value, 'row', pairs)]
    pallas_call x0 -> x4, Pallas kernels: none -> 26 us  [the longest x2 16.4 us: make_tiles(): pl.pallas_call(functools.partial(tiles_kernel, sources=count), grid_spec=...]
    all_gather x1 -> x0, waiting for transfers between devices: 24.4 us -> none  [on_device(): collected = lax.all_gather(own_column, 'col', axis=1, tiled=True)]
    add x3 -> x1, other arithmetic: 15.8 us -> 0.02 us  [on_device(): (away * 5 + kind) * blocks + ids % blocks]
    reshape x1 -> x2, local copies, waits for them, and re-layouts: 15.3 us -> 0.16 us  [the longest x1 0.08 us: on_device(): ((away * 5 + kind) * blocks + ids % blocks).astype(jnp.int32).reshape(-1)]
    select_n x18 -> x8, other arithmetic: 16.4 us -> 1.85 us  [the longest x4 0.91 us: on_device(): jnp.where(col == 0, layer[:, -1], layer[:, 0])]
    dynamic_update_slice x16 -> x0, local copies, waits for them, and re-layouts: 13.7 us -> none  [on_device(): return lax.map(block_tiles, (local_blocks, position, partners >= 0))]
  transfers between devices with their start and end apart: 9 -> 25, of which waited for: 6 -> 8; matrix products, arithmetic and copies ran while one was open for 3% -> 6% of each run, Pallas kernels for 0% -> 9%
where the time goes in v1:
time: 146 us; the launch traced here: 143 us
  waiting for transfers between devices  76.9 us (53%)
  Pallas kernels  26 us (18%)
  starting transfers between devices  25.1 us (17%)
  local copies, waits for them, and re-layouts  12.8 us (9%)
  other arithmetic  1.98 us (1%)
    ppermute x12, waiting for transfers between devices, shift_row(): return lax.ppermute(value, 'row', pairs)  76.2 us
    ppermute x12, starting transfers between devices, shift_row(): return lax.ppermute(value, 'row', pairs)  22.8 us
    pallas_call x2, Pallas kernels, make_tiles(): pl.pallas_call(functools.partial(tiles_kernel, sources=count), grid_spec=...  16.4 us
    pallas_call x2, Pallas kernels, make_panel(): pl.pallas_call(panel_kernel, grid=(1,), in_specs=[pl.BlockSpec(memory_spa...  9.63 us
    unnamed x22, local copies, waits for them, and re-layouts  4.06 us
  transfers between devices with their start and end apart: 25, of which 8 were waited for; matrix products, arithmetic and copies ran while one was open for 6% of the time, Pallas kernels for 9%

profile of v1, /device:TPU:0, one launch (start us, length us, event | category | flops | bytes accessed | tf_op | source)
XLA Modules:
  0.0 143.3 jit_solution(1168909942341246605)
XLA Ops:
  0.0 2.9 %fusion.14 = (bf16[1,256,1,8,128]{4,3,2,1,0:T(8,128)(2,1)}, bf16[1,256,1,8,128]{4,3,2,1,0:T(8,128)(2,1)}, bf16[1,256,1,8,128]{4,3,2,1,0:T(8,128)(2,1)}, bf16[1,256,1,8,128]{4,3,2,1,0:T(8,128)(2,1)S(1)}) fusion(bf16[2,256,2,8,128]{4,3,2,1,0:T(8,128)(2,1)} %bold_ref.3), kind=kLoop, calls=%fused_computation.48 | loop fusion | bytes 4194304 | tf_op jit(solution)/shard_map/slice | solution.py:205
  3.7 5.7 %collective-permute-start.13 = (bf16[256,8,128]{2,0,1:T(8,128)(2,1)}, bf16[256,8,128]{2,0,1:T(8,128)(2,1)}, u32[]{:S(2)}, u32[]{:S(2)}) collective-permute-start(bf16[256,8,128]{2,0,1:T(8,128)(2,1)} %bitcast.27), channel_id=1, source_target_pairs={{0,2},{2,4},{4,6},{6,8},{8,10},{10,12},{12,14},{1,3},{3,5},{5,7},{... | collective-permute-start | bytes 1572872 | tf_op jit(solution)/shard_map/ppermute | solution.py:172
  10.3 1.2 copy.41
  11.5 1.3 collective-permute-start.14
  12.8 4.6 %collective-permute-start = (bf16[256,8,128]{2,0,1:T(8,128)(2,1)S(1)}, bf16[256,8,128]{2,0,1:T(8,128)(2,1)S(1)}, u32[]{:S(2)}, u32[]{:S(2)}) collective-permute-start(bf16[256,8,128]{2,0,1:T(8,128)(2,1)S(1)} %bitcast.32), channel_id=1, source_target_pairs={{0,2},{2,4},{4,6},{6,8},{8,10},{10,12},{12,14},{1,3},{3,5},{5,7},{... | collective-permute-start | bytes 1572872 | tf_op jit(solution)/shard_map/ppermute | solution.py:172
  17.5 1.3 collective-permute-start.1
  18.9 24.8 %collective-permute-done.13 = bf16[256,8,128]{2,0,1:T(8,128)(2,1)} collective-permute-done((bf16[256,8,128]{2,0,1:T(8,128)(2,1)}, bf16[256,8,128]{2,0,1:T(8,128)(2,1)}, u32[]{:S(2)}, u32[]{:S(2)}) %collective-permute-start.13) | collective-permute-done | bytes 524320 | tf_op jit(solution)/shard_map/ppermute | solution.py:172
  43.7 0.9 fusion.2
  44.7 1.4 copy.25.low_ref
  46.4 7.2 %collective-permute-done = bf16[256,8,128]{2,0,1:T(8,128)(2,1)S(1)} collective-permute-done((bf16[256,8,128]{2,0,1:T(8,128)(2,1)S(1)}, bf16[256,8,128]{2,0,1:T(8,128)(2,1)S(1)}, u32[]{:S(2)}, u32[]{:S(2)}) %collective-permute-start) | collective-permute-done | bytes 524320 | tf_op jit(solution)/shard_map/ppermute | solution.py:172
  53.7 4.8 %blur_score_pick.3.refs_0_ = bf16[256,1024]{1,0:T(8,128)(2,1)} custom-call(s32[1]{0:T(128)} %bitcast.col_ref, bf16[2,256,2,8,128]{4,3,2,1,0:T(8,128)(2,1)S(1)} %copy-done, bf16[256,8,128]{2,1,0:T(8,128)(2,1)S(1)} %copy.25.low_ref, bf16[256,8,128]{2,1,0:T(8,128)(2,1)S(1)} %copy.26.high_ref, bf16[2,256,128]{2,1,0:T(8,128)(2,1)S(1)} %get-tuple-element.11.edge_ref, ...), custom_call_target="tpu_custom_call" | custom-call | flops 1073741824 | bytes 4194304 | tf_op jit(solution)/shard_map/blur_score_pick/pallas_call | solution.py:75
  58.5 5.4 %collective-permute-start.17 = (bf16[256,1024]{1,0:T(8,128)(2,1)}, bf16[256,1024]{1,0:T(8,128)(2,1)S(1)}, u32[]{:S(2)}, u32[]{:S(2)}) collective-permute-start(bf16[256,1024]{1,0:T(8,128)(2,1)} %blur_score_pick.3.refs_0_), channel_id=1, source_target_pairs={{4,0},{6,2},{8,4},{10,6},{12,8},{14,10},{0,12},{2,14},{5,1},{7,3},... | collective-permute-start | bytes 1572872 | tf_op jit(solution)/shard_map/ppermute | solution.py:172
  65.4 4.8 %blur_score_pick.2.refs_0_ = bf16[256,1024]{1,0:T(8,128)(2,1)} custom-call(s32[1]{0:T(128)} %bitcast.col_ref, bf16[2,256,2,8,128]{4,3,2,1,0:T(8,128)(2,1)S(1)} %copy-done, bf16[256,8,128]{2,1,0:T(8,128)(2,1)S(1)} %copy.21.low_ref, bf16[256,8,128]{2,1,0:T(8,128)(2,1)S(1)} %copy.22.high_ref, bf16[2,256,128]{2,1,0:T(8,128)(2,1)S(1)} %get-tuple-element.12.edge_ref, ...), custom_call_target="tpu_custom_call" | custom-call | flops 1073741824 | bytes 4194304 | tf_op jit(solution)/shard_map/blur_score_pick/pallas_call | solution.py:75
  70.2 3.8 %collective-permute-start.5 = (bf16[256,1024]{1,0:T(8,128)(2,1)}, bf16[256,1024]{1,0:T(8,128)(2,1)S(1)}, u32[]{:S(2)}, u32[]{:S(2)}) collective-permute-start(bf16[256,1024]{1,0:T(8,128)(2,1)} %blur_score_pick.2.refs_0_), channel_id=1, source_target_pairs={{4,0},{6,2},{8,4},{10,6},{12,8},{14,10},{0,12},{2,14},{5,1},{7,3},... | collective-permute-start | bytes 1572872 | tf_op jit(solution)/shard_map/ppermute | solution.py:172
  74.1 2.6 %collective-permute-done.17.refs_2_ = bf16[256,1024]{1,0:T(8,128)(2,1)S(1)} collective-permute-done((bf16[256,1024]{1,0:T(8,128)(2,1)}, bf16[256,1024]{1,0:T(8,128)(2,1)S(1)}, u32[]{:S(2)}, u32[]{:S(2)}) %collective-permute-start.17) | collective-permute-done | bytes 524320 | tf_op jit(solution)/shard_map/ppermute | solution.py:172
  76.6 12.0 %collective-permute-done.16.refs_1_ = bf16[256,1024]{1,0:T(8,128)(2,1)S(1)} collective-permute-done((bf16[256,1024]{1,0:T(8,128)(2,1)}, bf16[256,1024]{1,0:T(8,128)(2,1)S(1)}, u32[]{:S(2)}, u32[]{:S(2)}) %collective-permute-start.16) | collective-permute-done | bytes 524320 | tf_op jit(solution)/shard_map/ppermute | solution.py:172
  89.5 9.7 %collective-permute-done.5.refs_2_ = bf16[256,1024]{1,0:T(8,128)(2,1)S(1)} collective-permute-done((bf16[256,1024]{1,0:T(8,128)(2,1)}, bf16[256,1024]{1,0:T(8,128)(2,1)S(1)}, u32[]{:S(2)}, u32[]{:S(2)}) %collective-permute-start.5) | collective-permute-done | bytes 524320 | tf_op jit(solution)/shard_map/ppermute | solution.py:172
  99.2 11.1 %collective-permute-done.4.refs_1_ = bf16[256,1024]{1,0:T(8,128)(2,1)S(1)} collective-permute-done((bf16[256,1024]{1,0:T(8,128)(2,1)}, bf16[256,1024]{1,0:T(8,128)(2,1)S(1)}, u32[]{:S(2)}, u32[]{:S(2)}) %collective-permute-start.4) | collective-permute-done | bytes 524320 | tf_op jit(solution)/shard_map/ppermute | solution.py:172
  113.1 1.2 gather_fusion.1
  114.3 1.2 gather_fusion
  115.6 8.7 %collective-permute-done.7.refs_4_ = bf16[256,1024]{1,0:T(8,128)(2,1)S(1)} collective-permute-done((bf16[256,1024]{1,0:T(8,128)(2,1)}, bf16[256,1024]{1,0:T(8,128)(2,1)S(1)}, u32[]{:S(2)}, u32[]{:S(2)}) %collective-permute-start.7) | collective-permute-done | bytes 524320 | tf_op jit(solution)/shard_map/ppermute | solution.py:172
  125.7 1.0 copy-done.2
  126.7 8.3 %tiles.2.refs_10_ = bf16[8,16,2,128,128]{4,3,2,1,0:T(8,128)(2,1)} custom-call(s32[128]{0:T(128)S(1)} %reshape.92.place_ref, s32[128]{0:T(128)S(1)} %reshape.98.present_ref, bf16[256,1024]{1,0:T(8,128)(2,1)} %blur_score_pick.3.refs_0_, bf16[256,1024]{1,0:T(8,128)(2,1)S(1)} %collective-permute-done.16.refs_1_, ...), custom_call_target="tpu_custom_call" | custom-call | flops 1073741824 | bytes 10485760 | tf_op jit(solution)/shard_map/tiles/pallas_call | solution.py:138
  135.0 8.1 %tiles.3 = bf16[8,16,2,128,128]{4,3,2,1,0:T(8,128)(2,1)} custom-call(s32[128]{0:T(128)S(1)} %reshape.92.place_ref, s32[128]{0:T(128)S(1)} %reshape.98.present_ref, bf16[256,1024]{1,0:T(8,128)(2,1)} %blur_score_pick.2.refs_0_, bf16[256,1024]{1,0:T(8,128)(2,1)S(1)} %collective-permute-done.4.refs_1_, ...), custom_call_target="tpu_custom_call", output_to_operand_aliasing={{}: (12, {})} | custom-call | flops 1073741824 | bytes 10485760 | tf_op jit(solution)/shard_map/tiles/pallas_call | solution.py:138
  (79 shorter events, 8.7 us)
Async XLA Ops:
  3.7 40.0 %collective-permute-start.13 = (bf16[256,8,128]{2,0,1:T(8,128)(2,1)}, bf16[256,8,128]{2,0,1:T(8,128)(2,1)}, u32[]{:S(2)}, u32[]{:S(2)}) collective-permute-start(bf16[256,8,128]{2,0,1:T(8,128)(2,1)} %bitcast.27), channel_id=1, source_target_pairs={{0,2},{2,4},{4,6},{6,8},{8,10},{10,12},{12,14},{1,3},{3,5},{5,7},{... | collective-permute-start | bytes 1572872 | tf_op jit(solution)/shard_map/ppermute | solution.py:172
  10.2 8.7 %collective-permute-start.2 = (bf16[2,2,256,128]{3,2,1,0:T(8,128)(2,1)S(1)}, bf16[2,2,256,128]{3,2,1,0:T(8,128)(2,1)S(1)}, u32[]{:S(2)}, u32[]{:S(2)}) collective-permute-start(bf16[2,2,256,128]{3,2,1,0:T(8,128)(2,1)S(1)} %fusion), channel_id=1, source_target_pairs={{0,1},{1,0},{2,3},{3,2},{4,5},{5,4},{6,7},{7,6},{8,9},{9,8},{10,11... | collective-permute-start | bytes 786440 | tf_op jit(solution)/shard_map/ppermute | solution.py:175
  11.5 33.1 %collective-permute-start.14 = (bf16[256,8,128]{2,0,1:T(8,128)(2,1)S(1)}, bf16[256,8,128]{2,0,1:T(8,128)(2,1)S(1)}, u32[]{:S(2)}, u32[]{:S(2)}) collective-permute-start(bf16[256,8,128]{2,0,1:T(8,128)(2,1)S(1)} %bitcast.34), channel_id=1, source_target_pairs={{2,0},{4,2},{6,4},{8,6},{10,8},{12,10},{14,12},{3,1},{5,3},{7,5},{... | collective-permute-start | bytes 1572872 | tf_op jit(solution)/shard_map/ppermute | solution.py:172
  12.8 40.8 %collective-permute-start = (bf16[256,8,128]{2,0,1:T(8,128)(2,1)S(1)}, bf16[256,8,128]{2,0,1:T(8,128)(2,1)S(1)}, u32[]{:S(2)}, u32[]{:S(2)}) collective-permute-start(bf16[256,8,128]{2,0,1:T(8,128)(2,1)S(1)} %bitcast.32), channel_id=1, source_target_pairs={{0,2},{2,4},{4,6},{6,8},{8,10},{10,12},{12,14},{1,3},{3,5},{5,7},{... | collective-permute-start | bytes 1572872 | tf_op jit(solution)/shard_map/ppermute | solution.py:172
  17.5 36.2 %collective-permute-start.1 = (bf16[256,8,128]{2,0,1:T(8,128)(2,1)S(1)}, bf16[256,8,128]{2,0,1:T(8,128)(2,1)S(1)}, u32[]{:S(2)}, u32[]{:S(2)}) collective-permute-start(bf16[256,8,128]{2,0,1:T(8,128)(2,1)S(1)} %bitcast.33), channel_id=1, source_target_pairs={{2,0},{4,2},{6,4},{8,6},{10,8},{12,10},{14,12},{3,1},{5,3},{7,5},{... | collective-permute-start | bytes 1572872 | tf_op jit(solution)/shard_map/ppermute | solution.py:172
  44.6 9.1 %collective-permute-start.15 = (bf16[2,256,128]{2,1,0:T(8,128)(2,1)S(1)}, bf16[2,256,128]{2,1,0:T(8,128)(2,1)S(1)}, u32[]{:S(2)}, u32[]{:S(2)}) collective-permute-start(bf16[2,256,128]{2,1,0:T(8,128)(2,1)S(1)} %pad_maximum_fusion.1), channel_id=1, source_target_pairs={{0,1},{1,0},{2,3},{3,2},{4,5},{5,4},{6,7},{7,6},{8,9},{9,8},{10,11... | collective-permute-start | bytes 393224 | tf_op jit(solution)/shard_map/ppermute | solution.py:175
  58.5 18.1 %collective-permute-start.17 = (bf16[256,1024]{1,0:T(8,128)(2,1)}, bf16[256,1024]{1,0:T(8,128)(2,1)S(1)}, u32[]{:S(2)}, u32[]{:S(2)}) collective-permute-start(bf16[256,1024]{1,0:T(8,128)(2,1)} %blur_score_pick.3.refs_0_), channel_id=1, source_target_pairs={{4,0},{6,2},{8,4},{10,6},{12,8},{14,10},{0,12},{2,14},{5,1},{7,3},... | collective-permute-start | bytes 1572872 | tf_op jit(solution)/shard_map/ppermute | solution.py:172
  64.0 24.7 %collective-permute-start.16 = (bf16[256,1024]{1,0:T(8,128)(2,1)}, bf16[256,1024]{1,0:T(8,128)(2,1)S(1)}, u32[]{:S(2)}, u32[]{:S(2)}) collective-permute-start(bf16[256,1024]{1,0:T(8,128)(2,1)} %blur_score_pick.3.refs_0_), channel_id=1, source_target_pairs={{0,4},{2,6},{4,8},{6,10},{8,12},{10,14},{12,0},{14,2},{1,5},{3,7},... | collective-permute-start | bytes 1572872 | tf_op jit(solution)/shard_map/ppermute | solution.py:172
  70.2 28.9 %collective-permute-start.5 = (bf16[256,1024]{1,0:T(8,128)(2,1)}, bf16[256,1024]{1,0:T(8,128)(2,1)S(1)}, u32[]{:S(2)}, u32[]{:S(2)}) collective-permute-start(bf16[256,1024]{1,0:T(8,128)(2,1)} %blur_score_pick.2.refs_0_), channel_id=1, source_target_pairs={{4,0},{6,2},{8,4},{10,6},{12,8},{14,10},{0,12},{2,14},{5,1},{7,3},... | collective-permute-start | bytes 1572872 | tf_op jit(solution)/shard_map/ppermute | solution.py:172
  74.1 36.2 %collective-permute-start.4 = (bf16[256,1024]{1,0:T(8,128)(2,1)}, bf16[256,1024]{1,0:T(8,128)(2,1)S(1)}, u32[]{:S(2)}, u32[]{:S(2)}) collective-permute-start(bf16[256,1024]{1,0:T(8,128)(2,1)} %blur_score_pick.2.refs_0_), channel_id=1, source_target_pairs={{0,4},{2,6},{4,8},{6,10},{8,12},{10,14},{12,0},{14,2},{1,5},{3,7},... | collective-permute-start | bytes 1572872 | tf_op jit(solution)/shard_map/ppermute | solution.py:172
  74.1 37.0 %collective-permute-start.6 = (bf16[256,1024]{1,0:T(8,128)(2,1)}, bf16[256,1024]{1,0:T(8,128)(2,1)S(1)}, u32[]{:S(2)}, u32[]{:S(2)}) collective-permute-start(bf16[256,1024]{1,0:T(8,128)(2,1)} %blur_score_pick.2.refs_0_), channel_id=1, source_target_pairs={{0,2},{2,0},{4,6},{6,4},{8,10},{10,8},{12,14},{14,12},{1,3},{3,1},... | collective-permute-start | bytes 1572872 | tf_op jit(solution)/shard_map/ppermute | solution.py:172
  76.6 34.5 %collective-permute-start.20 = (bf16[256,1024]{1,0:T(8,128)(2,1)}, bf16[256,1024]{1,0:T(8,128)(2,1)S(1)}, u32[]{:S(2)}, u32[]{:S(2)}) collective-permute-start(bf16[256,1024]{1,0:T(8,128)(2,1)} %blur_score_pick.3.refs_0_), channel_id=1, source_target_pairs={{0,1},{1,0},{2,3},{3,2},{4,5},{5,4},{6,7},{7,6},{8,9},{9,8},{10,11... | collective-permute-start | bytes 1572872 | tf_op jit(solution)/shard_map/ppermute | solution.py:175
  88.7 23.7 %collective-permute-start.18 = (bf16[256,1024]{1,0:T(8,128)(2,1)}, bf16[256,1024]{1,0:T(8,128)(2,1)}, u32[]{:S(2)}, u32[]{:S(2)}) collective-permute-start(bf16[256,1024]{1,0:T(8,128)(2,1)} %blur_score_pick.3.refs_0_), channel_id=1, source_target_pairs={{0,2},{2,0},{4,6},{6,4},{8,10},{10,8},{12,14},{14,12},{1,3},{3,1},... | collective-permute-start | bytes 1572872 | tf_op jit(solution)/shard_map/ppermute | solution.py:172
  99.2 13.3 %collective-permute-start.19 = (bf16[256,1024]{1,0:T(8,128)(2,1)S(1)}, bf16[256,1024]{1,0:T(8,128)(2,1)}, u32[]{:S(2)}, u32[]{:S(2)}) collective-permute-start(bf16[256,1024]{1,0:T(8,128)(2,1)S(1)} %broadcast_select_fusion), channel_id=1, source_target_pairs={{0,2},{2,0},{4,6},{6,4},{8,10},{10,8},{12,14},{14,12},{1,3},{3,1},... | collective-permute-start | bytes 1572872 | tf_op jit(solution)/shard_map/ppermute | solution.py:172
  111.1 13.3 %collective-permute-start.7 = (bf16[256,1024]{1,0:T(8,128)(2,1)}, bf16[256,1024]{1,0:T(8,128)(2,1)S(1)}, u32[]{:S(2)}, u32[]{:S(2)}) collective-permute-start(bf16[256,1024]{1,0:T(8,128)(2,1)} %broadcast_select_fusion.1), channel_id=1, source_target_pairs={{0,2},{2,0},{4,6},{6,4},{8,10},{10,8},{12,14},{14,12},{1,3},{3,1},... | collective-permute-start | bytes 1572872 | tf_op jit(solution)/shard_map/ppermute | solution.py:172
  111.1 13.8 %collective-permute-start.22 = (bf16[256,1024]{1,0:T(8,128)(2,1)S(1)}, bf16[256,1024]{1,0:T(8,128)(2,1)}, u32[]{:S(2)}, u32[]{:S(2)}) collective-permute-start(bf16[256,1024]{1,0:T(8,128)(2,1)S(1)} %collective-permute-done.17.refs_2_), channel_id=1, source_target_pairs={{0,1},{1,0},{2,3},{3,2},{4,5},{5,4},{6,7},{7,6},{8,9},{9,8},{10,11... | collective-permute-start | bytes 1572872 | tf_op jit(solution)/shard_map/ppermute | solution.py:175
  111.9 13.1 %collective-permute-start.21 = (bf16[256,1024]{1,0:T(8,128)(2,1)S(1)}, bf16[256,1024]{1,0:T(8,128)(2,1)}, u32[]{:S(2)}, u32[]{:S(2)}) collective-permute-start(bf16[256,1024]{1,0:T(8,128)(2,1)S(1)} %collective-permute-done.16.refs_1_), channel_id=1, source_target_pairs={{0,1},{1,0},{2,3},{3,2},{4,5},{5,4},{6,7},{7,6},{8,9},{9,8},{10,11... | collective-permute-start | bytes 1572872 | tf_op jit(solution)/shard_map/ppermute | solution.py:175
  112.4 12.0 %collective-permute-start.23 = (bf16[256,1024]{1,0:T(8,128)(2,1)}, bf16[256,1024]{1,0:T(8,128)(2,1)}, u32[]{:S(2)}, u32[]{:S(2)}) collective-permute-start(bf16[256,1024]{1,0:T(8,128)(2,1)} %collective-permute-done.18.refs_3_), channel_id=1, source_target_pairs={{0,1},{1,0},{2,3},{3,2},{4,5},{5,4},{6,7},{7,6},{8,9},{9,8},{10,11... | collective-permute-start | bytes 1572872 | tf_op jit(solution)/shard_map/ppermute | solution.py:175
  112.4 13.0 %collective-permute-start.24 = (bf16[256,1024]{1,0:T(8,128)(2,1)}, bf16[256,1024]{1,0:T(8,128)(2,1)}, u32[]{:S(2)}, u32[]{:S(2)}) collective-permute-start(bf16[256,1024]{1,0:T(8,128)(2,1)} %collective-permute-done.19.refs_4_), channel_id=1, source_target_pairs={{0,1},{1,0},{2,3},{3,2},{4,5},{5,4},{6,7},{7,6},{8,9},{9,8},{10,11... | collective-permute-start | bytes 1572872 | tf_op jit(solution)/shard_map/ppermute | solution.py:175
  124.4 10.6 %collective-permute-start.8 = (bf16[256,1024]{1,0:T(8,128)(2,1)}, bf16[256,1024]{1,0:T(8,128)(2,1)}, u32[]{:S(2)}, u32[]{:S(2)}) collective-permute-start(bf16[256,1024]{1,0:T(8,128)(2,1)} %blur_score_pick.2.refs_0_), channel_id=1, source_target_pairs={{0,1},{1,0},{2,3},{3,2},{4,5},{5,4},{6,7},{7,6},{8,9},{9,8},{10,11... | collective-permute-start | bytes 1572872 | tf_op jit(solution)/shard_map/ppermute | solution.py:175
  124.4 10.6 %collective-permute-start.10 = (bf16[256,1024]{1,0:T(8,128)(2,1)S(1)}, bf16[256,1024]{1,0:T(8,128)(2,1)}, u32[]{:S(2)}, u32[]{:S(2)}) collective-permute-start(bf16[256,1024]{1,0:T(8,128)(2,1)S(1)} %collective-permute-done.5.refs_2_), channel_id=1, source_target_pairs={{0,1},{1,0},{2,3},{3,2},{4,5},{5,4},{6,7},{7,6},{8,9},{9,8},{10,11... | collective-permute-start | bytes 1572872 | tf_op jit(solution)/shard_map/ppermute | solution.py:175
  124.9 10.1 %collective-permute-start.9 = (bf16[256,1024]{1,0:T(8,128)(2,1)S(1)}, bf16[256,1024]{1,0:T(8,128)(2,1)}, u32[]{:S(2)}, u32[]{:S(2)}) collective-permute-start(bf16[256,1024]{1,0:T(8,128)(2,1)S(1)} %collective-permute-done.4.refs_1_), channel_id=1, source_target_pairs={{0,1},{1,0},{2,3},{3,2},{4,5},{5,4},{6,7},{7,6},{8,9},{9,8},{10,11... | collective-permute-start | bytes 1572872 | tf_op jit(solution)/shard_map/ppermute | solution.py:175
  125.0 10.0 %collective-permute-start.11 = (bf16[256,1024]{1,0:T(8,128)(2,1)S(1)}, bf16[256,1024]{1,0:T(8,128)(2,1)}, u32[]{:S(2)}, u32[]{:S(2)}) collective-permute-start(bf16[256,1024]{1,0:T(8,128)(2,1)S(1)} %collective-permute-done.6.refs_3_), channel_id=1, source_target_pairs={{0,1},{1,0},{2,3},{3,2},{4,5},{5,4},{6,7},{7,6},{8,9},{9,8},{10,11... | collective-permute-start | bytes 1572872 | tf_op jit(solution)/shard_map/ppermute | solution.py:175
  125.4 9.6 %collective-permute-start.12 = (bf16[256,1024]{1,0:T(8,128)(2,1)S(1)}, bf16[256,1024]{1,0:T(8,128)(2,1)}, u32[]{:S(2)}, u32[]{:S(2)}) collective-permute-start(bf16[256,1024]{1,0:T(8,128)(2,1)S(1)} %collective-permute-done.7.refs_4_), channel_id=1, source_target_pairs={{0,1},{1,0},{2,3},{3,2},{4,5},{5,4},{6,7},{7,6},{8,9},{9,8},{10,11... | collective-permute-start | bytes 1572872 | tf_op jit(solution)/shard_map/ppermute | solution.py:175
  (10 other events, 145.6 us)

commit v2 on v1

v2 whole, which is shorter than its diff:
```python
import functools
import math

import jax
import jax.numpy as jnp
from jax import lax
from jax.experimental import pallas as pl
from jax.experimental.pallas import tpu as pltpu
from jax.sharding import PartitionSpec as P

BLOCK = 128
SIDE = math.exp(-0.5) / (1.0 + 2.0 * math.exp(-0.5))
CENTRE = 1.0 / (1.0 + 2.0 * math.exp(-0.5))
SMALL = pl.CostEstimate(flops=1, bytes_accessed=1, transcendentals=0)
VMEM_BYTES = 24 * 1024 * 1024


def faces_kernel(col_ref, bold_ref, first_ref, last_ref, edge_ref, wide):
    frames, slab_x, slab_y, slab_z = bold_ref.shape[1:]
    per_frame = slab_x * slab_y
    wide[...] = bold_ref[0].reshape(frames * per_frame, slab_z).astype(jnp.float32)
    for x, layer_ref in enumerate((first_ref, last_ref)):
        for y in range(slab_y):
            plane = wide[pl.ds(x * slab_y + y, frames, stride=per_frame), :]
            layer_ref[y] = plane.astype(jnp.bfloat16)
        @pl.when(col_ref[0] == 0)
        def _():
            edge_ref[x] = layer_ref[slab_y - 1]

        @pl.when(col_ref[0] != 0)
        def _():
            edge_ref[x] = layer_ref[0]


def make_faces(window, col, bold):
    _, frames, slab_x, slab_y, slab_z = bold.shape
    layer = jax.ShapeDtypeStruct((slab_y, frames, slab_z), jnp.bfloat16)
    edge = jax.ShapeDtypeStruct((slab_x, frames, slab_z), jnp.bfloat16)
    whole = lambda array: pl.BlockSpec(array.shape, lambda _: (0,) * len(array.shape))
    return pl.pallas_call(
        faces_kernel,
        grid=(1,),
        in_specs=[
            pl.BlockSpec(memory_space=pltpu.SMEM),
            pl.BlockSpec((1, frames, slab_x, slab_y, slab_z), lambda _: (window, 0, 0, 0, 0)),
        ],
        out_specs=[whole(layer), whole(layer), whole(edge)],
        out_shape=[layer, layer, edge],
        scratch_shapes=[pltpu.VMEM((frames * slab_x * slab_y, slab_z), jnp.float32)],
        compiler_params=pltpu.CompilerParams(vmem_limit_bytes=VMEM_BYTES),
        cost_estimate=SMALL,
        name="faces",
    )(col, bold)


def panel_kernel(
    col_ref, first_ref, last_ref, low_ref, high_ref, edge_ref, corner_ref, gm_ref, out_ref,
    planes, scored,
):
    slab_y, frames, slab_z = first_ref.shape
    slab_x = edge_ref.shape[0]

    def along_x(before, here, after):
        return SIDE * before + CENTRE * here + SIDE * after

    for y in range(slab_y):
        layers = [ref[y].astype(jnp.float32) for ref in (low_ref, first_ref, last_ref, high_ref)]
        for x in range(slab_x):
            planes[x, y + 1] = along_x(*layers[x : x + 3])
    edges = [corner_ref[0], edge_ref[0], edge_ref[1], corner_ref[1]]
    edges = [edge.astype(jnp.float32) for edge in edges]
    for x in range(slab_x):
        edge = along_x(*edges[x : x + 3])
        planes[x, 0] = jnp.where(col_ref[0] == 0, 0.0, edge)
        planes[x, slab_y + 1] = jnp.where(col_ref[0] == 0, edge, 0.0)

    lane = lax.broadcasted_iota(jnp.int32, (frames, slab_z), 1)
    for x in range(slab_x):
        for y in range(slab_y):
            part = along_x(planes[x, y], planes[x, y + 1], planes[x, y + 2])
            before = jnp.where(lane == 0, 0.0, pltpu.roll(part, 1, 1))
            after = jnp.where(lane == slab_z - 1, 0.0, pltpu.roll(part, slab_z - 1, 1))
            smooth = along_x(before, part, after)
            centred = smooth - jnp.mean(smooth, axis=0, keepdims=True)
            spread = jnp.mean(centred * centred, axis=0, keepdims=True)
            value = centred * lax.rsqrt((spread + 1e-05) * frames)
            start = (x * slab_y + y) * slab_z
            scored[:, start : start + slab_z] = value.astype(jnp.bfloat16)

    voxels = slab_x * slab_y * slab_z
    rows = gm_ref.shape[1]
    step = 2 * BLOCK
    for start in range(0, rows, step):
        wanted = gm_ref[:, start : start + step]
        voxel = lax.broadcasted_iota(jnp.int32, (voxels, step), 0)
        chosen = jnp.where(voxel == wanted, 1.0, 0.0).astype(jnp.bfloat16)
        picked = jnp.dot(scored[...], chosen, preferred_element_type=jnp.float32)
        out_ref[:, start : start + step] = picked.astype(jnp.bfloat16)


def make_panel(col, first, last, low, high, edge, corner, gm):
    slab_y, frames, slab_z = first.shape
    slab_x = edge.shape[0]
    rows = gm.shape[1]
    voxels = slab_x * slab_y * slab_z
    whole = lambda array: pl.BlockSpec(array.shape, lambda _: (0,) * array.ndim)
    operands = (first, last, low, high, edge, corner, gm)
    return pl.pallas_call(
        panel_kernel,
        grid=(1,),
        in_specs=[pl.BlockSpec(memory_space=pltpu.SMEM)] + [whole(value) for value in operands],
        out_specs=pl.BlockSpec((frames, rows), lambda _: (0, 0)),
        out_shape=jax.ShapeDtypeStruct((frames, rows), jnp.bfloat16),
        scratch_shapes=[
            pltpu.VMEM((slab_x, slab_y + 2, frames, slab_z), jnp.float32),
            pltpu.VMEM((frames, voxels), jnp.bfloat16),
        ],
        compiler_params=pltpu.CompilerParams(vmem_limit_bytes=VMEM_BYTES),
        cost_estimate=SMALL,
        name="blur_score_pick",
    )(col, *operands)


def tiles_kernel(place_ref, present_ref, *refs, sources):
    parts = refs[:sources]
    out_ref, rows_ref, held, sems = refs[-4:]
    block = pl.program_id(0)
    slots = out_ref.shape[1]
    blocks_each = held.shape[2] // BLOCK

    @pl.when(block == 0)
    def _():
        copies, first = [], 0
        for n, part in enumerate(parts):
            target = held.at[pl.ds(first, part.shape[0])]
            copies.append(pltpu.make_async_copy(part, target, sems.at[n]))
            copies[-1].start()
            first += part.shape[0]
        for copy in copies:
            copy.wait()

    own = held[0, :, pl.ds(pl.multiple_of(block * BLOCK, BLOCK), BLOCK)].T
    rows_ref[...] = own

    def partner(slot):
        place = place_ref[block * slots + slot]
        start = pl.multiple_of(lax.rem(place, blocks_each) * BLOCK, BLOCK)
        return held[place // blocks_each, :, pl.ds(start, BLOCK)]

    for slot in range(0, slots, 2):
        pair = jnp.concatenate([partner(slot), partner(slot + 1)], axis=1)
        both = jnp.dot(own, pair, preferred_element_type=jnp.float32)
        for n in range(2):
            keep = present_ref[block * slots + slot + n] != 0
            tile = both[:, n * BLOCK : (n + 1) * BLOCK]
            out_ref[0, slot + n, 0] = jnp.where(keep, tile, 0.0).astype(jnp.bfloat16)


def make_tiles(window, windows, place, present, sources, earlier):
    frames, rows = sources[0].shape[1:]
    total = sum(value.shape[0] for value in sources)
    blocks = rows // BLOCK
    slots = place.shape[0] // blocks
    count = len(sources)
    anywhere = pl.BlockSpec(memory_space=pl.ANY)
    operands = list(sources) + ([] if earlier is None else [earlier])
    return pl.pallas_call(
        functools.partial(tiles_kernel, sources=count),
        grid_spec=pltpu.PrefetchScalarGridSpec(
            num_scalar_prefetch=2,
            grid=(blocks,),
            in_specs=[anywhere] * len(operands),
            out_specs=[
                pl.BlockSpec(
                    (1, slots, 1, BLOCK, BLOCK), lambda i, *_: (i, 0, window, 0, 0)
                ),
                pl.BlockSpec((BLOCK, frames), lambda i, *_: (i, 0)),
            ],
            scratch_shapes=[
                pltpu.VMEM((total, frames, rows), jnp.bfloat16),
                pltpu.SemaphoreType.DMA((count,)),
            ],
        ),
        out_shape=[
            jax.ShapeDtypeStruct((blocks, slots, windows, BLOCK, BLOCK), jnp.bfloat16),
            jax.ShapeDtypeStruct((rows, frames), jnp.bfloat16),
        ],
        input_output_aliases={} if earlier is None else {2 + count: 0},
        compiler_params=pltpu.CompilerParams(vmem_limit_bytes=VMEM_BYTES),
        cost_estimate=SMALL,
        name="tiles",
    )(place, present, *operands)


def late_kernel(
    order_ref, count_ref, place_ref, rows_ref, near_ref, far_ref, earlier_ref, out_ref,
    held, tiles, sems, *, window, group,
):
    blocks, slots = out_ref.shape[:2]
    held[0] = near_ref[...]
    held[1] = far_ref[...]

    def copy(entry):
        slot = order_ref[entry]
        target = out_ref.at[slot // slots, lax.rem(slot, slots), window]
        return pltpu.make_async_copy(tiles.at[entry], target, sems.at[entry])

    def some(step, carry):
        for n in range(group):
            entry = step * group + n
            slot = order_ref[entry]
            place = place_ref[slot]
            start = pl.multiple_of(lax.rem(place, blocks) * BLOCK, BLOCK)
            rows_start = pl.multiple_of(slot // slots * BLOCK, BLOCK)
            tile = jnp.dot(
                rows_ref[pl.ds(rows_start, BLOCK), :],
                held[place // blocks, :, pl.ds(start, BLOCK)],
                preferred_element_type=jnp.float32,
            )
            tiles[entry] = tile.astype(jnp.bfloat16)
        for n in range(group):
            entry = step * group + n

            @pl.when(entry < count_ref[0])
            def _():
                copy(entry).start()

        return carry

    lax.fori_loop(0, (count_ref[0] + group - 1) // group, some, 0)

    def finish(entry, carry):
        copy(entry).wait()
        return carry

    lax.fori_loop(0, count_ref[0], finish, 0)


def make_late(window, order, count, place, own, near, far, earlier):
    rows, frames = own.shape
    total = order.shape[0]
    mine = pl.BlockSpec((rows, frames), lambda *_: (0, 0))
    whole = pl.BlockSpec((frames, rows), lambda *_: (0, 0))
    anywhere = pl.BlockSpec(memory_space=pl.ANY)
    return pl.pallas_call(
        functools.partial(late_kernel, window=window, group=8),
        grid_spec=pltpu.PrefetchScalarGridSpec(
            num_scalar_prefetch=3,
            grid=(1,),
            in_specs=[mine, whole, whole, anywhere],
            out_specs=anywhere,
            scratch_shapes=[
                pltpu.VMEM((2, frames, rows), jnp.bfloat16),
                pltpu.VMEM((total, BLOCK, BLOCK), jnp.bfloat16),
                pltpu.SemaphoreType.DMA((total,)),
            ],
        ),
        out_shape=jax.ShapeDtypeStruct(earlier.shape, earlier.dtype),
        input_output_aliases={6: 0},
        compiler_params=pltpu.CompilerParams(vmem_limit_bytes=VMEM_BYTES),
        cost_estimate=SMALL,
        name="late_tiles",
    )(order, count, place, own, near, far, earlier)


def after(value, *earlier):
    return lax.optimization_barrier((value,) + earlier)[0]


def on_device(bold, gm_index, partners):
    row_total = lax.axis_size("row")
    col_total = lax.axis_size("col")
    row = lax.axis_index("row")
    col = lax.axis_index("col")
    even = row % 2 == 0

    def other_col(value):
        return lax.ppermute(value, "col", [(0, 1), (1, 0)])

    one_up = [(i, i + 1) for i in range(row_total - 1)]
    one_down = [(i + 1, i) for i in range(row_total - 1)]
    ahead = [((i + 2 * (-1) ** i) % row_total, i) for i in range(row_total)]
    behind = [(i, source) for source, i in ahead]
    in_pair = [(i, i ^ 1) for i in range(row_total)]

    gm = gm_index.reshape(1, -1)
    col_arg = col.reshape(1).astype(jnp.int32)

    blocks, slots = partners.shape
    ids = jnp.maximum(partners, 0)
    slab = ids // blocks
    hop = (slab // col_total - row + 2 + row_total) % row_total
    kind = jnp.where((hop == 1) == even, 4, 3)
    kind = jnp.where(hop == 2, 0, jnp.where((hop == 0) | (hop >= 4), 2 - (even == (hop >= 4)), kind))
    away = (slab % col_total != col).astype(jnp.int32)
    within = ids % blocks
    present = partners >= 0
    late = present & (kind == 4)
    early = present & (kind != 4)
    early_place = jnp.where(early, (kind // 2 * 4 + away * 2 + kind % 2) * blocks + within, 0)
    late_place = jnp.where(late, away * blocks + within, 0)
    early, late = early.reshape(-1).astype(jnp.int32), late.reshape(-1)
    early_place = early_place.reshape(-1).astype(jnp.int32)
    late_place = late_place.reshape(-1).astype(jnp.int32)
    entries = jnp.arange(blocks * slots, dtype=jnp.int32)
    rank = jnp.sum((entries[None, :] < entries[:, None]) & late[None, :], axis=1)
    order = jnp.sum(
        jnp.where(late[None, :] & (rank[None, :] == entries[:, None]), entries[None, :], 0), axis=1
    ).astype(jnp.int32)
    count = jnp.sum(late).astype(jnp.int32).reshape(1)

    def halo(first, last):
        return lax.ppermute(last, "row", one_up), lax.ppermute(first, "row", one_down)

    def halves(*parts):
        near = jnp.stack(parts, 0)
        return [near, other_col(near)]

    def corner_of(low, high):
        return other_col(
            jnp.stack([jnp.where(col == 0, part[-1], part[0]) for part in (low, high)], 0)
        )

    windows = bold.shape[0]
    first_0, last_0, face_0 = make_faces(0, col_arg, bold)
    low_0, high_0 = halo(first_0, last_0)
    edge_0 = other_col(face_0)
    first_1, last_1, face_1 = make_faces(1, col_arg, after(bold, edge_0))
    edge_1 = other_col(face_1)
    corner_0 = corner_of(low_0, high_0)
    first_1, last_1 = after(first_1, low_0, high_0, edge_1), after(last_1, low_0, high_0, edge_1)
    low_1, high_1 = halo(first_1, last_1)
    own_0 = make_panel(col_arg, first_0, last_0, low_0, high_0, edge_0, corner_0, gm)
    ahead_0 = lax.ppermute(own_0, "row", ahead)
    behind_0 = lax.ppermute(own_0, "row", behind)
    low_1, high_1 = after(low_1, own_0), after(high_1, own_0)
    pair_0 = lax.ppermute(after(own_0, low_1, high_1), "row", in_pair)
    corner_1 = corner_of(low_1, high_1)
    own_1 = make_panel(col_arg, first_1, last_1, low_1, high_1, edge_1, corner_1, gm)
    ahead_0, behind_0 = after(ahead_0, own_1), after(behind_0, own_1)
    ahead_1 = lax.ppermute(own_1, "row", ahead)
    rest_0 = lax.ppermute(ahead_0, "row", in_pair)
    pair_1 = lax.ppermute(own_1, "row", in_pair)
    sources = halves(own_0, ahead_0) + halves(behind_0, pair_0)
    out, rows_0 = make_tiles(0, windows, early_place, early, sources, None)
    behind_1 = lax.ppermute(after(own_1, ahead_1), "row", behind)
    rest_1 = lax.ppermute(after(ahead_1, rest_0), "row", in_pair)
    behind_1, rest_0 = after(behind_1, out), after(rest_0, out)
    out = make_late(0, order, count, late_place, rows_0, rest_0, other_col(rest_0), out)
    sources = halves(own_1, ahead_1) + halves(behind_1, pair_1)
    out, rows_1 = make_tiles(1, windows, early_place, early, sources, out)
    rest_1 = after(rest_1, out)
    return make_late(1, order, count, late_place, rows_1, rest_1, other_col(rest_1), out)


def solution(mesh):
    in_specs = (P("subj", None, "row", "col", None), P(("row", "col")), P(("row", "col"), None))
    out_specs = P(("row", "col"), None, "subj", None, None)
    return jax.shard_map(
        on_device, mesh=mesh, in_specs=in_specs, out_specs=out_specs, check_vma=False
    )
```

time: 146 us -> 127 us (0.87); the launches traced: 143 us -> 126 us
  waiting for transfers between devices: 76.9 us -> 46.4 us
  starting transfers between devices: 25.1 us -> 35.3 us
  Pallas kernels: 26 us -> 35.1 us
  local copies, waits for them, and re-layouts: 12.8 us -> 4.48 us
  other arithmetic: 1.98 us -> 4.83 us
    ppermute x12, waiting for transfers between devices: 76.2 us -> 37.4 us  [the longest x2 28 us: halo(): lax.ppermute(last, 'row', one_up)]
    pallas_call x0 -> x4, Pallas kernels: none -> 12.6 us  [the longest x2 10.6 us: make_late(): pl.pallas_call(functools.partial(late_kernel, window=window, group=8), gr...]
    ppermute x12, starting transfers between devices: 22.8 us -> 33.6 us  [the longest x2 9.95 us: halo(): lax.ppermute(last, 'row', one_up)]
    ppermute x13 -> x10, waiting for transfers between devices: 0.67 us -> 8.97 us  [other_col(): return lax.ppermute(value, 'col', [(0, 1), (1, 0)])]
    another operation x2 -> x6, other arithmetic: 0.03 us -> 3.87 us  [the longest x4 3.83 us: halves(): near = jnp.stack(parts, 0)]
    slice x2 -> x0, local copies, waits for them, and re-layouts: 3.53 us -> none  [the longest x1 2.85 us: on_device(): high = shift_row(bold[window, :, 0], down)]
    gather x2 -> x0, local copies, waits for them, and re-layouts: 2.45 us -> none  [the longest x1 1.23 us: on_device(): jnp.array([1, 4, 0, 3, 2], jnp.int32)[jnp.minimum(distance, 4)]]
    ppermute x4 -> x0, local copies, waits for them, and re-layouts: 2.42 us -> none  [shift_row(): return lax.ppermute(value, 'row', pairs)]
  transfers between devices with their start and end apart: 25 -> 22, of which waited for: 8 -> 10; matrix products, arithmetic and copies ran while one was open for 6% -> 4% of each run, Pallas kernels for 9% -> 23%
where the time goes in v2:
time: 127 us; the launch traced here: 126 us
  waiting for transfers between devices  46.4 us (37%)
  starting transfers between devices  35.3 us (28%)
  Pallas kernels  35.1 us (28%)
  other arithmetic  4.83 us (4%)
  local copies, waits for them, and re-layouts  4.48 us (4%)
    ppermute x2, waiting for transfers between devices, halo(): lax.ppermute(last, 'row', one_up)  28 us
    pallas_call x2, Pallas kernels, make_tiles(): pl.pallas_call(functools.partial(tiles_kernel, sources=count), grid_spec=...  15.1 us
    pallas_call x2, Pallas kernels, make_late(): pl.pallas_call(functools.partial(late_kernel, window=window, group=8), gr...  10.6 us
    ppermute x2, starting transfers between devices, halo(): lax.ppermute(last, 'row', one_up)  9.95 us
    ppermute x10, waiting for transfers between devices, other_col(): return lax.ppermute(value, 'col', [(0, 1), (1, 0)])  8.97 us
    ppermute x1, waiting for transfers between devices, on_device(): ahead_1 = lax.ppermute(own_1, 'row', ahead)  8.14 us
    pallas_call x2, Pallas kernels, make_panel(): pl.pallas_call(panel_kernel, grid=(1,), in_specs=[pl.BlockSpec(memory_spa...  7.32 us
    ppermute x1, starting transfers between devices, on_device(): ahead_1 = lax.ppermute(own_1, 'row', ahead)  6.64 us
  transfers between devices with their start and end apart: 22, of which 10 were waited for; matrix products, arithmetic and copies ran while one was open for 4% of the time, Pallas kernels for 23%

profile of v2, /device:TPU:0, one launch (start us, length us, event | category | flops | bytes accessed | tf_op | source)
XLA Modules:
  0.0 126.4 jit_solution(6796077762730082332)
XLA Ops:
  0.0 1.6 %copy-done = bf16[2,256,2,8,128]{4,3,2,1,0:T(8,128)(2,1)S(1)} copy-done((bf16[2,256,2,8,128]{4,3,2,1,0:T(8,128)(2,1)S(1)}, bf16[2,256,2,8,128]{4,3,2,1,0:T(8,128)(2,1)}, u32[]{:S(2)}) %copy-start) | copy-done | bytes 2097176
  2.6 4.9 %collective-permute-start.1 = (bf16[8,256,128]{2,1,0:T(8,128)(2,1)S(1)}, bf16[8,256,128]{2,1,0:T(8,128)(2,1)S(1)}, u32[]{:S(2)}, u32[]{:S(2)}) collective-permute-start(bf16[8,256,128]{2,1,0:T(8,128)(2,1)S(1)} %get-tuple-element.31.last_ref), channel_id=1, source_target_pairs={{0,2},{2,4},{4,6},{6,8},{8,10},{10,12},{12,14},{1,3},{3,5},{5,7},{... | collective-permute-start | bytes 1572872 | tf_op jit(solution)/shard_map/ppermute | solution.py:313
  8.9 1.3 %collective-permute-done.edge_ref = bf16[2,256,128]{2,1,0:T(8,128)(2,1)S(1)} collective-permute-done((bf16[2,256,128]{2,1,0:T(8,128)(2,1)S(1)}, bf16[2,256,128]{2,1,0:T(8,128)(2,1)S(1)}, u32[]{:S(2)}, u32[]{:S(2)}) %collective-permute-start) | collective-permute-done | bytes 131104 | tf_op jit(solution)/shard_map/ppermute | solution.py:278
  12.7 17.2 %collective-permute-done.1.low_ref = bf16[8,256,128]{2,1,0:T(8,128)(2,1)S(1)} collective-permute-done((bf16[8,256,128]{2,1,0:T(8,128)(2,1)S(1)}, bf16[8,256,128]{2,1,0:T(8,128)(2,1)S(1)}, u32[]{:S(2)}, u32[]{:S(2)}) %collective-permute-start.1) | collective-permute-done | bytes 524320 | tf_op jit(solution)/shard_map/ppermute | solution.py:313
  31.2 5.0 %collective-permute-start.4 = (bf16[8,256,128]{2,1,0:T(8,128)(2,1)S(1)}, bf16[8,256,128]{2,1,0:T(8,128)(2,1)S(1)}, u32[]{:S(2)}, u32[]{:S(2)}) collective-permute-start(bf16[8,256,128]{2,1,0:T(8,128)(2,1)S(1)} %get-tuple-element.36.last_ref), channel_id=1, source_target_pairs={{0,2},{2,4},{4,6},{6,8},{8,10},{10,12},{12,14},{1,3},{3,5},{5,7},{... | collective-permute-start | bytes 1572872 | tf_op jit(solution)/shard_map/ppermute | solution.py:313
  36.4 1.3 %collective-permute-done.5.corner_ref = bf16[2,256,128]{2,1,0:T(8,128)(2,1)S(1)} collective-permute-done((bf16[2,256,128]{2,1,0:T(8,128)(2,1)S(1)}, bf16[2,256,128]{2,1,0:T(8,128)(2,1)S(1)}, u32[]{:S(2)}, u32[]{:S(2)}) %collective-permute-start.5) | collective-permute-done | bytes 131104 | tf_op jit(solution)/shard_map/ppermute | solution.py:278
  38.4 3.2 %blur_score_pick.2 = bf16[256,1024]{1,0:T(8,128)(2,1)S(1)} custom-call(s32[1]{0:T(128)} %bitcast.1.col_ref, bf16[8,256,128]{2,1,0:T(8,128)(2,1)S(1)} %get-tuple-element.32.first_ref, bf16[8,256,128]{2,1,0:T(8,128)(2,1)S(1)} %get-tuple-element.31.last_ref, bf16[8,256,128]{2,1,0:T(8,128)(2,1)S(1)} %collective-permute-done.1.low_ref, ...), custom_call_target="tpu_custom_call" | custom-call | flops 1 | bytes 1 | tf_op jit(solution)/shard_map/blur_score_pick/pallas_call | solution.py:108
  41.7 3.0 %collective-permute-start.13 = (bf16[256,1024]{1,0:T(8,128)(2,1)S(1)}, bf16[256,1024]{1,0:T(8,128)(2,1)S(1)}, u32[]{:S(2)}, u32[]{:S(2)}) collective-permute-start(bf16[256,1024]{1,0:T(8,128)(2,1)S(1)} %blur_score_pick.2), channel_id=1, source_target_pairs={{0,4},{2,14},{4,8},{6,2},{8,12},{10,6},{12,0},{14,10},{1,5},{3,15}... | collective-permute-start | bytes 1572872 | tf_op jit(solution)/shard_map/ppermute | solution.py:335
  44.7 2.1 %collective-permute-start.11 = (bf16[256,1024]{1,0:T(8,128)(2,1)S(1)}, bf16[256,1024]{1,0:T(8,128)(2,1)}, u32[]{:S(2)}, u32[]{:S(2)}) collective-permute-start(bf16[256,1024]{1,0:T(8,128)(2,1)S(1)} %blur_score_pick.2), channel_id=1, source_target_pairs={{4,0},{14,2},{8,4},{2,6},{12,8},{6,10},{0,12},{10,14},{5,1},{15,3}... | collective-permute-start | bytes 1572872 | tf_op jit(solution)/shard_map/ppermute | solution.py:334
  46.8 10.8 %collective-permute-done.4.low_ref = bf16[8,256,128]{2,1,0:T(8,128)(2,1)S(1)} collective-permute-done((bf16[8,256,128]{2,1,0:T(8,128)(2,1)S(1)}, bf16[8,256,128]{2,1,0:T(8,128)(2,1)S(1)}, u32[]{:S(2)}, u32[]{:S(2)}) %collective-permute-start.4) | collective-permute-done | bytes 524320 | tf_op jit(solution)/shard_map/ppermute | solution.py:313
  57.6 2.5 %collective-permute-start.14 = (bf16[256,1024]{1,0:T(8,128)(2,1)S(1)}, bf16[256,1024]{1,0:T(8,128)(2,1)S(1)}, u32[]{:S(2)}, u32[]{:S(2)}) collective-permute-start(bf16[256,1024]{1,0:T(8,128)(2,1)S(1)} %blur_score_pick.2), channel_id=1, source_target_pairs={{0,2},{2,0},{4,6},{6,4},{8,10},{10,8},{12,14},{14,12},{1,3},{3,1},... | collective-permute-start | bytes 1572872 | tf_op jit(solution)/shard_map/ppermute | solution.py:337
  60.2 1.3 %collective-permute-done.7.corner_ref = bf16[2,256,128]{2,1,0:T(8,128)(2,1)S(1)} collective-permute-done((bf16[2,256,128]{2,1,0:T(8,128)(2,1)S(1)}, bf16[2,256,128]{2,1,0:T(8,128)(2,1)S(1)}, u32[]{:S(2)}, u32[]{:S(2)}) %collective-permute-start.7) | collective-permute-done | bytes 131104 | tf_op jit(solution)/shard_map/ppermute | solution.py:278
  61.5 4.1 %blur_score_pick.3 = bf16[256,1024]{1,0:T(8,128)(2,1)} custom-call(s32[1]{0:T(128)} %bitcast.1.col_ref, bf16[8,256,128]{2,1,0:T(8,128)(2,1)S(1)} %get-tuple-element.34.first_ref, bf16[8,256,128]{2,1,0:T(8,128)(2,1)S(1)} %get-tuple-element.36.last_ref, bf16[8,256,128]{2,1,0:T(8,128)(2,1)S(1)} %collective-permute-done.4.low_ref, ...), custom_call_target="tpu_custom_call" | custom-call | flops 1 | bytes 1 | tf_op jit(solution)/shard_map/blur_score_pick/pallas_call | solution.py:108
  65.6 6.6 %collective-permute-start.8 = (bf16[256,1024]{1,0:T(8,128)(2,1)}, bf16[256,1024]{1,0:T(8,128)(2,1)}, u32[]{:S(2)}, u32[]{:S(2)}) collective-permute-start(bf16[256,1024]{1,0:T(8,128)(2,1)} %blur_score_pick.3), channel_id=1, source_target_pairs={{4,0},{14,2},{8,4},{2,6},{12,8},{6,10},{0,12},{10,14},{5,1},{15,3}... | collective-permute-start | bytes 1572872 | tf_op jit(solution)/shard_map/ppermute | solution.py:341
  74.1 1.8 %collective-permute-start.16 = (bf16[256,1024]{1,0:T(8,128)(2,1)}, bf16[256,1024]{1,0:T(8,128)(2,1)}, u32[]{:S(2)}, u32[]{:S(2)}) collective-permute-start(bf16[256,1024]{1,0:T(8,128)(2,1)} %blur_score_pick.3), channel_id=1, source_target_pairs={{0,2},{2,0},{4,6},{6,4},{8,10},{10,8},{12,14},{14,12},{1,3},{3,1},... | collective-permute-start | bytes 1572872 | tf_op jit(solution)/shard_map/ppermute | solution.py:343
  75.9 8.1 %collective-permute-done.8 = bf16[256,1024]{1,0:T(8,128)(2,1)} collective-permute-done((bf16[256,1024]{1,0:T(8,128)(2,1)}, bf16[256,1024]{1,0:T(8,128)(2,1)}, u32[]{:S(2)}, u32[]{:S(2)}) %collective-permute-start.8) | collective-permute-done | bytes 524320 | tf_op jit(solution)/shard_map/ppermute | solution.py:341
  84.5 4.2 %collective-permute-start.18 = (bf16[256,1024]{1,0:T(8,128)(2,1)}, bf16[256,1024]{1,0:T(8,128)(2,1)}, u32[]{:S(2)}, u32[]{:S(2)}) collective-permute-start(bf16[256,1024]{1,0:T(8,128)(2,1)} %collective-permute-done.11), channel_id=1, source_target_pairs={{0,2},{2,0},{4,6},{6,4},{8,10},{10,8},{12,14},{14,12},{1,3},{3,1},... | collective-permute-start | bytes 1572872 | tf_op jit(solution)/shard_map/ppermute | solution.py:342
  90.2 7.7 %tiles.2 = (bf16[8,16,2,128,128]{4,3,2,1,0:T(8,128)(2,1)}, bf16[1024,256]{1,0:T(8,128)(2,1)S(1)}) custom-call(s32[128]{0:T(128)S(1)} %reshape.23.place_ref, s32[128]{0:T(128)S(1)} %reshape.26.present_ref, bf16[2,256,1024]{2,1,0:T(8,128)(2,1)S(1)} %pad_maximum_fusion.1.refs_0_, bf16[2,256,1024]{2,1,0:T(8,128)(2,1)} %collective-permute-done.12.refs_1_, ...), custom_call_target="tpu_custom_call" | custom-call | flops 1 | bytes 1 | tf_op jit(solution)/shard_map/tiles/pallas_call | solution.py:167
  98.7 1.3 %collective-permute-done.10 = bf16[256,1024]{1,0:T(8,128)(2,1)} collective-permute-done((bf16[256,1024]{1,0:T(8,128)(2,1)}, bf16[256,1024]{1,0:T(8,128)(2,1)}, u32[]{:S(2)}, u32[]{:S(2)}) %collective-permute-start.10) | collective-permute-done | bytes 524320 | tf_op jit(solution)/shard_map/ppermute | solution.py:346
  103.5 1.6 %collective-permute-done.19.far_ref = bf16[256,1024]{1,0:T(8,128)(2,1)} collective-permute-done((bf16[256,1024]{1,0:T(8,128)(2,1)}, bf16[256,1024]{1,0:T(8,128)(2,1)}, u32[]{:S(2)}, u32[]{:S(2)}) %collective-permute-start.19) | collective-permute-done | bytes 524320 | tf_op jit(solution)/shard_map/ppermute | solution.py:278
  106.2 5.4 %late_tiles.2.refs_4_ = bf16[8,16,2,128,128]{4,3,2,1,0:T(8,128)(2,1)} custom-call(s32[128]{0:T(128)S(1)} %select_reduce_fusion.order_ref, s32[1]{0:T(128)} %bitcast.count_ref, s32[128]{0:T(128)S(1)} %reshape.22.place_ref, bf16[1024,256]{1,0:T(8,128)(2,1)S(1)} %copy-done.2, ...), custom_call_target="tpu_custom_call", output_to_operand_aliasing={{}: (6, {})} | custom-call | flops 1 | bytes 1 | tf_op jit(solution)/shard_map/late_tiles/pallas_call | solution.py:245
  111.6 7.4 %tiles.3 = (bf16[8,16,2,128,128]{4,3,2,1,0:T(8,128)(2,1)}, bf16[1024,256]{1,0:T(8,128)(2,1)S(1)}) custom-call(s32[128]{0:T(128)S(1)} %reshape.23.place_ref, s32[128]{0:T(128)S(1)} %reshape.26.present_ref, bf16[2,256,1024]{2,1,0:T(8,128)(2,1)S(1)} %pad_maximum_fusion.refs_0_, ...), custom_call_target="tpu_custom_call", output_to_operand_aliasing={{0}: (6, {})} | custom-call | flops 1 | bytes 1 | tf_op jit(solution)/shard_map/tiles/pallas_call | solution.py:167
  119.1 2.1 %collective-permute-done.21.far_ref = bf16[256,1024]{1,0:T(8,128)(2,1)S(1)} collective-permute-done((bf16[256,1024]{1,0:T(8,128)(2,1)}, bf16[256,1024]{1,0:T(8,128)(2,1)S(1)}, u32[]{:S(2)}, u32[]{:S(2)}) %collective-permute-start.21) | collective-permute-done | bytes 524320 | tf_op jit(solution)/shard_map/ppermute | solution.py:278
  121.2 5.2 %late_tiles.3 = bf16[8,16,2,128,128]{4,3,2,1,0:T(8,128)(2,1)} custom-call(s32[128]{0:T(128)S(1)} %select_reduce_fusion.order_ref, s32[1]{0:T(128)} %bitcast.count_ref, s32[128]{0:T(128)S(1)} %reshape.22.place_ref, bf16[1024,256]{1,0:T(8,128)(2,1)S(1)} %get-tuple-element.47.rows_ref, ...), custom_call_target="tpu_custom_call", output_to_operand_aliasing={{}: (6, {})} | custom-call | flops 1 | bytes 1 | tf_op jit(solution)/shard_map/late_tiles/pallas_call | solution.py:245
  (58 shorter events, 16.1 us)
Async XLA Ops:
  0.0 61.5 %copy-start.4 = (s32[1024]{0:T(1024)S(1)}, s32[1024]{0:T(1024)}, u32[]{:S(2)}) copy-start(s32[1024]{0:T(1024)} %param.4) | copy-start | bytes 12292
  1.6 82.7 %copy-start.5 = (s32[8,16]{1,0:T(8,128)S(1)}, s32[8,16]{1,0:T(8,128)}, u32[]{:S(2)}) copy-start(s32[8,16]{1,0:T(8,128)} %param.5) | copy-start | bytes 1540
  2.6 27.3 %collective-permute-start.1 = (bf16[8,256,128]{2,1,0:T(8,128)(2,1)S(1)}, bf16[8,256,128]{2,1,0:T(8,128)(2,1)S(1)}, u32[]{:S(2)}, u32[]{:S(2)}) collective-permute-start(bf16[8,256,128]{2,1,0:T(8,128)(2,1)S(1)} %get-tuple-element.31.last_ref), channel_id=1, source_target_pairs={{0,2},{2,4},{4,6},{6,8},{8,10},{10,12},{12,14},{1,3},{3,5},{5,7},{... | collective-permute-start | bytes 1572872 | tf_op jit(solution)/shard_map/ppermute | solution.py:313
  7.6 22.4 %collective-permute-start.2 = (bf16[8,256,128]{2,1,0:T(8,128)(2,1)S(1)}, bf16[8,256,128]{2,1,0:T(8,128)(2,1)S(1)}, u32[]{:S(2)}, u32[]{:S(2)}) collective-permute-start(bf16[8,256,128]{2,1,0:T(8,128)(2,1)S(1)} %get-tuple-element.32.first_ref), channel_id=1, source_target_pairs={{2,0},{4,2},{6,4},{8,6},{10,8},{12,10},{14,12},{3,1},{5,3},{7,5},{... | collective-permute-start | bytes 1572872 | tf_op jit(solution)/shard_map/ppermute | solution.py:313
  8.9 1.4 %collective-permute-start = (bf16[2,256,128]{2,1,0:T(8,128)(2,1)S(1)}, bf16[2,256,128]{2,1,0:T(8,128)(2,1)S(1)}, u32[]{:S(2)}, u32[]{:S(2)}) collective-permute-start(bf16[2,256,128]{2,1,0:T(8,128)(2,1)S(1)} %get-tuple-element.28), channel_id=1, source_target_pairs={{0,1},{1,0},{2,3},{3,2},{4,5},{5,4},{6,7},{7,6},{8,9},{9,8},{10,11... | collective-permute-start | bytes 393224 | tf_op jit(solution)/shard_map/ppermute | solution.py:278
  11.3 1.4 %collective-permute-start.3 = (bf16[2,256,128]{2,1,0:T(8,128)(2,1)S(1)}, bf16[2,256,128]{2,1,0:T(8,128)(2,1)S(1)}, u32[]{:S(2)}, u32[]{:S(2)}) collective-permute-start(bf16[2,256,128]{2,1,0:T(8,128)(2,1)S(1)} %get-tuple-element.33), channel_id=1, source_target_pairs={{0,1},{1,0},{2,3},{3,2},{4,5},{5,4},{6,7},{7,6},{8,9},{9,8},{10,11... | collective-permute-start | bytes 393224 | tf_op jit(solution)/shard_map/ppermute | solution.py:278
  29.9 16.9 %collective-permute-start.6 = (bf16[8,256,128]{2,1,0:T(8,128)(2,1)S(1)}, bf16[8,256,128]{2,1,0:T(8,128)(2,1)S(1)}, u32[]{:S(2)}, u32[]{:S(2)}) collective-permute-start(bf16[8,256,128]{2,1,0:T(8,128)(2,1)S(1)} %get-tuple-element.34.first_ref), channel_id=1, source_target_pairs={{2,0},{4,2},{6,4},{8,6},{10,8},{12,10},{14,12},{3,1},{5,3},{7,5},{... | collective-permute-start | bytes 1572872 | tf_op jit(solution)/shard_map/ppermute | solution.py:313
  31.2 26.4 %collective-permute-start.4 = (bf16[8,256,128]{2,1,0:T(8,128)(2,1)S(1)}, bf16[8,256,128]{2,1,0:T(8,128)(2,1)S(1)}, u32[]{:S(2)}, u32[]{:S(2)}) collective-permute-start(bf16[8,256,128]{2,1,0:T(8,128)(2,1)S(1)} %get-tuple-element.36.last_ref), channel_id=1, source_target_pairs={{0,2},{2,4},{4,6},{6,8},{8,10},{10,12},{12,14},{1,3},{3,5},{5,7},{... | collective-permute-start | bytes 1572872 | tf_op jit(solution)/shard_map/ppermute | solution.py:313
  36.3 1.4 %collective-permute-start.5 = (bf16[2,256,128]{2,1,0:T(8,128)(2,1)S(1)}, bf16[2,256,128]{2,1,0:T(8,128)(2,1)S(1)}, u32[]{:S(2)}, u32[]{:S(2)}) collective-permute-start(bf16[2,256,128]{2,1,0:T(8,128)(2,1)S(1)} %pad_maximum_fusion.4), channel_id=1, source_target_pairs={{0,1},{1,0},{2,3},{3,2},{4,5},{5,4},{6,7},{7,6},{8,9},{9,8},{10,11... | collective-permute-start | bytes 393224 | tf_op jit(solution)/shard_map/ppermute | solution.py:278
  41.7 30.6 %collective-permute-start.13 = (bf16[256,1024]{1,0:T(8,128)(2,1)S(1)}, bf16[256,1024]{1,0:T(8,128)(2,1)S(1)}, u32[]{:S(2)}, u32[]{:S(2)}) collective-permute-start(bf16[256,1024]{1,0:T(8,128)(2,1)S(1)} %blur_score_pick.2), channel_id=1, source_target_pairs={{0,4},{2,14},{4,8},{6,2},{8,12},{10,6},{12,0},{14,10},{1,5},{3,15}... | collective-permute-start | bytes 1572872 | tf_op jit(solution)/shard_map/ppermute | solution.py:335
  44.7 27.6 %collective-permute-start.11 = (bf16[256,1024]{1,0:T(8,128)(2,1)S(1)}, bf16[256,1024]{1,0:T(8,128)(2,1)}, u32[]{:S(2)}, u32[]{:S(2)}) collective-permute-start(bf16[256,1024]{1,0:T(8,128)(2,1)S(1)} %blur_score_pick.2), channel_id=1, source_target_pairs={{4,0},{14,2},{8,4},{2,6},{12,8},{6,10},{0,12},{10,14},{5,1},{15,3}... | collective-permute-start | bytes 1572872 | tf_op jit(solution)/shard_map/ppermute | solution.py:334
  57.6 15.9 %collective-permute-start.14 = (bf16[256,1024]{1,0:T(8,128)(2,1)S(1)}, bf16[256,1024]{1,0:T(8,128)(2,1)S(1)}, u32[]{:S(2)}, u32[]{:S(2)}) collective-permute-start(bf16[256,1024]{1,0:T(8,128)(2,1)S(1)} %blur_score_pick.2), channel_id=1, source_target_pairs={{0,2},{2,0},{4,6},{6,4},{8,10},{10,8},{12,14},{14,12},{1,3},{3,1},... | collective-permute-start | bytes 1572872 | tf_op jit(solution)/shard_map/ppermute | solution.py:337
  60.1 1.4 %collective-permute-start.7 = (bf16[2,256,128]{2,1,0:T(8,128)(2,1)S(1)}, bf16[2,256,128]{2,1,0:T(8,128)(2,1)S(1)}, u32[]{:S(2)}, u32[]{:S(2)}) collective-permute-start(bf16[2,256,128]{2,1,0:T(8,128)(2,1)S(1)} %pad_maximum_fusion.5), channel_id=1, source_target_pairs={{0,1},{1,0},{2,3},{3,2},{4,5},{5,4},{6,7},{7,6},{8,9},{9,8},{10,11... | collective-permute-start | bytes 393224 | tf_op jit(solution)/shard_map/ppermute | solution.py:278
  65.6 18.5 %collective-permute-start.8 = (bf16[256,1024]{1,0:T(8,128)(2,1)}, bf16[256,1024]{1,0:T(8,128)(2,1)}, u32[]{:S(2)}, u32[]{:S(2)}) collective-permute-start(bf16[256,1024]{1,0:T(8,128)(2,1)} %blur_score_pick.3), channel_id=1, source_target_pairs={{4,0},{14,2},{8,4},{2,6},{12,8},{6,10},{0,12},{10,14},{5,1},{15,3}... | collective-permute-start | bytes 1572872 | tf_op jit(solution)/shard_map/ppermute | solution.py:341
  73.4 16.7 %collective-permute-start.12 = (bf16[2,256,1024]{2,1,0:T(8,128)(2,1)S(1)}, bf16[2,256,1024]{2,1,0:T(8,128)(2,1)}, u32[]{:S(2)}, u32[]{:S(2)}) collective-permute-start(bf16[2,256,1024]{2,1,0:T(8,128)(2,1)S(1)} %pad_maximum_fusion.1.refs_0_), channel_id=1, source_target_pairs={{0,1},{1,0},{2,3},{3,2},{4,5},{5,4},{6,7},{7,6},{8,9},{9,8},{10,11... | collective-permute-start | bytes 3145736 | tf_op jit(solution)/shard_map/ppermute | solution.py:278
  73.6 16.6 %collective-permute-start.15 = (bf16[2,256,1024]{2,1,0:T(8,128)(2,1)S(1)}, bf16[2,256,1024]{2,1,0:T(8,128)(2,1)}, u32[]{:S(2)}, u32[]{:S(2)}) collective-permute-start(bf16[2,256,1024]{2,1,0:T(8,128)(2,1)S(1)} %pad_maximum_fusion.2.refs_2_), channel_id=1, source_target_pairs={{0,1},{1,0},{2,3},{3,2},{4,5},{5,4},{6,7},{7,6},{8,9},{9,8},{10,11... | collective-permute-start | bytes 3145736 | tf_op jit(solution)/shard_map/ppermute | solution.py:278
  74.1 25.9 %collective-permute-start.16 = (bf16[256,1024]{1,0:T(8,128)(2,1)}, bf16[256,1024]{1,0:T(8,128)(2,1)}, u32[]{:S(2)}, u32[]{:S(2)}) collective-permute-start(bf16[256,1024]{1,0:T(8,128)(2,1)} %blur_score_pick.3), channel_id=1, source_target_pairs={{0,2},{2,0},{4,6},{6,4},{8,10},{10,8},{12,14},{14,12},{1,3},{3,1},... | collective-permute-start | bytes 1572872 | tf_op jit(solution)/shard_map/ppermute | solution.py:343
  84.0 16.0 %collective-permute-start.10 = (bf16[256,1024]{1,0:T(8,128)(2,1)}, bf16[256,1024]{1,0:T(8,128)(2,1)}, u32[]{:S(2)}, u32[]{:S(2)}) collective-permute-start(bf16[256,1024]{1,0:T(8,128)(2,1)} %blur_score_pick.3), channel_id=1, source_target_pairs={{0,4},{2,14},{4,8},{6,2},{8,12},{10,6},{12,0},{14,10},{1,5},{3,15}... | collective-permute-start | bytes 1572872 | tf_op jit(solution)/shard_map/ppermute | solution.py:346
  84.5 16.9 %collective-permute-start.18 = (bf16[256,1024]{1,0:T(8,128)(2,1)}, bf16[256,1024]{1,0:T(8,128)(2,1)}, u32[]{:S(2)}, u32[]{:S(2)}) collective-permute-start(bf16[256,1024]{1,0:T(8,128)(2,1)} %collective-permute-done.11), channel_id=1, source_target_pairs={{0,2},{2,0},{4,6},{6,4},{8,10},{10,8},{12,14},{14,12},{1,3},{3,1},... | collective-permute-start | bytes 1572872 | tf_op jit(solution)/shard_map/ppermute | solution.py:342
  90.1 21.5 %collective-permute-start.9 = (bf16[2,256,1024]{2,1,0:T(8,128)(2,1)S(1)}, bf16[2,256,1024]{2,1,0:T(8,128)(2,1)}, u32[]{:S(2)}, u32[]{:S(2)}) collective-permute-start(bf16[2,256,1024]{2,1,0:T(8,128)(2,1)S(1)} %pad_maximum_fusion.refs_0_), channel_id=1, source_target_pairs={{0,1},{1,0},{2,3},{3,2},{4,5},{5,4},{6,7},{7,6},{8,9},{9,8},{10,11... | collective-permute-start | bytes 3145736 | tf_op jit(solution)/shard_map/ppermute | solution.py:278
  101.4 10.2 %collective-permute-start.17 = (bf16[2,256,1024]{2,1,0:T(8,128)(2,1)S(1)}, bf16[2,256,1024]{2,1,0:T(8,128)(2,1)S(1)}, u32[]{:S(2)}, u32[]{:S(2)}) collective-permute-start(bf16[2,256,1024]{2,1,0:T(8,128)(2,1)S(1)} %pad_maximum_fusion.3.refs_2_), channel_id=1, source_target_pairs={{0,1},{1,0},{2,3},{3,2},{4,5},{5,4},{6,7},{7,6},{8,9},{9,8},{10,11... | collective-permute-start | bytes 3145736 | tf_op jit(solution)/shard_map/ppermute | solution.py:278
  101.4 3.7 %collective-permute-start.19 = (bf16[256,1024]{1,0:T(8,128)(2,1)}, bf16[256,1024]{1,0:T(8,128)(2,1)}, u32[]{:S(2)}, u32[]{:S(2)}) collective-permute-start(bf16[256,1024]{1,0:T(8,128)(2,1)} %collective-permute-done.18.near_ref), channel_id=1, source_target_pairs={{0,1},{1,0},{2,3},{3,2},{4,5},{5,4},{6,7},{7,6},{8,9},{9,8},{10,11... | collective-permute-start | bytes 1572872 | tf_op jit(solution)/shard_map/ppermute | solution.py:278
  101.9 17.1 %collective-permute-start.20 = (bf16[256,1024]{1,0:T(8,128)(2,1)}, bf16[256,1024]{1,0:T(8,128)(2,1)}, u32[]{:S(2)}, u32[]{:S(2)}) collective-permute-start(bf16[256,1024]{1,0:T(8,128)(2,1)} %collective-permute-done.8), channel_id=1, source_target_pairs={{0,2},{2,0},{4,6},{6,4},{8,10},{10,8},{12,14},{14,12},{1,3},{3,1},... | collective-permute-start | bytes 1572872 | tf_op jit(solution)/shard_map/ppermute | solution.py:347
  119.0 2.2 %collective-permute-start.21 = (bf16[256,1024]{1,0:T(8,128)(2,1)}, bf16[256,1024]{1,0:T(8,128)(2,1)S(1)}, u32[]{:S(2)}, u32[]{:S(2)}) collective-permute-start(bf16[256,1024]{1,0:T(8,128)(2,1)} %collective-permute-done.20.near_ref), channel_id=1, source_target_pairs={{0,1},{1,0},{2,3},{3,2},{4,5},{5,4},{6,7},{7,6},{8,9},{9,8},{10,11... | collective-permute-start | bytes 1572872 | tf_op jit(solution)/shard_map/ppermute | solution.py:278
  (4 other events, 4.2 us)

commit v3 on v2

--- a/solution.py
+++ b/solution.py
@@ -121,39 +121,43 @@
     )(col, *operands)
 
 
-def tiles_kernel(place_ref, present_ref, *refs, sources):
+def tiles_kernel(place_ref, present_ref, *refs, sources, window):
     parts = refs[:sources]
-    out_ref, rows_ref, held, sems = refs[-4:]
-    block = pl.program_id(0)
-    slots = out_ref.shape[1]
-    blocks_each = held.shape[2] // BLOCK
-
-    @pl.when(block == 0)
-    def _():
-        copies, first = [], 0
-        for n, part in enumerate(parts):
-            target = held.at[pl.ds(first, part.shape[0])]
-            copies.append(pltpu.make_async_copy(part, target, sems.at[n]))
-            copies[-1].start()
-            first += part.shape[0]
-        for copy in copies:
-            copy.wait()
-
-    own = held[0, :, pl.ds(pl.multiple_of(block * BLOCK, BLOCK), BLOCK)].T
-    rows_ref[...] = own
-
-    def partner(slot):
-        place = place_ref[block * slots + slot]
-        start = pl.multiple_of(lax.rem(place, blocks_each) * BLOCK, BLOCK)
-        return held[place // blocks_each, :, pl.ds(start, BLOCK)]
-
-    for slot in range(0, slots, 2):
-        pair = jnp.concatenate([partner(slot), partner(slot + 1)], axis=1)
-        both = jnp.dot(own, pair, preferred_element_type=jnp.float32)
-        for n in range(2):
-            keep = present_ref[block * slots + slot + n] != 0
-            tile = both[:, n * BLOCK : (n + 1) * BLOCK]
-            out_ref[0, slot + n, 0] = jnp.where(keep, tile, 0.0).astype(jnp.bfloat16)
+    out_ref, rows_ref, held, tiles, sems, out_sems = refs[-6:]
+    blocks, slots = out_ref.shape[:2]
+
+    loads, first = [], 0
+    for n, part in enumerate(parts):
+        target = held.at[pl.ds(first, part.shape[0])]
+        loads.append(pltpu.make_async_copy(part, target, sems.at[n]))
+        loads[-1].start()
+        first += part.shape[0]
+    for load in loads:
+        load.wait()
+
+    def partner(index):
+        place = place_ref[index]
+        start = pl.multiple_of(lax.rem(place, blocks) * BLOCK, BLOCK)
+        return held[lax.div(place, blocks), :, pl.ds(start, BLOCK)]
+
+    stores = []
+    for block in range(blocks):
+        own = held[0, :, block * BLOCK : (block + 1) * BLOCK].T
+        rows_ref[block * BLOCK : (block + 1) * BLOCK, :] = own
+        for slot in range(0, slots, 2):
+            index = block * slots + slot
+            pair = jnp.concatenate([partner(index), partner(index + 1)], axis=1)
+            both = jnp.dot(own, pair, preferred_element_type=jnp.float32)
+            for n in range(2):
+                tile = both[:, n * BLOCK : (n + 1) * BLOCK]
+                tile = jnp.where(present_ref[index + n] != 0, tile, 0.0)
+                tiles[block, slot + n] = tile.astype(jnp.bfloat16)
+        stores.append(
+            pltpu.make_async_copy(tiles.at[block], out_ref.at[block, :, window], out_sems.at[block])
+        )
+        stores[-1].start()
+    for store in stores:
+        store.wait()
 
 
 def make_tiles(window, windows, place, present, sources, earlier):
@@ -165,20 +169,17 @@
     anywhere = pl.BlockSpec(memory_space=pl.ANY)
     operands = list(sources) + ([] if earlier is None else [earlier])
     return pl.pallas_call(
-        functools.partial(tiles_kernel, sources=count),
+        functools.partial(tiles_kernel, sources=count, window=window),
         grid_spec=pltpu.PrefetchScalarGridSpec(
             num_scalar_prefetch=2,
-            grid=(blocks,),
+            grid=(1,),
             in_specs=[anywhere] * len(operands),
-            out_specs=[
-                pl.BlockSpec(
-                    (1, slots, 1, BLOCK, BLOCK), lambda i, *_: (i, 0, window, 0, 0)
-                ),
-                pl.BlockSpec((BLOCK, frames), lambda i, *_: (i, 0)),
-            ],
+            out_specs=[anywhere, pl.BlockSpec((rows, frames), lambda *_: (0, 0))],
             scratch_shapes=[
                 pltpu.VMEM((total, frames, rows), jnp.bfloat16),
+                pltpu.VMEM((blocks, slots, BLOCK, BLOCK), jnp.bfloat16),
                 pltpu.SemaphoreType.DMA((count,)),
+                pltpu.SemaphoreType.DMA((blocks,)),
             ],
         ),
         out_shape=[
@@ -193,12 +194,18 @@
 
 
 def late_kernel(
-    order_ref, count_ref, place_ref, rows_ref, near_ref, far_ref, earlier_ref, out_ref,
-    held, tiles, sems, *, window, group,
+    order_ref, count_ref, place_ref, rows_any, near_any, far_any, earlier_ref, out_ref,
+    rows_ref, held, tiles, sems, *, window, group,
 ):
     blocks, slots = out_ref.shape[:2]
-    held[0] = near_ref[...]
-    held[1] = far_ref[...]
+    loads = []
+    for n, (source, target) in enumerate(
+        ((rows_any, rows_ref), (near_any, held.at[0]), (far_any, held.at[1]))
+    ):
+        loads.append(pltpu.make_async_copy(source, target, sems.at[n]))
+        loads[-1].start()
+    for load in loads:
+        load.wait()
 
     def copy(entry):
         slot = order_ref[entry]
@@ -239,17 +246,16 @@
 def make_late(window, order, count, place, own, near, far, earlier):
     rows, frames = own.shape
     total = order.shape[0]
-    mine = pl.BlockSpec((rows, frames), lambda *_: (0, 0))
-    whole = pl.BlockSpec((frames, rows), lambda *_: (0, 0))
     anywhere = pl.BlockSpec(memory_space=pl.ANY)
     return pl.pallas_call(
-        functools.partial(late_kernel, window=window, group=8),
+        functools.partial(late_kernel, window=window, group=16),
         grid_spec=pltpu.PrefetchScalarGridSpec(
             num_scalar_prefetch=3,
             grid=(1,),
-            in_specs=[mine, whole, whole, anywhere],
+            in_specs=[anywhere] * 4,
             out_specs=anywhere,
             scratch_shapes=[
+                pltpu.VMEM((rows, frames), jnp.bfloat16),
                 pltpu.VMEM((2, frames, rows), jnp.bfloat16),
                 pltpu.VMEM((total, BLOCK, BLOCK), jnp.bfloat16),
                 pltpu.SemaphoreType.DMA((total,)),

time: 127 us -> 125 us (0.984)
  Pallas kernels: 35.1 us -> 31.3 us
  waiting for transfers between devices: 46.4 us -> 48.1 us
    pallas_call x4, Pallas kernels: 25.7 us -> 21.9 us  [the longest x2 11.4 us: make_tiles(): pl.pallas_call(functools.partial(tiles_kernel, sources=count, window=wind...]
    ppermute x1, waiting for transfers between devices: 1.31 us -> 3.18 us  [on_device(): behind_1 = lax.ppermute(after(own_1, ahead_1), 'row', behind)]
  transfers between devices with their start and end apart: 22 -> 22, of which waited for: 10 -> 10; matrix products, arithmetic and copies ran while one was open for 4% -> 4% of each run, Pallas kernels for 23% -> 20%
where the time goes in v3:
time: 125 us
  waiting for transfers between devices  48.1 us (38%)
  starting transfers between devices  35.5 us (28%)
  Pallas kernels  31.3 us (25%)
  other arithmetic  4.83 us (4%)
  local copies, waits for them, and re-layouts  4.48 us (4%)
    ppermute x2, waiting for transfers between devices, halo(): lax.ppermute(last, 'row', one_up)  28 us
    pallas_call x2, Pallas kernels, make_tiles(): pl.pallas_call(functools.partial(tiles_kernel, sources=count, window=wind...  11.4 us
    pallas_call x2, Pallas kernels, make_late(): pl.pallas_call(functools.partial(late_kernel, window=window, group=16), g...  10.5 us
    ppermute x2, starting transfers between devices, halo(): lax.ppermute(last, 'row', one_up)  9.95 us
    ppermute x10, waiting for transfers between devices, other_col(): return lax.ppermute(value, 'col', [(0, 1), (1, 0)])  8.83 us
    ppermute x1, waiting for transfers between devices, on_device(): ahead_1 = lax.ppermute(own_1, 'row', ahead)  8.13 us
    pallas_call x2, Pallas kernels, make_panel(): pl.pallas_call(panel_kernel, grid=(1,), in_specs=[pl.BlockSpec(memory_spa...  7.33 us
    ppermute x1, starting transfers between devices, on_device(): ahead_1 = lax.ppermute(own_1, 'row', ahead)  6.64 us
  transfers between devices with their start and end apart: 22, of which 10 were waited for; matrix products, arithmetic and copies ran while one was open for 4% of the time, Pallas kernels for 20%

profile of v3, /device:TPU:0, one launch (start us, length us, event | category | flops | bytes accessed | tf_op | source)
XLA Modules:
  0.0 124.6 jit_solution(8931608984779690903)
XLA Ops:
  0.0 1.6 %copy-done = bf16[2,256,2,8,128]{4,3,2,1,0:T(8,128)(2,1)S(1)} copy-done((bf16[2,256,2,8,128]{4,3,2,1,0:T(8,128)(2,1)S(1)}, bf16[2,256,2,8,128]{4,3,2,1,0:T(8,128)(2,1)}, u32[]{:S(2)}) %copy-start) | copy-done | bytes 2097176
  2.6 4.9 %collective-permute-start.1 = (bf16[8,256,128]{2,1,0:T(8,128)(2,1)S(1)}, bf16[8,256,128]{2,1,0:T(8,128)(2,1)S(1)}, u32[]{:S(2)}, u32[]{:S(2)}) collective-permute-start(bf16[8,256,128]{2,1,0:T(8,128)(2,1)S(1)} %get-tuple-element.31.last_ref), channel_id=1, source_target_pairs={{0,2},{2,4},{4,6},{6,8},{8,10},{10,12},{12,14},{1,3},{3,5},{5,7},{... | collective-permute-start | bytes 1572872 | tf_op jit(solution)/shard_map/ppermute | solution.py:319
  8.9 1.3 %collective-permute-done.edge_ref = bf16[2,256,128]{2,1,0:T(8,128)(2,1)S(1)} collective-permute-done((bf16[2,256,128]{2,1,0:T(8,128)(2,1)S(1)}, bf16[2,256,128]{2,1,0:T(8,128)(2,1)S(1)}, u32[]{:S(2)}, u32[]{:S(2)}) %collective-permute-start) | collective-permute-done | bytes 131104 | tf_op jit(solution)/shard_map/ppermute | solution.py:284
  12.7 17.2 %collective-permute-done.1.low_ref = bf16[8,256,128]{2,1,0:T(8,128)(2,1)S(1)} collective-permute-done((bf16[8,256,128]{2,1,0:T(8,128)(2,1)S(1)}, bf16[8,256,128]{2,1,0:T(8,128)(2,1)S(1)}, u32[]{:S(2)}, u32[]{:S(2)}) %collective-permute-start.1) | collective-permute-done | bytes 524320 | tf_op jit(solution)/shard_map/ppermute | solution.py:319
  31.2 5.0 %collective-permute-start.4 = (bf16[8,256,128]{2,1,0:T(8,128)(2,1)S(1)}, bf16[8,256,128]{2,1,0:T(8,128)(2,1)S(1)}, u32[]{:S(2)}, u32[]{:S(2)}) collective-permute-start(bf16[8,256,128]{2,1,0:T(8,128)(2,1)S(1)} %get-tuple-element.36.last_ref), channel_id=1, source_target_pairs={{0,2},{2,4},{4,6},{6,8},{8,10},{10,12},{12,14},{1,3},{3,5},{5,7},{... | collective-permute-start | bytes 1572872 | tf_op jit(solution)/shard_map/ppermute | solution.py:319
  36.4 1.3 %collective-permute-done.5.corner_ref = bf16[2,256,128]{2,1,0:T(8,128)(2,1)S(1)} collective-permute-done((bf16[2,256,128]{2,1,0:T(8,128)(2,1)S(1)}, bf16[2,256,128]{2,1,0:T(8,128)(2,1)S(1)}, u32[]{:S(2)}, u32[]{:S(2)}) %collective-permute-start.5) | collective-permute-done | bytes 131104 | tf_op jit(solution)/shard_map/ppermute | solution.py:284
  38.4 3.2 %blur_score_pick.2 = bf16[256,1024]{1,0:T(8,128)(2,1)S(1)} custom-call(s32[1]{0:T(128)} %bitcast.1.col_ref, bf16[8,256,128]{2,1,0:T(8,128)(2,1)S(1)} %get-tuple-element.32.first_ref, bf16[8,256,128]{2,1,0:T(8,128)(2,1)S(1)} %get-tuple-element.31.last_ref, bf16[8,256,128]{2,1,0:T(8,128)(2,1)S(1)} %collective-permute-done.1.low_ref, ...), custom_call_target="tpu_custom_call" | custom-call | flops 1 | bytes 1 | tf_op jit(solution)/shard_map/blur_score_pick/pallas_call | solution.py:108
  41.7 3.0 %collective-permute-start.13 = (bf16[256,1024]{1,0:T(8,128)(2,1)S(1)}, bf16[256,1024]{1,0:T(8,128)(2,1)S(1)}, u32[]{:S(2)}, u32[]{:S(2)}) collective-permute-start(bf16[256,1024]{1,0:T(8,128)(2,1)S(1)} %blur_score_pick.2), channel_id=1, source_target_pairs={{0,4},{2,14},{4,8},{6,2},{8,12},{10,6},{12,0},{14,10},{1,5},{3,15}... | collective-permute-start | bytes 1572872 | tf_op jit(solution)/shard_map/ppermute | solution.py:341
  44.7 2.1 %collective-permute-start.11 = (bf16[256,1024]{1,0:T(8,128)(2,1)S(1)}, bf16[256,1024]{1,0:T(8,128)(2,1)}, u32[]{:S(2)}, u32[]{:S(2)}) collective-permute-start(bf16[256,1024]{1,0:T(8,128)(2,1)S(1)} %blur_score_pick.2), channel_id=1, source_target_pairs={{4,0},{14,2},{8,4},{2,6},{12,8},{6,10},{0,12},{10,14},{5,1},{15,3}... | collective-permute-start | bytes 1572872 | tf_op jit(solution)/shard_map/ppermute | solution.py:340
  46.8 10.8 %collective-permute-done.4.low_ref = bf16[8,256,128]{2,1,0:T(8,128)(2,1)S(1)} collective-permute-done((bf16[8,256,128]{2,1,0:T(8,128)(2,1)S(1)}, bf16[8,256,128]{2,1,0:T(8,128)(2,1)S(1)}, u32[]{:S(2)}, u32[]{:S(2)}) %collective-permute-start.4) | collective-permute-done | bytes 524320 | tf_op jit(solution)/shard_map/ppermute | solution.py:319
  57.6 2.5 %collective-permute-start.14 = (bf16[256,1024]{1,0:T(8,128)(2,1)S(1)}, bf16[256,1024]{1,0:T(8,128)(2,1)S(1)}, u32[]{:S(2)}, u32[]{:S(2)}) collective-permute-start(bf16[256,1024]{1,0:T(8,128)(2,1)S(1)} %blur_score_pick.2), channel_id=1, source_target_pairs={{0,2},{2,0},{4,6},{6,4},{8,10},{10,8},{12,14},{14,12},{1,3},{3,1},... | collective-permute-start | bytes 1572872 | tf_op jit(solution)/shard_map/ppermute | solution.py:343
  60.2 1.3 %collective-permute-done.7.corner_ref = bf16[2,256,128]{2,1,0:T(8,128)(2,1)S(1)} collective-permute-done((bf16[2,256,128]{2,1,0:T(8,128)(2,1)S(1)}, bf16[2,256,128]{2,1,0:T(8,128)(2,1)S(1)}, u32[]{:S(2)}, u32[]{:S(2)}) %collective-permute-start.7) | collective-permute-done | bytes 131104 | tf_op jit(solution)/shard_map/ppermute | solution.py:284
  61.5 4.1 %blur_score_pick.3 = bf16[256,1024]{1,0:T(8,128)(2,1)} custom-call(s32[1]{0:T(128)} %bitcast.1.col_ref, bf16[8,256,128]{2,1,0:T(8,128)(2,1)S(1)} %get-tuple-element.34.first_ref, bf16[8,256,128]{2,1,0:T(8,128)(2,1)S(1)} %get-tuple-element.36.last_ref, bf16[8,256,128]{2,1,0:T(8,128)(2,1)S(1)} %collective-permute-done.4.low_ref, ...), custom_call_target="tpu_custom_call" | custom-call | flops 1 | bytes 1 | tf_op jit(solution)/shard_map/blur_score_pick/pallas_call | solution.py:108
  65.6 6.6 %collective-permute-start.8 = (bf16[256,1024]{1,0:T(8,128)(2,1)}, bf16[256,1024]{1,0:T(8,128)(2,1)}, u32[]{:S(2)}, u32[]{:S(2)}) collective-permute-start(bf16[256,1024]{1,0:T(8,128)(2,1)} %blur_score_pick.3), channel_id=1, source_target_pairs={{4,0},{14,2},{8,4},{2,6},{12,8},{6,10},{0,12},{10,14},{5,1},{15,3}... | collective-permute-start | bytes 1572872 | tf_op jit(solution)/shard_map/ppermute | solution.py:347
  74.1 1.8 %collective-permute-start.16 = (bf16[256,1024]{1,0:T(8,128)(2,1)}, bf16[256,1024]{1,0:T(8,128)(2,1)}, u32[]{:S(2)}, u32[]{:S(2)}) collective-permute-start(bf16[256,1024]{1,0:T(8,128)(2,1)} %blur_score_pick.3), channel_id=1, source_target_pairs={{0,2},{2,0},{4,6},{6,4},{8,10},{10,8},{12,14},{14,12},{1,3},{3,1},... | collective-permute-start | bytes 1572872 | tf_op jit(solution)/shard_map/ppermute | solution.py:349
  75.9 8.1 %collective-permute-done.8 = bf16[256,1024]{1,0:T(8,128)(2,1)} collective-permute-done((bf16[256,1024]{1,0:T(8,128)(2,1)}, bf16[256,1024]{1,0:T(8,128)(2,1)}, u32[]{:S(2)}, u32[]{:S(2)}) %collective-permute-start.8) | collective-permute-done | bytes 524320 | tf_op jit(solution)/shard_map/ppermute | solution.py:347
  84.6 4.2 %collective-permute-start.18 = (bf16[256,1024]{1,0:T(8,128)(2,1)}, bf16[256,1024]{1,0:T(8,128)(2,1)}, u32[]{:S(2)}, u32[]{:S(2)}) collective-permute-start(bf16[256,1024]{1,0:T(8,128)(2,1)} %collective-permute-done.11), channel_id=1, source_target_pairs={{0,2},{2,0},{4,6},{6,4},{8,10},{10,8},{12,14},{14,12},{1,3},{3,1},... | collective-permute-start | bytes 1572872 | tf_op jit(solution)/shard_map/ppermute | solution.py:348
  90.2 5.9 %tiles.2 = (bf16[8,16,2,128,128]{4,3,2,1,0:T(8,128)(2,1)}, bf16[1024,256]{1,0:T(8,128)(2,1)S(1)}) custom-call(s32[128]{0:T(128)S(1)} %reshape.23.place_ref, s32[128]{0:T(128)S(1)} %reshape.26.present_ref, bf16[2,256,1024]{2,1,0:T(8,128)(2,1)S(1)} %pad_maximum_fusion.1.refs_0_, bf16[2,256,1024]{2,1,0:T(8,128)(2,1)} %collective-permute-done.12.refs_1_, ...), custom_call_target="tpu_custom_call" | custom-call | flops 1 | bytes 1 | tf_op jit(solution)/shard_map/tiles/pallas_call | solution.py:171
  96.9 3.2 %collective-permute-done.10 = bf16[256,1024]{1,0:T(8,128)(2,1)} collective-permute-done((bf16[256,1024]{1,0:T(8,128)(2,1)}, bf16[256,1024]{1,0:T(8,128)(2,1)}, u32[]{:S(2)}, u32[]{:S(2)}) %collective-permute-start.10) | collective-permute-done | bytes 524320 | tf_op jit(solution)/shard_map/ppermute | solution.py:352
  103.5 1.6 %collective-permute-done.19.far_any = bf16[256,1024]{1,0:T(8,128)(2,1)} collective-permute-done((bf16[256,1024]{1,0:T(8,128)(2,1)}, bf16[256,1024]{1,0:T(8,128)(2,1)}, u32[]{:S(2)}, u32[]{:S(2)}) %collective-permute-start.19) | collective-permute-done | bytes 524320 | tf_op jit(solution)/shard_map/ppermute | solution.py:284
  106.2 5.3 %late_tiles.2.refs_4_ = bf16[8,16,2,128,128]{4,3,2,1,0:T(8,128)(2,1)} custom-call(s32[128]{0:T(128)S(1)} %select_reduce_fusion.order_ref, s32[1]{0:T(128)} %bitcast.count_ref, s32[128]{0:T(128)S(1)} %reshape.22.place_ref, bf16[1024,256]{1,0:T(8,128)(2,1)S(1)} %copy-done.2, ...), custom_call_target="tpu_custom_call", output_to_operand_aliasing={{}: (6, {})} | custom-call | flops 1 | bytes 1 | tf_op jit(solution)/shard_map/late_tiles/pallas_call | solution.py:250
  111.6 5.5 %tiles.3 = (bf16[8,16,2,128,128]{4,3,2,1,0:T(8,128)(2,1)}, bf16[1024,256]{1,0:T(8,128)(2,1)S(1)}) custom-call(s32[128]{0:T(128)S(1)} %reshape.23.place_ref, s32[128]{0:T(128)S(1)} %reshape.26.present_ref, bf16[2,256,1024]{2,1,0:T(8,128)(2,1)S(1)} %pad_maximum_fusion.refs_0_, ...), custom_call_target="tpu_custom_call", output_to_operand_aliasing={{0}: (6, {})} | custom-call | flops 1 | bytes 1 | tf_op jit(solution)/shard_map/tiles/pallas_call | solution.py:171
  117.3 2.0 %collective-permute-done.21.far_any = bf16[256,1024]{1,0:T(8,128)(2,1)S(1)} collective-permute-done((bf16[256,1024]{1,0:T(8,128)(2,1)}, bf16[256,1024]{1,0:T(8,128)(2,1)S(1)}, u32[]{:S(2)}, u32[]{:S(2)}) %collective-permute-start.21) | collective-permute-done | bytes 524320 | tf_op jit(solution)/shard_map/ppermute | solution.py:284
  119.3 5.2 %late_tiles.3 = bf16[8,16,2,128,128]{4,3,2,1,0:T(8,128)(2,1)} custom-call(s32[128]{0:T(128)S(1)} %select_reduce_fusion.order_ref, s32[1]{0:T(128)} %bitcast.count_ref, s32[128]{0:T(128)S(1)} %reshape.22.place_ref, bf16[1024,256]{1,0:T(8,128)(2,1)S(1)} %get-tuple-element.47.rows_any, ...), custom_call_target="tpu_custom_call", output_to_operand_aliasing={{}: (6, {})} | custom-call | flops 1 | bytes 1 | tf_op jit(solution)/shard_map/late_tiles/pallas_call | solution.py:250
  (58 shorter events, 16.3 us)
Async XLA Ops:
  0.0 61.5 %copy-start.4 = (s32[1024]{0:T(1024)S(1)}, s32[1024]{0:T(1024)}, u32[]{:S(2)}) copy-start(s32[1024]{0:T(1024)} %param.4) | copy-start | bytes 12292
  1.6 82.7 %copy-start.5 = (s32[8,16]{1,0:T(8,128)S(1)}, s32[8,16]{1,0:T(8,128)}, u32[]{:S(2)}) copy-start(s32[8,16]{1,0:T(8,128)} %param.5) | copy-start | bytes 1540
  2.6 27.3 %collective-permute-start.1 = (bf16[8,256,128]{2,1,0:T(8,128)(2,1)S(1)}, bf16[8,256,128]{2,1,0:T(8,128)(2,1)S(1)}, u32[]{:S(2)}, u32[]{:S(2)}) collective-permute-start(bf16[8,256,128]{2,1,0:T(8,128)(2,1)S(1)} %get-tuple-element.31.last_ref), channel_id=1, source_target_pairs={{0,2},{2,4},{4,6},{6,8},{8,10},{10,12},{12,14},{1,3},{3,5},{5,7},{... | collective-permute-start | bytes 1572872 | tf_op jit(solution)/shard_map/ppermute | solution.py:319
  7.6 22.4 %collective-permute-start.2 = (bf16[8,256,128]{2,1,0:T(8,128)(2,1)S(1)}, bf16[8,256,128]{2,1,0:T(8,128)(2,1)S(1)}, u32[]{:S(2)}, u32[]{:S(2)}) collective-permute-start(bf16[8,256,128]{2,1,0:T(8,128)(2,1)S(1)} %get-tuple-element.32.first_ref), channel_id=1, source_target_pairs={{2,0},{4,2},{6,4},{8,6},{10,8},{12,10},{14,12},{3,1},{5,3},{7,5},{... | collective-permute-start | bytes 1572872 | tf_op jit(solution)/shard_map/ppermute | solution.py:319
  8.9 1.4 %collective-permute-start = (bf16[2,256,128]{2,1,0:T(8,128)(2,1)S(1)}, bf16[2,256,128]{2,1,0:T(8,128)(2,1)S(1)}, u32[]{:S(2)}, u32[]{:S(2)}) collective-permute-start(bf16[2,256,128]{2,1,0:T(8,128)(2,1)S(1)} %get-tuple-element.28), channel_id=1, source_target_pairs={{0,1},{1,0},{2,3},{3,2},{4,5},{5,4},{6,7},{7,6},{8,9},{9,8},{10,11... | collective-permute-start | bytes 393224 | tf_op jit(solution)/shard_map/ppermute | solution.py:284
  11.3 1.4 %collective-permute-start.3 = (bf16[2,256,128]{2,1,0:T(8,128)(2,1)S(1)}, bf16[2,256,128]{2,1,0:T(8,128)(2,1)S(1)}, u32[]{:S(2)}, u32[]{:S(2)}) collective-permute-start(bf16[2,256,128]{2,1,0:T(8,128)(2,1)S(1)} %get-tuple-element.33), channel_id=1, source_target_pairs={{0,1},{1,0},{2,3},{3,2},{4,5},{5,4},{6,7},{7,6},{8,9},{9,8},{10,11... | collective-permute-start | bytes 393224 | tf_op jit(solution)/shard_map/ppermute | solution.py:284
  29.9 16.9 %collective-permute-start.6 = (bf16[8,256,128]{2,1,0:T(8,128)(2,1)S(1)}, bf16[8,256,128]{2,1,0:T(8,128)(2,1)S(1)}, u32[]{:S(2)}, u32[]{:S(2)}) collective-permute-start(bf16[8,256,128]{2,1,0:T(8,128)(2,1)S(1)} %get-tuple-element.34.first_ref), channel_id=1, source_target_pairs={{2,0},{4,2},{6,4},{8,6},{10,8},{12,10},{14,12},{3,1},{5,3},{7,5},{... | collective-permute-start | bytes 1572872 | tf_op jit(solution)/shard_map/ppermute | solution.py:319
  31.2 26.4 %collective-permute-start.4 = (bf16[8,256,128]{2,1,0:T(8,128)(2,1)S(1)}, bf16[8,256,128]{2,1,0:T(8,128)(2,1)S(1)}, u32[]{:S(2)}, u32[]{:S(2)}) collective-permute-start(bf16[8,256,128]{2,1,0:T(8,128)(2,1)S(1)} %get-tuple-element.36.last_ref), channel_id=1, source_target_pairs={{0,2},{2,4},{4,6},{6,8},{8,10},{10,12},{12,14},{1,3},{3,5},{5,7},{... | collective-permute-start | bytes 1572872 | tf_op jit(solution)/shard_map/ppermute | solution.py:319
  36.3 1.4 %collective-permute-start.5 = (bf16[2,256,128]{2,1,0:T(8,128)(2,1)S(1)}, bf16[2,256,128]{2,1,0:T(8,128)(2,1)S(1)}, u32[]{:S(2)}, u32[]{:S(2)}) collective-permute-start(bf16[2,256,128]{2,1,0:T(8,128)(2,1)S(1)} %pad_maximum_fusion.4), channel_id=1, source_target_pairs={{0,1},{1,0},{2,3},{3,2},{4,5},{5,4},{6,7},{7,6},{8,9},{9,8},{10,11... | collective-permute-start | bytes 393224 | tf_op jit(solution)/shard_map/ppermute | solution.py:284
  41.7 30.5 %collective-permute-start.13 = (bf16[256,1024]{1,0:T(8,128)(2,1)S(1)}, bf16[256,1024]{1,0:T(8,128)(2,1)S(1)}, u32[]{:S(2)}, u32[]{:S(2)}) collective-permute-start(bf16[256,1024]{1,0:T(8,128)(2,1)S(1)} %blur_score_pick.2), channel_id=1, source_target_pairs={{0,4},{2,14},{4,8},{6,2},{8,12},{10,6},{12,0},{14,10},{1,5},{3,15}... | collective-permute-start | bytes 1572872 | tf_op jit(solution)/shard_map/ppermute | solution.py:341
  44.7 27.6 %collective-permute-start.11 = (bf16[256,1024]{1,0:T(8,128)(2,1)S(1)}, bf16[256,1024]{1,0:T(8,128)(2,1)}, u32[]{:S(2)}, u32[]{:S(2)}) collective-permute-start(bf16[256,1024]{1,0:T(8,128)(2,1)S(1)} %blur_score_pick.2), channel_id=1, source_target_pairs={{4,0},{14,2},{8,4},{2,6},{12,8},{6,10},{0,12},{10,14},{5,1},{15,3}... | collective-permute-start | bytes 1572872 | tf_op jit(solution)/shard_map/ppermute | solution.py:340
  57.6 15.9 %collective-permute-start.14 = (bf16[256,1024]{1,0:T(8,128)(2,1)S(1)}, bf16[256,1024]{1,0:T(8,128)(2,1)S(1)}, u32[]{:S(2)}, u32[]{:S(2)}) collective-permute-start(bf16[256,1024]{1,0:T(8,128)(2,1)S(1)} %blur_score_pick.2), channel_id=1, source_target_pairs={{0,2},{2,0},{4,6},{6,4},{8,10},{10,8},{12,14},{14,12},{1,3},{3,1},... | collective-permute-start | bytes 1572872 | tf_op jit(solution)/shard_map/ppermute | solution.py:343
  60.1 1.4 %collective-permute-start.7 = (bf16[2,256,128]{2,1,0:T(8,128)(2,1)S(1)}, bf16[2,256,128]{2,1,0:T(8,128)(2,1)S(1)}, u32[]{:S(2)}, u32[]{:S(2)}) collective-permute-start(bf16[2,256,128]{2,1,0:T(8,128)(2,1)S(1)} %pad_maximum_fusion.5), channel_id=1, source_target_pairs={{0,1},{1,0},{2,3},{3,2},{4,5},{5,4},{6,7},{7,6},{8,9},{9,8},{10,11... | collective-permute-start | bytes 393224 | tf_op jit(solution)/shard_map/ppermute | solution.py:284
  65.6 18.4 %collective-permute-start.8 = (bf16[256,1024]{1,0:T(8,128)(2,1)}, bf16[256,1024]{1,0:T(8,128)(2,1)}, u32[]{:S(2)}, u32[]{:S(2)}) collective-permute-start(bf16[256,1024]{1,0:T(8,128)(2,1)} %blur_score_pick.3), channel_id=1, source_target_pairs={{4,0},{14,2},{8,4},{2,6},{12,8},{6,10},{0,12},{10,14},{5,1},{15,3}... | collective-permute-start | bytes 1572872 | tf_op jit(solution)/shard_map/ppermute | solution.py:347
  73.4 16.7 %collective-permute-start.12 = (bf16[2,256,1024]{2,1,0:T(8,128)(2,1)S(1)}, bf16[2,256,1024]{2,1,0:T(8,128)(2,1)}, u32[]{:S(2)}, u32[]{:S(2)}) collective-permute-start(bf16[2,256,1024]{2,1,0:T(8,128)(2,1)S(1)} %pad_maximum_fusion.1.refs_0_), channel_id=1, source_target_pairs={{0,1},{1,0},{2,3},{3,2},{4,5},{5,4},{6,7},{7,6},{8,9},{9,8},{10,11... | collective-permute-start | bytes 3145736 | tf_op jit(solution)/shard_map/ppermute | solution.py:284
  73.6 16.6 %collective-permute-start.15 = (bf16[2,256,1024]{2,1,0:T(8,128)(2,1)S(1)}, bf16[2,256,1024]{2,1,0:T(8,128)(2,1)}, u32[]{:S(2)}, u32[]{:S(2)}) collective-permute-start(bf16[2,256,1024]{2,1,0:T(8,128)(2,1)S(1)} %pad_maximum_fusion.2.refs_2_), channel_id=1, source_target_pairs={{0,1},{1,0},{2,3},{3,2},{4,5},{5,4},{6,7},{7,6},{8,9},{9,8},{10,11... | collective-permute-start | bytes 3145736 | tf_op jit(solution)/shard_map/ppermute | solution.py:284
  74.1 25.9 %collective-permute-start.16 = (bf16[256,1024]{1,0:T(8,128)(2,1)}, bf16[256,1024]{1,0:T(8,128)(2,1)}, u32[]{:S(2)}, u32[]{:S(2)}) collective-permute-start(bf16[256,1024]{1,0:T(8,128)(2,1)} %blur_score_pick.3), channel_id=1, source_target_pairs={{0,2},{2,0},{4,6},{6,4},{8,10},{10,8},{12,14},{14,12},{1,3},{3,1},... | collective-permute-start | bytes 1572872 | tf_op jit(solution)/shard_map/ppermute | solution.py:349
  84.0 16.0 %collective-permute-start.10 = (bf16[256,1024]{1,0:T(8,128)(2,1)}, bf16[256,1024]{1,0:T(8,128)(2,1)}, u32[]{:S(2)}, u32[]{:S(2)}) collective-permute-start(bf16[256,1024]{1,0:T(8,128)(2,1)} %blur_score_pick.3), channel_id=1, source_target_pairs={{0,4},{2,14},{4,8},{6,2},{8,12},{10,6},{12,0},{14,10},{1,5},{3,15}... | collective-permute-start | bytes 1572872 | tf_op jit(solution)/shard_map/ppermute | solution.py:352
  84.6 16.9 %collective-permute-start.18 = (bf16[256,1024]{1,0:T(8,128)(2,1)}, bf16[256,1024]{1,0:T(8,128)(2,1)}, u32[]{:S(2)}, u32[]{:S(2)}) collective-permute-start(bf16[256,1024]{1,0:T(8,128)(2,1)} %collective-permute-done.11), channel_id=1, source_target_pairs={{0,2},{2,0},{4,6},{6,4},{8,10},{10,8},{12,14},{14,12},{1,3},{3,1},... | collective-permute-start | bytes 1572872 | tf_op jit(solution)/shard_map/ppermute | solution.py:348
  90.1 21.5 %collective-permute-start.9 = (bf16[2,256,1024]{2,1,0:T(8,128)(2,1)S(1)}, bf16[2,256,1024]{2,1,0:T(8,128)(2,1)}, u32[]{:S(2)}, u32[]{:S(2)}) collective-permute-start(bf16[2,256,1024]{2,1,0:T(8,128)(2,1)S(1)} %pad_maximum_fusion.refs_0_), channel_id=1, source_target_pairs={{0,1},{1,0},{2,3},{3,2},{4,5},{5,4},{6,7},{7,6},{8,9},{9,8},{10,11... | collective-permute-start | bytes 3145736 | tf_op jit(solution)/shard_map/ppermute | solution.py:284
  101.3 10.2 %collective-permute-start.17 = (bf16[2,256,1024]{2,1,0:T(8,128)(2,1)S(1)}, bf16[2,256,1024]{2,1,0:T(8,128)(2,1)S(1)}, u32[]{:S(2)}, u32[]{:S(2)}) collective-permute-start(bf16[2,256,1024]{2,1,0:T(8,128)(2,1)S(1)} %pad_maximum_fusion.3.refs_2_), channel_id=1, source_target_pairs={{0,1},{1,0},{2,3},{3,2},{4,5},{5,4},{6,7},{7,6},{8,9},{9,8},{10,11... | collective-permute-start | bytes 3145736 | tf_op jit(solution)/shard_map/ppermute | solution.py:284
  101.4 3.7 %collective-permute-start.19 = (bf16[256,1024]{1,0:T(8,128)(2,1)}, bf16[256,1024]{1,0:T(8,128)(2,1)}, u32[]{:S(2)}, u32[]{:S(2)}) collective-permute-start(bf16[256,1024]{1,0:T(8,128)(2,1)} %collective-permute-done.18.near_any), channel_id=1, source_target_pairs={{0,1},{1,0},{2,3},{3,2},{4,5},{5,4},{6,7},{7,6},{8,9},{9,8},{10,11... | collective-permute-start | bytes 1572872 | tf_op jit(solution)/shard_map/ppermute | solution.py:284
  101.9 15.2 %collective-permute-start.20 = (bf16[256,1024]{1,0:T(8,128)(2,1)}, bf16[256,1024]{1,0:T(8,128)(2,1)}, u32[]{:S(2)}, u32[]{:S(2)}) collective-permute-start(bf16[256,1024]{1,0:T(8,128)(2,1)} %collective-permute-done.8), channel_id=1, source_target_pairs={{0,2},{2,0},{4,6},{6,4},{8,10},{10,8},{12,14},{14,12},{1,3},{3,1},... | collective-permute-start | bytes 1572872 | tf_op jit(solution)/shard_map/ppermute | solution.py:353
  117.1 2.2 %collective-permute-start.21 = (bf16[256,1024]{1,0:T(8,128)(2,1)}, bf16[256,1024]{1,0:T(8,128)(2,1)S(1)}, u32[]{:S(2)}, u32[]{:S(2)}) collective-permute-start(bf16[256,1024]{1,0:T(8,128)(2,1)} %collective-permute-done.20.near_any), channel_id=1, source_target_pairs={{0,1},{1,0},{2,3},{3,2},{4,5},{5,4},{6,7},{7,6},{8,9},{9,8},{10,11... | collective-permute-start | bytes 1572872 | tf_op jit(solution)/shard_map/ppermute | solution.py:284
  (4 other events, 4.2 us)

commit v4 on v3

--- a/solution.py
+++ b/solution.py
@@ -122,16 +122,18 @@
 
 
 def tiles_kernel(place_ref, present_ref, *refs, sources, window):
-    parts = refs[:sources]
-    out_ref, rows_ref, held, tiles, sems, out_sems = refs[-6:]
+    parts = refs[: len(sources)]
+    out_ref, held, tiles, sems, out_sems = refs[-5:]
     blocks, slots = out_ref.shape[:2]
 
-    loads, first = [], 0
-    for n, part in enumerate(parts):
-        target = held.at[pl.ds(first, part.shape[0])]
+    loads = []
+    for n, (part, (first, start)) in enumerate(zip(parts, sources)):
+        if len(part.shape) == 3:
+            target = held.at[pl.ds(first, part.shape[0])]
+        else:
+            target = held.at[first, pl.ds(start, part.shape[0])]
         loads.append(pltpu.make_async_copy(part, target, sems.at[n]))
         loads[-1].start()
-        first += part.shape[0]
     for load in loads:
         load.wait()
 
@@ -143,7 +145,6 @@
     stores = []
     for block in range(blocks):
         own = held[0, :, block * BLOCK : (block + 1) * BLOCK].T
-        rows_ref[block * BLOCK : (block + 1) * BLOCK, :] = own
         for slot in range(0, slots, 2):
             index = block * slots + slot
             pair = jnp.concatenate([partner(index), partner(index + 1)], axis=1)
@@ -161,112 +162,34 @@
 
 
 def make_tiles(window, windows, place, present, sources, earlier):
-    frames, rows = sources[0].shape[1:]
-    total = sum(value.shape[0] for value in sources)
+    _, frames, rows = sources[0][2].shape
     blocks = rows // BLOCK
     slots = place.shape[0] // blocks
     count = len(sources)
+    where = tuple(source[:2] for source in sources)
+    sources = [source[2] for source in sources]
     anywhere = pl.BlockSpec(memory_space=pl.ANY)
     operands = list(sources) + ([] if earlier is None else [earlier])
     return pl.pallas_call(
-        functools.partial(tiles_kernel, sources=count, window=window),
+        functools.partial(tiles_kernel, sources=where, window=window),
         grid_spec=pltpu.PrefetchScalarGridSpec(
             num_scalar_prefetch=2,
             grid=(1,),
             in_specs=[anywhere] * len(operands),
-            out_specs=[anywhere, pl.BlockSpec((rows, frames), lambda *_: (0, 0))],
+            out_specs=anywhere,
             scratch_shapes=[
-                pltpu.VMEM((total, frames, rows), jnp.bfloat16),
+                pltpu.VMEM((10, frames, rows), jnp.bfloat16),
                 pltpu.VMEM((blocks, slots, BLOCK, BLOCK), jnp.bfloat16),
                 pltpu.SemaphoreType.DMA((count,)),
                 pltpu.SemaphoreType.DMA((blocks,)),
             ],
         ),
-        out_shape=[
-            jax.ShapeDtypeStruct((blocks, slots, windows, BLOCK, BLOCK), jnp.bfloat16),
-            jax.ShapeDtypeStruct((rows, frames), jnp.bfloat16),
-        ],
+        out_shape=jax.ShapeDtypeStruct((blocks, slots, windows, BLOCK, BLOCK), jnp.bfloat16),
         input_output_aliases={} if earlier is None else {2 + count: 0},
         compiler_params=pltpu.CompilerParams(vmem_limit_bytes=VMEM_BYTES),
         cost_estimate=SMALL,
         name="tiles",
     )(place, present, *operands)
-
-
-def late_kernel(
-    order_ref, count_ref, place_ref, rows_any, near_any, far_any, earlier_ref, out_ref,
-    rows_ref, held, tiles, sems, *, window, group,
-):
-    blocks, slots = out_ref.shape[:2]
-    loads = []
-    for n, (source, target) in enumerate(
-        ((rows_any, rows_ref), (near_any, held.at[0]), (far_any, held.at[1]))
-    ):
-        loads.append(pltpu.make_async_copy(source, target, sems.at[n]))
-        loads[-1].start()
-    for load in loads:
-        load.wait()
-
-    def copy(entry):
-        slot = order_ref[entry]
-        target = out_ref.at[slot // slots, lax.rem(slot, slots), window]
-        return pltpu.make_async_copy(tiles.at[entry], target, sems.at[entry])
-
-    def some(step, carry):
-        for n in range(group):
-            entry = step * group + n
-            slot = order_ref[entry]
-            place = place_ref[slot]
-            start = pl.multiple_of(lax.rem(place, blocks) * BLOCK, BLOCK)
-            rows_start = pl.multiple_of(slot // slots * BLOCK, BLOCK)
-            tile = jnp.dot(
-                rows_ref[pl.ds(rows_start, BLOCK), :],
-                held[place // blocks, :, pl.ds(start, BLOCK)],
-                preferred_element_type=jnp.float32,
-            )
-            tiles[entry] = tile.astype(jnp.bfloat16)
-        for n in range(group):
-            entry = step * group + n
-
-            @pl.when(entry < count_ref[0])
-            def _():
-                copy(entry).start()
-
-        return carry
-
-    lax.fori_loop(0, (count_ref[0] + group - 1) // group, some, 0)
-
-    def finish(entry, carry):
-        copy(entry).wait()
-        return carry
-
-    lax.fori_loop(0, count_ref[0], finish, 0)
-
-
-def make_late(window, order, count, place, own, near, far, earlier):
-    rows, frames = own.shape
-    total = order.shape[0]
-    anywhere = pl.BlockSpec(memory_space=pl.ANY)
-    return pl.pallas_call(
-        functools.partial(late_kernel, window=window, group=16),
-        grid_spec=pltpu.PrefetchScalarGridSpec(
-            num_scalar_prefetch=3,
-            grid=(1,),
-            in_specs=[anywhere] * 4,
-            out_specs=anywhere,
-            scratch_shapes=[
-                pltpu.VMEM((rows, frames), jnp.bfloat16),
-                pltpu.VMEM((2, frames, rows), jnp.bfloat16),
-                pltpu.VMEM((total, BLOCK, BLOCK), jnp.bfloat16),
-                pltpu.SemaphoreType.DMA((total,)),
-            ],
-        ),
-        out_shape=jax.ShapeDtypeStruct(earlier.shape, earlier.dtype),
-        input_output_aliases={6: 0},
-        compiler_params=pltpu.CompilerParams(vmem_limit_bytes=VMEM_BYTES),
-        cost_estimate=SMALL,
-        name="late_tiles",
-    )(order, count, place, own, near, far, earlier)
 
 
 def after(value, *earlier):
@@ -301,26 +224,16 @@
     away = (slab % col_total != col).astype(jnp.int32)
     within = ids % blocks
     present = partners >= 0
-    late = present & (kind == 4)
-    early = present & (kind != 4)
-    early_place = jnp.where(early, (kind // 2 * 4 + away * 2 + kind % 2) * blocks + within, 0)
-    late_place = jnp.where(late, away * blocks + within, 0)
-    early, late = early.reshape(-1).astype(jnp.int32), late.reshape(-1)
-    early_place = early_place.reshape(-1).astype(jnp.int32)
-    late_place = late_place.reshape(-1).astype(jnp.int32)
-    entries = jnp.arange(blocks * slots, dtype=jnp.int32)
-    rank = jnp.sum((entries[None, :] < entries[:, None]) & late[None, :], axis=1)
-    order = jnp.sum(
-        jnp.where(late[None, :] & (rank[None, :] == entries[:, None]), entries[None, :], 0), axis=1
-    ).astype(jnp.int32)
-    count = jnp.sum(late).astype(jnp.int32).reshape(1)
+    part = jnp.where(kind < 2, kind + 2 * away, 2 * kind + away)
+    place = jnp.where(present, part * blocks + within, 0).reshape(-1).astype(jnp.int32)
+    present = present.reshape(-1).astype(jnp.int32)
 
     def halo(first, last):
         return lax.ppermute(last, "row", one_up), lax.ppermute(first, "row", one_down)
 
-    def halves(*parts):
+    def both(first, *parts):
         near = jnp.stack(parts, 0)
-        return [near, other_col(near)]
+        return [(first, 0, near), (first + len(parts), 0, other_col(near))]
 
     def corner_of(low, high):
         return other_col(
@@ -340,23 +253,26 @@
     ahead_0 = lax.ppermute(own_0, "row", ahead)
     behind_0 = lax.ppermute(own_0, "row", behind)
     low_1, high_1 = after(low_1, own_0), after(high_1, own_0)
+    ahead_0 = after(ahead_0, low_1, high_1)
     pair_0 = lax.ppermute(after(own_0, low_1, high_1), "row", in_pair)
+    rest_0 = lax.ppermute(ahead_0, "row", in_pair)
     corner_1 = corner_of(low_1, high_1)
     own_1 = make_panel(col_arg, first_1, last_1, low_1, high_1, edge_1, corner_1, gm)
-    ahead_0, behind_0 = after(ahead_0, own_1), after(behind_0, own_1)
     ahead_1 = lax.ppermute(own_1, "row", ahead)
-    rest_0 = lax.ppermute(ahead_0, "row", in_pair)
     pair_1 = lax.ppermute(own_1, "row", in_pair)
-    sources = halves(own_0, ahead_0) + halves(behind_0, pair_0)
-    out, rows_0 = make_tiles(0, windows, early_place, early, sources, None)
+    pair_0, rest_0 = after(pair_0, own_1), after(rest_0, own_1)
+    behind_0 = after(behind_0, own_1)
+    sources = both(0, own_0, ahead_0) + both(4, behind_0) + both(6, pair_0)
+    ahead_1 = after(ahead_1, rest_0, behind_0, pair_0)
     behind_1 = lax.ppermute(after(own_1, ahead_1), "row", behind)
-    rest_1 = lax.ppermute(after(ahead_1, rest_0), "row", in_pair)
-    behind_1, rest_0 = after(behind_1, out), after(rest_0, out)
-    out = make_late(0, order, count, late_place, rows_0, rest_0, other_col(rest_0), out)
-    sources = halves(own_1, ahead_1) + halves(behind_1, pair_1)
-    out, rows_1 = make_tiles(1, windows, early_place, early, sources, out)
-    rest_1 = after(rest_1, out)
-    return make_late(1, order, count, late_place, rows_1, rest_1, other_col(rest_1), out)
+    rest_1 = lax.ppermute(ahead_1, "row", in_pair)
+    swapped = [source[2] for source in sources]
+    pair_1 = after(pair_1, ahead_1, *swapped)
+    behind_1 = after(behind_1, pair_1)
+    out = make_tiles(0, windows, place, present, sources + both(8, rest_0), None)
+    sources = both(0, own_1, ahead_1) + both(4, behind_1) + both(6, pair_1)
+    rest_1 = after(rest_1, out, *(source[2] for source in sources))
+    return make_tiles(1, windows, place, present, sources + both(8, rest_1), out)
 
 
 def solution(mesh):

time: 125 us -> 122 us (0.976)
  Pallas kernels: 31.3 us -> 20.5 us
  local copies, waits for them, and re-layouts: 4.48 us -> 10.5 us
  starting transfers between devices: 35.5 us -> 40.5 us
  other arithmetic: 4.83 us -> 1.34 us
    pallas_call x4 -> x2, Pallas kernels: 21.9 us -> 11.9 us  [make_tiles(): pl.pallas_call(functools.partial(tiles_kernel, sources=where, window=wind...]
    ppermute x1, waiting for transfers between devices: 8.13 us -> 1.42 us  [on_device(): ahead_1 = lax.ppermute(own_1, 'row', ahead)]
    ppermute x1, waiting for transfers between devices: 0.01 us -> 6.54 us  [on_device(): pair_1 = lax.ppermute(own_1, 'row', in_pair)]
    ppermute x1, starting transfers between devices: 6.64 us -> 13 us  [on_device(): ahead_1 = lax.ppermute(own_1, 'row', ahead)]
    unnamed x12 -> x28, local copies, waits for them, and re-layouts: 4.15 us -> 10.3 us
    ppermute x1, waiting for transfers between devices: 0.01 us -> 4.59 us  [on_device(): rest_0 = lax.ppermute(ahead_0, 'row', in_pair)]
    ppermute x10 -> x12, waiting for transfers between devices: 8.83 us -> 5.65 us  [other_col(): return lax.ppermute(value, 'col', [(0, 1), (1, 0)])]
    ppermute x1, starting transfers between devices: 2.99 us -> 0.01 us  [on_device(): behind_0 = lax.ppermute(own_0, 'row', behind)]
  transfers between devices with their start and end apart: 22 -> 24, of which waited for: 10 -> 10; matrix products, arithmetic and copies ran while one was open for 4% -> 1% of each run, Pallas kernels for 20% -> 11%
where the time goes in v4:
time: 122 us; the launch traced here: 121 us
  waiting for transfers between devices  48.2 us (40%)
  starting transfers between devices  40.5 us (33%)
  Pallas kernels  20.5 us (17%)
  local copies, waits for them, and re-layouts  10.5 us (9%)
  other arithmetic  1.34 us (1%)
    ppermute x2, waiting for transfers between devices, halo(): lax.ppermute(last, 'row', one_up)  28 us
    ppermute x1, starting transfers between devices, on_device(): ahead_1 = lax.ppermute(own_1, 'row', ahead)  13 us
    pallas_call x2, Pallas kernels, make_tiles(): pl.pallas_call(functools.partial(tiles_kernel, sources=where, window=wind...  11.9 us
    unnamed x28, local copies, waits for them, and re-layouts  10.3 us
    ppermute x2, starting transfers between devices, halo(): lax.ppermute(last, 'row', one_up)  9.95 us
    ppermute x1, waiting for transfers between devices, on_device(): pair_1 = lax.ppermute(own_1, 'row', in_pair)  6.54 us
    pallas_call x2, Pallas kernels, make_panel(): pl.pallas_call(panel_kernel, grid=(1,), in_specs=[pl.BlockSpec(memory_spa...  6.51 us
    ppermute x12, waiting for transfers between devices, other_col(): return lax.ppermute(value, 'col', [(0, 1), (1, 0)])  5.65 us
  transfers between devices with their start and end apart: 24, of which 10 were waited for; matrix products, arithmetic and copies ran while one was open for 1% of the time, Pallas kernels for 11%

profile of v4, /device:TPU:0, one launch (start us, length us, event | category | flops | bytes accessed | tf_op | source)
XLA Modules:
  0.0 121.5 jit_solution(13835382406041424585)
XLA Ops:
  0.0 1.6 %copy-done = bf16[2,256,2,8,128]{4,3,2,1,0:T(8,128)(2,1)S(1)} copy-done((bf16[2,256,2,8,128]{4,3,2,1,0:T(8,128)(2,1)S(1)}, bf16[2,256,2,8,128]{4,3,2,1,0:T(8,128)(2,1)}, u32[]{:S(2)}) %copy-start) | copy-done | bytes 2097176
  2.6 4.9 %collective-permute-start.1 = (bf16[8,256,128]{2,1,0:T(8,128)(2,1)S(1)}, bf16[8,256,128]{2,1,0:T(8,128)(2,1)S(1)}, u32[]{:S(2)}, u32[]{:S(2)}) collective-permute-start(bf16[8,256,128]{2,1,0:T(8,128)(2,1)S(1)} %get-tuple-element.29.last_ref), channel_id=1, source_target_pairs={{0,2},{2,4},{4,6},{6,8},{8,10},{10,12},{12,14},{1,3},{3,5},{5,7},{... | collective-permute-start | bytes 1572872 | tf_op jit(solution)/shard_map/ppermute | solution.py:232
  7.6 1.3 %collective-permute-start.2 = (bf16[8,256,128]{2,1,0:T(8,128)(2,1)S(1)}, bf16[8,256,128]{2,1,0:T(8,128)(2,1)S(1)}, u32[]{:S(2)}, u32[]{:S(2)}) collective-permute-start(bf16[8,256,128]{2,1,0:T(8,128)(2,1)S(1)} %get-tuple-element.30.first_ref), channel_id=1, source_target_pairs={{2,0},{4,2},{6,4},{8,6},{10,8},{12,10},{14,12},{3,1},{5,3},{7,5},{... | collective-permute-start | bytes 1572872 | tf_op jit(solution)/shard_map/ppermute | solution.py:232
  8.9 1.3 %collective-permute-done.edge_ref = bf16[2,256,128]{2,1,0:T(8,128)(2,1)S(1)} collective-permute-done((bf16[2,256,128]{2,1,0:T(8,128)(2,1)S(1)}, bf16[2,256,128]{2,1,0:T(8,128)(2,1)S(1)}, u32[]{:S(2)}, u32[]{:S(2)}) %collective-permute-start) | collective-permute-done | bytes 131104 | tf_op jit(solution)/shard_map/ppermute | solution.py:207
  12.7 17.2 %collective-permute-done.1.low_ref = bf16[8,256,128]{2,1,0:T(8,128)(2,1)S(1)} collective-permute-done((bf16[8,256,128]{2,1,0:T(8,128)(2,1)S(1)}, bf16[8,256,128]{2,1,0:T(8,128)(2,1)S(1)}, u32[]{:S(2)}, u32[]{:S(2)}) %collective-permute-start.1) | collective-permute-done | bytes 524320 | tf_op jit(solution)/shard_map/ppermute | solution.py:232
  29.9 1.3 %collective-permute-start.6 = (bf16[8,256,128]{2,1,0:T(8,128)(2,1)S(1)}, bf16[8,256,128]{2,1,0:T(8,128)(2,1)S(1)}, u32[]{:S(2)}, u32[]{:S(2)}) collective-permute-start(bf16[8,256,128]{2,1,0:T(8,128)(2,1)S(1)} %get-tuple-element.32.first_ref), channel_id=1, source_target_pairs={{2,0},{4,2},{6,4},{8,6},{10,8},{12,10},{14,12},{3,1},{5,3},{7,5},{... | collective-permute-start | bytes 1572872 | tf_op jit(solution)/shard_map/ppermute | solution.py:232
  31.2 5.0 %collective-permute-start.4 = (bf16[8,256,128]{2,1,0:T(8,128)(2,1)S(1)}, bf16[8,256,128]{2,1,0:T(8,128)(2,1)S(1)}, u32[]{:S(2)}, u32[]{:S(2)}) collective-permute-start(bf16[8,256,128]{2,1,0:T(8,128)(2,1)S(1)} %get-tuple-element.34.last_ref), channel_id=1, source_target_pairs={{0,2},{2,4},{4,6},{6,8},{8,10},{10,12},{12,14},{1,3},{3,5},{5,7},{... | collective-permute-start | bytes 1572872 | tf_op jit(solution)/shard_map/ppermute | solution.py:232
  36.4 1.3 %collective-permute-done.5.corner_ref = bf16[2,256,128]{2,1,0:T(8,128)(2,1)S(1)} collective-permute-done((bf16[2,256,128]{2,1,0:T(8,128)(2,1)S(1)}, bf16[2,256,128]{2,1,0:T(8,128)(2,1)S(1)}, u32[]{:S(2)}, u32[]{:S(2)}) %collective-permute-start.5) | collective-permute-done | bytes 131104 | tf_op jit(solution)/shard_map/ppermute | solution.py:207
  38.4 3.2 %blur_score_pick.2 = bf16[256,1024]{1,0:T(8,128)(2,1)S(1)} custom-call(s32[1]{0:T(128)} %bitcast.col_ref, bf16[8,256,128]{2,1,0:T(8,128)(2,1)S(1)} %get-tuple-element.30.first_ref, bf16[8,256,128]{2,1,0:T(8,128)(2,1)S(1)} %get-tuple-element.29.last_ref, bf16[8,256,128]{2,1,0:T(8,128)(2,1)S(1)} %collective-permute-done.1.low_ref, ...), custom_call_target="tpu_custom_call" | custom-call | flops 1 | bytes 1 | tf_op jit(solution)/shard_map/blur_score_pick/pallas_call | solution.py:108
  41.7 5.0 %collective-permute-start.9 = (bf16[256,1024]{1,0:T(8,128)(2,1)S(1)}, bf16[256,1024]{1,0:T(8,128)(2,1)S(1)}, u32[]{:S(2)}, u32[]{:S(2)}) collective-permute-start(bf16[256,1024]{1,0:T(8,128)(2,1)S(1)} %blur_score_pick.2), channel_id=1, source_target_pairs={{4,0},{14,2},{8,4},{2,6},{12,8},{6,10},{0,12},{10,14},{5,1},{15,3}... | collective-permute-start | bytes 1572872 | tf_op jit(solution)/shard_map/ppermute | solution.py:253
  46.7 10.8 %collective-permute-done.4.low_ref = bf16[8,256,128]{2,1,0:T(8,128)(2,1)S(1)} collective-permute-done((bf16[8,256,128]{2,1,0:T(8,128)(2,1)S(1)}, bf16[8,256,128]{2,1,0:T(8,128)(2,1)S(1)}, u32[]{:S(2)}, u32[]{:S(2)}) %collective-permute-start.4) | collective-permute-done | bytes 524320 | tf_op jit(solution)/shard_map/ppermute | solution.py:232
  57.7 2.5 %collective-permute-start.12 = (bf16[256,1024]{1,0:T(8,128)(2,1)S(1)}, bf16[256,1024]{1,0:T(8,128)(2,1)S(1)}, u32[]{:S(2)}, u32[]{:S(2)}) collective-permute-start(bf16[256,1024]{1,0:T(8,128)(2,1)S(1)} %blur_score_pick.2), channel_id=1, source_target_pairs={{0,2},{2,0},{4,6},{6,4},{8,10},{10,8},{12,14},{14,12},{1,3},{3,1},... | collective-permute-start | bytes 1572872 | tf_op jit(solution)/shard_map/ppermute | solution.py:257
  60.2 2.5 %collective-permute-start.10 = (bf16[256,1024]{1,0:T(8,128)(2,1)S(1)}, bf16[256,1024]{1,0:T(8,128)(2,1)}, u32[]{:S(2)}, u32[]{:S(2)}) collective-permute-start(bf16[256,1024]{1,0:T(8,128)(2,1)S(1)} %collective-permute-done.9), channel_id=1, source_target_pairs={{0,2},{2,0},{4,6},{6,4},{8,10},{10,8},{12,14},{14,12},{1,3},{3,1},... | collective-permute-start | bytes 1572872 | tf_op jit(solution)/shard_map/ppermute | solution.py:258
  62.7 3.3 %blur_score_pick.3 = bf16[256,1024]{1,0:T(8,128)(2,1)S(1)} custom-call(s32[1]{0:T(128)} %bitcast.col_ref, bf16[8,256,128]{2,1,0:T(8,128)(2,1)S(1)} %get-tuple-element.32.first_ref, bf16[8,256,128]{2,1,0:T(8,128)(2,1)S(1)} %get-tuple-element.34.last_ref, bf16[8,256,128]{2,1,0:T(8,128)(2,1)S(1)} %collective-permute-done.4.low_ref, ...), custom_call_target="tpu_custom_call" | custom-call | flops 1 | bytes 1 | tf_op jit(solution)/shard_map/blur_score_pick/pallas_call | solution.py:108
  66.0 13.0 %collective-permute-start.8 = (bf16[256,1024]{1,0:T(8,128)(2,1)S(1)}, bf16[256,1024]{1,0:T(8,128)(2,1)}, u32[]{:S(2)}, u32[]{:S(2)}) collective-permute-start(bf16[256,1024]{1,0:T(8,128)(2,1)S(1)} %blur_score_pick.3), channel_id=1, source_target_pairs={{4,0},{14,2},{8,4},{2,6},{12,8},{6,10},{0,12},{10,14},{5,1},{15,3}... | collective-permute-start | bytes 1572872 | tf_op jit(solution)/shard_map/ppermute | solution.py:261
  79.8 4.6 %collective-permute-done.10 = bf16[256,1024]{1,0:T(8,128)(2,1)} collective-permute-done((bf16[256,1024]{1,0:T(8,128)(2,1)S(1)}, bf16[256,1024]{1,0:T(8,128)(2,1)}, u32[]{:S(2)}, u32[]{:S(2)}) %collective-permute-start.10) | collective-permute-done | bytes 524320 | tf_op jit(solution)/shard_map/ppermute | solution.py:258
  84.4 1.4 %collective-permute-done.8 = bf16[256,1024]{1,0:T(8,128)(2,1)} collective-permute-done((bf16[256,1024]{1,0:T(8,128)(2,1)S(1)}, bf16[256,1024]{1,0:T(8,128)(2,1)}, u32[]{:S(2)}, u32[]{:S(2)}) %collective-permute-start.8) | collective-permute-done | bytes 524320 | tf_op jit(solution)/shard_map/ppermute | solution.py:261
  88.8 6.5 %collective-permute-done.15 = bf16[256,1024]{1,0:T(8,128)(2,1)} collective-permute-done((bf16[256,1024]{1,0:T(8,128)(2,1)S(1)}, bf16[256,1024]{1,0:T(8,128)(2,1)}, u32[]{:S(2)}, u32[]{:S(2)}) %collective-permute-start.15) | collective-permute-done | bytes 524320 | tf_op jit(solution)/shard_map/ppermute | solution.py:262
  95.3 1.8 %collective-permute-start.21 = (bf16[256,1024]{1,0:T(8,128)(2,1)}, bf16[256,1024]{1,0:T(8,128)(2,1)}, u32[]{:S(2)}, u32[]{:S(2)}) collective-permute-start(bf16[256,1024]{1,0:T(8,128)(2,1)} %collective-permute-done.8), channel_id=1, source_target_pairs={{0,2},{2,0},{4,6},{6,4},{8,10},{10,8},{12,14},{14,12},{1,3},{3,1},... | collective-permute-start | bytes 1572872 | tf_op jit(solution)/shard_map/ppermute | solution.py:268
  99.4 2.0 %collective-permute-done.14 = bf16[256,1024]{1,0:T(8,128)(2,1)} collective-permute-done((bf16[256,1024]{1,0:T(8,128)(2,1)S(1)}, bf16[256,1024]{1,0:T(8,128)(2,1)}, u32[]{:S(2)}, u32[]{:S(2)}) %collective-permute-start.14) | collective-permute-done | bytes 524320 | tf_op jit(solution)/shard_map/ppermute | solution.py:267
  101.6 1.2 %copy-done.2 = bf16[2,256,1024]{2,1,0:T(8,128)(2,1)S(1)} copy-done((bf16[2,256,1024]{2,1,0:T(8,128)(2,1)S(1)}, bf16[2,256,1024]{2,1,0:T(8,128)(2,1)}, u32[]{:S(2)}) %copy-start.2) | copy-done | bytes 1048600
  107.0 5.8 %tiles.2.refs_8_ = bf16[8,16,2,128,128]{4,3,2,1,0:T(8,128)(2,1)} custom-call(s32[128]{0:T(128)S(1)} %reshape.12.place_ref, s32[128]{0:T(128)S(1)} %reshape.15.present_ref, bf16[2,256,1024]{2,1,0:T(8,128)(2,1)S(1)} %pad_maximum_fusion.1.refs_0_, bf16[2,256,1024]{2,1,0:T(8,128)(2,1)S(1)} %copy-done.2, bf16[1,256,1024]{2,1,0:T(8,128)(2,1)S(1)} %bitcast.15, ...), custom_call_target="tpu_custom_call" | custom-call | flops 1 | bytes 1 | tf_op jit(solution)/shard_map/tiles/pallas_call | solution.py:173
  113.4 1.7 %collective-permute-done.23.refs_7_ = bf16[1,256,1024]{2,1,0:T(8,128)(2,1)S(1)} collective-permute-done((bf16[1,256,1024]{2,1,0:T(8,128)(2,1)}, bf16[1,256,1024]{2,1,0:T(8,128)(2,1)S(1)}, u32[]{:S(2)}, u32[]{:S(2)}) %collective-permute-start.23) | collective-permute-done | bytes 524320 | tf_op jit(solution)/shard_map/ppermute | solution.py:207
  115.2 6.1 %tiles.3 = bf16[8,16,2,128,128]{4,3,2,1,0:T(8,128)(2,1)} custom-call(s32[128]{0:T(128)S(1)} %reshape.12.place_ref, s32[128]{0:T(128)S(1)} %reshape.15.present_ref, bf16[2,256,1024]{2,1,0:T(8,128)(2,1)S(1)} %pad_maximum_fusion.refs_0_, bf16[2,256,1024]{2,1,0:T(8,128)(2,1)S(1)} %collective-permute-done.13.refs_1_, ...), custom_call_target="tpu_custom_call", output_to_operand_aliasing={{}: (10, {})} | custom-call | flops 1 | bytes 1 | tf_op jit(solution)/shard_map/tiles/pallas_call | solution.py:173
  (69 shorter events, 15.4 us)
Async XLA Ops:
  2.6 27.3 %collective-permute-start.1 = (bf16[8,256,128]{2,1,0:T(8,128)(2,1)S(1)}, bf16[8,256,128]{2,1,0:T(8,128)(2,1)S(1)}, u32[]{:S(2)}, u32[]{:S(2)}) collective-permute-start(bf16[8,256,128]{2,1,0:T(8,128)(2,1)S(1)} %get-tuple-element.29.last_ref), channel_id=1, source_target_pairs={{0,2},{2,4},{4,6},{6,8},{8,10},{10,12},{12,14},{1,3},{3,5},{5,7},{... | collective-permute-start | bytes 1572872 | tf_op jit(solution)/shard_map/ppermute | solution.py:232
  7.6 22.4 %collective-permute-start.2 = (bf16[8,256,128]{2,1,0:T(8,128)(2,1)S(1)}, bf16[8,256,128]{2,1,0:T(8,128)(2,1)S(1)}, u32[]{:S(2)}, u32[]{:S(2)}) collective-permute-start(bf16[8,256,128]{2,1,0:T(8,128)(2,1)S(1)} %get-tuple-element.30.first_ref), channel_id=1, source_target_pairs={{2,0},{4,2},{6,4},{8,6},{10,8},{12,10},{14,12},{3,1},{5,3},{7,5},{... | collective-permute-start | bytes 1572872 | tf_op jit(solution)/shard_map/ppermute | solution.py:232
  8.9 1.4 %collective-permute-start = (bf16[2,256,128]{2,1,0:T(8,128)(2,1)S(1)}, bf16[2,256,128]{2,1,0:T(8,128)(2,1)S(1)}, u32[]{:S(2)}, u32[]{:S(2)}) collective-permute-start(bf16[2,256,128]{2,1,0:T(8,128)(2,1)S(1)} %get-tuple-element.26), channel_id=1, source_target_pairs={{0,1},{1,0},{2,3},{3,2},{4,5},{5,4},{6,7},{7,6},{8,9},{9,8},{10,11... | collective-permute-start | bytes 393224 | tf_op jit(solution)/shard_map/ppermute | solution.py:207
  11.3 1.4 %collective-permute-start.3 = (bf16[2,256,128]{2,1,0:T(8,128)(2,1)S(1)}, bf16[2,256,128]{2,1,0:T(8,128)(2,1)S(1)}, u32[]{:S(2)}, u32[]{:S(2)}) collective-permute-start(bf16[2,256,128]{2,1,0:T(8,128)(2,1)S(1)} %get-tuple-element.31), channel_id=1, source_target_pairs={{0,1},{1,0},{2,3},{3,2},{4,5},{5,4},{6,7},{7,6},{8,9},{9,8},{10,11... | collective-permute-start | bytes 393224 | tf_op jit(solution)/shard_map/ppermute | solution.py:207
  29.9 16.8 %collective-permute-start.6 = (bf16[8,256,128]{2,1,0:T(8,128)(2,1)S(1)}, bf16[8,256,128]{2,1,0:T(8,128)(2,1)S(1)}, u32[]{:S(2)}, u32[]{:S(2)}) collective-permute-start(bf16[8,256,128]{2,1,0:T(8,128)(2,1)S(1)} %get-tuple-element.32.first_ref), channel_id=1, source_target_pairs={{2,0},{4,2},{6,4},{8,6},{10,8},{12,10},{14,12},{3,1},{5,3},{7,5},{... | collective-permute-start | bytes 1572872 | tf_op jit(solution)/shard_map/ppermute | solution.py:232
  31.2 26.4 %collective-permute-start.4 = (bf16[8,256,128]{2,1,0:T(8,128)(2,1)S(1)}, bf16[8,256,128]{2,1,0:T(8,128)(2,1)S(1)}, u32[]{:S(2)}, u32[]{:S(2)}) collective-permute-start(bf16[8,256,128]{2,1,0:T(8,128)(2,1)S(1)} %get-tuple-element.34.last_ref), channel_id=1, source_target_pairs={{0,2},{2,4},{4,6},{6,8},{8,10},{10,12},{12,14},{1,3},{3,5},{5,7},{... | collective-permute-start | bytes 1572872 | tf_op jit(solution)/shard_map/ppermute | solution.py:232
  36.3 1.4 %collective-permute-start.5 = (bf16[2,256,128]{2,1,0:T(8,128)(2,1)S(1)}, bf16[2,256,128]{2,1,0:T(8,128)(2,1)S(1)}, u32[]{:S(2)}, u32[]{:S(2)}) collective-permute-start(bf16[2,256,128]{2,1,0:T(8,128)(2,1)S(1)} %pad_maximum_fusion.2), channel_id=1, source_target_pairs={{0,1},{1,0},{2,3},{3,2},{4,5},{5,4},{6,7},{7,6},{8,9},{9,8},{10,11... | collective-permute-start | bytes 393224 | tf_op jit(solution)/shard_map/ppermute | solution.py:207
  41.7 18.6 %collective-permute-start.9 = (bf16[256,1024]{1,0:T(8,128)(2,1)S(1)}, bf16[256,1024]{1,0:T(8,128)(2,1)S(1)}, u32[]{:S(2)}, u32[]{:S(2)}) collective-permute-start(bf16[256,1024]{1,0:T(8,128)(2,1)S(1)} %blur_score_pick.2), channel_id=1, source_target_pairs={{4,0},{14,2},{8,4},{2,6},{12,8},{6,10},{0,12},{10,14},{5,1},{15,3}... | collective-permute-start | bytes 1572872 | tf_op jit(solution)/shard_map/ppermute | solution.py:253
  46.7 32.5 %collective-permute-start.11 = (bf16[256,1024]{1,0:T(8,128)(2,1)S(1)}, bf16[256,1024]{1,0:T(8,128)(2,1)S(1)}, u32[]{:S(2)}, u32[]{:S(2)}) collective-permute-start(bf16[256,1024]{1,0:T(8,128)(2,1)S(1)} %blur_score_pick.2), channel_id=1, source_target_pairs={{0,4},{2,14},{4,8},{6,2},{8,12},{10,6},{12,0},{14,10},{1,5},{3,15}... | collective-permute-start | bytes 1572872 | tf_op jit(solution)/shard_map/ppermute | solution.py:254
  57.6 5.1 %collective-permute-start.7 = (bf16[2,256,128]{2,1,0:T(8,128)(2,1)S(1)}, bf16[2,256,128]{2,1,0:T(8,128)(2,1)S(1)}, u32[]{:S(2)}, u32[]{:S(2)}) collective-permute-start(bf16[2,256,128]{2,1,0:T(8,128)(2,1)S(1)} %pad_maximum_fusion.3), channel_id=1, source_target_pairs={{0,1},{1,0},{2,3},{3,2},{4,5},{5,4},{6,7},{7,6},{8,9},{9,8},{10,11... | collective-permute-start | bytes 393224 | tf_op jit(solution)/shard_map/ppermute | solution.py:207
  57.7 22.1 %collective-permute-start.12 = (bf16[256,1024]{1,0:T(8,128)(2,1)S(1)}, bf16[256,1024]{1,0:T(8,128)(2,1)S(1)}, u32[]{:S(2)}, u32[]{:S(2)}) collective-permute-start(bf16[256,1024]{1,0:T(8,128)(2,1)S(1)} %blur_score_pick.2), channel_id=1, source_target_pairs={{0,2},{2,0},{4,6},{6,4},{8,10},{10,8},{12,14},{14,12},{1,3},{3,1},... | collective-permute-start | bytes 1572872 | tf_op jit(solution)/shard_map/ppermute | solution.py:257
  60.2 24.1 %collective-permute-start.10 = (bf16[256,1024]{1,0:T(8,128)(2,1)S(1)}, bf16[256,1024]{1,0:T(8,128)(2,1)}, u32[]{:S(2)}, u32[]{:S(2)}) collective-permute-start(bf16[256,1024]{1,0:T(8,128)(2,1)S(1)} %collective-permute-done.9), channel_id=1, source_target_pairs={{0,2},{2,0},{4,6},{6,4},{8,10},{10,8},{12,14},{14,12},{1,3},{3,1},... | collective-permute-start | bytes 1572872 | tf_op jit(solution)/shard_map/ppermute | solution.py:258
  66.0 19.7 %collective-permute-start.8 = (bf16[256,1024]{1,0:T(8,128)(2,1)S(1)}, bf16[256,1024]{1,0:T(8,128)(2,1)}, u32[]{:S(2)}, u32[]{:S(2)}) collective-permute-start(bf16[256,1024]{1,0:T(8,128)(2,1)S(1)} %blur_score_pick.3), channel_id=1, source_target_pairs={{4,0},{14,2},{8,4},{2,6},{12,8},{6,10},{0,12},{10,14},{5,1},{15,3}... | collective-permute-start | bytes 1572872 | tf_op jit(solution)/shard_map/ppermute | solution.py:261
  79.2 18.7 %collective-permute-start.16 = (bf16[2,256,1024]{2,1,0:T(8,128)(2,1)S(1)}, bf16[2,256,1024]{2,1,0:T(8,128)(2,1)S(1)}, u32[]{:S(2)}, u32[]{:S(2)}) collective-permute-start(bf16[2,256,1024]{2,1,0:T(8,128)(2,1)S(1)} %pad_maximum_fusion.1.refs_0_), channel_id=1, source_target_pairs={{0,1},{1,0},{2,3},{3,2},{4,5},{5,4},{6,7},{7,6},{8,9},{9,8},{10,11... | collective-permute-start | bytes 3145736 | tf_op jit(solution)/shard_map/ppermute | solution.py:207
  79.3 8.5 %collective-permute-start.17 = (bf16[1,256,1024]{2,1,0:T(8,128)(2,1)S(1)}, bf16[1,256,1024]{2,1,0:T(8,128)(2,1)S(1)}, u32[]{:S(2)}, u32[]{:S(2)}) collective-permute-start(bf16[1,256,1024]{2,1,0:T(8,128)(2,1)S(1)} %bitcast.14), channel_id=1, source_target_pairs={{0,1},{1,0},{2,3},{3,2},{4,5},{5,4},{6,7},{7,6},{8,9},{9,8},{10,11... | collective-permute-start | bytes 1572872 | tf_op jit(solution)/shard_map/ppermute | solution.py:207
  79.8 15.6 %collective-permute-start.15 = (bf16[256,1024]{1,0:T(8,128)(2,1)S(1)}, bf16[256,1024]{1,0:T(8,128)(2,1)}, u32[]{:S(2)}, u32[]{:S(2)}) collective-permute-start(bf16[256,1024]{1,0:T(8,128)(2,1)S(1)} %blur_score_pick.3), channel_id=1, source_target_pairs={{0,2},{2,0},{4,6},{6,4},{8,10},{10,8},{12,14},{14,12},{1,3},{3,1},... | collective-permute-start | bytes 1572872 | tf_op jit(solution)/shard_map/ppermute | solution.py:262
  84.4 12.7 %collective-permute-start.18 = (bf16[1,256,1024]{2,1,0:T(8,128)(2,1)S(1)}, bf16[1,256,1024]{2,1,0:T(8,128)(2,1)S(1)}, u32[]{:S(2)}, u32[]{:S(2)}) collective-permute-start(bf16[1,256,1024]{2,1,0:T(8,128)(2,1)S(1)} %bitcast.16), channel_id=1, source_target_pairs={{0,1},{1,0},{2,3},{3,2},{4,5},{5,4},{6,7},{7,6},{8,9},{9,8},{10,11... | collective-permute-start | bytes 1572872 | tf_op jit(solution)/shard_map/ppermute | solution.py:207
  85.8 15.6 %collective-permute-start.14 = (bf16[256,1024]{1,0:T(8,128)(2,1)S(1)}, bf16[256,1024]{1,0:T(8,128)(2,1)}, u32[]{:S(2)}, u32[]{:S(2)}) collective-permute-start(bf16[256,1024]{1,0:T(8,128)(2,1)S(1)} %blur_score_pick.3), channel_id=1, source_target_pairs={{0,4},{2,14},{4,8},{6,2},{8,12},{10,6},{12,0},{14,10},{1,5},{3,15}... | collective-permute-start | bytes 1572872 | tf_op jit(solution)/shard_map/ppermute | solution.py:267
  88.6 24.3 %collective-permute-start.13 = (bf16[2,256,1024]{2,1,0:T(8,128)(2,1)S(1)}, bf16[2,256,1024]{2,1,0:T(8,128)(2,1)S(1)}, u32[]{:S(2)}, u32[]{:S(2)}) collective-permute-start(bf16[2,256,1024]{2,1,0:T(8,128)(2,1)S(1)} %pad_maximum_fusion.refs_0_), channel_id=1, source_target_pairs={{0,1},{1,0},{2,3},{3,2},{4,5},{5,4},{6,7},{7,6},{8,9},{9,8},{10,11... | collective-permute-start | bytes 3145736 | tf_op jit(solution)/shard_map/ppermute | solution.py:207
  95.3 17.5 %collective-permute-start.21 = (bf16[256,1024]{1,0:T(8,128)(2,1)}, bf16[256,1024]{1,0:T(8,128)(2,1)}, u32[]{:S(2)}, u32[]{:S(2)}) collective-permute-start(bf16[256,1024]{1,0:T(8,128)(2,1)} %collective-permute-done.8), channel_id=1, source_target_pairs={{0,2},{2,0},{4,6},{6,4},{8,10},{10,8},{12,14},{14,12},{1,3},{3,1},... | collective-permute-start | bytes 1572872 | tf_op jit(solution)/shard_map/ppermute | solution.py:268
  97.9 3.7 %collective-permute-start.22 = (bf16[1,256,1024]{2,1,0:T(8,128)(2,1)}, bf16[1,256,1024]{2,1,0:T(8,128)(2,1)}, u32[]{:S(2)}, u32[]{:S(2)}) collective-permute-start(bf16[1,256,1024]{2,1,0:T(8,128)(2,1)} %bitcast.10.refs_6_), channel_id=1, source_target_pairs={{0,1},{1,0},{2,3},{3,2},{4,5},{5,4},{6,7},{7,6},{8,9},{9,8},{10,11... | collective-permute-start | bytes 1572872 | tf_op jit(solution)/shard_map/ppermute | solution.py:207
  98.9 14.0 %collective-permute-start.20 = (bf16[1,256,1024]{2,1,0:T(8,128)(2,1)}, bf16[1,256,1024]{2,1,0:T(8,128)(2,1)}, u32[]{:S(2)}, u32[]{:S(2)}) collective-permute-start(bf16[1,256,1024]{2,1,0:T(8,128)(2,1)} %bitcast.9.refs_4_), channel_id=1, source_target_pairs={{0,1},{1,0},{2,3},{3,2},{4,5},{5,4},{6,7},{7,6},{8,9},{9,8},{10,11... | collective-permute-start | bytes 1572872 | tf_op jit(solution)/shard_map/ppermute | solution.py:207
  101.4 11.5 %collective-permute-start.19 = (bf16[1,256,1024]{2,1,0:T(8,128)(2,1)}, bf16[1,256,1024]{2,1,0:T(8,128)(2,1)}, u32[]{:S(2)}, u32[]{:S(2)}) collective-permute-start(bf16[1,256,1024]{2,1,0:T(8,128)(2,1)} %bitcast.8.refs_2_), channel_id=1, source_target_pairs={{0,1},{1,0},{2,3},{3,2},{4,5},{5,4},{6,7},{7,6},{8,9},{9,8},{10,11... | collective-permute-start | bytes 1572872 | tf_op jit(solution)/shard_map/ppermute | solution.py:207
  112.9 2.3 %collective-permute-start.23 = (bf16[1,256,1024]{2,1,0:T(8,128)(2,1)}, bf16[1,256,1024]{2,1,0:T(8,128)(2,1)S(1)}, u32[]{:S(2)}, u32[]{:S(2)}) collective-permute-start(bf16[1,256,1024]{2,1,0:T(8,128)(2,1)} %bitcast.11.refs_6_), channel_id=1, source_target_pairs={{0,1},{1,0},{2,3},{3,2},{4,5},{5,4},{6,7},{7,6},{8,9},{9,8},{10,11... | collective-permute-start | bytes 1572872 | tf_op jit(solution)/shard_map/ppermute | solution.py:207
  (14 other events, 216.6 us)

commit v5 on v4

--- a/solution.py
+++ b/solution.py
@@ -13,6 +13,7 @@
 CENTRE = 1.0 / (1.0 + 2.0 * math.exp(-0.5))
 SMALL = pl.CostEstimate(flops=1, bytes_accessed=1, transcendentals=0)
 VMEM_BYTES = 24 * 1024 * 1024
+TILES_VMEM_BYTES = 60 * 1024 * 1024
 
 
 def faces_kernel(col_ref, bold_ref, first_ref, last_ref, edge_ref, wide):
@@ -186,7 +187,7 @@
         ),
         out_shape=jax.ShapeDtypeStruct((blocks, slots, windows, BLOCK, BLOCK), jnp.bfloat16),
         input_output_aliases={} if earlier is None else {2 + count: 0},
-        compiler_params=pltpu.CompilerParams(vmem_limit_bytes=VMEM_BYTES),
+        compiler_params=pltpu.CompilerParams(vmem_limit_bytes=TILES_VMEM_BYTES),
         cost_estimate=SMALL,
         name="tiles",
     )(place, present, *operands)
@@ -263,11 +264,11 @@
     pair_0, rest_0 = after(pair_0, own_1), after(rest_0, own_1)
     behind_0 = after(behind_0, own_1)
     sources = both(0, own_0, ahead_0) + both(4, behind_0) + both(6, pair_0)
-    ahead_1 = after(ahead_1, rest_0, behind_0, pair_0)
+    swapped = [source[2] for source in sources]
+    ahead_1 = after(ahead_1, rest_0, *swapped)
     behind_1 = lax.ppermute(after(own_1, ahead_1), "row", behind)
     rest_1 = lax.ppermute(ahead_1, "row", in_pair)
-    swapped = [source[2] for source in sources]
-    pair_1 = after(pair_1, ahead_1, *swapped)
+    pair_1 = after(pair_1, ahead_1)
     behind_1 = after(behind_1, pair_1)
     out = make_tiles(0, windows, place, present, sources + both(8, rest_0), None)
     sources = both(0, own_1, ahead_1) + both(4, behind_1) + both(6, pair_1)

time: 122 us -> 127 us (1.041)
  starting transfers between devices: 40.5 us -> 45.7 us
  local copies, waits for them, and re-layouts: 10.5 us -> 6.18 us
  waiting for transfers between devices: 48.2 us -> 50.7 us
  Pallas kernels: 20.5 us -> 22.4 us
    ppermute x1, waiting for transfers between devices: 2 us -> 8.61 us  [on_device(): behind_1 = lax.ppermute(after(own_1, ahead_1), 'row', behind)]
    ppermute x1, waiting for transfers between devices: 6.54 us -> 0.01 us  [on_device(): pair_1 = lax.ppermute(own_1, 'row', in_pair)]
    unnamed x28 -> x26, local copies, waits for them, and re-layouts: 10.3 us -> 5.01 us
    ppermute x1, waiting for transfers between devices: 1.42 us -> 6.44 us  [on_device(): ahead_1 = lax.ppermute(own_1, 'row', ahead)]
    ppermute x1, starting transfers between devices: 1.76 us -> 4.57 us  [on_device(): rest_1 = lax.ppermute(ahead_1, 'row', in_pair)]
    ppermute x12, waiting for transfers between devices: 5.65 us -> 3.37 us  [other_col(): return lax.ppermute(value, 'col', [(0, 1), (1, 0)])]
    ppermute x1, waiting for transfers between devices: 4.59 us -> 2.43 us  [on_device(): rest_0 = lax.ppermute(ahead_0, 'row', in_pair)]
    pallas_call x2, Pallas kernels: 11.9 us -> 13.8 us  [make_tiles(): pl.pallas_call(functools.partial(tiles_kernel, sources=where, window=wind...]
  transfers between devices with their start and end apart: 24 -> 24, of which waited for: 10 -> 9; matrix products, arithmetic and copies ran while one was open for 1% -> 2% of each run, Pallas kernels for 11% -> 11%
where the time goes in v5:
time: 127 us
  waiting for transfers between devices  50.7 us (40%)
  starting transfers between devices  45.7 us (36%)
  Pallas kernels  22.4 us (18%)
  local copies, waits for them, and re-layouts  6.18 us (5%)
  other arithmetic  1.34 us (1%)
    ppermute x2, waiting for transfers between devices, halo(): lax.ppermute(last, 'row', one_up)  28.2 us
    ppermute x1, starting transfers between devices, on_device(): ahead_1 = lax.ppermute(own_1, 'row', ahead)  14.2 us
    pallas_call x2, Pallas kernels, make_tiles(): pl.pallas_call(functools.partial(tiles_kernel, sources=where, window=wind...  13.8 us
    ppermute x2, starting transfers between devices, halo(): lax.ppermute(last, 'row', one_up)  9.95 us
    ppermute x1, waiting for transfers between devices, on_device(): behind_1 = lax.ppermute(after(own_1, ahead_1), 'row', behind)  8.61 us
    pallas_call x2, Pallas kernels, make_panel(): pl.pallas_call(panel_kernel, grid=(1,), in_specs=[pl.BlockSpec(memory_spa...  6.52 us
    ppermute x1, waiting for transfers between devices, on_device(): ahead_1 = lax.ppermute(own_1, 'row', ahead)  6.44 us
    ppermute x1, starting transfers between devices, on_device(): ahead_0 = lax.ppermute(own_0, 'row', ahead)  5.02 us
  transfers between devices with their start and end apart: 24, of which 9 were waited for; matrix products, arithmetic and copies ran while one was open for 2% of the time, Pallas kernels for 11%

profile of v5, /device:TPU:0, one launch (start us, length us, event | category | flops | bytes accessed | tf_op | source)
XLA Modules:
  0.0 126.8 jit_solution(17450988998523318987)
XLA Ops:
  0.0 1.6 %copy-done = bf16[2,256,2,8,128]{4,3,2,1,0:T(8,128)(2,1)S(1)} copy-done((bf16[2,256,2,8,128]{4,3,2,1,0:T(8,128)(2,1)S(1)}, bf16[2,256,2,8,128]{4,3,2,1,0:T(8,128)(2,1)}, u32[]{:S(2)}) %copy-start) | copy-done | bytes 2097176
  2.6 4.9 %collective-permute-start.1 = (bf16[8,256,128]{2,1,0:T(8,128)(2,1)S(1)}, bf16[8,256,128]{2,1,0:T(8,128)(2,1)S(1)}, u32[]{:S(2)}, u32[]{:S(2)}) collective-permute-start(bf16[8,256,128]{2,1,0:T(8,128)(2,1)S(1)} %get-tuple-element.29.last_ref), channel_id=1, source_target_pairs={{0,2},{2,4},{4,6},{6,8},{8,10},{10,12},{12,14},{1,3},{3,5},{5,7},{... | collective-permute-start | bytes 1572872 | tf_op jit(solution)/shard_map/ppermute | solution.py:233
  7.6 1.3 %collective-permute-start.2 = (bf16[8,256,128]{2,1,0:T(8,128)(2,1)S(1)}, bf16[8,256,128]{2,1,0:T(8,128)(2,1)S(1)}, u32[]{:S(2)}, u32[]{:S(2)}) collective-permute-start(bf16[8,256,128]{2,1,0:T(8,128)(2,1)S(1)} %get-tuple-element.30.first_ref), channel_id=1, source_target_pairs={{2,0},{4,2},{6,4},{8,6},{10,8},{12,10},{14,12},{3,1},{5,3},{7,5},{... | collective-permute-start | bytes 1572872 | tf_op jit(solution)/shard_map/ppermute | solution.py:233
  8.9 1.3 %collective-permute-done.edge_ref = bf16[2,256,128]{2,1,0:T(8,128)(2,1)S(1)} collective-permute-done((bf16[2,256,128]{2,1,0:T(8,128)(2,1)S(1)}, bf16[2,256,128]{2,1,0:T(8,128)(2,1)S(1)}, u32[]{:S(2)}, u32[]{:S(2)}) %collective-permute-start) | collective-permute-done | bytes 131104 | tf_op jit(solution)/shard_map/ppermute | solution.py:208
  10.3 1.6 %copy-done.1 = bf16[2,256,2,8,128]{4,3,2,1,0:T(8,128)(2,1)S(1)} copy-done((bf16[2,256,2,8,128]{4,3,2,1,0:T(8,128)(2,1)S(1)}, bf16[2,256,2,8,128]{4,3,2,1,0:T(8,128)(2,1)}, u32[]{:S(2)}) %copy-start.1) | copy-done | bytes 2097176
  13.1 16.8 %collective-permute-done.1.low_ref = bf16[8,256,128]{2,1,0:T(8,128)(2,1)S(1)} collective-permute-done((bf16[8,256,128]{2,1,0:T(8,128)(2,1)S(1)}, bf16[8,256,128]{2,1,0:T(8,128)(2,1)S(1)}, u32[]{:S(2)}, u32[]{:S(2)}) %collective-permute-start.1) | collective-permute-done | bytes 524320 | tf_op jit(solution)/shard_map/ppermute | solution.py:233
  30.1 1.3 %collective-permute-start.6 = (bf16[8,256,128]{2,1,0:T(8,128)(2,1)S(1)}, bf16[8,256,128]{2,1,0:T(8,128)(2,1)S(1)}, u32[]{:S(2)}, u32[]{:S(2)}) collective-permute-start(bf16[8,256,128]{2,1,0:T(8,128)(2,1)S(1)} %get-tuple-element.32.first_ref), channel_id=1, source_target_pairs={{2,0},{4,2},{6,4},{8,6},{10,8},{12,10},{14,12},{3,1},{5,3},{7,5},{... | collective-permute-start | bytes 1572872 | tf_op jit(solution)/shard_map/ppermute | solution.py:233
  31.4 5.0 %collective-permute-start.4 = (bf16[8,256,128]{2,1,0:T(8,128)(2,1)S(1)}, bf16[8,256,128]{2,1,0:T(8,128)(2,1)S(1)}, u32[]{:S(2)}, u32[]{:S(2)}) collective-permute-start(bf16[8,256,128]{2,1,0:T(8,128)(2,1)S(1)} %get-tuple-element.34.last_ref), channel_id=1, source_target_pairs={{0,2},{2,4},{4,6},{6,8},{8,10},{10,12},{12,14},{1,3},{3,5},{5,7},{... | collective-permute-start | bytes 1572872 | tf_op jit(solution)/shard_map/ppermute | solution.py:233
  37.1 3.2 %blur_score_pick.2 = bf16[256,1024]{1,0:T(8,128)(2,1)S(1)} custom-call(s32[1]{0:T(128)} %bitcast.col_ref, bf16[8,256,128]{2,1,0:T(8,128)(2,1)S(1)} %get-tuple-element.30.first_ref, bf16[8,256,128]{2,1,0:T(8,128)(2,1)S(1)} %get-tuple-element.29.last_ref, bf16[8,256,128]{2,1,0:T(8,128)(2,1)S(1)} %collective-permute-done.1.low_ref, ...), custom_call_target="tpu_custom_call" | custom-call | flops 1 | bytes 1 | tf_op jit(solution)/shard_map/blur_score_pick/pallas_call | solution.py:109
  40.4 5.0 %collective-permute-start.9 = (bf16[256,1024]{1,0:T(8,128)(2,1)S(1)}, bf16[256,1024]{1,0:T(8,128)(2,1)S(1)}, u32[]{:S(2)}, u32[]{:S(2)}) collective-permute-start(bf16[256,1024]{1,0:T(8,128)(2,1)S(1)} %blur_score_pick.2), channel_id=1, source_target_pairs={{4,0},{14,2},{8,4},{2,6},{12,8},{6,10},{0,12},{10,14},{5,1},{15,3}... | collective-permute-start | bytes 1572872 | tf_op jit(solution)/shard_map/ppermute | solution.py:254
  45.4 1.6 %collective-permute-done.6.high_ref = bf16[8,256,128]{2,1,0:T(8,128)(2,1)S(1)} collective-permute-done((bf16[8,256,128]{2,1,0:T(8,128)(2,1)S(1)}, bf16[8,256,128]{2,1,0:T(8,128)(2,1)S(1)}, u32[]{:S(2)}, u32[]{:S(2)}) %collective-permute-start.6) | collective-permute-done | bytes 524320 | tf_op jit(solution)/shard_map/ppermute | solution.py:233
  47.0 11.4 %collective-permute-done.4.low_ref = bf16[8,256,128]{2,1,0:T(8,128)(2,1)S(1)} collective-permute-done((bf16[8,256,128]{2,1,0:T(8,128)(2,1)S(1)}, bf16[8,256,128]{2,1,0:T(8,128)(2,1)S(1)}, u32[]{:S(2)}, u32[]{:S(2)}) %collective-permute-start.4) | collective-permute-done | bytes 524320 | tf_op jit(solution)/shard_map/ppermute | solution.py:233
  58.4 2.5 %collective-permute-start.14 = (bf16[256,1024]{1,0:T(8,128)(2,1)S(1)}, bf16[256,1024]{1,0:T(8,128)(2,1)S(1)}, u32[]{:S(2)}, u32[]{:S(2)}) collective-permute-start(bf16[256,1024]{1,0:T(8,128)(2,1)S(1)} %blur_score_pick.2), channel_id=1, source_target_pairs={{0,2},{2,0},{4,6},{6,4},{8,10},{10,8},{12,14},{14,12},{1,3},{3,1},... | collective-permute-start | bytes 1572872 | tf_op jit(solution)/shard_map/ppermute | solution.py:258
  61.7 2.0 %collective-permute-start.10 = (bf16[256,1024]{1,0:T(8,128)(2,1)S(1)}, bf16[256,1024]{1,0:T(8,128)(2,1)}, u32[]{:S(2)}, u32[]{:S(2)}) collective-permute-start(bf16[256,1024]{1,0:T(8,128)(2,1)S(1)} %collective-permute-done.9), channel_id=1, source_target_pairs={{0,2},{2,0},{4,6},{6,4},{8,10},{10,8},{12,14},{14,12},{1,3},{3,1},... | collective-permute-start | bytes 1572872 | tf_op jit(solution)/shard_map/ppermute | solution.py:259
  63.9 3.3 %blur_score_pick.3 = bf16[256,1024]{1,0:T(8,128)(2,1)S(1)} custom-call(s32[1]{0:T(128)} %bitcast.col_ref, bf16[8,256,128]{2,1,0:T(8,128)(2,1)S(1)} %get-tuple-element.32.first_ref, bf16[8,256,128]{2,1,0:T(8,128)(2,1)S(1)} %get-tuple-element.34.last_ref, bf16[8,256,128]{2,1,0:T(8,128)(2,1)S(1)} %collective-permute-done.4.low_ref, ...), custom_call_target="tpu_custom_call" | custom-call | flops 1 | bytes 1 | tf_op jit(solution)/shard_map/blur_score_pick/pallas_call | solution.py:109
  67.2 14.2 %collective-permute-start.8 = (bf16[256,1024]{1,0:T(8,128)(2,1)S(1)}, bf16[256,1024]{1,0:T(8,128)(2,1)}, u32[]{:S(2)}, u32[]{:S(2)}) collective-permute-start(bf16[256,1024]{1,0:T(8,128)(2,1)S(1)} %blur_score_pick.3), channel_id=1, source_target_pairs={{4,0},{14,2},{8,4},{2,6},{12,8},{6,10},{0,12},{10,14},{5,1},{15,3}... | collective-permute-start | bytes 1572872 | tf_op jit(solution)/shard_map/ppermute | solution.py:262
  82.0 2.4 %collective-permute-done.10 = bf16[256,1024]{1,0:T(8,128)(2,1)} collective-permute-done((bf16[256,1024]{1,0:T(8,128)(2,1)S(1)}, bf16[256,1024]{1,0:T(8,128)(2,1)}, u32[]{:S(2)}, u32[]{:S(2)}) %collective-permute-start.10) | collective-permute-done | bytes 524320 | tf_op jit(solution)/shard_map/ppermute | solution.py:259
  84.4 1.7 %collective-permute-start.18 = (bf16[256,1024]{1,0:T(8,128)(2,1)S(1)}, bf16[256,1024]{1,0:T(8,128)(2,1)}, u32[]{:S(2)}, u32[]{:S(2)}) collective-permute-start(bf16[256,1024]{1,0:T(8,128)(2,1)S(1)} %blur_score_pick.3), channel_id=1, source_target_pairs={{0,2},{2,0},{4,6},{6,4},{8,10},{10,8},{12,14},{14,12},{1,3},{3,1},... | collective-permute-start | bytes 1572872 | tf_op jit(solution)/shard_map/ppermute | solution.py:263
  86.1 6.4 %collective-permute-done.8 = bf16[256,1024]{1,0:T(8,128)(2,1)} collective-permute-done((bf16[256,1024]{1,0:T(8,128)(2,1)S(1)}, bf16[256,1024]{1,0:T(8,128)(2,1)}, u32[]{:S(2)}, u32[]{:S(2)}) %collective-permute-start.8) | collective-permute-done | bytes 524320 | tf_op jit(solution)/shard_map/ppermute | solution.py:262
  95.1 4.6 %collective-permute-start.21 = (bf16[256,1024]{1,0:T(8,128)(2,1)}, bf16[256,1024]{1,0:T(8,128)(2,1)}, u32[]{:S(2)}, u32[]{:S(2)}) collective-permute-start(bf16[256,1024]{1,0:T(8,128)(2,1)} %collective-permute-done.8), channel_id=1, source_target_pairs={{0,2},{2,0},{4,6},{6,4},{8,10},{10,8},{12,14},{14,12},{1,3},{3,1},... | collective-permute-start | bytes 1572872 | tf_op jit(solution)/shard_map/ppermute | solution.py:270
  99.7 8.6 %collective-permute-done.17 = bf16[256,1024]{1,0:T(8,128)(2,1)} collective-permute-done((bf16[256,1024]{1,0:T(8,128)(2,1)S(1)}, bf16[256,1024]{1,0:T(8,128)(2,1)}, u32[]{:S(2)}, u32[]{:S(2)}) %collective-permute-start.17) | collective-permute-done | bytes 524320 | tf_op jit(solution)/shard_map/ppermute | solution.py:269
  109.7 6.9 %tiles.2.refs_8_ = bf16[8,16,2,128,128]{4,3,2,1,0:T(8,128)(2,1)} custom-call(s32[128]{0:T(128)} %reshape.12.place_ref, s32[128]{0:T(128)} %reshape.15.present_ref, bf16[2,256,1024]{2,1,0:T(8,128)(2,1)} %copy-done.4, bf16[2,256,1024]{2,1,0:T(8,128)(2,1)} %copy-done.6, bf16[1,256,1024]{2,1,0:T(8,128)(2,1)} %bitcast.17, bf16[1,256,1024]{2,1,0:T(8,128)(2,1)} %copy-done.9, ...), custom_call_target="tpu_custom_call" | custom-call | flops 1 | bytes 1 | tf_op jit(solution)/shard_map/tiles/pallas_call | solution.py:174
  117.2 1.7 %collective-permute-done.23.refs_7_ = bf16[1,256,1024]{2,1,0:T(8,128)(2,1)S(1)} collective-permute-done((bf16[1,256,1024]{2,1,0:T(8,128)(2,1)}, bf16[1,256,1024]{2,1,0:T(8,128)(2,1)S(1)}, u32[]{:S(2)}, u32[]{:S(2)}) %collective-permute-start.23) | collective-permute-done | bytes 524320 | tf_op jit(solution)/shard_map/ppermute | solution.py:208
  119.7 6.9 %tiles.3 = bf16[8,16,2,128,128]{4,3,2,1,0:T(8,128)(2,1)} custom-call(s32[128]{0:T(128)} %reshape.12.place_ref, s32[128]{0:T(128)} %reshape.15.present_ref, bf16[2,256,1024]{2,1,0:T(8,128)(2,1)} %copy-done.3, bf16[2,256,1024]{2,1,0:T(8,128)(2,1)} %copy-done.5, bf16[1,256,1024]{2,1,0:T(8,128)(2,1)} %bitcast.8.refs_2_, ...), custom_call_target="tpu_custom_call", output_to_operand_aliasing={{}: (10, {})} | custom-call | flops 1 | bytes 1 | tf_op jit(solution)/shard_map/tiles/pallas_call | solution.py:174
  (67 shorter events, 9.9 us)
Async XLA Ops:
  2.6 27.3 %collective-permute-start.1 = (bf16[8,256,128]{2,1,0:T(8,128)(2,1)S(1)}, bf16[8,256,128]{2,1,0:T(8,128)(2,1)S(1)}, u32[]{:S(2)}, u32[]{:S(2)}) collective-permute-start(bf16[8,256,128]{2,1,0:T(8,128)(2,1)S(1)} %get-tuple-element.29.last_ref), channel_id=1, source_target_pairs={{0,2},{2,4},{4,6},{6,8},{8,10},{10,12},{12,14},{1,3},{3,5},{5,7},{... | collective-permute-start | bytes 1572872 | tf_op jit(solution)/shard_map/ppermute | solution.py:233
  7.6 22.4 %collective-permute-start.2 = (bf16[8,256,128]{2,1,0:T(8,128)(2,1)S(1)}, bf16[8,256,128]{2,1,0:T(8,128)(2,1)S(1)}, u32[]{:S(2)}, u32[]{:S(2)}) collective-permute-start(bf16[8,256,128]{2,1,0:T(8,128)(2,1)S(1)} %get-tuple-element.30.first_ref), channel_id=1, source_target_pairs={{2,0},{4,2},{6,4},{8,6},{10,8},{12,10},{14,12},{3,1},{5,3},{7,5},{... | collective-permute-start | bytes 1572872 | tf_op jit(solution)/shard_map/ppermute | solution.py:233
  8.9 1.4 %collective-permute-start = (bf16[2,256,128]{2,1,0:T(8,128)(2,1)S(1)}, bf16[2,256,128]{2,1,0:T(8,128)(2,1)S(1)}, u32[]{:S(2)}, u32[]{:S(2)}) collective-permute-start(bf16[2,256,128]{2,1,0:T(8,128)(2,1)S(1)} %get-tuple-element.26), channel_id=1, source_target_pairs={{0,1},{1,0},{2,3},{3,2},{4,5},{5,4},{6,7},{7,6},{8,9},{9,8},{10,11... | collective-permute-start | bytes 393224 | tf_op jit(solution)/shard_map/ppermute | solution.py:208
  12.9 17.2 %collective-permute-start.3 = (bf16[2,256,128]{2,1,0:T(8,128)(2,1)S(1)}, bf16[2,256,128]{2,1,0:T(8,128)(2,1)S(1)}, u32[]{:S(2)}, u32[]{:S(2)}) collective-permute-start(bf16[2,256,128]{2,1,0:T(8,128)(2,1)S(1)} %get-tuple-element.31), channel_id=1, source_target_pairs={{0,1},{1,0},{2,3},{3,2},{4,5},{5,4},{6,7},{7,6},{8,9},{9,8},{10,11... | collective-permute-start | bytes 393224 | tf_op jit(solution)/shard_map/ppermute | solution.py:208
  30.0 6.4 %collective-permute-start.5 = (bf16[2,256,128]{2,1,0:T(8,128)(2,1)S(1)}, bf16[2,256,128]{2,1,0:T(8,128)(2,1)S(1)}, u32[]{:S(2)}, u32[]{:S(2)}) collective-permute-start(bf16[2,256,128]{2,1,0:T(8,128)(2,1)S(1)} %pad_maximum_fusion.2), channel_id=1, source_target_pairs={{0,1},{1,0},{2,3},{3,2},{4,5},{5,4},{6,7},{7,6},{8,9},{9,8},{10,11... | collective-permute-start | bytes 393224 | tf_op jit(solution)/shard_map/ppermute | solution.py:208
  30.1 16.9 %collective-permute-start.6 = (bf16[8,256,128]{2,1,0:T(8,128)(2,1)S(1)}, bf16[8,256,128]{2,1,0:T(8,128)(2,1)S(1)}, u32[]{:S(2)}, u32[]{:S(2)}) collective-permute-start(bf16[8,256,128]{2,1,0:T(8,128)(2,1)S(1)} %get-tuple-element.32.first_ref), channel_id=1, source_target_pairs={{2,0},{4,2},{6,4},{8,6},{10,8},{12,10},{14,12},{3,1},{5,3},{7,5},{... | collective-permute-start | bytes 1572872 | tf_op jit(solution)/shard_map/ppermute | solution.py:233
  31.4 27.1 %collective-permute-start.4 = (bf16[8,256,128]{2,1,0:T(8,128)(2,1)S(1)}, bf16[8,256,128]{2,1,0:T(8,128)(2,1)S(1)}, u32[]{:S(2)}, u32[]{:S(2)}) collective-permute-start(bf16[8,256,128]{2,1,0:T(8,128)(2,1)S(1)} %get-tuple-element.34.last_ref), channel_id=1, source_target_pairs={{0,2},{2,4},{4,6},{6,8},{8,10},{10,12},{12,14},{1,3},{3,5},{5,7},{... | collective-permute-start | bytes 1572872 | tf_op jit(solution)/shard_map/ppermute | solution.py:233
  40.4 20.5 %collective-permute-start.9 = (bf16[256,1024]{1,0:T(8,128)(2,1)S(1)}, bf16[256,1024]{1,0:T(8,128)(2,1)S(1)}, u32[]{:S(2)}, u32[]{:S(2)}) collective-permute-start(bf16[256,1024]{1,0:T(8,128)(2,1)S(1)} %blur_score_pick.2), channel_id=1, source_target_pairs={{4,0},{14,2},{8,4},{2,6},{12,8},{6,10},{0,12},{10,14},{5,1},{15,3}... | collective-permute-start | bytes 1572872 | tf_op jit(solution)/shard_map/ppermute | solution.py:254
  45.4 36.0 %collective-permute-start.12 = (bf16[256,1024]{1,0:T(8,128)(2,1)S(1)}, bf16[256,1024]{1,0:T(8,128)(2,1)S(1)}, u32[]{:S(2)}, u32[]{:S(2)}) collective-permute-start(bf16[256,1024]{1,0:T(8,128)(2,1)S(1)} %blur_score_pick.2), channel_id=1, source_target_pairs={{0,4},{2,14},{4,8},{6,2},{8,12},{10,6},{12,0},{14,10},{1,5},{3,15}... | collective-permute-start | bytes 1572872 | tf_op jit(solution)/shard_map/ppermute | solution.py:255
  58.4 23.0 %collective-permute-start.14 = (bf16[256,1024]{1,0:T(8,128)(2,1)S(1)}, bf16[256,1024]{1,0:T(8,128)(2,1)S(1)}, u32[]{:S(2)}, u32[]{:S(2)}) collective-permute-start(bf16[256,1024]{1,0:T(8,128)(2,1)S(1)} %blur_score_pick.2), channel_id=1, source_target_pairs={{0,2},{2,0},{4,6},{6,4},{8,10},{10,8},{12,14},{14,12},{1,3},{3,1},... | collective-permute-start | bytes 1572872 | tf_op jit(solution)/shard_map/ppermute | solution.py:258
  61.0 31.6 %collective-permute-start.11 = (bf16[2,256,1024]{2,1,0:T(8,128)(2,1)S(1)}, bf16[2,256,1024]{2,1,0:T(8,128)(2,1)S(1)}, u32[]{:S(2)}, u32[]{:S(2)}) collective-permute-start(bf16[2,256,1024]{2,1,0:T(8,128)(2,1)S(1)} %pad_maximum_fusion.refs_0_), channel_id=1, source_target_pairs={{0,1},{1,0},{2,3},{3,2},{4,5},{5,4},{6,7},{7,6},{8,9},{9,8},{10,11... | collective-permute-start | bytes 3145736 | tf_op jit(solution)/shard_map/ppermute | solution.py:208
  61.1 2.8 %collective-permute-start.7 = (bf16[2,256,128]{2,1,0:T(8,128)(2,1)S(1)}, bf16[2,256,128]{2,1,0:T(8,128)(2,1)S(1)}, u32[]{:S(2)}, u32[]{:S(2)}) collective-permute-start(bf16[2,256,128]{2,1,0:T(8,128)(2,1)S(1)} %pad_maximum_fusion.3), channel_id=1, source_target_pairs={{0,1},{1,0},{2,3},{3,2},{4,5},{5,4},{6,7},{7,6},{8,9},{9,8},{10,11... | collective-permute-start | bytes 393224 | tf_op jit(solution)/shard_map/ppermute | solution.py:208
  61.7 22.7 %collective-permute-start.10 = (bf16[256,1024]{1,0:T(8,128)(2,1)S(1)}, bf16[256,1024]{1,0:T(8,128)(2,1)}, u32[]{:S(2)}, u32[]{:S(2)}) collective-permute-start(bf16[256,1024]{1,0:T(8,128)(2,1)S(1)} %collective-permute-done.9), channel_id=1, source_target_pairs={{0,2},{2,0},{4,6},{6,4},{8,10},{10,8},{12,14},{14,12},{1,3},{3,1},... | collective-permute-start | bytes 1572872 | tf_op jit(solution)/shard_map/ppermute | solution.py:259
  67.2 25.4 %collective-permute-start.8 = (bf16[256,1024]{1,0:T(8,128)(2,1)S(1)}, bf16[256,1024]{1,0:T(8,128)(2,1)}, u32[]{:S(2)}, u32[]{:S(2)}) collective-permute-start(bf16[256,1024]{1,0:T(8,128)(2,1)S(1)} %blur_score_pick.3), channel_id=1, source_target_pairs={{4,0},{14,2},{8,4},{2,6},{12,8},{6,10},{0,12},{10,14},{5,1},{15,3}... | collective-permute-start | bytes 1572872 | tf_op jit(solution)/shard_map/ppermute | solution.py:262
  81.4 4.7 %collective-permute-start.13 = (bf16[1,256,1024]{2,1,0:T(8,128)(2,1)S(1)}, bf16[1,256,1024]{2,1,0:T(8,128)(2,1)S(1)}, u32[]{:S(2)}, u32[]{:S(2)}) collective-permute-start(bf16[1,256,1024]{2,1,0:T(8,128)(2,1)S(1)} %bitcast.16), channel_id=1, source_target_pairs={{0,1},{1,0},{2,3},{3,2},{4,5},{5,4},{6,7},{7,6},{8,9},{9,8},{10,11... | collective-permute-start | bytes 1572872 | tf_op jit(solution)/shard_map/ppermute | solution.py:208
  81.5 11.1 %collective-permute-start.15 = (bf16[1,256,1024]{2,1,0:T(8,128)(2,1)S(1)}, bf16[1,256,1024]{2,1,0:T(8,128)(2,1)S(1)}, u32[]{:S(2)}, u32[]{:S(2)}) collective-permute-start(bf16[1,256,1024]{2,1,0:T(8,128)(2,1)S(1)} %bitcast.18), channel_id=1, source_target_pairs={{0,1},{1,0},{2,3},{3,2},{4,5},{5,4},{6,7},{7,6},{8,9},{9,8},{10,11... | collective-permute-start | bytes 1572872 | tf_op jit(solution)/shard_map/ppermute | solution.py:208
  84.4 15.3 %collective-permute-start.18 = (bf16[256,1024]{1,0:T(8,128)(2,1)S(1)}, bf16[256,1024]{1,0:T(8,128)(2,1)}, u32[]{:S(2)}, u32[]{:S(2)}) collective-permute-start(bf16[256,1024]{1,0:T(8,128)(2,1)S(1)} %blur_score_pick.3), channel_id=1, source_target_pairs={{0,2},{2,0},{4,6},{6,4},{8,10},{10,8},{12,14},{14,12},{1,3},{3,1},... | collective-permute-start | bytes 1572872 | tf_op jit(solution)/shard_map/ppermute | solution.py:263
  92.6 15.7 %collective-permute-start.17 = (bf16[256,1024]{1,0:T(8,128)(2,1)S(1)}, bf16[256,1024]{1,0:T(8,128)(2,1)}, u32[]{:S(2)}, u32[]{:S(2)}) collective-permute-start(bf16[256,1024]{1,0:T(8,128)(2,1)S(1)} %blur_score_pick.3), channel_id=1, source_target_pairs={{0,4},{2,14},{4,8},{6,2},{8,12},{10,6},{12,0},{14,10},{1,5},{3,15}... | collective-permute-start | bytes 1572872 | tf_op jit(solution)/shard_map/ppermute | solution.py:269
  94.6 22.0 %collective-permute-start.16 = (bf16[2,256,1024]{2,1,0:T(8,128)(2,1)S(1)}, bf16[2,256,1024]{2,1,0:T(8,128)(2,1)S(1)}, u32[]{:S(2)}, u32[]{:S(2)}) collective-permute-start(bf16[2,256,1024]{2,1,0:T(8,128)(2,1)S(1)} %pad_maximum_fusion.1.refs_0_), channel_id=1, source_target_pairs={{0,1},{1,0},{2,3},{3,2},{4,5},{5,4},{6,7},{7,6},{8,9},{9,8},{10,11... | collective-permute-start | bytes 3145736 | tf_op jit(solution)/shard_map/ppermute | solution.py:208
  94.6 15.0 %collective-permute-start.22 = (bf16[1,256,1024]{2,1,0:T(8,128)(2,1)}, bf16[1,256,1024]{2,1,0:T(8,128)(2,1)}, u32[]{:S(2)}, u32[]{:S(2)}) collective-permute-start(bf16[1,256,1024]{2,1,0:T(8,128)(2,1)} %bitcast.10.refs_6_), channel_id=1, source_target_pairs={{0,1},{1,0},{2,3},{3,2},{4,5},{5,4},{6,7},{7,6},{8,9},{9,8},{10,11... | collective-permute-start | bytes 1572872 | tf_op jit(solution)/shard_map/ppermute | solution.py:208
  95.1 21.4 %collective-permute-start.21 = (bf16[256,1024]{1,0:T(8,128)(2,1)}, bf16[256,1024]{1,0:T(8,128)(2,1)}, u32[]{:S(2)}, u32[]{:S(2)}) collective-permute-start(bf16[256,1024]{1,0:T(8,128)(2,1)} %collective-permute-done.8), channel_id=1, source_target_pairs={{0,2},{2,0},{4,6},{6,4},{8,10},{10,8},{12,14},{14,12},{1,3},{3,1},... | collective-permute-start | bytes 1572872 | tf_op jit(solution)/shard_map/ppermute | solution.py:270
  99.7 16.8 %collective-permute-start.20 = (bf16[1,256,1024]{2,1,0:T(8,128)(2,1)}, bf16[1,256,1024]{2,1,0:T(8,128)(2,1)}, u32[]{:S(2)}, u32[]{:S(2)}) collective-permute-start(bf16[1,256,1024]{2,1,0:T(8,128)(2,1)} %bitcast.9.refs_4_), channel_id=1, source_target_pairs={{0,1},{1,0},{2,3},{3,2},{4,5},{5,4},{6,7},{7,6},{8,9},{9,8},{10,11... | collective-permute-start | bytes 1572872 | tf_op jit(solution)/shard_map/ppermute | solution.py:208
  108.3 8.2 %collective-permute-start.19 = (bf16[1,256,1024]{2,1,0:T(8,128)(2,1)}, bf16[1,256,1024]{2,1,0:T(8,128)(2,1)}, u32[]{:S(2)}, u32[]{:S(2)}) collective-permute-start(bf16[1,256,1024]{2,1,0:T(8,128)(2,1)} %bitcast.8.refs_2_), channel_id=1, source_target_pairs={{0,1},{1,0},{2,3},{3,2},{4,5},{5,4},{6,7},{7,6},{8,9},{9,8},{10,11... | collective-permute-start | bytes 1572872 | tf_op jit(solution)/shard_map/ppermute | solution.py:208
  116.6 2.3 %collective-permute-start.23 = (bf16[1,256,1024]{2,1,0:T(8,128)(2,1)}, bf16[1,256,1024]{2,1,0:T(8,128)(2,1)S(1)}, u32[]{:S(2)}, u32[]{:S(2)}) collective-permute-start(bf16[1,256,1024]{2,1,0:T(8,128)(2,1)} %bitcast.11.refs_6_), channel_id=1, source_target_pairs={{0,1},{1,0},{2,3},{3,2},{4,5},{5,4},{6,7},{7,6},{8,9},{9,8},{10,11... | collective-permute-start | bytes 1572872 | tf_op jit(solution)/shard_map/ppermute | solution.py:208
  (13 other events, 265.8 us)

commit v6 on v5

--- a/solution.py
+++ b/solution.py
@@ -123,18 +123,17 @@
 
 
 def tiles_kernel(place_ref, present_ref, *refs, sources, window):
-    parts = refs[: len(sources)]
+    parts = refs[:sources]
     out_ref, held, tiles, sems, out_sems = refs[-5:]
     blocks, slots = out_ref.shape[:2]
 
     loads = []
-    for n, (part, (first, start)) in enumerate(zip(parts, sources)):
-        if len(part.shape) == 3:
-            target = held.at[pl.ds(first, part.shape[0])]
-        else:
-            target = held.at[first, pl.ds(start, part.shape[0])]
+    first = 0
+    for n, part in enumerate(parts):
+        target = held.at[pl.ds(first, part.shape[0])]
         loads.append(pltpu.make_async_copy(part, target, sems.at[n]))
         loads[-1].start()
+        first += part.shape[0]
     for load in loads:
         load.wait()
 
@@ -163,23 +162,22 @@
 
 
 def make_tiles(window, windows, place, present, sources, earlier):
-    _, frames, rows = sources[0][2].shape
+    frames, rows = sources[0].shape[1:]
+    total = sum(source.shape[0] for source in sources)
     blocks = rows // BLOCK
     slots = place.shape[0] // blocks
     count = len(sources)
-    where = tuple(source[:2] for source in sources)
-    sources = [source[2] for source in sources]
     anywhere = pl.BlockSpec(memory_space=pl.ANY)
     operands = list(sources) + ([] if earlier is None else [earlier])
     return pl.pallas_call(
-        functools.partial(tiles_kernel, sources=where, window=window),
+        functools.partial(tiles_kernel, sources=count, window=window),
         grid_spec=pltpu.PrefetchScalarGridSpec(
             num_scalar_prefetch=2,
             grid=(1,),
             in_specs=[anywhere] * len(operands),
             out_specs=anywhere,
             scratch_shapes=[
-                pltpu.VMEM((10, frames, rows), jnp.bfloat16),
+                pltpu.VMEM((total, frames, rows), jnp.bfloat16),
                 pltpu.VMEM((blocks, slots, BLOCK, BLOCK), jnp.bfloat16),
                 pltpu.SemaphoreType.DMA((count,)),
                 pltpu.SemaphoreType.DMA((blocks,)),
@@ -225,16 +223,20 @@
     away = (slab % col_total != col).astype(jnp.int32)
     within = ids % blocks
     present = partners >= 0
-    part = jnp.where(kind < 2, kind + 2 * away, 2 * kind + away)
-    place = jnp.where(present, part * blocks + within, 0).reshape(-1).astype(jnp.int32)
+    parts_0 = jnp.where(kind == 4, 8 + away, kind + 4 * away)
+    parts_1 = jnp.where(kind < 2, kind + 2 * away, 2 * kind + away)
+    place_0, place_1 = (
+        jnp.where(present, part * blocks + within, 0).reshape(-1).astype(jnp.int32)
+        for part in (parts_0, parts_1)
+    )
     present = present.reshape(-1).astype(jnp.int32)
 
     def halo(first, last):
         return lax.ppermute(last, "row", one_up), lax.ppermute(first, "row", one_down)
 
-    def both(first, *parts):
+    def both(*parts):
         near = jnp.stack(parts, 0)
-        return [(first, 0, near), (first + len(parts), 0, other_col(near))]
+        return [near, other_col(near)]
 
     def corner_of(low, high):
         return other_col(
@@ -254,26 +256,25 @@
     ahead_0 = lax.ppermute(own_0, "row", ahead)
     behind_0 = lax.ppermute(own_0, "row", behind)
     low_1, high_1 = after(low_1, own_0), after(high_1, own_0)
-    ahead_0 = after(ahead_0, low_1, high_1)
     pair_0 = lax.ppermute(after(own_0, low_1, high_1), "row", in_pair)
-    rest_0 = lax.ppermute(ahead_0, "row", in_pair)
     corner_1 = corner_of(low_1, high_1)
     own_1 = make_panel(col_arg, first_1, last_1, low_1, high_1, edge_1, corner_1, gm)
     ahead_1 = lax.ppermute(own_1, "row", ahead)
+    ahead_0 = after(ahead_0, own_1)
+    rest_0 = lax.ppermute(ahead_0, "row", in_pair)
     pair_1 = lax.ppermute(own_1, "row", in_pair)
-    pair_0, rest_0 = after(pair_0, own_1), after(rest_0, own_1)
-    behind_0 = after(behind_0, own_1)
-    sources = both(0, own_0, ahead_0) + both(4, behind_0) + both(6, pair_0)
-    swapped = [source[2] for source in sources]
-    ahead_1 = after(ahead_1, rest_0, *swapped)
+    behind_0, pair_0 = after(behind_0, own_1), after(pair_0, own_1)
+    sources = both(own_0, ahead_0, behind_0, pair_0)
+    ahead_1 = after(ahead_1, behind_0, pair_0)
     behind_1 = lax.ppermute(after(own_1, ahead_1), "row", behind)
+    rest_0 = after(rest_0, ahead_1)
     rest_1 = lax.ppermute(ahead_1, "row", in_pair)
-    pair_1 = after(pair_1, ahead_1)
+    pair_1 = after(pair_1, rest_0)
     behind_1 = after(behind_1, pair_1)
-    out = make_tiles(0, windows, place, present, sources + both(8, rest_0), None)
-    sources = both(0, own_1, ahead_1) + both(4, behind_1) + both(6, pair_1)
-    rest_1 = after(rest_1, out, *(source[2] for source in sources))
-    return make_tiles(1, windows, place, present, sources + both(8, rest_1), out)
+    out = make_tiles(0, windows, place_0, present, sources + both(rest_0), None)
+    sources = both(own_1, ahead_1) + both(behind_1) + both(pair_1)
+    rest_1 = after(rest_1, out, *sources)
+    return make_tiles(1, windows, place_1, present, sources + both(rest_1), out)
 
 
 def solution(mesh):

time: 127 us -> 125 us (0.984)
  starting transfers between devices: 45.7 us -> 27 us
  waiting for transfers between devices: 50.7 us -> 67.9 us
    ppermute x1, starting transfers between devices: 14.2 us -> 3.25 us  [on_device(): ahead_1 = lax.ppermute(own_1, 'row', ahead)]
    ppermute x1, waiting for transfers between devices: 0.01 us -> 8.83 us  [on_device(): pair_1 = lax.ppermute(own_1, 'row', in_pair)]
    ppermute x1, waiting for transfers between devices: 0.01 us -> 7.09 us  [on_device(): behind_0 = lax.ppermute(own_0, 'row', behind)]
    ppermute x1, waiting for transfers between devices: 8.61 us -> 3.44 us  [on_device(): behind_1 = lax.ppermute(after(own_1, ahead_1), 'row', behind)]
    ppermute x1, starting transfers between devices: 4.57 us -> 0.28 us  [on_device(): rest_1 = lax.ppermute(ahead_1, 'row', in_pair)]
    ppermute x1, waiting for transfers between devices: 6.44 us -> 9.76 us  [on_device(): ahead_1 = lax.ppermute(own_1, 'row', ahead)]
    ppermute x12 -> x10, waiting for transfers between devices: 3.37 us -> 6.67 us  [other_col(): return lax.ppermute(value, 'col', [(0, 1), (1, 0)])]
    ppermute x1, starting transfers between devices: 1.96 us -> 0.12 us  [on_device(): rest_0 = lax.ppermute(ahead_0, 'row', in_pair)]
  transfers between devices with their start and end apart: 24 -> 22, of which waited for: 9 -> 14; matrix products, arithmetic and copies ran while one was open for 2% -> 3% of each run, Pallas kernels for 11% -> 12%
where the time goes in v6:
time: 125 us
  waiting for transfers between devices  67.9 us (54%)
  starting transfers between devices  27 us (22%)
  Pallas kernels  22.3 us (18%)
  local copies, waits for them, and re-layouts  5.22 us (4%)
  other arithmetic  1.7 us (1%)
    ppermute x2, waiting for transfers between devices, halo(): lax.ppermute(last, 'row', one_up)  28.7 us
    pallas_call x2, Pallas kernels, make_tiles(): pl.pallas_call(functools.partial(tiles_kernel, sources=count, window=wind...  13.8 us
    ppermute x2, starting transfers between devices, halo(): lax.ppermute(last, 'row', one_up)  9.95 us
    ppermute x1, waiting for transfers between devices, on_device(): ahead_1 = lax.ppermute(own_1, 'row', ahead)  9.76 us
    ppermute x1, waiting for transfers between devices, on_device(): pair_1 = lax.ppermute(own_1, 'row', in_pair)  8.83 us
    ppermute x1, waiting for transfers between devices, on_device(): behind_0 = lax.ppermute(own_0, 'row', behind)  7.09 us
    ppermute x10, waiting for transfers between devices, other_col(): return lax.ppermute(value, 'col', [(0, 1), (1, 0)])  6.67 us
    pallas_call x2, Pallas kernels, make_panel(): pl.pallas_call(panel_kernel, grid=(1,), in_specs=[pl.BlockSpec(memory_spa...  6.52 us
  transfers between devices with their start and end apart: 22, of which 14 were waited for; matrix products, arithmetic and copies ran while one was open for 3% of the time, Pallas kernels for 12%

profile of v6, /device:TPU:0, one launch (start us, length us, event | category | flops | bytes accessed | tf_op | source)
XLA Modules:
  0.0 124.6 jit_solution(11080343566115693030)
XLA Ops:
  0.0 1.6 %copy-done = bf16[2,256,2,8,128]{4,3,2,1,0:T(8,128)(2,1)S(1)} copy-done((bf16[2,256,2,8,128]{4,3,2,1,0:T(8,128)(2,1)S(1)}, bf16[2,256,2,8,128]{4,3,2,1,0:T(8,128)(2,1)}, u32[]{:S(2)}) %copy-start) | copy-done | bytes 2097176
  2.6 4.9 %collective-permute-start.1 = (bf16[8,256,128]{2,1,0:T(8,128)(2,1)S(1)}, bf16[8,256,128]{2,1,0:T(8,128)(2,1)S(1)}, u32[]{:S(2)}, u32[]{:S(2)}) collective-permute-start(bf16[8,256,128]{2,1,0:T(8,128)(2,1)S(1)} %get-tuple-element.29.last_ref), channel_id=1, source_target_pairs={{0,2},{2,4},{4,6},{6,8},{8,10},{10,12},{12,14},{1,3},{3,5},{5,7},{... | collective-permute-start | bytes 1572872 | tf_op jit(solution)/shard_map/ppermute | solution.py:235
  7.5 1.3 %collective-permute-start.2 = (bf16[8,256,128]{2,1,0:T(8,128)(2,1)S(1)}, bf16[8,256,128]{2,1,0:T(8,128)(2,1)S(1)}, u32[]{:S(2)}, u32[]{:S(2)}) collective-permute-start(bf16[8,256,128]{2,1,0:T(8,128)(2,1)S(1)} %get-tuple-element.30.first_ref), channel_id=1, source_target_pairs={{2,0},{4,2},{6,4},{8,6},{10,8},{12,10},{14,12},{3,1},{5,3},{7,5},{... | collective-permute-start | bytes 1572872 | tf_op jit(solution)/shard_map/ppermute | solution.py:235
  8.9 1.3 %collective-permute-done.edge_ref = bf16[2,256,128]{2,1,0:T(8,128)(2,1)S(1)} collective-permute-done((bf16[2,256,128]{2,1,0:T(8,128)(2,1)S(1)}, bf16[2,256,128]{2,1,0:T(8,128)(2,1)S(1)}, u32[]{:S(2)}, u32[]{:S(2)}) %collective-permute-start) | collective-permute-done | bytes 131104 | tf_op jit(solution)/shard_map/ppermute | solution.py:206
  12.7 17.2 %collective-permute-done.1.low_ref = bf16[8,256,128]{2,1,0:T(8,128)(2,1)S(1)} collective-permute-done((bf16[8,256,128]{2,1,0:T(8,128)(2,1)S(1)}, bf16[8,256,128]{2,1,0:T(8,128)(2,1)S(1)}, u32[]{:S(2)}, u32[]{:S(2)}) %collective-permute-start.1) | collective-permute-done | bytes 524320 | tf_op jit(solution)/shard_map/ppermute | solution.py:235
  31.2 5.0 %collective-permute-start.4 = (bf16[8,256,128]{2,1,0:T(8,128)(2,1)S(1)}, bf16[8,256,128]{2,1,0:T(8,128)(2,1)S(1)}, u32[]{:S(2)}, u32[]{:S(2)}) collective-permute-start(bf16[8,256,128]{2,1,0:T(8,128)(2,1)S(1)} %get-tuple-element.34.last_ref), channel_id=1, source_target_pairs={{0,2},{2,4},{4,6},{6,8},{8,10},{10,12},{12,14},{1,3},{3,5},{5,7},{... | collective-permute-start | bytes 1572872 | tf_op jit(solution)/shard_map/ppermute | solution.py:235
  36.4 1.3 %collective-permute-done.5.corner_ref = bf16[2,256,128]{2,1,0:T(8,128)(2,1)S(1)} collective-permute-done((bf16[2,256,128]{2,1,0:T(8,128)(2,1)S(1)}, bf16[2,256,128]{2,1,0:T(8,128)(2,1)S(1)}, u32[]{:S(2)}, u32[]{:S(2)}) %collective-permute-start.5) | collective-permute-done | bytes 131104 | tf_op jit(solution)/shard_map/ppermute | solution.py:206
  37.7 3.2 %blur_score_pick.2 = bf16[256,1024]{1,0:T(8,128)(2,1)S(1)} custom-call(s32[1]{0:T(128)} %bitcast.col_ref, bf16[8,256,128]{2,1,0:T(8,128)(2,1)S(1)} %get-tuple-element.30.first_ref, bf16[8,256,128]{2,1,0:T(8,128)(2,1)S(1)} %get-tuple-element.29.last_ref, bf16[8,256,128]{2,1,0:T(8,128)(2,1)S(1)} %collective-permute-done.1.low_ref, ...), custom_call_target="tpu_custom_call" | custom-call | flops 1 | bytes 1 | tf_op jit(solution)/shard_map/blur_score_pick/pallas_call | solution.py:109
  41.0 5.0 %collective-permute-start.14 = (bf16[256,1024]{1,0:T(8,128)(2,1)S(1)}, bf16[256,1024]{1,0:T(8,128)(2,1)S(1)}, u32[]{:S(2)}, u32[]{:S(2)}) collective-permute-start(bf16[256,1024]{1,0:T(8,128)(2,1)S(1)} %blur_score_pick.2), channel_id=1, source_target_pairs={{4,0},{14,2},{8,4},{2,6},{12,8},{6,10},{0,12},{10,14},{5,1},{15,3}... | collective-permute-start | bytes 1572872 | tf_op jit(solution)/shard_map/ppermute | solution.py:256
  46.0 11.5 %collective-permute-done.4.low_ref = bf16[8,256,128]{2,1,0:T(8,128)(2,1)S(1)} collective-permute-done((bf16[8,256,128]{2,1,0:T(8,128)(2,1)S(1)}, bf16[8,256,128]{2,1,0:T(8,128)(2,1)S(1)}, u32[]{:S(2)}, u32[]{:S(2)}) %collective-permute-start.4) | collective-permute-done | bytes 524320 | tf_op jit(solution)/shard_map/ppermute | solution.py:235
  57.6 2.5 %collective-permute-start.10 = (bf16[256,1024]{1,0:T(8,128)(2,1)S(1)}, bf16[256,1024]{1,0:T(8,128)(2,1)S(1)}, u32[]{:S(2)}, u32[]{:S(2)}) collective-permute-start(bf16[256,1024]{1,0:T(8,128)(2,1)S(1)} %blur_score_pick.2), channel_id=1, source_target_pairs={{0,2},{2,0},{4,6},{6,4},{8,10},{10,8},{12,14},{14,12},{1,3},{3,1},... | collective-permute-start | bytes 1572872 | tf_op jit(solution)/shard_map/ppermute | solution.py:259
  60.2 1.3 %collective-permute-done.7.corner_ref = bf16[2,256,128]{2,1,0:T(8,128)(2,1)S(1)} collective-permute-done((bf16[2,256,128]{2,1,0:T(8,128)(2,1)S(1)}, bf16[2,256,128]{2,1,0:T(8,128)(2,1)S(1)}, u32[]{:S(2)}, u32[]{:S(2)}) %collective-permute-start.7) | collective-permute-done | bytes 131104 | tf_op jit(solution)/shard_map/ppermute | solution.py:206
  61.5 3.3 %blur_score_pick.3 = bf16[256,1024]{1,0:T(8,128)(2,1)S(1)} custom-call(s32[1]{0:T(128)} %bitcast.col_ref, bf16[8,256,128]{2,1,0:T(8,128)(2,1)S(1)} %get-tuple-element.32.first_ref, bf16[8,256,128]{2,1,0:T(8,128)(2,1)S(1)} %get-tuple-element.34.last_ref, bf16[8,256,128]{2,1,0:T(8,128)(2,1)S(1)} %collective-permute-done.4.low_ref, ...), custom_call_target="tpu_custom_call" | custom-call | flops 1 | bytes 1 | tf_op jit(solution)/shard_map/blur_score_pick/pallas_call | solution.py:109
  64.8 7.1 %collective-permute-done.9 = bf16[256,1024]{1,0:T(8,128)(2,1)S(1)} collective-permute-done((bf16[256,1024]{1,0:T(8,128)(2,1)S(1)}, bf16[256,1024]{1,0:T(8,128)(2,1)S(1)}, u32[]{:S(2)}, u32[]{:S(2)}) %collective-permute-start.9) | collective-permute-done | bytes 524320 | tf_op jit(solution)/shard_map/ppermute | solution.py:257
  72.5 3.3 %collective-permute-start.8 = (bf16[256,1024]{1,0:T(8,128)(2,1)S(1)}, bf16[256,1024]{1,0:T(8,128)(2,1)}, u32[]{:S(2)}, u32[]{:S(2)}) collective-permute-start(bf16[256,1024]{1,0:T(8,128)(2,1)S(1)} %blur_score_pick.3), channel_id=1, source_target_pairs={{4,0},{14,2},{8,4},{2,6},{12,8},{6,10},{0,12},{10,14},{5,1},{15,3}... | collective-permute-start | bytes 1572872 | tf_op jit(solution)/shard_map/ppermute | solution.py:262
  75.9 1.9 %collective-permute-start.13 = (bf16[256,1024]{1,0:T(8,128)(2,1)S(1)}, bf16[256,1024]{1,0:T(8,128)(2,1)}, u32[]{:S(2)}, u32[]{:S(2)}) collective-permute-start(bf16[256,1024]{1,0:T(8,128)(2,1)S(1)} %blur_score_pick.3), channel_id=1, source_target_pairs={{0,2},{2,0},{4,6},{6,4},{8,10},{10,8},{12,14},{14,12},{1,3},{3,1},... | collective-permute-start | bytes 1572872 | tf_op jit(solution)/shard_map/ppermute | solution.py:265
  77.8 9.8 %collective-permute-done.8 = bf16[256,1024]{1,0:T(8,128)(2,1)} collective-permute-done((bf16[256,1024]{1,0:T(8,128)(2,1)S(1)}, bf16[256,1024]{1,0:T(8,128)(2,1)}, u32[]{:S(2)}, u32[]{:S(2)}) %collective-permute-start.8) | collective-permute-done | bytes 524320 | tf_op jit(solution)/shard_map/ppermute | solution.py:262
  87.5 3.0 %collective-permute-done.15 = bf16[256,1024]{1,0:T(8,128)(2,1)S(1)} collective-permute-done((bf16[256,1024]{1,0:T(8,128)(2,1)S(1)}, bf16[256,1024]{1,0:T(8,128)(2,1)S(1)}, u32[]{:S(2)}, u32[]{:S(2)}) %collective-permute-start.15) | collective-permute-done | bytes 524320 | tf_op jit(solution)/shard_map/ppermute | solution.py:264
  90.5 1.3 %pad_maximum_fusion.1.refs_0_ = bf16[2,256,1024]{2,1,0:T(8,128)(2,1)S(1)} fusion(bf16[1,256,1024]{2,1,0:T(8,128)(2,1)} %bitcast.3, bf16[1,256,1024]{2,1,0:T(8,128)(2,1)S(1)} %bitcast.12), kind=kLoop, calls=%fused_computation.1 | loop fusion | flops 524288 | bytes 2097152 | tf_op jit(solution)/shard_map/stack | solution.py:238
  92.3 8.8 %collective-permute-done.13 = bf16[256,1024]{1,0:T(8,128)(2,1)} collective-permute-done((bf16[256,1024]{1,0:T(8,128)(2,1)S(1)}, bf16[256,1024]{1,0:T(8,128)(2,1)}, u32[]{:S(2)}, u32[]{:S(2)}) %collective-permute-start.13) | collective-permute-done | bytes 524320 | tf_op jit(solution)/shard_map/ppermute | solution.py:265
  101.4 3.4 %collective-permute-done.12 = bf16[256,1024]{1,0:T(8,128)(2,1)} collective-permute-done((bf16[256,1024]{1,0:T(8,128)(2,1)S(1)}, bf16[256,1024]{1,0:T(8,128)(2,1)}, u32[]{:S(2)}, u32[]{:S(2)}) %collective-permute-start.12) | collective-permute-done | bytes 524320 | tf_op jit(solution)/shard_map/ppermute | solution.py:269
  107.5 6.9 %tiles.2.refs_8_ = bf16[8,16,2,128,128]{4,3,2,1,0:T(8,128)(2,1)} custom-call(s32[128]{0:T(128)} %reshape.18.place_ref, s32[128]{0:T(128)} %reshape.19.present_ref, bf16[4,256,1024]{2,1,0:T(8,128)(2,1)} %copy-done.2, bf16[4,256,1024]{2,1,0:T(8,128)(2,1)} %collective-permute-done.19.refs_1_, bf16[1,256,1024]{2,1,0:T(8,128)(2,1)} %bitcast.17, ...), custom_call_target="tpu_custom_call" | custom-call | flops 1 | bytes 1 | tf_op jit(solution)/shard_map/tiles/pallas_call | solution.py:172
  115.3 1.4 %collective-permute-done.21.refs_7_ = bf16[1,256,1024]{2,1,0:T(8,128)(2,1)S(1)} collective-permute-done((bf16[1,256,1024]{2,1,0:T(8,128)(2,1)}, bf16[1,256,1024]{2,1,0:T(8,128)(2,1)S(1)}, u32[]{:S(2)}, u32[]{:S(2)}) %collective-permute-start.21) | collective-permute-done | bytes 524320 | tf_op jit(solution)/shard_map/ppermute | solution.py:206
  117.5 6.9 %tiles.3 = bf16[8,16,2,128,128]{4,3,2,1,0:T(8,128)(2,1)} custom-call(s32[128]{0:T(128)} %reshape.15.place_ref, s32[128]{0:T(128)} %reshape.19.present_ref, bf16[2,256,1024]{2,1,0:T(8,128)(2,1)} %copy-done.3, bf16[2,256,1024]{2,1,0:T(8,128)(2,1)} %collective-permute-done.11.refs_1_, ...), custom_call_target="tpu_custom_call", output_to_operand_aliasing={{}: (10, {})} | custom-call | flops 1 | bytes 1 | tf_op jit(solution)/shard_map/tiles/pallas_call | solution.py:172
  (54 shorter events, 10.8 us)
Async XLA Ops:
  1.6 36.1 %copy-start.1 = (s32[1024]{0:T(1024)S(1)}, s32[1024]{0:T(1024)}, u32[]{:S(2)}) copy-start(s32[1024]{0:T(1024)} %param.4) | copy-start | bytes 12292
  2.6 27.3 %collective-permute-start.1 = (bf16[8,256,128]{2,1,0:T(8,128)(2,1)S(1)}, bf16[8,256,128]{2,1,0:T(8,128)(2,1)S(1)}, u32[]{:S(2)}, u32[]{:S(2)}) collective-permute-start(bf16[8,256,128]{2,1,0:T(8,128)(2,1)S(1)} %get-tuple-element.29.last_ref), channel_id=1, source_target_pairs={{0,2},{2,4},{4,6},{6,8},{8,10},{10,12},{12,14},{1,3},{3,5},{5,7},{... | collective-permute-start | bytes 1572872 | tf_op jit(solution)/shard_map/ppermute | solution.py:235
  7.5 22.4 %collective-permute-start.2 = (bf16[8,256,128]{2,1,0:T(8,128)(2,1)S(1)}, bf16[8,256,128]{2,1,0:T(8,128)(2,1)S(1)}, u32[]{:S(2)}, u32[]{:S(2)}) collective-permute-start(bf16[8,256,128]{2,1,0:T(8,128)(2,1)S(1)} %get-tuple-element.30.first_ref), channel_id=1, source_target_pairs={{2,0},{4,2},{6,4},{8,6},{10,8},{12,10},{14,12},{3,1},{5,3},{7,5},{... | collective-permute-start | bytes 1572872 | tf_op jit(solution)/shard_map/ppermute | solution.py:235
  8.8 1.4 %collective-permute-start = (bf16[2,256,128]{2,1,0:T(8,128)(2,1)S(1)}, bf16[2,256,128]{2,1,0:T(8,128)(2,1)S(1)}, u32[]{:S(2)}, u32[]{:S(2)}) collective-permute-start(bf16[2,256,128]{2,1,0:T(8,128)(2,1)S(1)} %get-tuple-element.26), channel_id=1, source_target_pairs={{0,1},{1,0},{2,3},{3,2},{4,5},{5,4},{6,7},{7,6},{8,9},{9,8},{10,11... | collective-permute-start | bytes 393224 | tf_op jit(solution)/shard_map/ppermute | solution.py:206
  11.3 1.4 %collective-permute-start.3 = (bf16[2,256,128]{2,1,0:T(8,128)(2,1)S(1)}, bf16[2,256,128]{2,1,0:T(8,128)(2,1)S(1)}, u32[]{:S(2)}, u32[]{:S(2)}) collective-permute-start(bf16[2,256,128]{2,1,0:T(8,128)(2,1)S(1)} %get-tuple-element.31), channel_id=1, source_target_pairs={{0,1},{1,0},{2,3},{3,2},{4,5},{5,4},{6,7},{7,6},{8,9},{9,8},{10,11... | collective-permute-start | bytes 393224 | tf_op jit(solution)/shard_map/ppermute | solution.py:206
  29.9 16.1 %collective-permute-start.6 = (bf16[8,256,128]{2,1,0:T(8,128)(2,1)S(1)}, bf16[8,256,128]{2,1,0:T(8,128)(2,1)S(1)}, u32[]{:S(2)}, u32[]{:S(2)}) collective-permute-start(bf16[8,256,128]{2,1,0:T(8,128)(2,1)S(1)} %get-tuple-element.32.first_ref), channel_id=1, source_target_pairs={{2,0},{4,2},{6,4},{8,6},{10,8},{12,10},{14,12},{3,1},{5,3},{7,5},{... | collective-permute-start | bytes 1572872 | tf_op jit(solution)/shard_map/ppermute | solution.py:235
  31.2 26.4 %collective-permute-start.4 = (bf16[8,256,128]{2,1,0:T(8,128)(2,1)S(1)}, bf16[8,256,128]{2,1,0:T(8,128)(2,1)S(1)}, u32[]{:S(2)}, u32[]{:S(2)}) collective-permute-start(bf16[8,256,128]{2,1,0:T(8,128)(2,1)S(1)} %get-tuple-element.34.last_ref), channel_id=1, source_target_pairs={{0,2},{2,4},{4,6},{6,8},{8,10},{10,12},{12,14},{1,3},{3,5},{5,7},{... | collective-permute-start | bytes 1572872 | tf_op jit(solution)/shard_map/ppermute | solution.py:235
  36.3 1.4 %collective-permute-start.5 = (bf16[2,256,128]{2,1,0:T(8,128)(2,1)S(1)}, bf16[2,256,128]{2,1,0:T(8,128)(2,1)S(1)}, u32[]{:S(2)}, u32[]{:S(2)}) collective-permute-start(bf16[2,256,128]{2,1,0:T(8,128)(2,1)S(1)} %pad_maximum_fusion.2), channel_id=1, source_target_pairs={{0,1},{1,0},{2,3},{3,2},{4,5},{5,4},{6,7},{7,6},{8,9},{9,8},{10,11... | collective-permute-start | bytes 393224 | tf_op jit(solution)/shard_map/ppermute | solution.py:206
  41.0 23.8 %collective-permute-start.14 = (bf16[256,1024]{1,0:T(8,128)(2,1)S(1)}, bf16[256,1024]{1,0:T(8,128)(2,1)S(1)}, u32[]{:S(2)}, u32[]{:S(2)}) collective-permute-start(bf16[256,1024]{1,0:T(8,128)(2,1)S(1)} %blur_score_pick.2), channel_id=1, source_target_pairs={{4,0},{14,2},{8,4},{2,6},{12,8},{6,10},{0,12},{10,14},{5,1},{15,3}... | collective-permute-start | bytes 1572872 | tf_op jit(solution)/shard_map/ppermute | solution.py:256
  46.0 25.9 %collective-permute-start.9 = (bf16[256,1024]{1,0:T(8,128)(2,1)S(1)}, bf16[256,1024]{1,0:T(8,128)(2,1)S(1)}, u32[]{:S(2)}, u32[]{:S(2)}) collective-permute-start(bf16[256,1024]{1,0:T(8,128)(2,1)S(1)} %blur_score_pick.2), channel_id=1, source_target_pairs={{0,4},{2,14},{4,8},{6,2},{8,12},{10,6},{12,0},{14,10},{1,5},{3,15}... | collective-permute-start | bytes 1572872 | tf_op jit(solution)/shard_map/ppermute | solution.py:257
  57.6 14.6 %collective-permute-start.10 = (bf16[256,1024]{1,0:T(8,128)(2,1)S(1)}, bf16[256,1024]{1,0:T(8,128)(2,1)S(1)}, u32[]{:S(2)}, u32[]{:S(2)}) collective-permute-start(bf16[256,1024]{1,0:T(8,128)(2,1)S(1)} %blur_score_pick.2), channel_id=1, source_target_pairs={{0,2},{2,0},{4,6},{6,4},{8,10},{10,8},{12,14},{14,12},{1,3},{3,1},... | collective-permute-start | bytes 1572872 | tf_op jit(solution)/shard_map/ppermute | solution.py:259
  60.1 1.4 %collective-permute-start.7 = (bf16[2,256,128]{2,1,0:T(8,128)(2,1)S(1)}, bf16[2,256,128]{2,1,0:T(8,128)(2,1)S(1)}, u32[]{:S(2)}, u32[]{:S(2)}) collective-permute-start(bf16[2,256,128]{2,1,0:T(8,128)(2,1)S(1)} %pad_maximum_fusion.3), channel_id=1, source_target_pairs={{0,1},{1,0},{2,3},{3,2},{4,5},{5,4},{6,7},{7,6},{8,9},{9,8},{10,11... | collective-permute-start | bytes 393224 | tf_op jit(solution)/shard_map/ppermute | solution.py:206
  72.4 35.1 %copy-start.2 = (bf16[4,256,1024]{2,1,0:T(8,128)(2,1)}, bf16[4,256,1024]{2,1,0:T(8,128)(2,1)S(1)}, u32[]{:S(2)}) copy-start(bf16[4,256,1024]{2,1,0:T(8,128)(2,1)S(1)} %pad_maximum_fusion.refs_0_) | copy-start | bytes 6291460
  72.4 35.1 %collective-permute-start.19 = (bf16[4,256,1024]{2,1,0:T(8,128)(2,1)S(1)}, bf16[4,256,1024]{2,1,0:T(8,128)(2,1)}, u32[]{:S(2)}, u32[]{:S(2)}) collective-permute-start(bf16[4,256,1024]{2,1,0:T(8,128)(2,1)S(1)} %pad_maximum_fusion.refs_0_), channel_id=1, source_target_pairs={{0,1},{1,0},{2,3},{3,2},{4,5},{5,4},{6,7},{7,6},{8,9},{9,8},{10,11... | collective-permute-start | bytes 6291464 | tf_op jit(solution)/shard_map/ppermute | solution.py:206
  72.5 15.0 %collective-permute-start.8 = (bf16[256,1024]{1,0:T(8,128)(2,1)S(1)}, bf16[256,1024]{1,0:T(8,128)(2,1)}, u32[]{:S(2)}, u32[]{:S(2)}) collective-permute-start(bf16[256,1024]{1,0:T(8,128)(2,1)S(1)} %blur_score_pick.3), channel_id=1, source_target_pairs={{4,0},{14,2},{8,4},{2,6},{12,8},{6,10},{0,12},{10,14},{5,1},{15,3}... | collective-permute-start | bytes 1572872 | tf_op jit(solution)/shard_map/ppermute | solution.py:262
  75.8 14.8 %collective-permute-start.15 = (bf16[256,1024]{1,0:T(8,128)(2,1)S(1)}, bf16[256,1024]{1,0:T(8,128)(2,1)S(1)}, u32[]{:S(2)}, u32[]{:S(2)}) collective-permute-start(bf16[256,1024]{1,0:T(8,128)(2,1)S(1)} %collective-permute-done.14), channel_id=1, source_target_pairs={{0,2},{2,0},{4,6},{6,4},{8,10},{10,8},{12,14},{14,12},{1,3},{3,1},... | collective-permute-start | bytes 1572872 | tf_op jit(solution)/shard_map/ppermute | solution.py:264
  75.9 25.2 %collective-permute-start.13 = (bf16[256,1024]{1,0:T(8,128)(2,1)S(1)}, bf16[256,1024]{1,0:T(8,128)(2,1)}, u32[]{:S(2)}, u32[]{:S(2)}) collective-permute-start(bf16[256,1024]{1,0:T(8,128)(2,1)S(1)} %blur_score_pick.3), channel_id=1, source_target_pairs={{0,2},{2,0},{4,6},{6,4},{8,10},{10,8},{12,14},{14,12},{1,3},{3,1},... | collective-permute-start | bytes 1572872 | tf_op jit(solution)/shard_map/ppermute | solution.py:265
  90.5 14.3 %collective-permute-start.12 = (bf16[256,1024]{1,0:T(8,128)(2,1)S(1)}, bf16[256,1024]{1,0:T(8,128)(2,1)}, u32[]{:S(2)}, u32[]{:S(2)}) collective-permute-start(bf16[256,1024]{1,0:T(8,128)(2,1)S(1)} %blur_score_pick.3), channel_id=1, source_target_pairs={{0,4},{2,14},{4,8},{6,2},{8,12},{10,6},{12,0},{14,10},{1,5},{3,15}... | collective-permute-start | bytes 1572872 | tf_op jit(solution)/shard_map/ppermute | solution.py:269
  90.5 14.3 %collective-permute-start.20 = (bf16[1,256,1024]{2,1,0:T(8,128)(2,1)S(1)}, bf16[1,256,1024]{2,1,0:T(8,128)(2,1)S(1)}, u32[]{:S(2)}, u32[]{:S(2)}) collective-permute-start(bf16[1,256,1024]{2,1,0:T(8,128)(2,1)S(1)} %bitcast.16), channel_id=1, source_target_pairs={{0,1},{1,0},{2,3},{3,2},{4,5},{5,4},{6,7},{7,6},{8,9},{9,8},{10,11... | collective-permute-start | bytes 1572872 | tf_op jit(solution)/shard_map/ppermute | solution.py:206
  91.9 22.7 %collective-permute-start.11 = (bf16[2,256,1024]{2,1,0:T(8,128)(2,1)S(1)}, bf16[2,256,1024]{2,1,0:T(8,128)(2,1)}, u32[]{:S(2)}, u32[]{:S(2)}) collective-permute-start(bf16[2,256,1024]{2,1,0:T(8,128)(2,1)S(1)} %pad_maximum_fusion.1.refs_0_), channel_id=1, source_target_pairs={{0,1},{1,0},{2,3},{3,2},{4,5},{5,4},{6,7},{7,6},{8,9},{9,8},{10,11... | collective-permute-start | bytes 3145736 | tf_op jit(solution)/shard_map/ppermute | solution.py:206
  101.1 13.5 %collective-permute-start.18 = (bf16[256,1024]{1,0:T(8,128)(2,1)}, bf16[256,1024]{1,0:T(8,128)(2,1)}, u32[]{:S(2)}, u32[]{:S(2)}) collective-permute-start(bf16[256,1024]{1,0:T(8,128)(2,1)} %collective-permute-done.8), channel_id=1, source_target_pairs={{0,2},{2,0},{4,6},{6,4},{8,10},{10,8},{12,14},{14,12},{1,3},{3,1},... | collective-permute-start | bytes 1572872 | tf_op jit(solution)/shard_map/ppermute | solution.py:271
  104.8 9.6 %collective-permute-start.17 = (bf16[1,256,1024]{2,1,0:T(8,128)(2,1)}, bf16[1,256,1024]{2,1,0:T(8,128)(2,1)}, u32[]{:S(2)}, u32[]{:S(2)}) collective-permute-start(bf16[1,256,1024]{2,1,0:T(8,128)(2,1)} %bitcast.5.refs_4_), channel_id=1, source_target_pairs={{0,1},{1,0},{2,3},{3,2},{4,5},{5,4},{6,7},{7,6},{8,9},{9,8},{10,11... | collective-permute-start | bytes 1572872 | tf_op jit(solution)/shard_map/ppermute | solution.py:206
  105.6 8.9 %collective-permute-start.16 = (bf16[1,256,1024]{2,1,0:T(8,128)(2,1)}, bf16[1,256,1024]{2,1,0:T(8,128)(2,1)}, u32[]{:S(2)}, u32[]{:S(2)}) collective-permute-start(bf16[1,256,1024]{2,1,0:T(8,128)(2,1)} %bitcast.4.refs_2_), channel_id=1, source_target_pairs={{0,1},{1,0},{2,3},{3,2},{4,5},{5,4},{6,7},{7,6},{8,9},{9,8},{10,11... | collective-permute-start | bytes 1572872 | tf_op jit(solution)/shard_map/ppermute | solution.py:206
  114.6 2.1 %collective-permute-start.21 = (bf16[1,256,1024]{2,1,0:T(8,128)(2,1)}, bf16[1,256,1024]{2,1,0:T(8,128)(2,1)S(1)}, u32[]{:S(2)}, u32[]{:S(2)}) collective-permute-start(bf16[1,256,1024]{2,1,0:T(8,128)(2,1)} %bitcast.11.refs_6_), channel_id=1, source_target_pairs={{0,1},{1,0},{2,3},{3,2},{4,5},{5,4},{6,7},{7,6},{8,9},{9,8},{10,11... | collective-permute-start | bytes 1572872 | tf_op jit(solution)/shard_map/ppermute | solution.py:206
  (6 other events, 73.8 us)

commit v7 on v6

--- a/solution.py
+++ b/solution.py
@@ -54,72 +54,175 @@
     )(col, bold)
 
 
-def panel_kernel(
-    col_ref, first_ref, last_ref, low_ref, high_ref, edge_ref, corner_ref, gm_ref, out_ref,
-    planes, scored,
-):
-    slab_y, frames, slab_z = first_ref.shape
-    slab_x = edge_ref.shape[0]
-
-    def along_x(before, here, after):
-        return SIDE * before + CENTRE * here + SIDE * after
-
-    for y in range(slab_y):
-        layers = [ref[y].astype(jnp.float32) for ref in (low_ref, first_ref, last_ref, high_ref)]
-        for x in range(slab_x):
-            planes[x, y + 1] = along_x(*layers[x : x + 3])
-    edges = [corner_ref[0], edge_ref[0], edge_ref[1], corner_ref[1]]
-    edges = [edge.astype(jnp.float32) for edge in edges]
-    for x in range(slab_x):
-        edge = along_x(*edges[x : x + 3])
-        planes[x, 0] = jnp.where(col_ref[0] == 0, 0.0, edge)
-        planes[x, slab_y + 1] = jnp.where(col_ref[0] == 0, edge, 0.0)
-
-    lane = lax.broadcasted_iota(jnp.int32, (frames, slab_z), 1)
-    for x in range(slab_x):
-        for y in range(slab_y):
-            part = along_x(planes[x, y], planes[x, y + 1], planes[x, y + 2])
-            before = jnp.where(lane == 0, 0.0, pltpu.roll(part, 1, 1))
-            after = jnp.where(lane == slab_z - 1, 0.0, pltpu.roll(part, slab_z - 1, 1))
-            smooth = along_x(before, part, after)
-            centred = smooth - jnp.mean(smooth, axis=0, keepdims=True)
-            spread = jnp.mean(centred * centred, axis=0, keepdims=True)
-            value = centred * lax.rsqrt((spread + 1e-05) * frames)
-            start = (x * slab_y + y) * slab_z
-            scored[:, start : start + slab_z] = value.astype(jnp.bfloat16)
-
-    voxels = slab_x * slab_y * slab_z
+def three_taps(before, here, after):
+    return SIDE * before + CENTRE * here + SIDE * after
+
+
+def along_z(part):
+    lane = lax.broadcasted_iota(jnp.int32, part.shape, 1)
+    last = part.shape[1] - 1
+    before = jnp.where(lane == 0, 0.0, pltpu.roll(part, 1, 1))
+    after = jnp.where(lane == last, 0.0, pltpu.roll(part, last, 1))
+    return three_taps(before, part, after)
+
+
+def place_edge(planes, x, edge, col):
+    planes[x, 0] = jnp.where(col == 0, 0.0, edge)
+    planes[x, planes.shape[1] - 1] = jnp.where(col == 0, edge, 0.0)
+
+
+def standardise(smooth):
+    frames = smooth.shape[0]
+    centred = smooth - jnp.mean(smooth, axis=0, keepdims=True)
+    spread = jnp.mean(centred * centred, axis=0, keepdims=True)
+    return (centred * lax.rsqrt((spread + 1e-05) * frames)).astype(jnp.bfloat16)
+
+
+def pick(parts, gm_ref, out_ref):
+    voxels = parts[0].shape[1]
     rows = gm_ref.shape[1]
     step = 2 * BLOCK
     for start in range(0, rows, step):
         wanted = gm_ref[:, start : start + step]
         voxel = lax.broadcasted_iota(jnp.int32, (voxels, step), 0)
         chosen = jnp.where(voxel == wanted, 1.0, 0.0).astype(jnp.bfloat16)
-        picked = jnp.dot(scored[...], chosen, preferred_element_type=jnp.float32)
-        out_ref[:, start : start + step] = picked.astype(jnp.bfloat16)
-
-
-def make_panel(col, first, last, low, high, edge, corner, gm):
-    slab_y, frames, slab_z = first.shape
-    slab_x = edge.shape[0]
-    rows = gm.shape[1]
-    voxels = slab_x * slab_y * slab_z
+        total = jnp.dot(parts[0][...], chosen, preferred_element_type=jnp.float32)
+        for part in parts[1:]:
+            total += jnp.dot(part[...], chosen, preferred_element_type=jnp.float32)
+        out_ref[:, start : start + step] = total.astype(out_ref.dtype)
+
+
+def panel_kernel(
+    place_ref, first_ref, last_ref, low_ref, high_ref, edge_ref, corner_ref, gm_ref, out_ref,
+    planes, scored,
+):
+    slab_y, frames, slab_z = first_ref.shape
+    slab_x = edge_ref.shape[0]
+    for y in range(slab_y):
+        layers = [ref[y].astype(jnp.float32) for ref in (low_ref, first_ref, last_ref, high_ref)]
+        for x in range(slab_x):
+            planes[x, y + 1] = three_taps(*layers[x : x + 3])
+    edges = [corner_ref[0], edge_ref[0], edge_ref[1], corner_ref[1]]
+    edges = [edge.astype(jnp.float32) for edge in edges]
+    for x in range(slab_x):
+        place_edge(planes, x, three_taps(*edges[x : x + 3]), place_ref[0])
+    for x in range(slab_x):
+        for y in range(slab_y):
+            part = three_taps(planes[x, y], planes[x, y + 1], planes[x, y + 2])
+            start = (x * slab_y + y) * slab_z
+            scored[:, start : start + slab_z] = standardise(along_z(part))
+    pick([scored], gm_ref, out_ref)
+
+
+def inner_kernel(
+    place_ref, first_ref, last_ref, edge_ref, gm_ref, out_ref, planes, high, middle, low
+):
+    slab_y, frames, slab_z = first_ref.shape
+    slab_x = edge_ref.shape[0]
+
+    def two_taps(here, other):
+        return CENTRE * here.astype(jnp.float32) + SIDE * other.astype(jnp.float32)
+
+    for y in range(slab_y):
+        planes[0, y + 1] = two_taps(first_ref[y], last_ref[y])
+        planes[1, y + 1] = two_taps(last_ref[y], first_ref[y])
+    for x in range(slab_x):
+        place_edge(planes, x, two_taps(edge_ref[x], edge_ref[1 - x]), place_ref[0])
+    for x in range(slab_x):
+        for y in range(slab_y):
+            part = along_z(three_taps(planes[x, y], planes[x, y + 1], planes[x, y + 2]))
+            start = (x * slab_y + y) * slab_z
+            for term in (high, middle, low):
+                rounded = part.astype(jnp.bfloat16)
+                term[:, start : start + slab_z] = rounded
+                part = part - rounded.astype(jnp.float32)
+    pick([high, middle, low], gm_ref, out_ref)
+
+
+def halo_kernel(
+    place_ref, first_ref, last_ref, beyond_ref, edge_ref, corner_ref, gm_ref, out_ref,
+    planes, scored,
+):
+    slab_y, frames, slab_z = first_ref.shape
+    even = place_ref[1] == 0
+
+    def sides(own, beyond):
+        own, beyond = own.astype(jnp.float32), beyond.astype(jnp.float32)
+        return jnp.where(even, own, beyond), jnp.where(even, beyond, own)
+
+    for y in range(slab_y):
+        own = jnp.where(even, last_ref[y], first_ref[y])
+        planes[0, y + 1], planes[1, y + 1] = sides(own, beyond_ref[y])
+    own = jnp.where(even, edge_ref[1], edge_ref[0])
+    for x, edge in enumerate(sides(own, corner_ref[2])):
+        place_edge(planes, x, edge, place_ref[0])
+    for x in range(2):
+        for y in range(slab_y):
+            part = three_taps(planes[x, y], planes[x, y + 1], planes[x, y + 2])
+            start = (x * slab_y + y) * slab_z
+            scored[:, start : start + slab_z] = along_z(part).astype(jnp.bfloat16)
+    pick([scored], gm_ref, out_ref)
+
+
+def join_kernel(inner_ref, halo_ref, out_ref):
+    for start in range(0, out_ref.shape[1], BLOCK):
+        span = slice(start, start + BLOCK)
+        smooth = inner_ref[:, span] + SIDE * halo_ref[:, span].astype(jnp.float32)
+        out_ref[:, span] = standardise(smooth)
+
+
+def call_on_rows(kernel, dtype, frames, place, operands, scratch, name):
+    rows = operands[-1].shape[1]
     whole = lambda array: pl.BlockSpec(array.shape, lambda _: (0,) * array.ndim)
-    operands = (first, last, low, high, edge, corner, gm)
+    scalars = [] if place is None else [place]
     return pl.pallas_call(
-        panel_kernel,
+        kernel,
         grid=(1,),
-        in_specs=[pl.BlockSpec(memory_space=pltpu.SMEM)] + [whole(value) for value in operands],
+        in_specs=[pl.BlockSpec(memory_space=pltpu.SMEM)] * len(scalars)
+        + [whole(value) for value in operands],
         out_specs=pl.BlockSpec((frames, rows), lambda _: (0, 0)),
-        out_shape=jax.ShapeDtypeStruct((frames, rows), jnp.bfloat16),
-        scratch_shapes=[
-            pltpu.VMEM((slab_x, slab_y + 2, frames, slab_z), jnp.float32),
-            pltpu.VMEM((frames, voxels), jnp.bfloat16),
-        ],
+        out_shape=jax.ShapeDtypeStruct((frames, rows), dtype),
+        scratch_shapes=scratch,
         compiler_params=pltpu.CompilerParams(vmem_limit_bytes=VMEM_BYTES),
         cost_estimate=SMALL,
-        name="blur_score_pick",
-    )(col, *operands)
+        name=name,
+    )(*scalars, *operands)
+
+
+def blur_scratch(first, terms):
+    slab_y, frames, slab_z = first.shape
+    planes = pltpu.VMEM((2, slab_y + 2, frames, slab_z), jnp.float32)
+    return [planes] + [pltpu.VMEM((frames, 2 * slab_y * slab_z), jnp.bfloat16)] * terms
+
+
+def make_panel(place, first, last, low, high, edge, corner, gm):
+    operands = (first, last, low, high, edge, corner, gm)
+    scratch = blur_scratch(first, 1)
+    return call_on_rows(
+        panel_kernel, jnp.bfloat16, first.shape[1], place, operands, scratch, "blur_score_pick"
+    )
+
+
+def make_inner(place, first, last, edge, gm):
+    operands = (first, last, edge, gm)
+    scratch = blur_scratch(first, 3)
+    return call_on_rows(
+        inner_kernel, jnp.float32, first.shape[1], place, operands, scratch, "inner_blur"
+    )
+
+
+def make_halo(place, first, last, beyond, edge, corner, gm):
+    operands = (first, last, beyond, edge, corner, gm)
+    scratch = blur_scratch(first, 1)
+    return call_on_rows(
+        halo_kernel, jnp.bfloat16, first.shape[1], place, operands, scratch, "halo_blur"
+    )
+
+
+def join(inner, halo):
+    return call_on_rows(
+        join_kernel, jnp.bfloat16, inner.shape[0], None, (inner, halo), [], "join_score"
+    )
 
 
 def tiles_kernel(place_ref, present_ref, *refs, sources, window):
@@ -209,10 +312,12 @@
     one_down = [(i + 1, i) for i in range(row_total - 1)]
     ahead = [((i + 2 * (-1) ** i) % row_total, i) for i in range(row_total)]
     behind = [(i, source) for source, i in ahead]
+    two_on = [(i, i + 2 * (-1) ** (i + 1)) for i in range(row_total)]
+    two_on = [(i, target) for i, target in two_on if 0 <= target < row_total]
     in_pair = [(i, i ^ 1) for i in range(row_total)]
 
     gm = gm_index.reshape(1, -1)
-    col_arg = col.reshape(1).astype(jnp.int32)
+    here = jnp.stack([col, row % 2]).astype(jnp.int32)
 
     blocks, slots = partners.shape
     ids = jnp.maximum(partners, 0)
@@ -223,7 +328,8 @@
     away = (slab % col_total != col).astype(jnp.int32)
     within = ids % blocks
     present = partners >= 0
-    parts_0 = jnp.where(kind == 4, 8 + away, kind + 4 * away)
+    parts_0 = jnp.where(kind == 2, 6, jnp.where(kind == 4, 8, jnp.where(kind == 3, 2, kind)))
+    parts_0 += away * jnp.where((kind == 2) | (kind == 4), 1, 3)
     parts_1 = jnp.where(kind < 2, kind + 2 * away, 2 * kind + away)
     place_0, place_1 = (
         jnp.where(present, part * blocks + within, 0).reshape(-1).astype(jnp.int32)
@@ -231,46 +337,44 @@
     )
     present = present.reshape(-1).astype(jnp.int32)
 
-    def halo(first, last):
-        return lax.ppermute(last, "row", one_up), lax.ppermute(first, "row", one_down)
-
     def both(*parts):
         near = jnp.stack(parts, 0)
         return [near, other_col(near)]
 
-    def corner_of(low, high):
-        return other_col(
-            jnp.stack([jnp.where(col == 0, part[-1], part[0]) for part in (low, high)], 0)
-        )
-
     windows = bold.shape[0]
-    first_0, last_0, face_0 = make_faces(0, col_arg, bold)
-    low_0, high_0 = halo(first_0, last_0)
+    gm_pair = lax.ppermute(gm, "row", in_pair)
+    first_0, last_0, face_0 = make_faces(0, here, bold)
+    low_0 = lax.ppermute(last_0, "row", one_up)
+    high_0 = lax.ppermute(first_0, "row", one_down)
     edge_0 = other_col(face_0)
-    first_1, last_1, face_1 = make_faces(1, col_arg, after(bold, edge_0))
+    first_1, last_1, face_1 = make_faces(1, here, after(bold, edge_0))
+    beyond_1 = lax.ppermute(jnp.where(even, first_1, last_1), "row", two_on)
     edge_1 = other_col(face_1)
-    corner_0 = corner_of(low_0, high_0)
-    first_1, last_1 = after(first_1, low_0, high_0, edge_1), after(last_1, low_0, high_0, edge_1)
-    low_1, high_1 = halo(first_1, last_1)
-    own_0 = make_panel(col_arg, first_0, last_0, low_0, high_0, edge_0, corner_0, gm)
+    inner_1 = make_inner(here, first_1, last_1, edge_1, after(gm, gm_pair))
+    beyond_1 = after(beyond_1, inner_1)
+    low_0, high_0 = after(low_0, inner_1), after(high_0, inner_1)
+    ends = [jnp.where(col == 0, part[-1], part[0]) for part in (low_0, high_0, beyond_1)]
+    corner = other_col(jnp.stack(ends, 0))
+    halo_1 = make_halo(here, first_1, last_1, beyond_1, edge_1, corner, gm_pair)
+    halo_1 = lax.ppermute(halo_1, "row", in_pair)
+    own_0 = make_panel(here, first_0, last_0, low_0, high_0, edge_0, corner, gm)
+    halo_1 = after(halo_1, own_0)
     ahead_0 = lax.ppermute(own_0, "row", ahead)
-    behind_0 = lax.ppermute(own_0, "row", behind)
-    low_1, high_1 = after(low_1, own_0), after(high_1, own_0)
-    pair_0 = lax.ppermute(after(own_0, low_1, high_1), "row", in_pair)
-    corner_1 = corner_of(low_1, high_1)
-    own_1 = make_panel(col_arg, first_1, last_1, low_1, high_1, edge_1, corner_1, gm)
+    own_1 = join(inner_1, halo_1)
+    pair_0 = lax.ppermute(after(own_0, halo_1), "row", in_pair)
+    ahead_0 = after(ahead_0, own_1)
+    behind_0 = lax.ppermute(after(own_0, ahead_0), "row", behind)
+    rest_0 = lax.ppermute(ahead_0, "row", in_pair)
     ahead_1 = lax.ppermute(own_1, "row", ahead)
-    ahead_0 = after(ahead_0, own_1)
-    rest_0 = lax.ppermute(ahead_0, "row", in_pair)
     pair_1 = lax.ppermute(own_1, "row", in_pair)
-    behind_0, pair_0 = after(behind_0, own_1), after(pair_0, own_1)
-    sources = both(own_0, ahead_0, behind_0, pair_0)
-    ahead_1 = after(ahead_1, behind_0, pair_0)
+    pair_0 = after(pair_0, ahead_0)
+    ahead_1 = after(ahead_1, pair_0)
     behind_1 = lax.ppermute(after(own_1, ahead_1), "row", behind)
-    rest_0 = after(rest_0, ahead_1)
     rest_1 = lax.ppermute(ahead_1, "row", in_pair)
-    pair_1 = after(pair_1, rest_0)
+    behind_0, rest_0 = after(behind_0, ahead_1), after(rest_0, ahead_1)
+    pair_1 = after(pair_1, rest_0, behind_0)
     behind_1 = after(behind_1, pair_1)
+    sources = both(own_0, ahead_0, pair_0) + both(behind_0)
     out = make_tiles(0, windows, place_0, present, sources + both(rest_0), None)
     sources = both(own_1, ahead_1) + both(behind_1) + both(pair_1)
     rest_1 = after(rest_1, out, *sources)

time: 125 us -> 125 us (level)
  waiting for transfers between devices: 67.9 us -> 51.9 us
  Pallas kernels: 22.3 us -> 31.7 us
  starting transfers between devices: 27 us -> 32.6 us
    ppermute x1, waiting for transfers between devices: 9.76 us -> 2.24 us  [on_device(): ahead_1 = lax.ppermute(own_1, 'row', ahead)]
    pallas_call x2 -> x4, Pallas kernels: 6.52 us -> 13.9 us  [call_on_rows(): pl.pallas_call(kernel, grid=(1,), in_specs=[pl.BlockSpec(memory_space=plt...]
    ppermute x1, waiting for transfers between devices: 8.83 us -> 2.34 us  [on_device(): pair_1 = lax.ppermute(own_1, 'row', in_pair)]
    ppermute x1, starting transfers between devices: 0.28 us -> 4.06 us  [on_device(): rest_1 = lax.ppermute(ahead_1, 'row', in_pair)]
    ppermute x10, waiting for transfers between devices: 6.67 us -> 2.95 us  [other_col(): return lax.ppermute(value, 'col', [(0, 1), (1, 0)])]
    ppermute x1, waiting for transfers between devices: 2.98 us -> 0.01 us  [on_device(): rest_0 = lax.ppermute(ahead_0, 'row', in_pair)]
    ppermute x1, waiting for transfers between devices: 3.44 us -> 6.2 us  [on_device(): behind_1 = lax.ppermute(after(own_1, ahead_1), 'row', behind)]
    ppermute x1, starting transfers between devices: 0.12 us -> 2.48 us  [on_device(): rest_0 = lax.ppermute(ahead_0, 'row', in_pair)]
  transfers between devices with their start and end apart: 22 -> 23, of which waited for: 14 -> 11; matrix products, arithmetic and copies ran while one was open for 3% -> 3% of each run, Pallas kernels for 12% -> 16%
where the time goes in v7:
time: 125 us; the launch traced here: 124 us
  waiting for transfers between devices  51.9 us (42%)
  starting transfers between devices  32.6 us (26%)
  Pallas kernels  31.7 us (25%)
  local copies, waits for them, and re-layouts  5.15 us (4%)
  other arithmetic  2.47 us (2%)
    ppermute x1, waiting for transfers between devices, on_device(): gm_pair = lax.ppermute(gm, 'row', in_pair)  13.9 us
    pallas_call x4, Pallas kernels, call_on_rows(): pl.pallas_call(kernel, grid=(1,), in_specs=[pl.BlockSpec(memory_space=plt...  13.9 us
    pallas_call x2, Pallas kernels, make_tiles(): pl.pallas_call(functools.partial(tiles_kernel, sources=count, window=wind...  13.8 us
    ppermute x1, waiting for transfers between devices, on_device(): behind_0 = lax.ppermute(after(own_0, ahead_0), 'row', behind)  12.6 us
    ppermute x1, waiting for transfers between devices, on_device(): behind_1 = lax.ppermute(after(own_1, ahead_1), 'row', behind)  6.2 us
    ppermute x1, starting transfers between devices, on_device(): low_0 = lax.ppermute(last_0, 'row', one_up)  5.23 us
    ppermute x1, waiting for transfers between devices, on_device(): pair_0 = lax.ppermute(after(own_0, halo_1), 'row', in_pair)  4.43 us
    ppermute x1, waiting for transfers between devices, on_device(): halo_1 = lax.ppermute(halo_1, 'row', in_pair)  4.4 us
  transfers between devices with their start and end apart: 23, of which 11 were waited for; matrix products, arithmetic and copies ran while one was open for 3% of the time, Pallas kernels for 16%

profile of v7, /device:TPU:0, one launch (start us, length us, event | category | flops | bytes accessed | tf_op | source)
XLA Modules:
  0.0 124.4 jit_solution(1151884159497991811)
XLA Ops:
  0.1 1.6 %copy-done = bf16[2,256,2,8,128]{4,3,2,1,0:T(8,128)(2,1)S(1)} copy-done((bf16[2,256,2,8,128]{4,3,2,1,0:T(8,128)(2,1)S(1)}, bf16[2,256,2,8,128]{4,3,2,1,0:T(8,128)(2,1)}, u32[]{:S(2)}) %copy-start) | copy-done | bytes 2097176
  1.7 2.5 %faces.2 = (bf16[8,256,128]{2,1,0:T(8,128)(2,1)}, bf16[8,256,128]{2,1,0:T(8,128)(2,1)}, bf16[2,256,128]{2,1,0:T(8,128)(2,1)S(1)}) custom-call(s32[2]{0:T(128)S(1)} %pad_add_fusion.col_ref.place_ref, bf16[2,256,2,8,128]{4,3,2,1,0:T(8,128)(2,1)S(1)} %copy-done), custom_call_target="tpu_custom_call" | custom-call | flops 1 | bytes 1 | tf_op jit(solution)/shard_map/faces/pallas_call | solution.py:41
  4.7 5.2 %collective-permute-start.4 = (bf16[8,256,128]{2,1,0:T(8,128)(2,1)}, bf16[8,256,128]{2,1,0:T(8,128)(2,1)}, u32[]{:S(2)}, u32[]{:S(2)}) collective-permute-start(bf16[8,256,128]{2,1,0:T(8,128)(2,1)} %get-tuple-element.35.last_ref), channel_id=1, source_target_pairs={{0,2},{2,4},{4,6},{6,8},{8,10},{10,12},{12,14},{1,3},{3,5},{5,7},{... | collective-permute-start | bytes 1572872 | tf_op jit(solution)/shard_map/ppermute | solution.py:347
  14.6 3.9 %collective-permute-start.2 = (s32[1,1024]{1,0:T(1,128)S(1)}, s32[1,1024]{1,0:T(1,128)S(1)}, u32[]{:S(2)}, u32[]{:S(2)}) collective-permute-start(s32[1,1024]{1,0:T(1,128)S(1)} %bitcast.15), channel_id=1, source_target_pairs={{0,2},{2,0},{4,6},{6,4},{8,10},{10,8},{12,14},{14,12},{1,3},{3,1},... | collective-permute-start | bytes 12296 | tf_op jit(solution)/shard_map/ppermute | solution.py:345
  18.6 13.9 %collective-permute-done.2.gm_ref = s32[1,1024]{1,0:T(1,128)S(1)} collective-permute-done((s32[1,1024]{1,0:T(1,128)S(1)}, s32[1,1024]{1,0:T(1,128)S(1)}, u32[]{:S(2)}, u32[]{:S(2)}) %collective-permute-start.2) | collective-permute-done | bytes 4128 | tf_op jit(solution)/shard_map/ppermute | solution.py:345
  32.5 5.7 %inner_blur.1.inner_ref = f32[256,1024]{1,0:T(8,128)S(1)} custom-call(s32[2]{0:T(128)S(1)} %pad_add_fusion.col_ref.place_ref, bf16[8,256,128]{2,1,0:T(8,128)(2,1)S(1)} %get-tuple-element.30.first_ref, bf16[8,256,128]{2,1,0:T(8,128)(2,1)S(1)} %get-tuple-element.31.last_ref, bf16[2,256,128]{2,1,0:T(8,128)(2,1)S(1)} %collective-permute-done.1.edge_ref, ...), custom_call_target="tpu_custom_call" | custom-call | flops 1 | bytes 1 | tf_op jit(solution)/shard_map/inner_blur/pallas_call | solution.py:178
  40.8 2.9 %halo_blur.1 = bf16[256,1024]{1,0:T(8,128)(2,1)S(1)} custom-call(s32[2]{0:T(128)S(1)} %pad_add_fusion.col_ref.place_ref, bf16[8,256,128]{2,1,0:T(8,128)(2,1)S(1)} %get-tuple-element.30.first_ref, bf16[8,256,128]{2,1,0:T(8,128)(2,1)S(1)} %get-tuple-element.31.last_ref, bf16[8,256,128]{2,1,0:T(8,128)(2,1)S(1)} %collective-permute-done.3.beyond_ref, ...), custom_call_target="tpu_custom_call" | custom-call | flops 1 | bytes 1 | tf_op jit(solution)/shard_map/halo_blur/pallas_call | solution.py:178
  43.7 2.5 %collective-permute-start.7 = (bf16[256,1024]{1,0:T(8,128)(2,1)S(1)}, bf16[256,1024]{1,0:T(8,128)(2,1)S(1)}, u32[]{:S(2)}, u32[]{:S(2)}) collective-permute-start(bf16[256,1024]{1,0:T(8,128)(2,1)S(1)} %halo_blur.1), channel_id=1, source_target_pairs={{0,2},{2,0},{4,6},{6,4},{8,10},{10,8},{12,14},{14,12},{1,3},{3,1},... | collective-permute-start | bytes 1572872 | tf_op jit(solution)/shard_map/ppermute | solution.py:359
  46.2 4.8 %blur_score_pick.1 = bf16[256,1024]{1,0:T(8,128)(2,1)S(1)} custom-call(s32[2]{0:T(128)S(1)} %pad_add_fusion.col_ref.place_ref, bf16[8,256,128]{2,1,0:T(8,128)(2,1)} %get-tuple-element.37.first_ref, bf16[8,256,128]{2,1,0:T(8,128)(2,1)} %get-tuple-element.35.last_ref, bf16[8,256,128]{2,1,0:T(8,128)(2,1)} %collective-permute-done.4.low_ref, ...), custom_call_target="tpu_custom_call" | custom-call | flops 1 | bytes 1 | tf_op jit(solution)/shard_map/blur_score_pick/pallas_call | solution.py:178
  51.0 3.0 %collective-permute-start.10 = (bf16[256,1024]{1,0:T(8,128)(2,1)S(1)}, bf16[256,1024]{1,0:T(8,128)(2,1)S(1)}, u32[]{:S(2)}, u32[]{:S(2)}) collective-permute-start(bf16[256,1024]{1,0:T(8,128)(2,1)S(1)} %blur_score_pick.1), channel_id=1, source_target_pairs={{4,0},{14,2},{8,4},{2,6},{12,8},{6,10},{0,12},{10,14},{5,1},{15,3}... | collective-permute-start | bytes 1572872 | tf_op jit(solution)/shard_map/ppermute | solution.py:362
  54.1 4.4 %collective-permute-done.7.halo_ref = bf16[256,1024]{1,0:T(8,128)(2,1)S(1)} collective-permute-done((bf16[256,1024]{1,0:T(8,128)(2,1)S(1)}, bf16[256,1024]{1,0:T(8,128)(2,1)S(1)}, u32[]{:S(2)}, u32[]{:S(2)}) %collective-permute-start.7) | collective-permute-done | bytes 524320 | tf_op jit(solution)/shard_map/ppermute | solution.py:359
  58.5 1.7 %collective-permute-start.9 = (bf16[256,1024]{1,0:T(8,128)(2,1)S(1)}, bf16[256,1024]{1,0:T(8,128)(2,1)S(1)}, u32[]{:S(2)}, u32[]{:S(2)}) collective-permute-start(bf16[256,1024]{1,0:T(8,128)(2,1)S(1)} %blur_score_pick.1), channel_id=1, source_target_pairs={{0,2},{2,0},{4,6},{6,4},{8,10},{10,8},{12,14},{14,12},{1,3},{3,1},... | collective-permute-start | bytes 1572872 | tf_op jit(solution)/shard_map/ppermute | solution.py:364
  60.7 3.3 %collective-permute-start.8 = (bf16[256,1024]{1,0:T(8,128)(2,1)S(1)}, bf16[256,1024]{1,0:T(8,128)(2,1)}, u32[]{:S(2)}, u32[]{:S(2)}) collective-permute-start(bf16[256,1024]{1,0:T(8,128)(2,1)S(1)} %join_score.1), channel_id=1, source_target_pairs={{4,0},{14,2},{8,4},{2,6},{12,8},{6,10},{0,12},{10,14},{5,1},{15,3}... | collective-permute-start | bytes 1572872 | tf_op jit(solution)/shard_map/ppermute | solution.py:368
  64.0 2.3 %collective-permute-done.10 = bf16[256,1024]{1,0:T(8,128)(2,1)S(1)} collective-permute-done((bf16[256,1024]{1,0:T(8,128)(2,1)S(1)}, bf16[256,1024]{1,0:T(8,128)(2,1)S(1)}, u32[]{:S(2)}, u32[]{:S(2)}) %collective-permute-start.10) | collective-permute-done | bytes 524320 | tf_op jit(solution)/shard_map/ppermute | solution.py:362
  66.3 2.5 %collective-permute-start.14 = (bf16[256,1024]{1,0:T(8,128)(2,1)S(1)}, bf16[256,1024]{1,0:T(8,128)(2,1)S(1)}, u32[]{:S(2)}, u32[]{:S(2)}) collective-permute-start(bf16[256,1024]{1,0:T(8,128)(2,1)S(1)} %collective-permute-done.10), channel_id=1, source_target_pairs={{0,2},{2,0},{4,6},{6,4},{8,10},{10,8},{12,14},{14,12},{1,3},{3,1},... | collective-permute-start | bytes 1572872 | tf_op jit(solution)/shard_map/ppermute | solution.py:367
  68.9 4.4 %collective-permute-done.9 = bf16[256,1024]{1,0:T(8,128)(2,1)S(1)} collective-permute-done((bf16[256,1024]{1,0:T(8,128)(2,1)S(1)}, bf16[256,1024]{1,0:T(8,128)(2,1)S(1)}, u32[]{:S(2)}, u32[]{:S(2)}) %collective-permute-start.9) | collective-permute-done | bytes 524320 | tf_op jit(solution)/shard_map/ppermute | solution.py:364
  73.6 1.8 %collective-permute-start.13 = (bf16[256,1024]{1,0:T(8,128)(2,1)S(1)}, bf16[256,1024]{1,0:T(8,128)(2,1)S(1)}, u32[]{:S(2)}, u32[]{:S(2)}) collective-permute-start(bf16[256,1024]{1,0:T(8,128)(2,1)S(1)} %join_score.1), channel_id=1, source_target_pairs={{0,2},{2,0},{4,6},{6,4},{8,10},{10,8},{12,14},{14,12},{1,3},{3,1},... | collective-permute-start | bytes 1572872 | tf_op jit(solution)/shard_map/ppermute | solution.py:369
  75.4 2.2 %collective-permute-done.8 = bf16[256,1024]{1,0:T(8,128)(2,1)} collective-permute-done((bf16[256,1024]{1,0:T(8,128)(2,1)S(1)}, bf16[256,1024]{1,0:T(8,128)(2,1)}, u32[]{:S(2)}, u32[]{:S(2)}) %collective-permute-start.8) | collective-permute-done | bytes 524320 | tf_op jit(solution)/shard_map/ppermute | solution.py:368
  77.8 12.6 %collective-permute-done.15 = bf16[256,1024]{1,0:T(8,128)(2,1)S(1)} collective-permute-done((bf16[256,1024]{1,0:T(8,128)(2,1)S(1)}, bf16[256,1024]{1,0:T(8,128)(2,1)S(1)}, u32[]{:S(2)}, u32[]{:S(2)}) %collective-permute-start.15) | collective-permute-done | bytes 524320 | tf_op jit(solution)/shard_map/ppermute | solution.py:366
  92.0 2.3 %collective-permute-done.13 = bf16[256,1024]{1,0:T(8,128)(2,1)S(1)} collective-permute-done((bf16[256,1024]{1,0:T(8,128)(2,1)S(1)}, bf16[256,1024]{1,0:T(8,128)(2,1)S(1)}, u32[]{:S(2)}, u32[]{:S(2)}) %collective-permute-start.13) | collective-permute-done | bytes 524320 | tf_op jit(solution)/shard_map/ppermute | solution.py:369
  94.4 6.2 %collective-permute-done.12 = bf16[256,1024]{1,0:T(8,128)(2,1)} collective-permute-done((bf16[256,1024]{1,0:T(8,128)(2,1)S(1)}, bf16[256,1024]{1,0:T(8,128)(2,1)}, u32[]{:S(2)}, u32[]{:S(2)}) %collective-permute-start.12) | collective-permute-done | bytes 524320 | tf_op jit(solution)/shard_map/ppermute | solution.py:372
  100.6 4.1 %collective-permute-start.18 = (bf16[256,1024]{1,0:T(8,128)(2,1)}, bf16[256,1024]{1,0:T(8,128)(2,1)}, u32[]{:S(2)}, u32[]{:S(2)}) collective-permute-start(bf16[256,1024]{1,0:T(8,128)(2,1)} %collective-permute-done.8), channel_id=1, source_target_pairs={{0,2},{2,0},{4,6},{6,4},{8,10},{10,8},{12,14},{14,12},{1,3},{3,1},... | collective-permute-start | bytes 1572872 | tf_op jit(solution)/shard_map/ppermute | solution.py:373
  106.9 6.9 %tiles.2.refs_8_ = bf16[8,16,2,128,128]{4,3,2,1,0:T(8,128)(2,1)} custom-call(s32[128]{0:T(128)} %reshape.14.place_ref, s32[128]{0:T(128)} %reshape.15.present_ref, bf16[3,256,1024]{2,1,0:T(8,128)(2,1)} %copy-done.3, bf16[3,256,1024]{2,1,0:T(8,128)(2,1)} %collective-permute-done.19.refs_1_, bf16[1,256,1024]{2,1,0:T(8,128)(2,1)} %bitcast.23, ...), custom_call_target="tpu_custom_call" | custom-call | flops 1 | bytes 1 | tf_op jit(solution)/shard_map/tiles/pallas_call | solution.py:275
  117.3 6.9 %tiles.3 = bf16[8,16,2,128,128]{4,3,2,1,0:T(8,128)(2,1)} custom-call(s32[128]{0:T(128)} %reshape.12.place_ref, s32[128]{0:T(128)} %reshape.15.present_ref, bf16[2,256,1024]{2,1,0:T(8,128)(2,1)} %copy-done.4, bf16[2,256,1024]{2,1,0:T(8,128)(2,1)} %collective-permute-done.11.refs_1_, ...), custom_call_target="tpu_custom_call", output_to_operand_aliasing={{}: (10, {})} | custom-call | flops 1 | bytes 1 | tf_op jit(solution)/shard_map/tiles/pallas_call | solution.py:275
  (66 shorter events, 16.0 us)
Async XLA Ops:
  4.2 7.0 %collective-permute-start = (bf16[2,256,128]{2,1,0:T(8,128)(2,1)S(1)}, bf16[2,256,128]{2,1,0:T(8,128)(2,1)S(1)}, u32[]{:S(2)}, u32[]{:S(2)}) collective-permute-start(bf16[2,256,128]{2,1,0:T(8,128)(2,1)S(1)} %get-tuple-element.28), channel_id=1, source_target_pairs={{0,1},{1,0},{2,3},{3,2},{4,5},{5,4},{6,7},{7,6},{8,9},{9,8},{10,11... | collective-permute-start | bytes 393224 | tf_op jit(solution)/shard_map/ppermute | solution.py:309
  4.7 33.6 %collective-permute-start.4 = (bf16[8,256,128]{2,1,0:T(8,128)(2,1)}, bf16[8,256,128]{2,1,0:T(8,128)(2,1)}, u32[]{:S(2)}, u32[]{:S(2)}) collective-permute-start(bf16[8,256,128]{2,1,0:T(8,128)(2,1)} %get-tuple-element.35.last_ref), channel_id=1, source_target_pairs={{0,2},{2,4},{4,6},{6,8},{8,10},{10,12},{12,14},{1,3},{3,5},{5,7},{... | collective-permute-start | bytes 1572872 | tf_op jit(solution)/shard_map/ppermute | solution.py:347
  9.9 28.3 %collective-permute-start.5 = (bf16[8,256,128]{2,1,0:T(8,128)(2,1)}, bf16[8,256,128]{2,1,0:T(8,128)(2,1)}, u32[]{:S(2)}, u32[]{:S(2)}) collective-permute-start(bf16[8,256,128]{2,1,0:T(8,128)(2,1)} %get-tuple-element.37.first_ref), channel_id=1, source_target_pairs={{2,0},{4,2},{6,4},{8,6},{10,8},{12,10},{14,12},{3,1},{5,3},{7,5},{... | collective-permute-start | bytes 1572872 | tf_op jit(solution)/shard_map/ppermute | solution.py:348
  12.9 26.3 %collective-permute-start.3 = (bf16[8,256,128]{2,1,0:T(8,128)(2,1)S(1)}, bf16[8,256,128]{2,1,0:T(8,128)(2,1)S(1)}, u32[]{:S(2)}, u32[]{:S(2)}) collective-permute-start(bf16[8,256,128]{2,1,0:T(8,128)(2,1)S(1)} %broadcast_select_fusion), channel_id=1, source_target_pairs={{2,6},{4,0},{6,10},{8,4},{10,14},{12,8},{3,7},{5,1},{7,11},{9,5},{... | collective-permute-start | bytes 1572872 | tf_op jit(solution)/shard_map/ppermute | solution.py:351
  14.3 18.2 %collective-permute-start.1 = (bf16[2,256,128]{2,1,0:T(8,128)(2,1)S(1)}, bf16[2,256,128]{2,1,0:T(8,128)(2,1)S(1)}, u32[]{:S(2)}, u32[]{:S(2)}) collective-permute-start(bf16[2,256,128]{2,1,0:T(8,128)(2,1)S(1)} %get-tuple-element.32), channel_id=1, source_target_pairs={{0,1},{1,0},{2,3},{3,2},{4,5},{5,4},{6,7},{7,6},{8,9},{9,8},{10,11... | collective-permute-start | bytes 393224 | tf_op jit(solution)/shard_map/ppermute | solution.py:309
  14.6 17.9 %collective-permute-start.2 = (s32[1,1024]{1,0:T(1,128)S(1)}, s32[1,1024]{1,0:T(1,128)S(1)}, u32[]{:S(2)}, u32[]{:S(2)}) collective-permute-start(s32[1,1024]{1,0:T(1,128)S(1)} %bitcast.15), channel_id=1, source_target_pairs={{0,2},{2,0},{4,6},{6,4},{8,10},{10,8},{12,14},{14,12},{1,3},{3,1},... | collective-permute-start | bytes 12296 | tf_op jit(solution)/shard_map/ppermute | solution.py:345
  39.2 1.5 %collective-permute-start.6 = (bf16[3,256,128]{2,1,0:T(8,128)(2,1)S(1)}, bf16[3,256,128]{2,1,0:T(8,128)(2,1)S(1)}, u32[]{:S(2)}, u32[]{:S(2)}) collective-permute-start(bf16[3,256,128]{2,1,0:T(8,128)(2,1)S(1)} %pad_maximum_fusion.2), channel_id=1, source_target_pairs={{0,1},{1,0},{2,3},{3,2},{4,5},{5,4},{6,7},{7,6},{8,9},{9,8},{10,11... | collective-permute-start | bytes 589832 | tf_op jit(solution)/shard_map/ppermute | solution.py:309
  43.7 14.8 %collective-permute-start.7 = (bf16[256,1024]{1,0:T(8,128)(2,1)S(1)}, bf16[256,1024]{1,0:T(8,128)(2,1)S(1)}, u32[]{:S(2)}, u32[]{:S(2)}) collective-permute-start(bf16[256,1024]{1,0:T(8,128)(2,1)S(1)} %halo_blur.1), channel_id=1, source_target_pairs={{0,2},{2,0},{4,6},{6,4},{8,10},{10,8},{12,14},{14,12},{1,3},{3,1},... | collective-permute-start | bytes 1572872 | tf_op jit(solution)/shard_map/ppermute | solution.py:359
  51.0 15.3 %collective-permute-start.10 = (bf16[256,1024]{1,0:T(8,128)(2,1)S(1)}, bf16[256,1024]{1,0:T(8,128)(2,1)S(1)}, u32[]{:S(2)}, u32[]{:S(2)}) collective-permute-start(bf16[256,1024]{1,0:T(8,128)(2,1)S(1)} %blur_score_pick.1), channel_id=1, source_target_pairs={{4,0},{14,2},{8,4},{2,6},{12,8},{6,10},{0,12},{10,14},{5,1},{15,3}... | collective-permute-start | bytes 1572872 | tf_op jit(solution)/shard_map/ppermute | solution.py:362
  58.5 14.8 %collective-permute-start.9 = (bf16[256,1024]{1,0:T(8,128)(2,1)S(1)}, bf16[256,1024]{1,0:T(8,128)(2,1)S(1)}, u32[]{:S(2)}, u32[]{:S(2)}) collective-permute-start(bf16[256,1024]{1,0:T(8,128)(2,1)S(1)} %blur_score_pick.1), channel_id=1, source_target_pairs={{0,2},{2,0},{4,6},{6,4},{8,10},{10,8},{12,14},{14,12},{1,3},{3,1},... | collective-permute-start | bytes 1572872 | tf_op jit(solution)/shard_map/ppermute | solution.py:364
  60.7 17.0 %collective-permute-start.8 = (bf16[256,1024]{1,0:T(8,128)(2,1)S(1)}, bf16[256,1024]{1,0:T(8,128)(2,1)}, u32[]{:S(2)}, u32[]{:S(2)}) collective-permute-start(bf16[256,1024]{1,0:T(8,128)(2,1)S(1)} %join_score.1), channel_id=1, source_target_pairs={{4,0},{14,2},{8,4},{2,6},{12,8},{6,10},{0,12},{10,14},{5,1},{15,3}... | collective-permute-start | bytes 1572872 | tf_op jit(solution)/shard_map/ppermute | solution.py:368
  66.3 24.0 %collective-permute-start.14 = (bf16[256,1024]{1,0:T(8,128)(2,1)S(1)}, bf16[256,1024]{1,0:T(8,128)(2,1)S(1)}, u32[]{:S(2)}, u32[]{:S(2)}) collective-permute-start(bf16[256,1024]{1,0:T(8,128)(2,1)S(1)} %collective-permute-done.10), channel_id=1, source_target_pairs={{0,2},{2,0},{4,6},{6,4},{8,10},{10,8},{12,14},{14,12},{1,3},{3,1},... | collective-permute-start | bytes 1572872 | tf_op jit(solution)/shard_map/ppermute | solution.py:367
  68.8 21.6 %collective-permute-start.15 = (bf16[256,1024]{1,0:T(8,128)(2,1)S(1)}, bf16[256,1024]{1,0:T(8,128)(2,1)S(1)}, u32[]{:S(2)}, u32[]{:S(2)}) collective-permute-start(bf16[256,1024]{1,0:T(8,128)(2,1)S(1)} %blur_score_pick.1), channel_id=1, source_target_pairs={{0,4},{2,14},{4,8},{6,2},{8,12},{10,6},{12,0},{14,10},{1,5},{3,15}... | collective-permute-start | bytes 1572872 | tf_op jit(solution)/shard_map/ppermute | solution.py:366
  73.5 33.5 %copy-start.3 = (bf16[3,256,1024]{2,1,0:T(8,128)(2,1)}, bf16[3,256,1024]{2,1,0:T(8,128)(2,1)S(1)}, u32[]{:S(2)}) copy-start(bf16[3,256,1024]{2,1,0:T(8,128)(2,1)S(1)} %pad_maximum_fusion.refs_0_) | copy-start | bytes 4718596
  73.5 33.4 %collective-permute-start.19 = (bf16[3,256,1024]{2,1,0:T(8,128)(2,1)S(1)}, bf16[3,256,1024]{2,1,0:T(8,128)(2,1)}, u32[]{:S(2)}, u32[]{:S(2)}) collective-permute-start(bf16[3,256,1024]{2,1,0:T(8,128)(2,1)S(1)} %pad_maximum_fusion.refs_0_), channel_id=1, source_target_pairs={{0,1},{1,0},{2,3},{3,2},{4,5},{5,4},{6,7},{7,6},{8,9},{9,8},{10,11... | collective-permute-start | bytes 4718600 | tf_op jit(solution)/shard_map/ppermute | solution.py:309
  73.6 20.8 %collective-permute-start.13 = (bf16[256,1024]{1,0:T(8,128)(2,1)S(1)}, bf16[256,1024]{1,0:T(8,128)(2,1)S(1)}, u32[]{:S(2)}, u32[]{:S(2)}) collective-permute-start(bf16[256,1024]{1,0:T(8,128)(2,1)S(1)} %join_score.1), channel_id=1, source_target_pairs={{0,2},{2,0},{4,6},{6,4},{8,10},{10,8},{12,14},{14,12},{1,3},{3,1},... | collective-permute-start | bytes 1572872 | tf_op jit(solution)/shard_map/ppermute | solution.py:369
  77.6 22.9 %collective-permute-start.12 = (bf16[256,1024]{1,0:T(8,128)(2,1)S(1)}, bf16[256,1024]{1,0:T(8,128)(2,1)}, u32[]{:S(2)}, u32[]{:S(2)}) collective-permute-start(bf16[256,1024]{1,0:T(8,128)(2,1)S(1)} %join_score.1), channel_id=1, source_target_pairs={{0,4},{2,14},{4,8},{6,2},{8,12},{10,6},{12,0},{14,10},{1,5},{3,15}... | collective-permute-start | bytes 1572872 | tf_op jit(solution)/shard_map/ppermute | solution.py:372
  90.4 14.3 %collective-permute-start.20 = (bf16[1,256,1024]{2,1,0:T(8,128)(2,1)S(1)}, bf16[1,256,1024]{2,1,0:T(8,128)(2,1)S(1)}, u32[]{:S(2)}, u32[]{:S(2)}) collective-permute-start(bf16[1,256,1024]{2,1,0:T(8,128)(2,1)S(1)} %bitcast.22), channel_id=1, source_target_pairs={{0,1},{1,0},{2,3},{3,2},{4,5},{5,4},{6,7},{7,6},{8,9},{9,8},{10,11... | collective-permute-start | bytes 1572872 | tf_op jit(solution)/shard_map/ppermute | solution.py:309
  90.4 14.3 %collective-permute-start.21 = (bf16[1,256,1024]{2,1,0:T(8,128)(2,1)S(1)}, bf16[1,256,1024]{2,1,0:T(8,128)(2,1)S(1)}, u32[]{:S(2)}, u32[]{:S(2)}) collective-permute-start(bf16[1,256,1024]{2,1,0:T(8,128)(2,1)S(1)} %bitcast.20), channel_id=1, source_target_pairs={{0,1},{1,0},{2,3},{3,2},{4,5},{5,4},{6,7},{7,6},{8,9},{9,8},{10,11... | collective-permute-start | bytes 1572872 | tf_op jit(solution)/shard_map/ppermute | solution.py:309
  94.4 19.9 %collective-permute-start.11 = (bf16[2,256,1024]{2,1,0:T(8,128)(2,1)S(1)}, bf16[2,256,1024]{2,1,0:T(8,128)(2,1)}, u32[]{:S(2)}, u32[]{:S(2)}) collective-permute-start(bf16[2,256,1024]{2,1,0:T(8,128)(2,1)S(1)} %pad_maximum_fusion.1.refs_0_), channel_id=1, source_target_pairs={{0,1},{1,0},{2,3},{3,2},{4,5},{5,4},{6,7},{7,6},{8,9},{9,8},{10,11... | collective-permute-start | bytes 3145736 | tf_op jit(solution)/shard_map/ppermute | solution.py:309
  100.6 13.7 %collective-permute-start.18 = (bf16[256,1024]{1,0:T(8,128)(2,1)}, bf16[256,1024]{1,0:T(8,128)(2,1)}, u32[]{:S(2)}, u32[]{:S(2)}) collective-permute-start(bf16[256,1024]{1,0:T(8,128)(2,1)} %collective-permute-done.8), channel_id=1, source_target_pairs={{0,2},{2,0},{4,6},{6,4},{8,10},{10,8},{12,14},{14,12},{1,3},{3,1},... | collective-permute-start | bytes 1572872 | tf_op jit(solution)/shard_map/ppermute | solution.py:373
  104.7 9.7 %collective-permute-start.17 = (bf16[1,256,1024]{2,1,0:T(8,128)(2,1)S(1)}, bf16[1,256,1024]{2,1,0:T(8,128)(2,1)}, u32[]{:S(2)}, u32[]{:S(2)}) collective-permute-start(bf16[1,256,1024]{2,1,0:T(8,128)(2,1)S(1)} %bitcast.18), channel_id=1, source_target_pairs={{0,1},{1,0},{2,3},{3,2},{4,5},{5,4},{6,7},{7,6},{8,9},{9,8},{10,11... | collective-permute-start | bytes 1572872 | tf_op jit(solution)/shard_map/ppermute | solution.py:309
  105.4 8.9 %collective-permute-start.16 = (bf16[1,256,1024]{2,1,0:T(8,128)(2,1)}, bf16[1,256,1024]{2,1,0:T(8,128)(2,1)}, u32[]{:S(2)}, u32[]{:S(2)}) collective-permute-start(bf16[1,256,1024]{2,1,0:T(8,128)(2,1)} %bitcast.5.refs_2_), channel_id=1, source_target_pairs={{0,1},{1,0},{2,3},{3,2},{4,5},{5,4},{6,7},{7,6},{8,9},{9,8},{10,11... | collective-permute-start | bytes 1572872 | tf_op jit(solution)/shard_map/ppermute | solution.py:309
  114.3 2.2 %collective-permute-start.22 = (bf16[1,256,1024]{2,1,0:T(8,128)(2,1)}, bf16[1,256,1024]{2,1,0:T(8,128)(2,1)S(1)}, u32[]{:S(2)}, u32[]{:S(2)}) collective-permute-start(bf16[1,256,1024]{2,1,0:T(8,128)(2,1)} %bitcast.12.refs_6_), channel_id=1, source_target_pairs={{0,1},{1,0},{2,3},{3,2},{4,5},{5,4},{6,7},{7,6},{8,9},{9,8},{10,11... | collective-permute-start | bytes 1572872 | tf_op jit(solution)/shard_map/ppermute | solution.py:309
  (11 other events, 119.1 us)

commit v8 on v7

--- a/solution.py
+++ b/solution.py
@@ -12,7 +12,7 @@
 SIDE = math.exp(-0.5) / (1.0 + 2.0 * math.exp(-0.5))
 CENTRE = 1.0 / (1.0 + 2.0 * math.exp(-0.5))
 SMALL = pl.CostEstimate(flops=1, bytes_accessed=1, transcendentals=0)
-VMEM_BYTES = 24 * 1024 * 1024
+VMEM_BYTES = 20 * 1024 * 1024
 TILES_VMEM_BYTES = 60 * 1024 * 1024
 
 
@@ -234,14 +234,14 @@
     first = 0
     for n, part in enumerate(parts):
         target = held.at[pl.ds(first, part.shape[0])]
+        first += part.shape[0]
         loads.append(pltpu.make_async_copy(part, target, sems.at[n]))
         loads[-1].start()
-        first += part.shape[0]
     for load in loads:
         load.wait()
 
-    def partner(index):
-        place = place_ref[index]
+    def partner(block, slot):
+        place = place_ref[block, slot]
         start = pl.multiple_of(lax.rem(place, blocks) * BLOCK, BLOCK)
         return held[lax.div(place, blocks), :, pl.ds(start, BLOCK)]
 
@@ -249,12 +249,11 @@
     for block in range(blocks):
         own = held[0, :, block * BLOCK : (block + 1) * BLOCK].T
         for slot in range(0, slots, 2):
-            index = block * slots + slot
-            pair = jnp.concatenate([partner(index), partner(index + 1)], axis=1)
+            pair = jnp.concatenate([partner(block, slot), partner(block, slot + 1)], axis=1)
             both = jnp.dot(own, pair, preferred_element_type=jnp.float32)
             for n in range(2):
                 tile = both[:, n * BLOCK : (n + 1) * BLOCK]
-                tile = jnp.where(present_ref[index + n] != 0, tile, 0.0)
+                tile = jnp.where(present_ref[block, slot + n] != 0, tile, 0.0)
                 tiles[block, slot + n] = tile.astype(jnp.bfloat16)
         stores.append(
             pltpu.make_async_copy(tiles.at[block], out_ref.at[block, :, window], out_sems.at[block])
@@ -268,7 +267,7 @@
     frames, rows = sources[0].shape[1:]
     total = sum(source.shape[0] for source in sources)
     blocks = rows // BLOCK
-    slots = place.shape[0] // blocks
+    slots = place.shape[1]
     count = len(sources)
     anywhere = pl.BlockSpec(memory_space=pl.ANY)
     operands = list(sources) + ([] if earlier is None else [earlier])
@@ -288,7 +287,7 @@
         ),
         out_shape=jax.ShapeDtypeStruct((blocks, slots, windows, BLOCK, BLOCK), jnp.bfloat16),
         input_output_aliases={} if earlier is None else {2 + count: 0},
-        compiler_params=pltpu.CompilerParams(vmem_limit_bytes=TILES_VMEM_BYTES),
+        compiler_params=pltpu.CompilerParams(vmem_limit_bytes=VMEM_BYTES if window else TILES_VMEM_BYTES),
         cost_estimate=SMALL,
         name="tiles",
     )(place, present, *operands)
@@ -328,14 +327,13 @@
     away = (slab % col_total != col).astype(jnp.int32)
     within = ids % blocks
     present = partners >= 0
-    parts_0 = jnp.where(kind == 2, 6, jnp.where(kind == 4, 8, jnp.where(kind == 3, 2, kind)))
-    parts_0 += away * jnp.where((kind == 2) | (kind == 4), 1, 3)
-    parts_1 = jnp.where(kind < 2, kind + 2 * away, 2 * kind + away)
+    parts_0 = jnp.where(kind == 4, 8 + away, kind // 2 * 4 + kind % 2 + 2 * away)
+    parts_1 = jnp.where(kind == 3, 4 + away, jnp.where(kind < 2, kind, kind // 2 + 5) + 2 * away)
     place_0, place_1 = (
-        jnp.where(present, part * blocks + within, 0).reshape(-1).astype(jnp.int32)
+        jnp.where(present, part * blocks + within, 0).astype(jnp.int32)
         for part in (parts_0, parts_1)
     )
-    present = present.reshape(-1).astype(jnp.int32)
+    present = present.astype(jnp.int32)
 
     def both(*parts):
         near = jnp.stack(parts, 0)
@@ -347,10 +345,10 @@
     low_0 = lax.ppermute(last_0, "row", one_up)
     high_0 = lax.ppermute(first_0, "row", one_down)
     edge_0 = other_col(face_0)
-    first_1, last_1, face_1 = make_faces(1, here, after(bold, edge_0))
+    first_1, last_1, face_1 = make_faces(1, here, after(bold, edge_0, gm_pair))
     beyond_1 = lax.ppermute(jnp.where(even, first_1, last_1), "row", two_on)
     edge_1 = other_col(face_1)
-    inner_1 = make_inner(here, first_1, last_1, edge_1, after(gm, gm_pair))
+    inner_1 = make_inner(here, first_1, last_1, edge_1, gm)
     beyond_1 = after(beyond_1, inner_1)
     low_0, high_0 = after(low_0, inner_1), after(high_0, inner_1)
     ends = [jnp.where(col == 0, part[-1], part[0]) for part in (low_0, high_0, beyond_1)]
@@ -373,12 +371,12 @@
     rest_1 = lax.ppermute(ahead_1, "row", in_pair)
     behind_0, rest_0 = after(behind_0, ahead_1), after(rest_0, ahead_1)
     pair_1 = after(pair_1, rest_0, behind_0)
-    behind_1 = after(behind_1, pair_1)
-    sources = both(own_0, ahead_0, pair_0) + both(behind_0)
+    sources = both(own_0, ahead_0) + both(behind_0, pair_0)
     out = make_tiles(0, windows, place_0, present, sources + both(rest_0), None)
-    sources = both(own_1, ahead_1) + both(behind_1) + both(pair_1)
-    rest_1 = after(rest_1, out, *sources)
-    return make_tiles(1, windows, place_1, present, sources + both(rest_1), out)
+    sources = both(own_1, ahead_1) + both(pair_1)
+    behind_1, rest_1 = after(behind_1, out, *sources), after(rest_1, out, *sources)
+    sources += both(behind_1, rest_1)
+    return make_tiles(1, windows, place_1, present, sources, out)
 
 
 def solution(mesh):

time: 125 us -> 120 us (0.960)
  starting transfers between devices: 32.6 us -> 19.1 us
  waiting for transfers between devices: 51.9 us -> 60.2 us
  other arithmetic: 2.47 us -> 5.13 us
  Pallas kernels: 31.7 us -> 29.1 us
    ppermute x1, waiting for transfers between devices: 13.9 us -> 0.01 us  [on_device(): gm_pair = lax.ppermute(gm, 'row', in_pair)]
    ppermute x1, waiting for transfers between devices: 0.01 us -> 6.41 us  [on_device(): low_0 = lax.ppermute(last_0, 'row', one_up)]
    ppermute x1, waiting for transfers between devices: 0.01 us -> 6.02 us  [on_device(): beyond_1 = lax.ppermute(jnp.where(even, first_1, last_1), 'row', two_on)]
    ppermute x1, waiting for transfers between devices: 4.4 us -> 7.9 us  [on_device(): halo_1 = lax.ppermute(halo_1, 'row', in_pair)]
    ppermute x1, starting transfers between devices: 4.06 us -> 0.6 us  [on_device(): rest_1 = lax.ppermute(ahead_1, 'row', in_pair)]
    ppermute x1, starting transfers between devices: 5.23 us -> 1.93 us  [on_device(): low_0 = lax.ppermute(last_0, 'row', one_up)]
    ppermute x1, waiting for transfers between devices: 2.34 us -> 5.04 us  [on_device(): pair_1 = lax.ppermute(own_1, 'row', in_pair)]
    ppermute x1, starting transfers between devices: 2.54 us -> 0.07 us  [on_device(): halo_1 = lax.ppermute(halo_1, 'row', in_pair)]
  transfers between devices with their start and end apart: 23 -> 22, of which waited for: 11 -> 13; matrix products, arithmetic and copies ran while one was open for 3% -> 3% of each run, Pallas kernels for 16% -> 16%
where the time goes in v8:
time: 120 us
  waiting for transfers between devices  60.2 us (50%)
  Pallas kernels  29.1 us (24%)
  starting transfers between devices  19.1 us (16%)
  local copies, waits for them, and re-layouts  5.7 us (5%)
  other arithmetic  5.13 us (4%)
    pallas_call x4, Pallas kernels, call_on_rows(): pl.pallas_call(kernel, grid=(1,), in_specs=[pl.BlockSpec(memory_space=plt...  13.4 us
    ppermute x1, waiting for transfers between devices, on_device(): behind_0 = lax.ppermute(after(own_0, ahead_0), 'row', behind)  13.2 us
    pallas_call x2, Pallas kernels, make_tiles(): pl.pallas_call(functools.partial(tiles_kernel, sources=count, window=wind...  11.8 us
    ppermute x1, waiting for transfers between devices, on_device(): halo_1 = lax.ppermute(halo_1, 'row', in_pair)  7.9 us
    ppermute x1, waiting for transfers between devices, on_device(): low_0 = lax.ppermute(last_0, 'row', one_up)  6.41 us
    ppermute x1, waiting for transfers between devices, on_device(): beyond_1 = lax.ppermute(jnp.where(even, first_1, last_1), 'row', two_on)  6.02 us
    ppermute x1, waiting for transfers between devices, on_device(): pair_0 = lax.ppermute(after(own_0, halo_1), 'row', in_pair)  5.99 us
    unnamed x22, local copies, waits for them, and re-layouts  5.7 us
  transfers between devices with their start and end apart: 22, of which 13 were waited for; matrix products, arithmetic and copies ran while one was open for 3% of the time, Pallas kernels for 16%

profile of v8, /device:TPU:0, one launch (start us, length us, event | category | flops | bytes accessed | tf_op | source)
XLA Modules:
  0.0 119.7 jit_solution(575874345737637378)
XLA Ops:
  0.1 1.6 %copy-done = bf16[2,256,2,8,128]{4,3,2,1,0:T(8,128)(2,1)S(1)} copy-done((bf16[2,256,2,8,128]{4,3,2,1,0:T(8,128)(2,1)S(1)}, bf16[2,256,2,8,128]{4,3,2,1,0:T(8,128)(2,1)}, u32[]{:S(2)}) %copy-start) | copy-done | bytes 2097176
  1.7 2.4 %faces.2 = (bf16[8,256,128]{2,1,0:T(8,128)(2,1)S(1)}, bf16[8,256,128]{2,1,0:T(8,128)(2,1)}, bf16[2,256,128]{2,1,0:T(8,128)(2,1)S(1)}) custom-call(s32[2]{0:T(128)S(1)} %pad_add_fusion.col_ref.place_ref, bf16[2,256,2,8,128]{4,3,2,1,0:T(8,128)(2,1)S(1)} %copy-done), custom_call_target="tpu_custom_call" | custom-call | flops 1 | bytes 1 | tf_op jit(solution)/shard_map/faces/pallas_call | solution.py:41
  4.5 2.5 %collective-permute-start.1 = (s32[1,1024]{1,0:T(1,128)}, s32[1,1024]{1,0:T(1,128)S(1)}, u32[]{:S(2)}, u32[]{:S(2)}) collective-permute-start(s32[1,1024]{1,0:T(1,128)} %bitcast.17), channel_id=1, source_target_pairs={{0,2},{2,0},{4,6},{6,4},{8,10},{10,8},{12,14},{14,12},{1,3},{3,1},... | collective-permute-start | bytes 12296 | tf_op jit(solution)/shard_map/ppermute | solution.py:343
  7.0 1.9 %collective-permute-start.4 = (bf16[8,256,128]{2,1,0:T(8,128)(2,1)}, bf16[8,256,128]{2,1,0:T(8,128)(2,1)S(1)}, u32[]{:S(2)}, u32[]{:S(2)}) collective-permute-start(bf16[8,256,128]{2,1,0:T(8,128)(2,1)} %get-tuple-element.33.last_ref), channel_id=1, source_target_pairs={{0,2},{2,4},{4,6},{6,8},{8,10},{10,12},{12,14},{1,3},{3,5},{5,7},{... | collective-permute-start | bytes 1572872 | tf_op jit(solution)/shard_map/ppermute | solution.py:345
  10.3 1.6 %copy-done.1 = bf16[2,256,2,8,128]{4,3,2,1,0:T(8,128)(2,1)S(1)} copy-done((bf16[2,256,2,8,128]{4,3,2,1,0:T(8,128)(2,1)S(1)}, bf16[2,256,2,8,128]{4,3,2,1,0:T(8,128)(2,1)}, u32[]{:S(2)}) %copy-start.1) | copy-done | bytes 2097176
  17.9 5.7 %inner_blur.1.inner_ref = f32[256,1024]{1,0:T(8,128)S(1)} custom-call(s32[2]{0:T(128)S(1)} %pad_add_fusion.col_ref.place_ref, bf16[8,256,128]{2,1,0:T(8,128)(2,1)S(1)} %get-tuple-element.29.first_ref, bf16[8,256,128]{2,1,0:T(8,128)(2,1)S(1)} %get-tuple-element.30.last_ref, bf16[2,256,128]{2,1,0:T(8,128)(2,1)S(1)} %collective-permute-done.2.edge_ref, ...), custom_call_target="tpu_custom_call" | custom-call | flops 1 | bytes 1 | tf_op jit(solution)/shard_map/inner_blur/pallas_call | solution.py:178
  23.5 2.3 %collective-permute-done.5.high_ref = bf16[8,256,128]{2,1,0:T(8,128)(2,1)S(1)} collective-permute-done((bf16[8,256,128]{2,1,0:T(8,128)(2,1)S(1)}, bf16[8,256,128]{2,1,0:T(8,128)(2,1)S(1)}, u32[]{:S(2)}, u32[]{:S(2)}) %collective-permute-start.5) | collective-permute-done | bytes 524320 | tf_op jit(solution)/shard_map/ppermute | solution.py:346
  25.9 6.4 %collective-permute-done.4.low_ref = bf16[8,256,128]{2,1,0:T(8,128)(2,1)S(1)} collective-permute-done((bf16[8,256,128]{2,1,0:T(8,128)(2,1)}, bf16[8,256,128]{2,1,0:T(8,128)(2,1)S(1)}, u32[]{:S(2)}, u32[]{:S(2)}) %collective-permute-start.4) | collective-permute-done | bytes 524320 | tf_op jit(solution)/shard_map/ppermute | solution.py:345
  32.3 6.0 %collective-permute-done.3.beyond_ref = bf16[8,256,128]{2,1,0:T(8,128)(2,1)S(1)} collective-permute-done((bf16[8,256,128]{2,1,0:T(8,128)(2,1)}, bf16[8,256,128]{2,1,0:T(8,128)(2,1)S(1)}, u32[]{:S(2)}, u32[]{:S(2)}) %collective-permute-start.3) | collective-permute-done | bytes 524320 | tf_op jit(solution)/shard_map/ppermute | solution.py:349
  39.9 2.9 %halo_blur.1 = bf16[256,1024]{1,0:T(8,128)(2,1)S(1)} custom-call(s32[2]{0:T(128)S(1)} %pad_add_fusion.col_ref.place_ref, bf16[8,256,128]{2,1,0:T(8,128)(2,1)S(1)} %get-tuple-element.29.first_ref, bf16[8,256,128]{2,1,0:T(8,128)(2,1)S(1)} %get-tuple-element.30.last_ref, bf16[8,256,128]{2,1,0:T(8,128)(2,1)S(1)} %collective-permute-done.3.beyond_ref, ...), custom_call_target="tpu_custom_call" | custom-call | flops 1 | bytes 1 | tf_op jit(solution)/shard_map/halo_blur/pallas_call | solution.py:178
  42.9 4.3 %blur_score_pick.1 = bf16[256,1024]{1,0:T(8,128)(2,1)S(1)} custom-call(s32[2]{0:T(128)S(1)} %pad_add_fusion.col_ref.place_ref, bf16[8,256,128]{2,1,0:T(8,128)(2,1)S(1)} %get-tuple-element.35.first_ref, bf16[8,256,128]{2,1,0:T(8,128)(2,1)} %get-tuple-element.33.last_ref, bf16[8,256,128]{2,1,0:T(8,128)(2,1)S(1)} %collective-permute-done.4.low_ref, ...), custom_call_target="tpu_custom_call" | custom-call | flops 1 | bytes 1 | tf_op jit(solution)/shard_map/blur_score_pick/pallas_call | solution.py:178
  47.2 1.7 %collective-permute-start.10 = (bf16[256,1024]{1,0:T(8,128)(2,1)S(1)}, bf16[256,1024]{1,0:T(8,128)(2,1)S(1)}, u32[]{:S(2)}, u32[]{:S(2)}) collective-permute-start(bf16[256,1024]{1,0:T(8,128)(2,1)S(1)} %blur_score_pick.1), channel_id=1, source_target_pairs={{4,0},{14,2},{8,4},{2,6},{12,8},{6,10},{0,12},{10,14},{5,1},{15,3}... | collective-permute-start | bytes 1572872 | tf_op jit(solution)/shard_map/ppermute | solution.py:360
  49.0 7.9 %collective-permute-done.7.halo_ref = bf16[256,1024]{1,0:T(8,128)(2,1)S(1)} collective-permute-done((bf16[256,1024]{1,0:T(8,128)(2,1)S(1)}, bf16[256,1024]{1,0:T(8,128)(2,1)S(1)}, u32[]{:S(2)}, u32[]{:S(2)}) %collective-permute-start.7) | collective-permute-done | bytes 524320 | tf_op jit(solution)/shard_map/ppermute | solution.py:357
  57.7 1.7 %collective-permute-start.8 = (bf16[256,1024]{1,0:T(8,128)(2,1)S(1)}, bf16[256,1024]{1,0:T(8,128)(2,1)}, u32[]{:S(2)}, u32[]{:S(2)}) collective-permute-start(bf16[256,1024]{1,0:T(8,128)(2,1)S(1)} %join_score.1), channel_id=1, source_target_pairs={{4,0},{14,2},{8,4},{2,6},{12,8},{6,10},{0,12},{10,14},{5,1},{15,3}... | collective-permute-start | bytes 1572872 | tf_op jit(solution)/shard_map/ppermute | solution.py:366
  59.4 2.7 %collective-permute-done.10 = bf16[256,1024]{1,0:T(8,128)(2,1)S(1)} collective-permute-done((bf16[256,1024]{1,0:T(8,128)(2,1)S(1)}, bf16[256,1024]{1,0:T(8,128)(2,1)S(1)}, u32[]{:S(2)}, u32[]{:S(2)}) %collective-permute-start.10) | collective-permute-done | bytes 524320 | tf_op jit(solution)/shard_map/ppermute | solution.py:360
  62.0 1.6 %collective-permute-start.14 = (bf16[256,1024]{1,0:T(8,128)(2,1)S(1)}, bf16[256,1024]{1,0:T(8,128)(2,1)S(1)}, u32[]{:S(2)}, u32[]{:S(2)}) collective-permute-start(bf16[256,1024]{1,0:T(8,128)(2,1)S(1)} %blur_score_pick.1), channel_id=1, source_target_pairs={{0,4},{2,14},{4,8},{6,2},{8,12},{10,6},{12,0},{14,10},{1,5},{3,15}... | collective-permute-start | bytes 1572872 | tf_op jit(solution)/shard_map/ppermute | solution.py:364
  63.6 2.5 %collective-permute-start.13 = (bf16[256,1024]{1,0:T(8,128)(2,1)S(1)}, bf16[256,1024]{1,0:T(8,128)(2,1)S(1)}, u32[]{:S(2)}, u32[]{:S(2)}) collective-permute-start(bf16[256,1024]{1,0:T(8,128)(2,1)S(1)} %collective-permute-done.10), channel_id=1, source_target_pairs={{0,2},{2,0},{4,6},{6,4},{8,10},{10,8},{12,14},{14,12},{1,3},{3,1},... | collective-permute-start | bytes 1572872 | tf_op jit(solution)/shard_map/ppermute | solution.py:365
  66.3 6.0 %collective-permute-done.9 = bf16[256,1024]{1,0:T(8,128)(2,1)S(1)} collective-permute-done((bf16[256,1024]{1,0:T(8,128)(2,1)S(1)}, bf16[256,1024]{1,0:T(8,128)(2,1)S(1)}, u32[]{:S(2)}, u32[]{:S(2)}) %collective-permute-start.9) | collective-permute-done | bytes 524320 | tf_op jit(solution)/shard_map/ppermute | solution.py:362
  72.6 13.2 %collective-permute-done.14 = bf16[256,1024]{1,0:T(8,128)(2,1)S(1)} collective-permute-done((bf16[256,1024]{1,0:T(8,128)(2,1)S(1)}, bf16[256,1024]{1,0:T(8,128)(2,1)S(1)}, u32[]{:S(2)}, u32[]{:S(2)}) %collective-permute-start.14) | collective-permute-done | bytes 524320 | tf_op jit(solution)/shard_map/ppermute | solution.py:364
  88.0 5.0 %collective-permute-done.12 = bf16[256,1024]{1,0:T(8,128)(2,1)S(1)} collective-permute-done((bf16[256,1024]{1,0:T(8,128)(2,1)S(1)}, bf16[256,1024]{1,0:T(8,128)(2,1)S(1)}, u32[]{:S(2)}, u32[]{:S(2)}) %collective-permute-start.12) | collective-permute-done | bytes 524320 | tf_op jit(solution)/shard_map/ppermute | solution.py:367
  98.3 7.0 %tiles.2.refs_6_ = bf16[8,16,2,128,128]{4,3,2,1,0:T(8,128)(2,1)} custom-call(s32[8,16]{1,0:T(8,128)} %get-tuple-element.49.place_ref, s32[8,16]{1,0:T(8,128)} %fusion.18.present_ref, bf16[2,256,1024]{2,1,0:T(8,128)(2,1)} %copy-done.4, bf16[2,256,1024]{2,1,0:T(8,128)(2,1)} %copy-done.6, bf16[2,256,1024]{2,1,0:T(8,128)(2,1)} %copy-done.5, ...), custom_call_target="tpu_custom_call" | custom-call | flops 1 | bytes 1 | tf_op jit(solution)/shard_map/tiles/pallas_call | solution.py:274
  105.6 5.1 %collective-permute-done.16 = bf16[256,1024]{1,0:T(8,128)(2,1)} collective-permute-done((bf16[256,1024]{1,0:T(8,128)(2,1)S(1)}, bf16[256,1024]{1,0:T(8,128)(2,1)}, u32[]{:S(2)}, u32[]{:S(2)}) %collective-permute-start.16) | collective-permute-done | bytes 524320 | tf_op jit(solution)/shard_map/ppermute | solution.py:370
  112.1 2.6 %collective-permute-done.21.refs_5_ = bf16[2,256,1024]{2,1,0:T(8,128)(2,1)S(1)} collective-permute-done((bf16[2,256,1024]{2,1,0:T(8,128)(2,1)S(1)}, bf16[2,256,1024]{2,1,0:T(8,128)(2,1)S(1)}, u32[]{:S(2)}, u32[]{:S(2)}) %collective-permute-start.21) | collective-permute-done | bytes 1048608 | tf_op jit(solution)/shard_map/ppermute | solution.py:308
  114.7 4.8 %tiles.3 = bf16[8,16,2,128,128]{4,3,2,1,0:T(8,128)(2,1)} custom-call(s32[8,16]{1,0:T(8,128)S(1)} %get-tuple-element.50.place_ref, s32[8,16]{1,0:T(8,128)S(1)} %copy-done.2, bf16[2,256,1024]{2,1,0:T(8,128)(2,1)S(1)} %pad_maximum_fusion.refs_0_, bf16[2,256,1024]{2,1,0:T(8,128)(2,1)S(1)} %collective-permute-done.11.refs_1_, ...), custom_call_target="tpu_custom_call", output_to_operand_aliasing={{}: (8, {})} | custom-call | flops 1 | bytes 1 | tf_op jit(solution)/shard_map/tiles/pallas_call | solution.py:274
  (61 shorter events, 19.8 us)
Async XLA Ops:
  4.0 6.2 %collective-permute-start = (bf16[2,256,128]{2,1,0:T(8,128)(2,1)S(1)}, bf16[2,256,128]{2,1,0:T(8,128)(2,1)S(1)}, u32[]{:S(2)}, u32[]{:S(2)}) collective-permute-start(bf16[2,256,128]{2,1,0:T(8,128)(2,1)S(1)} %get-tuple-element.27), channel_id=1, source_target_pairs={{0,1},{1,0},{2,3},{3,2},{4,5},{5,4},{6,7},{7,6},{8,9},{9,8},{10,11... | collective-permute-start | bytes 393224 | tf_op jit(solution)/shard_map/ppermute | solution.py:308
  4.5 5.8 %collective-permute-start.1 = (s32[1,1024]{1,0:T(1,128)}, s32[1,1024]{1,0:T(1,128)S(1)}, u32[]{:S(2)}, u32[]{:S(2)}) collective-permute-start(s32[1,1024]{1,0:T(1,128)} %bitcast.17), channel_id=1, source_target_pairs={{0,2},{2,0},{4,6},{6,4},{8,10},{10,8},{12,14},{14,12},{1,3},{3,1},... | collective-permute-start | bytes 12296 | tf_op jit(solution)/shard_map/ppermute | solution.py:343
  7.0 25.3 %collective-permute-start.4 = (bf16[8,256,128]{2,1,0:T(8,128)(2,1)}, bf16[8,256,128]{2,1,0:T(8,128)(2,1)S(1)}, u32[]{:S(2)}, u32[]{:S(2)}) collective-permute-start(bf16[8,256,128]{2,1,0:T(8,128)(2,1)} %get-tuple-element.33.last_ref), channel_id=1, source_target_pairs={{0,2},{2,4},{4,6},{6,8},{8,10},{10,12},{12,14},{1,3},{3,5},{5,7},{... | collective-permute-start | bytes 1572872 | tf_op jit(solution)/shard_map/ppermute | solution.py:345
  8.9 16.9 %collective-permute-start.5 = (bf16[8,256,128]{2,1,0:T(8,128)(2,1)S(1)}, bf16[8,256,128]{2,1,0:T(8,128)(2,1)S(1)}, u32[]{:S(2)}, u32[]{:S(2)}) collective-permute-start(bf16[8,256,128]{2,1,0:T(8,128)(2,1)S(1)} %get-tuple-element.35.first_ref), channel_id=1, source_target_pairs={{2,0},{4,2},{6,4},{8,6},{10,8},{12,10},{14,12},{3,1},{5,3},{7,5},{... | collective-permute-start | bytes 1572872 | tf_op jit(solution)/shard_map/ppermute | solution.py:346
  14.3 24.0 %collective-permute-start.3 = (bf16[8,256,128]{2,1,0:T(8,128)(2,1)}, bf16[8,256,128]{2,1,0:T(8,128)(2,1)S(1)}, u32[]{:S(2)}, u32[]{:S(2)}) collective-permute-start(bf16[8,256,128]{2,1,0:T(8,128)(2,1)} %broadcast_select_fusion), channel_id=1, source_target_pairs={{2,6},{4,0},{6,10},{8,4},{10,14},{12,8},{3,7},{5,1},{7,11},{9,5},{... | collective-permute-start | bytes 1572872 | tf_op jit(solution)/shard_map/ppermute | solution.py:349
  15.8 1.4 %collective-permute-start.2 = (bf16[2,256,128]{2,1,0:T(8,128)(2,1)S(1)}, bf16[2,256,128]{2,1,0:T(8,128)(2,1)S(1)}, u32[]{:S(2)}, u32[]{:S(2)}) collective-permute-start(bf16[2,256,128]{2,1,0:T(8,128)(2,1)S(1)} %get-tuple-element.31), channel_id=1, source_target_pairs={{0,1},{1,0},{2,3},{3,2},{4,5},{5,4},{6,7},{7,6},{8,9},{9,8},{10,11... | collective-permute-start | bytes 393224 | tf_op jit(solution)/shard_map/ppermute | solution.py:308
  17.9 78.2 %copy-start.10 = (s32[8,16]{1,0:T(8,128)S(1)}, s32[8,16]{1,0:T(8,128)}, u32[]{:S(2)}) copy-start(s32[8,16]{1,0:T(8,128)} %param.5) | copy-start | bytes 1540
  38.4 1.5 %collective-permute-start.6 = (bf16[3,256,128]{2,1,0:T(8,128)(2,1)S(1)}, bf16[3,256,128]{2,1,0:T(8,128)(2,1)S(1)}, u32[]{:S(2)}, u32[]{:S(2)}) collective-permute-start(bf16[3,256,128]{2,1,0:T(8,128)(2,1)S(1)} %pad_maximum_fusion.4), channel_id=1, source_target_pairs={{0,1},{1,0},{2,3},{3,2},{4,5},{5,4},{6,7},{7,6},{8,9},{9,8},{10,11... | collective-permute-start | bytes 589832 | tf_op jit(solution)/shard_map/ppermute | solution.py:308
  42.8 14.0 %collective-permute-start.7 = (bf16[256,1024]{1,0:T(8,128)(2,1)S(1)}, bf16[256,1024]{1,0:T(8,128)(2,1)S(1)}, u32[]{:S(2)}, u32[]{:S(2)}) collective-permute-start(bf16[256,1024]{1,0:T(8,128)(2,1)S(1)} %halo_blur.1), channel_id=1, source_target_pairs={{0,2},{2,0},{4,6},{6,4},{8,10},{10,8},{12,14},{14,12},{1,3},{3,1},... | collective-permute-start | bytes 1572872 | tf_op jit(solution)/shard_map/ppermute | solution.py:357
  47.2 14.8 %collective-permute-start.10 = (bf16[256,1024]{1,0:T(8,128)(2,1)S(1)}, bf16[256,1024]{1,0:T(8,128)(2,1)S(1)}, u32[]{:S(2)}, u32[]{:S(2)}) collective-permute-start(bf16[256,1024]{1,0:T(8,128)(2,1)S(1)} %blur_score_pick.1), channel_id=1, source_target_pairs={{4,0},{14,2},{8,4},{2,6},{12,8},{6,10},{0,12},{10,14},{5,1},{15,3}... | collective-permute-start | bytes 1572872 | tf_op jit(solution)/shard_map/ppermute | solution.py:360
  57.3 14.9 %collective-permute-start.9 = (bf16[256,1024]{1,0:T(8,128)(2,1)S(1)}, bf16[256,1024]{1,0:T(8,128)(2,1)S(1)}, u32[]{:S(2)}, u32[]{:S(2)}) collective-permute-start(bf16[256,1024]{1,0:T(8,128)(2,1)S(1)} %blur_score_pick.1), channel_id=1, source_target_pairs={{0,2},{2,0},{4,6},{6,4},{8,10},{10,8},{12,14},{14,12},{1,3},{3,1},... | collective-permute-start | bytes 1572872 | tf_op jit(solution)/shard_map/ppermute | solution.py:362
  57.7 14.9 %collective-permute-start.8 = (bf16[256,1024]{1,0:T(8,128)(2,1)S(1)}, bf16[256,1024]{1,0:T(8,128)(2,1)}, u32[]{:S(2)}, u32[]{:S(2)}) collective-permute-start(bf16[256,1024]{1,0:T(8,128)(2,1)S(1)} %join_score.1), channel_id=1, source_target_pairs={{4,0},{14,2},{8,4},{2,6},{12,8},{6,10},{0,12},{10,14},{5,1},{15,3}... | collective-permute-start | bytes 1572872 | tf_op jit(solution)/shard_map/ppermute | solution.py:366
  62.0 23.7 %collective-permute-start.14 = (bf16[256,1024]{1,0:T(8,128)(2,1)S(1)}, bf16[256,1024]{1,0:T(8,128)(2,1)S(1)}, u32[]{:S(2)}, u32[]{:S(2)}) collective-permute-start(bf16[256,1024]{1,0:T(8,128)(2,1)S(1)} %blur_score_pick.1), channel_id=1, source_target_pairs={{0,4},{2,14},{4,8},{6,2},{8,12},{10,6},{12,0},{14,10},{1,5},{3,15}... | collective-permute-start | bytes 1572872 | tf_op jit(solution)/shard_map/ppermute | solution.py:364
  63.6 23.8 %collective-permute-start.13 = (bf16[256,1024]{1,0:T(8,128)(2,1)S(1)}, bf16[256,1024]{1,0:T(8,128)(2,1)S(1)}, u32[]{:S(2)}, u32[]{:S(2)}) collective-permute-start(bf16[256,1024]{1,0:T(8,128)(2,1)S(1)} %collective-permute-done.10), channel_id=1, source_target_pairs={{0,2},{2,0},{4,6},{6,4},{8,10},{10,8},{12,14},{14,12},{1,3},{3,1},... | collective-permute-start | bytes 1572872 | tf_op jit(solution)/shard_map/ppermute | solution.py:365
  66.2 29.9 %copy-start.4 = (bf16[2,256,1024]{2,1,0:T(8,128)(2,1)}, bf16[2,256,1024]{2,1,0:T(8,128)(2,1)S(1)}, u32[]{:S(2)}) copy-start(bf16[2,256,1024]{2,1,0:T(8,128)(2,1)S(1)} %pad_maximum_fusion.1.refs_0_) | copy-start | bytes 3145732
  66.2 27.4 %collective-permute-start.17 = (bf16[2,256,1024]{2,1,0:T(8,128)(2,1)S(1)}, bf16[2,256,1024]{2,1,0:T(8,128)(2,1)S(1)}, u32[]{:S(2)}, u32[]{:S(2)}) collective-permute-start(bf16[2,256,1024]{2,1,0:T(8,128)(2,1)S(1)} %pad_maximum_fusion.1.refs_0_), channel_id=1, source_target_pairs={{0,1},{1,0},{2,3},{3,2},{4,5},{5,4},{6,7},{7,6},{8,9},{9,8},{10,11... | collective-permute-start | bytes 3145736 | tf_op jit(solution)/shard_map/ppermute | solution.py:308
  72.3 20.7 %collective-permute-start.12 = (bf16[256,1024]{1,0:T(8,128)(2,1)S(1)}, bf16[256,1024]{1,0:T(8,128)(2,1)S(1)}, u32[]{:S(2)}, u32[]{:S(2)}) collective-permute-start(bf16[256,1024]{1,0:T(8,128)(2,1)S(1)} %join_score.1), channel_id=1, source_target_pairs={{0,2},{2,0},{4,6},{6,4},{8,10},{10,8},{12,14},{14,12},{1,3},{3,1},... | collective-permute-start | bytes 1572872 | tf_op jit(solution)/shard_map/ppermute | solution.py:367
  85.9 11.5 %collective-permute-start.18 = (bf16[2,256,1024]{2,1,0:T(8,128)(2,1)S(1)}, bf16[2,256,1024]{2,1,0:T(8,128)(2,1)S(1)}, u32[]{:S(2)}, u32[]{:S(2)}) collective-permute-start(bf16[2,256,1024]{2,1,0:T(8,128)(2,1)S(1)} %pad_maximum_fusion.2.refs_2_), channel_id=1, source_target_pairs={{0,1},{1,0},{2,3},{3,2},{4,5},{5,4},{6,7},{7,6},{8,9},{9,8},{10,11... | collective-permute-start | bytes 3145736 | tf_op jit(solution)/shard_map/ppermute | solution.py:308
  87.4 18.2 %collective-permute-start.11 = (bf16[2,256,1024]{2,1,0:T(8,128)(2,1)S(1)}, bf16[2,256,1024]{2,1,0:T(8,128)(2,1)S(1)}, u32[]{:S(2)}, u32[]{:S(2)}) collective-permute-start(bf16[2,256,1024]{2,1,0:T(8,128)(2,1)S(1)} %pad_maximum_fusion.refs_0_), channel_id=1, source_target_pairs={{0,1},{1,0},{2,3},{3,2},{4,5},{5,4},{6,7},{7,6},{8,9},{9,8},{10,11... | collective-permute-start | bytes 3145736 | tf_op jit(solution)/shard_map/ppermute | solution.py:308
  87.7 6.0 %collective-permute-start.19 = (bf16[1,256,1024]{2,1,0:T(8,128)(2,1)S(1)}, bf16[1,256,1024]{2,1,0:T(8,128)(2,1)S(1)}, u32[]{:S(2)}, u32[]{:S(2)}) collective-permute-start(bf16[1,256,1024]{2,1,0:T(8,128)(2,1)S(1)} %bitcast.20), channel_id=1, source_target_pairs={{0,1},{1,0},{2,3},{3,2},{4,5},{5,4},{6,7},{7,6},{8,9},{9,8},{10,11... | collective-permute-start | bytes 1572872 | tf_op jit(solution)/shard_map/ppermute | solution.py:308
  93.0 12.5 %collective-permute-start.20 = (bf16[256,1024]{1,0:T(8,128)(2,1)}, bf16[256,1024]{1,0:T(8,128)(2,1)}, u32[]{:S(2)}, u32[]{:S(2)}) collective-permute-start(bf16[256,1024]{1,0:T(8,128)(2,1)} %collective-permute-done.8), channel_id=1, source_target_pairs={{0,2},{2,0},{4,6},{6,4},{8,10},{10,8},{12,14},{14,12},{1,3},{3,1},... | collective-permute-start | bytes 1572872 | tf_op jit(solution)/shard_map/ppermute | solution.py:371
  93.6 11.9 %collective-permute-start.15 = (bf16[1,256,1024]{2,1,0:T(8,128)(2,1)S(1)}, bf16[1,256,1024]{2,1,0:T(8,128)(2,1)S(1)}, u32[]{:S(2)}, u32[]{:S(2)}) collective-permute-start(bf16[1,256,1024]{2,1,0:T(8,128)(2,1)S(1)} %bitcast.15), channel_id=1, source_target_pairs={{0,1},{1,0},{2,3},{3,2},{4,5},{5,4},{6,7},{7,6},{8,9},{9,8},{10,11... | collective-permute-start | bytes 1572872 | tf_op jit(solution)/shard_map/ppermute | solution.py:308
  94.5 16.2 %collective-permute-start.16 = (bf16[256,1024]{1,0:T(8,128)(2,1)S(1)}, bf16[256,1024]{1,0:T(8,128)(2,1)}, u32[]{:S(2)}, u32[]{:S(2)}) collective-permute-start(bf16[256,1024]{1,0:T(8,128)(2,1)S(1)} %join_score.1), channel_id=1, source_target_pairs={{0,4},{2,14},{4,8},{6,2},{8,12},{10,6},{12,0},{14,10},{1,5},{3,15}... | collective-permute-start | bytes 1572872 | tf_op jit(solution)/shard_map/ppermute | solution.py:370
  112.0 2.7 %collective-permute-start.21 = (bf16[2,256,1024]{2,1,0:T(8,128)(2,1)S(1)}, bf16[2,256,1024]{2,1,0:T(8,128)(2,1)S(1)}, u32[]{:S(2)}, u32[]{:S(2)}) collective-permute-start(bf16[2,256,1024]{2,1,0:T(8,128)(2,1)S(1)} %pad_maximum_fusion.3.refs_4_), channel_id=1, source_target_pairs={{0,1},{1,0},{2,3},{3,2},{4,5},{5,4},{6,7},{7,6},{8,9},{9,8},{10,11... | collective-permute-start | bytes 3145736 | tf_op jit(solution)/shard_map/ppermute | solution.py:308
  (9 other events, 48.2 us)

commit v9 on v8

--- a/solution.py
+++ b/solution.py
@@ -13,7 +13,6 @@
 CENTRE = 1.0 / (1.0 + 2.0 * math.exp(-0.5))
 SMALL = pl.CostEstimate(flops=1, bytes_accessed=1, transcendentals=0)
 VMEM_BYTES = 20 * 1024 * 1024
-TILES_VMEM_BYTES = 60 * 1024 * 1024
 
 
 def faces_kernel(col_ref, bold_ref, first_ref, last_ref, edge_ref, wide):
@@ -92,28 +91,6 @@
         out_ref[:, start : start + step] = total.astype(out_ref.dtype)
 
 
-def panel_kernel(
-    place_ref, first_ref, last_ref, low_ref, high_ref, edge_ref, corner_ref, gm_ref, out_ref,
-    planes, scored,
-):
-    slab_y, frames, slab_z = first_ref.shape
-    slab_x = edge_ref.shape[0]
-    for y in range(slab_y):
-        layers = [ref[y].astype(jnp.float32) for ref in (low_ref, first_ref, last_ref, high_ref)]
-        for x in range(slab_x):
-            planes[x, y + 1] = three_taps(*layers[x : x + 3])
-    edges = [corner_ref[0], edge_ref[0], edge_ref[1], corner_ref[1]]
-    edges = [edge.astype(jnp.float32) for edge in edges]
-    for x in range(slab_x):
-        place_edge(planes, x, three_taps(*edges[x : x + 3]), place_ref[0])
-    for x in range(slab_x):
-        for y in range(slab_y):
-            part = three_taps(planes[x, y], planes[x, y + 1], planes[x, y + 2])
-            start = (x * slab_y + y) * slab_z
-            scored[:, start : start + slab_z] = standardise(along_z(part))
-    pick([scored], gm_ref, out_ref)
-
-
 def inner_kernel(
     place_ref, first_ref, last_ref, edge_ref, gm_ref, out_ref, planes, high, middle, low
 ):
@@ -154,7 +131,7 @@
         own = jnp.where(even, last_ref[y], first_ref[y])
         planes[0, y + 1], planes[1, y + 1] = sides(own, beyond_ref[y])
     own = jnp.where(even, edge_ref[1], edge_ref[0])
-    for x, edge in enumerate(sides(own, corner_ref[2])):
+    for x, edge in enumerate(sides(own, corner_ref[...])):
         place_edge(planes, x, edge, place_ref[0])
     for x in range(2):
         for y in range(slab_y):
@@ -193,14 +170,6 @@
     slab_y, frames, slab_z = first.shape
     planes = pltpu.VMEM((2, slab_y + 2, frames, slab_z), jnp.float32)
     return [planes] + [pltpu.VMEM((frames, 2 * slab_y * slab_z), jnp.bfloat16)] * terms
-
-
-def make_panel(place, first, last, low, high, edge, corner, gm):
-    operands = (first, last, low, high, edge, corner, gm)
-    scratch = blur_scratch(first, 1)
-    return call_on_rows(
-        panel_kernel, jnp.bfloat16, first.shape[1], place, operands, scratch, "blur_score_pick"
-    )
 
 
 def make_inner(place, first, last, edge, gm):
@@ -287,7 +256,7 @@
         ),
         out_shape=jax.ShapeDtypeStruct((blocks, slots, windows, BLOCK, BLOCK), jnp.bfloat16),
         input_output_aliases={} if earlier is None else {2 + count: 0},
-        compiler_params=pltpu.CompilerParams(vmem_limit_bytes=VMEM_BYTES if window else TILES_VMEM_BYTES),
+        compiler_params=pltpu.CompilerParams(vmem_limit_bytes=VMEM_BYTES),
         cost_estimate=SMALL,
         name="tiles",
     )(place, present, *operands)
@@ -307,8 +276,6 @@
     def other_col(value):
         return lax.ppermute(value, "col", [(0, 1), (1, 0)])
 
-    one_up = [(i, i + 1) for i in range(row_total - 1)]
-    one_down = [(i + 1, i) for i in range(row_total - 1)]
     ahead = [((i + 2 * (-1) ** i) % row_total, i) for i in range(row_total)]
     behind = [(i, source) for source, i in ahead]
     two_on = [(i, i + 2 * (-1) ** (i + 1)) for i in range(row_total)]
@@ -341,21 +308,29 @@
 
     windows = bold.shape[0]
     gm_pair = lax.ppermute(gm, "row", in_pair)
+
+    def outer(first, last):
+        return lax.ppermute(jnp.where(even, first, last), "row", two_on)
+
+    def halo_for_pair(first, last, beyond, edge):
+        corner = other_col(jnp.where(col == 0, beyond[-1], beyond[0]))
+        return make_halo(here, first, last, beyond, edge, corner, gm_pair)
+
     first_0, last_0, face_0 = make_faces(0, here, bold)
-    low_0 = lax.ppermute(last_0, "row", one_up)
-    high_0 = lax.ppermute(first_0, "row", one_down)
+    beyond_0 = outer(first_0, last_0)
     edge_0 = other_col(face_0)
     first_1, last_1, face_1 = make_faces(1, here, after(bold, edge_0, gm_pair))
-    beyond_1 = lax.ppermute(jnp.where(even, first_1, last_1), "row", two_on)
+    beyond_1 = outer(first_1, last_1)
     edge_1 = other_col(face_1)
-    inner_1 = make_inner(here, first_1, last_1, edge_1, gm)
+    inner_0 = make_inner(here, first_0, last_0, edge_0, after(gm, edge_1))
+    beyond_0 = after(beyond_0, inner_0)
+    given_0 = halo_for_pair(first_0, last_0, beyond_0, edge_0)
+    halo_0 = lax.ppermute(given_0, "row", in_pair)
+    inner_1 = make_inner(here, first_1, last_1, edge_1, after(gm, given_0))
     beyond_1 = after(beyond_1, inner_1)
-    low_0, high_0 = after(low_0, inner_1), after(high_0, inner_1)
-    ends = [jnp.where(col == 0, part[-1], part[0]) for part in (low_0, high_0, beyond_1)]
-    corner = other_col(jnp.stack(ends, 0))
-    halo_1 = make_halo(here, first_1, last_1, beyond_1, edge_1, corner, gm_pair)
-    halo_1 = lax.ppermute(halo_1, "row", in_pair)
-    own_0 = make_panel(here, first_0, last_0, low_0, high_0, edge_0, corner, gm)
+    given_1 = halo_for_pair(first_1, last_1, beyond_1, edge_1)
+    halo_1 = lax.ppermute(given_1, "row", in_pair)
+    own_0 = join(inner_0, after(halo_0, given_1))
     halo_1 = after(halo_1, own_0)
     ahead_0 = lax.ppermute(own_0, "row", ahead)
     own_1 = join(inner_1, halo_1)
@@ -371,12 +346,11 @@
     rest_1 = lax.ppermute(ahead_1, "row", in_pair)
     behind_0, rest_0 = after(behind_0, ahead_1), after(rest_0, ahead_1)
     pair_1 = after(pair_1, rest_0, behind_0)
-    sources = both(own_0, ahead_0) + both(behind_0, pair_0)
-    out = make_tiles(0, windows, place_0, present, sources + both(rest_0), None)
-    sources = both(own_1, ahead_1) + both(pair_1)
-    behind_1, rest_1 = after(behind_1, out, *sources), after(rest_1, out, *sources)
-    sources += both(behind_1, rest_1)
-    return make_tiles(1, windows, place_1, present, sources, out)
+    sources_0 = both(own_0, ahead_0) + both(behind_0, pair_0) + both(rest_0)
+    sources_1 = both(own_1, ahead_1) + both(pair_1)
+    sources_1 += both(behind_1, rest_1)
+    out = make_tiles(0, windows, place_0, present, sources_0, None)
+    return make_tiles(1, windows, place_1, present, sources_1, out)
 
 
 def solution(mesh):

time: 120 us -> 123 us (1.025)
  starting transfers between devices: 19.1 us -> 47.6 us
  waiting for transfers between devices: 60.2 us -> 37.1 us
  other arithmetic: 5.13 us -> 2.25 us
  Pallas kernels: 29.1 us -> 31.1 us
  local copies, waits for them, and re-layouts: 5.7 us -> 3.88 us
    ppermute x1, starting transfers between devices: 1.58 us -> 23 us  [on_device(): behind_1 = lax.ppermute(after(own_1, ahead_1), 'row', behind)]
    ppermute x1, waiting for transfers between devices: 13.2 us -> 0.01 us  [on_device(): behind_0 = lax.ppermute(after(own_0, ahead_0), 'row', behind)]
    ppermute x4, waiting for transfers between devices: 22.7 us -> 10.6 us  [the longest x1 8.61 us: on_device(): halo_1 = lax.ppermute(given_1, 'row', in_pair)]
    pallas_call x4 -> x6, Pallas kernels: 13.4 us -> 18.4 us  [call_on_rows(): pl.pallas_call(kernel, grid=(1,), in_specs=[pl.BlockSpec(memory_space=plt...]
    ppermute x1, waiting for transfers between devices: 2.66 us -> 0.01 us  [on_device(): ahead_0 = lax.ppermute(own_0, 'row', ahead)]
    another operation x4, other arithmetic: 2.93 us -> 0.39 us  [both(): near = jnp.stack(parts, 0)]
    ppermute x1, waiting for transfers between devices: 5.99 us -> 8.46 us  [on_device(): pair_0 = lax.ppermute(after(own_0, halo_1), 'row', in_pair)]
    ppermute x4, starting transfers between devices: 4.75 us -> 7.09 us  [the longest x1 4.27 us: on_device(): halo_0 = lax.ppermute(given_0, 'row', in_pair)]
  transfers between devices with their start and end apart: 22 -> 23, of which waited for: 13 -> 11; matrix products, arithmetic and copies ran while one was open for 3% -> 2% of each run, Pallas kernels for 16% -> 20%
where the time goes in v9:
time: 123 us; the launch traced here: 122 us
  starting transfers between devices  47.6 us (39%)
  waiting for transfers between devices  37.1 us (30%)
  Pallas kernels  31.1 us (25%)
  local copies, waits for them, and re-layouts  3.88 us (3%)
  other arithmetic  2.25 us (2%)
    ppermute x1, starting transfers between devices, on_device(): behind_1 = lax.ppermute(after(own_1, ahead_1), 'row', behind)  23 us
    pallas_call x6, Pallas kernels, call_on_rows(): pl.pallas_call(kernel, grid=(1,), in_specs=[pl.BlockSpec(memory_space=plt...  18.4 us
    pallas_call x2, Pallas kernels, make_tiles(): pl.pallas_call(functools.partial(tiles_kernel, sources=count, window=wind...  9.53 us
    ppermute x1, waiting for transfers between devices, on_device(): halo_1 = lax.ppermute(given_1, 'row', in_pair)  8.61 us
    ppermute x1, waiting for transfers between devices, on_device(): pair_0 = lax.ppermute(after(own_0, halo_1), 'row', in_pair)  8.46 us
    ppermute x1, waiting for transfers between devices, on_device(): pair_1 = lax.ppermute(own_1, 'row', in_pair)  5.51 us
    ppermute x1, starting transfers between devices, on_device(): gm_pair = lax.ppermute(gm, 'row', in_pair)  4.83 us
    ppermute x1, starting transfers between devices, on_device(): halo_0 = lax.ppermute(given_0, 'row', in_pair)  4.27 us
  transfers between devices with their start and end apart: 23, of which 11 were waited for; matrix products, arithmetic and copies ran while one was open for 2% of the time, Pallas kernels for 20%

profile of v9, /device:TPU:0, one launch (start us, length us, event | category | flops | bytes accessed | tf_op | source)
XLA Modules:
  0.0 122.3 jit_solution(3274069697382381892)
XLA Ops:
  0.1 1.6 %copy-done = bf16[2,256,2,8,128]{4,3,2,1,0:T(8,128)(2,1)S(1)} copy-done((bf16[2,256,2,8,128]{4,3,2,1,0:T(8,128)(2,1)S(1)}, bf16[2,256,2,8,128]{4,3,2,1,0:T(8,128)(2,1)}, u32[]{:S(2)}) %copy-start) | copy-done | bytes 2097176
  1.7 1.6 %faces.2 = (bf16[8,256,128]{2,1,0:T(8,128)(2,1)S(1)}, bf16[8,256,128]{2,1,0:T(8,128)(2,1)S(1)}, bf16[2,256,128]{2,1,0:T(8,128)(2,1)S(1)}) custom-call(s32[2]{0:T(128)S(1)} %pad_add_fusion.col_ref.place_ref, bf16[2,256,2,8,128]{4,3,2,1,0:T(8,128)(2,1)S(1)} %copy-done), custom_call_target="tpu_custom_call" | custom-call | flops 1 | bytes 1 | tf_op jit(solution)/shard_map/faces/pallas_call | solution.py:40
  5.9 4.8 %collective-permute-start.1 = (s32[1,1024]{1,0:T(1,128)}, s32[1,1024]{1,0:T(1,128)S(1)}, u32[]{:S(2)}, u32[]{:S(2)}) collective-permute-start(s32[1,1024]{1,0:T(1,128)} %bitcast.23), channel_id=1, source_target_pairs={{0,2},{2,0},{4,6},{6,4},{8,10},{10,8},{12,14},{14,12},{1,3},{3,1},... | collective-permute-start | bytes 12296 | tf_op jit(solution)/shard_map/ppermute | solution.py:310
  10.7 1.8 %collective-permute-done.1.gm_ref = s32[1,1024]{1,0:T(1,128)S(1)} collective-permute-done((s32[1,1024]{1,0:T(1,128)}, s32[1,1024]{1,0:T(1,128)S(1)}, u32[]{:S(2)}, u32[]{:S(2)}) %collective-permute-start.1) | collective-permute-done | bytes 4128 | tf_op jit(solution)/shard_map/ppermute | solution.py:310
  12.5 1.6 %copy-done.1 = bf16[2,256,2,8,128]{4,3,2,1,0:T(8,128)(2,1)S(1)} copy-done((bf16[2,256,2,8,128]{4,3,2,1,0:T(8,128)(2,1)S(1)}, bf16[2,256,2,8,128]{4,3,2,1,0:T(8,128)(2,1)}, u32[]{:S(2)}) %copy-start.1) | copy-done | bytes 2097176
  14.1 1.6 %faces.3 = (bf16[8,256,128]{2,1,0:T(8,128)(2,1)S(1)}, bf16[8,256,128]{2,1,0:T(8,128)(2,1)S(1)}, bf16[2,256,128]{2,1,0:T(8,128)(2,1)S(1)}) custom-call(s32[2]{0:T(128)S(1)} %pad_add_fusion.col_ref.place_ref, bf16[2,256,2,8,128]{4,3,2,1,0:T(8,128)(2,1)S(1)} %copy-done.1), custom_call_target="tpu_custom_call" | custom-call | flops 1 | bytes 1 | tf_op jit(solution)/shard_map/faces/pallas_call | solution.py:40
  20.1 5.7 %inner_blur.2.inner_ref = f32[256,1024]{1,0:T(8,128)S(1)} custom-call(s32[2]{0:T(128)S(1)} %pad_add_fusion.col_ref.place_ref, bf16[8,256,128]{2,1,0:T(8,128)(2,1)S(1)} %get-tuple-element.32.first_ref, bf16[8,256,128]{2,1,0:T(8,128)(2,1)S(1)} %get-tuple-element.33.last_ref, bf16[2,256,128]{2,1,0:T(8,128)(2,1)S(1)} %collective-permute-done.edge_ref, ...), custom_call_target="tpu_custom_call" | custom-call | flops 1 | bytes 1 | tf_op jit(solution)/shard_map/inner_blur/pallas_call | solution.py:155
  27.2 2.9 %halo_blur.2 = bf16[256,1024]{1,0:T(8,128)(2,1)S(1)} custom-call(s32[2]{0:T(128)S(1)} %pad_add_fusion.col_ref.place_ref, bf16[8,256,128]{2,1,0:T(8,128)(2,1)S(1)} %get-tuple-element.32.first_ref, bf16[8,256,128]{2,1,0:T(8,128)(2,1)S(1)} %get-tuple-element.33.last_ref, bf16[8,256,128]{2,1,0:T(8,128)(2,1)S(1)} %collective-permute-done.3.beyond_ref, ...), custom_call_target="tpu_custom_call" | custom-call | flops 1 | bytes 1 | tf_op jit(solution)/shard_map/halo_blur/pallas_call | solution.py:155
  30.1 4.3 %collective-permute-start.8 = (bf16[256,1024]{1,0:T(8,128)(2,1)S(1)}, bf16[256,1024]{1,0:T(8,128)(2,1)S(1)}, u32[]{:S(2)}, u32[]{:S(2)}) collective-permute-start(bf16[256,1024]{1,0:T(8,128)(2,1)S(1)} %halo_blur.2), channel_id=1, source_target_pairs={{0,2},{2,0},{4,6},{6,4},{8,10},{10,8},{12,14},{14,12},{1,3},{3,1},... | collective-permute-start | bytes 1572872 | tf_op jit(solution)/shard_map/ppermute | solution.py:328
  34.4 5.7 %inner_blur.3.inner_ref = f32[256,1024]{1,0:T(8,128)S(1)} custom-call(s32[2]{0:T(128)S(1)} %pad_add_fusion.col_ref.place_ref, bf16[8,256,128]{2,1,0:T(8,128)(2,1)S(1)} %get-tuple-element.29.first_ref, bf16[8,256,128]{2,1,0:T(8,128)(2,1)S(1)} %get-tuple-element.30.last_ref, bf16[2,256,128]{2,1,0:T(8,128)(2,1)S(1)} %collective-permute-done.2.edge_ref, ...), custom_call_target="tpu_custom_call" | custom-call | flops 1 | bytes 1 | tf_op jit(solution)/shard_map/inner_blur/pallas_call | solution.py:155
  41.4 3.1 %halo_blur.3 = bf16[256,1024]{1,0:T(8,128)(2,1)S(1)} custom-call(s32[2]{0:T(128)S(1)} %pad_add_fusion.col_ref.place_ref, bf16[8,256,128]{2,1,0:T(8,128)(2,1)S(1)} %get-tuple-element.29.first_ref, bf16[8,256,128]{2,1,0:T(8,128)(2,1)S(1)} %get-tuple-element.30.last_ref, bf16[8,256,128]{2,1,0:T(8,128)(2,1)S(1)} %collective-permute-done.5.beyond_ref, ...), custom_call_target="tpu_custom_call" | custom-call | flops 1 | bytes 1 | tf_op jit(solution)/shard_map/halo_blur/pallas_call | solution.py:155
  44.6 2.0 %collective-permute-done.8.halo_ref = bf16[256,1024]{1,0:T(8,128)(2,1)S(1)} collective-permute-done((bf16[256,1024]{1,0:T(8,128)(2,1)S(1)}, bf16[256,1024]{1,0:T(8,128)(2,1)S(1)}, u32[]{:S(2)}, u32[]{:S(2)}) %collective-permute-start.8) | collective-permute-done | bytes 524320 | tf_op jit(solution)/shard_map/ppermute | solution.py:328
  47.1 2.9 %collective-permute-start.11 = (bf16[256,1024]{1,0:T(8,128)(2,1)S(1)}, bf16[256,1024]{1,0:T(8,128)(2,1)S(1)}, u32[]{:S(2)}, u32[]{:S(2)}) collective-permute-start(bf16[256,1024]{1,0:T(8,128)(2,1)S(1)} %join_score.2), channel_id=1, source_target_pairs={{4,0},{14,2},{8,4},{2,6},{12,8},{6,10},{0,12},{10,14},{5,1},{15,3}... | collective-permute-start | bytes 1572872 | tf_op jit(solution)/shard_map/ppermute | solution.py:335
  50.0 8.6 %collective-permute-done.7.halo_ref = bf16[256,1024]{1,0:T(8,128)(2,1)S(1)} collective-permute-done((bf16[256,1024]{1,0:T(8,128)(2,1)S(1)}, bf16[256,1024]{1,0:T(8,128)(2,1)S(1)}, u32[]{:S(2)}, u32[]{:S(2)}) %collective-permute-start.7) | collective-permute-done | bytes 524320 | tf_op jit(solution)/shard_map/ppermute | solution.py:332
  60.1 1.6 %collective-permute-start.9 = (bf16[256,1024]{1,0:T(8,128)(2,1)S(1)}, bf16[256,1024]{1,0:T(8,128)(2,1)S(1)}, u32[]{:S(2)}, u32[]{:S(2)}) collective-permute-start(bf16[256,1024]{1,0:T(8,128)(2,1)S(1)} %join_score.3), channel_id=1, source_target_pairs={{4,0},{14,2},{8,4},{2,6},{12,8},{6,10},{0,12},{10,14},{5,1},{15,3}... | collective-permute-start | bytes 1572872 | tf_op jit(solution)/shard_map/ppermute | solution.py:341
  62.2 2.8 %collective-permute-start.14 = (bf16[256,1024]{1,0:T(8,128)(2,1)S(1)}, bf16[256,1024]{1,0:T(8,128)(2,1)S(1)}, u32[]{:S(2)}, u32[]{:S(2)}) collective-permute-start(bf16[256,1024]{1,0:T(8,128)(2,1)S(1)} %collective-permute-done.11), channel_id=1, source_target_pairs={{0,2},{2,0},{4,6},{6,4},{8,10},{10,8},{12,14},{14,12},{1,3},{3,1},... | collective-permute-start | bytes 1572872 | tf_op jit(solution)/shard_map/ppermute | solution.py:340
  65.0 8.5 %collective-permute-done.10 = bf16[256,1024]{1,0:T(8,128)(2,1)S(1)} collective-permute-done((bf16[256,1024]{1,0:T(8,128)(2,1)S(1)}, bf16[256,1024]{1,0:T(8,128)(2,1)S(1)}, u32[]{:S(2)}, u32[]{:S(2)}) %collective-permute-start.10) | collective-permute-done | bytes 524320 | tf_op jit(solution)/shard_map/ppermute | solution.py:337
  74.2 23.0 %collective-permute-start.17 = (bf16[256,1024]{1,0:T(8,128)(2,1)S(1)}, bf16[256,1024]{1,0:T(8,128)(2,1)S(1)}, u32[]{:S(2)}, u32[]{:S(2)}) collective-permute-start(bf16[256,1024]{1,0:T(8,128)(2,1)S(1)} %join_score.3), channel_id=1, source_target_pairs={{0,4},{2,14},{4,8},{6,2},{8,12},{10,6},{12,0},{14,10},{1,5},{3,15}... | collective-permute-start | bytes 1572872 | tf_op jit(solution)/shard_map/ppermute | solution.py:345
  97.2 2.0 %collective-permute-start.13 = (bf16[256,1024]{1,0:T(8,128)(2,1)S(1)}, bf16[256,1024]{1,0:T(8,128)(2,1)S(1)}, u32[]{:S(2)}, u32[]{:S(2)}) collective-permute-start(bf16[256,1024]{1,0:T(8,128)(2,1)S(1)} %join_score.3), channel_id=1, source_target_pairs={{0,2},{2,0},{4,6},{6,4},{8,10},{10,8},{12,14},{14,12},{1,3},{3,1},... | collective-permute-start | bytes 1572872 | tf_op jit(solution)/shard_map/ppermute | solution.py:342
  100.1 3.8 %collective-permute-done.17 = bf16[256,1024]{1,0:T(8,128)(2,1)S(1)} collective-permute-done((bf16[256,1024]{1,0:T(8,128)(2,1)S(1)}, bf16[256,1024]{1,0:T(8,128)(2,1)S(1)}, u32[]{:S(2)}, u32[]{:S(2)}) %collective-permute-start.17) | collective-permute-done | bytes 524320 | tf_op jit(solution)/shard_map/ppermute | solution.py:345
  103.9 2.5 %collective-permute-done.18 = bf16[256,1024]{1,0:T(8,128)(2,1)S(1)} collective-permute-done((bf16[256,1024]{1,0:T(8,128)(2,1)S(1)}, bf16[256,1024]{1,0:T(8,128)(2,1)S(1)}, u32[]{:S(2)}, u32[]{:S(2)}) %collective-permute-start.18) | collective-permute-done | bytes 524320 | tf_op jit(solution)/shard_map/ppermute | solution.py:346
  106.5 5.5 %collective-permute-done.13 = bf16[256,1024]{1,0:T(8,128)(2,1)S(1)} collective-permute-done((bf16[256,1024]{1,0:T(8,128)(2,1)S(1)}, bf16[256,1024]{1,0:T(8,128)(2,1)S(1)}, u32[]{:S(2)}, u32[]{:S(2)}) %collective-permute-start.13) | collective-permute-done | bytes 524320 | tf_op jit(solution)/shard_map/ppermute | solution.py:342
  112.6 4.8 %tiles.2.refs_6_ = bf16[8,16,2,128,128]{4,3,2,1,0:T(8,128)(2,1)} custom-call(s32[8,16]{1,0:T(8,128)S(1)} %get-tuple-element.49.place_ref, s32[8,16]{1,0:T(8,128)S(1)} %fusion.18.present_ref, bf16[2,256,1024]{2,1,0:T(8,128)(2,1)S(1)} %pad_maximum_fusion.2.refs_0_, bf16[2,256,1024]{2,1,0:T(8,128)(2,1)S(1)} %collective-permute-done.20.refs_1_, ...), custom_call_target="tpu_custom_call" | custom-call | flops 1 | bytes 1 | tf_op jit(solution)/shard_map/tiles/pallas_call | solution.py:243
  117.4 4.8 %tiles.3 = bf16[8,16,2,128,128]{4,3,2,1,0:T(8,128)(2,1)} custom-call(s32[8,16]{1,0:T(8,128)S(1)} %get-tuple-element.50.place_ref, s32[8,16]{1,0:T(8,128)S(1)} %fusion.18.present_ref, bf16[2,256,1024]{2,1,0:T(8,128)(2,1)S(1)} %pad_maximum_fusion.refs_0_, bf16[2,256,1024]{2,1,0:T(8,128)(2,1)S(1)} %collective-permute-done.12.refs_1_, ...), custom_call_target="tpu_custom_call", output_to_operand_aliasing={{}: (8, {})} | custom-call | flops 1 | bytes 1 | tf_op jit(solution)/shard_map/tiles/pallas_call | solution.py:243
  (51 shorter events, 14.7 us)
Async XLA Ops:
  3.2 9.3 %collective-permute-start = (bf16[2,256,128]{2,1,0:T(8,128)(2,1)S(1)}, bf16[2,256,128]{2,1,0:T(8,128)(2,1)S(1)}, u32[]{:S(2)}, u32[]{:S(2)}) collective-permute-start(bf16[2,256,128]{2,1,0:T(8,128)(2,1)S(1)} %get-tuple-element.27), channel_id=1, source_target_pairs={{0,1},{1,0},{2,3},{3,2},{4,5},{5,4},{6,7},{7,6},{8,9},{9,8},{10,11... | collective-permute-start | bytes 393224 | tf_op jit(solution)/shard_map/ppermute | solution.py:277
  4.6 21.2 %collective-permute-start.3 = (bf16[8,256,128]{2,1,0:T(8,128)(2,1)}, bf16[8,256,128]{2,1,0:T(8,128)(2,1)S(1)}, u32[]{:S(2)}, u32[]{:S(2)}) collective-permute-start(bf16[8,256,128]{2,1,0:T(8,128)(2,1)} %broadcast_select_fusion.1), channel_id=1, source_target_pairs={{2,6},{4,0},{6,10},{8,4},{10,14},{12,8},{3,7},{5,1},{7,11},{9,5},{... | collective-permute-start | bytes 1572872 | tf_op jit(solution)/shard_map/ppermute | solution.py:313
  5.9 6.6 %collective-permute-start.1 = (s32[1,1024]{1,0:T(1,128)}, s32[1,1024]{1,0:T(1,128)S(1)}, u32[]{:S(2)}, u32[]{:S(2)}) collective-permute-start(s32[1,1024]{1,0:T(1,128)} %bitcast.23), channel_id=1, source_target_pairs={{0,2},{2,0},{4,6},{6,4},{8,10},{10,8},{12,14},{14,12},{1,3},{3,1},... | collective-permute-start | bytes 12296 | tf_op jit(solution)/shard_map/ppermute | solution.py:310
  16.6 23.5 %collective-permute-start.5 = (bf16[8,256,128]{2,1,0:T(8,128)(2,1)}, bf16[8,256,128]{2,1,0:T(8,128)(2,1)S(1)}, u32[]{:S(2)}, u32[]{:S(2)}) collective-permute-start(bf16[8,256,128]{2,1,0:T(8,128)(2,1)} %broadcast_select_fusion), channel_id=1, source_target_pairs={{2,6},{4,0},{6,10},{8,4},{10,14},{12,8},{3,7},{5,1},{7,11},{9,5},{... | collective-permute-start | bytes 1572872 | tf_op jit(solution)/shard_map/ppermute | solution.py:313
  18.0 1.4 %collective-permute-start.2 = (bf16[2,256,128]{2,1,0:T(8,128)(2,1)S(1)}, bf16[2,256,128]{2,1,0:T(8,128)(2,1)S(1)}, u32[]{:S(2)}, u32[]{:S(2)}) collective-permute-start(bf16[2,256,128]{2,1,0:T(8,128)(2,1)S(1)} %get-tuple-element.31), channel_id=1, source_target_pairs={{0,1},{1,0},{2,3},{3,2},{4,5},{5,4},{6,7},{7,6},{8,9},{9,8},{10,11... | collective-permute-start | bytes 393224 | tf_op jit(solution)/shard_map/ppermute | solution.py:277
  25.8 1.3 %collective-permute-start.4 = (bf16[256,128]{1,0:T(8,128)(2,1)S(1)}, bf16[256,128]{1,0:T(8,128)(2,1)S(1)}, u32[]{:S(2)}, u32[]{:S(2)}) collective-permute-start(bf16[256,128]{1,0:T(8,128)(2,1)S(1)} %select_bitcast_fusion.1), channel_id=1, source_target_pairs={{0,1},{1,0},{2,3},{3,2},{4,5},{5,4},{6,7},{7,6},{8,9},{9,8},{10,11... | collective-permute-start | bytes 196616 | tf_op jit(solution)/shard_map/ppermute | solution.py:277
  30.1 82.4 %copy-start.3 = (s32[8,16]{1,0:T(8,128)S(1)}, s32[8,16]{1,0:T(8,128)}, u32[]{:S(2)}) copy-start(s32[8,16]{1,0:T(8,128)} %param.5) | copy-start | bytes 1540
  30.1 16.5 %collective-permute-start.8 = (bf16[256,1024]{1,0:T(8,128)(2,1)S(1)}, bf16[256,1024]{1,0:T(8,128)(2,1)S(1)}, u32[]{:S(2)}, u32[]{:S(2)}) collective-permute-start(bf16[256,1024]{1,0:T(8,128)(2,1)S(1)} %halo_blur.2), channel_id=1, source_target_pairs={{0,2},{2,0},{4,6},{6,4},{8,10},{10,8},{12,14},{14,12},{1,3},{3,1},... | collective-permute-start | bytes 1572872 | tf_op jit(solution)/shard_map/ppermute | solution.py:328
  40.1 1.3 %collective-permute-start.6 = (bf16[256,128]{1,0:T(8,128)(2,1)S(1)}, bf16[256,128]{1,0:T(8,128)(2,1)S(1)}, u32[]{:S(2)}, u32[]{:S(2)}) collective-permute-start(bf16[256,128]{1,0:T(8,128)(2,1)S(1)} %select_bitcast_fusion), channel_id=1, source_target_pairs={{0,1},{1,0},{2,3},{3,2},{4,5},{5,4},{6,7},{7,6},{8,9},{9,8},{10,11... | collective-permute-start | bytes 196616 | tf_op jit(solution)/shard_map/ppermute | solution.py:277
  44.6 14.1 %collective-permute-start.7 = (bf16[256,1024]{1,0:T(8,128)(2,1)S(1)}, bf16[256,1024]{1,0:T(8,128)(2,1)S(1)}, u32[]{:S(2)}, u32[]{:S(2)}) collective-permute-start(bf16[256,1024]{1,0:T(8,128)(2,1)S(1)} %halo_blur.3), channel_id=1, source_target_pairs={{0,2},{2,0},{4,6},{6,4},{8,10},{10,8},{12,14},{14,12},{1,3},{3,1},... | collective-permute-start | bytes 1572872 | tf_op jit(solution)/shard_map/ppermute | solution.py:332
  47.1 14.5 %collective-permute-start.11 = (bf16[256,1024]{1,0:T(8,128)(2,1)S(1)}, bf16[256,1024]{1,0:T(8,128)(2,1)S(1)}, u32[]{:S(2)}, u32[]{:S(2)}) collective-permute-start(bf16[256,1024]{1,0:T(8,128)(2,1)S(1)} %join_score.2), channel_id=1, source_target_pairs={{4,0},{14,2},{8,4},{2,6},{12,8},{6,10},{0,12},{10,14},{5,1},{15,3}... | collective-permute-start | bytes 1572872 | tf_op jit(solution)/shard_map/ppermute | solution.py:335
  58.6 14.9 %collective-permute-start.10 = (bf16[256,1024]{1,0:T(8,128)(2,1)S(1)}, bf16[256,1024]{1,0:T(8,128)(2,1)S(1)}, u32[]{:S(2)}, u32[]{:S(2)}) collective-permute-start(bf16[256,1024]{1,0:T(8,128)(2,1)S(1)} %join_score.2), channel_id=1, source_target_pairs={{0,2},{2,0},{4,6},{6,4},{8,10},{10,8},{12,14},{14,12},{1,3},{3,1},... | collective-permute-start | bytes 1572872 | tf_op jit(solution)/shard_map/ppermute | solution.py:337
  60.1 14.1 %collective-permute-start.9 = (bf16[256,1024]{1,0:T(8,128)(2,1)S(1)}, bf16[256,1024]{1,0:T(8,128)(2,1)S(1)}, u32[]{:S(2)}, u32[]{:S(2)}) collective-permute-start(bf16[256,1024]{1,0:T(8,128)(2,1)S(1)} %join_score.3), channel_id=1, source_target_pairs={{4,0},{14,2},{8,4},{2,6},{12,8},{6,10},{0,12},{10,14},{5,1},{15,3}... | collective-permute-start | bytes 1572872 | tf_op jit(solution)/shard_map/ppermute | solution.py:341
  61.7 37.8 %collective-permute-start.15 = (bf16[256,1024]{1,0:T(8,128)(2,1)S(1)}, bf16[256,1024]{1,0:T(8,128)(2,1)S(1)}, u32[]{:S(2)}, u32[]{:S(2)}) collective-permute-start(bf16[256,1024]{1,0:T(8,128)(2,1)S(1)} %join_score.2), channel_id=1, source_target_pairs={{0,4},{2,14},{4,8},{6,2},{8,12},{10,6},{12,0},{14,10},{1,5},{3,15}... | collective-permute-start | bytes 1572872 | tf_op jit(solution)/shard_map/ppermute | solution.py:339
  62.2 37.3 %collective-permute-start.14 = (bf16[256,1024]{1,0:T(8,128)(2,1)S(1)}, bf16[256,1024]{1,0:T(8,128)(2,1)S(1)}, u32[]{:S(2)}, u32[]{:S(2)}) collective-permute-start(bf16[256,1024]{1,0:T(8,128)(2,1)S(1)} %collective-permute-done.11), channel_id=1, source_target_pairs={{0,2},{2,0},{4,6},{6,4},{8,10},{10,8},{12,14},{14,12},{1,3},{3,1},... | collective-permute-start | bytes 1572872 | tf_op jit(solution)/shard_map/ppermute | solution.py:340
  74.2 29.7 %collective-permute-start.17 = (bf16[256,1024]{1,0:T(8,128)(2,1)S(1)}, bf16[256,1024]{1,0:T(8,128)(2,1)S(1)}, u32[]{:S(2)}, u32[]{:S(2)}) collective-permute-start(bf16[256,1024]{1,0:T(8,128)(2,1)S(1)} %join_score.3), channel_id=1, source_target_pairs={{0,4},{2,14},{4,8},{6,2},{8,12},{10,6},{12,0},{14,10},{1,5},{3,15}... | collective-permute-start | bytes 1572872 | tf_op jit(solution)/shard_map/ppermute | solution.py:345
  97.2 9.2 %collective-permute-start.18 = (bf16[256,1024]{1,0:T(8,128)(2,1)S(1)}, bf16[256,1024]{1,0:T(8,128)(2,1)S(1)}, u32[]{:S(2)}, u32[]{:S(2)}) collective-permute-start(bf16[256,1024]{1,0:T(8,128)(2,1)S(1)} %collective-permute-done.9), channel_id=1, source_target_pairs={{0,2},{2,0},{4,6},{6,4},{8,10},{10,8},{12,14},{14,12},{1,3},{3,1},... | collective-permute-start | bytes 1572872 | tf_op jit(solution)/shard_map/ppermute | solution.py:346
  97.2 14.8 %collective-permute-start.13 = (bf16[256,1024]{1,0:T(8,128)(2,1)S(1)}, bf16[256,1024]{1,0:T(8,128)(2,1)S(1)}, u32[]{:S(2)}, u32[]{:S(2)}) collective-permute-start(bf16[256,1024]{1,0:T(8,128)(2,1)S(1)} %join_score.3), channel_id=1, source_target_pairs={{0,2},{2,0},{4,6},{6,4},{8,10},{10,8},{12,14},{14,12},{1,3},{3,1},... | collective-permute-start | bytes 1572872 | tf_op jit(solution)/shard_map/ppermute | solution.py:342
  99.4 13.1 %collective-permute-start.20 = (bf16[2,256,1024]{2,1,0:T(8,128)(2,1)S(1)}, bf16[2,256,1024]{2,1,0:T(8,128)(2,1)S(1)}, u32[]{:S(2)}, u32[]{:S(2)}) collective-permute-start(bf16[2,256,1024]{2,1,0:T(8,128)(2,1)S(1)} %pad_maximum_fusion.2.refs_0_), channel_id=1, source_target_pairs={{0,1},{1,0},{2,3},{3,2},{4,5},{5,4},{6,7},{7,6},{8,9},{9,8},{10,11... | collective-permute-start | bytes 3145736 | tf_op jit(solution)/shard_map/ppermute | solution.py:277
  99.5 17.8 %collective-permute-start.12 = (bf16[2,256,1024]{2,1,0:T(8,128)(2,1)S(1)}, bf16[2,256,1024]{2,1,0:T(8,128)(2,1)S(1)}, u32[]{:S(2)}, u32[]{:S(2)}) collective-permute-start(bf16[2,256,1024]{2,1,0:T(8,128)(2,1)S(1)} %pad_maximum_fusion.refs_0_), channel_id=1, source_target_pairs={{0,1},{1,0},{2,3},{3,2},{4,5},{5,4},{6,7},{7,6},{8,9},{9,8},{10,11... | collective-permute-start | bytes 3145736 | tf_op jit(solution)/shard_map/ppermute | solution.py:277
  103.9 8.1 %collective-permute-start.22 = (bf16[1,256,1024]{2,1,0:T(8,128)(2,1)S(1)}, bf16[1,256,1024]{2,1,0:T(8,128)(2,1)S(1)}, u32[]{:S(2)}, u32[]{:S(2)}) collective-permute-start(bf16[1,256,1024]{2,1,0:T(8,128)(2,1)S(1)} %bitcast.19), channel_id=1, source_target_pairs={{0,1},{1,0},{2,3},{3,2},{4,5},{5,4},{6,7},{7,6},{8,9},{9,8},{10,11... | collective-permute-start | bytes 1572872 | tf_op jit(solution)/shard_map/ppermute | solution.py:277
  106.4 6.2 %collective-permute-start.21 = (bf16[2,256,1024]{2,1,0:T(8,128)(2,1)S(1)}, bf16[2,256,1024]{2,1,0:T(8,128)(2,1)S(1)}, u32[]{:S(2)}, u32[]{:S(2)}) collective-permute-start(bf16[2,256,1024]{2,1,0:T(8,128)(2,1)S(1)} %pad_maximum_fusion.3.refs_2_), channel_id=1, source_target_pairs={{0,1},{1,0},{2,3},{3,2},{4,5},{5,4},{6,7},{7,6},{8,9},{9,8},{10,11... | collective-permute-start | bytes 3145736 | tf_op jit(solution)/shard_map/ppermute | solution.py:277
  112.0 5.4 %collective-permute-start.19 = (bf16[2,256,1024]{2,1,0:T(8,128)(2,1)S(1)}, bf16[2,256,1024]{2,1,0:T(8,128)(2,1)S(1)}, u32[]{:S(2)}, u32[]{:S(2)}) collective-permute-start(bf16[2,256,1024]{2,1,0:T(8,128)(2,1)S(1)} %pad_maximum_fusion.1.refs_4_), channel_id=1, source_target_pairs={{0,1},{1,0},{2,3},{3,2},{4,5},{5,4},{6,7},{7,6},{8,9},{9,8},{10,11... | collective-permute-start | bytes 3145736 | tf_op jit(solution)/shard_map/ppermute | solution.py:277
  112.0 5.4 %collective-permute-start.16 = (bf16[1,256,1024]{2,1,0:T(8,128)(2,1)S(1)}, bf16[1,256,1024]{2,1,0:T(8,128)(2,1)S(1)}, u32[]{:S(2)}, u32[]{:S(2)}) collective-permute-start(bf16[1,256,1024]{2,1,0:T(8,128)(2,1)S(1)} %bitcast.21), channel_id=1, source_target_pairs={{0,1},{1,0},{2,3},{3,2},{4,5},{5,4},{6,7},{7,6},{8,9},{9,8},{10,11... | collective-permute-start | bytes 1572872 | tf_op jit(solution)/shard_map/ppermute | solution.py:277
  (3 other events, 3.9 us)

commit v10 on v9

--- a/solution.py
+++ b/solution.py
@@ -15,42 +15,50 @@
 VMEM_BYTES = 20 * 1024 * 1024
 
 
-def faces_kernel(col_ref, bold_ref, first_ref, last_ref, edge_ref, wide):
-    frames, slab_x, slab_y, slab_z = bold_ref.shape[1:]
+def faces_kernel(place_ref, bold_ref, *refs):
+    windows, frames, slab_x, slab_y, slab_z = bold_ref.shape
     per_frame = slab_x * slab_y
-    wide[...] = bold_ref[0].reshape(frames * per_frame, slab_z).astype(jnp.float32)
-    for x, layer_ref in enumerate((first_ref, last_ref)):
-        for y in range(slab_y):
-            plane = wide[pl.ds(x * slab_y + y, frames, stride=per_frame), :]
-            layer_ref[y] = plane.astype(jnp.bfloat16)
-        @pl.when(col_ref[0] == 0)
-        def _():
-            edge_ref[x] = layer_ref[slab_y - 1]
-
-        @pl.when(col_ref[0] != 0)
-        def _():
-            edge_ref[x] = layer_ref[0]
-
-
-def make_faces(window, col, bold):
-    _, frames, slab_x, slab_y, slab_z = bold.shape
+    wide = refs[-1]
+    for window in range(windows):
+        near_ref, outer_ref, edge_ref = refs[3 * window : 3 * window + 3]
+        wide[...] = bold_ref[window].reshape(frames * per_frame, slab_z).astype(jnp.float32)
+
+        def plane(x, y):
+            taken = wide[pl.ds(x * slab_y + y, frames, stride=per_frame), :]
+            return taken.astype(jnp.bfloat16)
+
+        def layers(first_ref, last_ref):
+            for y in range(slab_y):
+                first_ref[y] = plane(0, y)
+                last_ref[y] = plane(1, y)
+
+        pl.when(place_ref[1] == 0)(functools.partial(layers, outer_ref, near_ref))
+        pl.when(place_ref[1] != 0)(functools.partial(layers, near_ref, outer_ref))
+
+        def edges(y):
+            for x in range(slab_x):
+                edge_ref[x] = plane(x, y)
+
+        pl.when(place_ref[0] == 0)(functools.partial(edges, slab_y - 1))
+        pl.when(place_ref[0] != 0)(functools.partial(edges, 0))
+
+
+def make_faces(place, bold):
+    windows, frames, slab_x, slab_y, slab_z = bold.shape
     layer = jax.ShapeDtypeStruct((slab_y, frames, slab_z), jnp.bfloat16)
     edge = jax.ShapeDtypeStruct((slab_x, frames, slab_z), jnp.bfloat16)
     whole = lambda array: pl.BlockSpec(array.shape, lambda _: (0,) * len(array.shape))
     return pl.pallas_call(
         faces_kernel,
         grid=(1,),
-        in_specs=[
-            pl.BlockSpec(memory_space=pltpu.SMEM),
-            pl.BlockSpec((1, frames, slab_x, slab_y, slab_z), lambda _: (window, 0, 0, 0, 0)),
-        ],
-        out_specs=[whole(layer), whole(layer), whole(edge)],
-        out_shape=[layer, layer, edge],
+        in_specs=[pl.BlockSpec(memory_space=pltpu.SMEM), whole(bold)],
+        out_specs=[whole(layer), whole(layer), whole(edge)] * windows,
+        out_shape=[layer, layer, edge] * windows,
         scratch_shapes=[pltpu.VMEM((frames * slab_x * slab_y, slab_z), jnp.float32)],
         compiler_params=pltpu.CompilerParams(vmem_limit_bytes=VMEM_BYTES),
         cost_estimate=SMALL,
         name="faces",
-    )(col, bold)
+    )(place, bold)
 
 
 def three_taps(before, here, after):
@@ -92,19 +100,23 @@
 
 
 def inner_kernel(
-    place_ref, first_ref, last_ref, edge_ref, gm_ref, out_ref, planes, high, middle, low
+    place_ref, near_ref, outer_ref, edge_ref, gm_ref, out_ref, planes, high, middle, low
 ):
-    slab_y, frames, slab_z = first_ref.shape
+    slab_y, frames, slab_z = near_ref.shape
     slab_x = edge_ref.shape[0]
+    even = place_ref[1] == 0
 
     def two_taps(here, other):
-        return CENTRE * here.astype(jnp.float32) + SIDE * other.astype(jnp.float32)
+        return CENTRE * here + SIDE * other
 
     for y in range(slab_y):
-        planes[0, y + 1] = two_taps(first_ref[y], last_ref[y])
-        planes[1, y + 1] = two_taps(last_ref[y], first_ref[y])
+        near, outer = near_ref[y].astype(jnp.float32), outer_ref[y].astype(jnp.float32)
+        first, last = jnp.where(even, outer, near), jnp.where(even, near, outer)
+        planes[0, y + 1] = two_taps(first, last)
+        planes[1, y + 1] = two_taps(last, first)
+    edges = [edge_ref[x].astype(jnp.float32) for x in range(slab_x)]
     for x in range(slab_x):
-        place_edge(planes, x, two_taps(edge_ref[x], edge_ref[1 - x]), place_ref[0])
+        place_edge(planes, x, two_taps(edges[x], edges[1 - x]), place_ref[0])
     for x in range(slab_x):
         for y in range(slab_y):
             part = along_z(three_taps(planes[x, y], planes[x, y + 1], planes[x, y + 2]))
@@ -117,10 +129,9 @@
 
 
 def halo_kernel(
-    place_ref, first_ref, last_ref, beyond_ref, edge_ref, corner_ref, gm_ref, out_ref,
-    planes, scored,
+    place_ref, near_ref, beyond_ref, edge_ref, corner_ref, gm_ref, out_ref, planes, scored
 ):
-    slab_y, frames, slab_z = first_ref.shape
+    slab_y, frames, slab_z = near_ref.shape
     even = place_ref[1] == 0
 
     def sides(own, beyond):
@@ -128,8 +139,7 @@
         return jnp.where(even, own, beyond), jnp.where(even, beyond, own)
 
     for y in range(slab_y):
-        own = jnp.where(even, last_ref[y], first_ref[y])
-        planes[0, y + 1], planes[1, y + 1] = sides(own, beyond_ref[y])
+        planes[0, y + 1], planes[1, y + 1] = sides(near_ref[y], beyond_ref[y])
     own = jnp.where(even, edge_ref[1], edge_ref[0])
     for x, edge in enumerate(sides(own, corner_ref[...])):
         place_edge(planes, x, edge, place_ref[0])
@@ -172,19 +182,19 @@
     return [planes] + [pltpu.VMEM((frames, 2 * slab_y * slab_z), jnp.bfloat16)] * terms
 
 
-def make_inner(place, first, last, edge, gm):
-    operands = (first, last, edge, gm)
-    scratch = blur_scratch(first, 3)
+def make_inner(place, near, outer, edge, gm):
+    operands = (near, outer, edge, gm)
+    scratch = blur_scratch(near, 3)
     return call_on_rows(
-        inner_kernel, jnp.float32, first.shape[1], place, operands, scratch, "inner_blur"
+        inner_kernel, jnp.float32, near.shape[1], place, operands, scratch, "inner_blur"
     )
 
 
-def make_halo(place, first, last, beyond, edge, corner, gm):
-    operands = (first, last, beyond, edge, corner, gm)
-    scratch = blur_scratch(first, 1)
+def make_halo(place, near, beyond, edge, corner, gm):
+    operands = (near, beyond, edge, corner, gm)
+    scratch = blur_scratch(near, 1)
     return call_on_rows(
-        halo_kernel, jnp.bfloat16, first.shape[1], place, operands, scratch, "halo_blur"
+        halo_kernel, jnp.bfloat16, near.shape[1], place, operands, scratch, "halo_blur"
     )
 
 
@@ -294,12 +304,8 @@
     away = (slab % col_total != col).astype(jnp.int32)
     within = ids % blocks
     present = partners >= 0
-    parts_0 = jnp.where(kind == 4, 8 + away, kind // 2 * 4 + kind % 2 + 2 * away)
-    parts_1 = jnp.where(kind == 3, 4 + away, jnp.where(kind < 2, kind, kind // 2 + 5) + 2 * away)
-    place_0, place_1 = (
-        jnp.where(present, part * blocks + within, 0).astype(jnp.int32)
-        for part in (parts_0, parts_1)
-    )
+    part = jnp.where(kind == 4, 8 + away, kind // 2 * 4 + kind % 2 + 2 * away)
+    place = jnp.where(present, part * blocks + within, 0).astype(jnp.int32)
     present = present.astype(jnp.int32)
 
     def both(*parts):
@@ -309,48 +315,42 @@
     windows = bold.shape[0]
     gm_pair = lax.ppermute(gm, "row", in_pair)
 
-    def outer(first, last):
-        return lax.ppermute(jnp.where(even, first, last), "row", two_on)
-
-    def halo_for_pair(first, last, beyond, edge):
+    def give_halo(near, beyond, edge):
         corner = other_col(jnp.where(col == 0, beyond[-1], beyond[0]))
-        return make_halo(here, first, last, beyond, edge, corner, gm_pair)
-
-    first_0, last_0, face_0 = make_faces(0, here, bold)
-    beyond_0 = outer(first_0, last_0)
-    edge_0 = other_col(face_0)
-    first_1, last_1, face_1 = make_faces(1, here, after(bold, edge_0, gm_pair))
-    beyond_1 = outer(first_1, last_1)
-    edge_1 = other_col(face_1)
-    inner_0 = make_inner(here, first_0, last_0, edge_0, after(gm, edge_1))
+        return make_halo(here, near, beyond, edge, corner, gm_pair)
+
+    near_0, outer_0, face_0, near_1, outer_1, face_1 = make_faces(after(here, gm_pair), bold)
+    beyond_0 = lax.ppermute(outer_0, "row", two_on)
+    edge_0, edge_1 = other_col(face_0), other_col(face_1)
+    inner_0 = make_inner(here, near_0, outer_0, edge_0, after(gm, edge_1))
     beyond_0 = after(beyond_0, inner_0)
-    given_0 = halo_for_pair(first_0, last_0, beyond_0, edge_0)
+    beyond_1 = lax.ppermute(after(outer_1, beyond_0), "row", two_on)
+    given_0 = give_halo(near_0, beyond_0, edge_0)
     halo_0 = lax.ppermute(given_0, "row", in_pair)
-    inner_1 = make_inner(here, first_1, last_1, edge_1, after(gm, given_0))
-    beyond_1 = after(beyond_1, inner_1)
-    given_1 = halo_for_pair(first_1, last_1, beyond_1, edge_1)
+    inner_1 = make_inner(here, near_1, outer_1, edge_1, after(gm, given_0))
+    given_1 = give_halo(near_1, after(beyond_1, inner_1), edge_1)
     halo_1 = lax.ppermute(given_1, "row", in_pair)
     own_0 = join(inner_0, after(halo_0, given_1))
+    ahead_0 = lax.ppermute(own_0, "row", ahead)
+    behind_0 = lax.ppermute(own_0, "row", behind)
     halo_1 = after(halo_1, own_0)
-    ahead_0 = lax.ppermute(own_0, "row", ahead)
     own_1 = join(inner_1, halo_1)
     pair_0 = lax.ppermute(after(own_0, halo_1), "row", in_pair)
-    ahead_0 = after(ahead_0, own_1)
-    behind_0 = lax.ppermute(after(own_0, ahead_0), "row", behind)
+    pair_1 = lax.ppermute(own_1, "row", in_pair)
+    ahead_1 = lax.ppermute(own_1, "row", ahead)
+    behind_1 = lax.ppermute(own_1, "row", behind)
+    ahead_0, behind_0 = after(ahead_0, own_1), after(behind_0, own_1)
     rest_0 = lax.ppermute(ahead_0, "row", in_pair)
-    ahead_1 = lax.ppermute(own_1, "row", ahead)
-    pair_1 = lax.ppermute(own_1, "row", in_pair)
-    pair_0 = after(pair_0, ahead_0)
-    ahead_1 = after(ahead_1, pair_0)
-    behind_1 = lax.ppermute(after(own_1, ahead_1), "row", behind)
+    pair_0, pair_1 = after(pair_0, ahead_0, behind_0), after(pair_1, ahead_0, behind_0)
+    ahead_1 = after(ahead_1, pair_0, pair_1)
+    behind_1 = after(behind_1, ahead_1)
     rest_1 = lax.ppermute(ahead_1, "row", in_pair)
-    behind_0, rest_0 = after(behind_0, ahead_1), after(rest_0, ahead_1)
-    pair_1 = after(pair_1, rest_0, behind_0)
+    rest_0 = after(rest_0, ahead_1, behind_1)
     sources_0 = both(own_0, ahead_0) + both(behind_0, pair_0) + both(rest_0)
-    sources_1 = both(own_1, ahead_1) + both(pair_1)
-    sources_1 += both(behind_1, rest_1)
-    out = make_tiles(0, windows, place_0, present, sources_0, None)
-    return make_tiles(1, windows, place_1, present, sources_1, out)
+    out = make_tiles(0, windows, place, present, sources_0, None)
+    rest_1 = after(rest_1, out)
+    sources_1 = both(own_1, ahead_1) + both(behind_1, pair_1) + both(rest_1)
+    return make_tiles(1, windows, place, present, sources_1, out)
 
 
 def solution(mesh):

time: 123 us -> 120 us (0.976)
  starting transfers between devices: 47.6 us -> 21.3 us
  waiting for transfers between devices: 37.1 us -> 55.1 us
  Pallas kernels: 31.1 us -> 34.7 us
  local copies, waits for them, and re-layouts: 3.88 us -> 5.87 us
    ppermute x4, waiting for transfers between devices: 3.78 us -> 26.9 us  [the longest x1 11.1 us: on_device(): behind_0 = lax.ppermute(own_0, 'row', behind)]
    ppermute x4, starting transfers between devices: 26.2 us -> 3.39 us  [the longest x1 1.46 us: on_device(): beyond_1 = lax.ppermute(after(outer_1, beyond_0), 'row', two_on)]
    ppermute x1, waiting for transfers between devices: 8.46 us -> 0.01 us  [on_device(): pair_0 = lax.ppermute(after(own_0, halo_1), 'row', in_pair)]
    pallas_call x2, Pallas kernels: 9.53 us -> 12.5 us  [make_tiles(): pl.pallas_call(functools.partial(tiles_kernel, sources=count, window=wind...]
    ppermute x1, waiting for transfers between devices: 5.51 us -> 8.07 us  [on_device(): pair_1 = lax.ppermute(own_1, 'row', in_pair)]
    another operation x4, other arithmetic: 0.39 us -> 2.42 us  [both(): near = jnp.stack(parts, 0)]
    unnamed x8 -> x16, local copies, waits for them, and re-layouts: 3.88 us -> 5.87 us
    ppermute x10, waiting for transfers between devices: 3.7 us -> 5.63 us  [other_col(): return lax.ppermute(value, 'col', [(0, 1), (1, 0)])]
  transfers between devices with their start and end apart: 23 -> 23, of which waited for: 11 -> 14; matrix products, arithmetic and copies ran while one was open for 2% -> 2% of each run, Pallas kernels for 20% -> 21%
where the time goes in v10:
time: 120 us
  waiting for transfers between devices  55.1 us (46%)
  Pallas kernels  34.7 us (29%)
  starting transfers between devices  21.3 us (18%)
  local copies, waits for them, and re-layouts  5.87 us (5%)
  other arithmetic  2.56 us (2%)
    pallas_call x6, Pallas kernels, call_on_rows(): pl.pallas_call(kernel, grid=(1,), in_specs=[pl.BlockSpec(memory_space=plt...  18.6 us
    pallas_call x2, Pallas kernels, make_tiles(): pl.pallas_call(functools.partial(tiles_kernel, sources=count, window=wind...  12.5 us
    ppermute x1, waiting for transfers between devices, on_device(): behind_0 = lax.ppermute(own_0, 'row', behind)  11.1 us
    ppermute x1, waiting for transfers between devices, on_device(): behind_1 = lax.ppermute(own_1, 'row', behind)  10.3 us
    ppermute x1, waiting for transfers between devices, on_device(): halo_1 = lax.ppermute(given_1, 'row', in_pair)  9.77 us
    ppermute x1, waiting for transfers between devices, on_device(): pair_1 = lax.ppermute(own_1, 'row', in_pair)  8.07 us
    unnamed x16, local copies, waits for them, and re-layouts  5.87 us
    ppermute x10, waiting for transfers between devices, other_col(): return lax.ppermute(value, 'col', [(0, 1), (1, 0)])  5.63 us
  transfers between devices with their start and end apart: 23, of which 14 were waited for; matrix products, arithmetic and copies ran while one was open for 2% of the time, Pallas kernels for 21%

profile of v10, /device:TPU:0, one launch (start us, length us, event | category | flops | bytes accessed | tf_op | source)
XLA Modules:
  0.0 120.1 jit_solution(11857791214152678202)
XLA Ops:
  0.0 3.0 %collective-permute-start = (s32[1,1024]{1,0:T(1,128)}, s32[1,1024]{1,0:T(1,128)S(1)}, u32[]{:S(2)}, u32[]{:S(2)}) collective-permute-start(s32[1,1024]{1,0:T(1,128)} %bitcast.21), channel_id=1, source_target_pairs={{0,2},{2,0},{4,6},{6,4},{8,10},{10,8},{12,14},{14,12},{1,3},{3,1},... | collective-permute-start | bytes 12296 | tf_op jit(solution)/shard_map/ppermute | solution.py:316
  3.0 1.7 %collective-permute-done.gm_ref = s32[1,1024]{1,0:T(1,128)S(1)} collective-permute-done((s32[1,1024]{1,0:T(1,128)}, s32[1,1024]{1,0:T(1,128)S(1)}, u32[]{:S(2)}, u32[]{:S(2)}) %collective-permute-start) | collective-permute-done | bytes 4128 | tf_op jit(solution)/shard_map/ppermute | solution.py:316
  4.8 1.6 %copy-done = bf16[2,256,2,8,128]{4,3,2,1,0:T(8,128)(2,1)S(1)} copy-done((bf16[2,256,2,8,128]{4,3,2,1,0:T(8,128)(2,1)S(1)}, bf16[2,256,2,8,128]{4,3,2,1,0:T(8,128)(2,1)}, u32[]{:S(2)}) %copy-start) | copy-done | bytes 2097176
  6.4 3.6 %faces.1 = (bf16[8,256,128]{2,1,0:T(8,128)(2,1)S(1)}, bf16[8,256,128]{2,1,0:T(8,128)(2,1)S(1)}, bf16[2,256,128]{2,1,0:T(8,128)(2,1)S(1)}, bf16[8,256,128]{2,1,0:...) custom-call(s32[2]{0:T(128)S(1)} %pad_add_fusion.place_ref, ...), custom_call_target="tpu_custom_call" | custom-call | flops 1 | bytes 1 | tf_op jit(solution)/shard_map/faces/pallas_call | solution.py:51
  9.9 1.3 %collective-permute-start.2 = (bf16[8,256,128]{2,1,0:T(8,128)(2,1)S(1)}, bf16[8,256,128]{2,1,0:T(8,128)(2,1)S(1)}, u32[]{:S(2)}, u32[]{:S(2)}) collective-permute-start(bf16[8,256,128]{2,1,0:T(8,128)(2,1)S(1)} %get-tuple-element.33.outer_ref), channel_id=1, source_target_pairs={{2,6},{4,0},{6,10},{8,4},{10,14},{12,8},{3,7},{5,1},{7,11},{9,5},{... | collective-permute-start | bytes 1572872 | tf_op jit(solution)/shard_map/ppermute | solution.py:323
  13.5 5.7 %inner_blur.2.inner_ref = f32[256,1024]{1,0:T(8,128)S(1)} custom-call(s32[2]{0:T(128)S(1)} %pad_add_fusion.place_ref, bf16[8,256,128]{2,1,0:T(8,128)(2,1)S(1)} %get-tuple-element.32.near_ref, bf16[8,256,128]{2,1,0:T(8,128)(2,1)S(1)} %get-tuple-element.33.outer_ref, bf16[2,256,128]{2,1,0:T(8,128)(2,1)S(1)} %collective-permute-done.3.edge_ref, ...), custom_call_target="tpu_custom_call" | custom-call | flops 1 | bytes 1 | tf_op jit(solution)/shard_map/inner_blur/pallas_call | solution.py:165
  19.2 5.5 %collective-permute-done.2.beyond_ref = bf16[8,256,128]{2,1,0:T(8,128)(2,1)S(1)} collective-permute-done((bf16[8,256,128]{2,1,0:T(8,128)(2,1)S(1)}, bf16[8,256,128]{2,1,0:T(8,128)(2,1)S(1)}, u32[]{:S(2)}, u32[]{:S(2)}) %collective-permute-start.2) | collective-permute-done | bytes 524320 | tf_op jit(solution)/shard_map/ppermute | solution.py:323
  24.7 1.5 %collective-permute-start.5 = (bf16[8,256,128]{2,1,0:T(8,128)(2,1)}, bf16[8,256,128]{2,1,0:T(8,128)(2,1)S(1)}, u32[]{:S(2)}, u32[]{:S(2)}) collective-permute-start(bf16[8,256,128]{2,1,0:T(8,128)(2,1)} %get-tuple-element.38.outer_ref), channel_id=1, source_target_pairs={{2,6},{4,0},{6,10},{8,4},{10,14},{12,8},{3,7},{5,1},{7,11},{9,5},{... | collective-permute-start | bytes 1572872 | tf_op jit(solution)/shard_map/ppermute | solution.py:327
  27.5 2.9 %halo_blur.2 = bf16[256,1024]{1,0:T(8,128)(2,1)S(1)} custom-call(s32[2]{0:T(128)S(1)} %pad_add_fusion.place_ref, bf16[8,256,128]{2,1,0:T(8,128)(2,1)S(1)} %get-tuple-element.32.near_ref, bf16[8,256,128]{2,1,0:T(8,128)(2,1)S(1)} %collective-permute-done.2.beyond_ref, bf16[2,256,128]{2,1,0:T(8,128)(2,1)S(1)} %collective-permute-done.3.edge_ref, ...), custom_call_target="tpu_custom_call" | custom-call | flops 1 | bytes 1 | tf_op jit(solution)/shard_map/halo_blur/pallas_call | solution.py:165
  30.4 4.0 %collective-permute-start.8 = (bf16[256,1024]{1,0:T(8,128)(2,1)S(1)}, bf16[256,1024]{1,0:T(8,128)(2,1)S(1)}, u32[]{:S(2)}, u32[]{:S(2)}) collective-permute-start(bf16[256,1024]{1,0:T(8,128)(2,1)S(1)} %halo_blur.2), channel_id=1, source_target_pairs={{0,2},{2,0},{4,6},{6,4},{8,10},{10,8},{12,14},{14,12},{1,3},{3,1},... | collective-permute-start | bytes 1572872 | tf_op jit(solution)/shard_map/ppermute | solution.py:329
  35.1 6.2 %inner_blur.3.inner_ref = f32[256,1024]{1,0:T(8,128)S(1)} custom-call(s32[2]{0:T(128)S(1)} %pad_add_fusion.place_ref, bf16[8,256,128]{2,1,0:T(8,128)(2,1)S(1)} %get-tuple-element.29.near_ref, bf16[8,256,128]{2,1,0:T(8,128)(2,1)} %get-tuple-element.38.outer_ref, bf16[2,256,128]{2,1,0:T(8,128)(2,1)S(1)} %collective-permute-done.1.edge_ref, s32[1,1024]{1,0:T(1,128)S(1)} %bitcast.23), custom_call_target="tpu_custom_call" | custom-call | flops 1 | bytes 1 | tf_op jit(solution)/shard_map/inner_blur/pallas_call | solution.py:165
  42.6 2.9 %halo_blur.3 = bf16[256,1024]{1,0:T(8,128)(2,1)S(1)} custom-call(s32[2]{0:T(128)S(1)} %pad_add_fusion.place_ref, bf16[8,256,128]{2,1,0:T(8,128)(2,1)S(1)} %get-tuple-element.29.near_ref, bf16[8,256,128]{2,1,0:T(8,128)(2,1)S(1)} %collective-permute-done.5.beyond_ref, bf16[2,256,128]{2,1,0:T(8,128)(2,1)S(1)} %collective-permute-done.1.edge_ref, ...), custom_call_target="tpu_custom_call" | custom-call | flops 1 | bytes 1 | tf_op jit(solution)/shard_map/halo_blur/pallas_call | solution.py:165
  47.1 2.7 %collective-permute-start.11 = (bf16[256,1024]{1,0:T(8,128)(2,1)S(1)}, bf16[256,1024]{1,0:T(8,128)(2,1)S(1)}, u32[]{:S(2)}, u32[]{:S(2)}) collective-permute-start(bf16[256,1024]{1,0:T(8,128)(2,1)S(1)} %join_score.2), channel_id=1, source_target_pairs={{4,0},{14,2},{8,4},{2,6},{12,8},{6,10},{0,12},{10,14},{5,1},{15,3}... | collective-permute-start | bytes 1572872 | tf_op jit(solution)/shard_map/ppermute | solution.py:334
  49.8 9.8 %collective-permute-done.7.halo_ref = bf16[256,1024]{1,0:T(8,128)(2,1)S(1)} collective-permute-done((bf16[256,1024]{1,0:T(8,128)(2,1)S(1)}, bf16[256,1024]{1,0:T(8,128)(2,1)S(1)}, u32[]{:S(2)}, u32[]{:S(2)}) %collective-permute-start.7) | collective-permute-done | bytes 524320 | tf_op jit(solution)/shard_map/ppermute | solution.py:332
  60.3 1.8 %collective-permute-start.13 = (bf16[256,1024]{1,0:T(8,128)(2,1)S(1)}, bf16[256,1024]{1,0:T(8,128)(2,1)S(1)}, u32[]{:S(2)}, u32[]{:S(2)}) collective-permute-start(bf16[256,1024]{1,0:T(8,128)(2,1)S(1)} %join_score.3), channel_id=1, source_target_pairs={{0,2},{2,0},{4,6},{6,4},{8,10},{10,8},{12,14},{14,12},{1,3},{3,1},... | collective-permute-start | bytes 1572872 | tf_op jit(solution)/shard_map/ppermute | solution.py:339
  62.2 1.4 %collective-permute-start.9 = (bf16[256,1024]{1,0:T(8,128)(2,1)S(1)}, bf16[256,1024]{1,0:T(8,128)(2,1)}, u32[]{:S(2)}, u32[]{:S(2)}) collective-permute-start(bf16[256,1024]{1,0:T(8,128)(2,1)S(1)} %join_score.3), channel_id=1, source_target_pairs={{4,0},{14,2},{8,4},{2,6},{12,8},{6,10},{0,12},{10,14},{5,1},{15,3}... | collective-permute-start | bytes 1572872 | tf_op jit(solution)/shard_map/ppermute | solution.py:340
  64.2 11.1 %collective-permute-done.12 = bf16[256,1024]{1,0:T(8,128)(2,1)S(1)} collective-permute-done((bf16[256,1024]{1,0:T(8,128)(2,1)S(1)}, bf16[256,1024]{1,0:T(8,128)(2,1)S(1)}, u32[]{:S(2)}, u32[]{:S(2)}) %collective-permute-start.12) | collective-permute-done | bytes 524320 | tf_op jit(solution)/shard_map/ppermute | solution.py:335
  75.3 2.2 %collective-permute-start.20 = (bf16[256,1024]{1,0:T(8,128)(2,1)S(1)}, bf16[256,1024]{1,0:T(8,128)(2,1)S(1)}, u32[]{:S(2)}, u32[]{:S(2)}) collective-permute-start(bf16[256,1024]{1,0:T(8,128)(2,1)S(1)} %collective-permute-done.11), channel_id=1, source_target_pairs={{0,2},{2,0},{4,6},{6,4},{8,10},{10,8},{12,14},{14,12},{1,3},{3,1},... | collective-permute-start | bytes 1572872 | tf_op jit(solution)/shard_map/ppermute | solution.py:343
  77.6 8.1 %collective-permute-done.13 = bf16[256,1024]{1,0:T(8,128)(2,1)S(1)} collective-permute-done((bf16[256,1024]{1,0:T(8,128)(2,1)S(1)}, bf16[256,1024]{1,0:T(8,128)(2,1)S(1)}, u32[]{:S(2)}, u32[]{:S(2)}) %collective-permute-start.13) | collective-permute-done | bytes 524320 | tf_op jit(solution)/shard_map/ppermute | solution.py:339
  86.0 10.3 %collective-permute-done.15 = bf16[256,1024]{1,0:T(8,128)(2,1)S(1)} collective-permute-done((bf16[256,1024]{1,0:T(8,128)(2,1)S(1)}, bf16[256,1024]{1,0:T(8,128)(2,1)S(1)}, u32[]{:S(2)}, u32[]{:S(2)}) %collective-permute-start.15) | collective-permute-done | bytes 524320 | tf_op jit(solution)/shard_map/ppermute | solution.py:341
  103.5 6.0 %tiles.2.refs_6_ = bf16[8,16,2,128,128]{4,3,2,1,0:T(8,128)(2,1)} custom-call(s32[8,16]{1,0:T(8,128)S(1)} %fusion.10.place_ref, s32[8,16]{1,0:T(8,128)S(1)} %fusion.17.present_ref, bf16[2,256,1024]{2,1,0:T(8,128)(2,1)S(1)} %pad_maximum_fusion.2.refs_0_, bf16[2,256,1024]{2,1,0:T(8,128)(2,1)} %collective-permute-done.18.refs_1_, ...), custom_call_target="tpu_custom_call" | custom-call | flops 1 | bytes 1 | tf_op jit(solution)/shard_map/tiles/pallas_call | solution.py:253
  109.5 1.7 %collective-permute-done.17 = bf16[256,1024]{1,0:T(8,128)(2,1)} collective-permute-done((bf16[256,1024]{1,0:T(8,128)(2,1)}, bf16[256,1024]{1,0:T(8,128)(2,1)}, u32[]{:S(2)}, u32[]{:S(2)}) %collective-permute-start.17) | collective-permute-done | bytes 524320 | tf_op jit(solution)/shard_map/ppermute | solution.py:347
  111.3 2.1 %collective-permute-done.22.refs_5_ = bf16[1,256,1024]{2,1,0:T(8,128)(2,1)S(1)} collective-permute-done((bf16[1,256,1024]{2,1,0:T(8,128)(2,1)}, bf16[1,256,1024]{2,1,0:T(8,128)(2,1)S(1)}, u32[]{:S(2)}, u32[]{:S(2)}) %collective-permute-start.22) | collective-permute-done | bytes 524320 | tf_op jit(solution)/shard_map/ppermute | solution.py:287
  113.4 6.5 %tiles.3 = bf16[8,16,2,128,128]{4,3,2,1,0:T(8,128)(2,1)} custom-call(s32[8,16]{1,0:T(8,128)S(1)} %fusion.10.place_ref, s32[8,16]{1,0:T(8,128)S(1)} %fusion.17.present_ref, bf16[2,256,1024]{2,1,0:T(8,128)(2,1)S(1)} %pad_maximum_fusion.refs_0_, bf16[2,256,1024]{2,1,0:T(8,128)(2,1)} %collective-permute-done.14.refs_1_, ...), custom_call_target="tpu_custom_call", output_to_operand_aliasing={{}: (8, {})} | custom-call | flops 1 | bytes 1 | tf_op jit(solution)/shard_map/tiles/pallas_call | solution.py:253
  (56 shorter events, 16.2 us)
Async XLA Ops:
  0.0 4.8 %collective-permute-start = (s32[1,1024]{1,0:T(1,128)}, s32[1,1024]{1,0:T(1,128)S(1)}, u32[]{:S(2)}, u32[]{:S(2)}) collective-permute-start(s32[1,1024]{1,0:T(1,128)} %bitcast.21), channel_id=1, source_target_pairs={{0,2},{2,0},{4,6},{6,4},{8,10},{10,8},{12,14},{14,12},{1,3},{3,1},... | collective-permute-start | bytes 12296 | tf_op jit(solution)/shard_map/ppermute | solution.py:316
  9.9 14.7 %collective-permute-start.2 = (bf16[8,256,128]{2,1,0:T(8,128)(2,1)S(1)}, bf16[8,256,128]{2,1,0:T(8,128)(2,1)S(1)}, u32[]{:S(2)}, u32[]{:S(2)}) collective-permute-start(bf16[8,256,128]{2,1,0:T(8,128)(2,1)S(1)} %get-tuple-element.33.outer_ref), channel_id=1, source_target_pairs={{2,6},{4,0},{6,10},{8,4},{10,14},{12,8},{3,7},{5,1},{7,11},{9,5},{... | collective-permute-start | bytes 1572872 | tf_op jit(solution)/shard_map/ppermute | solution.py:323
  11.2 1.4 %collective-permute-start.1 = (bf16[2,256,128]{2,1,0:T(8,128)(2,1)S(1)}, bf16[2,256,128]{2,1,0:T(8,128)(2,1)S(1)}, u32[]{:S(2)}, u32[]{:S(2)}) collective-permute-start(bf16[2,256,128]{2,1,0:T(8,128)(2,1)S(1)} %get-tuple-element.31), channel_id=1, source_target_pairs={{0,1},{1,0},{2,3},{3,2},{4,5},{5,4},{6,7},{7,6},{8,9},{9,8},{10,11... | collective-permute-start | bytes 393224 | tf_op jit(solution)/shard_map/ppermute | solution.py:287
  11.3 1.5 %collective-permute-start.3 = (bf16[2,256,128]{2,1,0:T(8,128)(2,1)S(1)}, bf16[2,256,128]{2,1,0:T(8,128)(2,1)S(1)}, u32[]{:S(2)}, u32[]{:S(2)}) collective-permute-start(bf16[2,256,128]{2,1,0:T(8,128)(2,1)S(1)} %get-tuple-element.34), channel_id=1, source_target_pairs={{0,1},{1,0},{2,3},{3,2},{4,5},{5,4},{6,7},{7,6},{8,9},{9,8},{10,11... | collective-permute-start | bytes 393224 | tf_op jit(solution)/shard_map/ppermute | solution.py:287
  24.7 16.6 %collective-permute-start.5 = (bf16[8,256,128]{2,1,0:T(8,128)(2,1)}, bf16[8,256,128]{2,1,0:T(8,128)(2,1)S(1)}, u32[]{:S(2)}, u32[]{:S(2)}) collective-permute-start(bf16[8,256,128]{2,1,0:T(8,128)(2,1)} %get-tuple-element.38.outer_ref), channel_id=1, source_target_pairs={{2,6},{4,0},{6,10},{8,4},{10,14},{12,8},{3,7},{5,1},{7,11},{9,5},{... | collective-permute-start | bytes 1572872 | tf_op jit(solution)/shard_map/ppermute | solution.py:327
  26.2 1.3 %collective-permute-start.4 = (bf16[256,128]{1,0:T(8,128)(2,1)S(1)}, bf16[256,128]{1,0:T(8,128)(2,1)S(1)}, u32[]{:S(2)}, u32[]{:S(2)}) collective-permute-start(bf16[256,128]{1,0:T(8,128)(2,1)S(1)} %select_bitcast_fusion.1), channel_id=1, source_target_pairs={{0,1},{1,0},{2,3},{3,2},{4,5},{5,4},{6,7},{7,6},{8,9},{9,8},{10,11... | collective-permute-start | bytes 196616 | tf_op jit(solution)/shard_map/ppermute | solution.py:287
  30.4 16.2 %collective-permute-start.8 = (bf16[256,1024]{1,0:T(8,128)(2,1)S(1)}, bf16[256,1024]{1,0:T(8,128)(2,1)S(1)}, u32[]{:S(2)}, u32[]{:S(2)}) collective-permute-start(bf16[256,1024]{1,0:T(8,128)(2,1)S(1)} %halo_blur.2), channel_id=1, source_target_pairs={{0,2},{2,0},{4,6},{6,4},{8,10},{10,8},{12,14},{14,12},{1,3},{3,1},... | collective-permute-start | bytes 1572872 | tf_op jit(solution)/shard_map/ppermute | solution.py:329
  35.1 66.3 %copy-start.7 = (s32[8,16]{1,0:T(8,128)S(1)}, s32[8,16]{1,0:T(8,128)}, u32[]{:S(2)}) copy-start(s32[8,16]{1,0:T(8,128)} %param.5) | copy-start | bytes 1540
  41.3 1.3 %collective-permute-start.6 = (bf16[256,128]{1,0:T(8,128)(2,1)S(1)}, bf16[256,128]{1,0:T(8,128)(2,1)S(1)}, u32[]{:S(2)}, u32[]{:S(2)}) collective-permute-start(bf16[256,128]{1,0:T(8,128)(2,1)S(1)} %select_bitcast_fusion), channel_id=1, source_target_pairs={{0,1},{1,0},{2,3},{3,2},{4,5},{5,4},{6,7},{7,6},{8,9},{9,8},{10,11... | collective-permute-start | bytes 196616 | tf_op jit(solution)/shard_map/ppermute | solution.py:287
  45.5 14.1 %collective-permute-start.7 = (bf16[256,1024]{1,0:T(8,128)(2,1)S(1)}, bf16[256,1024]{1,0:T(8,128)(2,1)S(1)}, u32[]{:S(2)}, u32[]{:S(2)}) collective-permute-start(bf16[256,1024]{1,0:T(8,128)(2,1)S(1)} %halo_blur.3), channel_id=1, source_target_pairs={{0,2},{2,0},{4,6},{6,4},{8,10},{10,8},{12,14},{14,12},{1,3},{3,1},... | collective-permute-start | bytes 1572872 | tf_op jit(solution)/shard_map/ppermute | solution.py:332
  47.1 16.4 %collective-permute-start.11 = (bf16[256,1024]{1,0:T(8,128)(2,1)S(1)}, bf16[256,1024]{1,0:T(8,128)(2,1)S(1)}, u32[]{:S(2)}, u32[]{:S(2)}) collective-permute-start(bf16[256,1024]{1,0:T(8,128)(2,1)S(1)} %join_score.2), channel_id=1, source_target_pairs={{4,0},{14,2},{8,4},{2,6},{12,8},{6,10},{0,12},{10,14},{5,1},{15,3}... | collective-permute-start | bytes 1572872 | tf_op jit(solution)/shard_map/ppermute | solution.py:334
  49.8 25.4 %collective-permute-start.12 = (bf16[256,1024]{1,0:T(8,128)(2,1)S(1)}, bf16[256,1024]{1,0:T(8,128)(2,1)S(1)}, u32[]{:S(2)}, u32[]{:S(2)}) collective-permute-start(bf16[256,1024]{1,0:T(8,128)(2,1)S(1)} %join_score.2), channel_id=1, source_target_pairs={{0,4},{2,14},{4,8},{6,2},{8,12},{10,6},{12,0},{14,10},{1,5},{3,15}... | collective-permute-start | bytes 1572872 | tf_op jit(solution)/shard_map/ppermute | solution.py:335
  59.6 17.9 %collective-permute-start.10 = (bf16[256,1024]{1,0:T(8,128)(2,1)S(1)}, bf16[256,1024]{1,0:T(8,128)(2,1)S(1)}, u32[]{:S(2)}, u32[]{:S(2)}) collective-permute-start(bf16[256,1024]{1,0:T(8,128)(2,1)S(1)} %join_score.2), channel_id=1, source_target_pairs={{0,2},{2,0},{4,6},{6,4},{8,10},{10,8},{12,14},{14,12},{1,3},{3,1},... | collective-permute-start | bytes 1572872 | tf_op jit(solution)/shard_map/ppermute | solution.py:338
  60.3 25.3 %collective-permute-start.13 = (bf16[256,1024]{1,0:T(8,128)(2,1)S(1)}, bf16[256,1024]{1,0:T(8,128)(2,1)S(1)}, u32[]{:S(2)}, u32[]{:S(2)}) collective-permute-start(bf16[256,1024]{1,0:T(8,128)(2,1)S(1)} %join_score.3), channel_id=1, source_target_pairs={{0,2},{2,0},{4,6},{6,4},{8,10},{10,8},{12,14},{14,12},{1,3},{3,1},... | collective-permute-start | bytes 1572872 | tf_op jit(solution)/shard_map/ppermute | solution.py:339
  62.2 23.9 %collective-permute-start.9 = (bf16[256,1024]{1,0:T(8,128)(2,1)S(1)}, bf16[256,1024]{1,0:T(8,128)(2,1)}, u32[]{:S(2)}, u32[]{:S(2)}) collective-permute-start(bf16[256,1024]{1,0:T(8,128)(2,1)S(1)} %join_score.3), channel_id=1, source_target_pairs={{4,0},{14,2},{8,4},{2,6},{12,8},{6,10},{0,12},{10,14},{5,1},{15,3}... | collective-permute-start | bytes 1572872 | tf_op jit(solution)/shard_map/ppermute | solution.py:340
  63.5 32.8 %collective-permute-start.15 = (bf16[256,1024]{1,0:T(8,128)(2,1)S(1)}, bf16[256,1024]{1,0:T(8,128)(2,1)S(1)}, u32[]{:S(2)}, u32[]{:S(2)}) collective-permute-start(bf16[256,1024]{1,0:T(8,128)(2,1)S(1)} %join_score.3), channel_id=1, source_target_pairs={{0,4},{2,14},{4,8},{6,2},{8,12},{10,6},{12,0},{14,10},{1,5},{3,15}... | collective-permute-start | bytes 1572872 | tf_op jit(solution)/shard_map/ppermute | solution.py:341
  75.3 21.3 %collective-permute-start.20 = (bf16[256,1024]{1,0:T(8,128)(2,1)S(1)}, bf16[256,1024]{1,0:T(8,128)(2,1)S(1)}, u32[]{:S(2)}, u32[]{:S(2)}) collective-permute-start(bf16[256,1024]{1,0:T(8,128)(2,1)S(1)} %collective-permute-done.11), channel_id=1, source_target_pairs={{0,2},{2,0},{4,6},{6,4},{8,10},{10,8},{12,14},{14,12},{1,3},{3,1},... | collective-permute-start | bytes 1572872 | tf_op jit(solution)/shard_map/ppermute | solution.py:343
  77.5 23.9 %collective-permute-start.18 = (bf16[2,256,1024]{2,1,0:T(8,128)(2,1)S(1)}, bf16[2,256,1024]{2,1,0:T(8,128)(2,1)}, u32[]{:S(2)}, u32[]{:S(2)}) collective-permute-start(bf16[2,256,1024]{2,1,0:T(8,128)(2,1)S(1)} %pad_maximum_fusion.2.refs_0_), channel_id=1, source_target_pairs={{0,1},{1,0},{2,3},{3,2},{4,5},{5,4},{6,7},{7,6},{8,9},{9,8},{10,11... | collective-permute-start | bytes 3145736 | tf_op jit(solution)/shard_map/ppermute | solution.py:287
  96.5 4.9 %collective-permute-start.19 = (bf16[2,256,1024]{2,1,0:T(8,128)(2,1)S(1)}, bf16[2,256,1024]{2,1,0:T(8,128)(2,1)}, u32[]{:S(2)}, u32[]{:S(2)}) collective-permute-start(bf16[2,256,1024]{2,1,0:T(8,128)(2,1)S(1)} %pad_maximum_fusion.3.refs_2_), channel_id=1, source_target_pairs={{0,1},{1,0},{2,3},{3,2},{4,5},{5,4},{6,7},{7,6},{8,9},{9,8},{10,11... | collective-permute-start | bytes 3145736 | tf_op jit(solution)/shard_map/ppermute | solution.py:287
  96.6 3.5 %collective-permute-start.21 = (bf16[1,256,1024]{2,1,0:T(8,128)(2,1)S(1)}, bf16[1,256,1024]{2,1,0:T(8,128)(2,1)S(1)}, u32[]{:S(2)}, u32[]{:S(2)}) collective-permute-start(bf16[1,256,1024]{2,1,0:T(8,128)(2,1)S(1)} %bitcast.19), channel_id=1, source_target_pairs={{0,1},{1,0},{2,3},{3,2},{4,5},{5,4},{6,7},{7,6},{8,9},{9,8},{10,11... | collective-permute-start | bytes 1572872 | tf_op jit(solution)/shard_map/ppermute | solution.py:287
  97.0 14.2 %collective-permute-start.17 = (bf16[256,1024]{1,0:T(8,128)(2,1)}, bf16[256,1024]{1,0:T(8,128)(2,1)}, u32[]{:S(2)}, u32[]{:S(2)}) collective-permute-start(bf16[256,1024]{1,0:T(8,128)(2,1)} %collective-permute-done.9), channel_id=1, source_target_pairs={{0,2},{2,0},{4,6},{6,4},{8,10},{10,8},{12,14},{14,12},{1,3},{3,1},... | collective-permute-start | bytes 1572872 | tf_op jit(solution)/shard_map/ppermute | solution.py:347
  98.9 12.4 %collective-permute-start.14 = (bf16[2,256,1024]{2,1,0:T(8,128)(2,1)S(1)}, bf16[2,256,1024]{2,1,0:T(8,128)(2,1)}, u32[]{:S(2)}, u32[]{:S(2)}) collective-permute-start(bf16[2,256,1024]{2,1,0:T(8,128)(2,1)S(1)} %pad_maximum_fusion.refs_0_), channel_id=1, source_target_pairs={{0,1},{1,0},{2,3},{3,2},{4,5},{5,4},{6,7},{7,6},{8,9},{9,8},{10,11... | collective-permute-start | bytes 3145736 | tf_op jit(solution)/shard_map/ppermute | solution.py:287
  100.8 10.4 %collective-permute-start.16 = (bf16[2,256,1024]{2,1,0:T(8,128)(2,1)}, bf16[2,256,1024]{2,1,0:T(8,128)(2,1)}, u32[]{:S(2)}, u32[]{:S(2)}) collective-permute-start(bf16[2,256,1024]{2,1,0:T(8,128)(2,1)} %pad_maximum_fusion.1.refs_2_), channel_id=1, source_target_pairs={{0,1},{1,0},{2,3},{3,2},{4,5},{5,4},{6,7},{7,6},{8,9},{9,8},{10,11... | collective-permute-start | bytes 3145736 | tf_op jit(solution)/shard_map/ppermute | solution.py:287
  111.3 2.1 %collective-permute-start.22 = (bf16[1,256,1024]{2,1,0:T(8,128)(2,1)}, bf16[1,256,1024]{2,1,0:T(8,128)(2,1)S(1)}, u32[]{:S(2)}, u32[]{:S(2)}) collective-permute-start(bf16[1,256,1024]{2,1,0:T(8,128)(2,1)} %bitcast.14.refs_4_), channel_id=1, source_target_pairs={{0,1},{1,0},{2,3},{3,2},{4,5},{5,4},{6,7},{7,6},{8,9},{9,8},{10,11... | collective-permute-start | bytes 1572872 | tf_op jit(solution)/shard_map/ppermute | solution.py:287
  (7 other events, 8.2 us)

commit v11 on v10

--- a/solution.py
+++ b/solution.py
@@ -13,6 +13,34 @@
 CENTRE = 1.0 / (1.0 + 2.0 * math.exp(-0.5))
 SMALL = pl.CostEstimate(flops=1, bytes_accessed=1, transcendentals=0)
 VMEM_BYTES = 20 * 1024 * 1024
+OUTER_VMEM_BYTES = 60 * 1024 * 1024
+
+
+def outer_kernel(place_ref, bold_ref, out_ref, wide):
+    frames, _, slab_y, slab_z = bold_ref.shape[1:]
+    wide[...] = bold_ref[0].reshape(frames * slab_y, slab_z).astype(jnp.float32)
+    for y in range(slab_y):
+        out_ref[y] = wide[pl.ds(y, frames, stride=slab_y), :].astype(jnp.bfloat16)
+
+
+def make_outer(place, bold):
+    _, frames, _, slab_y, slab_z = bold.shape
+    return pl.pallas_call(
+        outer_kernel,
+        grid_spec=pltpu.PrefetchScalarGridSpec(
+            num_scalar_prefetch=1,
+            grid=(1,),
+            in_specs=[
+                pl.BlockSpec((1, frames, 1, slab_y, slab_z), lambda _, at: (0, 0, at[1], 0, 0))
+            ],
+            out_specs=pl.BlockSpec((slab_y, frames, slab_z), lambda _, at: (0, 0, 0)),
+            scratch_shapes=[pltpu.VMEM((frames * slab_y, slab_z), jnp.float32)],
+        ),
+        out_shape=jax.ShapeDtypeStruct((slab_y, frames, slab_z), jnp.bfloat16),
+        compiler_params=pltpu.CompilerParams(vmem_limit_bytes=OUTER_VMEM_BYTES),
+        cost_estimate=SMALL,
+        name="outer_layer",
+    )(place, bold)
 
 
 def faces_kernel(place_ref, bold_ref, *refs):
@@ -304,7 +332,8 @@
     away = (slab % col_total != col).astype(jnp.int32)
     within = ids % blocks
     present = partners >= 0
-    part = jnp.where(kind == 4, 8 + away, kind // 2 * 4 + kind % 2 + 2 * away)
+    order = jnp.where(kind == 3, 2, jnp.where(kind == 2, 6, jnp.where(kind == 4, 8, kind)))
+    part = order + away * jnp.where(order < 3, 3, 1)
     place = jnp.where(present, part * blocks + within, 0).astype(jnp.int32)
     present = present.astype(jnp.int32)
 
@@ -319,8 +348,8 @@
         corner = other_col(jnp.where(col == 0, beyond[-1], beyond[0]))
         return make_halo(here, near, beyond, edge, corner, gm_pair)
 
+    beyond_0 = lax.ppermute(after(make_outer(here, bold), gm_pair), "row", two_on)
     near_0, outer_0, face_0, near_1, outer_1, face_1 = make_faces(after(here, gm_pair), bold)
-    beyond_0 = lax.ppermute(outer_0, "row", two_on)
     edge_0, edge_1 = other_col(face_0), other_col(face_1)
     inner_0 = make_inner(here, near_0, outer_0, edge_0, after(gm, edge_1))
     beyond_0 = after(beyond_0, inner_0)
@@ -328,28 +357,27 @@
     given_0 = give_halo(near_0, beyond_0, edge_0)
     halo_0 = lax.ppermute(given_0, "row", in_pair)
     inner_1 = make_inner(here, near_1, outer_1, edge_1, after(gm, given_0))
-    given_1 = give_halo(near_1, after(beyond_1, inner_1), edge_1)
-    halo_1 = lax.ppermute(given_1, "row", in_pair)
-    own_0 = join(inner_0, after(halo_0, given_1))
+    own_0 = join(inner_0, after(halo_0, inner_1))
     ahead_0 = lax.ppermute(own_0, "row", ahead)
     behind_0 = lax.ppermute(own_0, "row", behind)
-    halo_1 = after(halo_1, own_0)
-    own_1 = join(inner_1, halo_1)
-    pair_0 = lax.ppermute(after(own_0, halo_1), "row", in_pair)
+    pair_0 = lax.ppermute(own_0, "row", in_pair)
+    given_1 = give_halo(near_1, after(beyond_1, own_0), edge_1)
+    halo_1 = lax.ppermute(given_1, "row", in_pair)
+    pair_0 = after(pair_0, given_1)
+    ahead_0, behind_0 = after(ahead_0, pair_0), after(behind_0, pair_0)
+    own_1 = join(inner_1, after(halo_1, ahead_0, behind_0))
     pair_1 = lax.ppermute(own_1, "row", in_pair)
     ahead_1 = lax.ppermute(own_1, "row", ahead)
     behind_1 = lax.ppermute(own_1, "row", behind)
-    ahead_0, behind_0 = after(ahead_0, own_1), after(behind_0, own_1)
-    rest_0 = lax.ppermute(ahead_0, "row", in_pair)
-    pair_0, pair_1 = after(pair_0, ahead_0, behind_0), after(pair_1, ahead_0, behind_0)
-    ahead_1 = after(ahead_1, pair_0, pair_1)
+    rest_0 = lax.ppermute(after(ahead_0, own_1), "row", in_pair)
+    ahead_1 = after(ahead_1, pair_1)
     behind_1 = after(behind_1, ahead_1)
     rest_1 = lax.ppermute(ahead_1, "row", in_pair)
     rest_0 = after(rest_0, ahead_1, behind_1)
-    sources_0 = both(own_0, ahead_0) + both(behind_0, pair_0) + both(rest_0)
+    sources_0 = both(own_0, ahead_0, pair_0) + both(behind_0) + both(rest_0)
     out = make_tiles(0, windows, place, present, sources_0, None)
     rest_1 = after(rest_1, out)
-    sources_1 = both(own_1, ahead_1) + both(behind_1, pair_1) + both(rest_1)
+    sources_1 = both(own_1, ahead_1, pair_1) + both(behind_1) + both(rest_1)
     return make_tiles(1, windows, place, present, sources_1, out)
 
 

time: 120 us -> 124 us (1.033)
  Pallas kernels: 34.7 us -> 37.4 us
  local copies, waits for them, and re-layouts: 5.87 us -> 3.45 us
  starting transfers between devices: 21.3 us -> 23.2 us
    ppermute x1, waiting for transfers between devices: 9.77 us -> 0.01 us  [on_device(): halo_1 = lax.ppermute(given_1, 'row', in_pair)]
    ppermute x1, waiting for transfers between devices: 0.01 us -> 9.28 us  [on_device(): ahead_0 = lax.ppermute(own_0, 'row', ahead)]
    ppermute x1, waiting for transfers between devices: 11.1 us -> 2.1 us  [on_device(): behind_0 = lax.ppermute(own_0, 'row', behind)]
    ppermute x1, waiting for transfers between devices: 1.74 us -> 6.05 us  [on_device(): rest_1 = lax.ppermute(ahead_1, 'row', in_pair)]
    ppermute x1, waiting for transfers between devices: 0.99 us -> 5.06 us  [on_device(): halo_0 = lax.ppermute(given_0, 'row', in_pair)]
    ppermute x1, waiting for transfers between devices: 10.3 us -> 6.63 us  [on_device(): behind_1 = lax.ppermute(own_1, 'row', behind)]
    ppermute x3, waiting for transfers between devices: 5.46 us -> 8.46 us  [the longest x1 7.7 us: on_device(): pair_0 = lax.ppermute(own_0, 'row', in_pair)]
    ppermute x1, waiting for transfers between devices: 0.01 us -> 2.87 us  [on_device(): beyond_1 = lax.ppermute(after(outer_1, beyond_0), 'row', two_on)]
  transfers between devices with their start and end apart: 23 -> 23, of which waited for: 14 -> 13; matrix products, arithmetic and copies ran while one was open for 2% -> 2% of each run, Pallas kernels for 21% -> 22%
where the time goes in v11:
time: 124 us
  waiting for transfers between devices  56.3 us (45%)
  Pallas kernels  37.4 us (30%)
  starting transfers between devices  23.2 us (19%)
  local copies, waits for them, and re-layouts  3.45 us (3%)
  other arithmetic  2.91 us (2%)
    pallas_call x6, Pallas kernels, call_on_rows(): pl.pallas_call(kernel, grid=(1,), in_specs=[pl.BlockSpec(memory_space=plt...  18.6 us
    pallas_call x2, Pallas kernels, make_tiles(): pl.pallas_call(functools.partial(tiles_kernel, sources=count, window=wind...  12.5 us
    ppermute x1, waiting for transfers between devices, on_device(): ahead_0 = lax.ppermute(own_0, 'row', ahead)  9.28 us
    ppermute x1, waiting for transfers between devices, on_device(): pair_1 = lax.ppermute(own_1, 'row', in_pair)  8.4 us
    ppermute x1, waiting for transfers between devices, on_device(): pair_0 = lax.ppermute(own_0, 'row', in_pair)  7.7 us
    ppermute x1, waiting for transfers between devices, on_device(): behind_1 = lax.ppermute(own_1, 'row', behind)  6.63 us
    ppermute x1, waiting for transfers between devices, on_device(): rest_1 = lax.ppermute(ahead_1, 'row', in_pair)  6.05 us
    ppermute x1, waiting for transfers between devices, on_device(): halo_0 = lax.ppermute(given_0, 'row', in_pair)  5.06 us
  transfers between devices with their start and end apart: 23, of which 13 were waited for; matrix products, arithmetic and copies ran while one was open for 2% of the time, Pallas kernels for 22%

profile of v11, /device:TPU:0, one launch (start us, length us, event | category | flops | bytes accessed | tf_op | source)
XLA Modules:
  0.0 123.7 jit_solution(17592310151151478320)
XLA Ops:
  0.0 3.0 %collective-permute-start = (s32[1,1024]{1,0:T(1,128)}, s32[1,1024]{1,0:T(1,128)S(1)}, u32[]{:S(2)}, u32[]{:S(2)}) collective-permute-start(s32[1,1024]{1,0:T(1,128)} %bitcast.21), channel_id=1, source_target_pairs={{0,2},{2,0},{4,6},{6,4},{8,10},{10,8},{12,14},{14,12},{1,3},{3,1},... | collective-permute-start | bytes 12296 | tf_op jit(solution)/shard_map/ppermute | solution.py:345
  3.6 2.9 %outer_layer.1 = bf16[8,256,128]{2,1,0:T(8,128)(2,1)} custom-call(s32[2]{0:T(128)} %pad_add_fusion.place_ref, bf16[2,256,2,8,128]{4,3,2,1,0:T(8,128)(2,1)} %bold_ref.3), custom_call_target="tpu_custom_call" | custom-call | flops 1 | bytes 1 | tf_op jit(solution)/shard_map/outer_layer/pallas_call | solution.py:28
  7.9 3.4 %faces.1 = (bf16[8,256,128]{2,1,0:T(8,128)(2,1)S(1)}, bf16[8,256,128]{2,1,0:T(8,128)(2,1)S(1)}, bf16[2,256,128]{2,1,0:T(8,128)(2,1)S(1)}, bf16[8,256,128]{2,1,0:...) custom-call(s32[2]{0:T(128)S(1)} %copy-done.7, bf16[2,256,2,8,128]{4,3,2,1,0:T(8,128)(2,1)S(1)} %copy-done), custom_call_target="tpu_custom_call" | custom-call | flops 1 | bytes 1 | tf_op jit(solution)/shard_map/faces/pallas_call | solution.py:79
  15.7 5.7 %inner_blur.2.inner_ref = f32[256,1024]{1,0:T(8,128)S(1)} custom-call(s32[2]{0:T(128)S(1)} %copy-done.7, bf16[8,256,128]{2,1,0:T(8,128)(2,1)S(1)} %get-tuple-element.32.near_ref, bf16[8,256,128]{2,1,0:T(8,128)(2,1)S(1)} %copy-done.6, bf16[2,256,128]{2,1,0:T(8,128)(2,1)S(1)} %collective-permute-done.3.edge_ref, s32[1,1024]{1,0:T(1,128)S(1)} %bitcast.22), custom_call_target="tpu_custom_call" | custom-call | flops 1 | bytes 1 | tf_op jit(solution)/shard_map/inner_blur/pallas_call | solution.py:193
  24.3 3.4 %halo_blur.2 = bf16[256,1024]{1,0:T(8,128)(2,1)S(1)} custom-call(s32[2]{0:T(128)S(1)} %copy-done.7, bf16[8,256,128]{2,1,0:T(8,128)(2,1)S(1)} %get-tuple-element.32.near_ref, bf16[8,256,128]{2,1,0:T(8,128)(2,1)} %collective-permute-done.2.beyond_ref, bf16[2,256,128]{2,1,0:T(8,128)(2,1)S(1)} %collective-permute-done.3.edge_ref, ...), custom_call_target="tpu_custom_call" | custom-call | flops 1 | bytes 1 | tf_op jit(solution)/shard_map/halo_blur/pallas_call | solution.py:193
  27.8 2.8 %collective-permute-start.6 = (bf16[256,1024]{1,0:T(8,128)(2,1)S(1)}, bf16[256,1024]{1,0:T(8,128)(2,1)S(1)}, u32[]{:S(2)}, u32[]{:S(2)}) collective-permute-start(bf16[256,1024]{1,0:T(8,128)(2,1)S(1)} %halo_blur.2), channel_id=1, source_target_pairs={{0,2},{2,0},{4,6},{6,4},{8,10},{10,8},{12,14},{14,12},{1,3},{3,1},... | collective-permute-start | bytes 1572872 | tf_op jit(solution)/shard_map/ppermute | solution.py:358
  32.1 5.7 %inner_blur.3.inner_ref = f32[256,1024]{1,0:T(8,128)S(1)} custom-call(s32[2]{0:T(128)S(1)} %copy-done.7, bf16[8,256,128]{2,1,0:T(8,128)(2,1)S(1)} %get-tuple-element.29.near_ref, bf16[8,256,128]{2,1,0:T(8,128)(2,1)S(1)} %copy-done.4, bf16[2,256,128]{2,1,0:T(8,128)(2,1)S(1)} %collective-permute-done.1.edge_ref, s32[1,1024]{1,0:T(1,128)S(1)} %bitcast.23), custom_call_target="tpu_custom_call" | custom-call | flops 1 | bytes 1 | tf_op jit(solution)/shard_map/inner_blur/pallas_call | solution.py:193
  37.8 5.1 %collective-permute-done.6.halo_ref = bf16[256,1024]{1,0:T(8,128)(2,1)S(1)} collective-permute-done((bf16[256,1024]{1,0:T(8,128)(2,1)S(1)}, bf16[256,1024]{1,0:T(8,128)(2,1)S(1)}, u32[]{:S(2)}, u32[]{:S(2)}) %collective-permute-start.6) | collective-permute-done | bytes 524320 | tf_op jit(solution)/shard_map/ppermute | solution.py:358
  43.3 2.9 %collective-permute-done.5.beyond_ref = bf16[8,256,128]{2,1,0:T(8,128)(2,1)S(1)} collective-permute-done((bf16[8,256,128]{2,1,0:T(8,128)(2,1)S(1)}, bf16[8,256,128]{2,1,0:T(8,128)(2,1)S(1)}, u32[]{:S(2)}, u32[]{:S(2)}) %collective-permute-start.5) | collective-permute-done | bytes 524320 | tf_op jit(solution)/shard_map/ppermute | solution.py:356
  47.5 2.8 %collective-permute-start.9 = (bf16[256,1024]{1,0:T(8,128)(2,1)S(1)}, bf16[256,1024]{1,0:T(8,128)(2,1)S(1)}, u32[]{:S(2)}, u32[]{:S(2)}) collective-permute-start(bf16[256,1024]{1,0:T(8,128)(2,1)S(1)} %join_score.2), channel_id=1, source_target_pairs={{4,0},{14,2},{8,4},{2,6},{12,8},{6,10},{0,12},{10,14},{5,1},{15,3}... | collective-permute-start | bytes 1572872 | tf_op jit(solution)/shard_map/ppermute | solution.py:361
  50.3 2.9 %halo_blur.3 = bf16[256,1024]{1,0:T(8,128)(2,1)S(1)} custom-call(s32[2]{0:T(128)S(1)} %copy-done.7, bf16[8,256,128]{2,1,0:T(8,128)(2,1)S(1)} %get-tuple-element.29.near_ref, bf16[8,256,128]{2,1,0:T(8,128)(2,1)S(1)} %collective-permute-done.5.beyond_ref, bf16[2,256,128]{2,1,0:T(8,128)(2,1)S(1)} %collective-permute-done.1.edge_ref, ...), custom_call_target="tpu_custom_call" | custom-call | flops 1 | bytes 1 | tf_op jit(solution)/shard_map/halo_blur/pallas_call | solution.py:193
  53.4 7.7 %collective-permute-done.10 = bf16[256,1024]{1,0:T(8,128)(2,1)S(1)} collective-permute-done((bf16[256,1024]{1,0:T(8,128)(2,1)S(1)}, bf16[256,1024]{1,0:T(8,128)(2,1)S(1)}, u32[]{:S(2)}, u32[]{:S(2)}) %collective-permute-start.10) | collective-permute-done | bytes 524320 | tf_op jit(solution)/shard_map/ppermute | solution.py:363
  61.1 2.1 %collective-permute-done.11 = bf16[256,1024]{1,0:T(8,128)(2,1)} collective-permute-done((bf16[256,1024]{1,0:T(8,128)(2,1)S(1)}, bf16[256,1024]{1,0:T(8,128)(2,1)}, u32[]{:S(2)}, u32[]{:S(2)}) %collective-permute-start.11) | collective-permute-done | bytes 524320 | tf_op jit(solution)/shard_map/ppermute | solution.py:362
  63.2 9.3 %collective-permute-done.9 = bf16[256,1024]{1,0:T(8,128)(2,1)S(1)} collective-permute-done((bf16[256,1024]{1,0:T(8,128)(2,1)S(1)}, bf16[256,1024]{1,0:T(8,128)(2,1)S(1)}, u32[]{:S(2)}, u32[]{:S(2)}) %collective-permute-start.9) | collective-permute-done | bytes 524320 | tf_op jit(solution)/shard_map/ppermute | solution.py:361
  72.9 2.5 %collective-permute-start.13 = (bf16[256,1024]{1,0:T(8,128)(2,1)S(1)}, bf16[256,1024]{1,0:T(8,128)(2,1)S(1)}, u32[]{:S(2)}, u32[]{:S(2)}) collective-permute-start(bf16[256,1024]{1,0:T(8,128)(2,1)S(1)} %join_score.3), channel_id=1, source_target_pairs={{0,2},{2,0},{4,6},{6,4},{8,10},{10,8},{12,14},{14,12},{1,3},{3,1},... | collective-permute-start | bytes 1572872 | tf_op jit(solution)/shard_map/ppermute | solution.py:369
  77.9 1.9 %collective-permute-start.20 = (bf16[256,1024]{1,0:T(8,128)(2,1)S(1)}, bf16[256,1024]{1,0:T(8,128)(2,1)}, u32[]{:S(2)}, u32[]{:S(2)}) collective-permute-start(bf16[256,1024]{1,0:T(8,128)(2,1)S(1)} %collective-permute-done.9), channel_id=1, source_target_pairs={{0,2},{2,0},{4,6},{6,4},{8,10},{10,8},{12,14},{14,12},{1,3},{3,1},... | collective-permute-start | bytes 1572872 | tf_op jit(solution)/shard_map/ppermute | solution.py:372
  79.8 8.4 %collective-permute-done.13 = bf16[256,1024]{1,0:T(8,128)(2,1)S(1)} collective-permute-done((bf16[256,1024]{1,0:T(8,128)(2,1)S(1)}, bf16[256,1024]{1,0:T(8,128)(2,1)S(1)}, u32[]{:S(2)}, u32[]{:S(2)}) %collective-permute-start.13) | collective-permute-done | bytes 524320 | tf_op jit(solution)/shard_map/ppermute | solution.py:369
  88.2 2.9 %collective-permute-done.12 = bf16[256,1024]{1,0:T(8,128)(2,1)} collective-permute-done((bf16[256,1024]{1,0:T(8,128)(2,1)S(1)}, bf16[256,1024]{1,0:T(8,128)(2,1)}, u32[]{:S(2)}, u32[]{:S(2)}) %collective-permute-start.12) | collective-permute-done | bytes 524320 | tf_op jit(solution)/shard_map/ppermute | solution.py:370
  92.9 6.6 %collective-permute-done.15 = bf16[256,1024]{1,0:T(8,128)(2,1)S(1)} collective-permute-done((bf16[256,1024]{1,0:T(8,128)(2,1)S(1)}, bf16[256,1024]{1,0:T(8,128)(2,1)S(1)}, u32[]{:S(2)}, u32[]{:S(2)}) %collective-permute-start.15) | collective-permute-done | bytes 524320 | tf_op jit(solution)/shard_map/ppermute | solution.py:371
  100.3 2.2 %collective-permute-start.17 = (bf16[256,1024]{1,0:T(8,128)(2,1)}, bf16[256,1024]{1,0:T(8,128)(2,1)}, u32[]{:S(2)}, u32[]{:S(2)}) collective-permute-start(bf16[256,1024]{1,0:T(8,128)(2,1)} %collective-permute-done.12), channel_id=1, source_target_pairs={{0,2},{2,0},{4,6},{6,4},{8,10},{10,8},{12,14},{14,12},{1,3},{3,1},... | collective-permute-start | bytes 1572872 | tf_op jit(solution)/shard_map/ppermute | solution.py:375
  102.8 6.5 %tiles.2.refs_6_ = bf16[8,16,2,128,128]{4,3,2,1,0:T(8,128)(2,1)} custom-call(s32[8,16]{1,0:T(8,128)S(1)} %fusion.5.place_ref, s32[8,16]{1,0:T(8,128)S(1)} %fusion.10.present_ref, bf16[3,256,1024]{2,1,0:T(8,128)(2,1)S(1)} %pad_maximum_fusion.1.refs_0_, bf16[3,256,1024]{2,1,0:T(8,128)(2,1)} %collective-permute-done.18.refs_1_, ...), custom_call_target="tpu_custom_call" | custom-call | flops 1 | bytes 1 | tf_op jit(solution)/shard_map/tiles/pallas_call | solution.py:281
  109.3 6.0 %collective-permute-done.17 = bf16[256,1024]{1,0:T(8,128)(2,1)} collective-permute-done((bf16[256,1024]{1,0:T(8,128)(2,1)}, bf16[256,1024]{1,0:T(8,128)(2,1)}, u32[]{:S(2)}, u32[]{:S(2)}) %collective-permute-start.17) | collective-permute-done | bytes 524320 | tf_op jit(solution)/shard_map/ppermute | solution.py:375
  115.3 2.1 %collective-permute-done.22.refs_5_ = bf16[1,256,1024]{2,1,0:T(8,128)(2,1)S(1)} collective-permute-done((bf16[1,256,1024]{2,1,0:T(8,128)(2,1)}, bf16[1,256,1024]{2,1,0:T(8,128)(2,1)S(1)}, u32[]{:S(2)}, u32[]{:S(2)}) %collective-permute-start.22) | collective-permute-done | bytes 524320 | tf_op jit(solution)/shard_map/ppermute | solution.py:315
  117.5 6.0 %tiles.3 = bf16[8,16,2,128,128]{4,3,2,1,0:T(8,128)(2,1)} custom-call(s32[8,16]{1,0:T(8,128)S(1)} %fusion.5.place_ref, s32[8,16]{1,0:T(8,128)S(1)} %fusion.10.present_ref, bf16[3,256,1024]{2,1,0:T(8,128)(2,1)S(1)} %pad_maximum_fusion.refs_0_, bf16[3,256,1024]{2,1,0:T(8,128)(2,1)} %collective-permute-done.14.refs_1_, ...), custom_call_target="tpu_custom_call", output_to_operand_aliasing={{}: (8, {})} | custom-call | flops 1 | bytes 1 | tf_op jit(solution)/shard_map/tiles/pallas_call | solution.py:281
  (59 shorter events, 18.6 us)
Async XLA Ops:
  0.0 6.4 %collective-permute-start = (s32[1,1024]{1,0:T(1,128)}, s32[1,1024]{1,0:T(1,128)S(1)}, u32[]{:S(2)}, u32[]{:S(2)}) collective-permute-start(s32[1,1024]{1,0:T(1,128)} %bitcast.21), channel_id=1, source_target_pairs={{0,2},{2,0},{4,6},{6,4},{8,10},{10,8},{12,14},{14,12},{1,3},{3,1},... | collective-permute-start | bytes 12296 | tf_op jit(solution)/shard_map/ppermute | solution.py:345
  6.4 15.7 %collective-permute-start.2 = (bf16[8,256,128]{2,1,0:T(8,128)(2,1)}, bf16[8,256,128]{2,1,0:T(8,128)(2,1)}, u32[]{:S(2)}, u32[]{:S(2)}) collective-permute-start(bf16[8,256,128]{2,1,0:T(8,128)(2,1)} %outer_layer.1), channel_id=1, source_target_pairs={{2,6},{4,0},{6,10},{8,4},{10,14},{12,8},{3,7},{5,1},{7,11},{9,5},{... | collective-permute-start | bytes 1572872 | tf_op jit(solution)/shard_map/ppermute | solution.py:351
  12.9 1.7 %collective-permute-start.1 = (bf16[2,256,128]{2,1,0:T(8,128)(2,1)}, bf16[2,256,128]{2,1,0:T(8,128)(2,1)S(1)}, u32[]{:S(2)}, u32[]{:S(2)}) collective-permute-start(bf16[2,256,128]{2,1,0:T(8,128)(2,1)} %get-tuple-element.31), channel_id=1, source_target_pairs={{0,1},{1,0},{2,3},{3,2},{4,5},{5,4},{6,7},{7,6},{8,9},{9,8},{10,11... | collective-permute-start | bytes 393224 | tf_op jit(solution)/shard_map/ppermute | solution.py:315
  12.9 1.7 %collective-permute-start.3 = (bf16[2,256,128]{2,1,0:T(8,128)(2,1)S(1)}, bf16[2,256,128]{2,1,0:T(8,128)(2,1)S(1)}, u32[]{:S(2)}, u32[]{:S(2)}) collective-permute-start(bf16[2,256,128]{2,1,0:T(8,128)(2,1)S(1)} %get-tuple-element.35), channel_id=1, source_target_pairs={{0,1},{1,0},{2,3},{3,2},{4,5},{5,4},{6,7},{7,6},{8,9},{9,8},{10,11... | collective-permute-start | bytes 393224 | tf_op jit(solution)/shard_map/ppermute | solution.py:315
  23.0 1.3 %collective-permute-start.4 = (bf16[256,128]{1,0:T(8,128)(2,1)S(1)}, bf16[256,128]{1,0:T(8,128)(2,1)S(1)}, u32[]{:S(2)}, u32[]{:S(2)}) collective-permute-start(bf16[256,128]{1,0:T(8,128)(2,1)S(1)} %select_bitcast_fusion.1), channel_id=1, source_target_pairs={{0,1},{1,0},{2,3},{3,2},{4,5},{5,4},{6,7},{7,6},{8,9},{9,8},{10,11... | collective-permute-start | bytes 196616 | tf_op jit(solution)/shard_map/ppermute | solution.py:315
  27.8 15.1 %collective-permute-start.6 = (bf16[256,1024]{1,0:T(8,128)(2,1)S(1)}, bf16[256,1024]{1,0:T(8,128)(2,1)S(1)}, u32[]{:S(2)}, u32[]{:S(2)}) collective-permute-start(bf16[256,1024]{1,0:T(8,128)(2,1)S(1)} %halo_blur.2), channel_id=1, source_target_pairs={{0,2},{2,0},{4,6},{6,4},{8,10},{10,8},{12,14},{14,12},{1,3},{3,1},... | collective-permute-start | bytes 1572872 | tf_op jit(solution)/shard_map/ppermute | solution.py:358
  30.6 15.6 %collective-permute-start.5 = (bf16[8,256,128]{2,1,0:T(8,128)(2,1)S(1)}, bf16[8,256,128]{2,1,0:T(8,128)(2,1)S(1)}, u32[]{:S(2)}, u32[]{:S(2)}) collective-permute-start(bf16[8,256,128]{2,1,0:T(8,128)(2,1)S(1)} %copy-done.4), channel_id=1, source_target_pairs={{2,6},{4,0},{6,10},{8,4},{10,14},{12,8},{3,7},{5,1},{7,11},{9,5},{... | collective-permute-start | bytes 1572872 | tf_op jit(solution)/shard_map/ppermute | solution.py:356
  46.2 4.1 %collective-permute-start.7 = (bf16[256,128]{1,0:T(8,128)(2,1)S(1)}, bf16[256,128]{1,0:T(8,128)(2,1)S(1)}, u32[]{:S(2)}, u32[]{:S(2)}) collective-permute-start(bf16[256,128]{1,0:T(8,128)(2,1)S(1)} %select_bitcast_fusion), channel_id=1, source_target_pairs={{0,1},{1,0},{2,3},{3,2},{4,5},{5,4},{6,7},{7,6},{8,9},{9,8},{10,11... | collective-permute-start | bytes 196616 | tf_op jit(solution)/shard_map/ppermute | solution.py:315
  46.3 14.8 %collective-permute-start.10 = (bf16[256,1024]{1,0:T(8,128)(2,1)S(1)}, bf16[256,1024]{1,0:T(8,128)(2,1)S(1)}, u32[]{:S(2)}, u32[]{:S(2)}) collective-permute-start(bf16[256,1024]{1,0:T(8,128)(2,1)S(1)} %join_score.2), channel_id=1, source_target_pairs={{0,2},{2,0},{4,6},{6,4},{8,10},{10,8},{12,14},{14,12},{1,3},{3,1},... | collective-permute-start | bytes 1572872 | tf_op jit(solution)/shard_map/ppermute | solution.py:363
  46.3 16.8 %collective-permute-start.11 = (bf16[256,1024]{1,0:T(8,128)(2,1)S(1)}, bf16[256,1024]{1,0:T(8,128)(2,1)}, u32[]{:S(2)}, u32[]{:S(2)}) collective-permute-start(bf16[256,1024]{1,0:T(8,128)(2,1)S(1)} %join_score.2), channel_id=1, source_target_pairs={{0,4},{2,14},{4,8},{6,2},{8,12},{10,6},{12,0},{14,10},{1,5},{3,15}... | collective-permute-start | bytes 1572872 | tf_op jit(solution)/shard_map/ppermute | solution.py:362
  47.5 24.9 %collective-permute-start.9 = (bf16[256,1024]{1,0:T(8,128)(2,1)S(1)}, bf16[256,1024]{1,0:T(8,128)(2,1)S(1)}, u32[]{:S(2)}, u32[]{:S(2)}) collective-permute-start(bf16[256,1024]{1,0:T(8,128)(2,1)S(1)} %join_score.2), channel_id=1, source_target_pairs={{4,0},{14,2},{8,4},{2,6},{12,8},{6,10},{0,12},{10,14},{5,1},{15,3}... | collective-permute-start | bytes 1572872 | tf_op jit(solution)/shard_map/ppermute | solution.py:361
  53.2 19.2 %collective-permute-start.8 = (bf16[256,1024]{1,0:T(8,128)(2,1)S(1)}, bf16[256,1024]{1,0:T(8,128)(2,1)S(1)}, u32[]{:S(2)}, u32[]{:S(2)}) collective-permute-start(bf16[256,1024]{1,0:T(8,128)(2,1)S(1)} %halo_blur.3), channel_id=1, source_target_pairs={{0,2},{2,0},{4,6},{6,4},{8,10},{10,8},{12,14},{14,12},{1,3},{3,1},... | collective-permute-start | bytes 1572872 | tf_op jit(solution)/shard_map/ppermute | solution.py:365
  72.9 15.3 %collective-permute-start.13 = (bf16[256,1024]{1,0:T(8,128)(2,1)S(1)}, bf16[256,1024]{1,0:T(8,128)(2,1)S(1)}, u32[]{:S(2)}, u32[]{:S(2)}) collective-permute-start(bf16[256,1024]{1,0:T(8,128)(2,1)S(1)} %join_score.3), channel_id=1, source_target_pairs={{0,2},{2,0},{4,6},{6,4},{8,10},{10,8},{12,14},{14,12},{1,3},{3,1},... | collective-permute-start | bytes 1572872 | tf_op jit(solution)/shard_map/ppermute | solution.py:369
  75.4 15.7 %collective-permute-start.12 = (bf16[256,1024]{1,0:T(8,128)(2,1)S(1)}, bf16[256,1024]{1,0:T(8,128)(2,1)}, u32[]{:S(2)}, u32[]{:S(2)}) collective-permute-start(bf16[256,1024]{1,0:T(8,128)(2,1)S(1)} %join_score.3), channel_id=1, source_target_pairs={{4,0},{14,2},{8,4},{2,6},{12,8},{6,10},{0,12},{10,14},{5,1},{15,3}... | collective-permute-start | bytes 1572872 | tf_op jit(solution)/shard_map/ppermute | solution.py:370
  77.3 25.5 %collective-permute-start.18 = (bf16[3,256,1024]{2,1,0:T(8,128)(2,1)S(1)}, bf16[3,256,1024]{2,1,0:T(8,128)(2,1)}, u32[]{:S(2)}, u32[]{:S(2)}) collective-permute-start(bf16[3,256,1024]{2,1,0:T(8,128)(2,1)S(1)} %pad_maximum_fusion.1.refs_0_), channel_id=1, source_target_pairs={{0,1},{1,0},{2,3},{3,2},{4,5},{5,4},{6,7},{7,6},{8,9},{9,8},{10,11... | collective-permute-start | bytes 4718600 | tf_op jit(solution)/shard_map/ppermute | solution.py:315
  77.4 22.1 %collective-permute-start.15 = (bf16[256,1024]{1,0:T(8,128)(2,1)S(1)}, bf16[256,1024]{1,0:T(8,128)(2,1)S(1)}, u32[]{:S(2)}, u32[]{:S(2)}) collective-permute-start(bf16[256,1024]{1,0:T(8,128)(2,1)S(1)} %join_score.3), channel_id=1, source_target_pairs={{0,4},{2,14},{4,8},{6,2},{8,12},{10,6},{12,0},{14,10},{1,5},{3,15}... | collective-permute-start | bytes 1572872 | tf_op jit(solution)/shard_map/ppermute | solution.py:371
  77.9 22.4 %collective-permute-start.20 = (bf16[256,1024]{1,0:T(8,128)(2,1)S(1)}, bf16[256,1024]{1,0:T(8,128)(2,1)}, u32[]{:S(2)}, u32[]{:S(2)}) collective-permute-start(bf16[256,1024]{1,0:T(8,128)(2,1)S(1)} %collective-permute-done.9), channel_id=1, source_target_pairs={{0,2},{2,0},{4,6},{6,4},{8,10},{10,8},{12,14},{14,12},{1,3},{3,1},... | collective-permute-start | bytes 1572872 | tf_op jit(solution)/shard_map/ppermute | solution.py:372
  92.3 25.2 %collective-permute-start.14 = (bf16[3,256,1024]{2,1,0:T(8,128)(2,1)S(1)}, bf16[3,256,1024]{2,1,0:T(8,128)(2,1)}, u32[]{:S(2)}, u32[]{:S(2)}) collective-permute-start(bf16[3,256,1024]{2,1,0:T(8,128)(2,1)S(1)} %pad_maximum_fusion.refs_0_), channel_id=1, source_target_pairs={{0,1},{1,0},{2,3},{3,2},{4,5},{5,4},{6,7},{7,6},{8,9},{9,8},{10,11... | collective-permute-start | bytes 4718600 | tf_op jit(solution)/shard_map/ppermute | solution.py:315
  92.4 10.2 %collective-permute-start.19 = (bf16[1,256,1024]{2,1,0:T(8,128)(2,1)}, bf16[1,256,1024]{2,1,0:T(8,128)(2,1)}, u32[]{:S(2)}, u32[]{:S(2)}) collective-permute-start(bf16[1,256,1024]{2,1,0:T(8,128)(2,1)} %bitcast.12.refs_2_), channel_id=1, source_target_pairs={{0,1},{1,0},{2,3},{3,2},{4,5},{5,4},{6,7},{7,6},{8,9},{9,8},{10,11... | collective-permute-start | bytes 1572872 | tf_op jit(solution)/shard_map/ppermute | solution.py:315
  100.3 2.5 %collective-permute-start.21 = (bf16[1,256,1024]{2,1,0:T(8,128)(2,1)}, bf16[1,256,1024]{2,1,0:T(8,128)(2,1)}, u32[]{:S(2)}, u32[]{:S(2)}) collective-permute-start(bf16[1,256,1024]{2,1,0:T(8,128)(2,1)} %bitcast.13.refs_4_), channel_id=1, source_target_pairs={{0,1},{1,0},{2,3},{3,2},{4,5},{5,4},{6,7},{7,6},{8,9},{9,8},{10,11... | collective-permute-start | bytes 1572872 | tf_op jit(solution)/shard_map/ppermute | solution.py:315
  100.3 15.1 %collective-permute-start.17 = (bf16[256,1024]{1,0:T(8,128)(2,1)}, bf16[256,1024]{1,0:T(8,128)(2,1)}, u32[]{:S(2)}, u32[]{:S(2)}) collective-permute-start(bf16[256,1024]{1,0:T(8,128)(2,1)} %collective-permute-done.12), channel_id=1, source_target_pairs={{0,2},{2,0},{4,6},{6,4},{8,10},{10,8},{12,14},{14,12},{1,3},{3,1},... | collective-permute-start | bytes 1572872 | tf_op jit(solution)/shard_map/ppermute | solution.py:375
  102.5 14.9 %copy-start.2 = (bf16[256,1024]{1,0:T(8,128)(2,1)S(1)}, bf16[256,1024]{1,0:T(8,128)(2,1)}, u32[]{:S(2)}) copy-start(bf16[256,1024]{1,0:T(8,128)(2,1)} %copy-done.1) | copy-start | bytes 1572868
  102.5 12.8 %collective-permute-start.16 = (bf16[1,256,1024]{2,1,0:T(8,128)(2,1)}, bf16[1,256,1024]{2,1,0:T(8,128)(2,1)S(1)}, u32[]{:S(2)}, u32[]{:S(2)}) collective-permute-start(bf16[1,256,1024]{2,1,0:T(8,128)(2,1)} %bitcast.19), channel_id=1, source_target_pairs={{0,1},{1,0},{2,3},{3,2},{4,5},{5,4},{6,7},{7,6},{8,9},{9,8},{10,11... | collective-permute-start | bytes 1572872 | tf_op jit(solution)/shard_map/ppermute | solution.py:315
  115.3 2.1 %collective-permute-start.22 = (bf16[1,256,1024]{2,1,0:T(8,128)(2,1)}, bf16[1,256,1024]{2,1,0:T(8,128)(2,1)S(1)}, u32[]{:S(2)}, u32[]{:S(2)}) collective-permute-start(bf16[1,256,1024]{2,1,0:T(8,128)(2,1)} %bitcast.14.refs_4_), channel_id=1, source_target_pairs={{0,1},{1,0},{2,3},{3,2},{4,5},{5,4},{6,7},{7,6},{8,9},{9,8},{10,11... | collective-permute-start | bytes 1572872 | tf_op jit(solution)/shard_map/ppermute | solution.py:315
  (9 other events, 50.1 us)

commit v12 on v11

--- a/solution.py
+++ b/solution.py
@@ -23,7 +23,7 @@
         out_ref[y] = wide[pl.ds(y, frames, stride=slab_y), :].astype(jnp.bfloat16)
 
 
-def make_outer(place, bold):
+def make_outer(window, place, bold):
     _, frames, _, slab_y, slab_z = bold.shape
     return pl.pallas_call(
         outer_kernel,
@@ -31,7 +31,7 @@
             num_scalar_prefetch=1,
             grid=(1,),
             in_specs=[
-                pl.BlockSpec((1, frames, 1, slab_y, slab_z), lambda _, at: (0, 0, at[1], 0, 0))
+                pl.BlockSpec((1, frames, 1, slab_y, slab_z), lambda _, at: (window, 0, at[1], 0, 0))
             ],
             out_specs=pl.BlockSpec((slab_y, frames, slab_z), lambda _, at: (0, 0, 0)),
             scratch_shapes=[pltpu.VMEM((frames * slab_y, slab_z), jnp.float32)],
@@ -125,6 +125,34 @@
         for part in parts[1:]:
             total += jnp.dot(part[...], chosen, preferred_element_type=jnp.float32)
         out_ref[:, start : start + step] = total.astype(out_ref.dtype)
+
+
+def panel_kernel(
+    place_ref, near_ref, outer_ref, facing_ref, across_ref, edge_ref, corner_ref, gm_ref, out_ref,
+    planes, scored,
+):
+    slab_y, frames, slab_z = near_ref.shape
+    even = place_ref[1] == 0
+
+    def along_x(across, outer, near, facing):
+        layers = [part.astype(jnp.float32) for part in (across, outer, near, facing)]
+        outer, near = three_taps(*layers[:3]), three_taps(*layers[1:])
+        return jnp.where(even, outer, near), jnp.where(even, near, outer)
+
+    for y in range(slab_y):
+        planes[0, y + 1], planes[1, y + 1] = along_x(
+            across_ref[y], outer_ref[y], near_ref[y], facing_ref[y]
+        )
+    outer = jnp.where(even, edge_ref[0], edge_ref[1])
+    near = jnp.where(even, edge_ref[1], edge_ref[0])
+    for x, edge in enumerate(along_x(corner_ref[0], outer, near, corner_ref[1])):
+        place_edge(planes, x, edge, place_ref[0])
+    for x in range(2):
+        for y in range(slab_y):
+            part = three_taps(planes[x, y], planes[x, y + 1], planes[x, y + 2])
+            start = (x * slab_y + y) * slab_z
+            scored[:, start : start + slab_z] = standardise(along_z(part))
+    pick([scored], gm_ref, out_ref)
 
 
 def inner_kernel(
@@ -210,6 +238,14 @@
     return [planes] + [pltpu.VMEM((frames, 2 * slab_y * slab_z), jnp.bfloat16)] * terms
 
 
+def make_panel(place, near, outer, facing, across, edge, corner, gm):
+    operands = (near, outer, facing, across, edge, corner, gm)
+    scratch = blur_scratch(near, 1)
+    return call_on_rows(
+        panel_kernel, jnp.bfloat16, near.shape[1], place, operands, scratch, "blur_score_pick"
+    )
+
+
 def make_inner(place, near, outer, edge, gm):
     operands = (near, outer, edge, gm)
     scratch = blur_scratch(near, 3)
@@ -238,11 +274,9 @@
     blocks, slots = out_ref.shape[:2]
 
     loads = []
-    first = 0
     for n, part in enumerate(parts):
-        target = held.at[pl.ds(first, part.shape[0])]
-        first += part.shape[0]
-        loads.append(pltpu.make_async_copy(part, target, sems.at[n]))
+        mine = part.at[window] if len(part.shape) == 3 else part
+        loads.append(pltpu.make_async_copy(mine, held.at[n], sems.at[n]))
         loads[-1].start()
     for load in loads:
         load.wait()
@@ -271,8 +305,7 @@
 
 
 def make_tiles(window, windows, place, present, sources, earlier):
-    frames, rows = sources[0].shape[1:]
-    total = sum(source.shape[0] for source in sources)
+    frames, rows = sources[0].shape[-2:]
     blocks = rows // BLOCK
     slots = place.shape[1]
     count = len(sources)
@@ -286,7 +319,7 @@
             in_specs=[anywhere] * len(operands),
             out_specs=anywhere,
             scratch_shapes=[
-                pltpu.VMEM((total, frames, rows), jnp.bfloat16),
+                pltpu.VMEM((count, frames, rows), jnp.bfloat16),
                 pltpu.VMEM((blocks, slots, BLOCK, BLOCK), jnp.bfloat16),
                 pltpu.SemaphoreType.DMA((count,)),
                 pltpu.SemaphoreType.DMA((blocks,)),
@@ -315,9 +348,11 @@
         return lax.ppermute(value, "col", [(0, 1), (1, 0)])
 
     ahead = [((i + 2 * (-1) ** i) % row_total, i) for i in range(row_total)]
-    behind = [(i, source) for source, i in ahead]
+    behind_pairs = [(i, source) for source, i in ahead]
     two_on = [(i, i + 2 * (-1) ** (i + 1)) for i in range(row_total)]
     two_on = [(i, target) for i, target in two_on if 0 <= target < row_total]
+    across_pairs = [(i, i - (-1) ** i) for i in range(row_total)]
+    across_pairs = [(i, target) for i, target in across_pairs if 0 <= target < row_total]
     in_pair = [(i, i ^ 1) for i in range(row_total)]
 
     gm = gm_index.reshape(1, -1)
@@ -332,53 +367,51 @@
     away = (slab % col_total != col).astype(jnp.int32)
     within = ids % blocks
     present = partners >= 0
-    order = jnp.where(kind == 3, 2, jnp.where(kind == 2, 6, jnp.where(kind == 4, 8, kind)))
-    part = order + away * jnp.where(order < 3, 3, 1)
-    place = jnp.where(present, part * blocks + within, 0).astype(jnp.int32)
+    place = jnp.where(present, (kind + 5 * away) * blocks + within, 0).astype(jnp.int32)
     present = present.astype(jnp.int32)
-
-    def both(*parts):
-        near = jnp.stack(parts, 0)
-        return [near, other_col(near)]
 
     windows = bold.shape[0]
     gm_pair = lax.ppermute(gm, "row", in_pair)
 
-    def give_halo(near, beyond, edge):
-        corner = other_col(jnp.where(col == 0, beyond[-1], beyond[0]))
-        return make_halo(here, near, beyond, edge, corner, gm_pair)
-
-    beyond_0 = lax.ppermute(after(make_outer(here, bold), gm_pair), "row", two_on)
-    near_0, outer_0, face_0, near_1, outer_1, face_1 = make_faces(after(here, gm_pair), bold)
+    def ends(*layers):
+        return other_col(jnp.stack([jnp.where(col == 0, layer[-1], layer[0]) for layer in layers], 0))
+
+    beyond_1 = lax.ppermute(make_outer(1, here, bold), "row", two_on)
+    near_0, outer_0, face_0, near_1, outer_1, face_1 = make_faces(here, bold)
+    facing_0 = lax.ppermute(after(near_0, gm_pair), "row", in_pair)
+    across_0 = lax.ppermute(after(outer_0, gm_pair), "row", across_pairs)
     edge_0, edge_1 = other_col(face_0), other_col(face_1)
-    inner_0 = make_inner(here, near_0, outer_0, edge_0, after(gm, edge_1))
-    beyond_0 = after(beyond_0, inner_0)
-    beyond_1 = lax.ppermute(after(outer_1, beyond_0), "row", two_on)
-    given_0 = give_halo(near_0, beyond_0, edge_0)
-    halo_0 = lax.ppermute(given_0, "row", in_pair)
-    inner_1 = make_inner(here, near_1, outer_1, edge_1, after(gm, given_0))
-    own_0 = join(inner_0, after(halo_0, inner_1))
+    inner_1 = make_inner(here, near_1, outer_1, edge_1, after(gm, edge_0))
+    beyond_1 = after(beyond_1, inner_1)
+    given_1 = make_halo(here, near_1, beyond_1, edge_1, ends(beyond_1)[0], gm_pair)
+    facing_0, across_0 = after(facing_0, given_1), after(across_0, given_1)
+    halo_1 = lax.ppermute(after(given_1, facing_0, across_0), "row", in_pair)
+    corner_0 = ends(across_0, facing_0)
+    own_0 = make_panel(here, near_0, outer_0, facing_0, across_0, edge_0, corner_0, gm)
     ahead_0 = lax.ppermute(own_0, "row", ahead)
-    behind_0 = lax.ppermute(own_0, "row", behind)
-    pair_0 = lax.ppermute(own_0, "row", in_pair)
-    given_1 = give_halo(near_1, after(beyond_1, own_0), edge_1)
-    halo_1 = lax.ppermute(given_1, "row", in_pair)
-    pair_0 = after(pair_0, given_1)
-    ahead_0, behind_0 = after(ahead_0, pair_0), after(behind_0, pair_0)
-    own_1 = join(inner_1, after(halo_1, ahead_0, behind_0))
-    pair_1 = lax.ppermute(own_1, "row", in_pair)
+    halo_1 = after(halo_1, own_0)
+    own_1 = join(inner_1, halo_1)
+    own = jnp.stack([own_0, own_1], 0)
     ahead_1 = lax.ppermute(own_1, "row", ahead)
-    behind_1 = lax.ppermute(own_1, "row", behind)
-    rest_0 = lax.ppermute(after(ahead_0, own_1), "row", in_pair)
-    ahead_1 = after(ahead_1, pair_1)
-    behind_1 = after(behind_1, ahead_1)
+    pair = lax.ppermute(own, "row", in_pair)
+    behind = lax.ppermute(own, "row", behind_pairs)
+    own_far = other_col(own)
+    ahead_0 = after(ahead_0, own)
+    rest_0 = lax.ppermute(ahead_0, "row", in_pair)
+    ahead_1, pair = after(ahead_1, ahead_0), after(pair, ahead_0)
     rest_1 = lax.ppermute(ahead_1, "row", in_pair)
-    rest_0 = after(rest_0, ahead_1, behind_1)
-    sources_0 = both(own_0, ahead_0, pair_0) + both(behind_0) + both(rest_0)
-    out = make_tiles(0, windows, place, present, sources_0, None)
-    rest_1 = after(rest_1, out)
-    sources_1 = both(own_1, ahead_1, pair_1) + both(behind_1) + both(rest_1)
-    return make_tiles(1, windows, place, present, sources_1, out)
+    rest_0 = after(rest_0, ahead_1)
+    behind = after(behind, rest_0, pair)
+    pair_far = other_col(pair)
+    behind_far = [other_col(behind[window]) for window in range(windows)]
+    ahead_far = [other_col(ahead_0), other_col(ahead_1)]
+    rest_far_0 = other_col(rest_0)
+    sources = [own, ahead_0, behind, pair, rest_0]
+    sources += [own_far, ahead_far[0], behind_far[0], pair_far, rest_far_0]
+    out = make_tiles(0, windows, place, present, sources, None)
+    sources = [own, ahead_1, behind, pair, rest_1]
+    sources += [own_far, ahead_far[1], behind_far[1], pair_far, other_col(rest_1)]
+    return make_tiles(1, windows, place, present, sources, out)
 
 
 def solution(mesh):

time: 124 us -> 133 us (1.073)
  local copies, waits for them, and re-layouts: 3.45 us -> 14.4 us
  Pallas kernels: 37.4 us -> 31.4 us
  starting transfers between devices: 23.2 us -> 28.3 us
  other arithmetic: 2.91 us -> 0.79 us
    ppermute x1, waiting for transfers between devices: 2.86 us -> 31 us  [on_device(): ahead_1 = lax.ppermute(own_1, 'row', ahead)]
    ppermute x9 -> x7, waiting for transfers between devices: 33.5 us -> 11.1 us  [the longest x1 6.31 us: on_device(): facing_0 = lax.ppermute(after(near_0, gm_pair), 'row', in_pair)]
    unnamed x20 -> x36, local copies, waits for them, and re-layouts: 3.45 us -> 13.3 us
    ppermute x1, waiting for transfers between devices: 9.28 us -> 2.04 us  [on_device(): ahead_0 = lax.ppermute(own_0, 'row', ahead)]
    pallas_call x6 -> x4, Pallas kernels: 18.6 us -> 12.9 us  [call_on_rows(): pl.pallas_call(kernel, grid=(1,), in_specs=[pl.BlockSpec(memory_space=plt...]
    ppermute x1, waiting for transfers between devices: 6.05 us -> 8.99 us  [on_device(): rest_1 = lax.ppermute(ahead_1, 'row', in_pair)]
    ppermute x1, starting transfers between devices: 2.97 us -> 5.25 us  [on_device(): gm_pair = lax.ppermute(gm, 'row', in_pair)]
    ppermute x9 -> x7, starting transfers between devices: 11.9 us -> 14.2 us  [the longest x1 4.29 us: on_device(): facing_0 = lax.ppermute(after(near_0, gm_pair), 'row', in_pair)]
  transfers between devices with their start and end apart: 23 -> 23, of which waited for: 13 -> 8; matrix products, arithmetic and copies ran while one was open for 2% -> 1% of each run, Pallas kernels for 22% -> 17%
where the time goes in v12:
time: 133 us; the launch traced here: 132 us
  waiting for transfers between devices  56.8 us (43%)
  Pallas kernels  31.4 us (24%)
  starting transfers between devices  28.3 us (21%)
  local copies, waits for them, and re-layouts  14.4 us (11%)
    ppermute x1, waiting for transfers between devices, on_device(): ahead_1 = lax.ppermute(own_1, 'row', ahead)  31 us
    unnamed x36, local copies, waits for them, and re-layouts  13.3 us
    pallas_call x4, Pallas kernels, call_on_rows(): pl.pallas_call(kernel, grid=(1,), in_specs=[pl.BlockSpec(memory_space=plt...  12.9 us
    pallas_call x2, Pallas kernels, make_tiles(): pl.pallas_call(functools.partial(tiles_kernel, sources=count, window=wind...  12.2 us
    ppermute x1, waiting for transfers between devices, on_device(): rest_1 = lax.ppermute(ahead_1, 'row', in_pair)  8.99 us
    ppermute x1, waiting for transfers between devices, on_device(): facing_0 = lax.ppermute(after(near_0, gm_pair), 'row', in_pair)  6.31 us
    ppermute x1, starting transfers between devices, on_device(): gm_pair = lax.ppermute(gm, 'row', in_pair)  5.25 us
    ppermute x1, waiting for transfers between devices, on_device(): halo_1 = lax.ppermute(after(given_1, facing_0, across_0), 'row', in_pair)  4.75 us
  transfers between devices with their start and end apart: 23, of which 8 were waited for; matrix products, arithmetic and copies ran while one was open for 1% of the time, Pallas kernels for 17%

profile of v12, /device:TPU:0, one launch (start us, length us, event | category | flops | bytes accessed | tf_op | source)
XLA Modules:
  0.0 132.0 jit_solution(6140014128827196346)
XLA Ops:
  0.6 2.8 %outer_layer.1 = bf16[8,256,128]{2,1,0:T(8,128)(2,1)} custom-call(s32[2]{0:T(128)} %pad_add_fusion.place_ref, bf16[2,256,2,8,128]{4,3,2,1,0:T(8,128)(2,1)} %bold_ref.3), custom_call_target="tpu_custom_call" | custom-call | flops 1 | bytes 1 | tf_op jit(solution)/shard_map/outer_layer/pallas_call | solution.py:28
  3.5 1.3 collective-permute-start.2
  4.8 5.3 %collective-permute-start = (s32[1,1024]{1,0:T(1,128)}, s32[1,1024]{1,0:T(1,128)S(1)}, u32[]{:S(2)}, u32[]{:S(2)}) collective-permute-start(s32[1,1024]{1,0:T(1,128)} %bitcast.13), channel_id=1, source_target_pairs={{0,2},{2,0},{4,6},{6,4},{8,10},{10,8},{12,14},{14,12},{1,3},{3,1},... | collective-permute-start | bytes 12296 | tf_op jit(solution)/shard_map/ppermute | solution.py:374
  10.0 1.6 %copy-done = bf16[2,256,2,8,128]{4,3,2,1,0:T(8,128)(2,1)S(1)} copy-done((bf16[2,256,2,8,128]{4,3,2,1,0:T(8,128)(2,1)S(1)}, bf16[2,256,2,8,128]{4,3,2,1,0:T(8,128)(2,1)}, u32[]{:S(2)}) %copy-start) | copy-done | bytes 2097176
  12.2 3.4 %faces.1 = (bf16[8,256,128]{2,1,0:T(8,128)(2,1)S(1)}, bf16[8,256,128]{2,1,0:T(8,128)(2,1)S(1)}, bf16[2,256,128]{2,1,0:T(8,128)(2,1)}, bf16[8,256,128]{2,1,0:T(8,...) custom-call(s32[2]{0:T(128)S(1)} %copy-done.15, bf16[2,256,2,8,128]{4,3,2,1,0:T(8,128)(2,1)S(1)} %copy-done), custom_call_target="tpu_custom_call" | custom-call | flops 1 | bytes 1 | tf_op jit(solution)/shard_map/faces/pallas_call | solution.py:79
  17.3 4.3 %collective-permute-start.1 = (bf16[8,256,128]{2,1,0:T(8,128)(2,1)S(1)}, bf16[8,256,128]{2,1,0:T(8,128)(2,1)S(1)}, u32[]{:S(2)}, u32[]{:S(2)}) collective-permute-start(bf16[8,256,128]{2,1,0:T(8,128)(2,1)S(1)} %get-tuple-element.26.near_ref), channel_id=1, source_target_pairs={{0,2},{2,0},{4,6},{6,4},{8,10},{10,8},{12,14},{14,12},{1,3},{3,1},... | collective-permute-start | bytes 1572872 | tf_op jit(solution)/shard_map/ppermute | solution.py:381
  25.7 5.7 %inner_blur.1.inner_ref = f32[256,1024]{1,0:T(8,128)S(1)} custom-call(s32[2]{0:T(128)S(1)} %copy-done.16, bf16[8,256,128]{2,1,0:T(8,128)(2,1)S(1)} %get-tuple-element.27.near_ref, bf16[8,256,128]{2,1,0:T(8,128)(2,1)S(1)} %copy-done.12, bf16[2,256,128]{2,1,0:T(8,128)(2,1)S(1)} %collective-permute-done.3.edge_ref, s32[1,1024]{1,0:T(1,128)S(1)} %bitcast.14), custom_call_target="tpu_custom_call" | custom-call | flops 1 | bytes 1 | tf_op jit(solution)/shard_map/inner_blur/pallas_call | solution.py:221
  32.7 2.9 %halo_blur.1 = bf16[256,1024]{1,0:T(8,128)(2,1)S(1)} custom-call(s32[2]{0:T(128)S(1)} %copy-done.16, bf16[8,256,128]{2,1,0:T(8,128)(2,1)S(1)} %get-tuple-element.27.near_ref, bf16[8,256,128]{2,1,0:T(8,128)(2,1)S(1)} %collective-permute-done.2.beyond_ref, bf16[2,256,128]{2,1,0:T(8,128)(2,1)S(1)} %collective-permute-done.3.edge_ref, ...), custom_call_target="tpu_custom_call" | custom-call | flops 1 | bytes 1 | tf_op jit(solution)/shard_map/halo_blur/pallas_call | solution.py:221
  35.6 6.3 %collective-permute-done.1.facing_ref = bf16[8,256,128]{2,1,0:T(8,128)(2,1)S(1)} collective-permute-done((bf16[8,256,128]{2,1,0:T(8,128)(2,1)S(1)}, bf16[8,256,128]{2,1,0:T(8,128)(2,1)S(1)}, u32[]{:S(2)}, u32[]{:S(2)}) %collective-permute-start.1) | collective-permute-done | bytes 524320 | tf_op jit(solution)/shard_map/ppermute | solution.py:381
  42.0 2.5 %collective-permute-start.8 = (bf16[256,1024]{1,0:T(8,128)(2,1)S(1)}, bf16[256,1024]{1,0:T(8,128)(2,1)S(1)}, u32[]{:S(2)}, u32[]{:S(2)}) collective-permute-start(bf16[256,1024]{1,0:T(8,128)(2,1)S(1)} %halo_blur.1), channel_id=1, source_target_pairs={{0,2},{2,0},{4,6},{6,4},{8,10},{10,8},{12,14},{14,12},{1,3},{3,1},... | collective-permute-start | bytes 1572872 | tf_op jit(solution)/shard_map/ppermute | solution.py:388
  44.6 1.3 %collective-permute-done.7.corner_ref = bf16[2,256,128]{2,1,0:T(8,128)(2,1)S(1)} collective-permute-done((bf16[2,256,128]{2,1,0:T(8,128)(2,1)S(1)}, bf16[2,256,128]{2,1,0:T(8,128)(2,1)S(1)}, u32[]{:S(2)}, u32[]{:S(2)}) %collective-permute-start.7) | collective-permute-done | bytes 131104 | tf_op jit(solution)/shard_map/ppermute | solution.py:348
  45.9 3.8 %blur_score_pick.1 = bf16[256,1024]{1,0:T(8,128)(2,1)S(1)} custom-call(s32[2]{0:T(128)S(1)} %copy-done.16, bf16[8,256,128]{2,1,0:T(8,128)(2,1)S(1)} %get-tuple-element.26.near_ref, bf16[8,256,128]{2,1,0:T(8,128)(2,1)S(1)} %get-tuple-element.34.outer_ref, bf16[8,256,128]{2,1,0:T(8,128)(2,1)S(1)} %collective-permute-done.1.facing_ref, ...), custom_call_target="tpu_custom_call" | custom-call | flops 1 | bytes 1 | tf_op jit(solution)/shard_map/blur_score_pick/pallas_call | solution.py:221
  49.7 2.0 %collective-permute-start.10 = (bf16[256,1024]{1,0:T(8,128)(2,1)S(1)}, bf16[256,1024]{1,0:T(8,128)(2,1)S(1)}, u32[]{:S(2)}, u32[]{:S(2)}) collective-permute-start(bf16[256,1024]{1,0:T(8,128)(2,1)S(1)} %blur_score_pick.1), channel_id=1, source_target_pairs={{4,0},{14,2},{8,4},{2,6},{12,8},{6,10},{0,12},{10,14},{5,1},{15,3}... | collective-permute-start | bytes 1572872 | tf_op jit(solution)/shard_map/ppermute | solution.py:391
  51.8 4.8 %collective-permute-done.8.halo_ref = bf16[256,1024]{1,0:T(8,128)(2,1)S(1)} collective-permute-done((bf16[256,1024]{1,0:T(8,128)(2,1)S(1)}, bf16[256,1024]{1,0:T(8,128)(2,1)S(1)}, u32[]{:S(2)}, u32[]{:S(2)}) %collective-permute-start.8) | collective-permute-done | bytes 524320 | tf_op jit(solution)/shard_map/ppermute | solution.py:388
  57.1 1.8 %collective-permute-start.13 = (bf16[2,256,1024]{2,1,0:T(8,128)(2,1)S(1)}, bf16[2,256,1024]{2,1,0:T(8,128)(2,1)S(1)}, u32[]{:S(2)}, u32[]{:S(2)}) collective-permute-start(bf16[2,256,1024]{2,1,0:T(8,128)(2,1)S(1)} %pad_maximum_fusion.refs_0_), channel_id=1, source_target_pairs={{0,2},{2,0},{4,6},{6,4},{8,10},{10,8},{12,14},{14,12},{1,3},{3,1},... | collective-permute-start | bytes 3145736 | tf_op jit(solution)/shard_map/ppermute | solution.py:396
  59.0 1.7 %collective-permute-start.11 = (bf16[2,256,1024]{2,1,0:T(8,128)(2,1)S(1)}, bf16[2,256,1024]{2,1,0:T(8,128)(2,1)S(1)}, u32[]{:S(2)}, u32[]{:S(2)}) collective-permute-start(bf16[2,256,1024]{2,1,0:T(8,128)(2,1)S(1)} %pad_maximum_fusion.refs_0_), channel_id=1, source_target_pairs={{0,4},{2,14},{4,8},{6,2},{8,12},{10,6},{12,0},{14,10},{1,5},{3,15}... | collective-permute-start | bytes 3145736 | tf_op jit(solution)/shard_map/ppermute | solution.py:397
  60.7 2.1 %collective-permute-start.9 = (bf16[256,1024]{1,0:T(8,128)(2,1)S(1)}, bf16[256,1024]{1,0:T(8,128)(2,1)}, u32[]{:S(2)}, u32[]{:S(2)}) collective-permute-start(bf16[256,1024]{1,0:T(8,128)(2,1)S(1)} %join_score.1), channel_id=1, source_target_pairs={{4,0},{14,2},{8,4},{2,6},{12,8},{6,10},{0,12},{10,14},{5,1},{15,3}... | collective-permute-start | bytes 1572872 | tf_op jit(solution)/shard_map/ppermute | solution.py:395
  62.8 2.0 %collective-permute-done.10.refs_1_ = bf16[256,1024]{1,0:T(8,128)(2,1)S(1)} collective-permute-done((bf16[256,1024]{1,0:T(8,128)(2,1)S(1)}, bf16[256,1024]{1,0:T(8,128)(2,1)S(1)}, u32[]{:S(2)}, u32[]{:S(2)}) %collective-permute-start.10) | collective-permute-done | bytes 524320 | tf_op jit(solution)/shard_map/ppermute | solution.py:391
  64.8 1.8 %collective-permute-start.12 = (bf16[256,1024]{1,0:T(8,128)(2,1)S(1)}, bf16[256,1024]{1,0:T(8,128)(2,1)S(1)}, u32[]{:S(2)}, u32[]{:S(2)}) collective-permute-start(bf16[256,1024]{1,0:T(8,128)(2,1)S(1)} %collective-permute-done.10.refs_1_), channel_id=1, source_target_pairs={{0,2},{2,0},{4,6},{6,4},{8,10},{10,8},{12,14},{14,12},{1,3},{3,1},... | collective-permute-start | bytes 1572872 | tf_op jit(solution)/shard_map/ppermute | solution.py:400
  66.6 31.0 %collective-permute-done.9.refs_1_ = bf16[256,1024]{1,0:T(8,128)(2,1)} collective-permute-done((bf16[256,1024]{1,0:T(8,128)(2,1)S(1)}, bf16[256,1024]{1,0:T(8,128)(2,1)}, u32[]{:S(2)}, u32[]{:S(2)}) %collective-permute-start.9) | collective-permute-done | bytes 524320 | tf_op jit(solution)/shard_map/ppermute | solution.py:395
  97.6 2.4 %collective-permute-start.14 = (bf16[256,1024]{1,0:T(8,128)(2,1)}, bf16[256,1024]{1,0:T(8,128)(2,1)}, u32[]{:S(2)}, u32[]{:S(2)}) collective-permute-start(bf16[256,1024]{1,0:T(8,128)(2,1)} %collective-permute-done.9.refs_1_), channel_id=1, source_target_pairs={{0,2},{2,0},{4,6},{6,4},{8,10},{10,8},{12,14},{14,12},{1,3},{3,1},... | collective-permute-start | bytes 1572872 | tf_op jit(solution)/shard_map/ppermute | solution.py:402
  103.8 9.0 %collective-permute-done.14.refs_4_ = bf16[256,1024]{1,0:T(8,128)(2,1)} collective-permute-done((bf16[256,1024]{1,0:T(8,128)(2,1)}, bf16[256,1024]{1,0:T(8,128)(2,1)}, u32[]{:S(2)}, u32[]{:S(2)}) %collective-permute-start.14) | collective-permute-done | bytes 524320 | tf_op jit(solution)/shard_map/ppermute | solution.py:402
  119.6 5.9 %tiles.2.refs_10_ = bf16[8,16,2,128,128]{4,3,2,1,0:T(8,128)(2,1)} custom-call(s32[8,16]{1,0:T(8,128)S(1)} %fusion.5.place_ref, s32[8,16]{1,0:T(8,128)S(1)} %fusion.8.present_ref, bf16[2,256,1024]{2,1,0:T(8,128)(2,1)S(1)} %pad_maximum_fusion.refs_0_, bf16[256,1024]{1,0:T(8,128)(2,1)S(1)} %copy-done.4, ...), custom_call_target="tpu_custom_call" | custom-call | flops 1 | bytes 1 | tf_op jit(solution)/shard_map/tiles/pallas_call | solution.py:314
  125.5 6.3 %tiles.3 = bf16[8,16,2,128,128]{4,3,2,1,0:T(8,128)(2,1)} custom-call(s32[8,16]{1,0:T(8,128)S(1)} %fusion.5.place_ref, s32[8,16]{1,0:T(8,128)S(1)} %fusion.8.present_ref, bf16[2,256,1024]{2,1,0:T(8,128)(2,1)S(1)} %pad_maximum_fusion.refs_0_, bf16[256,1024]{1,0:T(8,128)(2,1)} %collective-permute-done.9.refs_1_, ...), custom_call_target="tpu_custom_call", output_to_operand_aliasing={{}: (12, {})} | custom-call | flops 1 | bytes 1 | tf_op jit(solution)/shard_map/tiles/pallas_call | solution.py:314
  (74 shorter events, 19.6 us)
Async XLA Ops:
  0.6 113.5 %copy-start.17 = (s32[8,16]{1,0:T(8,128)S(1)}, s32[8,16]{1,0:T(8,128)}, u32[]{:S(2)}) copy-start(s32[8,16]{1,0:T(8,128)} %param.5) | copy-start | bytes 1540
  3.5 27.9 %collective-permute-start.2 = (bf16[8,256,128]{2,1,0:T(8,128)(2,1)}, bf16[8,256,128]{2,1,0:T(8,128)(2,1)S(1)}, u32[]{:S(2)}, u32[]{:S(2)}) collective-permute-start(bf16[8,256,128]{2,1,0:T(8,128)(2,1)} %outer_layer.1), channel_id=1, source_target_pairs={{2,6},{4,0},{6,10},{8,4},{10,14},{12,8},{3,7},{5,1},{7,11},{9,5},{... | collective-permute-start | bytes 1572872 | tf_op jit(solution)/shard_map/ppermute | solution.py:379
  4.8 11.7 %collective-permute-start = (s32[1,1024]{1,0:T(1,128)}, s32[1,1024]{1,0:T(1,128)S(1)}, u32[]{:S(2)}, u32[]{:S(2)}) collective-permute-start(s32[1,1024]{1,0:T(1,128)} %bitcast.13), channel_id=1, source_target_pairs={{0,2},{2,0},{4,6},{6,4},{8,10},{10,8},{12,14},{14,12},{1,3},{3,1},... | collective-permute-start | bytes 12296 | tf_op jit(solution)/shard_map/ppermute | solution.py:374
  16.4 19.2 %collective-permute-start.6 = (bf16[8,256,128]{2,1,0:T(8,128)(2,1)S(1)}, bf16[8,256,128]{2,1,0:T(8,128)(2,1)S(1)}, u32[]{:S(2)}, u32[]{:S(2)}) collective-permute-start(bf16[8,256,128]{2,1,0:T(8,128)(2,1)S(1)} %get-tuple-element.34.outer_ref), channel_id=1, source_target_pairs={{2,4},{4,2},{6,8},{8,6},{10,12},{12,10},{3,5},{5,3},{7,9},{9,7},{1... | collective-permute-start | bytes 1572872 | tf_op jit(solution)/shard_map/ppermute | solution.py:382
  17.3 24.7 %collective-permute-start.1 = (bf16[8,256,128]{2,1,0:T(8,128)(2,1)S(1)}, bf16[8,256,128]{2,1,0:T(8,128)(2,1)S(1)}, u32[]{:S(2)}, u32[]{:S(2)}) collective-permute-start(bf16[8,256,128]{2,1,0:T(8,128)(2,1)S(1)} %get-tuple-element.26.near_ref), channel_id=1, source_target_pairs={{0,2},{2,0},{4,6},{6,4},{8,10},{10,8},{12,14},{14,12},{1,3},{3,1},... | collective-permute-start | bytes 1572872 | tf_op jit(solution)/shard_map/ppermute | solution.py:381
  21.6 1.7 %collective-permute-start.4 = (bf16[2,256,128]{2,1,0:T(8,128)(2,1)}, bf16[2,256,128]{2,1,0:T(8,128)(2,1)S(1)}, u32[]{:S(2)}, u32[]{:S(2)}) collective-permute-start(bf16[2,256,128]{2,1,0:T(8,128)(2,1)} %get-tuple-element.30), channel_id=1, source_target_pairs={{0,1},{1,0},{2,3},{3,2},{4,5},{5,4},{6,7},{7,6},{8,9},{9,8},{10,11... | collective-permute-start | bytes 393224 | tf_op jit(solution)/shard_map/ppermute | solution.py:348
  21.6 1.7 %collective-permute-start.3 = (bf16[2,256,128]{2,1,0:T(8,128)(2,1)S(1)}, bf16[2,256,128]{2,1,0:T(8,128)(2,1)S(1)}, u32[]{:S(2)}, u32[]{:S(2)}) collective-permute-start(bf16[2,256,128]{2,1,0:T(8,128)(2,1)S(1)} %get-tuple-element.29), channel_id=1, source_target_pairs={{0,1},{1,0},{2,3},{3,2},{4,5},{5,4},{6,7},{7,6},{8,9},{9,8},{10,11... | collective-permute-start | bytes 393224 | tf_op jit(solution)/shard_map/ppermute | solution.py:348
  31.4 1.3 collective-permute-start.5
  42.0 14.6 %collective-permute-start.8 = (bf16[256,1024]{1,0:T(8,128)(2,1)S(1)}, bf16[256,1024]{1,0:T(8,128)(2,1)S(1)}, u32[]{:S(2)}, u32[]{:S(2)}) collective-permute-start(bf16[256,1024]{1,0:T(8,128)(2,1)S(1)} %halo_blur.1), channel_id=1, source_target_pairs={{0,2},{2,0},{4,6},{6,4},{8,10},{10,8},{12,14},{14,12},{1,3},{3,1},... | collective-permute-start | bytes 1572872 | tf_op jit(solution)/shard_map/ppermute | solution.py:388
  44.5 1.4 %collective-permute-start.7 = (bf16[2,256,128]{2,1,0:T(8,128)(2,1)S(1)}, bf16[2,256,128]{2,1,0:T(8,128)(2,1)S(1)}, u32[]{:S(2)}, u32[]{:S(2)}) collective-permute-start(bf16[2,256,128]{2,1,0:T(8,128)(2,1)S(1)} %pad_maximum_fusion.1), channel_id=1, source_target_pairs={{0,1},{1,0},{2,3},{3,2},{4,5},{5,4},{6,7},{7,6},{8,9},{9,8},{10,11... | collective-permute-start | bytes 393224 | tf_op jit(solution)/shard_map/ppermute | solution.py:348
  49.7 15.1 %collective-permute-start.10 = (bf16[256,1024]{1,0:T(8,128)(2,1)S(1)}, bf16[256,1024]{1,0:T(8,128)(2,1)S(1)}, u32[]{:S(2)}, u32[]{:S(2)}) collective-permute-start(bf16[256,1024]{1,0:T(8,128)(2,1)S(1)} %blur_score_pick.1), channel_id=1, source_target_pairs={{4,0},{14,2},{8,4},{2,6},{12,8},{6,10},{0,12},{10,14},{5,1},{15,3}... | collective-permute-start | bytes 1572872 | tf_op jit(solution)/shard_map/ppermute | solution.py:391
  57.1 42.8 %collective-permute-start.13 = (bf16[2,256,1024]{2,1,0:T(8,128)(2,1)S(1)}, bf16[2,256,1024]{2,1,0:T(8,128)(2,1)S(1)}, u32[]{:S(2)}, u32[]{:S(2)}) collective-permute-start(bf16[2,256,1024]{2,1,0:T(8,128)(2,1)S(1)} %pad_maximum_fusion.refs_0_), channel_id=1, source_target_pairs={{0,2},{2,0},{4,6},{6,4},{8,10},{10,8},{12,14},{14,12},{1,3},{3,1},... | collective-permute-start | bytes 3145736 | tf_op jit(solution)/shard_map/ppermute | solution.py:396
  59.0 41.2 %collective-permute-start.11 = (bf16[2,256,1024]{2,1,0:T(8,128)(2,1)S(1)}, bf16[2,256,1024]{2,1,0:T(8,128)(2,1)S(1)}, u32[]{:S(2)}, u32[]{:S(2)}) collective-permute-start(bf16[2,256,1024]{2,1,0:T(8,128)(2,1)S(1)} %pad_maximum_fusion.refs_0_), channel_id=1, source_target_pairs={{0,4},{2,14},{4,8},{6,2},{8,12},{10,6},{12,0},{14,10},{1,5},{3,15}... | collective-permute-start | bytes 3145736 | tf_op jit(solution)/shard_map/ppermute | solution.py:397
  60.7 36.9 %collective-permute-start.9 = (bf16[256,1024]{1,0:T(8,128)(2,1)S(1)}, bf16[256,1024]{1,0:T(8,128)(2,1)}, u32[]{:S(2)}, u32[]{:S(2)}) collective-permute-start(bf16[256,1024]{1,0:T(8,128)(2,1)S(1)} %join_score.1), channel_id=1, source_target_pairs={{4,0},{14,2},{8,4},{2,6},{12,8},{6,10},{0,12},{10,14},{5,1},{15,3}... | collective-permute-start | bytes 1572872 | tf_op jit(solution)/shard_map/ppermute | solution.py:395
  64.8 32.8 %collective-permute-start.12 = (bf16[256,1024]{1,0:T(8,128)(2,1)S(1)}, bf16[256,1024]{1,0:T(8,128)(2,1)S(1)}, u32[]{:S(2)}, u32[]{:S(2)}) collective-permute-start(bf16[256,1024]{1,0:T(8,128)(2,1)S(1)} %collective-permute-done.10.refs_1_), channel_id=1, source_target_pairs={{0,2},{2,0},{4,6},{6,4},{8,10},{10,8},{12,14},{14,12},{1,3},{3,1},... | collective-permute-start | bytes 1572872 | tf_op jit(solution)/shard_map/ppermute | solution.py:400
  66.6 35.9 %collective-permute-start.15 = (bf16[2,256,1024]{2,1,0:T(8,128)(2,1)S(1)}, bf16[2,256,1024]{2,1,0:T(8,128)(2,1)S(1)}, u32[]{:S(2)}, u32[]{:S(2)}) collective-permute-start(bf16[2,256,1024]{2,1,0:T(8,128)(2,1)S(1)} %pad_maximum_fusion.refs_0_), channel_id=1, source_target_pairs={{0,1},{1,0},{2,3},{3,2},{4,5},{5,4},{6,7},{7,6},{8,9},{9,8},{10,11... | collective-permute-start | bytes 3145736 | tf_op jit(solution)/shard_map/ppermute | solution.py:348
  97.6 4.0 %collective-permute-start.20 = (bf16[256,1024]{1,0:T(8,128)(2,1)S(1)}, bf16[256,1024]{1,0:T(8,128)(2,1)S(1)}, u32[]{:S(2)}, u32[]{:S(2)}) collective-permute-start(bf16[256,1024]{1,0:T(8,128)(2,1)S(1)} %collective-permute-done.10.refs_1_), channel_id=1, source_target_pairs={{0,1},{1,0},{2,3},{3,2},{4,5},{5,4},{6,7},{7,6},{8,9},{9,8},{10,11... | collective-permute-start | bytes 1572872 | tf_op jit(solution)/shard_map/ppermute | solution.py:348
  97.6 15.2 %collective-permute-start.14 = (bf16[256,1024]{1,0:T(8,128)(2,1)}, bf16[256,1024]{1,0:T(8,128)(2,1)}, u32[]{:S(2)}, u32[]{:S(2)}) collective-permute-start(bf16[256,1024]{1,0:T(8,128)(2,1)} %collective-permute-done.9.refs_1_), channel_id=1, source_target_pairs={{0,2},{2,0},{4,6},{6,4},{8,10},{10,8},{12,14},{14,12},{1,3},{3,1},... | collective-permute-start | bytes 1572872 | tf_op jit(solution)/shard_map/ppermute | solution.py:402
  100.0 14.2 %collective-permute-start.18 = (bf16[2,256,1024]{2,1,0:T(8,128)(2,1)S(1)}, bf16[2,256,1024]{2,1,0:T(8,128)(2,1)}, u32[]{:S(2)}, u32[]{:S(2)}) collective-permute-start(bf16[2,256,1024]{2,1,0:T(8,128)(2,1)S(1)} %collective-permute-done.13.refs_3_), channel_id=1, source_target_pairs={{0,1},{1,0},{2,3},{3,2},{4,5},{5,4},{6,7},{7,6},{8,9},{9,8},{10,11... | collective-permute-start | bytes 3145736 | tf_op jit(solution)/shard_map/ppermute | solution.py:348
  100.1 12.7 %collective-permute-start.22 = (bf16[256,1024]{1,0:T(8,128)(2,1)S(1)}, bf16[256,1024]{1,0:T(8,128)(2,1)S(1)}, u32[]{:S(2)}, u32[]{:S(2)}) collective-permute-start(bf16[256,1024]{1,0:T(8,128)(2,1)S(1)} %collective-permute-done.12.refs_4_), channel_id=1, source_target_pairs={{0,1},{1,0},{2,3},{3,2},{4,5},{5,4},{6,7},{7,6},{8,9},{9,8},{10,11... | collective-permute-start | bytes 1572872 | tf_op jit(solution)/shard_map/ppermute | solution.py:348
  102.3 23.2 %collective-permute-start.16 = (bf16[256,1024]{1,0:T(8,128)(2,1)}, bf16[256,1024]{1,0:T(8,128)(2,1)}, u32[]{:S(2)}, u32[]{:S(2)}) collective-permute-start(bf16[256,1024]{1,0:T(8,128)(2,1)} %collective-permute-done.9.refs_1_), channel_id=1, source_target_pairs={{0,1},{1,0},{2,3},{3,2},{4,5},{5,4},{6,7},{7,6},{8,9},{9,8},{10,11... | collective-permute-start | bytes 1572872 | tf_op jit(solution)/shard_map/ppermute | solution.py:348
  103.5 10.7 %collective-permute-start.21 = (bf16[256,1024]{1,0:T(8,128)(2,1)}, bf16[256,1024]{1,0:T(8,128)(2,1)}, u32[]{:S(2)}, u32[]{:S(2)}) collective-permute-start(bf16[256,1024]{1,0:T(8,128)(2,1)} %get-tuple-element.43), channel_id=1, source_target_pairs={{0,1},{1,0},{2,3},{3,2},{4,5},{5,4},{6,7},{7,6},{8,9},{9,8},{10,11... | collective-permute-start | bytes 1572872 | tf_op jit(solution)/shard_map/ppermute | solution.py:348
  112.8 12.7 %collective-permute-start.17 = (bf16[256,1024]{1,0:T(8,128)(2,1)}, bf16[256,1024]{1,0:T(8,128)(2,1)}, u32[]{:S(2)}, u32[]{:S(2)}) collective-permute-start(bf16[256,1024]{1,0:T(8,128)(2,1)} %get-tuple-element.44), channel_id=1, source_target_pairs={{0,1},{1,0},{2,3},{3,2},{4,5},{5,4},{6,7},{7,6},{8,9},{9,8},{10,11... | collective-permute-start | bytes 1572872 | tf_op jit(solution)/shard_map/ppermute | solution.py:348
  113.6 11.9 %collective-permute-start.19 = (bf16[256,1024]{1,0:T(8,128)(2,1)}, bf16[256,1024]{1,0:T(8,128)(2,1)}, u32[]{:S(2)}, u32[]{:S(2)}) collective-permute-start(bf16[256,1024]{1,0:T(8,128)(2,1)} %collective-permute-done.14.refs_4_), channel_id=1, source_target_pairs={{0,1},{1,0},{2,3},{3,2},{4,5},{5,4},{6,7},{7,6},{8,9},{9,8},{10,11... | collective-permute-start | bytes 1572872 | tf_op jit(solution)/shard_map/ppermute | solution.py:348
  (17 other events, 102.8 us)

commit v13 on v10

--- a/solution.py
+++ b/solution.py
@@ -15,7 +15,15 @@
 VMEM_BYTES = 20 * 1024 * 1024
 
 
-def faces_kernel(place_ref, bold_ref, *refs):
+def is_even():
+    return lax.axis_index("row") % 2 == 0
+
+
+def is_first():
+    return lax.axis_index("col") == 0
+
+
+def faces_kernel(bold_ref, *refs):
     windows, frames, slab_x, slab_y, slab_z = bold_ref.shape
     per_frame = slab_x * slab_y
     wide = refs[-1]
@@ -32,18 +40,18 @@
                 first_ref[y] = plane(0, y)
                 last_ref[y] = plane(1, y)
 
-        pl.when(place_ref[1] == 0)(functools.partial(layers, outer_ref, near_ref))
-        pl.when(place_ref[1] != 0)(functools.partial(layers, near_ref, outer_ref))
+        pl.when(is_even())(functools.partial(layers, outer_ref, near_ref))
+        pl.when(~is_even())(functools.partial(layers, near_ref, outer_ref))
 
         def edges(y):
             for x in range(slab_x):
                 edge_ref[x] = plane(x, y)
 
-        pl.when(place_ref[0] == 0)(functools.partial(edges, slab_y - 1))
-        pl.when(place_ref[0] != 0)(functools.partial(edges, 0))
-
-
-def make_faces(place, bold):
+        pl.when(is_first())(functools.partial(edges, slab_y - 1))
+        pl.when(~is_first())(functools.partial(edges, 0))
+
+
+def make_faces(bold):
     windows, frames, slab_x, slab_y, slab_z = bold.shape
     layer = jax.ShapeDtypeStruct((slab_y, frames, slab_z), jnp.bfloat16)
     edge = jax.ShapeDtypeStruct((slab_x, frames, slab_z), jnp.bfloat16)
@@ -51,14 +59,14 @@
     return pl.pallas_call(
         faces_kernel,
         grid=(1,),
-        in_specs=[pl.BlockSpec(memory_space=pltpu.SMEM), whole(bold)],
+        in_specs=[whole(bold)],
         out_specs=[whole(layer), whole(layer), whole(edge)] * windows,
         out_shape=[layer, layer, edge] * windows,
         scratch_shapes=[pltpu.VMEM((frames * slab_x * slab_y, slab_z), jnp.float32)],
         compiler_params=pltpu.CompilerParams(vmem_limit_bytes=VMEM_BYTES),
         cost_estimate=SMALL,
         name="faces",
-    )(place, bold)
+    )(bold)
 
 
 def three_taps(before, here, after):
@@ -73,9 +81,9 @@
     return three_taps(before, part, after)
 
 
-def place_edge(planes, x, edge, col):
-    planes[x, 0] = jnp.where(col == 0, 0.0, edge)
-    planes[x, planes.shape[1] - 1] = jnp.where(col == 0, edge, 0.0)
+def place_edge(planes, x, edge):
+    planes[x, 0] = jnp.where(is_first(), 0.0, edge)
+    planes[x, planes.shape[1] - 1] = jnp.where(is_first(), edge, 0.0)
 
 
 def standardise(smooth):
@@ -99,12 +107,40 @@
         out_ref[:, start : start + step] = total.astype(out_ref.dtype)
 
 
+def panel_kernel(
+    near_ref, outer_ref, facing_ref, across_ref, edge_ref, corner_ref, gm_ref, out_ref,
+    planes, scored,
+):
+    slab_y, frames, slab_z = near_ref.shape
+    even = is_even()
+
+    def along_x(across, outer, near, facing):
+        layers = [part.astype(jnp.float32) for part in (across, outer, near, facing)]
+        outer, near = three_taps(*layers[:3]), three_taps(*layers[1:])
+        return jnp.where(even, outer, near), jnp.where(even, near, outer)
+
+    for y in range(slab_y):
+        planes[0, y + 1], planes[1, y + 1] = along_x(
+            across_ref[y], outer_ref[y], near_ref[y], facing_ref[y]
+        )
+    outer = jnp.where(even, edge_ref[0], edge_ref[1])
+    near = jnp.where(even, edge_ref[1], edge_ref[0])
+    for x, edge in enumerate(along_x(corner_ref[0], outer, near, corner_ref[1])):
+        place_edge(planes, x, edge)
+    for x in range(2):
+        for y in range(slab_y):
+            part = three_taps(planes[x, y], planes[x, y + 1], planes[x, y + 2])
+            start = (x * slab_y + y) * slab_z
+            scored[:, start : start + slab_z] = standardise(along_z(part))
+    pick([scored], gm_ref, out_ref)
+
+
 def inner_kernel(
-    place_ref, near_ref, outer_ref, edge_ref, gm_ref, out_ref, planes, high, middle, low
+    near_ref, outer_ref, edge_ref, gm_ref, out_ref, planes, high, middle, low
 ):
     slab_y, frames, slab_z = near_ref.shape
     slab_x = edge_ref.shape[0]
-    even = place_ref[1] == 0
+    even = is_even()
 
     def two_taps(here, other):
         return CENTRE * here + SIDE * other
@@ -116,7 +152,7 @@
         planes[1, y + 1] = two_taps(last, first)
     edges = [edge_ref[x].astype(jnp.float32) for x in range(slab_x)]
     for x in range(slab_x):
-        place_edge(planes, x, two_taps(edges[x], edges[1 - x]), place_ref[0])
+        place_edge(planes, x, two_taps(edges[x], edges[1 - x]))
     for x in range(slab_x):
         for y in range(slab_y):
             part = along_z(three_taps(planes[x, y], planes[x, y + 1], planes[x, y + 2]))
@@ -129,10 +165,10 @@
 
 
 def halo_kernel(
-    place_ref, near_ref, beyond_ref, edge_ref, corner_ref, gm_ref, out_ref, planes, scored
+    near_ref, beyond_ref, edge_ref, corner_ref, gm_ref, out_ref, planes, scored
 ):
     slab_y, frames, slab_z = near_ref.shape
-    even = place_ref[1] == 0
+    even = is_even()
 
     def sides(own, beyond):
         own, beyond = own.astype(jnp.float32), beyond.astype(jnp.float32)
@@ -142,7 +178,7 @@
         planes[0, y + 1], planes[1, y + 1] = sides(near_ref[y], beyond_ref[y])
     own = jnp.where(even, edge_ref[1], edge_ref[0])
     for x, edge in enumerate(sides(own, corner_ref[...])):
-        place_edge(planes, x, edge, place_ref[0])
+        place_edge(planes, x, edge)
     for x in range(2):
         for y in range(slab_y):
             part = three_taps(planes[x, y], planes[x, y + 1], planes[x, y + 2])
@@ -158,22 +194,20 @@
         out_ref[:, span] = standardise(smooth)
 
 
-def call_on_rows(kernel, dtype, frames, place, operands, scratch, name):
+def call_on_rows(kernel, dtype, frames, operands, scratch, name):
     rows = operands[-1].shape[1]
     whole = lambda array: pl.BlockSpec(array.shape, lambda _: (0,) * array.ndim)
-    scalars = [] if place is None else [place]
     return pl.pallas_call(
         kernel,
         grid=(1,),
-        in_specs=[pl.BlockSpec(memory_space=pltpu.SMEM)] * len(scalars)
-        + [whole(value) for value in operands],
+        in_specs=[whole(value) for value in operands],
         out_specs=pl.BlockSpec((frames, rows), lambda _: (0, 0)),
         out_shape=jax.ShapeDtypeStruct((frames, rows), dtype),
         scratch_shapes=scratch,
         compiler_params=pltpu.CompilerParams(vmem_limit_bytes=VMEM_BYTES),
         cost_estimate=SMALL,
         name=name,
-    )(*scalars, *operands)
+    )(*operands)
 
 
 def blur_scratch(first, terms):
@@ -182,25 +216,33 @@
     return [planes] + [pltpu.VMEM((frames, 2 * slab_y * slab_z), jnp.bfloat16)] * terms
 
 
-def make_inner(place, near, outer, edge, gm):
+def make_panel(near, outer, facing, across, edge, corner, gm):
+    operands = (near, outer, facing, across, edge, corner, gm)
+    scratch = blur_scratch(near, 1)
+    return call_on_rows(
+        panel_kernel, jnp.bfloat16, near.shape[1], operands, scratch, "blur_score_pick"
+    )
+
+
+def make_inner(near, outer, edge, gm):
     operands = (near, outer, edge, gm)
     scratch = blur_scratch(near, 3)
     return call_on_rows(
-        inner_kernel, jnp.float32, near.shape[1], place, operands, scratch, "inner_blur"
-    )
-
-
-def make_halo(place, near, beyond, edge, corner, gm):
+        inner_kernel, jnp.float32, near.shape[1], operands, scratch, "inner_blur"
+    )
+
+
+def make_halo(near, beyond, edge, corner, gm):
     operands = (near, beyond, edge, corner, gm)
     scratch = blur_scratch(near, 1)
     return call_on_rows(
-        halo_kernel, jnp.bfloat16, near.shape[1], place, operands, scratch, "halo_blur"
+        halo_kernel, jnp.bfloat16, near.shape[1], operands, scratch, "halo_blur"
     )
 
 
 def join(inner, halo):
     return call_on_rows(
-        join_kernel, jnp.bfloat16, inner.shape[0], None, (inner, halo), [], "join_score"
+        join_kernel, jnp.bfloat16, inner.shape[0], (inner, halo), [], "join_score"
     )
 
 
@@ -290,11 +332,11 @@
     behind = [(i, source) for source, i in ahead]
     two_on = [(i, i + 2 * (-1) ** (i + 1)) for i in range(row_total)]
     two_on = [(i, target) for i, target in two_on if 0 <= target < row_total]
+    across_pairs = [(i, i - (-1) ** i) for i in range(row_total)]
+    across_pairs = [(i, target) for i, target in across_pairs if 0 <= target < row_total]
     in_pair = [(i, i ^ 1) for i in range(row_total)]
 
     gm = gm_index.reshape(1, -1)
-    here = jnp.stack([col, row % 2]).astype(jnp.int32)
-
     blocks, slots = partners.shape
     ids = jnp.maximum(partners, 0)
     slab = ids // blocks
@@ -304,8 +346,12 @@
     away = (slab % col_total != col).astype(jnp.int32)
     within = ids % blocks
     present = partners >= 0
-    part = jnp.where(kind == 4, 8 + away, kind // 2 * 4 + kind % 2 + 2 * away)
-    place = jnp.where(present, part * blocks + within, 0).astype(jnp.int32)
+    parts_0 = jnp.where(kind == 4, 8 + away, kind // 2 * 4 + kind % 2 + 2 * away)
+    parts_1 = jnp.where(kind == 3, 4 + away, jnp.where(kind < 2, kind, kind // 2 + 5) + 2 * away)
+    place_0, place_1 = (
+        jnp.where(present, part * blocks + within, 0).astype(jnp.int32)
+        for part in (parts_0, parts_1)
+    )
     present = present.astype(jnp.int32)
 
     def both(*parts):
@@ -315,42 +361,40 @@
     windows = bold.shape[0]
     gm_pair = lax.ppermute(gm, "row", in_pair)
 
-    def give_halo(near, beyond, edge):
-        corner = other_col(jnp.where(col == 0, beyond[-1], beyond[0]))
-        return make_halo(here, near, beyond, edge, corner, gm_pair)
-
-    near_0, outer_0, face_0, near_1, outer_1, face_1 = make_faces(after(here, gm_pair), bold)
-    beyond_0 = lax.ppermute(outer_0, "row", two_on)
+    def ends(*layers):
+        return other_col(jnp.stack([jnp.where(col == 0, layer[-1], layer[0]) for layer in layers], 0))
+
+    near_0, outer_0, face_0, near_1, outer_1, face_1 = make_faces(bold)
+    beyond_1 = lax.ppermute(outer_1, "row", two_on)
+    facing_0 = lax.ppermute(after(near_0, gm_pair), "row", in_pair)
+    across_0 = lax.ppermute(after(outer_0, gm_pair), "row", across_pairs)
     edge_0, edge_1 = other_col(face_0), other_col(face_1)
-    inner_0 = make_inner(here, near_0, outer_0, edge_0, after(gm, edge_1))
-    beyond_0 = after(beyond_0, inner_0)
-    beyond_1 = lax.ppermute(after(outer_1, beyond_0), "row", two_on)
-    given_0 = give_halo(near_0, beyond_0, edge_0)
-    halo_0 = lax.ppermute(given_0, "row", in_pair)
-    inner_1 = make_inner(here, near_1, outer_1, edge_1, after(gm, given_0))
-    given_1 = give_halo(near_1, after(beyond_1, inner_1), edge_1)
-    halo_1 = lax.ppermute(given_1, "row", in_pair)
-    own_0 = join(inner_0, after(halo_0, given_1))
+    inner_1 = make_inner(near_1, outer_1, edge_1, after(gm, edge_0))
+    beyond_1 = after(beyond_1, inner_1)
+    given_1 = make_halo(near_1, beyond_1, edge_1, ends(beyond_1)[0], gm_pair)
+    facing_0, across_0 = after(facing_0, given_1), after(across_0, given_1)
+    halo_1 = lax.ppermute(after(given_1, facing_0, across_0), "row", in_pair)
+    corner_0 = ends(across_0, facing_0)
+    own_0 = make_panel(near_0, outer_0, facing_0, across_0, edge_0, corner_0, gm)
     ahead_0 = lax.ppermute(own_0, "row", ahead)
-    behind_0 = lax.ppermute(own_0, "row", behind)
     halo_1 = after(halo_1, own_0)
     own_1 = join(inner_1, halo_1)
     pair_0 = lax.ppermute(after(own_0, halo_1), "row", in_pair)
     pair_1 = lax.ppermute(own_1, "row", in_pair)
     ahead_1 = lax.ppermute(own_1, "row", ahead)
-    behind_1 = lax.ppermute(own_1, "row", behind)
-    ahead_0, behind_0 = after(ahead_0, own_1), after(behind_0, own_1)
+    ahead_0 = after(ahead_0, own_1)
+    behind_0 = lax.ppermute(after(own_0, ahead_0), "row", behind)
     rest_0 = lax.ppermute(ahead_0, "row", in_pair)
-    pair_0, pair_1 = after(pair_0, ahead_0, behind_0), after(pair_1, ahead_0, behind_0)
-    ahead_1 = after(ahead_1, pair_0, pair_1)
-    behind_1 = after(behind_1, ahead_1)
+    pair_0 = after(pair_0, ahead_0)
+    pair_1 = after(pair_1, pair_0)
+    ahead_1 = after(ahead_1, pair_1)
+    behind_1 = lax.ppermute(after(own_1, ahead_1), "row", behind)
     rest_1 = lax.ppermute(ahead_1, "row", in_pair)
-    rest_0 = after(rest_0, ahead_1, behind_1)
+    behind_0, rest_0 = after(behind_0, ahead_1), after(rest_0, ahead_1)
     sources_0 = both(own_0, ahead_0) + both(behind_0, pair_0) + both(rest_0)
-    out = make_tiles(0, windows, place, present, sources_0, None)
-    rest_1 = after(rest_1, out)
-    sources_1 = both(own_1, ahead_1) + both(behind_1, pair_1) + both(rest_1)
-    return make_tiles(1, windows, place, present, sources_1, out)
+    sources_1 = both(own_1, ahead_1) + both(pair_1) + both(behind_1, rest_1)
+    out = make_tiles(0, windows, place_0, present, sources_0, None)
+    return make_tiles(1, windows, place_1, present, sources_1, out)
 
 
 def solution(mesh):

time: 120 us -> 126 us (1.050); the launches traced: 120 us -> 124 us
  starting transfers between devices: 21.3 us -> 45.8 us
  waiting for transfers between devices: 55.1 us -> 43.1 us
  Pallas kernels: 34.7 us -> 28.2 us
    ppermute x6, waiting for transfers between devices: 37.6 us -> 16.5 us  [the longest x1 9.94 us: on_device(): facing_0 = lax.ppermute(after(near_0, gm_pair), 'row', in_pair)]
    ppermute x6, starting transfers between devices: 7.46 us -> 25.6 us  [the longest x1 15.1 us: on_device(): behind_1 = lax.ppermute(after(own_1, ahead_1), 'row', behind)]
    pallas_call x7 -> x5, Pallas kernels: 22.2 us -> 15.4 us  [the longest x4 12.4 us: call_on_rows(): pl.pallas_call(kernel, grid=(1,), in_specs=[whole(value) for value in ope...]
    ppermute x1, waiting for transfers between devices: 0.01 us -> 5.03 us  [on_device(): rest_0 = lax.ppermute(ahead_0, 'row', in_pair)]
    ppermute x1, waiting for transfers between devices: 0.01 us -> 4.46 us  [on_device(): ahead_0 = lax.ppermute(own_0, 'row', ahead)]
    ppermute x1, starting transfers between devices: 1.38 us -> 4.41 us  [on_device(): ahead_1 = lax.ppermute(own_1, 'row', ahead)]
    ppermute x1, starting transfers between devices: 2.97 us -> 5.28 us  [on_device(): gm_pair = lax.ppermute(gm, 'row', in_pair)]
    ppermute x1, waiting for transfers between devices: 0.01 us -> 1.82 us  [on_device(): pair_0 = lax.ppermute(after(own_0, halo_1), 'row', in_pair)]
  transfers between devices with their start and end apart: 23 -> 23, of which waited for: 14 -> 12; matrix products, arithmetic and copies ran while one was open for 2% -> 1% of each run, Pallas kernels for 21% -> 15%
where the time goes in v13:
time: 126 us; the launch traced here: 124 us
  starting transfers between devices  45.8 us (36%)
  waiting for transfers between devices  43.1 us (34%)
  Pallas kernels  28.2 us (22%)
  local copies, waits for them, and re-layouts  5.17 us (4%)
  other arithmetic  1.47 us (1%)
    ppermute x1, starting transfers between devices, on_device(): behind_1 = lax.ppermute(after(own_1, ahead_1), 'row', behind)  15.1 us
    pallas_call x2, Pallas kernels, make_tiles(): pl.pallas_call(functools.partial(tiles_kernel, sources=count, window=wind...  12.8 us
    pallas_call x4, Pallas kernels, call_on_rows(): pl.pallas_call(kernel, grid=(1,), in_specs=[whole(value) for value in ope...  12.4 us
    ppermute x1, waiting for transfers between devices, on_device(): facing_0 = lax.ppermute(after(near_0, gm_pair), 'row', in_pair)  9.94 us
    ppermute x1, waiting for transfers between devices, on_device(): pair_1 = lax.ppermute(own_1, 'row', in_pair)  9.06 us
    ppermute x1, waiting for transfers between devices, on_device(): behind_1 = lax.ppermute(after(own_1, ahead_1), 'row', behind)  5.48 us
    ppermute x1, starting transfers between devices, on_device(): gm_pair = lax.ppermute(gm, 'row', in_pair)  5.28 us
    unnamed x12, local copies, waits for them, and re-layouts  5.17 us
  transfers between devices with their start and end apart: 23, of which 12 were waited for; matrix products, arithmetic and copies ran while one was open for 1% of the time, Pallas kernels for 15%

profile of v13, /device:TPU:0, one launch (start us, length us, event | category | flops | bytes accessed | tf_op | source)
XLA Modules:
  0.0 124.1 jit_solution(9537050216180898090)
XLA Ops:
  0.0 1.6 %copy-done = bf16[2,256,2,8,128]{4,3,2,1,0:T(8,128)(2,1)S(1)} copy-done((bf16[2,256,2,8,128]{4,3,2,1,0:T(8,128)(2,1)S(1)}, bf16[2,256,2,8,128]{4,3,2,1,0:T(8,128)(2,1)}, u32[]{:S(2)}) %copy-start) | copy-done | bytes 2097176
  1.6 3.0 %faces.1 = (bf16[8,256,128]{2,1,0:T(8,128)(2,1)S(1)}, bf16[8,256,128]{2,1,0:T(8,128)(2,1)}, bf16[2,256,128]{2,1,0:T(8,128)(2,1)}, bf16[8,256,128]{2,1,0:T(8,128)...) custom-call(bf16[2,256,2,8,128]{4,3,2,1,0:T(8,128)(2,1)S(1)} %copy-done), custom_call_target="tpu_custom_call" | custom-call | flops 1 | bytes 1 | tf_op jit(solution)/shard_map/faces/pallas_call | solution.py:59
  5.9 5.3 %collective-permute-start.4 = (s32[1,1024]{1,0:T(1,128)}, s32[1,1024]{1,0:T(1,128)S(1)}, u32[]{:S(2)}, u32[]{:S(2)}) collective-permute-start(s32[1,1024]{1,0:T(1,128)} %bitcast.15), channel_id=1, source_target_pairs={{0,2},{2,0},{4,6},{6,4},{8,10},{10,8},{12,14},{14,12},{1,3},{3,1},... | collective-permute-start | bytes 12296 | tf_op jit(solution)/shard_map/ppermute | solution.py:362
  11.2 1.8 %collective-permute-done.4.gm_ref = s32[1,1024]{1,0:T(1,128)S(1)} collective-permute-done((s32[1,1024]{1,0:T(1,128)}, s32[1,1024]{1,0:T(1,128)S(1)}, u32[]{:S(2)}, u32[]{:S(2)}) %collective-permute-start.4) | collective-permute-done | bytes 4128 | tf_op jit(solution)/shard_map/ppermute | solution.py:362
  13.9 4.3 %collective-permute-start.5 = (bf16[8,256,128]{2,1,0:T(8,128)(2,1)S(1)}, bf16[8,256,128]{2,1,0:T(8,128)(2,1)S(1)}, u32[]{:S(2)}, u32[]{:S(2)}) collective-permute-start(bf16[8,256,128]{2,1,0:T(8,128)(2,1)S(1)} %get-tuple-element.35.near_ref), channel_id=1, source_target_pairs={{0,2},{2,0},{4,6},{6,4},{8,10},{10,8},{12,14},{14,12},{1,3},{3,1},... | collective-permute-start | bytes 1572872 | tf_op jit(solution)/shard_map/ppermute | solution.py:369
  20.6 5.2 %inner_blur.1.inner_ref = f32[256,1024]{1,0:T(8,128)S(1)} custom-call(bf16[8,256,128]{2,1,0:T(8,128)(2,1)S(1)} %get-tuple-element.28.near_ref, bf16[8,256,128]{2,1,0:T(8,128)(2,1)S(1)} %get-tuple-element.29.outer_ref, bf16[2,256,128]{2,1,0:T(8,128)(2,1)S(1)} %collective-permute-done.edge_ref, s32[1,1024]{1,0:T(1,128)S(1)} %bitcast.16), custom_call_target="tpu_custom_call" | custom-call | flops 1 | bytes 1 | tf_op jit(solution)/shard_map/inner_blur/pallas_call | solution.py:200
  27.1 2.4 %halo_blur.1 = bf16[256,1024]{1,0:T(8,128)(2,1)S(1)} custom-call(bf16[8,256,128]{2,1,0:T(8,128)(2,1)S(1)} %get-tuple-element.28.near_ref, bf16[8,256,128]{2,1,0:T(8,128)(2,1)S(1)} %collective-permute-done.2.beyond_ref, bf16[2,256,128]{2,1,0:T(8,128)(2,1)S(1)} %collective-permute-done.edge_ref, bf16[256,128]{1,0:T(8,128)(2,1)S(1)} %bitcast.14, ...), custom_call_target="tpu_custom_call" | custom-call | flops 1 | bytes 1 | tf_op jit(solution)/shard_map/halo_blur/pallas_call | solution.py:200
  29.5 9.9 %collective-permute-done.5.facing_ref = bf16[8,256,128]{2,1,0:T(8,128)(2,1)S(1)} collective-permute-done((bf16[8,256,128]{2,1,0:T(8,128)(2,1)S(1)}, bf16[8,256,128]{2,1,0:T(8,128)(2,1)S(1)}, u32[]{:S(2)}, u32[]{:S(2)}) %collective-permute-start.5) | collective-permute-done | bytes 524320 | tf_op jit(solution)/shard_map/ppermute | solution.py:369
  39.4 2.5 %collective-permute-start.7 = (bf16[256,1024]{1,0:T(8,128)(2,1)S(1)}, bf16[256,1024]{1,0:T(8,128)(2,1)S(1)}, u32[]{:S(2)}, u32[]{:S(2)}) collective-permute-start(bf16[256,1024]{1,0:T(8,128)(2,1)S(1)} %halo_blur.1), channel_id=1, source_target_pairs={{0,2},{2,0},{4,6},{6,4},{8,10},{10,8},{12,14},{14,12},{1,3},{3,1},... | collective-permute-start | bytes 1572872 | tf_op jit(solution)/shard_map/ppermute | solution.py:376
  42.0 1.3 %collective-permute-done.8.corner_ref = bf16[2,256,128]{2,1,0:T(8,128)(2,1)S(1)} collective-permute-done((bf16[2,256,128]{2,1,0:T(8,128)(2,1)S(1)}, bf16[2,256,128]{2,1,0:T(8,128)(2,1)S(1)}, u32[]{:S(2)}, u32[]{:S(2)}) %collective-permute-start.8) | collective-permute-done | bytes 131104 | tf_op jit(solution)/shard_map/ppermute | solution.py:329
  44.1 4.4 %blur_score_pick.1 = bf16[256,1024]{1,0:T(8,128)(2,1)S(1)} custom-call(bf16[8,256,128]{2,1,0:T(8,128)(2,1)S(1)} %get-tuple-element.35.near_ref, bf16[8,256,128]{2,1,0:T(8,128)(2,1)} %get-tuple-element.38.outer_ref, bf16[8,256,128]{2,1,0:T(8,128)(2,1)S(1)} %collective-permute-done.5.facing_ref, bf16[8,256,128]{2,1,0:T(8,128)(2,1)S(1)} %collective-permute-done.6.across_ref, ...), custom_call_target="tpu_custom_call" | custom-call | flops 1 | bytes 1 | tf_op jit(solution)/shard_map/blur_score_pick/pallas_call | solution.py:200
  48.4 2.2 %collective-permute-start.12 = (bf16[256,1024]{1,0:T(8,128)(2,1)S(1)}, bf16[256,1024]{1,0:T(8,128)(2,1)S(1)}, u32[]{:S(2)}, u32[]{:S(2)}) collective-permute-start(bf16[256,1024]{1,0:T(8,128)(2,1)S(1)} %blur_score_pick.1), channel_id=1, source_target_pairs={{4,0},{14,2},{8,4},{2,6},{12,8},{6,10},{0,12},{10,14},{5,1},{15,3}... | collective-permute-start | bytes 1572872 | tf_op jit(solution)/shard_map/ppermute | solution.py:379
  51.8 1.8 %collective-permute-start.11 = (bf16[256,1024]{1,0:T(8,128)(2,1)S(1)}, bf16[256,1024]{1,0:T(8,128)(2,1)S(1)}, u32[]{:S(2)}, u32[]{:S(2)}) collective-permute-start(bf16[256,1024]{1,0:T(8,128)(2,1)S(1)} %blur_score_pick.1), channel_id=1, source_target_pairs={{0,2},{2,0},{4,6},{6,4},{8,10},{10,8},{12,14},{14,12},{1,3},{3,1},... | collective-permute-start | bytes 1572872 | tf_op jit(solution)/shard_map/ppermute | solution.py:382
  54.4 4.4 %collective-permute-start.9 = (bf16[256,1024]{1,0:T(8,128)(2,1)S(1)}, bf16[256,1024]{1,0:T(8,128)(2,1)S(1)}, u32[]{:S(2)}, u32[]{:S(2)}) collective-permute-start(bf16[256,1024]{1,0:T(8,128)(2,1)S(1)} %join_score.1), channel_id=1, source_target_pairs={{4,0},{14,2},{8,4},{2,6},{12,8},{6,10},{0,12},{10,14},{5,1},{15,3}... | collective-permute-start | bytes 1572872 | tf_op jit(solution)/shard_map/ppermute | solution.py:384
  58.8 4.5 %collective-permute-done.12 = bf16[256,1024]{1,0:T(8,128)(2,1)S(1)} collective-permute-done((bf16[256,1024]{1,0:T(8,128)(2,1)S(1)}, bf16[256,1024]{1,0:T(8,128)(2,1)S(1)}, u32[]{:S(2)}, u32[]{:S(2)}) %collective-permute-start.12) | collective-permute-done | bytes 524320 | tf_op jit(solution)/shard_map/ppermute | solution.py:379
  63.3 1.6 %collective-permute-start.19 = (bf16[256,1024]{1,0:T(8,128)(2,1)S(1)}, bf16[256,1024]{1,0:T(8,128)(2,1)S(1)}, u32[]{:S(2)}, u32[]{:S(2)}) collective-permute-start(bf16[256,1024]{1,0:T(8,128)(2,1)S(1)} %blur_score_pick.1), channel_id=1, source_target_pairs={{0,4},{2,14},{4,8},{6,2},{8,12},{10,6},{12,0},{14,10},{1,5},{3,15}... | collective-permute-start | bytes 1572872 | tf_op jit(solution)/shard_map/ppermute | solution.py:386
  64.8 1.8 %collective-permute-done.11 = bf16[256,1024]{1,0:T(8,128)(2,1)S(1)} collective-permute-done((bf16[256,1024]{1,0:T(8,128)(2,1)S(1)}, bf16[256,1024]{1,0:T(8,128)(2,1)S(1)}, u32[]{:S(2)}, u32[]{:S(2)}) %collective-permute-start.11) | collective-permute-done | bytes 524320 | tf_op jit(solution)/shard_map/ppermute | solution.py:382
  66.7 9.1 %collective-permute-done.10 = bf16[256,1024]{1,0:T(8,128)(2,1)} collective-permute-done((bf16[256,1024]{1,0:T(8,128)(2,1)S(1)}, bf16[256,1024]{1,0:T(8,128)(2,1)}, u32[]{:S(2)}, u32[]{:S(2)}) %collective-permute-start.10) | collective-permute-done | bytes 524320 | tf_op jit(solution)/shard_map/ppermute | solution.py:383
  76.7 15.1 %collective-permute-start.15 = (bf16[256,1024]{1,0:T(8,128)(2,1)S(1)}, bf16[256,1024]{1,0:T(8,128)(2,1)S(1)}, u32[]{:S(2)}, u32[]{:S(2)}) collective-permute-start(bf16[256,1024]{1,0:T(8,128)(2,1)S(1)} %join_score.1), channel_id=1, source_target_pairs={{0,4},{2,14},{4,8},{6,2},{8,12},{10,6},{12,0},{14,10},{1,5},{3,15}... | collective-permute-start | bytes 1572872 | tf_op jit(solution)/shard_map/ppermute | solution.py:391
  92.0 3.0 %collective-permute-start.21 = (bf16[256,1024]{1,0:T(8,128)(2,1)S(1)}, bf16[256,1024]{1,0:T(8,128)(2,1)}, u32[]{:S(2)}, u32[]{:S(2)}) collective-permute-start(bf16[256,1024]{1,0:T(8,128)(2,1)S(1)} %collective-permute-done.12), channel_id=1, source_target_pairs={{0,2},{2,0},{4,6},{6,4},{8,10},{10,8},{12,14},{14,12},{1,3},{3,1},... | collective-permute-start | bytes 1572872 | tf_op jit(solution)/shard_map/ppermute | solution.py:387
  96.4 5.5 %collective-permute-done.15 = bf16[256,1024]{1,0:T(8,128)(2,1)S(1)} collective-permute-done((bf16[256,1024]{1,0:T(8,128)(2,1)S(1)}, bf16[256,1024]{1,0:T(8,128)(2,1)S(1)}, u32[]{:S(2)}, u32[]{:S(2)}) %collective-permute-start.15) | collective-permute-done | bytes 524320 | tf_op jit(solution)/shard_map/ppermute | solution.py:391
  102.6 5.0 %collective-permute-done.21 = bf16[256,1024]{1,0:T(8,128)(2,1)} collective-permute-done((bf16[256,1024]{1,0:T(8,128)(2,1)S(1)}, bf16[256,1024]{1,0:T(8,128)(2,1)}, u32[]{:S(2)}, u32[]{:S(2)}) %collective-permute-start.21) | collective-permute-done | bytes 524320 | tf_op jit(solution)/shard_map/ppermute | solution.py:387
  111.1 6.4 %tiles.2.refs_6_ = bf16[8,16,2,128,128]{4,3,2,1,0:T(8,128)(2,1)} custom-call(s32[8,16]{1,0:T(8,128)S(1)} %get-tuple-element.51.place_ref, s32[8,16]{1,0:T(8,128)S(1)} %fusion.18.present_ref, bf16[2,256,1024]{2,1,0:T(8,128)(2,1)S(1)} %pad_maximum_fusion.2.refs_0_, bf16[2,256,1024]{2,1,0:T(8,128)(2,1)S(1)} %copy-done.2, ...), custom_call_target="tpu_custom_call" | custom-call | flops 1 | bytes 1 | tf_op jit(solution)/shard_map/tiles/pallas_call | solution.py:295
  117.5 6.4 %tiles.3 = bf16[8,16,2,128,128]{4,3,2,1,0:T(8,128)(2,1)} custom-call(s32[8,16]{1,0:T(8,128)S(1)} %get-tuple-element.52.place_ref, s32[8,16]{1,0:T(8,128)S(1)} %fusion.18.present_ref, bf16[2,256,1024]{2,1,0:T(8,128)(2,1)S(1)} %pad_maximum_fusion.refs_0_, bf16[2,256,1024]{2,1,0:T(8,128)(2,1)} %collective-permute-done.13.refs_1_, ...), custom_call_target="tpu_custom_call", output_to_operand_aliasing={{}: (8, {})} | custom-call | flops 1 | bytes 1 | tf_op jit(solution)/shard_map/tiles/pallas_call | solution.py:295
  (50 shorter events, 15.3 us)
Async XLA Ops:
  4.6 21.1 %collective-permute-start.2 = (bf16[8,256,128]{2,1,0:T(8,128)(2,1)S(1)}, bf16[8,256,128]{2,1,0:T(8,128)(2,1)S(1)}, u32[]{:S(2)}, u32[]{:S(2)}) collective-permute-start(bf16[8,256,128]{2,1,0:T(8,128)(2,1)S(1)} %get-tuple-element.29.outer_ref), channel_id=1, source_target_pairs={{2,6},{4,0},{6,10},{8,4},{10,14},{12,8},{3,7},{5,1},{7,11},{9,5},{... | collective-permute-start | bytes 1572872 | tf_op jit(solution)/shard_map/ppermute | solution.py:368
  5.9 7.1 %collective-permute-start.4 = (s32[1,1024]{1,0:T(1,128)}, s32[1,1024]{1,0:T(1,128)S(1)}, u32[]{:S(2)}, u32[]{:S(2)}) collective-permute-start(s32[1,1024]{1,0:T(1,128)} %bitcast.15), channel_id=1, source_target_pairs={{0,2},{2,0},{4,6},{6,4},{8,10},{10,8},{12,14},{14,12},{1,3},{3,1},... | collective-permute-start | bytes 12296 | tf_op jit(solution)/shard_map/ppermute | solution.py:362
  13.0 16.5 %collective-permute-start.6 = (bf16[8,256,128]{2,1,0:T(8,128)(2,1)}, bf16[8,256,128]{2,1,0:T(8,128)(2,1)S(1)}, u32[]{:S(2)}, u32[]{:S(2)}) collective-permute-start(bf16[8,256,128]{2,1,0:T(8,128)(2,1)} %get-tuple-element.38.outer_ref), channel_id=1, source_target_pairs={{2,4},{4,2},{6,8},{8,6},{10,12},{12,10},{3,5},{5,3},{7,9},{9,7},{1... | collective-permute-start | bytes 1572872 | tf_op jit(solution)/shard_map/ppermute | solution.py:370
  13.9 25.6 %collective-permute-start.5 = (bf16[8,256,128]{2,1,0:T(8,128)(2,1)S(1)}, bf16[8,256,128]{2,1,0:T(8,128)(2,1)S(1)}, u32[]{:S(2)}, u32[]{:S(2)}) collective-permute-start(bf16[8,256,128]{2,1,0:T(8,128)(2,1)S(1)} %get-tuple-element.35.near_ref), channel_id=1, source_target_pairs={{0,2},{2,0},{4,6},{6,4},{8,10},{10,8},{12,14},{14,12},{1,3},{3,1},... | collective-permute-start | bytes 1572872 | tf_op jit(solution)/shard_map/ppermute | solution.py:369
  18.2 1.7 %collective-permute-start.1 = (bf16[2,256,128]{2,1,0:T(8,128)(2,1)}, bf16[2,256,128]{2,1,0:T(8,128)(2,1)S(1)}, u32[]{:S(2)}, u32[]{:S(2)}) collective-permute-start(bf16[2,256,128]{2,1,0:T(8,128)(2,1)} %get-tuple-element.31), channel_id=1, source_target_pairs={{0,1},{1,0},{2,3},{3,2},{4,5},{5,4},{6,7},{7,6},{8,9},{9,8},{10,11... | collective-permute-start | bytes 393224 | tf_op jit(solution)/shard_map/ppermute | solution.py:329
  18.2 1.7 %collective-permute-start = (bf16[2,256,128]{2,1,0:T(8,128)(2,1)S(1)}, bf16[2,256,128]{2,1,0:T(8,128)(2,1)S(1)}, u32[]{:S(2)}, u32[]{:S(2)}) collective-permute-start(bf16[2,256,128]{2,1,0:T(8,128)(2,1)S(1)} %get-tuple-element.30), channel_id=1, source_target_pairs={{0,1},{1,0},{2,3},{3,2},{4,5},{5,4},{6,7},{7,6},{8,9},{9,8},{10,11... | collective-permute-start | bytes 393224 | tf_op jit(solution)/shard_map/ppermute | solution.py:329
  25.8 83.4 %copy-start.5 = (s32[8,16]{1,0:T(8,128)S(1)}, s32[8,16]{1,0:T(8,128)}, u32[]{:S(2)}) copy-start(s32[8,16]{1,0:T(8,128)} %param.5) | copy-start | bytes 1540
  25.8 1.3 %collective-permute-start.3 = (bf16[1,256,128]{2,1,0:T(8,128)(2,1)S(1)}, bf16[1,256,128]{2,1,0:T(8,128)(2,1)S(1)}, u32[]{:S(2)}, u32[]{:S(2)}) collective-permute-start(bf16[1,256,128]{2,1,0:T(8,128)(2,1)S(1)} %slice_select_fusion.2), channel_id=1, source_target_pairs={{0,1},{1,0},{2,3},{3,2},{4,5},{5,4},{6,7},{7,6},{8,9},{9,8},{10,11... | collective-permute-start | bytes 196616 | tf_op jit(solution)/shard_map/ppermute | solution.py:329
  39.4 12.3 %collective-permute-start.7 = (bf16[256,1024]{1,0:T(8,128)(2,1)S(1)}, bf16[256,1024]{1,0:T(8,128)(2,1)S(1)}, u32[]{:S(2)}, u32[]{:S(2)}) collective-permute-start(bf16[256,1024]{1,0:T(8,128)(2,1)S(1)} %halo_blur.1), channel_id=1, source_target_pairs={{0,2},{2,0},{4,6},{6,4},{8,10},{10,8},{12,14},{14,12},{1,3},{3,1},... | collective-permute-start | bytes 1572872 | tf_op jit(solution)/shard_map/ppermute | solution.py:376
  42.0 1.4 %collective-permute-start.8 = (bf16[2,256,128]{2,1,0:T(8,128)(2,1)S(1)}, bf16[2,256,128]{2,1,0:T(8,128)(2,1)S(1)}, u32[]{:S(2)}, u32[]{:S(2)}) collective-permute-start(bf16[2,256,128]{2,1,0:T(8,128)(2,1)S(1)} %pad_maximum_fusion.4), channel_id=1, source_target_pairs={{0,1},{1,0},{2,3},{3,2},{4,5},{5,4},{6,7},{7,6},{8,9},{9,8},{10,11... | collective-permute-start | bytes 393224 | tf_op jit(solution)/shard_map/ppermute | solution.py:329
  48.4 14.8 %collective-permute-start.12 = (bf16[256,1024]{1,0:T(8,128)(2,1)S(1)}, bf16[256,1024]{1,0:T(8,128)(2,1)S(1)}, u32[]{:S(2)}, u32[]{:S(2)}) collective-permute-start(bf16[256,1024]{1,0:T(8,128)(2,1)S(1)} %blur_score_pick.1), channel_id=1, source_target_pairs={{4,0},{14,2},{8,4},{2,6},{12,8},{6,10},{0,12},{10,14},{5,1},{15,3}... | collective-permute-start | bytes 1572872 | tf_op jit(solution)/shard_map/ppermute | solution.py:379
  51.8 14.9 %collective-permute-start.11 = (bf16[256,1024]{1,0:T(8,128)(2,1)S(1)}, bf16[256,1024]{1,0:T(8,128)(2,1)S(1)}, u32[]{:S(2)}, u32[]{:S(2)}) collective-permute-start(bf16[256,1024]{1,0:T(8,128)(2,1)S(1)} %blur_score_pick.1), channel_id=1, source_target_pairs={{0,2},{2,0},{4,6},{6,4},{8,10},{10,8},{12,14},{14,12},{1,3},{3,1},... | collective-permute-start | bytes 1572872 | tf_op jit(solution)/shard_map/ppermute | solution.py:382
  54.1 21.7 %collective-permute-start.10 = (bf16[256,1024]{1,0:T(8,128)(2,1)S(1)}, bf16[256,1024]{1,0:T(8,128)(2,1)}, u32[]{:S(2)}, u32[]{:S(2)}) collective-permute-start(bf16[256,1024]{1,0:T(8,128)(2,1)S(1)} %join_score.1), channel_id=1, source_target_pairs={{0,2},{2,0},{4,6},{6,4},{8,10},{10,8},{12,14},{14,12},{1,3},{3,1},... | collective-permute-start | bytes 1572872 | tf_op jit(solution)/shard_map/ppermute | solution.py:383
  54.4 21.3 %collective-permute-start.9 = (bf16[256,1024]{1,0:T(8,128)(2,1)S(1)}, bf16[256,1024]{1,0:T(8,128)(2,1)S(1)}, u32[]{:S(2)}, u32[]{:S(2)}) collective-permute-start(bf16[256,1024]{1,0:T(8,128)(2,1)S(1)} %join_score.1), channel_id=1, source_target_pairs={{4,0},{14,2},{8,4},{2,6},{12,8},{6,10},{0,12},{10,14},{5,1},{15,3}... | collective-permute-start | bytes 1572872 | tf_op jit(solution)/shard_map/ppermute | solution.py:384
  63.3 31.9 %collective-permute-start.19 = (bf16[256,1024]{1,0:T(8,128)(2,1)S(1)}, bf16[256,1024]{1,0:T(8,128)(2,1)S(1)}, u32[]{:S(2)}, u32[]{:S(2)}) collective-permute-start(bf16[256,1024]{1,0:T(8,128)(2,1)S(1)} %blur_score_pick.1), channel_id=1, source_target_pairs={{0,4},{2,14},{4,8},{6,2},{8,12},{10,6},{12,0},{14,10},{1,5},{3,15}... | collective-permute-start | bytes 1572872 | tf_op jit(solution)/shard_map/ppermute | solution.py:386
  75.7 26.2 %collective-permute-start.16 = (bf16[256,1024]{1,0:T(8,128)(2,1)S(1)}, bf16[256,1024]{1,0:T(8,128)(2,1)S(1)}, u32[]{:S(2)}, u32[]{:S(2)}) collective-permute-start(bf16[256,1024]{1,0:T(8,128)(2,1)S(1)} %collective-permute-done.9), channel_id=1, source_target_pairs={{0,2},{2,0},{4,6},{6,4},{8,10},{10,8},{12,14},{14,12},{1,3},{3,1},... | collective-permute-start | bytes 1572872 | tf_op jit(solution)/shard_map/ppermute | solution.py:392
  76.7 25.2 %collective-permute-start.15 = (bf16[256,1024]{1,0:T(8,128)(2,1)S(1)}, bf16[256,1024]{1,0:T(8,128)(2,1)S(1)}, u32[]{:S(2)}, u32[]{:S(2)}) collective-permute-start(bf16[256,1024]{1,0:T(8,128)(2,1)S(1)} %join_score.1), channel_id=1, source_target_pairs={{0,4},{2,14},{4,8},{6,2},{8,12},{10,6},{12,0},{14,10},{1,5},{3,15}... | collective-permute-start | bytes 1572872 | tf_op jit(solution)/shard_map/ppermute | solution.py:391
  92.0 15.7 %collective-permute-start.18 = (bf16[2,256,1024]{2,1,0:T(8,128)(2,1)S(1)}, bf16[2,256,1024]{2,1,0:T(8,128)(2,1)S(1)}, u32[]{:S(2)}, u32[]{:S(2)}) collective-permute-start(bf16[2,256,1024]{2,1,0:T(8,128)(2,1)S(1)} %pad_maximum_fusion.2.refs_0_), channel_id=1, source_target_pairs={{0,1},{1,0},{2,3},{3,2},{4,5},{5,4},{6,7},{7,6},{8,9},{9,8},{10,11... | collective-permute-start | bytes 3145736 | tf_op jit(solution)/shard_map/ppermute | solution.py:329
  92.0 15.6 %collective-permute-start.21 = (bf16[256,1024]{1,0:T(8,128)(2,1)S(1)}, bf16[256,1024]{1,0:T(8,128)(2,1)}, u32[]{:S(2)}, u32[]{:S(2)}) collective-permute-start(bf16[256,1024]{1,0:T(8,128)(2,1)S(1)} %collective-permute-done.12), channel_id=1, source_target_pairs={{0,2},{2,0},{4,6},{6,4},{8,10},{10,8},{12,14},{14,12},{1,3},{3,1},... | collective-permute-start | bytes 1572872 | tf_op jit(solution)/shard_map/ppermute | solution.py:387
  95.1 22.4 %collective-permute-start.13 = (bf16[2,256,1024]{2,1,0:T(8,128)(2,1)S(1)}, bf16[2,256,1024]{2,1,0:T(8,128)(2,1)}, u32[]{:S(2)}, u32[]{:S(2)}) collective-permute-start(bf16[2,256,1024]{2,1,0:T(8,128)(2,1)S(1)} %pad_maximum_fusion.refs_0_), channel_id=1, source_target_pairs={{0,1},{1,0},{2,3},{3,2},{4,5},{5,4},{6,7},{7,6},{8,9},{9,8},{10,11... | collective-permute-start | bytes 3145736 | tf_op jit(solution)/shard_map/ppermute | solution.py:329
  101.9 8.0 %collective-permute-start.20 = (bf16[2,256,1024]{2,1,0:T(8,128)(2,1)}, bf16[2,256,1024]{2,1,0:T(8,128)(2,1)}, u32[]{:S(2)}, u32[]{:S(2)}) collective-permute-start(bf16[2,256,1024]{2,1,0:T(8,128)(2,1)} %pad_maximum_fusion.3.refs_2_), channel_id=1, source_target_pairs={{0,1},{1,0},{2,3},{3,2},{4,5},{5,4},{6,7},{7,6},{8,9},{9,8},{10,11... | collective-permute-start | bytes 3145736 | tf_op jit(solution)/shard_map/ppermute | solution.py:329
  102.0 15.5 %collective-permute-start.17 = (bf16[2,256,1024]{2,1,0:T(8,128)(2,1)S(1)}, bf16[2,256,1024]{2,1,0:T(8,128)(2,1)}, u32[]{:S(2)}, u32[]{:S(2)}) collective-permute-start(bf16[2,256,1024]{2,1,0:T(8,128)(2,1)S(1)} %pad_maximum_fusion.1.refs_4_), channel_id=1, source_target_pairs={{0,1},{1,0},{2,3},{3,2},{4,5},{5,4},{6,7},{7,6},{8,9},{9,8},{10,11... | collective-permute-start | bytes 3145736 | tf_op jit(solution)/shard_map/ppermute | solution.py:329
  107.6 2.3 %collective-permute-start.22 = (bf16[1,256,1024]{2,1,0:T(8,128)(2,1)}, bf16[1,256,1024]{2,1,0:T(8,128)(2,1)}, u32[]{:S(2)}, u32[]{:S(2)}) collective-permute-start(bf16[1,256,1024]{2,1,0:T(8,128)(2,1)} %bitcast.11.refs_4_), channel_id=1, source_target_pairs={{0,1},{1,0},{2,3},{3,2},{4,5},{5,4},{6,7},{7,6},{8,9},{9,8},{10,11... | collective-permute-start | bytes 1572872 | tf_op jit(solution)/shard_map/ppermute | solution.py:329
  108.6 8.9 %collective-permute-start.14 = (bf16[1,256,1024]{2,1,0:T(8,128)(2,1)}, bf16[1,256,1024]{2,1,0:T(8,128)(2,1)}, u32[]{:S(2)}, u32[]{:S(2)}) collective-permute-start(bf16[1,256,1024]{2,1,0:T(8,128)(2,1)} %bitcast.4.refs_2_), channel_id=1, source_target_pairs={{0,1},{1,0},{2,3},{3,2},{4,5},{5,4},{6,7},{7,6},{8,9},{9,8},{10,11... | collective-permute-start | bytes 1572872 | tf_op jit(solution)/shard_map/ppermute | solution.py:329
  (5 other events, 5.2 us)

commit v14 on v13

--- a/solution.py
+++ b/solution.py
@@ -347,7 +347,8 @@
     within = ids % blocks
     present = partners >= 0
     parts_0 = jnp.where(kind == 4, 8 + away, kind // 2 * 4 + kind % 2 + 2 * away)
-    parts_1 = jnp.where(kind == 3, 4 + away, jnp.where(kind < 2, kind, kind // 2 + 5) + 2 * away)
+    alone = jnp.where(kind == 3, 4, jnp.where(kind == 4, 6, 8)) + away
+    parts_1 = jnp.where(kind < 2, kind + 2 * away, alone)
     place_0, place_1 = (
         jnp.where(present, part * blocks + within, 0).astype(jnp.int32)
         for part in (parts_0, parts_1)
@@ -388,12 +389,14 @@
     pair_0 = after(pair_0, ahead_0)
     pair_1 = after(pair_1, pair_0)
     ahead_1 = after(ahead_1, pair_1)
-    behind_1 = lax.ppermute(after(own_1, ahead_1), "row", behind)
-    rest_1 = lax.ppermute(ahead_1, "row", in_pair)
-    behind_0, rest_0 = after(behind_0, ahead_1), after(rest_0, ahead_1)
+    rest_0 = after(rest_0, ahead_1)
+    behind_0 = after(behind_0, rest_0)
+    rest_1 = lax.ppermute(after(ahead_1, rest_0), "row", in_pair)
+    behind_1 = lax.ppermute(after(own_1, rest_0), "row", behind)
     sources_0 = both(own_0, ahead_0) + both(behind_0, pair_0) + both(rest_0)
-    sources_1 = both(own_1, ahead_1) + both(pair_1) + both(behind_1, rest_1)
     out = make_tiles(0, windows, place_0, present, sources_0, None)
+    rest_1, behind_1 = after(rest_1, out), after(behind_1, out)
+    sources_1 = both(own_1, ahead_1) + both(pair_1) + both(rest_1) + both(behind_1)
     return make_tiles(1, windows, place_1, present, sources_1, out)
 
 

time: 126 us -> 114 us (0.905); the launches traced: 124 us -> 114 us
  starting transfers between devices: 45.8 us -> 29.1 us
  waiting for transfers between devices: 43.1 us -> 47.6 us
  Pallas kernels: 28.2 us -> 29.9 us
    ppermute x2, starting transfers between devices: 16.1 us -> 1.88 us  [the longest x1 1.37 us: on_device(): behind_1 = lax.ppermute(after(own_1, rest_0), 'row', behind)]
    ppermute x1, waiting for transfers between devices: 5.03 us -> 9.21 us  [on_device(): rest_0 = lax.ppermute(ahead_0, 'row', in_pair)]
    ppermute x1, waiting for transfers between devices: 9.06 us -> 11.2 us  [on_device(): pair_1 = lax.ppermute(own_1, 'row', in_pair)]
    pallas_call x4, Pallas kernels: 12.4 us -> 14.4 us  [call_on_rows(): pl.pallas_call(kernel, grid=(1,), in_specs=[whole(value) for value in ope...]
    ppermute x1, starting transfers between devices: 1.58 us -> 0.01 us  [on_device(): behind_0 = lax.ppermute(after(own_0, ahead_0), 'row', behind)]
    ppermute x10 -> x11, waiting for transfers between devices: 4.38 us -> 5.66 us  [other_col(): return lax.ppermute(value, 'col', [(0, 1), (1, 0)])]
    unnamed x12 -> x16, local copies, waits for them, and re-layouts: 5.17 us -> 5.16 us
  transfers between devices with their start and end apart: 23 -> 24, of which waited for: 12 -> 14; matrix products, arithmetic and copies ran while one was open for 1% -> 1% of each run, Pallas kernels for 15% -> 18%
where the time goes in v14:
time: 114 us
  waiting for transfers between devices  47.6 us (42%)
  Pallas kernels  29.9 us (26%)
  starting transfers between devices  29.1 us (26%)
  local copies, waits for them, and re-layouts  5.16 us (5%)
  other arithmetic  1.58 us (1%)
    pallas_call x4, Pallas kernels, call_on_rows(): pl.pallas_call(kernel, grid=(1,), in_specs=[whole(value) for value in ope...  14.4 us
    pallas_call x2, Pallas kernels, make_tiles(): pl.pallas_call(functools.partial(tiles_kernel, sources=count, window=wind...  12.1 us
    ppermute x1, waiting for transfers between devices, on_device(): pair_1 = lax.ppermute(own_1, 'row', in_pair)  11.2 us
    ppermute x1, waiting for transfers between devices, on_device(): facing_0 = lax.ppermute(after(near_0, gm_pair), 'row', in_pair)  9.42 us
    ppermute x1, waiting for transfers between devices, on_device(): rest_0 = lax.ppermute(ahead_0, 'row', in_pair)  9.21 us
    ppermute x11, waiting for transfers between devices, other_col(): return lax.ppermute(value, 'col', [(0, 1), (1, 0)])  5.66 us
    ppermute x1, starting transfers between devices, on_device(): gm_pair = lax.ppermute(gm, 'row', in_pair)  5.28 us
    unnamed x16, local copies, waits for them, and re-layouts  5.16 us
  transfers between devices with their start and end apart: 24, of which 14 were waited for; matrix products, arithmetic and copies ran while one was open for 1% of the time, Pallas kernels for 18%

profile of v14, /device:TPU:0, one launch (start us, length us, event | category | flops | bytes accessed | tf_op | source)
XLA Modules:
  0.0 113.7 jit_solution(13891946997890882926)
XLA Ops:
  0.0 1.6 %copy-done = bf16[2,256,2,8,128]{4,3,2,1,0:T(8,128)(2,1)S(1)} copy-done((bf16[2,256,2,8,128]{4,3,2,1,0:T(8,128)(2,1)S(1)}, bf16[2,256,2,8,128]{4,3,2,1,0:T(8,128)(2,1)}, u32[]{:S(2)}) %copy-start) | copy-done | bytes 2097176
  1.6 3.4 %faces.1 = (bf16[8,256,128]{2,1,0:T(8,128)(2,1)}, bf16[8,256,128]{2,1,0:T(8,128)(2,1)}, bf16[2,256,128]{2,1,0:T(8,128)(2,1)S(1)}, bf16[8,256,128]{2,1,0:T(8,128)...) custom-call(bf16[2,256,2,8,128]{4,3,2,1,0:T(8,128)(2,1)S(1)} %copy-done), custom_call_target="tpu_custom_call" | custom-call | flops 1 | bytes 1 | tf_op jit(solution)/shard_map/faces/pallas_call | solution.py:59
  5.0 1.4 %collective-permute-start.2 = (bf16[8,256,128]{2,1,0:T(8,128)(2,1)}, bf16[8,256,128]{2,1,0:T(8,128)(2,1)S(1)}, u32[]{:S(2)}, u32[]{:S(2)}) collective-permute-start(bf16[8,256,128]{2,1,0:T(8,128)(2,1)} %get-tuple-element.32.outer_ref), channel_id=1, source_target_pairs={{2,6},{4,0},{6,10},{8,4},{10,14},{12,8},{3,7},{5,1},{7,11},{9,5},{... | collective-permute-start | bytes 1572872 | tf_op jit(solution)/shard_map/ppermute | solution.py:369
  6.4 5.3 %collective-permute-start.4 = (s32[1,1024]{1,0:T(1,128)}, s32[1,1024]{1,0:T(1,128)S(1)}, u32[]{:S(2)}, u32[]{:S(2)}) collective-permute-start(s32[1,1024]{1,0:T(1,128)} %bitcast.16), channel_id=1, source_target_pairs={{0,2},{2,0},{4,6},{6,4},{8,10},{10,8},{12,14},{14,12},{1,3},{3,1},... | collective-permute-start | bytes 12296 | tf_op jit(solution)/shard_map/ppermute | solution.py:363
  11.7 1.8 %collective-permute-done.4.gm_ref = s32[1,1024]{1,0:T(1,128)S(1)} collective-permute-done((s32[1,1024]{1,0:T(1,128)}, s32[1,1024]{1,0:T(1,128)S(1)}, u32[]{:S(2)}, u32[]{:S(2)}) %collective-permute-start.4) | collective-permute-done | bytes 4128 | tf_op jit(solution)/shard_map/ppermute | solution.py:363
  14.3 4.3 %collective-permute-start.5 = (bf16[8,256,128]{2,1,0:T(8,128)(2,1)}, bf16[8,256,128]{2,1,0:T(8,128)(2,1)S(1)}, u32[]{:S(2)}, u32[]{:S(2)}) collective-permute-start(bf16[8,256,128]{2,1,0:T(8,128)(2,1)} %get-tuple-element.38.near_ref), channel_id=1, source_target_pairs={{0,2},{2,0},{4,6},{6,4},{8,10},{10,8},{12,14},{14,12},{1,3},{3,1},... | collective-permute-start | bytes 1572872 | tf_op jit(solution)/shard_map/ppermute | solution.py:370
  20.8 6.2 %inner_blur.1.inner_ref = f32[256,1024]{1,0:T(8,128)S(1)} custom-call(bf16[8,256,128]{2,1,0:T(8,128)(2,1)S(1)} %get-tuple-element.31.near_ref, bf16[8,256,128]{2,1,0:T(8,128)(2,1)} %get-tuple-element.32.outer_ref, bf16[2,256,128]{2,1,0:T(8,128)(2,1)S(1)} %collective-permute-done.edge_ref, s32[1,1024]{1,0:T(1,128)S(1)} %bitcast.17), custom_call_target="tpu_custom_call" | custom-call | flops 1 | bytes 1 | tf_op jit(solution)/shard_map/inner_blur/pallas_call | solution.py:200
  28.4 2.4 %halo_blur.1 = bf16[256,1024]{1,0:T(8,128)(2,1)S(1)} custom-call(bf16[8,256,128]{2,1,0:T(8,128)(2,1)S(1)} %get-tuple-element.31.near_ref, bf16[8,256,128]{2,1,0:T(8,128)(2,1)S(1)} %collective-permute-done.2.beyond_ref, bf16[2,256,128]{2,1,0:T(8,128)(2,1)S(1)} %collective-permute-done.edge_ref, bf16[256,128]{1,0:T(8,128)(2,1)S(1)} %bitcast.15, ...), custom_call_target="tpu_custom_call" | custom-call | flops 1 | bytes 1 | tf_op jit(solution)/shard_map/halo_blur/pallas_call | solution.py:200
  30.8 9.4 %collective-permute-done.5.facing_ref = bf16[8,256,128]{2,1,0:T(8,128)(2,1)S(1)} collective-permute-done((bf16[8,256,128]{2,1,0:T(8,128)(2,1)}, bf16[8,256,128]{2,1,0:T(8,128)(2,1)S(1)}, u32[]{:S(2)}, u32[]{:S(2)}) %collective-permute-start.5) | collective-permute-done | bytes 524320 | tf_op jit(solution)/shard_map/ppermute | solution.py:370
  40.2 2.4 %collective-permute-start.7 = (bf16[256,1024]{1,0:T(8,128)(2,1)S(1)}, bf16[256,1024]{1,0:T(8,128)(2,1)S(1)}, u32[]{:S(2)}, u32[]{:S(2)}) collective-permute-start(bf16[256,1024]{1,0:T(8,128)(2,1)S(1)} %halo_blur.1), channel_id=1, source_target_pairs={{0,2},{2,0},{4,6},{6,4},{8,10},{10,8},{12,14},{14,12},{1,3},{3,1},... | collective-permute-start | bytes 1572872 | tf_op jit(solution)/shard_map/ppermute | solution.py:377
  42.7 1.3 %collective-permute-done.8.corner_ref = bf16[2,256,128]{2,1,0:T(8,128)(2,1)S(1)} collective-permute-done((bf16[2,256,128]{2,1,0:T(8,128)(2,1)S(1)}, bf16[2,256,128]{2,1,0:T(8,128)(2,1)S(1)}, u32[]{:S(2)}, u32[]{:S(2)}) %collective-permute-start.8) | collective-permute-done | bytes 131104 | tf_op jit(solution)/shard_map/ppermute | solution.py:329
  44.7 4.5 %blur_score_pick.1 = bf16[256,1024]{1,0:T(8,128)(2,1)S(1)} custom-call(bf16[8,256,128]{2,1,0:T(8,128)(2,1)} %get-tuple-element.38.near_ref, bf16[8,256,128]{2,1,0:T(8,128)(2,1)} %get-tuple-element.41.outer_ref, bf16[8,256,128]{2,1,0:T(8,128)(2,1)S(1)} %collective-permute-done.5.facing_ref, bf16[8,256,128]{2,1,0:T(8,128)(2,1)S(1)} %collective-permute-done.6.across_ref, ...), custom_call_target="tpu_custom_call" | custom-call | flops 1 | bytes 1 | tf_op jit(solution)/shard_map/blur_score_pick/pallas_call | solution.py:200
  49.2 2.2 %collective-permute-start.12 = (bf16[256,1024]{1,0:T(8,128)(2,1)S(1)}, bf16[256,1024]{1,0:T(8,128)(2,1)S(1)}, u32[]{:S(2)}, u32[]{:S(2)}) collective-permute-start(bf16[256,1024]{1,0:T(8,128)(2,1)S(1)} %blur_score_pick.1), channel_id=1, source_target_pairs={{4,0},{14,2},{8,4},{2,6},{12,8},{6,10},{0,12},{10,14},{5,1},{15,3}... | collective-permute-start | bytes 1572872 | tf_op jit(solution)/shard_map/ppermute | solution.py:380
  52.5 1.7 %collective-permute-start.11 = (bf16[256,1024]{1,0:T(8,128)(2,1)S(1)}, bf16[256,1024]{1,0:T(8,128)(2,1)S(1)}, u32[]{:S(2)}, u32[]{:S(2)}) collective-permute-start(bf16[256,1024]{1,0:T(8,128)(2,1)S(1)} %blur_score_pick.1), channel_id=1, source_target_pairs={{0,2},{2,0},{4,6},{6,4},{8,10},{10,8},{12,14},{14,12},{1,3},{3,1},... | collective-permute-start | bytes 1572872 | tf_op jit(solution)/shard_map/ppermute | solution.py:383
  55.8 4.4 %collective-permute-start.9 = (bf16[256,1024]{1,0:T(8,128)(2,1)}, bf16[256,1024]{1,0:T(8,128)(2,1)}, u32[]{:S(2)}, u32[]{:S(2)}) collective-permute-start(bf16[256,1024]{1,0:T(8,128)(2,1)} %join_score.1), channel_id=1, source_target_pairs={{4,0},{14,2},{8,4},{2,6},{12,8},{6,10},{0,12},{10,14},{5,1},{15,3}... | collective-permute-start | bytes 1572872 | tf_op jit(solution)/shard_map/ppermute | solution.py:385
  60.2 3.9 %collective-permute-done.12 = bf16[256,1024]{1,0:T(8,128)(2,1)S(1)} collective-permute-done((bf16[256,1024]{1,0:T(8,128)(2,1)S(1)}, bf16[256,1024]{1,0:T(8,128)(2,1)S(1)}, u32[]{:S(2)}, u32[]{:S(2)}) %collective-permute-start.12) | collective-permute-done | bytes 524320 | tf_op jit(solution)/shard_map/ppermute | solution.py:380
  64.1 2.2 %collective-permute-start.15 = (bf16[256,1024]{1,0:T(8,128)(2,1)S(1)}, bf16[256,1024]{1,0:T(8,128)(2,1)}, u32[]{:S(2)}, u32[]{:S(2)}) collective-permute-start(bf16[256,1024]{1,0:T(8,128)(2,1)S(1)} %collective-permute-done.12), channel_id=1, source_target_pairs={{0,2},{2,0},{4,6},{6,4},{8,10},{10,8},{12,14},{14,12},{1,3},{3,1},... | collective-permute-start | bytes 1572872 | tf_op jit(solution)/shard_map/ppermute | solution.py:388
  67.3 11.2 %collective-permute-done.10 = bf16[256,1024]{1,0:T(8,128)(2,1)S(1)} collective-permute-done((bf16[256,1024]{1,0:T(8,128)(2,1)}, bf16[256,1024]{1,0:T(8,128)(2,1)S(1)}, u32[]{:S(2)}, u32[]{:S(2)}) %collective-permute-start.10) | collective-permute-done | bytes 524320 | tf_op jit(solution)/shard_map/ppermute | solution.py:384
  78.6 9.2 %collective-permute-done.15 = bf16[256,1024]{1,0:T(8,128)(2,1)} collective-permute-done((bf16[256,1024]{1,0:T(8,128)(2,1)S(1)}, bf16[256,1024]{1,0:T(8,128)(2,1)}, u32[]{:S(2)}, u32[]{:S(2)}) %collective-permute-start.15) | collective-permute-done | bytes 524320 | tf_op jit(solution)/shard_map/ppermute | solution.py:388
  88.5 1.4 %collective-permute-start.22 = (bf16[256,1024]{1,0:T(8,128)(2,1)}, bf16[256,1024]{1,0:T(8,128)(2,1)}, u32[]{:S(2)}, u32[]{:S(2)}) collective-permute-start(bf16[256,1024]{1,0:T(8,128)(2,1)} %join_score.1), channel_id=1, source_target_pairs={{0,4},{2,14},{4,8},{6,2},{8,12},{10,6},{12,0},{14,10},{1,5},{3,15}... | collective-permute-start | bytes 1572872 | tf_op jit(solution)/shard_map/ppermute | solution.py:395
  94.0 6.1 %tiles.2.refs_8_ = bf16[8,16,2,128,128]{4,3,2,1,0:T(8,128)(2,1)} custom-call(s32[8,16]{1,0:T(8,128)S(1)} %get-tuple-element.57.place_ref, s32[8,16]{1,0:T(8,128)S(1)} %fusion.21.present_ref, bf16[2,256,1024]{2,1,0:T(8,128)(2,1)S(1)} %pad_maximum_fusion.1.refs_0_, bf16[2,256,1024]{2,1,0:T(8,128)(2,1)S(1)} %copy-done.2, ...), custom_call_target="tpu_custom_call" | custom-call | flops 1 | bytes 1 | tf_op jit(solution)/shard_map/tiles/pallas_call | solution.py:295
  100.1 4.4 %collective-permute-done.22 = bf16[256,1024]{1,0:T(8,128)(2,1)} collective-permute-done((bf16[256,1024]{1,0:T(8,128)(2,1)}, bf16[256,1024]{1,0:T(8,128)(2,1)}, u32[]{:S(2)}, u32[]{:S(2)}) %collective-permute-start.22) | collective-permute-done | bytes 524320 | tf_op jit(solution)/shard_map/ppermute | solution.py:395
  105.1 1.6 %collective-permute-done.21.refs_5_ = bf16[1,256,1024]{2,1,0:T(8,128)(2,1)S(1)} collective-permute-done((bf16[1,256,1024]{2,1,0:T(8,128)(2,1)}, bf16[1,256,1024]{2,1,0:T(8,128)(2,1)S(1)}, u32[]{:S(2)}, u32[]{:S(2)}) %collective-permute-start.21) | collective-permute-done | bytes 524320 | tf_op jit(solution)/shard_map/ppermute | solution.py:329
  107.5 6.0 %tiles.3 = bf16[8,16,2,128,128]{4,3,2,1,0:T(8,128)(2,1)} custom-call(s32[8,16]{1,0:T(8,128)S(1)} %get-tuple-element.58.place_ref, s32[8,16]{1,0:T(8,128)S(1)} %fusion.21.present_ref, bf16[2,256,1024]{2,1,0:T(8,128)(2,1)S(1)} %pad_maximum_fusion.refs_0_, bf16[2,256,1024]{2,1,0:T(8,128)(2,1)} %collective-permute-done.13.refs_1_, ...), custom_call_target="tpu_custom_call", output_to_operand_aliasing={{}: (10, {})} | custom-call | flops 1 | bytes 1 | tf_op jit(solution)/shard_map/tiles/pallas_call | solution.py:295
  (55 shorter events, 14.9 us)
Async XLA Ops:
  5.0 22.1 %collective-permute-start.2 = (bf16[8,256,128]{2,1,0:T(8,128)(2,1)}, bf16[8,256,128]{2,1,0:T(8,128)(2,1)S(1)}, u32[]{:S(2)}, u32[]{:S(2)}) collective-permute-start(bf16[8,256,128]{2,1,0:T(8,128)(2,1)} %get-tuple-element.32.outer_ref), channel_id=1, source_target_pairs={{2,6},{4,0},{6,10},{8,4},{10,14},{12,8},{3,7},{5,1},{7,11},{9,5},{... | collective-permute-start | bytes 1572872 | tf_op jit(solution)/shard_map/ppermute | solution.py:369
  6.4 7.1 %collective-permute-start.4 = (s32[1,1024]{1,0:T(1,128)}, s32[1,1024]{1,0:T(1,128)S(1)}, u32[]{:S(2)}, u32[]{:S(2)}) collective-permute-start(s32[1,1024]{1,0:T(1,128)} %bitcast.16), channel_id=1, source_target_pairs={{0,2},{2,0},{4,6},{6,4},{8,10},{10,8},{12,14},{14,12},{1,3},{3,1},... | collective-permute-start | bytes 12296 | tf_op jit(solution)/shard_map/ppermute | solution.py:363
  13.5 17.3 %collective-permute-start.6 = (bf16[8,256,128]{2,1,0:T(8,128)(2,1)}, bf16[8,256,128]{2,1,0:T(8,128)(2,1)S(1)}, u32[]{:S(2)}, u32[]{:S(2)}) collective-permute-start(bf16[8,256,128]{2,1,0:T(8,128)(2,1)} %get-tuple-element.41.outer_ref), channel_id=1, source_target_pairs={{2,4},{4,2},{6,8},{8,6},{10,12},{12,10},{3,5},{5,3},{7,9},{9,7},{1... | collective-permute-start | bytes 1572872 | tf_op jit(solution)/shard_map/ppermute | solution.py:371
  14.3 25.9 %collective-permute-start.5 = (bf16[8,256,128]{2,1,0:T(8,128)(2,1)}, bf16[8,256,128]{2,1,0:T(8,128)(2,1)S(1)}, u32[]{:S(2)}, u32[]{:S(2)}) collective-permute-start(bf16[8,256,128]{2,1,0:T(8,128)(2,1)} %get-tuple-element.38.near_ref), channel_id=1, source_target_pairs={{0,2},{2,0},{4,6},{6,4},{8,10},{10,8},{12,14},{14,12},{1,3},{3,1},... | collective-permute-start | bytes 1572872 | tf_op jit(solution)/shard_map/ppermute | solution.py:370
  18.6 1.3 %collective-permute-start.1 = (bf16[2,256,128]{2,1,0:T(8,128)(2,1)S(1)}, bf16[2,256,128]{2,1,0:T(8,128)(2,1)S(1)}, u32[]{:S(2)}, u32[]{:S(2)}) collective-permute-start(bf16[2,256,128]{2,1,0:T(8,128)(2,1)S(1)} %get-tuple-element.34), channel_id=1, source_target_pairs={{0,1},{1,0},{2,3},{3,2},{4,5},{5,4},{6,7},{7,6},{8,9},{9,8},{10,11... | collective-permute-start | bytes 393224 | tf_op jit(solution)/shard_map/ppermute | solution.py:329
  18.6 1.5 %collective-permute-start = (bf16[2,256,128]{2,1,0:T(8,128)(2,1)S(1)}, bf16[2,256,128]{2,1,0:T(8,128)(2,1)S(1)}, u32[]{:S(2)}, u32[]{:S(2)}) collective-permute-start(bf16[2,256,128]{2,1,0:T(8,128)(2,1)S(1)} %get-tuple-element.33), channel_id=1, source_target_pairs={{0,1},{1,0},{2,3},{3,2},{4,5},{5,4},{6,7},{7,6},{8,9},{9,8},{10,11... | collective-permute-start | bytes 393224 | tf_op jit(solution)/shard_map/ppermute | solution.py:329
  27.1 1.3 %collective-permute-start.3 = (bf16[1,256,128]{2,1,0:T(8,128)(2,1)S(1)}, bf16[1,256,128]{2,1,0:T(8,128)(2,1)S(1)}, u32[]{:S(2)}, u32[]{:S(2)}) collective-permute-start(bf16[1,256,128]{2,1,0:T(8,128)(2,1)S(1)} %slice_select_fusion.2), channel_id=1, source_target_pairs={{0,1},{1,0},{2,3},{3,2},{4,5},{5,4},{6,7},{7,6},{8,9},{9,8},{10,11... | collective-permute-start | bytes 196616 | tf_op jit(solution)/shard_map/ppermute | solution.py:329
  40.2 12.2 %collective-permute-start.7 = (bf16[256,1024]{1,0:T(8,128)(2,1)S(1)}, bf16[256,1024]{1,0:T(8,128)(2,1)S(1)}, u32[]{:S(2)}, u32[]{:S(2)}) collective-permute-start(bf16[256,1024]{1,0:T(8,128)(2,1)S(1)} %halo_blur.1), channel_id=1, source_target_pairs={{0,2},{2,0},{4,6},{6,4},{8,10},{10,8},{12,14},{14,12},{1,3},{3,1},... | collective-permute-start | bytes 1572872 | tf_op jit(solution)/shard_map/ppermute | solution.py:377
  42.6 1.4 %collective-permute-start.8 = (bf16[2,256,128]{2,1,0:T(8,128)(2,1)S(1)}, bf16[2,256,128]{2,1,0:T(8,128)(2,1)S(1)}, u32[]{:S(2)}, u32[]{:S(2)}) collective-permute-start(bf16[2,256,128]{2,1,0:T(8,128)(2,1)S(1)} %pad_maximum_fusion.3), channel_id=1, source_target_pairs={{0,1},{1,0},{2,3},{3,2},{4,5},{5,4},{6,7},{7,6},{8,9},{9,8},{10,11... | collective-permute-start | bytes 393224 | tf_op jit(solution)/shard_map/ppermute | solution.py:329
  49.2 14.8 %collective-permute-start.12 = (bf16[256,1024]{1,0:T(8,128)(2,1)S(1)}, bf16[256,1024]{1,0:T(8,128)(2,1)S(1)}, u32[]{:S(2)}, u32[]{:S(2)}) collective-permute-start(bf16[256,1024]{1,0:T(8,128)(2,1)S(1)} %blur_score_pick.1), channel_id=1, source_target_pairs={{4,0},{14,2},{8,4},{2,6},{12,8},{6,10},{0,12},{10,14},{5,1},{15,3}... | collective-permute-start | bytes 1572872 | tf_op jit(solution)/shard_map/ppermute | solution.py:380
  52.5 14.9 %collective-permute-start.11 = (bf16[256,1024]{1,0:T(8,128)(2,1)S(1)}, bf16[256,1024]{1,0:T(8,128)(2,1)S(1)}, u32[]{:S(2)}, u32[]{:S(2)}) collective-permute-start(bf16[256,1024]{1,0:T(8,128)(2,1)S(1)} %blur_score_pick.1), channel_id=1, source_target_pairs={{0,2},{2,0},{4,6},{6,4},{8,10},{10,8},{12,14},{14,12},{1,3},{3,1},... | collective-permute-start | bytes 1572872 | tf_op jit(solution)/shard_map/ppermute | solution.py:383
  55.5 23.1 %collective-permute-start.10 = (bf16[256,1024]{1,0:T(8,128)(2,1)}, bf16[256,1024]{1,0:T(8,128)(2,1)S(1)}, u32[]{:S(2)}, u32[]{:S(2)}) collective-permute-start(bf16[256,1024]{1,0:T(8,128)(2,1)} %join_score.1), channel_id=1, source_target_pairs={{0,2},{2,0},{4,6},{6,4},{8,10},{10,8},{12,14},{14,12},{1,3},{3,1},... | collective-permute-start | bytes 1572872 | tf_op jit(solution)/shard_map/ppermute | solution.py:384
  55.8 22.8 %collective-permute-start.9 = (bf16[256,1024]{1,0:T(8,128)(2,1)}, bf16[256,1024]{1,0:T(8,128)(2,1)}, u32[]{:S(2)}, u32[]{:S(2)}) collective-permute-start(bf16[256,1024]{1,0:T(8,128)(2,1)} %join_score.1), channel_id=1, source_target_pairs={{4,0},{14,2},{8,4},{2,6},{12,8},{6,10},{0,12},{10,14},{5,1},{15,3}... | collective-permute-start | bytes 1572872 | tf_op jit(solution)/shard_map/ppermute | solution.py:385
  64.1 23.7 %collective-permute-start.15 = (bf16[256,1024]{1,0:T(8,128)(2,1)S(1)}, bf16[256,1024]{1,0:T(8,128)(2,1)}, u32[]{:S(2)}, u32[]{:S(2)}) collective-permute-start(bf16[256,1024]{1,0:T(8,128)(2,1)S(1)} %collective-permute-done.12), channel_id=1, source_target_pairs={{0,2},{2,0},{4,6},{6,4},{8,10},{10,8},{12,14},{14,12},{1,3},{3,1},... | collective-permute-start | bytes 1572872 | tf_op jit(solution)/shard_map/ppermute | solution.py:388
  66.2 21.5 %collective-permute-start.18 = (bf16[256,1024]{1,0:T(8,128)(2,1)S(1)}, bf16[256,1024]{1,0:T(8,128)(2,1)S(1)}, u32[]{:S(2)}, u32[]{:S(2)}) collective-permute-start(bf16[256,1024]{1,0:T(8,128)(2,1)S(1)} %blur_score_pick.1), channel_id=1, source_target_pairs={{0,4},{2,14},{4,8},{6,2},{8,12},{10,6},{12,0},{14,10},{1,5},{3,15}... | collective-permute-start | bytes 1572872 | tf_op jit(solution)/shard_map/ppermute | solution.py:387
  67.3 23.8 %collective-permute-start.17 = (bf16[2,256,1024]{2,1,0:T(8,128)(2,1)S(1)}, bf16[2,256,1024]{2,1,0:T(8,128)(2,1)S(1)}, u32[]{:S(2)}, u32[]{:S(2)}) collective-permute-start(bf16[2,256,1024]{2,1,0:T(8,128)(2,1)S(1)} %pad_maximum_fusion.1.refs_0_), channel_id=1, source_target_pairs={{0,1},{1,0},{2,3},{3,2},{4,5},{5,4},{6,7},{7,6},{8,9},{9,8},{10,11... | collective-permute-start | bytes 3145736 | tf_op jit(solution)/shard_map/ppermute | solution.py:329
  87.9 4.9 %collective-permute-start.19 = (bf16[2,256,1024]{2,1,0:T(8,128)(2,1)S(1)}, bf16[2,256,1024]{2,1,0:T(8,128)(2,1)}, u32[]{:S(2)}, u32[]{:S(2)}) collective-permute-start(bf16[2,256,1024]{2,1,0:T(8,128)(2,1)S(1)} %pad_maximum_fusion.2.refs_2_), channel_id=1, source_target_pairs={{0,1},{1,0},{2,3},{3,2},{4,5},{5,4},{6,7},{7,6},{8,9},{9,8},{10,11... | collective-permute-start | bytes 3145736 | tf_op jit(solution)/shard_map/ppermute | solution.py:329
  88.0 16.6 %collective-permute-start.16 = (bf16[256,1024]{1,0:T(8,128)(2,1)}, bf16[256,1024]{1,0:T(8,128)(2,1)}, u32[]{:S(2)}, u32[]{:S(2)}) collective-permute-start(bf16[256,1024]{1,0:T(8,128)(2,1)} %collective-permute-done.9), channel_id=1, source_target_pairs={{0,2},{2,0},{4,6},{6,4},{8,10},{10,8},{12,14},{14,12},{1,3},{3,1},... | collective-permute-start | bytes 1572872 | tf_op jit(solution)/shard_map/ppermute | solution.py:394
  88.5 16.1 %collective-permute-start.22 = (bf16[256,1024]{1,0:T(8,128)(2,1)}, bf16[256,1024]{1,0:T(8,128)(2,1)}, u32[]{:S(2)}, u32[]{:S(2)}) collective-permute-start(bf16[256,1024]{1,0:T(8,128)(2,1)} %join_score.1), channel_id=1, source_target_pairs={{0,4},{2,14},{4,8},{6,2},{8,12},{10,6},{12,0},{14,10},{1,5},{3,15}... | collective-permute-start | bytes 1572872 | tf_op jit(solution)/shard_map/ppermute | solution.py:395
  89.8 2.9 %collective-permute-start.20 = (bf16[1,256,1024]{2,1,0:T(8,128)(2,1)}, bf16[1,256,1024]{2,1,0:T(8,128)(2,1)}, u32[]{:S(2)}, u32[]{:S(2)}) collective-permute-start(bf16[1,256,1024]{2,1,0:T(8,128)(2,1)} %bitcast.9.refs_4_), channel_id=1, source_target_pairs={{0,1},{1,0},{2,3},{3,2},{4,5},{5,4},{6,7},{7,6},{8,9},{9,8},{10,11... | collective-permute-start | bytes 1572872 | tf_op jit(solution)/shard_map/ppermute | solution.py:329
  92.1 13.0 %collective-permute-start.13 = (bf16[2,256,1024]{2,1,0:T(8,128)(2,1)S(1)}, bf16[2,256,1024]{2,1,0:T(8,128)(2,1)}, u32[]{:S(2)}, u32[]{:S(2)}) collective-permute-start(bf16[2,256,1024]{2,1,0:T(8,128)(2,1)S(1)} %pad_maximum_fusion.refs_0_), channel_id=1, source_target_pairs={{0,1},{1,0},{2,3},{3,2},{4,5},{5,4},{6,7},{7,6},{8,9},{9,8},{10,11... | collective-permute-start | bytes 3145736 | tf_op jit(solution)/shard_map/ppermute | solution.py:329
  92.7 12.4 %collective-permute-start.14 = (bf16[1,256,1024]{2,1,0:T(8,128)(2,1)}, bf16[1,256,1024]{2,1,0:T(8,128)(2,1)S(1)}, u32[]{:S(2)}, u32[]{:S(2)}) collective-permute-start(bf16[1,256,1024]{2,1,0:T(8,128)(2,1)} %bitcast.13), channel_id=1, source_target_pairs={{0,1},{1,0},{2,3},{3,2},{4,5},{5,4},{6,7},{7,6},{8,9},{9,8},{10,11... | collective-permute-start | bytes 1572872 | tf_op jit(solution)/shard_map/ppermute | solution.py:329
  104.6 2.1 %collective-permute-start.21 = (bf16[1,256,1024]{2,1,0:T(8,128)(2,1)}, bf16[1,256,1024]{2,1,0:T(8,128)(2,1)S(1)}, u32[]{:S(2)}, u32[]{:S(2)}) collective-permute-start(bf16[1,256,1024]{2,1,0:T(8,128)(2,1)} %bitcast.10.refs_4_), channel_id=1, source_target_pairs={{0,1},{1,0},{2,3},{3,2},{4,5},{5,4},{6,7},{7,6},{8,9},{9,8},{10,11... | collective-permute-start | bytes 1572872 | tf_op jit(solution)/shard_map/ppermute | solution.py:329
  104.6 2.9 %collective-permute-start.23 = (bf16[1,256,1024]{2,1,0:T(8,128)(2,1)}, bf16[1,256,1024]{2,1,0:T(8,128)(2,1)S(1)}, u32[]{:S(2)}, u32[]{:S(2)}) collective-permute-start(bf16[1,256,1024]{2,1,0:T(8,128)(2,1)} %bitcast.11.refs_6_), channel_id=1, source_target_pairs={{0,1},{1,0},{2,3},{3,2},{4,5},{5,4},{6,7},{7,6},{8,9},{9,8},{10,11... | collective-permute-start | bytes 1572872 | tf_op jit(solution)/shard_map/ppermute | solution.py:329
  (8 other events, 117.6 us)

commit v15 on v14

--- a/solution.py
+++ b/solution.py
@@ -23,7 +23,11 @@
     return lax.axis_index("col") == 0
 
 
-def faces_kernel(bold_ref, *refs):
+def plane_of(layer, y, frames):
+    return layer[y] if len(layer.shape) == 3 else layer[y * frames : (y + 1) * frames]
+
+
+def faces_kernel(bold_ref, gm_ref, *refs):
     windows, frames, slab_x, slab_y, slab_z = bold_ref.shape
     per_frame = slab_x * slab_y
     wide = refs[-1]
@@ -35,10 +39,16 @@
             taken = wide[pl.ds(x * slab_y + y, frames, stride=per_frame), :]
             return taken.astype(jnp.bfloat16)
 
+        def store(layer_ref, y, value):
+            if len(layer_ref.shape) == 3:
+                layer_ref[y] = value
+            else:
+                layer_ref[y * frames : (y + 1) * frames] = value
+
         def layers(first_ref, last_ref):
             for y in range(slab_y):
-                first_ref[y] = plane(0, y)
-                last_ref[y] = plane(1, y)
+                store(first_ref, y, plane(0, y))
+                store(last_ref, y, plane(1, y))
 
         pl.when(is_even())(functools.partial(layers, outer_ref, near_ref))
         pl.when(~is_even())(functools.partial(layers, near_ref, outer_ref))
@@ -47,26 +57,35 @@
             for x in range(slab_x):
                 edge_ref[x] = plane(x, y)
 
+        if len(near_ref.shape) == 2:
+            number = gm_ref[...] + 1
+            parts = jnp.concatenate([lax.shift_right_logical(number, 6), number & 63], axis=0)
+            near_ref[slab_y * frames :] = parts.astype(jnp.float32).astype(jnp.bfloat16)
+
         pl.when(is_first())(functools.partial(edges, slab_y - 1))
         pl.when(~is_first())(functools.partial(edges, 0))
 
 
-def make_faces(bold):
+def make_faces(bold, gm):
     windows, frames, slab_x, slab_y, slab_z = bold.shape
     layer = jax.ShapeDtypeStruct((slab_y, frames, slab_z), jnp.bfloat16)
     edge = jax.ShapeDtypeStruct((slab_x, frames, slab_z), jnp.bfloat16)
+    with_gm = jax.ShapeDtypeStruct(
+        (slab_y * frames + 2 * gm.shape[0], slab_z), jnp.bfloat16
+    )
+    outs = [with_gm, layer, edge] + [layer, layer, edge] * (windows - 1)
     whole = lambda array: pl.BlockSpec(array.shape, lambda _: (0,) * len(array.shape))
     return pl.pallas_call(
         faces_kernel,
         grid=(1,),
-        in_specs=[whole(bold)],
-        out_specs=[whole(layer), whole(layer), whole(edge)] * windows,
-        out_shape=[layer, layer, edge] * windows,
+        in_specs=[whole(bold), whole(gm)],
+        out_specs=[whole(value) for value in outs],
+        out_shape=outs,
         scratch_shapes=[pltpu.VMEM((frames * slab_x * slab_y, slab_z), jnp.float32)],
         compiler_params=pltpu.CompilerParams(vmem_limit_bytes=VMEM_BYTES),
         cost_estimate=SMALL,
         name="faces",
-    )(bold)
+    )(bold, gm)
 
 
 def three_taps(before, here, after):
@@ -93,25 +112,24 @@
     return (centred * lax.rsqrt((spread + 1e-05) * frames)).astype(jnp.bfloat16)
 
 
-def pick(parts, gm_ref, out_ref):
+def pick(parts, gm, out_ref):
     voxels = parts[0].shape[1]
-    rows = gm_ref.shape[1]
-    step = 2 * BLOCK
-    for start in range(0, rows, step):
-        wanted = gm_ref[:, start : start + step]
-        voxel = lax.broadcasted_iota(jnp.int32, (voxels, step), 0)
+    for line in range(0, gm.shape[0], 2):
+        wanted = jnp.concatenate([gm[line : line + 1], gm[line + 1 : line + 2]], axis=1)
+        voxel = lax.broadcasted_iota(jnp.int32, (voxels, 2 * BLOCK), 0)
         chosen = jnp.where(voxel == wanted, 1.0, 0.0).astype(jnp.bfloat16)
         total = jnp.dot(parts[0][...], chosen, preferred_element_type=jnp.float32)
         for part in parts[1:]:
             total += jnp.dot(part[...], chosen, preferred_element_type=jnp.float32)
-        out_ref[:, start : start + step] = total.astype(out_ref.dtype)
+        start = line * BLOCK
+        out_ref[:, start : start + 2 * BLOCK] = total.astype(out_ref.dtype)
 
 
 def panel_kernel(
     near_ref, outer_ref, facing_ref, across_ref, edge_ref, corner_ref, gm_ref, out_ref,
     planes, scored,
 ):
-    slab_y, frames, slab_z = near_ref.shape
+    slab_y, frames, slab_z = outer_ref.shape
     even = is_even()
 
     def along_x(across, outer, near, facing):
@@ -121,7 +139,10 @@
 
     for y in range(slab_y):
         planes[0, y + 1], planes[1, y + 1] = along_x(
-            across_ref[y], outer_ref[y], near_ref[y], facing_ref[y]
+            across_ref[y],
+            outer_ref[y],
+            plane_of(near_ref, y, frames),
+            plane_of(facing_ref, y, frames),
         )
     outer = jnp.where(even, edge_ref[0], edge_ref[1])
     near = jnp.where(even, edge_ref[1], edge_ref[0])
@@ -132,7 +153,7 @@
             part = three_taps(planes[x, y], planes[x, y + 1], planes[x, y + 2])
             start = (x * slab_y + y) * slab_z
             scored[:, start : start + slab_z] = standardise(along_z(part))
-    pick([scored], gm_ref, out_ref)
+    pick([scored], gm_ref[...], out_ref)
 
 
 def inner_kernel(
@@ -161,7 +182,7 @@
                 rounded = part.astype(jnp.bfloat16)
                 term[:, start : start + slab_z] = rounded
                 part = part - rounded.astype(jnp.float32)
-    pick([high, middle, low], gm_ref, out_ref)
+    pick([high, middle, low], gm_ref[...], out_ref)
 
 
 def halo_kernel(
@@ -177,14 +198,16 @@
     for y in range(slab_y):
         planes[0, y + 1], planes[1, y + 1] = sides(near_ref[y], beyond_ref[y])
     own = jnp.where(even, edge_ref[1], edge_ref[0])
-    for x, edge in enumerate(sides(own, corner_ref[...])):
+    for x, edge in enumerate(sides(own, corner_ref[2])):
         place_edge(planes, x, edge)
     for x in range(2):
         for y in range(slab_y):
             part = three_taps(planes[x, y], planes[x, y + 1], planes[x, y + 2])
             start = (x * slab_y + y) * slab_z
             scored[:, start : start + slab_z] = along_z(part).astype(jnp.bfloat16)
-    pick([scored], gm_ref, out_ref)
+    lines = gm_ref.shape[0] // 2
+    number = gm_ref[...].astype(jnp.float32).astype(jnp.int32)
+    pick([scored], number[:lines] * 64 + number[lines:] - 1, out_ref)
 
 
 def join_kernel(inner_ref, halo_ref, out_ref):
@@ -194,8 +217,7 @@
         out_ref[:, span] = standardise(smooth)
 
 
-def call_on_rows(kernel, dtype, frames, operands, scratch, name):
-    rows = operands[-1].shape[1]
+def call_on_rows(kernel, dtype, frames, rows, operands, scratch, name):
     whole = lambda array: pl.BlockSpec(array.shape, lambda _: (0,) * array.ndim)
     return pl.pallas_call(
         kernel,
@@ -218,9 +240,9 @@
 
 def make_panel(near, outer, facing, across, edge, corner, gm):
     operands = (near, outer, facing, across, edge, corner, gm)
-    scratch = blur_scratch(near, 1)
+    scratch = blur_scratch(outer, 1)
     return call_on_rows(
-        panel_kernel, jnp.bfloat16, near.shape[1], operands, scratch, "blur_score_pick"
+        panel_kernel, jnp.bfloat16, outer.shape[1], gm.size, operands, scratch, "blur_score_pick"
     )
 
 
@@ -228,7 +250,7 @@
     operands = (near, outer, edge, gm)
     scratch = blur_scratch(near, 3)
     return call_on_rows(
-        inner_kernel, jnp.float32, near.shape[1], operands, scratch, "inner_blur"
+        inner_kernel, jnp.float32, near.shape[1], gm.size, operands, scratch, "inner_blur"
     )
 
 
@@ -236,13 +258,13 @@
     operands = (near, beyond, edge, corner, gm)
     scratch = blur_scratch(near, 1)
     return call_on_rows(
-        halo_kernel, jnp.bfloat16, near.shape[1], operands, scratch, "halo_blur"
+        halo_kernel, jnp.bfloat16, near.shape[1], gm.size // 2, operands, scratch, "halo_blur"
     )
 
 
 def join(inner, halo):
     return call_on_rows(
-        join_kernel, jnp.bfloat16, inner.shape[0], (inner, halo), [], "join_score"
+        join_kernel, jnp.bfloat16, *inner.shape, (inner, halo), [], "join_score"
     )
 
 
@@ -336,7 +358,7 @@
     across_pairs = [(i, target) for i, target in across_pairs if 0 <= target < row_total]
     in_pair = [(i, i ^ 1) for i in range(row_total)]
 
-    gm = gm_index.reshape(1, -1)
+    gm = gm_index.reshape(-1, BLOCK)
     blocks, slots = partners.shape
     ids = jnp.maximum(partners, 0)
     slab = ids // blocks
@@ -360,23 +382,29 @@
         return [near, other_col(near)]
 
     windows = bold.shape[0]
-    gm_pair = lax.ppermute(gm, "row", in_pair)
+    frames, slab_y = bold.shape[1], bold.shape[3]
 
     def ends(*layers):
-        return other_col(jnp.stack([jnp.where(col == 0, layer[-1], layer[0]) for layer in layers], 0))
-
-    near_0, outer_0, face_0, near_1, outer_1, face_1 = make_faces(bold)
+        planes = [
+            jnp.where(col == 0, plane_of(layer, slab_y - 1, frames), plane_of(layer, 0, frames))
+            for layer in layers
+        ]
+        return other_col(jnp.stack(planes, 0))
+
+    near_0, outer_0, face_0, near_1, outer_1, face_1 = make_faces(bold, gm)
+    facing_0 = lax.ppermute(near_0, "row", in_pair)
+    across_0 = lax.ppermute(outer_0, "row", across_pairs)
     beyond_1 = lax.ppermute(outer_1, "row", two_on)
-    facing_0 = lax.ppermute(after(near_0, gm_pair), "row", in_pair)
-    across_0 = lax.ppermute(after(outer_0, gm_pair), "row", across_pairs)
     edge_0, edge_1 = other_col(face_0), other_col(face_1)
     inner_1 = make_inner(near_1, outer_1, edge_1, after(gm, edge_0))
-    beyond_1 = after(beyond_1, inner_1)
-    given_1 = make_halo(near_1, beyond_1, edge_1, ends(beyond_1)[0], gm_pair)
-    facing_0, across_0 = after(facing_0, given_1), after(across_0, given_1)
-    halo_1 = lax.ppermute(after(given_1, facing_0, across_0), "row", in_pair)
-    corner_0 = ends(across_0, facing_0)
-    own_0 = make_panel(near_0, outer_0, facing_0, across_0, edge_0, corner_0, gm)
+    facing_0, across_0 = after(facing_0, inner_1), after(across_0, inner_1)
+    beyond_1 = after(beyond_1, facing_0, across_0)
+    gm_pair = facing_0[slab_y * frames :]
+    corner = ends(across_0, facing_0, beyond_1)
+    given_1 = make_halo(near_1, beyond_1, edge_1, corner, gm_pair)
+    halo_1 = lax.ppermute(given_1, "row", in_pair)
+    corner = after(corner, given_1)
+    own_0 = make_panel(near_0, outer_0, facing_0, across_0, edge_0, corner, gm)
     ahead_0 = lax.ppermute(own_0, "row", ahead)
     halo_1 = after(halo_1, own_0)
     own_1 = join(inner_1, halo_1)

time: 114 us -> 116 us (1.018)
  waiting for transfers between devices: 47.6 us -> 57 us
  starting transfers between devices: 29.1 us -> 21.9 us
  Pallas kernels: 29.9 us -> 28.3 us
  local copies, waits for them, and re-layouts: 5.16 us -> 6.54 us
    ppermute x4 -> x3, starting transfers between devices: 12.8 us -> 4.45 us  [the longest x1 2.99 us: on_device(): facing_0 = lax.ppermute(near_0, 'row', in_pair)]
    ppermute x1, waiting for transfers between devices: 0.99 us -> 5.62 us  [on_device(): pair_0 = lax.ppermute(after(own_0, halo_1), 'row', in_pair)]
    ppermute x4 -> x3, waiting for transfers between devices: 12.2 us -> 16.5 us  [the longest x1 12.8 us: on_device(): facing_0 = lax.ppermute(near_0, 'row', in_pair)]
    ppermute x1, waiting for transfers between devices: 0.01 us -> 4.1 us  [on_device(): beyond_1 = lax.ppermute(outer_1, 'row', two_on)]
    ppermute x1, starting transfers between devices: 2.24 us -> 4.56 us  [on_device(): ahead_0 = lax.ppermute(own_0, 'row', ahead)]
    ppermute x1, starting transfers between devices: 2.15 us -> 0.2 us  [on_device(): rest_0 = lax.ppermute(ahead_0, 'row', in_pair)]
    ppermute x1, waiting for transfers between devices: 3.88 us -> 1.93 us  [on_device(): ahead_0 = lax.ppermute(own_0, 'row', ahead)]
    unnamed x16 -> x22, local copies, waits for them, and re-layouts: 5.16 us -> 6.54 us
  transfers between devices with their start and end apart: 24 -> 22, of which waited for: 14 -> 12; matrix products, arithmetic and copies ran while one was open for 1% -> 1% of each run, Pallas kernels for 18% -> 15%
where the time goes in v15:
time: 116 us
  waiting for transfers between devices  57 us (49%)
  Pallas kernels  28.3 us (24%)
  starting transfers between devices  21.9 us (19%)
  local copies, waits for them, and re-layouts  6.54 us (6%)
  other arithmetic  1.6 us (1%)
    pallas_call x4, Pallas kernels, call_on_rows(): pl.pallas_call(kernel, grid=(1,), in_specs=[whole(value) for value in ope...  13.2 us
    ppermute x1, waiting for transfers between devices, on_device(): facing_0 = lax.ppermute(near_0, 'row', in_pair)  12.8 us
    pallas_call x2, Pallas kernels, make_tiles(): pl.pallas_call(functools.partial(tiles_kernel, sources=count, window=wind...  12.1 us
    ppermute x1, waiting for transfers between devices, on_device(): pair_1 = lax.ppermute(own_1, 'row', in_pair)  11.2 us
    ppermute x1, waiting for transfers between devices, on_device(): rest_0 = lax.ppermute(ahead_0, 'row', in_pair)  9.51 us
    unnamed x22, local copies, waits for them, and re-layouts  6.54 us
    ppermute x1, waiting for transfers between devices, on_device(): pair_0 = lax.ppermute(after(own_0, halo_1), 'row', in_pair)  5.62 us
    ppermute x10, waiting for transfers between devices, other_col(): return lax.ppermute(value, 'col', [(0, 1), (1, 0)])  4.83 us
  transfers between devices with their start and end apart: 22, of which 12 were waited for; matrix products, arithmetic and copies ran while one was open for 1% of the time, Pallas kernels for 15%

profile of v15, /device:TPU:0, one launch (start us, length us, event | category | flops | bytes accessed | tf_op | source)
XLA Modules:
  0.0 115.7 jit_solution(9148284779747658675)
XLA Ops:
  0.0 1.6 %copy-done = bf16[2,256,2,8,128]{4,3,2,1,0:T(8,128)(2,1)S(1)} copy-done((bf16[2,256,2,8,128]{4,3,2,1,0:T(8,128)(2,1)S(1)}, bf16[2,256,2,8,128]{4,3,2,1,0:T(8,128)(2,1)}, u32[]{:S(2)}) %copy-start) | copy-done | bytes 2097176
  2.3 3.0 %faces.1 = (bf16[2064,128]{1,0:T(8,128)(2,1)S(1)}, bf16[8,256,128]{2,1,0:T(8,128)(2,1)}, bf16[2,256,128]{2,1,0:T(8,128)(2,1)}, bf16[8,256,128]{2,1,0:T(8,128)(2,...) custom-call(bf16[2,256,2,8,128]{4,3,2,1,0:T(8,128)(2,1)S(1)} %copy-done, s32[8,128]{1,0:T(8,128)S(1)} %bitcast.18), custom_call_target="tpu_custom_call" | custom-call | flops 1 | bytes 1 | tf_op jit(solution)/shard_map/faces/pallas_call | solution.py:78
  5.3 3.0 %collective-permute-start.3 = (bf16[2064,128]{1,0:T(8,128)(2,1)S(1)}, bf16[2064,128]{1,0:T(8,128)(2,1)S(1)}, u32[]{:S(2)}, u32[]{:S(2)}) collective-permute-start(bf16[2064,128]{1,0:T(8,128)(2,1)S(1)} %get-tuple-element.34.near_ref), channel_id=1, source_target_pairs={{0,2},{2,0},{4,6},{6,4},{8,10},{10,8},{12,14},{14,12},{1,3},{3,1},... | collective-permute-start | bytes 1585160 | tf_op jit(solution)/shard_map/ppermute | solution.py:395
  9.0 1.5 %collective-permute-start.2 = (bf16[8,256,128]{2,1,0:T(8,128)(2,1)S(1)}, bf16[8,256,128]{2,1,0:T(8,128)(2,1)S(1)}, u32[]{:S(2)}, u32[]{:S(2)}) collective-permute-start(bf16[8,256,128]{2,1,0:T(8,128)(2,1)S(1)} %get-tuple-element.30.outer_ref), channel_id=1, source_target_pairs={{2,6},{4,0},{6,10},{8,4},{10,14},{12,8},{3,7},{5,1},{7,11},{9,5},{... | collective-permute-start | bytes 1572872 | tf_op jit(solution)/shard_map/ppermute | solution.py:397
  12.8 5.2 %inner_blur.1.inner_ref = f32[256,1024]{1,0:T(8,128)S(1)} custom-call(bf16[8,256,128]{2,1,0:T(8,128)(2,1)S(1)} %get-tuple-element.29.near_ref, bf16[8,256,128]{2,1,0:T(8,128)(2,1)S(1)} %get-tuple-element.30.outer_ref, bf16[2,256,128]{2,1,0:T(8,128)(2,1)S(1)} %collective-permute-done.edge_ref, s32[8,128]{1,0:T(8,128)S(1)} %bitcast.19), custom_call_target="tpu_custom_call" | custom-call | flops 1 | bytes 1 | tf_op jit(solution)/shard_map/inner_blur/pallas_call | solution.py:222
  18.0 12.8 %collective-permute-done.3.facing_ref = bf16[2064,128]{1,0:T(8,128)(2,1)S(1)} collective-permute-done((bf16[2064,128]{1,0:T(8,128)(2,1)S(1)}, bf16[2064,128]{1,0:T(8,128)(2,1)S(1)}, u32[]{:S(2)}, u32[]{:S(2)}) %collective-permute-start.3) | collective-permute-done | bytes 528416 | tf_op jit(solution)/shard_map/ppermute | solution.py:395
  30.8 4.1 %collective-permute-done.2.beyond_ref = bf16[8,256,128]{2,1,0:T(8,128)(2,1)S(1)} collective-permute-done((bf16[8,256,128]{2,1,0:T(8,128)(2,1)S(1)}, bf16[8,256,128]{2,1,0:T(8,128)(2,1)S(1)}, u32[]{:S(2)}, u32[]{:S(2)}) %collective-permute-start.2) | collective-permute-done | bytes 524320 | tf_op jit(solution)/shard_map/ppermute | solution.py:397
  35.1 1.4 %collective-permute-done.5.corner_ref = bf16[3,256,128]{2,1,0:T(8,128)(2,1)S(1)} collective-permute-done((bf16[3,256,128]{2,1,0:T(8,128)(2,1)S(1)}, bf16[3,256,128]{2,1,0:T(8,128)(2,1)S(1)}, u32[]{:S(2)}, u32[]{:S(2)}) %collective-permute-start.5) | collective-permute-done | bytes 196640 | tf_op jit(solution)/shard_map/ppermute | solution.py:351
  36.5 2.4 %halo_blur.1 = bf16[256,1024]{1,0:T(8,128)(2,1)S(1)} custom-call(bf16[8,256,128]{2,1,0:T(8,128)(2,1)S(1)} %get-tuple-element.29.near_ref, bf16[8,256,128]{2,1,0:T(8,128)(2,1)S(1)} %collective-permute-done.2.beyond_ref, bf16[2,256,128]{2,1,0:T(8,128)(2,1)S(1)} %collective-permute-done.edge_ref, bf16[3,256,128]{2,1,0:T(8,128)(2,1)S(1)} %collective-permute-done.5.corner_ref, ...), custom_call_target="tpu_custom_call" | custom-call | flops 1 | bytes 1 | tf_op jit(solution)/shard_map/halo_blur/pallas_call | solution.py:222
  40.3 4.4 %blur_score_pick.1 = bf16[256,1024]{1,0:T(8,128)(2,1)S(1)} custom-call(bf16[2064,128]{1,0:T(8,128)(2,1)S(1)} %get-tuple-element.34.near_ref, bf16[8,256,128]{2,1,0:T(8,128)(2,1)} %get-tuple-element.36.outer_ref, bf16[2064,128]{1,0:T(8,128)(2,1)S(1)} %collective-permute-done.3.facing_ref, bf16[8,256,128]{2,1,0:T(8,128)(2,1)S(1)} %collective-permute-done.4.across_ref, ...), custom_call_target="tpu_custom_call" | custom-call | flops 1 | bytes 1 | tf_op jit(solution)/shard_map/blur_score_pick/pallas_call | solution.py:222
  44.7 4.6 %collective-permute-start.10 = (bf16[256,1024]{1,0:T(8,128)(2,1)S(1)}, bf16[256,1024]{1,0:T(8,128)(2,1)S(1)}, u32[]{:S(2)}, u32[]{:S(2)}) collective-permute-start(bf16[256,1024]{1,0:T(8,128)(2,1)S(1)} %blur_score_pick.1), channel_id=1, source_target_pairs={{4,0},{14,2},{8,4},{2,6},{12,8},{6,10},{0,12},{10,14},{5,1},{15,3}... | collective-permute-start | bytes 1572872 | tf_op jit(solution)/shard_map/ppermute | solution.py:408
  49.3 3.6 %collective-permute-done.6.halo_ref = bf16[256,1024]{1,0:T(8,128)(2,1)S(1)} collective-permute-done((bf16[256,1024]{1,0:T(8,128)(2,1)S(1)}, bf16[256,1024]{1,0:T(8,128)(2,1)S(1)}, u32[]{:S(2)}, u32[]{:S(2)}) %collective-permute-start.6) | collective-permute-done | bytes 524320 | tf_op jit(solution)/shard_map/ppermute | solution.py:405
  54.9 1.3 %collective-permute-start.8 = (bf16[256,1024]{1,0:T(8,128)(2,1)}, bf16[256,1024]{1,0:T(8,128)(2,1)S(1)}, u32[]{:S(2)}, u32[]{:S(2)}) collective-permute-start(bf16[256,1024]{1,0:T(8,128)(2,1)} %join_score.1), channel_id=1, source_target_pairs={{0,2},{2,0},{4,6},{6,4},{8,10},{10,8},{12,14},{14,12},{1,3},{3,1},... | collective-permute-start | bytes 1572872 | tf_op jit(solution)/shard_map/ppermute | solution.py:412
  56.2 3.5 %collective-permute-start.7 = (bf16[256,1024]{1,0:T(8,128)(2,1)}, bf16[256,1024]{1,0:T(8,128)(2,1)}, u32[]{:S(2)}, u32[]{:S(2)}) collective-permute-start(bf16[256,1024]{1,0:T(8,128)(2,1)} %join_score.1), channel_id=1, source_target_pairs={{4,0},{14,2},{8,4},{2,6},{12,8},{6,10},{0,12},{10,14},{5,1},{15,3}... | collective-permute-start | bytes 1572872 | tf_op jit(solution)/shard_map/ppermute | solution.py:413
  59.7 1.9 %collective-permute-done.10 = bf16[256,1024]{1,0:T(8,128)(2,1)S(1)} collective-permute-done((bf16[256,1024]{1,0:T(8,128)(2,1)S(1)}, bf16[256,1024]{1,0:T(8,128)(2,1)S(1)}, u32[]{:S(2)}, u32[]{:S(2)}) %collective-permute-start.10) | collective-permute-done | bytes 524320 | tf_op jit(solution)/shard_map/ppermute | solution.py:408
  62.1 5.6 %collective-permute-done.9 = bf16[256,1024]{1,0:T(8,128)(2,1)S(1)} collective-permute-done((bf16[256,1024]{1,0:T(8,128)(2,1)S(1)}, bf16[256,1024]{1,0:T(8,128)(2,1)S(1)}, u32[]{:S(2)}, u32[]{:S(2)}) %collective-permute-start.9) | collective-permute-done | bytes 524320 | tf_op jit(solution)/shard_map/ppermute | solution.py:411
  67.8 11.2 %collective-permute-done.8 = bf16[256,1024]{1,0:T(8,128)(2,1)S(1)} collective-permute-done((bf16[256,1024]{1,0:T(8,128)(2,1)}, bf16[256,1024]{1,0:T(8,128)(2,1)S(1)}, u32[]{:S(2)}, u32[]{:S(2)}) %collective-permute-start.8) | collective-permute-done | bytes 524320 | tf_op jit(solution)/shard_map/ppermute | solution.py:412
  79.0 9.5 %collective-permute-done.13 = bf16[256,1024]{1,0:T(8,128)(2,1)S(1)} collective-permute-done((bf16[256,1024]{1,0:T(8,128)(2,1)S(1)}, bf16[256,1024]{1,0:T(8,128)(2,1)S(1)}, u32[]{:S(2)}, u32[]{:S(2)}) %collective-permute-start.13) | collective-permute-done | bytes 524320 | tf_op jit(solution)/shard_map/ppermute | solution.py:416
  89.9 2.5 %collective-permute-start.20 = (bf16[256,1024]{1,0:T(8,128)(2,1)}, bf16[256,1024]{1,0:T(8,128)(2,1)}, u32[]{:S(2)}, u32[]{:S(2)}) collective-permute-start(bf16[256,1024]{1,0:T(8,128)(2,1)} %join_score.1), channel_id=1, source_target_pairs={{0,4},{2,14},{4,8},{6,2},{8,12},{10,6},{12,0},{14,10},{1,5},{3,15}... | collective-permute-start | bytes 1572872 | tf_op jit(solution)/shard_map/ppermute | solution.py:423
  92.4 1.3 %pad_maximum_fusion.refs_0_ = bf16[2,256,1024]{2,1,0:T(8,128)(2,1)S(1)} fusion(bf16[1,256,1024]{2,1,0:T(8,128)(2,1)} %bitcast.3, bf16[1,256,1024]{2,1,0:T(8,128)(2,1)} %bitcast.2), kind=kLoop, calls=%fused_computation | loop fusion | flops 524288 | bytes 2097152 | tf_op jit(solution)/shard_map/stack | solution.py:381
  97.3 6.0 %tiles.2.refs_8_ = bf16[8,16,2,128,128]{4,3,2,1,0:T(8,128)(2,1)} custom-call(s32[8,16]{1,0:T(8,128)S(1)} %get-tuple-element.53.place_ref, s32[8,16]{1,0:T(8,128)S(1)} %fusion.21.present_ref, bf16[2,256,1024]{2,1,0:T(8,128)(2,1)S(1)} %pad_maximum_fusion.1.refs_0_, bf16[2,256,1024]{2,1,0:T(8,128)(2,1)} %collective-permute-done.15.refs_1_, ...), custom_call_target="tpu_custom_call" | custom-call | flops 1 | bytes 1 | tf_op jit(solution)/shard_map/tiles/pallas_call | solution.py:317
  103.3 3.3 %collective-permute-done.20 = bf16[256,1024]{1,0:T(8,128)(2,1)} collective-permute-done((bf16[256,1024]{1,0:T(8,128)(2,1)}, bf16[256,1024]{1,0:T(8,128)(2,1)}, u32[]{:S(2)}, u32[]{:S(2)}) %collective-permute-start.20) | collective-permute-done | bytes 524320 | tf_op jit(solution)/shard_map/ppermute | solution.py:423
  107.1 1.6 %collective-permute-done.19.refs_5_ = bf16[1,256,1024]{2,1,0:T(8,128)(2,1)S(1)} collective-permute-done((bf16[1,256,1024]{2,1,0:T(8,128)(2,1)}, bf16[1,256,1024]{2,1,0:T(8,128)(2,1)S(1)}, u32[]{:S(2)}, u32[]{:S(2)}) %collective-permute-start.19) | collective-permute-done | bytes 524320 | tf_op jit(solution)/shard_map/ppermute | solution.py:351
  109.5 6.0 %tiles.3 = bf16[8,16,2,128,128]{4,3,2,1,0:T(8,128)(2,1)} custom-call(s32[8,16]{1,0:T(8,128)S(1)} %get-tuple-element.54.place_ref, s32[8,16]{1,0:T(8,128)S(1)} %fusion.21.present_ref, bf16[2,256,1024]{2,1,0:T(8,128)(2,1)S(1)} %pad_maximum_fusion.refs_0_, bf16[2,256,1024]{2,1,0:T(8,128)(2,1)} %collective-permute-done.11.refs_1_, ...), custom_call_target="tpu_custom_call", output_to_operand_aliasing={{}: (10, {})} | custom-call | flops 1 | bytes 1 | tf_op jit(solution)/shard_map/tiles/pallas_call | solution.py:317
  (58 shorter events, 14.0 us)
Async XLA Ops:
  5.3 89.2 %copy-start.10 = (s32[8,16]{1,0:T(8,128)S(1)}, s32[8,16]{1,0:T(8,128)}, u32[]{:S(2)}) copy-start(s32[8,16]{1,0:T(8,128)} %param.5) | copy-start | bytes 1540
  5.3 25.5 %collective-permute-start.3 = (bf16[2064,128]{1,0:T(8,128)(2,1)S(1)}, bf16[2064,128]{1,0:T(8,128)(2,1)S(1)}, u32[]{:S(2)}, u32[]{:S(2)}) collective-permute-start(bf16[2064,128]{1,0:T(8,128)(2,1)S(1)} %get-tuple-element.34.near_ref), channel_id=1, source_target_pairs={{0,2},{2,0},{4,6},{6,4},{8,10},{10,8},{12,14},{14,12},{1,3},{3,1},... | collective-permute-start | bytes 1585160 | tf_op jit(solution)/shard_map/ppermute | solution.py:395
  8.3 9.7 %collective-permute-start.4 = (bf16[8,256,128]{2,1,0:T(8,128)(2,1)}, bf16[8,256,128]{2,1,0:T(8,128)(2,1)S(1)}, u32[]{:S(2)}, u32[]{:S(2)}) collective-permute-start(bf16[8,256,128]{2,1,0:T(8,128)(2,1)} %get-tuple-element.36.outer_ref), channel_id=1, source_target_pairs={{2,4},{4,2},{6,8},{8,6},{10,12},{12,10},{3,5},{5,3},{7,9},{9,7},{1... | collective-permute-start | bytes 1572872 | tf_op jit(solution)/shard_map/ppermute | solution.py:396
  9.0 25.9 %collective-permute-start.2 = (bf16[8,256,128]{2,1,0:T(8,128)(2,1)S(1)}, bf16[8,256,128]{2,1,0:T(8,128)(2,1)S(1)}, u32[]{:S(2)}, u32[]{:S(2)}) collective-permute-start(bf16[8,256,128]{2,1,0:T(8,128)(2,1)S(1)} %get-tuple-element.30.outer_ref), channel_id=1, source_target_pairs={{2,6},{4,0},{6,10},{8,4},{10,14},{12,8},{3,7},{5,1},{7,11},{9,5},{... | collective-permute-start | bytes 1572872 | tf_op jit(solution)/shard_map/ppermute | solution.py:397
  10.5 1.6 %collective-permute-start.1 = (bf16[2,256,128]{2,1,0:T(8,128)(2,1)}, bf16[2,256,128]{2,1,0:T(8,128)(2,1)S(1)}, u32[]{:S(2)}, u32[]{:S(2)}) collective-permute-start(bf16[2,256,128]{2,1,0:T(8,128)(2,1)} %get-tuple-element.32), channel_id=1, source_target_pairs={{0,1},{1,0},{2,3},{3,2},{4,5},{5,4},{6,7},{7,6},{8,9},{9,8},{10,11... | collective-permute-start | bytes 393224 | tf_op jit(solution)/shard_map/ppermute | solution.py:351
  10.6 1.5 %collective-permute-start = (bf16[2,256,128]{2,1,0:T(8,128)(2,1)S(1)}, bf16[2,256,128]{2,1,0:T(8,128)(2,1)S(1)}, u32[]{:S(2)}, u32[]{:S(2)}) collective-permute-start(bf16[2,256,128]{2,1,0:T(8,128)(2,1)S(1)} %get-tuple-element.31), channel_id=1, source_target_pairs={{0,1},{1,0},{2,3},{3,2},{4,5},{5,4},{6,7},{7,6},{8,9},{9,8},{10,11... | collective-permute-start | bytes 393224 | tf_op jit(solution)/shard_map/ppermute | solution.py:351
  35.0 1.5 %collective-permute-start.5 = (bf16[3,256,128]{2,1,0:T(8,128)(2,1)S(1)}, bf16[3,256,128]{2,1,0:T(8,128)(2,1)S(1)}, u32[]{:S(2)}, u32[]{:S(2)}) collective-permute-start(bf16[3,256,128]{2,1,0:T(8,128)(2,1)S(1)} %pad_maximum_fusion.3), channel_id=1, source_target_pairs={{0,1},{1,0},{2,3},{3,2},{4,5},{5,4},{6,7},{7,6},{8,9},{9,8},{10,11... | collective-permute-start | bytes 589832 | tf_op jit(solution)/shard_map/ppermute | solution.py:351
  38.9 14.0 %collective-permute-start.6 = (bf16[256,1024]{1,0:T(8,128)(2,1)S(1)}, bf16[256,1024]{1,0:T(8,128)(2,1)S(1)}, u32[]{:S(2)}, u32[]{:S(2)}) collective-permute-start(bf16[256,1024]{1,0:T(8,128)(2,1)S(1)} %halo_blur.1), channel_id=1, source_target_pairs={{0,2},{2,0},{4,6},{6,4},{8,10},{10,8},{12,14},{14,12},{1,3},{3,1},... | collective-permute-start | bytes 1572872 | tf_op jit(solution)/shard_map/ppermute | solution.py:405
  44.7 16.9 %collective-permute-start.10 = (bf16[256,1024]{1,0:T(8,128)(2,1)S(1)}, bf16[256,1024]{1,0:T(8,128)(2,1)S(1)}, u32[]{:S(2)}, u32[]{:S(2)}) collective-permute-start(bf16[256,1024]{1,0:T(8,128)(2,1)S(1)} %blur_score_pick.1), channel_id=1, source_target_pairs={{4,0},{14,2},{8,4},{2,6},{12,8},{6,10},{0,12},{10,14},{5,1},{15,3}... | collective-permute-start | bytes 1572872 | tf_op jit(solution)/shard_map/ppermute | solution.py:408
  52.9 14.9 %collective-permute-start.9 = (bf16[256,1024]{1,0:T(8,128)(2,1)S(1)}, bf16[256,1024]{1,0:T(8,128)(2,1)S(1)}, u32[]{:S(2)}, u32[]{:S(2)}) collective-permute-start(bf16[256,1024]{1,0:T(8,128)(2,1)S(1)} %blur_score_pick.1), channel_id=1, source_target_pairs={{0,2},{2,0},{4,6},{6,4},{8,10},{10,8},{12,14},{14,12},{1,3},{3,1},... | collective-permute-start | bytes 1572872 | tf_op jit(solution)/shard_map/ppermute | solution.py:411
  54.9 24.1 %collective-permute-start.8 = (bf16[256,1024]{1,0:T(8,128)(2,1)}, bf16[256,1024]{1,0:T(8,128)(2,1)S(1)}, u32[]{:S(2)}, u32[]{:S(2)}) collective-permute-start(bf16[256,1024]{1,0:T(8,128)(2,1)} %join_score.1), channel_id=1, source_target_pairs={{0,2},{2,0},{4,6},{6,4},{8,10},{10,8},{12,14},{14,12},{1,3},{3,1},... | collective-permute-start | bytes 1572872 | tf_op jit(solution)/shard_map/ppermute | solution.py:412
  56.2 22.8 %collective-permute-start.7 = (bf16[256,1024]{1,0:T(8,128)(2,1)}, bf16[256,1024]{1,0:T(8,128)(2,1)}, u32[]{:S(2)}, u32[]{:S(2)}) collective-permute-start(bf16[256,1024]{1,0:T(8,128)(2,1)} %join_score.1), channel_id=1, source_target_pairs={{4,0},{14,2},{8,4},{2,6},{12,8},{6,10},{0,12},{10,14},{5,1},{15,3}... | collective-permute-start | bytes 1572872 | tf_op jit(solution)/shard_map/ppermute | solution.py:413
  61.6 26.9 %collective-permute-start.13 = (bf16[256,1024]{1,0:T(8,128)(2,1)S(1)}, bf16[256,1024]{1,0:T(8,128)(2,1)S(1)}, u32[]{:S(2)}, u32[]{:S(2)}) collective-permute-start(bf16[256,1024]{1,0:T(8,128)(2,1)S(1)} %collective-permute-done.10), channel_id=1, source_target_pairs={{0,2},{2,0},{4,6},{6,4},{8,10},{10,8},{12,14},{14,12},{1,3},{3,1},... | collective-permute-start | bytes 1572872 | tf_op jit(solution)/shard_map/ppermute | solution.py:416
  61.8 26.7 %collective-permute-start.16 = (bf16[256,1024]{1,0:T(8,128)(2,1)S(1)}, bf16[256,1024]{1,0:T(8,128)(2,1)S(1)}, u32[]{:S(2)}, u32[]{:S(2)}) collective-permute-start(bf16[256,1024]{1,0:T(8,128)(2,1)S(1)} %blur_score_pick.1), channel_id=1, source_target_pairs={{0,4},{2,14},{4,8},{6,2},{8,12},{10,6},{12,0},{14,10},{1,5},{3,15}... | collective-permute-start | bytes 1572872 | tf_op jit(solution)/shard_map/ppermute | solution.py:415
  67.8 26.8 %collective-permute-start.15 = (bf16[2,256,1024]{2,1,0:T(8,128)(2,1)S(1)}, bf16[2,256,1024]{2,1,0:T(8,128)(2,1)}, u32[]{:S(2)}, u32[]{:S(2)}) collective-permute-start(bf16[2,256,1024]{2,1,0:T(8,128)(2,1)S(1)} %pad_maximum_fusion.1.refs_0_), channel_id=1, source_target_pairs={{0,1},{1,0},{2,3},{3,2},{4,5},{5,4},{6,7},{7,6},{8,9},{9,8},{10,11... | collective-permute-start | bytes 3145736 | tf_op jit(solution)/shard_map/ppermute | solution.py:351
  88.6 6.5 %collective-permute-start.17 = (bf16[2,256,1024]{2,1,0:T(8,128)(2,1)S(1)}, bf16[2,256,1024]{2,1,0:T(8,128)(2,1)}, u32[]{:S(2)}, u32[]{:S(2)}) collective-permute-start(bf16[2,256,1024]{2,1,0:T(8,128)(2,1)S(1)} %pad_maximum_fusion.2.refs_2_), channel_id=1, source_target_pairs={{0,1},{1,0},{2,3},{3,2},{4,5},{5,4},{6,7},{7,6},{8,9},{9,8},{10,11... | collective-permute-start | bytes 3145736 | tf_op jit(solution)/shard_map/ppermute | solution.py:351
  88.7 5.0 %collective-permute-start.18 = (bf16[1,256,1024]{2,1,0:T(8,128)(2,1)S(1)}, bf16[1,256,1024]{2,1,0:T(8,128)(2,1)S(1)}, u32[]{:S(2)}, u32[]{:S(2)}) collective-permute-start(bf16[1,256,1024]{2,1,0:T(8,128)(2,1)S(1)} %bitcast.16), channel_id=1, source_target_pairs={{0,1},{1,0},{2,3},{3,2},{4,5},{5,4},{6,7},{7,6},{8,9},{9,8},{10,11... | collective-permute-start | bytes 1572872 | tf_op jit(solution)/shard_map/ppermute | solution.py:351
  89.2 17.4 %collective-permute-start.14 = (bf16[256,1024]{1,0:T(8,128)(2,1)}, bf16[256,1024]{1,0:T(8,128)(2,1)}, u32[]{:S(2)}, u32[]{:S(2)}) collective-permute-start(bf16[256,1024]{1,0:T(8,128)(2,1)} %collective-permute-done.7), channel_id=1, source_target_pairs={{0,2},{2,0},{4,6},{6,4},{8,10},{10,8},{12,14},{14,12},{1,3},{3,1},... | collective-permute-start | bytes 1572872 | tf_op jit(solution)/shard_map/ppermute | solution.py:422
  89.9 16.7 %collective-permute-start.20 = (bf16[256,1024]{1,0:T(8,128)(2,1)}, bf16[256,1024]{1,0:T(8,128)(2,1)}, u32[]{:S(2)}, u32[]{:S(2)}) collective-permute-start(bf16[256,1024]{1,0:T(8,128)(2,1)} %join_score.1), channel_id=1, source_target_pairs={{0,4},{2,14},{4,8},{6,2},{8,12},{10,6},{12,0},{14,10},{1,5},{3,15}... | collective-permute-start | bytes 1572872 | tf_op jit(solution)/shard_map/ppermute | solution.py:423
  94.5 12.6 %collective-permute-start.11 = (bf16[2,256,1024]{2,1,0:T(8,128)(2,1)S(1)}, bf16[2,256,1024]{2,1,0:T(8,128)(2,1)}, u32[]{:S(2)}, u32[]{:S(2)}) collective-permute-start(bf16[2,256,1024]{2,1,0:T(8,128)(2,1)S(1)} %pad_maximum_fusion.refs_0_), channel_id=1, source_target_pairs={{0,1},{1,0},{2,3},{3,2},{4,5},{5,4},{6,7},{7,6},{8,9},{9,8},{10,11... | collective-permute-start | bytes 3145736 | tf_op jit(solution)/shard_map/ppermute | solution.py:351
  94.5 15.0 %copy-start.2 = (bf16[256,1024]{1,0:T(8,128)(2,1)S(1)}, bf16[256,1024]{1,0:T(8,128)(2,1)}, u32[]{:S(2)}) copy-start(bf16[256,1024]{1,0:T(8,128)(2,1)} %copy-done.1) | copy-start | bytes 1572868
  94.6 12.5 %collective-permute-start.12 = (bf16[1,256,1024]{2,1,0:T(8,128)(2,1)}, bf16[1,256,1024]{2,1,0:T(8,128)(2,1)S(1)}, u32[]{:S(2)}, u32[]{:S(2)}) collective-permute-start(bf16[1,256,1024]{2,1,0:T(8,128)(2,1)} %bitcast.14), channel_id=1, source_target_pairs={{0,1},{1,0},{2,3},{3,2},{4,5},{5,4},{6,7},{7,6},{8,9},{9,8},{10,11... | collective-permute-start | bytes 1572872 | tf_op jit(solution)/shard_map/ppermute | solution.py:351
  106.6 2.1 %collective-permute-start.19 = (bf16[1,256,1024]{2,1,0:T(8,128)(2,1)}, bf16[1,256,1024]{2,1,0:T(8,128)(2,1)S(1)}, u32[]{:S(2)}, u32[]{:S(2)}) collective-permute-start(bf16[1,256,1024]{2,1,0:T(8,128)(2,1)} %bitcast.10.refs_4_), channel_id=1, source_target_pairs={{0,1},{1,0},{2,3},{3,2},{4,5},{5,4},{6,7},{7,6},{8,9},{9,8},{10,11... | collective-permute-start | bytes 1572872 | tf_op jit(solution)/shard_map/ppermute | solution.py:351
  106.6 2.9 %collective-permute-start.21 = (bf16[1,256,1024]{2,1,0:T(8,128)(2,1)}, bf16[1,256,1024]{2,1,0:T(8,128)(2,1)S(1)}, u32[]{:S(2)}, u32[]{:S(2)}) collective-permute-start(bf16[1,256,1024]{2,1,0:T(8,128)(2,1)} %bitcast.11.refs_6_), channel_id=1, source_target_pairs={{0,1},{1,0},{2,3},{3,2},{4,5},{5,4},{6,7},{7,6},{8,9},{9,8},{10,11... | collective-permute-start | bytes 1572872 | tf_op jit(solution)/shard_map/ppermute | solution.py:351
  (9 other events, 26.4 us)

commit v16 on v15

--- a/solution.py
+++ b/solution.py
@@ -368,8 +368,9 @@
     away = (slab % col_total != col).astype(jnp.int32)
     within = ids % blocks
     present = partners >= 0
-    parts_0 = jnp.where(kind == 4, 8 + away, kind // 2 * 4 + kind % 2 + 2 * away)
+    joined = jnp.where(kind == 3, 2, kind) + 3 * away
     alone = jnp.where(kind == 3, 4, jnp.where(kind == 4, 6, 8)) + away
+    parts_0 = jnp.where(kind == 2, 6 + away, jnp.where(kind == 4, 8 + away, joined))
     parts_1 = jnp.where(kind < 2, kind + 2 * away, alone)
     place_0, place_1 = (
         jnp.where(present, part * blocks + within, 0).astype(jnp.int32)
@@ -419,11 +420,10 @@
     ahead_1 = after(ahead_1, pair_1)
     rest_0 = after(rest_0, ahead_1)
     behind_0 = after(behind_0, rest_0)
-    rest_1 = lax.ppermute(after(ahead_1, rest_0), "row", in_pair)
-    behind_1 = lax.ppermute(after(own_1, rest_0), "row", behind)
-    sources_0 = both(own_0, ahead_0) + both(behind_0, pair_0) + both(rest_0)
+    rest_1 = lax.ppermute(ahead_1, "row", in_pair)
+    behind_1 = lax.ppermute(after(own_1, ahead_1), "row", behind)
+    sources_0 = both(own_0, ahead_0, pair_0) + both(behind_0) + both(rest_0)
     out = make_tiles(0, windows, place_0, present, sources_0, None)
-    rest_1, behind_1 = after(rest_1, out), after(behind_1, out)
     sources_1 = both(own_1, ahead_1) + both(pair_1) + both(rest_1) + both(behind_1)
     return make_tiles(1, windows, place_1, present, sources_1, out)
 

time: 116 us -> 117 us (level)
  starting transfers between devices: 21.9 us -> 23.8 us
  local copies, waits for them, and re-layouts: 6.54 us -> 8.07 us
  other arithmetic: 1.6 us -> 0.37 us
    ppermute x1, waiting for transfers between devices: 9.51 us -> 5.47 us  [on_device(): rest_0 = lax.ppermute(ahead_0, 'row', in_pair)]
    ppermute x2, waiting for transfers between devices: 3.32 us -> 6.79 us  [the longest x1 4.59 us: on_device(): behind_1 = lax.ppermute(after(own_1, ahead_1), 'row', behind)]
    ppermute x10, waiting for transfers between devices: 4.83 us -> 2.49 us  [other_col(): return lax.ppermute(value, 'col', [(0, 1), (1, 0)])]
    ppermute x2, starting transfers between devices: 3.19 us -> 5.49 us  [the longest x1 3.57 us: on_device(): rest_1 = lax.ppermute(ahead_1, 'row', in_pair)]
    unnamed x22 -> x24, local copies, waits for them, and re-layouts: 6.54 us -> 8.07 us
    another operation x3 -> x2, other arithmetic: 1.49 us -> 0.27 us  [both(): near = jnp.stack(parts, 0)]
  transfers between devices with their start and end apart: 22 -> 22, of which waited for: 12 -> 11; matrix products, arithmetic and copies ran while one was open for 1% -> 0% of each run, Pallas kernels for 15% -> 14%
where the time goes in v16:
time: 117 us
  waiting for transfers between devices  56.2 us (48%)
  Pallas kernels  27.8 us (24%)
  starting transfers between devices  23.8 us (20%)
  local copies, waits for them, and re-layouts  8.07 us (7%)
    ppermute x1, waiting for transfers between devices, on_device(): facing_0 = lax.ppermute(near_0, 'row', in_pair)  13.5 us
    pallas_call x4, Pallas kernels, call_on_rows(): pl.pallas_call(kernel, grid=(1,), in_specs=[whole(value) for value in ope...  12.4 us
    pallas_call x2, Pallas kernels, make_tiles(): pl.pallas_call(functools.partial(tiles_kernel, sources=count, window=wind...  12.4 us
    ppermute x1, waiting for transfers between devices, on_device(): pair_1 = lax.ppermute(own_1, 'row', in_pair)  11.2 us
    unnamed x24, local copies, waits for them, and re-layouts  8.07 us
    ppermute x1, waiting for transfers between devices, on_device(): pair_0 = lax.ppermute(after(own_0, halo_1), 'row', in_pair)  6.38 us
    ppermute x1, waiting for transfers between devices, on_device(): rest_0 = lax.ppermute(ahead_0, 'row', in_pair)  5.47 us
    ppermute x1, waiting for transfers between devices, on_device(): behind_1 = lax.ppermute(after(own_1, ahead_1), 'row', behind)  4.59 us
  transfers between devices with their start and end apart: 22, of which 11 were waited for; matrix products, arithmetic and copies ran while one was open for 0% of the time, Pallas kernels for 14%

profile of v16, /device:TPU:0, one launch (start us, length us, event | category | flops | bytes accessed | tf_op | source)
XLA Modules:
  0.0 116.7 jit_solution(3684184945649431394)
XLA Ops:
  0.0 1.6 %copy-done = bf16[2,256,2,8,128]{4,3,2,1,0:T(8,128)(2,1)S(1)} copy-done((bf16[2,256,2,8,128]{4,3,2,1,0:T(8,128)(2,1)S(1)}, bf16[2,256,2,8,128]{4,3,2,1,0:T(8,128)(2,1)}, u32[]{:S(2)}) %copy-start) | copy-done | bytes 2097176
  2.3 3.0 %faces.1 = (bf16[2064,128]{1,0:T(8,128)(2,1)S(1)}, bf16[8,256,128]{2,1,0:T(8,128)(2,1)}, bf16[2,256,128]{2,1,0:T(8,128)(2,1)}, bf16[8,256,128]{2,1,0:T(8,128)(2,...) custom-call(bf16[2,256,2,8,128]{4,3,2,1,0:T(8,128)(2,1)S(1)} %copy-done, s32[8,128]{1,0:T(8,128)S(1)} %bitcast.21), custom_call_target="tpu_custom_call" | custom-call | flops 1 | bytes 1 | tf_op jit(solution)/shard_map/faces/pallas_call | solution.py:78
  5.3 3.0 %collective-permute-start.3 = (bf16[2064,128]{1,0:T(8,128)(2,1)S(1)}, bf16[2064,128]{1,0:T(8,128)(2,1)S(1)}, u32[]{:S(2)}, u32[]{:S(2)}) collective-permute-start(bf16[2064,128]{1,0:T(8,128)(2,1)S(1)} %get-tuple-element.31.near_ref), channel_id=1, source_target_pairs={{0,2},{2,0},{4,6},{6,4},{8,10},{10,8},{12,14},{14,12},{1,3},{3,1},... | collective-permute-start | bytes 1585160 | tf_op jit(solution)/shard_map/ppermute | solution.py:396
  9.0 1.5 %collective-permute-start.2 = (bf16[8,256,128]{2,1,0:T(8,128)(2,1)S(1)}, bf16[8,256,128]{2,1,0:T(8,128)(2,1)S(1)}, u32[]{:S(2)}, u32[]{:S(2)}) collective-permute-start(bf16[8,256,128]{2,1,0:T(8,128)(2,1)S(1)} %get-tuple-element.27.outer_ref), channel_id=1, source_target_pairs={{2,6},{4,0},{6,10},{8,4},{10,14},{12,8},{3,7},{5,1},{7,11},{9,5},{... | collective-permute-start | bytes 1572872 | tf_op jit(solution)/shard_map/ppermute | solution.py:398
  12.1 5.2 %inner_blur.1.inner_ref = f32[256,1024]{1,0:T(8,128)S(1)} custom-call(bf16[8,256,128]{2,1,0:T(8,128)(2,1)S(1)} %get-tuple-element.26.near_ref, bf16[8,256,128]{2,1,0:T(8,128)(2,1)S(1)} %get-tuple-element.27.outer_ref, bf16[2,256,128]{2,1,0:T(8,128)(2,1)S(1)} %collective-permute-done.edge_ref, s32[8,128]{1,0:T(8,128)S(1)} %bitcast.22), custom_call_target="tpu_custom_call" | custom-call | flops 1 | bytes 1 | tf_op jit(solution)/shard_map/inner_blur/pallas_call | solution.py:222
  17.3 13.5 %collective-permute-done.3.facing_ref = bf16[2064,128]{1,0:T(8,128)(2,1)S(1)} collective-permute-done((bf16[2064,128]{1,0:T(8,128)(2,1)S(1)}, bf16[2064,128]{1,0:T(8,128)(2,1)S(1)}, u32[]{:S(2)}, u32[]{:S(2)}) %collective-permute-start.3) | collective-permute-done | bytes 528416 | tf_op jit(solution)/shard_map/ppermute | solution.py:396
  30.8 4.1 %collective-permute-done.2.beyond_ref = bf16[8,256,128]{2,1,0:T(8,128)(2,1)S(1)} collective-permute-done((bf16[8,256,128]{2,1,0:T(8,128)(2,1)S(1)}, bf16[8,256,128]{2,1,0:T(8,128)(2,1)S(1)}, u32[]{:S(2)}, u32[]{:S(2)}) %collective-permute-start.2) | collective-permute-done | bytes 524320 | tf_op jit(solution)/shard_map/ppermute | solution.py:398
  35.1 1.4 %collective-permute-done.5.corner_ref = bf16[3,256,128]{2,1,0:T(8,128)(2,1)S(1)} collective-permute-done((bf16[3,256,128]{2,1,0:T(8,128)(2,1)S(1)}, bf16[3,256,128]{2,1,0:T(8,128)(2,1)S(1)}, u32[]{:S(2)}, u32[]{:S(2)}) %collective-permute-start.5) | collective-permute-done | bytes 196640 | tf_op jit(solution)/shard_map/ppermute | solution.py:351
  36.5 2.4 %halo_blur.1 = bf16[256,1024]{1,0:T(8,128)(2,1)S(1)} custom-call(bf16[8,256,128]{2,1,0:T(8,128)(2,1)S(1)} %get-tuple-element.26.near_ref, bf16[8,256,128]{2,1,0:T(8,128)(2,1)S(1)} %collective-permute-done.2.beyond_ref, bf16[2,256,128]{2,1,0:T(8,128)(2,1)S(1)} %collective-permute-done.edge_ref, bf16[3,256,128]{2,1,0:T(8,128)(2,1)S(1)} %collective-permute-done.5.corner_ref, ...), custom_call_target="tpu_custom_call" | custom-call | flops 1 | bytes 1 | tf_op jit(solution)/shard_map/halo_blur/pallas_call | solution.py:222
  39.7 4.4 %blur_score_pick.1 = bf16[256,1024]{1,0:T(8,128)(2,1)S(1)} custom-call(bf16[2064,128]{1,0:T(8,128)(2,1)S(1)} %get-tuple-element.31.near_ref, bf16[8,256,128]{2,1,0:T(8,128)(2,1)} %get-tuple-element.33.outer_ref, bf16[2064,128]{1,0:T(8,128)(2,1)S(1)} %collective-permute-done.3.facing_ref, bf16[8,256,128]{2,1,0:T(8,128)(2,1)S(1)} %collective-permute-done.4.across_ref, ...), custom_call_target="tpu_custom_call" | custom-call | flops 1 | bytes 1 | tf_op jit(solution)/shard_map/blur_score_pick/pallas_call | solution.py:222
  44.0 4.6 %collective-permute-start.10 = (bf16[256,1024]{1,0:T(8,128)(2,1)S(1)}, bf16[256,1024]{1,0:T(8,128)(2,1)S(1)}, u32[]{:S(2)}, u32[]{:S(2)}) collective-permute-start(bf16[256,1024]{1,0:T(8,128)(2,1)S(1)} %blur_score_pick.1), channel_id=1, source_target_pairs={{4,0},{14,2},{8,4},{2,6},{12,8},{6,10},{0,12},{10,14},{5,1},{15,3}... | collective-permute-start | bytes 1572872 | tf_op jit(solution)/shard_map/ppermute | solution.py:409
  48.6 4.3 %collective-permute-done.6.halo_ref = bf16[256,1024]{1,0:T(8,128)(2,1)S(1)} collective-permute-done((bf16[256,1024]{1,0:T(8,128)(2,1)S(1)}, bf16[256,1024]{1,0:T(8,128)(2,1)S(1)}, u32[]{:S(2)}, u32[]{:S(2)}) %collective-permute-start.6) | collective-permute-done | bytes 524320 | tf_op jit(solution)/shard_map/ppermute | solution.py:406
  54.1 1.4 %collective-permute-start.8 = (bf16[256,1024]{1,0:T(8,128)(2,1)S(1)}, bf16[256,1024]{1,0:T(8,128)(2,1)S(1)}, u32[]{:S(2)}, u32[]{:S(2)}) collective-permute-start(bf16[256,1024]{1,0:T(8,128)(2,1)S(1)} %join_score.1), channel_id=1, source_target_pairs={{0,2},{2,0},{4,6},{6,4},{8,10},{10,8},{12,14},{14,12},{1,3},{3,1},... | collective-permute-start | bytes 1572872 | tf_op jit(solution)/shard_map/ppermute | solution.py:413
  55.5 3.5 %collective-permute-start.7 = (bf16[256,1024]{1,0:T(8,128)(2,1)S(1)}, bf16[256,1024]{1,0:T(8,128)(2,1)S(1)}, u32[]{:S(2)}, u32[]{:S(2)}) collective-permute-start(bf16[256,1024]{1,0:T(8,128)(2,1)S(1)} %join_score.1), channel_id=1, source_target_pairs={{4,0},{14,2},{8,4},{2,6},{12,8},{6,10},{0,12},{10,14},{5,1},{15,3}... | collective-permute-start | bytes 1572872 | tf_op jit(solution)/shard_map/ppermute | solution.py:414
  59.0 1.9 %collective-permute-done.10 = bf16[256,1024]{1,0:T(8,128)(2,1)S(1)} collective-permute-done((bf16[256,1024]{1,0:T(8,128)(2,1)S(1)}, bf16[256,1024]{1,0:T(8,128)(2,1)S(1)}, u32[]{:S(2)}, u32[]{:S(2)}) %collective-permute-start.10) | collective-permute-done | bytes 524320 | tf_op jit(solution)/shard_map/ppermute | solution.py:409
  61.4 6.4 %collective-permute-done.9 = bf16[256,1024]{1,0:T(8,128)(2,1)S(1)} collective-permute-done((bf16[256,1024]{1,0:T(8,128)(2,1)S(1)}, bf16[256,1024]{1,0:T(8,128)(2,1)S(1)}, u32[]{:S(2)}, u32[]{:S(2)}) %collective-permute-start.9) | collective-permute-done | bytes 524320 | tf_op jit(solution)/shard_map/ppermute | solution.py:412
  67.8 11.2 %collective-permute-done.8 = bf16[256,1024]{1,0:T(8,128)(2,1)S(1)} collective-permute-done((bf16[256,1024]{1,0:T(8,128)(2,1)S(1)}, bf16[256,1024]{1,0:T(8,128)(2,1)S(1)}, u32[]{:S(2)}, u32[]{:S(2)}) %collective-permute-start.8) | collective-permute-done | bytes 524320 | tf_op jit(solution)/shard_map/ppermute | solution.py:413
  79.3 1.9 %collective-permute-start.15 = (bf16[256,1024]{1,0:T(8,128)(2,1)S(1)}, bf16[256,1024]{1,0:T(8,128)(2,1)}, u32[]{:S(2)}, u32[]{:S(2)}) collective-permute-start(bf16[256,1024]{1,0:T(8,128)(2,1)S(1)} %join_score.1), channel_id=1, source_target_pairs={{0,4},{2,14},{4,8},{6,2},{8,12},{10,6},{12,0},{14,10},{1,5},{3,15}... | collective-permute-start | bytes 1572872 | tf_op jit(solution)/shard_map/ppermute | solution.py:424
  81.2 3.6 %collective-permute-start.13 = (bf16[256,1024]{1,0:T(8,128)(2,1)S(1)}, bf16[256,1024]{1,0:T(8,128)(2,1)}, u32[]{:S(2)}, u32[]{:S(2)}) collective-permute-start(bf16[256,1024]{1,0:T(8,128)(2,1)S(1)} %collective-permute-done.7), channel_id=1, source_target_pairs={{0,2},{2,0},{4,6},{6,4},{8,10},{10,8},{12,14},{14,12},{1,3},{3,1},... | collective-permute-start | bytes 1572872 | tf_op jit(solution)/shard_map/ppermute | solution.py:423
  84.8 5.5 %collective-permute-done.19 = bf16[256,1024]{1,0:T(8,128)(2,1)S(1)} collective-permute-done((bf16[256,1024]{1,0:T(8,128)(2,1)S(1)}, bf16[256,1024]{1,0:T(8,128)(2,1)S(1)}, u32[]{:S(2)}, u32[]{:S(2)}) %collective-permute-start.19) | collective-permute-done | bytes 524320 | tf_op jit(solution)/shard_map/ppermute | solution.py:417
  90.9 4.6 %collective-permute-done.15 = bf16[256,1024]{1,0:T(8,128)(2,1)} collective-permute-done((bf16[256,1024]{1,0:T(8,128)(2,1)S(1)}, bf16[256,1024]{1,0:T(8,128)(2,1)}, u32[]{:S(2)}, u32[]{:S(2)}) %collective-permute-start.15) | collective-permute-done | bytes 524320 | tf_op jit(solution)/shard_map/ppermute | solution.py:424
  97.7 2.2 %collective-permute-done.13 = bf16[256,1024]{1,0:T(8,128)(2,1)} collective-permute-done((bf16[256,1024]{1,0:T(8,128)(2,1)S(1)}, bf16[256,1024]{1,0:T(8,128)(2,1)}, u32[]{:S(2)}, u32[]{:S(2)}) %collective-permute-start.13) | collective-permute-done | bytes 524320 | tf_op jit(solution)/shard_map/ppermute | solution.py:423
  104.1 5.9 %tiles.2.refs_8_ = bf16[8,16,2,128,128]{4,3,2,1,0:T(8,128)(2,1)} custom-call(s32[8,16]{1,0:T(8,128)S(1)} %get-tuple-element.47.place_ref, s32[8,16]{1,0:T(8,128)S(1)} %fusion.17.present_ref, bf16[3,256,1024]{2,1,0:T(8,128)(2,1)S(1)} %pad_maximum_fusion.refs_0_, bf16[3,256,1024]{2,1,0:T(8,128)(2,1)} %collective-permute-done.17.refs_1_, ...), custom_call_target="tpu_custom_call" | custom-call | flops 1 | bytes 1 | tf_op jit(solution)/shard_map/tiles/pallas_call | solution.py:317
  110.0 6.5 %tiles.3 = bf16[8,16,2,128,128]{4,3,2,1,0:T(8,128)(2,1)} custom-call(s32[8,16]{1,0:T(8,128)S(1)} %get-tuple-element.48.place_ref, s32[8,16]{1,0:T(8,128)S(1)} %fusion.17.present_ref, bf16[2,256,1024]{2,1,0:T(8,128)(2,1)S(1)} %pad_maximum_fusion.1.refs_0_, bf16[2,256,1024]{2,1,0:T(8,128)(2,1)} %collective-permute-done.11.refs_1_, ...), custom_call_target="tpu_custom_call", output_to_operand_aliasing={{}: (10, {})} | custom-call | flops 1 | bytes 1 | tf_op jit(solution)/shard_map/tiles/pallas_call | solution.py:317
  (59 shorter events, 12.9 us)
Async XLA Ops:
  2.3 9.8 %copy-start.10 = (s32[1024]{0:T(1024)S(1)}, s32[1024]{0:T(1024)}, u32[]{:S(2)}) copy-start(s32[1024]{0:T(1024)} %param.4) | copy-start | bytes 12292
  5.3 25.5 %collective-permute-start.3 = (bf16[2064,128]{1,0:T(8,128)(2,1)S(1)}, bf16[2064,128]{1,0:T(8,128)(2,1)S(1)}, u32[]{:S(2)}, u32[]{:S(2)}) collective-permute-start(bf16[2064,128]{1,0:T(8,128)(2,1)S(1)} %get-tuple-element.31.near_ref), channel_id=1, source_target_pairs={{0,2},{2,0},{4,6},{6,4},{8,10},{10,8},{12,14},{14,12},{1,3},{3,1},... | collective-permute-start | bytes 1585160 | tf_op jit(solution)/shard_map/ppermute | solution.py:396
  8.3 9.0 %collective-permute-start.4 = (bf16[8,256,128]{2,1,0:T(8,128)(2,1)}, bf16[8,256,128]{2,1,0:T(8,128)(2,1)S(1)}, u32[]{:S(2)}, u32[]{:S(2)}) collective-permute-start(bf16[8,256,128]{2,1,0:T(8,128)(2,1)} %get-tuple-element.33.outer_ref), channel_id=1, source_target_pairs={{2,4},{4,2},{6,8},{8,6},{10,12},{12,10},{3,5},{5,3},{7,9},{9,7},{1... | collective-permute-start | bytes 1572872 | tf_op jit(solution)/shard_map/ppermute | solution.py:397
  9.0 25.9 %collective-permute-start.2 = (bf16[8,256,128]{2,1,0:T(8,128)(2,1)S(1)}, bf16[8,256,128]{2,1,0:T(8,128)(2,1)S(1)}, u32[]{:S(2)}, u32[]{:S(2)}) collective-permute-start(bf16[8,256,128]{2,1,0:T(8,128)(2,1)S(1)} %get-tuple-element.27.outer_ref), channel_id=1, source_target_pairs={{2,6},{4,0},{6,10},{8,4},{10,14},{12,8},{3,7},{5,1},{7,11},{9,5},{... | collective-permute-start | bytes 1572872 | tf_op jit(solution)/shard_map/ppermute | solution.py:398
  10.5 1.6 %collective-permute-start.1 = (bf16[2,256,128]{2,1,0:T(8,128)(2,1)}, bf16[2,256,128]{2,1,0:T(8,128)(2,1)S(1)}, u32[]{:S(2)}, u32[]{:S(2)}) collective-permute-start(bf16[2,256,128]{2,1,0:T(8,128)(2,1)} %get-tuple-element.29), channel_id=1, source_target_pairs={{0,1},{1,0},{2,3},{3,2},{4,5},{5,4},{6,7},{7,6},{8,9},{9,8},{10,11... | collective-permute-start | bytes 393224 | tf_op jit(solution)/shard_map/ppermute | solution.py:351
  10.6 1.5 %collective-permute-start = (bf16[2,256,128]{2,1,0:T(8,128)(2,1)S(1)}, bf16[2,256,128]{2,1,0:T(8,128)(2,1)S(1)}, u32[]{:S(2)}, u32[]{:S(2)}) collective-permute-start(bf16[2,256,128]{2,1,0:T(8,128)(2,1)S(1)} %get-tuple-element.28), channel_id=1, source_target_pairs={{0,1},{1,0},{2,3},{3,2},{4,5},{5,4},{6,7},{7,6},{8,9},{9,8},{10,11... | collective-permute-start | bytes 393224 | tf_op jit(solution)/shard_map/ppermute | solution.py:351
  35.0 1.5 %collective-permute-start.5 = (bf16[3,256,128]{2,1,0:T(8,128)(2,1)S(1)}, bf16[3,256,128]{2,1,0:T(8,128)(2,1)S(1)}, u32[]{:S(2)}, u32[]{:S(2)}) collective-permute-start(bf16[3,256,128]{2,1,0:T(8,128)(2,1)S(1)} %pad_maximum_fusion.2), channel_id=1, source_target_pairs={{0,1},{1,0},{2,3},{3,2},{4,5},{5,4},{6,7},{7,6},{8,9},{9,8},{10,11... | collective-permute-start | bytes 589832 | tf_op jit(solution)/shard_map/ppermute | solution.py:351
  38.9 14.0 %collective-permute-start.6 = (bf16[256,1024]{1,0:T(8,128)(2,1)S(1)}, bf16[256,1024]{1,0:T(8,128)(2,1)S(1)}, u32[]{:S(2)}, u32[]{:S(2)}) collective-permute-start(bf16[256,1024]{1,0:T(8,128)(2,1)S(1)} %halo_blur.1), channel_id=1, source_target_pairs={{0,2},{2,0},{4,6},{6,4},{8,10},{10,8},{12,14},{14,12},{1,3},{3,1},... | collective-permute-start | bytes 1572872 | tf_op jit(solution)/shard_map/ppermute | solution.py:406
  44.0 16.9 %collective-permute-start.10 = (bf16[256,1024]{1,0:T(8,128)(2,1)S(1)}, bf16[256,1024]{1,0:T(8,128)(2,1)S(1)}, u32[]{:S(2)}, u32[]{:S(2)}) collective-permute-start(bf16[256,1024]{1,0:T(8,128)(2,1)S(1)} %blur_score_pick.1), channel_id=1, source_target_pairs={{4,0},{14,2},{8,4},{2,6},{12,8},{6,10},{0,12},{10,14},{5,1},{15,3}... | collective-permute-start | bytes 1572872 | tf_op jit(solution)/shard_map/ppermute | solution.py:409
  52.9 14.9 %collective-permute-start.9 = (bf16[256,1024]{1,0:T(8,128)(2,1)S(1)}, bf16[256,1024]{1,0:T(8,128)(2,1)S(1)}, u32[]{:S(2)}, u32[]{:S(2)}) collective-permute-start(bf16[256,1024]{1,0:T(8,128)(2,1)S(1)} %blur_score_pick.1), channel_id=1, source_target_pairs={{0,2},{2,0},{4,6},{6,4},{8,10},{10,8},{12,14},{14,12},{1,3},{3,1},... | collective-permute-start | bytes 1572872 | tf_op jit(solution)/shard_map/ppermute | solution.py:412
  54.1 24.9 %collective-permute-start.8 = (bf16[256,1024]{1,0:T(8,128)(2,1)S(1)}, bf16[256,1024]{1,0:T(8,128)(2,1)S(1)}, u32[]{:S(2)}, u32[]{:S(2)}) collective-permute-start(bf16[256,1024]{1,0:T(8,128)(2,1)S(1)} %join_score.1), channel_id=1, source_target_pairs={{0,2},{2,0},{4,6},{6,4},{8,10},{10,8},{12,14},{14,12},{1,3},{3,1},... | collective-permute-start | bytes 1572872 | tf_op jit(solution)/shard_map/ppermute | solution.py:413
  55.5 23.5 %collective-permute-start.7 = (bf16[256,1024]{1,0:T(8,128)(2,1)S(1)}, bf16[256,1024]{1,0:T(8,128)(2,1)S(1)}, u32[]{:S(2)}, u32[]{:S(2)}) collective-permute-start(bf16[256,1024]{1,0:T(8,128)(2,1)S(1)} %join_score.1), channel_id=1, source_target_pairs={{4,0},{14,2},{8,4},{2,6},{12,8},{6,10},{0,12},{10,14},{5,1},{15,3}... | collective-permute-start | bytes 1572872 | tf_op jit(solution)/shard_map/ppermute | solution.py:414
  60.9 29.3 %collective-permute-start.19 = (bf16[256,1024]{1,0:T(8,128)(2,1)S(1)}, bf16[256,1024]{1,0:T(8,128)(2,1)S(1)}, u32[]{:S(2)}, u32[]{:S(2)}) collective-permute-start(bf16[256,1024]{1,0:T(8,128)(2,1)S(1)} %collective-permute-done.10), channel_id=1, source_target_pairs={{0,2},{2,0},{4,6},{6,4},{8,10},{10,8},{12,14},{14,12},{1,3},{3,1},... | collective-permute-start | bytes 1572872 | tf_op jit(solution)/shard_map/ppermute | solution.py:417
  61.4 28.9 %collective-permute-start.18 = (bf16[256,1024]{1,0:T(8,128)(2,1)S(1)}, bf16[256,1024]{1,0:T(8,128)(2,1)S(1)}, u32[]{:S(2)}, u32[]{:S(2)}) collective-permute-start(bf16[256,1024]{1,0:T(8,128)(2,1)S(1)} %blur_score_pick.1), channel_id=1, source_target_pairs={{0,4},{2,14},{4,8},{6,2},{8,12},{10,6},{12,0},{14,10},{1,5},{3,15}... | collective-permute-start | bytes 1572872 | tf_op jit(solution)/shard_map/ppermute | solution.py:416
  79.2 20.7 %copy-start.11 = (s32[8,16]{1,0:T(8,128)S(1)}, s32[8,16]{1,0:T(8,128)}, u32[]{:S(2)}) copy-start(s32[8,16]{1,0:T(8,128)} %param.5) | copy-start | bytes 1540
  79.2 20.7 %collective-permute-start.17 = (bf16[3,256,1024]{2,1,0:T(8,128)(2,1)S(1)}, bf16[3,256,1024]{2,1,0:T(8,128)(2,1)}, u32[]{:S(2)}, u32[]{:S(2)}) collective-permute-start(bf16[3,256,1024]{2,1,0:T(8,128)(2,1)S(1)} %pad_maximum_fusion.refs_0_), channel_id=1, source_target_pairs={{0,1},{1,0},{2,3},{3,2},{4,5},{5,4},{6,7},{7,6},{8,9},{9,8},{10,11... | collective-permute-start | bytes 4718600 | tf_op jit(solution)/shard_map/ppermute | solution.py:351
  79.3 16.2 %collective-permute-start.15 = (bf16[256,1024]{1,0:T(8,128)(2,1)S(1)}, bf16[256,1024]{1,0:T(8,128)(2,1)}, u32[]{:S(2)}, u32[]{:S(2)}) collective-permute-start(bf16[256,1024]{1,0:T(8,128)(2,1)S(1)} %join_score.1), channel_id=1, source_target_pairs={{0,4},{2,14},{4,8},{6,2},{8,12},{10,6},{12,0},{14,10},{1,5},{3,15}... | collective-permute-start | bytes 1572872 | tf_op jit(solution)/shard_map/ppermute | solution.py:424
  81.2 18.7 %collective-permute-start.13 = (bf16[256,1024]{1,0:T(8,128)(2,1)S(1)}, bf16[256,1024]{1,0:T(8,128)(2,1)}, u32[]{:S(2)}, u32[]{:S(2)}) collective-permute-start(bf16[256,1024]{1,0:T(8,128)(2,1)S(1)} %collective-permute-done.7), channel_id=1, source_target_pairs={{0,2},{2,0},{4,6},{6,4},{8,10},{10,8},{12,14},{14,12},{1,3},{3,1},... | collective-permute-start | bytes 1572872 | tf_op jit(solution)/shard_map/ppermute | solution.py:423
  90.2 5.3 %collective-permute-start.20 = (bf16[1,256,1024]{2,1,0:T(8,128)(2,1)S(1)}, bf16[1,256,1024]{2,1,0:T(8,128)(2,1)S(1)}, u32[]{:S(2)}, u32[]{:S(2)}) collective-permute-start(bf16[1,256,1024]{2,1,0:T(8,128)(2,1)S(1)} %bitcast.19), channel_id=1, source_target_pairs={{0,1},{1,0},{2,3},{3,2},{4,5},{5,4},{6,7},{7,6},{8,9},{9,8},{10,11... | collective-permute-start | bytes 1572872 | tf_op jit(solution)/shard_map/ppermute | solution.py:351
  90.3 6.5 %collective-permute-start.21 = (bf16[1,256,1024]{2,1,0:T(8,128)(2,1)S(1)}, bf16[1,256,1024]{2,1,0:T(8,128)(2,1)S(1)}, u32[]{:S(2)}, u32[]{:S(2)}) collective-permute-start(bf16[1,256,1024]{2,1,0:T(8,128)(2,1)S(1)} %bitcast.17), channel_id=1, source_target_pairs={{0,1},{1,0},{2,3},{3,2},{4,5},{5,4},{6,7},{7,6},{8,9},{9,8},{10,11... | collective-permute-start | bytes 1572872 | tf_op jit(solution)/shard_map/ppermute | solution.py:351
  95.5 14.5 %collective-permute-start.11 = (bf16[2,256,1024]{2,1,0:T(8,128)(2,1)S(1)}, bf16[2,256,1024]{2,1,0:T(8,128)(2,1)}, u32[]{:S(2)}, u32[]{:S(2)}) collective-permute-start(bf16[2,256,1024]{2,1,0:T(8,128)(2,1)S(1)} %pad_maximum_fusion.1.refs_0_), channel_id=1, source_target_pairs={{0,1},{1,0},{2,3},{3,2},{4,5},{5,4},{6,7},{7,6},{8,9},{9,8},{10,11... | collective-permute-start | bytes 3145736 | tf_op jit(solution)/shard_map/ppermute | solution.py:351
  96.3 13.7 %collective-permute-start.12 = (bf16[1,256,1024]{2,1,0:T(8,128)(2,1)S(1)}, bf16[1,256,1024]{2,1,0:T(8,128)(2,1)}, u32[]{:S(2)}, u32[]{:S(2)}) collective-permute-start(bf16[1,256,1024]{2,1,0:T(8,128)(2,1)S(1)} %bitcast.15), channel_id=1, source_target_pairs={{0,1},{1,0},{2,3},{3,2},{4,5},{5,4},{6,7},{7,6},{8,9},{9,8},{10,11... | collective-permute-start | bytes 1572872 | tf_op jit(solution)/shard_map/ppermute | solution.py:351
  97.7 12.4 %collective-permute-start.16 = (bf16[1,256,1024]{2,1,0:T(8,128)(2,1)}, bf16[1,256,1024]{2,1,0:T(8,128)(2,1)}, u32[]{:S(2)}, u32[]{:S(2)}) collective-permute-start(bf16[1,256,1024]{2,1,0:T(8,128)(2,1)} %bitcast.6.refs_6_), channel_id=1, source_target_pairs={{0,1},{1,0},{2,3},{3,2},{4,5},{5,4},{6,7},{7,6},{8,9},{9,8},{10,11... | collective-permute-start | bytes 1572872 | tf_op jit(solution)/shard_map/ppermute | solution.py:351
  99.9 10.2 %collective-permute-start.14 = (bf16[1,256,1024]{2,1,0:T(8,128)(2,1)}, bf16[1,256,1024]{2,1,0:T(8,128)(2,1)}, u32[]{:S(2)}, u32[]{:S(2)}) collective-permute-start(bf16[1,256,1024]{2,1,0:T(8,128)(2,1)} %bitcast.5.refs_4_), channel_id=1, source_target_pairs={{0,1},{1,0},{2,3},{3,2},{4,5},{5,4},{6,7},{7,6},{8,9},{9,8},{10,11... | collective-permute-start | bytes 1572872 | tf_op jit(solution)/shard_map/ppermute | solution.py:351
  (10 other events, 19.9 us)

commit v17 on v16

--- a/solution.py
+++ b/solution.py
@@ -13,6 +13,7 @@
 CENTRE = 1.0 / (1.0 + 2.0 * math.exp(-0.5))
 SMALL = pl.CostEstimate(flops=1, bytes_accessed=1, transcendentals=0)
 VMEM_BYTES = 20 * 1024 * 1024
+TILES_VMEM_BYTES = 28 * 1024 * 1024
 
 
 def is_even():
@@ -268,72 +269,79 @@
     )
 
 
-def tiles_kernel(place_ref, present_ref, *refs, sources, window):
-    parts = refs[:sources]
+def tiles_kernel(*refs, counts):
+    windows = len(counts)
+    places, present_ref = refs[:windows], refs[windows]
     out_ref, held, tiles, sems, out_sems = refs[-5:]
     blocks, slots = out_ref.shape[:2]
 
-    loads = []
-    first = 0
-    for n, part in enumerate(parts):
-        target = held.at[pl.ds(first, part.shape[0])]
-        first += part.shape[0]
-        loads.append(pltpu.make_async_copy(part, target, sems.at[n]))
-        loads[-1].start()
-    for load in loads:
-        load.wait()
-
-    def partner(block, slot):
-        place = place_ref[block, slot]
-        start = pl.multiple_of(lax.rem(place, blocks) * BLOCK, BLOCK)
-        return held[lax.div(place, blocks), :, pl.ds(start, BLOCK)]
+    loads, used = [], windows + 1
+    for window, count in enumerate(counts):
+        first, here = 0, []
+        for n, part in enumerate(refs[used : used + count]):
+            target = held.at[window, pl.ds(first, part.shape[0])]
+            here.append(pltpu.make_async_copy(part, target, sems.at[window, n]))
+            here[-1].start()
+            first += part.shape[0]
+        loads.append(here)
+        used += count
 
     stores = []
-    for block in range(blocks):
-        own = held[0, :, block * BLOCK : (block + 1) * BLOCK].T
-        for slot in range(0, slots, 2):
-            pair = jnp.concatenate([partner(block, slot), partner(block, slot + 1)], axis=1)
-            both = jnp.dot(own, pair, preferred_element_type=jnp.float32)
-            for n in range(2):
-                tile = both[:, n * BLOCK : (n + 1) * BLOCK]
-                tile = jnp.where(present_ref[block, slot + n] != 0, tile, 0.0)
-                tiles[block, slot + n] = tile.astype(jnp.bfloat16)
-        stores.append(
-            pltpu.make_async_copy(tiles.at[block], out_ref.at[block, :, window], out_sems.at[block])
-        )
-        stores[-1].start()
+    for window in range(windows):
+        for load in loads[window]:
+            load.wait()
+
+        def partner(block, slot):
+            place = places[window][block, slot]
+            start = pl.multiple_of(lax.rem(place, blocks) * BLOCK, BLOCK)
+            return held[window, lax.div(place, blocks), :, pl.ds(start, BLOCK)]
+
+        for block in range(blocks):
+            own = held[window, 0, :, block * BLOCK : (block + 1) * BLOCK].T
+            for slot in range(0, slots, 2):
+                pair = jnp.concatenate([partner(block, slot), partner(block, slot + 1)], axis=1)
+                both = jnp.dot(own, pair, preferred_element_type=jnp.float32)
+                for n in range(2):
+                    tile = both[:, n * BLOCK : (n + 1) * BLOCK]
+                    tile = jnp.where(present_ref[block, slot + n] != 0, tile, 0.0)
+                    tiles[window, block, slot + n] = tile.astype(jnp.bfloat16)
+            store = pltpu.make_async_copy(
+                tiles.at[window, block], out_ref.at[block, :, window], out_sems.at[window, block]
+            )
+            store.start()
+            stores.append(store)
     for store in stores:
         store.wait()
 
 
-def make_tiles(window, windows, place, present, sources, earlier):
-    frames, rows = sources[0].shape[1:]
-    total = sum(source.shape[0] for source in sources)
+def make_tiles(places, present, sources):
+    frames, rows = sources[0][0].shape[1:]
+    windows = len(sources)
+    total = sum(part.shape[0] for part in sources[0])
+    counts = tuple(len(parts) for parts in sources)
+    operands = [part for parts in sources for part in parts]
     blocks = rows // BLOCK
-    slots = place.shape[1]
-    count = len(sources)
+    slots = present.shape[1]
     anywhere = pl.BlockSpec(memory_space=pl.ANY)
-    operands = list(sources) + ([] if earlier is None else [earlier])
     return pl.pallas_call(
-        functools.partial(tiles_kernel, sources=count, window=window),
+        functools.partial(tiles_kernel, counts=counts),
         grid_spec=pltpu.PrefetchScalarGridSpec(
-            num_scalar_prefetch=2,
+            num_scalar_prefetch=windows + 1,
             grid=(1,),
             in_specs=[anywhere] * len(operands),
             out_specs=anywhere,
             scratch_shapes=[
-                pltpu.VMEM((total, frames, rows), jnp.bfloat16),
-                pltpu.VMEM((blocks, slots, BLOCK, BLOCK), jnp.bfloat16),
-                pltpu.SemaphoreType.DMA((count,)),
-                pltpu.SemaphoreType.DMA((blocks,)),
+                pltpu.VMEM((windows, total, frames, rows), jnp.bfloat16),
+                pltpu.VMEM((windows, blocks, slots, BLOCK, BLOCK), jnp.bfloat16),
+                pltpu.SemaphoreType.DMA((windows, max(counts))),
+                pltpu.SemaphoreType.DMA((windows, blocks)),
             ],
         ),
         out_shape=jax.ShapeDtypeStruct((blocks, slots, windows, BLOCK, BLOCK), jnp.bfloat16),
-        input_output_aliases={} if earlier is None else {2 + count: 0},
-        compiler_params=pltpu.CompilerParams(vmem_limit_bytes=VMEM_BYTES),
+        compiler_params=pltpu.CompilerParams(vmem_limit_bytes=TILES_VMEM_BYTES),
         cost_estimate=SMALL,
         name="tiles",
-    )(place, present, *operands)
+    )(*places, present, *operands)
 
 
 def after(value, *earlier):
@@ -382,7 +390,6 @@
         near = jnp.stack(parts, 0)
         return [near, other_col(near)]
 
-    windows = bold.shape[0]
     frames, slab_y = bold.shape[1], bold.shape[3]
 
     def ends(*layers):
@@ -423,9 +430,8 @@
     rest_1 = lax.ppermute(ahead_1, "row", in_pair)
     behind_1 = lax.ppermute(after(own_1, ahead_1), "row", behind)
     sources_0 = both(own_0, ahead_0, pair_0) + both(behind_0) + both(rest_0)
-    out = make_tiles(0, windows, place_0, present, sources_0, None)
     sources_1 = both(own_1, ahead_1) + both(pair_1) + both(rest_1) + both(behind_1)
-    return make_tiles(1, windows, place_1, present, sources_1, out)
+    return make_tiles((place_0, place_1), present, (sources_0, sources_1))
 
 
 def solution(mesh):

time: 117 us -> 123 us (1.051)
  waiting for transfers between devices: 56.2 us -> 68 us
  Pallas kernels: 27.8 us -> 24.6 us
  starting transfers between devices: 23.8 us -> 21.7 us
    ppermute x1, waiting for transfers between devices: 4.59 us -> 12.1 us  [on_device(): behind_1 = lax.ppermute(after(own_1, ahead_1), 'row', behind)]
    ppermute x1, waiting for transfers between devices: 5.47 us -> 9.86 us  [on_device(): rest_0 = lax.ppermute(ahead_0, 'row', in_pair)]
    pallas_call x2 -> x1, Pallas kernels: 12.4 us -> 9.19 us  [make_tiles(): pl.pallas_call(functools.partial(tiles_kernel, counts=counts), grid_spec=...]
    ppermute x1, starting transfers between devices: 3.57 us -> 0.72 us  [on_device(): rest_1 = lax.ppermute(ahead_1, 'row', in_pair)]
    ppermute x1, waiting for transfers between devices: 6.38 us -> 3.68 us  [on_device(): pair_0 = lax.ppermute(after(own_0, halo_1), 'row', in_pair)]
    ppermute x10, waiting for transfers between devices: 2.49 us -> 4.9 us  [other_col(): return lax.ppermute(value, 'col', [(0, 1), (1, 0)])]
    ppermute x1, waiting for transfers between devices: 1.93 us -> 4.3 us  [on_device(): ahead_0 = lax.ppermute(own_0, 'row', ahead)]
    ppermute x1, waiting for transfers between devices: 2.2 us -> 0.01 us  [on_device(): rest_1 = lax.ppermute(ahead_1, 'row', in_pair)]
  transfers between devices with their start and end apart: 22 -> 22, of which waited for: 11 -> 12; matrix products, arithmetic and copies ran while one was open for 0% -> 0% of each run, Pallas kernels for 14% -> 8%
where the time goes in v17:
time: 123 us; the launch traced here: 122 us
  waiting for transfers between devices  68 us (55%)
  Pallas kernels  24.6 us (20%)
  starting transfers between devices  21.7 us (18%)
  local copies, waits for them, and re-layouts  7.02 us (6%)
    ppermute x1, waiting for transfers between devices, on_device(): facing_0 = lax.ppermute(near_0, 'row', in_pair)  13.5 us
    pallas_call x4, Pallas kernels, call_on_rows(): pl.pallas_call(kernel, grid=(1,), in_specs=[whole(value) for value in ope...  12.4 us
    ppermute x1, waiting for transfers between devices, on_device(): behind_1 = lax.ppermute(after(own_1, ahead_1), 'row', behind)  12.1 us
    ppermute x1, waiting for transfers between devices, on_device(): pair_1 = lax.ppermute(own_1, 'row', in_pair)  11.2 us
    ppermute x1, waiting for transfers between devices, on_device(): rest_0 = lax.ppermute(ahead_0, 'row', in_pair)  9.86 us
    pallas_call x1, Pallas kernels, make_tiles(): pl.pallas_call(functools.partial(tiles_kernel, counts=counts), grid_spec=...  9.19 us
    unnamed x20, local copies, waits for them, and re-layouts  7.01 us
    ppermute x10, waiting for transfers between devices, other_col(): return lax.ppermute(value, 'col', [(0, 1), (1, 0)])  4.9 us
  transfers between devices with their start and end apart: 22, of which 12 were waited for; matrix products, arithmetic and copies ran while one was open for 0% of the time, Pallas kernels for 8%

profile of v17, /device:TPU:0, one launch (start us, length us, event | category | flops | bytes accessed | tf_op | source)
XLA Modules:
  0.0 122.1 jit_solution(2247558422701277326)
XLA Ops:
  0.0 1.6 %copy-done = bf16[2,256,2,8,128]{4,3,2,1,0:T(8,128)(2,1)S(1)} copy-done((bf16[2,256,2,8,128]{4,3,2,1,0:T(8,128)(2,1)S(1)}, bf16[2,256,2,8,128]{4,3,2,1,0:T(8,128)(2,1)}, u32[]{:S(2)}) %copy-start) | copy-done | bytes 2097176
  2.3 3.0 %faces.1 = (bf16[2064,128]{1,0:T(8,128)(2,1)S(1)}, bf16[8,256,128]{2,1,0:T(8,128)(2,1)}, bf16[2,256,128]{2,1,0:T(8,128)(2,1)}, bf16[8,256,128]{2,1,0:T(8,128)(2,...) custom-call(bf16[2,256,2,8,128]{4,3,2,1,0:T(8,128)(2,1)S(1)} %copy-done, s32[8,128]{1,0:T(8,128)S(1)} %bitcast.19), custom_call_target="tpu_custom_call" | custom-call | flops 1 | bytes 1 | tf_op jit(solution)/shard_map/faces/pallas_call | solution.py:79
  5.3 3.0 %collective-permute-start = (bf16[2064,128]{1,0:T(8,128)(2,1)S(1)}, bf16[2064,128]{1,0:T(8,128)(2,1)S(1)}, u32[]{:S(2)}, u32[]{:S(2)}) collective-permute-start(bf16[2064,128]{1,0:T(8,128)(2,1)S(1)} %get-tuple-element.26.near_ref), channel_id=1, source_target_pairs={{0,2},{2,0},{4,6},{6,4},{8,10},{10,8},{12,14},{14,12},{1,3},{3,1},... | collective-permute-start | bytes 1585160 | tf_op jit(solution)/shard_map/ppermute | solution.py:403
  9.0 1.5 %collective-permute-start.4 = (bf16[8,256,128]{2,1,0:T(8,128)(2,1)S(1)}, bf16[8,256,128]{2,1,0:T(8,128)(2,1)S(1)}, u32[]{:S(2)}, u32[]{:S(2)}) collective-permute-start(bf16[8,256,128]{2,1,0:T(8,128)(2,1)S(1)} %get-tuple-element.29.outer_ref), channel_id=1, source_target_pairs={{2,6},{4,0},{6,10},{8,4},{10,14},{12,8},{3,7},{5,1},{7,11},{9,5},{... | collective-permute-start | bytes 1572872 | tf_op jit(solution)/shard_map/ppermute | solution.py:405
  11.1 1.0 collective-permute-done.2.edge_ref
  12.1 5.2 %inner_blur.1.inner_ref = f32[256,1024]{1,0:T(8,128)S(1)} custom-call(bf16[8,256,128]{2,1,0:T(8,128)(2,1)S(1)} %get-tuple-element.28.near_ref, bf16[8,256,128]{2,1,0:T(8,128)(2,1)S(1)} %get-tuple-element.29.outer_ref, bf16[2,256,128]{2,1,0:T(8,128)(2,1)S(1)} %collective-permute-done.1.edge_ref, s32[8,128]{1,0:T(8,128)S(1)} %bitcast.20), custom_call_target="tpu_custom_call" | custom-call | flops 1 | bytes 1 | tf_op jit(solution)/shard_map/inner_blur/pallas_call | solution.py:223
  17.3 13.5 %collective-permute-done.facing_ref = bf16[2064,128]{1,0:T(8,128)(2,1)S(1)} collective-permute-done((bf16[2064,128]{1,0:T(8,128)(2,1)S(1)}, bf16[2064,128]{1,0:T(8,128)(2,1)S(1)}, u32[]{:S(2)}, u32[]{:S(2)}) %collective-permute-start) | collective-permute-done | bytes 528416 | tf_op jit(solution)/shard_map/ppermute | solution.py:403
  30.8 4.1 %collective-permute-done.4.beyond_ref = bf16[8,256,128]{2,1,0:T(8,128)(2,1)S(1)} collective-permute-done((bf16[8,256,128]{2,1,0:T(8,128)(2,1)S(1)}, bf16[8,256,128]{2,1,0:T(8,128)(2,1)S(1)}, u32[]{:S(2)}, u32[]{:S(2)}) %collective-permute-start.4) | collective-permute-done | bytes 524320 | tf_op jit(solution)/shard_map/ppermute | solution.py:405
  35.1 1.4 %collective-permute-done.5.corner_ref = bf16[3,256,128]{2,1,0:T(8,128)(2,1)S(1)} collective-permute-done((bf16[3,256,128]{2,1,0:T(8,128)(2,1)S(1)}, bf16[3,256,128]{2,1,0:T(8,128)(2,1)S(1)}, u32[]{:S(2)}, u32[]{:S(2)}) %collective-permute-start.5) | collective-permute-done | bytes 196640 | tf_op jit(solution)/shard_map/ppermute | solution.py:359
  36.5 2.4 %halo_blur.1 = bf16[256,1024]{1,0:T(8,128)(2,1)S(1)} custom-call(bf16[8,256,128]{2,1,0:T(8,128)(2,1)S(1)} %get-tuple-element.28.near_ref, bf16[8,256,128]{2,1,0:T(8,128)(2,1)S(1)} %collective-permute-done.4.beyond_ref, bf16[2,256,128]{2,1,0:T(8,128)(2,1)S(1)} %collective-permute-done.1.edge_ref, bf16[3,256,128]{2,1,0:T(8,128)(2,1)S(1)} %collective-permute-done.5.corner_ref, ...), custom_call_target="tpu_custom_call" | custom-call | flops 1 | bytes 1 | tf_op jit(solution)/shard_map/halo_blur/pallas_call | solution.py:223
  39.7 4.4 %blur_score_pick.1 = bf16[256,1024]{1,0:T(8,128)(2,1)S(1)} custom-call(bf16[2064,128]{1,0:T(8,128)(2,1)S(1)} %get-tuple-element.26.near_ref, bf16[8,256,128]{2,1,0:T(8,128)(2,1)} %get-tuple-element.27.outer_ref, bf16[2064,128]{1,0:T(8,128)(2,1)S(1)} %collective-permute-done.facing_ref, bf16[8,256,128]{2,1,0:T(8,128)(2,1)S(1)} %collective-permute-done.3.across_ref, ...), custom_call_target="tpu_custom_call" | custom-call | flops 1 | bytes 1 | tf_op jit(solution)/shard_map/blur_score_pick/pallas_call | solution.py:223
  44.0 4.6 %collective-permute-start.6 = (bf16[256,1024]{1,0:T(8,128)(2,1)S(1)}, bf16[256,1024]{1,0:T(8,128)(2,1)S(1)}, u32[]{:S(2)}, u32[]{:S(2)}) collective-permute-start(bf16[256,1024]{1,0:T(8,128)(2,1)S(1)} %blur_score_pick.1), channel_id=1, source_target_pairs={{4,0},{14,2},{8,4},{2,6},{12,8},{6,10},{0,12},{10,14},{5,1},{15,3}... | collective-permute-start | bytes 1572872 | tf_op jit(solution)/shard_map/ppermute | solution.py:416
  48.6 4.3 %collective-permute-done.7.halo_ref = bf16[256,1024]{1,0:T(8,128)(2,1)S(1)} collective-permute-done((bf16[256,1024]{1,0:T(8,128)(2,1)S(1)}, bf16[256,1024]{1,0:T(8,128)(2,1)S(1)}, u32[]{:S(2)}, u32[]{:S(2)}) %collective-permute-start.7) | collective-permute-done | bytes 524320 | tf_op jit(solution)/shard_map/ppermute | solution.py:413
  54.1 1.4 %collective-permute-start.13 = (bf16[256,1024]{1,0:T(8,128)(2,1)S(1)}, bf16[256,1024]{1,0:T(8,128)(2,1)S(1)}, u32[]{:S(2)}, u32[]{:S(2)}) collective-permute-start(bf16[256,1024]{1,0:T(8,128)(2,1)S(1)} %join_score.1), channel_id=1, source_target_pairs={{0,2},{2,0},{4,6},{6,4},{8,10},{10,8},{12,14},{14,12},{1,3},{3,1},... | collective-permute-start | bytes 1572872 | tf_op jit(solution)/shard_map/ppermute | solution.py:420
  55.5 4.3 %collective-permute-done.6 = bf16[256,1024]{1,0:T(8,128)(2,1)S(1)} collective-permute-done((bf16[256,1024]{1,0:T(8,128)(2,1)S(1)}, bf16[256,1024]{1,0:T(8,128)(2,1)S(1)}, u32[]{:S(2)}, u32[]{:S(2)}) %collective-permute-start.6) | collective-permute-done | bytes 524320 | tf_op jit(solution)/shard_map/ppermute | solution.py:416
  59.8 1.1 collective-permute-start.11
  60.9 3.2 %collective-permute-start.12 = (bf16[256,1024]{1,0:T(8,128)(2,1)S(1)}, bf16[256,1024]{1,0:T(8,128)(2,1)S(1)}, u32[]{:S(2)}, u32[]{:S(2)}) collective-permute-start(bf16[256,1024]{1,0:T(8,128)(2,1)S(1)} %join_score.1), channel_id=1, source_target_pairs={{4,0},{14,2},{8,4},{2,6},{12,8},{6,10},{0,12},{10,14},{5,1},{15,3}... | collective-permute-start | bytes 1572872 | tf_op jit(solution)/shard_map/ppermute | solution.py:421
  64.1 3.7 %collective-permute-done.8 = bf16[256,1024]{1,0:T(8,128)(2,1)S(1)} collective-permute-done((bf16[256,1024]{1,0:T(8,128)(2,1)S(1)}, bf16[256,1024]{1,0:T(8,128)(2,1)S(1)}, u32[]{:S(2)}, u32[]{:S(2)}) %collective-permute-start.8) | collective-permute-done | bytes 524320 | tf_op jit(solution)/shard_map/ppermute | solution.py:419
  67.8 11.2 %collective-permute-done.13 = bf16[256,1024]{1,0:T(8,128)(2,1)S(1)} collective-permute-done((bf16[256,1024]{1,0:T(8,128)(2,1)S(1)}, bf16[256,1024]{1,0:T(8,128)(2,1)S(1)}, u32[]{:S(2)}, u32[]{:S(2)}) %collective-permute-start.13) | collective-permute-done | bytes 524320 | tf_op jit(solution)/shard_map/ppermute | solution.py:420
  80.5 9.9 %collective-permute-done.11 = bf16[256,1024]{1,0:T(8,128)(2,1)} collective-permute-done((bf16[256,1024]{1,0:T(8,128)(2,1)S(1)}, bf16[256,1024]{1,0:T(8,128)(2,1)}, u32[]{:S(2)}, u32[]{:S(2)}) %collective-permute-start.11) | collective-permute-done | bytes 524320 | tf_op jit(solution)/shard_map/ppermute | solution.py:424
  90.4 1.9 %collective-permute-start.20 = (bf16[256,1024]{1,0:T(8,128)(2,1)S(1)}, bf16[256,1024]{1,0:T(8,128)(2,1)}, u32[]{:S(2)}, u32[]{:S(2)}) collective-permute-start(bf16[256,1024]{1,0:T(8,128)(2,1)S(1)} %join_score.1), channel_id=1, source_target_pairs={{0,4},{2,14},{4,8},{6,2},{8,12},{10,6},{12,0},{14,10},{1,5},{3,15}... | collective-permute-start | bytes 1572872 | tf_op jit(solution)/shard_map/ppermute | solution.py:431
  94.5 12.1 %collective-permute-done.20 = bf16[256,1024]{1,0:T(8,128)(2,1)} collective-permute-done((bf16[256,1024]{1,0:T(8,128)(2,1)S(1)}, bf16[256,1024]{1,0:T(8,128)(2,1)}, u32[]{:S(2)}, u32[]{:S(2)}) %collective-permute-start.20) | collective-permute-done | bytes 524320 | tf_op jit(solution)/shard_map/ppermute | solution.py:431
  107.2 1.7 %collective-permute-done.21.refs_16_ = bf16[1,256,1024]{2,1,0:T(8,128)(2,1)} collective-permute-done((bf16[1,256,1024]{2,1,0:T(8,128)(2,1)}, bf16[1,256,1024]{2,1,0:T(8,128)(2,1)}, u32[]{:S(2)}, u32[]{:S(2)}) %collective-permute-start.21) | collective-permute-done | bytes 524320 | tf_op jit(solution)/shard_map/ppermute | solution.py:359
  112.7 9.2 %tiles.1 = bf16[8,16,2,128,128]{4,3,2,1,0:T(8,128)(2,1)} custom-call(s32[8,16]{1,0:T(8,128)S(1)} %get-tuple-element.48.refs_0_, s32[8,16]{1,0:T(8,128)S(1)} %get-tuple-element.47.refs_1_, s32[8,16]{1,0:T(8,128)S(1)} %fusion.17.refs_2_, bf16[3,256,1024]{2,1,0:T(8,128)(2,1)S(1)} %pad_maximum_fusion.refs_3_, ...), custom_call_target="tpu_custom_call" | custom-call | flops 1 | bytes 1 | tf_op jit(solution)/shard_map/tiles/pallas_call | solution.py:326
  (54 shorter events, 12.2 us)
Async XLA Ops:
  5.3 25.5 %collective-permute-start = (bf16[2064,128]{1,0:T(8,128)(2,1)S(1)}, bf16[2064,128]{1,0:T(8,128)(2,1)S(1)}, u32[]{:S(2)}, u32[]{:S(2)}) collective-permute-start(bf16[2064,128]{1,0:T(8,128)(2,1)S(1)} %get-tuple-element.26.near_ref), channel_id=1, source_target_pairs={{0,2},{2,0},{4,6},{6,4},{8,10},{10,8},{12,14},{14,12},{1,3},{3,1},... | collective-permute-start | bytes 1585160 | tf_op jit(solution)/shard_map/ppermute | solution.py:403
  8.3 9.0 %collective-permute-start.3 = (bf16[8,256,128]{2,1,0:T(8,128)(2,1)}, bf16[8,256,128]{2,1,0:T(8,128)(2,1)S(1)}, u32[]{:S(2)}, u32[]{:S(2)}) collective-permute-start(bf16[8,256,128]{2,1,0:T(8,128)(2,1)} %get-tuple-element.27.outer_ref), channel_id=1, source_target_pairs={{2,4},{4,2},{6,8},{8,6},{10,12},{12,10},{3,5},{5,3},{7,9},{9,7},{1... | collective-permute-start | bytes 1572872 | tf_op jit(solution)/shard_map/ppermute | solution.py:404
  9.0 25.9 %collective-permute-start.4 = (bf16[8,256,128]{2,1,0:T(8,128)(2,1)S(1)}, bf16[8,256,128]{2,1,0:T(8,128)(2,1)S(1)}, u32[]{:S(2)}, u32[]{:S(2)}) collective-permute-start(bf16[8,256,128]{2,1,0:T(8,128)(2,1)S(1)} %get-tuple-element.29.outer_ref), channel_id=1, source_target_pairs={{2,6},{4,0},{6,10},{8,4},{10,14},{12,8},{3,7},{5,1},{7,11},{9,5},{... | collective-permute-start | bytes 1572872 | tf_op jit(solution)/shard_map/ppermute | solution.py:405
  10.5 1.6 %collective-permute-start.2 = (bf16[2,256,128]{2,1,0:T(8,128)(2,1)}, bf16[2,256,128]{2,1,0:T(8,128)(2,1)S(1)}, u32[]{:S(2)}, u32[]{:S(2)}) collective-permute-start(bf16[2,256,128]{2,1,0:T(8,128)(2,1)} %get-tuple-element.31), channel_id=1, source_target_pairs={{0,1},{1,0},{2,3},{3,2},{4,5},{5,4},{6,7},{7,6},{8,9},{9,8},{10,11... | collective-permute-start | bytes 393224 | tf_op jit(solution)/shard_map/ppermute | solution.py:359
  10.6 1.5 %collective-permute-start.1 = (bf16[2,256,128]{2,1,0:T(8,128)(2,1)S(1)}, bf16[2,256,128]{2,1,0:T(8,128)(2,1)S(1)}, u32[]{:S(2)}, u32[]{:S(2)}) collective-permute-start(bf16[2,256,128]{2,1,0:T(8,128)(2,1)S(1)} %get-tuple-element.30), channel_id=1, source_target_pairs={{0,1},{1,0},{2,3},{3,2},{4,5},{5,4},{6,7},{7,6},{8,9},{9,8},{10,11... | collective-permute-start | bytes 393224 | tf_op jit(solution)/shard_map/ppermute | solution.py:359
  35.0 1.5 %collective-permute-start.5 = (bf16[3,256,128]{2,1,0:T(8,128)(2,1)S(1)}, bf16[3,256,128]{2,1,0:T(8,128)(2,1)S(1)}, u32[]{:S(2)}, u32[]{:S(2)}) collective-permute-start(bf16[3,256,128]{2,1,0:T(8,128)(2,1)S(1)} %pad_maximum_fusion.2), channel_id=1, source_target_pairs={{0,1},{1,0},{2,3},{3,2},{4,5},{5,4},{6,7},{7,6},{8,9},{9,8},{10,11... | collective-permute-start | bytes 589832 | tf_op jit(solution)/shard_map/ppermute | solution.py:359
  38.9 14.0 %collective-permute-start.7 = (bf16[256,1024]{1,0:T(8,128)(2,1)S(1)}, bf16[256,1024]{1,0:T(8,128)(2,1)S(1)}, u32[]{:S(2)}, u32[]{:S(2)}) collective-permute-start(bf16[256,1024]{1,0:T(8,128)(2,1)S(1)} %halo_blur.1), channel_id=1, source_target_pairs={{0,2},{2,0},{4,6},{6,4},{8,10},{10,8},{12,14},{14,12},{1,3},{3,1},... | collective-permute-start | bytes 1572872 | tf_op jit(solution)/shard_map/ppermute | solution.py:413
  44.0 15.8 %collective-permute-start.6 = (bf16[256,1024]{1,0:T(8,128)(2,1)S(1)}, bf16[256,1024]{1,0:T(8,128)(2,1)S(1)}, u32[]{:S(2)}, u32[]{:S(2)}) collective-permute-start(bf16[256,1024]{1,0:T(8,128)(2,1)S(1)} %blur_score_pick.1), channel_id=1, source_target_pairs={{4,0},{14,2},{8,4},{2,6},{12,8},{6,10},{0,12},{10,14},{5,1},{15,3}... | collective-permute-start | bytes 1572872 | tf_op jit(solution)/shard_map/ppermute | solution.py:416
  52.9 14.9 %collective-permute-start.8 = (bf16[256,1024]{1,0:T(8,128)(2,1)S(1)}, bf16[256,1024]{1,0:T(8,128)(2,1)S(1)}, u32[]{:S(2)}, u32[]{:S(2)}) collective-permute-start(bf16[256,1024]{1,0:T(8,128)(2,1)S(1)} %blur_score_pick.1), channel_id=1, source_target_pairs={{0,2},{2,0},{4,6},{6,4},{8,10},{10,8},{12,14},{14,12},{1,3},{3,1},... | collective-permute-start | bytes 1572872 | tf_op jit(solution)/shard_map/ppermute | solution.py:419
  54.1 24.9 %collective-permute-start.13 = (bf16[256,1024]{1,0:T(8,128)(2,1)S(1)}, bf16[256,1024]{1,0:T(8,128)(2,1)S(1)}, u32[]{:S(2)}, u32[]{:S(2)}) collective-permute-start(bf16[256,1024]{1,0:T(8,128)(2,1)S(1)} %join_score.1), channel_id=1, source_target_pairs={{0,2},{2,0},{4,6},{6,4},{8,10},{10,8},{12,14},{14,12},{1,3},{3,1},... | collective-permute-start | bytes 1572872 | tf_op jit(solution)/shard_map/ppermute | solution.py:420
  59.8 30.5 %collective-permute-start.11 = (bf16[256,1024]{1,0:T(8,128)(2,1)S(1)}, bf16[256,1024]{1,0:T(8,128)(2,1)}, u32[]{:S(2)}, u32[]{:S(2)}) collective-permute-start(bf16[256,1024]{1,0:T(8,128)(2,1)S(1)} %collective-permute-done.6), channel_id=1, source_target_pairs={{0,2},{2,0},{4,6},{6,4},{8,10},{10,8},{12,14},{14,12},{1,3},{3,1},... | collective-permute-start | bytes 1572872 | tf_op jit(solution)/shard_map/ppermute | solution.py:424
  60.9 18.9 %collective-permute-start.12 = (bf16[256,1024]{1,0:T(8,128)(2,1)S(1)}, bf16[256,1024]{1,0:T(8,128)(2,1)S(1)}, u32[]{:S(2)}, u32[]{:S(2)}) collective-permute-start(bf16[256,1024]{1,0:T(8,128)(2,1)S(1)} %join_score.1), channel_id=1, source_target_pairs={{4,0},{14,2},{8,4},{2,6},{12,8},{6,10},{0,12},{10,14},{5,1},{15,3}... | collective-permute-start | bytes 1572872 | tf_op jit(solution)/shard_map/ppermute | solution.py:421
  64.1 26.3 %collective-permute-start.10 = (bf16[256,1024]{1,0:T(8,128)(2,1)S(1)}, bf16[256,1024]{1,0:T(8,128)(2,1)S(1)}, u32[]{:S(2)}, u32[]{:S(2)}) collective-permute-start(bf16[256,1024]{1,0:T(8,128)(2,1)S(1)} %blur_score_pick.1), channel_id=1, source_target_pairs={{0,4},{2,14},{4,8},{6,2},{8,12},{10,6},{12,0},{14,10},{1,5},{3,15}... | collective-permute-start | bytes 1572872 | tf_op jit(solution)/shard_map/ppermute | solution.py:423
  79.0 13.4 %collective-permute-start.17 = (bf16[1,256,1024]{2,1,0:T(8,128)(2,1)S(1)}, bf16[1,256,1024]{2,1,0:T(8,128)(2,1)S(1)}, u32[]{:S(2)}, u32[]{:S(2)}) collective-permute-start(bf16[1,256,1024]{2,1,0:T(8,128)(2,1)S(1)} %bitcast.15), channel_id=1, source_target_pairs={{0,1},{1,0},{2,3},{3,2},{4,5},{5,4},{6,7},{7,6},{8,9},{9,8},{10,11... | collective-permute-start | bytes 1572872 | tf_op jit(solution)/shard_map/ppermute | solution.py:359
  79.2 27.9 %copy-start.9 = (s32[8,16]{1,0:T(8,128)S(1)}, s32[8,16]{1,0:T(8,128)}, u32[]{:S(2)}) copy-start(s32[8,16]{1,0:T(8,128)} %param.5) | copy-start | bytes 1540
  79.2 30.4 %collective-permute-start.9 = (bf16[3,256,1024]{2,1,0:T(8,128)(2,1)S(1)}, bf16[3,256,1024]{2,1,0:T(8,128)(2,1)}, u32[]{:S(2)}, u32[]{:S(2)}) collective-permute-start(bf16[3,256,1024]{2,1,0:T(8,128)(2,1)S(1)} %pad_maximum_fusion.refs_3_), channel_id=1, source_target_pairs={{0,1},{1,0},{2,3},{3,2},{4,5},{5,4},{6,7},{7,6},{8,9},{9,8},{10,11... | collective-permute-start | bytes 4718600 | tf_op jit(solution)/shard_map/ppermute | solution.py:359
  79.8 26.8 %collective-permute-start.18 = (bf16[256,1024]{1,0:T(8,128)(2,1)S(1)}, bf16[256,1024]{1,0:T(8,128)(2,1)}, u32[]{:S(2)}, u32[]{:S(2)}) collective-permute-start(bf16[256,1024]{1,0:T(8,128)(2,1)S(1)} %collective-permute-done.12), channel_id=1, source_target_pairs={{0,2},{2,0},{4,6},{6,4},{8,10},{10,8},{12,14},{14,12},{1,3},{3,1},... | collective-permute-start | bytes 1572872 | tf_op jit(solution)/shard_map/ppermute | solution.py:430
  90.3 16.2 %copy-start.1 = (bf16[256,1024]{1,0:T(8,128)(2,1)}, bf16[256,1024]{1,0:T(8,128)(2,1)S(1)}, u32[]{:S(2)}) copy-start(bf16[256,1024]{1,0:T(8,128)(2,1)S(1)} %collective-permute-done.10) | copy-start | bytes 1572868
  90.3 2.8 %collective-permute-start.14 = (bf16[1,256,1024]{2,1,0:T(8,128)(2,1)S(1)}, bf16[1,256,1024]{2,1,0:T(8,128)(2,1)S(1)}, u32[]{:S(2)}, u32[]{:S(2)}) collective-permute-start(bf16[1,256,1024]{2,1,0:T(8,128)(2,1)S(1)} %bitcast.17), channel_id=1, source_target_pairs={{0,1},{1,0},{2,3},{3,2},{4,5},{5,4},{6,7},{7,6},{8,9},{9,8},{10,11... | collective-permute-start | bytes 1572872 | tf_op jit(solution)/shard_map/ppermute | solution.py:359
  90.4 16.2 %collective-permute-start.20 = (bf16[256,1024]{1,0:T(8,128)(2,1)S(1)}, bf16[256,1024]{1,0:T(8,128)(2,1)}, u32[]{:S(2)}, u32[]{:S(2)}) collective-permute-start(bf16[256,1024]{1,0:T(8,128)(2,1)S(1)} %join_score.1), channel_id=1, source_target_pairs={{0,4},{2,14},{4,8},{6,2},{8,12},{10,6},{12,0},{14,10},{1,5},{3,15}... | collective-permute-start | bytes 1572872 | tf_op jit(solution)/shard_map/ppermute | solution.py:431
  93.2 14.0 %collective-permute-start.16 = (bf16[2,256,1024]{2,1,0:T(8,128)(2,1)S(1)}, bf16[2,256,1024]{2,1,0:T(8,128)(2,1)}, u32[]{:S(2)}, u32[]{:S(2)}) collective-permute-start(bf16[2,256,1024]{2,1,0:T(8,128)(2,1)S(1)} %pad_maximum_fusion.1.refs_9_), channel_id=1, source_target_pairs={{0,1},{1,0},{2,3},{3,2},{4,5},{5,4},{6,7},{7,6},{8,9},{9,8},{10,11... | collective-permute-start | bytes 3145736 | tf_op jit(solution)/shard_map/ppermute | solution.py:359
  94.0 13.2 %collective-permute-start.15 = (bf16[1,256,1024]{2,1,0:T(8,128)(2,1)}, bf16[1,256,1024]{2,1,0:T(8,128)(2,1)}, u32[]{:S(2)}, u32[]{:S(2)}) collective-permute-start(bf16[1,256,1024]{2,1,0:T(8,128)(2,1)} %bitcast.6.refs_7_), channel_id=1, source_target_pairs={{0,1},{1,0},{2,3},{3,2},{4,5},{5,4},{6,7},{7,6},{8,9},{9,8},{10,11... | collective-permute-start | bytes 1572872 | tf_op jit(solution)/shard_map/ppermute | solution.py:359
  106.6 2.3 %collective-permute-start.21 = (bf16[1,256,1024]{2,1,0:T(8,128)(2,1)}, bf16[1,256,1024]{2,1,0:T(8,128)(2,1)}, u32[]{:S(2)}, u32[]{:S(2)}) collective-permute-start(bf16[1,256,1024]{2,1,0:T(8,128)(2,1)} %bitcast.11.refs_15_), channel_id=1, source_target_pairs={{0,1},{1,0},{2,3},{3,2},{4,5},{5,4},{6,7},{7,6},{8,9},{9,8},{10,11... | collective-permute-start | bytes 1572872 | tf_op jit(solution)/shard_map/ppermute | solution.py:359
  106.6 3.0 %collective-permute-start.19 = (bf16[1,256,1024]{2,1,0:T(8,128)(2,1)}, bf16[1,256,1024]{2,1,0:T(8,128)(2,1)}, u32[]{:S(2)}, u32[]{:S(2)}) collective-permute-start(bf16[1,256,1024]{2,1,0:T(8,128)(2,1)} %bitcast.10.refs_13_), channel_id=1, source_target_pairs={{0,1},{1,0},{2,3},{3,2},{4,5},{5,4},{6,7},{7,6},{8,9},{9,8},{10,11... | collective-permute-start | bytes 1572872 | tf_op jit(solution)/shard_map/ppermute | solution.py:359
  (8 other events, 16.8 us)

commit v18 on v16

--- a/solution.py
+++ b/solution.py
@@ -12,7 +12,7 @@
 SIDE = math.exp(-0.5) / (1.0 + 2.0 * math.exp(-0.5))
 CENTRE = 1.0 / (1.0 + 2.0 * math.exp(-0.5))
 SMALL = pl.CostEstimate(flops=1, bytes_accessed=1, transcendentals=0)
-VMEM_BYTES = 20 * 1024 * 1024
+VMEM_BYTES = 12 * 1024 * 1024
 
 
 def is_even():

time: 117 us -> 117 us (level)
  no operation moved by 1% of the time
where the time goes in v18:
time: 117 us
  waiting for transfers between devices  56.2 us (48%)
  Pallas kernels  27.9 us (24%)
  starting transfers between devices  23.8 us (20%)
  local copies, waits for them, and re-layouts  8.07 us (7%)
    ppermute x1, waiting for transfers between devices, on_device(): facing_0 = lax.ppermute(near_0, 'row', in_pair)  13.5 us
    pallas_call x2, Pallas kernels, make_tiles(): pl.pallas_call(functools.partial(tiles_kernel, sources=count, window=wind...  12.5 us
    pallas_call x4, Pallas kernels, call_on_rows(): pl.pallas_call(kernel, grid=(1,), in_specs=[whole(value) for value in ope...  12.4 us
    ppermute x1, waiting for transfers between devices, on_device(): pair_1 = lax.ppermute(own_1, 'row', in_pair)  11.2 us
    unnamed x24, local copies, waits for them, and re-layouts  8.07 us
    ppermute x1, waiting for transfers between devices, on_device(): pair_0 = lax.ppermute(after(own_0, halo_1), 'row', in_pair)  6.38 us
    ppermute x1, waiting for transfers between devices, on_device(): rest_0 = lax.ppermute(ahead_0, 'row', in_pair)  5.47 us
    ppermute x1, waiting for transfers between devices, on_device(): behind_1 = lax.ppermute(after(own_1, ahead_1), 'row', behind)  4.59 us
  transfers between devices with their start and end apart: 22, of which 11 were waited for; matrix products, arithmetic and copies ran while one was open for 0% of the time, Pallas kernels for 14%

profile of v18, /device:TPU:0, one launch (start us, length us, event | category | flops | bytes accessed | tf_op | source)
XLA Modules:
  0.0 116.8 jit_solution(12405718497756436530)
XLA Ops:
  0.0 1.6 %copy-done = bf16[2,256,2,8,128]{4,3,2,1,0:T(8,128)(2,1)S(1)} copy-done((bf16[2,256,2,8,128]{4,3,2,1,0:T(8,128)(2,1)S(1)}, bf16[2,256,2,8,128]{4,3,2,1,0:T(8,128)(2,1)}, u32[]{:S(2)}) %copy-start) | copy-done | bytes 2097176
  2.3 3.0 %faces.1 = (bf16[2064,128]{1,0:T(8,128)(2,1)S(1)}, bf16[8,256,128]{2,1,0:T(8,128)(2,1)}, bf16[2,256,128]{2,1,0:T(8,128)(2,1)}, bf16[8,256,128]{2,1,0:T(8,128)(2,...) custom-call(bf16[2,256,2,8,128]{4,3,2,1,0:T(8,128)(2,1)S(1)} %copy-done, s32[8,128]{1,0:T(8,128)S(1)} %bitcast.21), custom_call_target="tpu_custom_call" | custom-call | flops 1 | bytes 1 | tf_op jit(solution)/shard_map/faces/pallas_call | solution.py:78
  5.3 3.0 %collective-permute-start.3 = (bf16[2064,128]{1,0:T(8,128)(2,1)S(1)}, bf16[2064,128]{1,0:T(8,128)(2,1)S(1)}, u32[]{:S(2)}, u32[]{:S(2)}) collective-permute-start(bf16[2064,128]{1,0:T(8,128)(2,1)S(1)} %get-tuple-element.31.near_ref), channel_id=1, source_target_pairs={{0,2},{2,0},{4,6},{6,4},{8,10},{10,8},{12,14},{14,12},{1,3},{3,1},... | collective-permute-start | bytes 1585160 | tf_op jit(solution)/shard_map/ppermute | solution.py:396
  9.0 1.5 %collective-permute-start.2 = (bf16[8,256,128]{2,1,0:T(8,128)(2,1)S(1)}, bf16[8,256,128]{2,1,0:T(8,128)(2,1)S(1)}, u32[]{:S(2)}, u32[]{:S(2)}) collective-permute-start(bf16[8,256,128]{2,1,0:T(8,128)(2,1)S(1)} %get-tuple-element.27.outer_ref), channel_id=1, source_target_pairs={{2,6},{4,0},{6,10},{8,4},{10,14},{12,8},{3,7},{5,1},{7,11},{9,5},{... | collective-permute-start | bytes 1572872 | tf_op jit(solution)/shard_map/ppermute | solution.py:398
  12.1 5.2 %inner_blur.1.inner_ref = f32[256,1024]{1,0:T(8,128)S(1)} custom-call(bf16[8,256,128]{2,1,0:T(8,128)(2,1)S(1)} %get-tuple-element.26.near_ref, bf16[8,256,128]{2,1,0:T(8,128)(2,1)S(1)} %get-tuple-element.27.outer_ref, bf16[2,256,128]{2,1,0:T(8,128)(2,1)S(1)} %collective-permute-done.edge_ref, s32[8,128]{1,0:T(8,128)S(1)} %bitcast.22), custom_call_target="tpu_custom_call" | custom-call | flops 1 | bytes 1 | tf_op jit(solution)/shard_map/inner_blur/pallas_call | solution.py:222
  17.3 13.5 %collective-permute-done.3.facing_ref = bf16[2064,128]{1,0:T(8,128)(2,1)S(1)} collective-permute-done((bf16[2064,128]{1,0:T(8,128)(2,1)S(1)}, bf16[2064,128]{1,0:T(8,128)(2,1)S(1)}, u32[]{:S(2)}, u32[]{:S(2)}) %collective-permute-start.3) | collective-permute-done | bytes 528416 | tf_op jit(solution)/shard_map/ppermute | solution.py:396
  30.8 4.1 %collective-permute-done.2.beyond_ref = bf16[8,256,128]{2,1,0:T(8,128)(2,1)S(1)} collective-permute-done((bf16[8,256,128]{2,1,0:T(8,128)(2,1)S(1)}, bf16[8,256,128]{2,1,0:T(8,128)(2,1)S(1)}, u32[]{:S(2)}, u32[]{:S(2)}) %collective-permute-start.2) | collective-permute-done | bytes 524320 | tf_op jit(solution)/shard_map/ppermute | solution.py:398
  35.1 1.4 %collective-permute-done.5.corner_ref = bf16[3,256,128]{2,1,0:T(8,128)(2,1)S(1)} collective-permute-done((bf16[3,256,128]{2,1,0:T(8,128)(2,1)S(1)}, bf16[3,256,128]{2,1,0:T(8,128)(2,1)S(1)}, u32[]{:S(2)}, u32[]{:S(2)}) %collective-permute-start.5) | collective-permute-done | bytes 196640 | tf_op jit(solution)/shard_map/ppermute | solution.py:351
  36.5 2.4 %halo_blur.1 = bf16[256,1024]{1,0:T(8,128)(2,1)S(1)} custom-call(bf16[8,256,128]{2,1,0:T(8,128)(2,1)S(1)} %get-tuple-element.26.near_ref, bf16[8,256,128]{2,1,0:T(8,128)(2,1)S(1)} %collective-permute-done.2.beyond_ref, bf16[2,256,128]{2,1,0:T(8,128)(2,1)S(1)} %collective-permute-done.edge_ref, bf16[3,256,128]{2,1,0:T(8,128)(2,1)S(1)} %collective-permute-done.5.corner_ref, ...), custom_call_target="tpu_custom_call" | custom-call | flops 1 | bytes 1 | tf_op jit(solution)/shard_map/halo_blur/pallas_call | solution.py:222
  39.7 4.4 %blur_score_pick.1 = bf16[256,1024]{1,0:T(8,128)(2,1)S(1)} custom-call(bf16[2064,128]{1,0:T(8,128)(2,1)S(1)} %get-tuple-element.31.near_ref, bf16[8,256,128]{2,1,0:T(8,128)(2,1)} %get-tuple-element.33.outer_ref, bf16[2064,128]{1,0:T(8,128)(2,1)S(1)} %collective-permute-done.3.facing_ref, bf16[8,256,128]{2,1,0:T(8,128)(2,1)S(1)} %collective-permute-done.4.across_ref, ...), custom_call_target="tpu_custom_call" | custom-call | flops 1 | bytes 1 | tf_op jit(solution)/shard_map/blur_score_pick/pallas_call | solution.py:222
  44.0 4.6 %collective-permute-start.10 = (bf16[256,1024]{1,0:T(8,128)(2,1)S(1)}, bf16[256,1024]{1,0:T(8,128)(2,1)S(1)}, u32[]{:S(2)}, u32[]{:S(2)}) collective-permute-start(bf16[256,1024]{1,0:T(8,128)(2,1)S(1)} %blur_score_pick.1), channel_id=1, source_target_pairs={{4,0},{14,2},{8,4},{2,6},{12,8},{6,10},{0,12},{10,14},{5,1},{15,3}... | collective-permute-start | bytes 1572872 | tf_op jit(solution)/shard_map/ppermute | solution.py:409
  48.6 4.3 %collective-permute-done.6.halo_ref = bf16[256,1024]{1,0:T(8,128)(2,1)S(1)} collective-permute-done((bf16[256,1024]{1,0:T(8,128)(2,1)S(1)}, bf16[256,1024]{1,0:T(8,128)(2,1)S(1)}, u32[]{:S(2)}, u32[]{:S(2)}) %collective-permute-start.6) | collective-permute-done | bytes 524320 | tf_op jit(solution)/shard_map/ppermute | solution.py:406
  54.1 1.4 %collective-permute-start.8 = (bf16[256,1024]{1,0:T(8,128)(2,1)S(1)}, bf16[256,1024]{1,0:T(8,128)(2,1)S(1)}, u32[]{:S(2)}, u32[]{:S(2)}) collective-permute-start(bf16[256,1024]{1,0:T(8,128)(2,1)S(1)} %join_score.1), channel_id=1, source_target_pairs={{0,2},{2,0},{4,6},{6,4},{8,10},{10,8},{12,14},{14,12},{1,3},{3,1},... | collective-permute-start | bytes 1572872 | tf_op jit(solution)/shard_map/ppermute | solution.py:413
  55.5 3.5 %collective-permute-start.7 = (bf16[256,1024]{1,0:T(8,128)(2,1)S(1)}, bf16[256,1024]{1,0:T(8,128)(2,1)S(1)}, u32[]{:S(2)}, u32[]{:S(2)}) collective-permute-start(bf16[256,1024]{1,0:T(8,128)(2,1)S(1)} %join_score.1), channel_id=1, source_target_pairs={{4,0},{14,2},{8,4},{2,6},{12,8},{6,10},{0,12},{10,14},{5,1},{15,3}... | collective-permute-start | bytes 1572872 | tf_op jit(solution)/shard_map/ppermute | solution.py:414
  59.0 1.9 %collective-permute-done.10 = bf16[256,1024]{1,0:T(8,128)(2,1)S(1)} collective-permute-done((bf16[256,1024]{1,0:T(8,128)(2,1)S(1)}, bf16[256,1024]{1,0:T(8,128)(2,1)S(1)}, u32[]{:S(2)}, u32[]{:S(2)}) %collective-permute-start.10) | collective-permute-done | bytes 524320 | tf_op jit(solution)/shard_map/ppermute | solution.py:409
  61.4 6.4 %collective-permute-done.9 = bf16[256,1024]{1,0:T(8,128)(2,1)S(1)} collective-permute-done((bf16[256,1024]{1,0:T(8,128)(2,1)S(1)}, bf16[256,1024]{1,0:T(8,128)(2,1)S(1)}, u32[]{:S(2)}, u32[]{:S(2)}) %collective-permute-start.9) | collective-permute-done | bytes 524320 | tf_op jit(solution)/shard_map/ppermute | solution.py:412
  67.8 11.2 %collective-permute-done.8 = bf16[256,1024]{1,0:T(8,128)(2,1)S(1)} collective-permute-done((bf16[256,1024]{1,0:T(8,128)(2,1)S(1)}, bf16[256,1024]{1,0:T(8,128)(2,1)S(1)}, u32[]{:S(2)}, u32[]{:S(2)}) %collective-permute-start.8) | collective-permute-done | bytes 524320 | tf_op jit(solution)/shard_map/ppermute | solution.py:413
  79.3 1.9 %collective-permute-start.15 = (bf16[256,1024]{1,0:T(8,128)(2,1)S(1)}, bf16[256,1024]{1,0:T(8,128)(2,1)}, u32[]{:S(2)}, u32[]{:S(2)}) collective-permute-start(bf16[256,1024]{1,0:T(8,128)(2,1)S(1)} %join_score.1), channel_id=1, source_target_pairs={{0,4},{2,14},{4,8},{6,2},{8,12},{10,6},{12,0},{14,10},{1,5},{3,15}... | collective-permute-start | bytes 1572872 | tf_op jit(solution)/shard_map/ppermute | solution.py:424
  81.2 3.6 %collective-permute-start.13 = (bf16[256,1024]{1,0:T(8,128)(2,1)S(1)}, bf16[256,1024]{1,0:T(8,128)(2,1)}, u32[]{:S(2)}, u32[]{:S(2)}) collective-permute-start(bf16[256,1024]{1,0:T(8,128)(2,1)S(1)} %collective-permute-done.7), channel_id=1, source_target_pairs={{0,2},{2,0},{4,6},{6,4},{8,10},{10,8},{12,14},{14,12},{1,3},{3,1},... | collective-permute-start | bytes 1572872 | tf_op jit(solution)/shard_map/ppermute | solution.py:423
  84.8 5.5 %collective-permute-done.19 = bf16[256,1024]{1,0:T(8,128)(2,1)S(1)} collective-permute-done((bf16[256,1024]{1,0:T(8,128)(2,1)S(1)}, bf16[256,1024]{1,0:T(8,128)(2,1)S(1)}, u32[]{:S(2)}, u32[]{:S(2)}) %collective-permute-start.19) | collective-permute-done | bytes 524320 | tf_op jit(solution)/shard_map/ppermute | solution.py:417
  90.9 4.6 %collective-permute-done.15 = bf16[256,1024]{1,0:T(8,128)(2,1)} collective-permute-done((bf16[256,1024]{1,0:T(8,128)(2,1)S(1)}, bf16[256,1024]{1,0:T(8,128)(2,1)}, u32[]{:S(2)}, u32[]{:S(2)}) %collective-permute-start.15) | collective-permute-done | bytes 524320 | tf_op jit(solution)/shard_map/ppermute | solution.py:424
  97.7 2.2 %collective-permute-done.13 = bf16[256,1024]{1,0:T(8,128)(2,1)} collective-permute-done((bf16[256,1024]{1,0:T(8,128)(2,1)S(1)}, bf16[256,1024]{1,0:T(8,128)(2,1)}, u32[]{:S(2)}, u32[]{:S(2)}) %collective-permute-start.13) | collective-permute-done | bytes 524320 | tf_op jit(solution)/shard_map/ppermute | solution.py:423
  104.1 5.9 %tiles.2.refs_8_ = bf16[8,16,2,128,128]{4,3,2,1,0:T(8,128)(2,1)} custom-call(s32[8,16]{1,0:T(8,128)S(1)} %get-tuple-element.47.place_ref, s32[8,16]{1,0:T(8,128)S(1)} %fusion.17.present_ref, bf16[3,256,1024]{2,1,0:T(8,128)(2,1)S(1)} %pad_maximum_fusion.refs_0_, bf16[3,256,1024]{2,1,0:T(8,128)(2,1)} %collective-permute-done.17.refs_1_, ...), custom_call_target="tpu_custom_call" | custom-call | flops 1 | bytes 1 | tf_op jit(solution)/shard_map/tiles/pallas_call | solution.py:317
  110.1 6.5 %tiles.3 = bf16[8,16,2,128,128]{4,3,2,1,0:T(8,128)(2,1)} custom-call(s32[8,16]{1,0:T(8,128)S(1)} %get-tuple-element.48.place_ref, s32[8,16]{1,0:T(8,128)S(1)} %fusion.17.present_ref, bf16[2,256,1024]{2,1,0:T(8,128)(2,1)S(1)} %pad_maximum_fusion.1.refs_0_, bf16[2,256,1024]{2,1,0:T(8,128)(2,1)} %collective-permute-done.11.refs_1_, ...), custom_call_target="tpu_custom_call", output_to_operand_aliasing={{}: (10, {})} | custom-call | flops 1 | bytes 1 | tf_op jit(solution)/shard_map/tiles/pallas_call | solution.py:317
  (59 shorter events, 12.8 us)
Async XLA Ops:
  2.3 9.8 %copy-start.10 = (s32[1024]{0:T(1024)S(1)}, s32[1024]{0:T(1024)}, u32[]{:S(2)}) copy-start(s32[1024]{0:T(1024)} %param.4) | copy-start | bytes 12292
  5.3 25.5 %collective-permute-start.3 = (bf16[2064,128]{1,0:T(8,128)(2,1)S(1)}, bf16[2064,128]{1,0:T(8,128)(2,1)S(1)}, u32[]{:S(2)}, u32[]{:S(2)}) collective-permute-start(bf16[2064,128]{1,0:T(8,128)(2,1)S(1)} %get-tuple-element.31.near_ref), channel_id=1, source_target_pairs={{0,2},{2,0},{4,6},{6,4},{8,10},{10,8},{12,14},{14,12},{1,3},{3,1},... | collective-permute-start | bytes 1585160 | tf_op jit(solution)/shard_map/ppermute | solution.py:396
  8.3 9.0 %collective-permute-start.4 = (bf16[8,256,128]{2,1,0:T(8,128)(2,1)}, bf16[8,256,128]{2,1,0:T(8,128)(2,1)S(1)}, u32[]{:S(2)}, u32[]{:S(2)}) collective-permute-start(bf16[8,256,128]{2,1,0:T(8,128)(2,1)} %get-tuple-element.33.outer_ref), channel_id=1, source_target_pairs={{2,4},{4,2},{6,8},{8,6},{10,12},{12,10},{3,5},{5,3},{7,9},{9,7},{1... | collective-permute-start | bytes 1572872 | tf_op jit(solution)/shard_map/ppermute | solution.py:397
  9.0 25.9 %collective-permute-start.2 = (bf16[8,256,128]{2,1,0:T(8,128)(2,1)S(1)}, bf16[8,256,128]{2,1,0:T(8,128)(2,1)S(1)}, u32[]{:S(2)}, u32[]{:S(2)}) collective-permute-start(bf16[8,256,128]{2,1,0:T(8,128)(2,1)S(1)} %get-tuple-element.27.outer_ref), channel_id=1, source_target_pairs={{2,6},{4,0},{6,10},{8,4},{10,14},{12,8},{3,7},{5,1},{7,11},{9,5},{... | collective-permute-start | bytes 1572872 | tf_op jit(solution)/shard_map/ppermute | solution.py:398
  10.5 1.6 %collective-permute-start.1 = (bf16[2,256,128]{2,1,0:T(8,128)(2,1)}, bf16[2,256,128]{2,1,0:T(8,128)(2,1)S(1)}, u32[]{:S(2)}, u32[]{:S(2)}) collective-permute-start(bf16[2,256,128]{2,1,0:T(8,128)(2,1)} %get-tuple-element.29), channel_id=1, source_target_pairs={{0,1},{1,0},{2,3},{3,2},{4,5},{5,4},{6,7},{7,6},{8,9},{9,8},{10,11... | collective-permute-start | bytes 393224 | tf_op jit(solution)/shard_map/ppermute | solution.py:351
  10.6 1.5 %collective-permute-start = (bf16[2,256,128]{2,1,0:T(8,128)(2,1)S(1)}, bf16[2,256,128]{2,1,0:T(8,128)(2,1)S(1)}, u32[]{:S(2)}, u32[]{:S(2)}) collective-permute-start(bf16[2,256,128]{2,1,0:T(8,128)(2,1)S(1)} %get-tuple-element.28), channel_id=1, source_target_pairs={{0,1},{1,0},{2,3},{3,2},{4,5},{5,4},{6,7},{7,6},{8,9},{9,8},{10,11... | collective-permute-start | bytes 393224 | tf_op jit(solution)/shard_map/ppermute | solution.py:351
  35.0 1.5 %collective-permute-start.5 = (bf16[3,256,128]{2,1,0:T(8,128)(2,1)S(1)}, bf16[3,256,128]{2,1,0:T(8,128)(2,1)S(1)}, u32[]{:S(2)}, u32[]{:S(2)}) collective-permute-start(bf16[3,256,128]{2,1,0:T(8,128)(2,1)S(1)} %pad_maximum_fusion.2), channel_id=1, source_target_pairs={{0,1},{1,0},{2,3},{3,2},{4,5},{5,4},{6,7},{7,6},{8,9},{9,8},{10,11... | collective-permute-start | bytes 589832 | tf_op jit(solution)/shard_map/ppermute | solution.py:351
  38.9 14.0 %collective-permute-start.6 = (bf16[256,1024]{1,0:T(8,128)(2,1)S(1)}, bf16[256,1024]{1,0:T(8,128)(2,1)S(1)}, u32[]{:S(2)}, u32[]{:S(2)}) collective-permute-start(bf16[256,1024]{1,0:T(8,128)(2,1)S(1)} %halo_blur.1), channel_id=1, source_target_pairs={{0,2},{2,0},{4,6},{6,4},{8,10},{10,8},{12,14},{14,12},{1,3},{3,1},... | collective-permute-start | bytes 1572872 | tf_op jit(solution)/shard_map/ppermute | solution.py:406
  44.0 16.9 %collective-permute-start.10 = (bf16[256,1024]{1,0:T(8,128)(2,1)S(1)}, bf16[256,1024]{1,0:T(8,128)(2,1)S(1)}, u32[]{:S(2)}, u32[]{:S(2)}) collective-permute-start(bf16[256,1024]{1,0:T(8,128)(2,1)S(1)} %blur_score_pick.1), channel_id=1, source_target_pairs={{4,0},{14,2},{8,4},{2,6},{12,8},{6,10},{0,12},{10,14},{5,1},{15,3}... | collective-permute-start | bytes 1572872 | tf_op jit(solution)/shard_map/ppermute | solution.py:409
  52.9 14.9 %collective-permute-start.9 = (bf16[256,1024]{1,0:T(8,128)(2,1)S(1)}, bf16[256,1024]{1,0:T(8,128)(2,1)S(1)}, u32[]{:S(2)}, u32[]{:S(2)}) collective-permute-start(bf16[256,1024]{1,0:T(8,128)(2,1)S(1)} %blur_score_pick.1), channel_id=1, source_target_pairs={{0,2},{2,0},{4,6},{6,4},{8,10},{10,8},{12,14},{14,12},{1,3},{3,1},... | collective-permute-start | bytes 1572872 | tf_op jit(solution)/shard_map/ppermute | solution.py:412
  54.1 24.9 %collective-permute-start.8 = (bf16[256,1024]{1,0:T(8,128)(2,1)S(1)}, bf16[256,1024]{1,0:T(8,128)(2,1)S(1)}, u32[]{:S(2)}, u32[]{:S(2)}) collective-permute-start(bf16[256,1024]{1,0:T(8,128)(2,1)S(1)} %join_score.1), channel_id=1, source_target_pairs={{0,2},{2,0},{4,6},{6,4},{8,10},{10,8},{12,14},{14,12},{1,3},{3,1},... | collective-permute-start | bytes 1572872 | tf_op jit(solution)/shard_map/ppermute | solution.py:413
  55.5 23.5 %collective-permute-start.7 = (bf16[256,1024]{1,0:T(8,128)(2,1)S(1)}, bf16[256,1024]{1,0:T(8,128)(2,1)S(1)}, u32[]{:S(2)}, u32[]{:S(2)}) collective-permute-start(bf16[256,1024]{1,0:T(8,128)(2,1)S(1)} %join_score.1), channel_id=1, source_target_pairs={{4,0},{14,2},{8,4},{2,6},{12,8},{6,10},{0,12},{10,14},{5,1},{15,3}... | collective-permute-start | bytes 1572872 | tf_op jit(solution)/shard_map/ppermute | solution.py:414
  60.9 29.3 %collective-permute-start.19 = (bf16[256,1024]{1,0:T(8,128)(2,1)S(1)}, bf16[256,1024]{1,0:T(8,128)(2,1)S(1)}, u32[]{:S(2)}, u32[]{:S(2)}) collective-permute-start(bf16[256,1024]{1,0:T(8,128)(2,1)S(1)} %collective-permute-done.10), channel_id=1, source_target_pairs={{0,2},{2,0},{4,6},{6,4},{8,10},{10,8},{12,14},{14,12},{1,3},{3,1},... | collective-permute-start | bytes 1572872 | tf_op jit(solution)/shard_map/ppermute | solution.py:417
  61.4 28.9 %collective-permute-start.18 = (bf16[256,1024]{1,0:T(8,128)(2,1)S(1)}, bf16[256,1024]{1,0:T(8,128)(2,1)S(1)}, u32[]{:S(2)}, u32[]{:S(2)}) collective-permute-start(bf16[256,1024]{1,0:T(8,128)(2,1)S(1)} %blur_score_pick.1), channel_id=1, source_target_pairs={{0,4},{2,14},{4,8},{6,2},{8,12},{10,6},{12,0},{14,10},{1,5},{3,15}... | collective-permute-start | bytes 1572872 | tf_op jit(solution)/shard_map/ppermute | solution.py:416
  79.2 20.7 %copy-start.11 = (s32[8,16]{1,0:T(8,128)S(1)}, s32[8,16]{1,0:T(8,128)}, u32[]{:S(2)}) copy-start(s32[8,16]{1,0:T(8,128)} %param.5) | copy-start | bytes 1540
  79.2 20.7 %collective-permute-start.17 = (bf16[3,256,1024]{2,1,0:T(8,128)(2,1)S(1)}, bf16[3,256,1024]{2,1,0:T(8,128)(2,1)}, u32[]{:S(2)}, u32[]{:S(2)}) collective-permute-start(bf16[3,256,1024]{2,1,0:T(8,128)(2,1)S(1)} %pad_maximum_fusion.refs_0_), channel_id=1, source_target_pairs={{0,1},{1,0},{2,3},{3,2},{4,5},{5,4},{6,7},{7,6},{8,9},{9,8},{10,11... | collective-permute-start | bytes 4718600 | tf_op jit(solution)/shard_map/ppermute | solution.py:351
  79.3 16.2 %collective-permute-start.15 = (bf16[256,1024]{1,0:T(8,128)(2,1)S(1)}, bf16[256,1024]{1,0:T(8,128)(2,1)}, u32[]{:S(2)}, u32[]{:S(2)}) collective-permute-start(bf16[256,1024]{1,0:T(8,128)(2,1)S(1)} %join_score.1), channel_id=1, source_target_pairs={{0,4},{2,14},{4,8},{6,2},{8,12},{10,6},{12,0},{14,10},{1,5},{3,15}... | collective-permute-start | bytes 1572872 | tf_op jit(solution)/shard_map/ppermute | solution.py:424
  81.2 18.7 %collective-permute-start.13 = (bf16[256,1024]{1,0:T(8,128)(2,1)S(1)}, bf16[256,1024]{1,0:T(8,128)(2,1)}, u32[]{:S(2)}, u32[]{:S(2)}) collective-permute-start(bf16[256,1024]{1,0:T(8,128)(2,1)S(1)} %collective-permute-done.7), channel_id=1, source_target_pairs={{0,2},{2,0},{4,6},{6,4},{8,10},{10,8},{12,14},{14,12},{1,3},{3,1},... | collective-permute-start | bytes 1572872 | tf_op jit(solution)/shard_map/ppermute | solution.py:423
  90.2 5.3 %collective-permute-start.20 = (bf16[1,256,1024]{2,1,0:T(8,128)(2,1)S(1)}, bf16[1,256,1024]{2,1,0:T(8,128)(2,1)S(1)}, u32[]{:S(2)}, u32[]{:S(2)}) collective-permute-start(bf16[1,256,1024]{2,1,0:T(8,128)(2,1)S(1)} %bitcast.19), channel_id=1, source_target_pairs={{0,1},{1,0},{2,3},{3,2},{4,5},{5,4},{6,7},{7,6},{8,9},{9,8},{10,11... | collective-permute-start | bytes 1572872 | tf_op jit(solution)/shard_map/ppermute | solution.py:351
  90.3 6.5 %collective-permute-start.21 = (bf16[1,256,1024]{2,1,0:T(8,128)(2,1)S(1)}, bf16[1,256,1024]{2,1,0:T(8,128)(2,1)S(1)}, u32[]{:S(2)}, u32[]{:S(2)}) collective-permute-start(bf16[1,256,1024]{2,1,0:T(8,128)(2,1)S(1)} %bitcast.17), channel_id=1, source_target_pairs={{0,1},{1,0},{2,3},{3,2},{4,5},{5,4},{6,7},{7,6},{8,9},{9,8},{10,11... | collective-permute-start | bytes 1572872 | tf_op jit(solution)/shard_map/ppermute | solution.py:351
  95.5 14.6 %collective-permute-start.11 = (bf16[2,256,1024]{2,1,0:T(8,128)(2,1)S(1)}, bf16[2,256,1024]{2,1,0:T(8,128)(2,1)}, u32[]{:S(2)}, u32[]{:S(2)}) collective-permute-start(bf16[2,256,1024]{2,1,0:T(8,128)(2,1)S(1)} %pad_maximum_fusion.1.refs_0_), channel_id=1, source_target_pairs={{0,1},{1,0},{2,3},{3,2},{4,5},{5,4},{6,7},{7,6},{8,9},{9,8},{10,11... | collective-permute-start | bytes 3145736 | tf_op jit(solution)/shard_map/ppermute | solution.py:351
  96.3 13.7 %collective-permute-start.12 = (bf16[1,256,1024]{2,1,0:T(8,128)(2,1)S(1)}, bf16[1,256,1024]{2,1,0:T(8,128)(2,1)}, u32[]{:S(2)}, u32[]{:S(2)}) collective-permute-start(bf16[1,256,1024]{2,1,0:T(8,128)(2,1)S(1)} %bitcast.15), channel_id=1, source_target_pairs={{0,1},{1,0},{2,3},{3,2},{4,5},{5,4},{6,7},{7,6},{8,9},{9,8},{10,11... | collective-permute-start | bytes 1572872 | tf_op jit(solution)/shard_map/ppermute | solution.py:351
  97.7 12.4 %collective-permute-start.16 = (bf16[1,256,1024]{2,1,0:T(8,128)(2,1)}, bf16[1,256,1024]{2,1,0:T(8,128)(2,1)}, u32[]{:S(2)}, u32[]{:S(2)}) collective-permute-start(bf16[1,256,1024]{2,1,0:T(8,128)(2,1)} %bitcast.6.refs_6_), channel_id=1, source_target_pairs={{0,1},{1,0},{2,3},{3,2},{4,5},{5,4},{6,7},{7,6},{8,9},{9,8},{10,11... | collective-permute-start | bytes 1572872 | tf_op jit(solution)/shard_map/ppermute | solution.py:351
  99.9 10.2 %collective-permute-start.14 = (bf16[1,256,1024]{2,1,0:T(8,128)(2,1)}, bf16[1,256,1024]{2,1,0:T(8,128)(2,1)}, u32[]{:S(2)}, u32[]{:S(2)}) collective-permute-start(bf16[1,256,1024]{2,1,0:T(8,128)(2,1)} %bitcast.5.refs_4_), channel_id=1, source_target_pairs={{0,1},{1,0},{2,3},{3,2},{4,5},{5,4},{6,7},{7,6},{8,9},{9,8},{10,11... | collective-permute-start | bytes 1572872 | tf_op jit(solution)/shard_map/ppermute | solution.py:351
  (10 other events, 19.9 us)

commit v19 on v18

--- a/solution.py
+++ b/solution.py
@@ -313,13 +313,14 @@
     slots = place.shape[1]
     count = len(sources)
     anywhere = pl.BlockSpec(memory_space=pl.ANY)
+    in_hbm = pl.BlockSpec(memory_space=pltpu.HBM)
     operands = list(sources) + ([] if earlier is None else [earlier])
     return pl.pallas_call(
         functools.partial(tiles_kernel, sources=count, window=window),
         grid_spec=pltpu.PrefetchScalarGridSpec(
             num_scalar_prefetch=2,
             grid=(1,),
-            in_specs=[anywhere] * len(operands),
+            in_specs=[in_hbm] * len(operands),
             out_specs=anywhere,
             scratch_shapes=[
                 pltpu.VMEM((total, frames, rows), jnp.bfloat16),

time: 117 us -> 117 us (level)
  no operation moved by 1% of the time
where the time goes in v19:
time: 117 us
  waiting for transfers between devices  56.2 us (48%)
  Pallas kernels  27.9 us (24%)
  starting transfers between devices  23.8 us (20%)
  local copies, waits for them, and re-layouts  8.07 us (7%)
    ppermute x1, waiting for transfers between devices, on_device(): facing_0 = lax.ppermute(near_0, 'row', in_pair)  13.5 us
    pallas_call x2, Pallas kernels, make_tiles(): pl.pallas_call(functools.partial(tiles_kernel, sources=count, window=wind...  12.4 us
    pallas_call x4, Pallas kernels, call_on_rows(): pl.pallas_call(kernel, grid=(1,), in_specs=[whole(value) for value in ope...  12.4 us
    ppermute x1, waiting for transfers between devices, on_device(): pair_1 = lax.ppermute(own_1, 'row', in_pair)  11.2 us
    unnamed x24, local copies, waits for them, and re-layouts  8.07 us
    ppermute x1, waiting for transfers between devices, on_device(): pair_0 = lax.ppermute(after(own_0, halo_1), 'row', in_pair)  6.38 us
    ppermute x1, waiting for transfers between devices, on_device(): rest_0 = lax.ppermute(ahead_0, 'row', in_pair)  5.47 us
    ppermute x1, waiting for transfers between devices, on_device(): behind_1 = lax.ppermute(after(own_1, ahead_1), 'row', behind)  4.59 us
  transfers between devices with their start and end apart: 22, of which 11 were waited for; matrix products, arithmetic and copies ran while one was open for 0% of the time, Pallas kernels for 14%

profile of v19, /device:TPU:0, one launch (start us, length us, event | category | flops | bytes accessed | tf_op | source)
XLA Modules:
  0.0 116.7 jit_solution(12405718497756436530)
XLA Ops:
  0.0 1.6 %copy-done = bf16[2,256,2,8,128]{4,3,2,1,0:T(8,128)(2,1)S(1)} copy-done((bf16[2,256,2,8,128]{4,3,2,1,0:T(8,128)(2,1)S(1)}, bf16[2,256,2,8,128]{4,3,2,1,0:T(8,128)(2,1)}, u32[]{:S(2)}) %copy-start) | copy-done | bytes 2097176
  2.3 3.0 %faces.1 = (bf16[2064,128]{1,0:T(8,128)(2,1)S(1)}, bf16[8,256,128]{2,1,0:T(8,128)(2,1)}, bf16[2,256,128]{2,1,0:T(8,128)(2,1)}, bf16[8,256,128]{2,1,0:T(8,128)(2,...) custom-call(bf16[2,256,2,8,128]{4,3,2,1,0:T(8,128)(2,1)S(1)} %copy-done, s32[8,128]{1,0:T(8,128)S(1)} %bitcast.21), custom_call_target="tpu_custom_call" | custom-call | flops 1 | bytes 1 | tf_op jit(solution)/shard_map/faces/pallas_call | solution.py:78
  5.3 3.0 %collective-permute-start.3 = (bf16[2064,128]{1,0:T(8,128)(2,1)S(1)}, bf16[2064,128]{1,0:T(8,128)(2,1)S(1)}, u32[]{:S(2)}, u32[]{:S(2)}) collective-permute-start(bf16[2064,128]{1,0:T(8,128)(2,1)S(1)} %get-tuple-element.31.near_ref), channel_id=1, source_target_pairs={{0,2},{2,0},{4,6},{6,4},{8,10},{10,8},{12,14},{14,12},{1,3},{3,1},... | collective-permute-start | bytes 1585160 | tf_op jit(solution)/shard_map/ppermute | solution.py:397
  9.0 1.5 %collective-permute-start.2 = (bf16[8,256,128]{2,1,0:T(8,128)(2,1)S(1)}, bf16[8,256,128]{2,1,0:T(8,128)(2,1)S(1)}, u32[]{:S(2)}, u32[]{:S(2)}) collective-permute-start(bf16[8,256,128]{2,1,0:T(8,128)(2,1)S(1)} %get-tuple-element.27.outer_ref), channel_id=1, source_target_pairs={{2,6},{4,0},{6,10},{8,4},{10,14},{12,8},{3,7},{5,1},{7,11},{9,5},{... | collective-permute-start | bytes 1572872 | tf_op jit(solution)/shard_map/ppermute | solution.py:399
  12.1 5.2 %inner_blur.1.inner_ref = f32[256,1024]{1,0:T(8,128)S(1)} custom-call(bf16[8,256,128]{2,1,0:T(8,128)(2,1)S(1)} %get-tuple-element.26.near_ref, bf16[8,256,128]{2,1,0:T(8,128)(2,1)S(1)} %get-tuple-element.27.outer_ref, bf16[2,256,128]{2,1,0:T(8,128)(2,1)S(1)} %collective-permute-done.edge_ref, s32[8,128]{1,0:T(8,128)S(1)} %bitcast.22), custom_call_target="tpu_custom_call" | custom-call | flops 1 | bytes 1 | tf_op jit(solution)/shard_map/inner_blur/pallas_call | solution.py:222
  17.3 13.5 %collective-permute-done.3.facing_ref = bf16[2064,128]{1,0:T(8,128)(2,1)S(1)} collective-permute-done((bf16[2064,128]{1,0:T(8,128)(2,1)S(1)}, bf16[2064,128]{1,0:T(8,128)(2,1)S(1)}, u32[]{:S(2)}, u32[]{:S(2)}) %collective-permute-start.3) | collective-permute-done | bytes 528416 | tf_op jit(solution)/shard_map/ppermute | solution.py:397
  30.8 4.1 %collective-permute-done.2.beyond_ref = bf16[8,256,128]{2,1,0:T(8,128)(2,1)S(1)} collective-permute-done((bf16[8,256,128]{2,1,0:T(8,128)(2,1)S(1)}, bf16[8,256,128]{2,1,0:T(8,128)(2,1)S(1)}, u32[]{:S(2)}, u32[]{:S(2)}) %collective-permute-start.2) | collective-permute-done | bytes 524320 | tf_op jit(solution)/shard_map/ppermute | solution.py:399
  35.1 1.4 %collective-permute-done.5.corner_ref = bf16[3,256,128]{2,1,0:T(8,128)(2,1)S(1)} collective-permute-done((bf16[3,256,128]{2,1,0:T(8,128)(2,1)S(1)}, bf16[3,256,128]{2,1,0:T(8,128)(2,1)S(1)}, u32[]{:S(2)}, u32[]{:S(2)}) %collective-permute-start.5) | collective-permute-done | bytes 196640 | tf_op jit(solution)/shard_map/ppermute | solution.py:352
  36.5 2.4 %halo_blur.1 = bf16[256,1024]{1,0:T(8,128)(2,1)S(1)} custom-call(bf16[8,256,128]{2,1,0:T(8,128)(2,1)S(1)} %get-tuple-element.26.near_ref, bf16[8,256,128]{2,1,0:T(8,128)(2,1)S(1)} %collective-permute-done.2.beyond_ref, bf16[2,256,128]{2,1,0:T(8,128)(2,1)S(1)} %collective-permute-done.edge_ref, bf16[3,256,128]{2,1,0:T(8,128)(2,1)S(1)} %collective-permute-done.5.corner_ref, ...), custom_call_target="tpu_custom_call" | custom-call | flops 1 | bytes 1 | tf_op jit(solution)/shard_map/halo_blur/pallas_call | solution.py:222
  39.7 4.4 %blur_score_pick.1 = bf16[256,1024]{1,0:T(8,128)(2,1)S(1)} custom-call(bf16[2064,128]{1,0:T(8,128)(2,1)S(1)} %get-tuple-element.31.near_ref, bf16[8,256,128]{2,1,0:T(8,128)(2,1)} %get-tuple-element.33.outer_ref, bf16[2064,128]{1,0:T(8,128)(2,1)S(1)} %collective-permute-done.3.facing_ref, bf16[8,256,128]{2,1,0:T(8,128)(2,1)S(1)} %collective-permute-done.4.across_ref, ...), custom_call_target="tpu_custom_call" | custom-call | flops 1 | bytes 1 | tf_op jit(solution)/shard_map/blur_score_pick/pallas_call | solution.py:222
  44.0 4.6 %collective-permute-start.10 = (bf16[256,1024]{1,0:T(8,128)(2,1)S(1)}, bf16[256,1024]{1,0:T(8,128)(2,1)S(1)}, u32[]{:S(2)}, u32[]{:S(2)}) collective-permute-start(bf16[256,1024]{1,0:T(8,128)(2,1)S(1)} %blur_score_pick.1), channel_id=1, source_target_pairs={{4,0},{14,2},{8,4},{2,6},{12,8},{6,10},{0,12},{10,14},{5,1},{15,3}... | collective-permute-start | bytes 1572872 | tf_op jit(solution)/shard_map/ppermute | solution.py:410
  48.6 4.3 %collective-permute-done.6.halo_ref = bf16[256,1024]{1,0:T(8,128)(2,1)S(1)} collective-permute-done((bf16[256,1024]{1,0:T(8,128)(2,1)S(1)}, bf16[256,1024]{1,0:T(8,128)(2,1)S(1)}, u32[]{:S(2)}, u32[]{:S(2)}) %collective-permute-start.6) | collective-permute-done | bytes 524320 | tf_op jit(solution)/shard_map/ppermute | solution.py:407
  54.1 1.4 %collective-permute-start.8 = (bf16[256,1024]{1,0:T(8,128)(2,1)S(1)}, bf16[256,1024]{1,0:T(8,128)(2,1)S(1)}, u32[]{:S(2)}, u32[]{:S(2)}) collective-permute-start(bf16[256,1024]{1,0:T(8,128)(2,1)S(1)} %join_score.1), channel_id=1, source_target_pairs={{0,2},{2,0},{4,6},{6,4},{8,10},{10,8},{12,14},{14,12},{1,3},{3,1},... | collective-permute-start | bytes 1572872 | tf_op jit(solution)/shard_map/ppermute | solution.py:414
  55.5 3.5 %collective-permute-start.7 = (bf16[256,1024]{1,0:T(8,128)(2,1)S(1)}, bf16[256,1024]{1,0:T(8,128)(2,1)S(1)}, u32[]{:S(2)}, u32[]{:S(2)}) collective-permute-start(bf16[256,1024]{1,0:T(8,128)(2,1)S(1)} %join_score.1), channel_id=1, source_target_pairs={{4,0},{14,2},{8,4},{2,6},{12,8},{6,10},{0,12},{10,14},{5,1},{15,3}... | collective-permute-start | bytes 1572872 | tf_op jit(solution)/shard_map/ppermute | solution.py:415
  59.0 1.9 %collective-permute-done.10 = bf16[256,1024]{1,0:T(8,128)(2,1)S(1)} collective-permute-done((bf16[256,1024]{1,0:T(8,128)(2,1)S(1)}, bf16[256,1024]{1,0:T(8,128)(2,1)S(1)}, u32[]{:S(2)}, u32[]{:S(2)}) %collective-permute-start.10) | collective-permute-done | bytes 524320 | tf_op jit(solution)/shard_map/ppermute | solution.py:410
  61.4 6.4 %collective-permute-done.9 = bf16[256,1024]{1,0:T(8,128)(2,1)S(1)} collective-permute-done((bf16[256,1024]{1,0:T(8,128)(2,1)S(1)}, bf16[256,1024]{1,0:T(8,128)(2,1)S(1)}, u32[]{:S(2)}, u32[]{:S(2)}) %collective-permute-start.9) | collective-permute-done | bytes 524320 | tf_op jit(solution)/shard_map/ppermute | solution.py:413
  67.8 11.2 %collective-permute-done.8 = bf16[256,1024]{1,0:T(8,128)(2,1)S(1)} collective-permute-done((bf16[256,1024]{1,0:T(8,128)(2,1)S(1)}, bf16[256,1024]{1,0:T(8,128)(2,1)S(1)}, u32[]{:S(2)}, u32[]{:S(2)}) %collective-permute-start.8) | collective-permute-done | bytes 524320 | tf_op jit(solution)/shard_map/ppermute | solution.py:414
  79.3 1.9 %collective-permute-start.15 = (bf16[256,1024]{1,0:T(8,128)(2,1)S(1)}, bf16[256,1024]{1,0:T(8,128)(2,1)}, u32[]{:S(2)}, u32[]{:S(2)}) collective-permute-start(bf16[256,1024]{1,0:T(8,128)(2,1)S(1)} %join_score.1), channel_id=1, source_target_pairs={{0,4},{2,14},{4,8},{6,2},{8,12},{10,6},{12,0},{14,10},{1,5},{3,15}... | collective-permute-start | bytes 1572872 | tf_op jit(solution)/shard_map/ppermute | solution.py:425
  81.2 3.6 %collective-permute-start.13 = (bf16[256,1024]{1,0:T(8,128)(2,1)S(1)}, bf16[256,1024]{1,0:T(8,128)(2,1)}, u32[]{:S(2)}, u32[]{:S(2)}) collective-permute-start(bf16[256,1024]{1,0:T(8,128)(2,1)S(1)} %collective-permute-done.7), channel_id=1, source_target_pairs={{0,2},{2,0},{4,6},{6,4},{8,10},{10,8},{12,14},{14,12},{1,3},{3,1},... | collective-permute-start | bytes 1572872 | tf_op jit(solution)/shard_map/ppermute | solution.py:424
  84.8 5.5 %collective-permute-done.19 = bf16[256,1024]{1,0:T(8,128)(2,1)S(1)} collective-permute-done((bf16[256,1024]{1,0:T(8,128)(2,1)S(1)}, bf16[256,1024]{1,0:T(8,128)(2,1)S(1)}, u32[]{:S(2)}, u32[]{:S(2)}) %collective-permute-start.19) | collective-permute-done | bytes 524320 | tf_op jit(solution)/shard_map/ppermute | solution.py:418
  90.9 4.6 %collective-permute-done.15 = bf16[256,1024]{1,0:T(8,128)(2,1)} collective-permute-done((bf16[256,1024]{1,0:T(8,128)(2,1)S(1)}, bf16[256,1024]{1,0:T(8,128)(2,1)}, u32[]{:S(2)}, u32[]{:S(2)}) %collective-permute-start.15) | collective-permute-done | bytes 524320 | tf_op jit(solution)/shard_map/ppermute | solution.py:425
  97.7 2.2 %collective-permute-done.13 = bf16[256,1024]{1,0:T(8,128)(2,1)} collective-permute-done((bf16[256,1024]{1,0:T(8,128)(2,1)S(1)}, bf16[256,1024]{1,0:T(8,128)(2,1)}, u32[]{:S(2)}, u32[]{:S(2)}) %collective-permute-start.13) | collective-permute-done | bytes 524320 | tf_op jit(solution)/shard_map/ppermute | solution.py:424
  104.1 5.9 %tiles.2.refs_8_ = bf16[8,16,2,128,128]{4,3,2,1,0:T(8,128)(2,1)} custom-call(s32[8,16]{1,0:T(8,128)S(1)} %get-tuple-element.47.place_ref, s32[8,16]{1,0:T(8,128)S(1)} %fusion.17.present_ref, bf16[3,256,1024]{2,1,0:T(8,128)(2,1)S(1)} %pad_maximum_fusion.refs_0_, bf16[3,256,1024]{2,1,0:T(8,128)(2,1)} %collective-permute-done.17.refs_1_, ...), custom_call_target="tpu_custom_call" | custom-call | flops 1 | bytes 1 | tf_op jit(solution)/shard_map/tiles/pallas_call | solution.py:318
  110.1 6.5 %tiles.3 = bf16[8,16,2,128,128]{4,3,2,1,0:T(8,128)(2,1)} custom-call(s32[8,16]{1,0:T(8,128)S(1)} %get-tuple-element.48.place_ref, s32[8,16]{1,0:T(8,128)S(1)} %fusion.17.present_ref, bf16[2,256,1024]{2,1,0:T(8,128)(2,1)S(1)} %pad_maximum_fusion.1.refs_0_, bf16[2,256,1024]{2,1,0:T(8,128)(2,1)} %collective-permute-done.11.refs_1_, ...), custom_call_target="tpu_custom_call", output_to_operand_aliasing={{}: (10, {})} | custom-call | flops 1 | bytes 1 | tf_op jit(solution)/shard_map/tiles/pallas_call | solution.py:318
  (59 shorter events, 12.8 us)
Async XLA Ops:
  2.3 9.8 %copy-start.10 = (s32[1024]{0:T(1024)S(1)}, s32[1024]{0:T(1024)}, u32[]{:S(2)}) copy-start(s32[1024]{0:T(1024)} %param.4) | copy-start | bytes 12292
  5.3 25.5 %collective-permute-start.3 = (bf16[2064,128]{1,0:T(8,128)(2,1)S(1)}, bf16[2064,128]{1,0:T(8,128)(2,1)S(1)}, u32[]{:S(2)}, u32[]{:S(2)}) collective-permute-start(bf16[2064,128]{1,0:T(8,128)(2,1)S(1)} %get-tuple-element.31.near_ref), channel_id=1, source_target_pairs={{0,2},{2,0},{4,6},{6,4},{8,10},{10,8},{12,14},{14,12},{1,3},{3,1},... | collective-permute-start | bytes 1585160 | tf_op jit(solution)/shard_map/ppermute | solution.py:397
  8.3 9.0 %collective-permute-start.4 = (bf16[8,256,128]{2,1,0:T(8,128)(2,1)}, bf16[8,256,128]{2,1,0:T(8,128)(2,1)S(1)}, u32[]{:S(2)}, u32[]{:S(2)}) collective-permute-start(bf16[8,256,128]{2,1,0:T(8,128)(2,1)} %get-tuple-element.33.outer_ref), channel_id=1, source_target_pairs={{2,4},{4,2},{6,8},{8,6},{10,12},{12,10},{3,5},{5,3},{7,9},{9,7},{1... | collective-permute-start | bytes 1572872 | tf_op jit(solution)/shard_map/ppermute | solution.py:398
  9.0 25.9 %collective-permute-start.2 = (bf16[8,256,128]{2,1,0:T(8,128)(2,1)S(1)}, bf16[8,256,128]{2,1,0:T(8,128)(2,1)S(1)}, u32[]{:S(2)}, u32[]{:S(2)}) collective-permute-start(bf16[8,256,128]{2,1,0:T(8,128)(2,1)S(1)} %get-tuple-element.27.outer_ref), channel_id=1, source_target_pairs={{2,6},{4,0},{6,10},{8,4},{10,14},{12,8},{3,7},{5,1},{7,11},{9,5},{... | collective-permute-start | bytes 1572872 | tf_op jit(solution)/shard_map/ppermute | solution.py:399
  10.5 1.6 %collective-permute-start.1 = (bf16[2,256,128]{2,1,0:T(8,128)(2,1)}, bf16[2,256,128]{2,1,0:T(8,128)(2,1)S(1)}, u32[]{:S(2)}, u32[]{:S(2)}) collective-permute-start(bf16[2,256,128]{2,1,0:T(8,128)(2,1)} %get-tuple-element.29), channel_id=1, source_target_pairs={{0,1},{1,0},{2,3},{3,2},{4,5},{5,4},{6,7},{7,6},{8,9},{9,8},{10,11... | collective-permute-start | bytes 393224 | tf_op jit(solution)/shard_map/ppermute | solution.py:352
  10.6 1.5 %collective-permute-start = (bf16[2,256,128]{2,1,0:T(8,128)(2,1)S(1)}, bf16[2,256,128]{2,1,0:T(8,128)(2,1)S(1)}, u32[]{:S(2)}, u32[]{:S(2)}) collective-permute-start(bf16[2,256,128]{2,1,0:T(8,128)(2,1)S(1)} %get-tuple-element.28), channel_id=1, source_target_pairs={{0,1},{1,0},{2,3},{3,2},{4,5},{5,4},{6,7},{7,6},{8,9},{9,8},{10,11... | collective-permute-start | bytes 393224 | tf_op jit(solution)/shard_map/ppermute | solution.py:352
  35.0 1.5 %collective-permute-start.5 = (bf16[3,256,128]{2,1,0:T(8,128)(2,1)S(1)}, bf16[3,256,128]{2,1,0:T(8,128)(2,1)S(1)}, u32[]{:S(2)}, u32[]{:S(2)}) collective-permute-start(bf16[3,256,128]{2,1,0:T(8,128)(2,1)S(1)} %pad_maximum_fusion.2), channel_id=1, source_target_pairs={{0,1},{1,0},{2,3},{3,2},{4,5},{5,4},{6,7},{7,6},{8,9},{9,8},{10,11... | collective-permute-start | bytes 589832 | tf_op jit(solution)/shard_map/ppermute | solution.py:352
  38.9 14.0 %collective-permute-start.6 = (bf16[256,1024]{1,0:T(8,128)(2,1)S(1)}, bf16[256,1024]{1,0:T(8,128)(2,1)S(1)}, u32[]{:S(2)}, u32[]{:S(2)}) collective-permute-start(bf16[256,1024]{1,0:T(8,128)(2,1)S(1)} %halo_blur.1), channel_id=1, source_target_pairs={{0,2},{2,0},{4,6},{6,4},{8,10},{10,8},{12,14},{14,12},{1,3},{3,1},... | collective-permute-start | bytes 1572872 | tf_op jit(solution)/shard_map/ppermute | solution.py:407
  44.0 16.9 %collective-permute-start.10 = (bf16[256,1024]{1,0:T(8,128)(2,1)S(1)}, bf16[256,1024]{1,0:T(8,128)(2,1)S(1)}, u32[]{:S(2)}, u32[]{:S(2)}) collective-permute-start(bf16[256,1024]{1,0:T(8,128)(2,1)S(1)} %blur_score_pick.1), channel_id=1, source_target_pairs={{4,0},{14,2},{8,4},{2,6},{12,8},{6,10},{0,12},{10,14},{5,1},{15,3}... | collective-permute-start | bytes 1572872 | tf_op jit(solution)/shard_map/ppermute | solution.py:410
  52.9 14.9 %collective-permute-start.9 = (bf16[256,1024]{1,0:T(8,128)(2,1)S(1)}, bf16[256,1024]{1,0:T(8,128)(2,1)S(1)}, u32[]{:S(2)}, u32[]{:S(2)}) collective-permute-start(bf16[256,1024]{1,0:T(8,128)(2,1)S(1)} %blur_score_pick.1), channel_id=1, source_target_pairs={{0,2},{2,0},{4,6},{6,4},{8,10},{10,8},{12,14},{14,12},{1,3},{3,1},... | collective-permute-start | bytes 1572872 | tf_op jit(solution)/shard_map/ppermute | solution.py:413
  54.1 24.9 %collective-permute-start.8 = (bf16[256,1024]{1,0:T(8,128)(2,1)S(1)}, bf16[256,1024]{1,0:T(8,128)(2,1)S(1)}, u32[]{:S(2)}, u32[]{:S(2)}) collective-permute-start(bf16[256,1024]{1,0:T(8,128)(2,1)S(1)} %join_score.1), channel_id=1, source_target_pairs={{0,2},{2,0},{4,6},{6,4},{8,10},{10,8},{12,14},{14,12},{1,3},{3,1},... | collective-permute-start | bytes 1572872 | tf_op jit(solution)/shard_map/ppermute | solution.py:414
  55.5 23.5 %collective-permute-start.7 = (bf16[256,1024]{1,0:T(8,128)(2,1)S(1)}, bf16[256,1024]{1,0:T(8,128)(2,1)S(1)}, u32[]{:S(2)}, u32[]{:S(2)}) collective-permute-start(bf16[256,1024]{1,0:T(8,128)(2,1)S(1)} %join_score.1), channel_id=1, source_target_pairs={{4,0},{14,2},{8,4},{2,6},{12,8},{6,10},{0,12},{10,14},{5,1},{15,3}... | collective-permute-start | bytes 1572872 | tf_op jit(solution)/shard_map/ppermute | solution.py:415
  60.9 29.3 %collective-permute-start.19 = (bf16[256,1024]{1,0:T(8,128)(2,1)S(1)}, bf16[256,1024]{1,0:T(8,128)(2,1)S(1)}, u32[]{:S(2)}, u32[]{:S(2)}) collective-permute-start(bf16[256,1024]{1,0:T(8,128)(2,1)S(1)} %collective-permute-done.10), channel_id=1, source_target_pairs={{0,2},{2,0},{4,6},{6,4},{8,10},{10,8},{12,14},{14,12},{1,3},{3,1},... | collective-permute-start | bytes 1572872 | tf_op jit(solution)/shard_map/ppermute | solution.py:418
  61.4 28.9 %collective-permute-start.18 = (bf16[256,1024]{1,0:T(8,128)(2,1)S(1)}, bf16[256,1024]{1,0:T(8,128)(2,1)S(1)}, u32[]{:S(2)}, u32[]{:S(2)}) collective-permute-start(bf16[256,1024]{1,0:T(8,128)(2,1)S(1)} %blur_score_pick.1), channel_id=1, source_target_pairs={{0,4},{2,14},{4,8},{6,2},{8,12},{10,6},{12,0},{14,10},{1,5},{3,15}... | collective-permute-start | bytes 1572872 | tf_op jit(solution)/shard_map/ppermute | solution.py:417
  79.2 20.7 %copy-start.11 = (s32[8,16]{1,0:T(8,128)S(1)}, s32[8,16]{1,0:T(8,128)}, u32[]{:S(2)}) copy-start(s32[8,16]{1,0:T(8,128)} %param.5) | copy-start | bytes 1540
  79.2 20.7 %collective-permute-start.17 = (bf16[3,256,1024]{2,1,0:T(8,128)(2,1)S(1)}, bf16[3,256,1024]{2,1,0:T(8,128)(2,1)}, u32[]{:S(2)}, u32[]{:S(2)}) collective-permute-start(bf16[3,256,1024]{2,1,0:T(8,128)(2,1)S(1)} %pad_maximum_fusion.refs_0_), channel_id=1, source_target_pairs={{0,1},{1,0},{2,3},{3,2},{4,5},{5,4},{6,7},{7,6},{8,9},{9,8},{10,11... | collective-permute-start | bytes 4718600 | tf_op jit(solution)/shard_map/ppermute | solution.py:352
  79.3 16.2 %collective-permute-start.15 = (bf16[256,1024]{1,0:T(8,128)(2,1)S(1)}, bf16[256,1024]{1,0:T(8,128)(2,1)}, u32[]{:S(2)}, u32[]{:S(2)}) collective-permute-start(bf16[256,1024]{1,0:T(8,128)(2,1)S(1)} %join_score.1), channel_id=1, source_target_pairs={{0,4},{2,14},{4,8},{6,2},{8,12},{10,6},{12,0},{14,10},{1,5},{3,15}... | collective-permute-start | bytes 1572872 | tf_op jit(solution)/shard_map/ppermute | solution.py:425
  81.2 18.7 %collective-permute-start.13 = (bf16[256,1024]{1,0:T(8,128)(2,1)S(1)}, bf16[256,1024]{1,0:T(8,128)(2,1)}, u32[]{:S(2)}, u32[]{:S(2)}) collective-permute-start(bf16[256,1024]{1,0:T(8,128)(2,1)S(1)} %collective-permute-done.7), channel_id=1, source_target_pairs={{0,2},{2,0},{4,6},{6,4},{8,10},{10,8},{12,14},{14,12},{1,3},{3,1},... | collective-permute-start | bytes 1572872 | tf_op jit(solution)/shard_map/ppermute | solution.py:424
  90.2 5.3 %collective-permute-start.20 = (bf16[1,256,1024]{2,1,0:T(8,128)(2,1)S(1)}, bf16[1,256,1024]{2,1,0:T(8,128)(2,1)S(1)}, u32[]{:S(2)}, u32[]{:S(2)}) collective-permute-start(bf16[1,256,1024]{2,1,0:T(8,128)(2,1)S(1)} %bitcast.19), channel_id=1, source_target_pairs={{0,1},{1,0},{2,3},{3,2},{4,5},{5,4},{6,7},{7,6},{8,9},{9,8},{10,11... | collective-permute-start | bytes 1572872 | tf_op jit(solution)/shard_map/ppermute | solution.py:352
  90.3 6.5 %collective-permute-start.21 = (bf16[1,256,1024]{2,1,0:T(8,128)(2,1)S(1)}, bf16[1,256,1024]{2,1,0:T(8,128)(2,1)S(1)}, u32[]{:S(2)}, u32[]{:S(2)}) collective-permute-start(bf16[1,256,1024]{2,1,0:T(8,128)(2,1)S(1)} %bitcast.17), channel_id=1, source_target_pairs={{0,1},{1,0},{2,3},{3,2},{4,5},{5,4},{6,7},{7,6},{8,9},{9,8},{10,11... | collective-permute-start | bytes 1572872 | tf_op jit(solution)/shard_map/ppermute | solution.py:352
  95.5 14.5 %collective-permute-start.11 = (bf16[2,256,1024]{2,1,0:T(8,128)(2,1)S(1)}, bf16[2,256,1024]{2,1,0:T(8,128)(2,1)}, u32[]{:S(2)}, u32[]{:S(2)}) collective-permute-start(bf16[2,256,1024]{2,1,0:T(8,128)(2,1)S(1)} %pad_maximum_fusion.1.refs_0_), channel_id=1, source_target_pairs={{0,1},{1,0},{2,3},{3,2},{4,5},{5,4},{6,7},{7,6},{8,9},{9,8},{10,11... | collective-permute-start | bytes 3145736 | tf_op jit(solution)/shard_map/ppermute | solution.py:352
  96.3 13.7 %collective-permute-start.12 = (bf16[1,256,1024]{2,1,0:T(8,128)(2,1)S(1)}, bf16[1,256,1024]{2,1,0:T(8,128)(2,1)}, u32[]{:S(2)}, u32[]{:S(2)}) collective-permute-start(bf16[1,256,1024]{2,1,0:T(8,128)(2,1)S(1)} %bitcast.15), channel_id=1, source_target_pairs={{0,1},{1,0},{2,3},{3,2},{4,5},{5,4},{6,7},{7,6},{8,9},{9,8},{10,11... | collective-permute-start | bytes 1572872 | tf_op jit(solution)/shard_map/ppermute | solution.py:352
  97.7 12.4 %collective-permute-start.16 = (bf16[1,256,1024]{2,1,0:T(8,128)(2,1)}, bf16[1,256,1024]{2,1,0:T(8,128)(2,1)}, u32[]{:S(2)}, u32[]{:S(2)}) collective-permute-start(bf16[1,256,1024]{2,1,0:T(8,128)(2,1)} %bitcast.6.refs_6_), channel_id=1, source_target_pairs={{0,1},{1,0},{2,3},{3,2},{4,5},{5,4},{6,7},{7,6},{8,9},{9,8},{10,11... | collective-permute-start | bytes 1572872 | tf_op jit(solution)/shard_map/ppermute | solution.py:352
  99.9 10.2 %collective-permute-start.14 = (bf16[1,256,1024]{2,1,0:T(8,128)(2,1)}, bf16[1,256,1024]{2,1,0:T(8,128)(2,1)}, u32[]{:S(2)}, u32[]{:S(2)}) collective-permute-start(bf16[1,256,1024]{2,1,0:T(8,128)(2,1)} %bitcast.5.refs_4_), channel_id=1, source_target_pairs={{0,1},{1,0},{2,3},{3,2},{4,5},{5,4},{6,7},{7,6},{8,9},{9,8},{10,11... | collective-permute-start | bytes 1572872 | tf_op jit(solution)/shard_map/ppermute | solution.py:352
  (10 other events, 19.9 us)

commit v20 on v16

--- a/solution.py
+++ b/solution.py
@@ -13,6 +13,7 @@
 CENTRE = 1.0 / (1.0 + 2.0 * math.exp(-0.5))
 SMALL = pl.CostEstimate(flops=1, bytes_accessed=1, transcendentals=0)
 VMEM_BYTES = 20 * 1024 * 1024
+TILES_VMEM_BYTES = 60 * 1024 * 1024
 
 
 def is_even():
@@ -330,7 +331,7 @@
         ),
         out_shape=jax.ShapeDtypeStruct((blocks, slots, windows, BLOCK, BLOCK), jnp.bfloat16),
         input_output_aliases={} if earlier is None else {2 + count: 0},
-        compiler_params=pltpu.CompilerParams(vmem_limit_bytes=VMEM_BYTES),
+        compiler_params=pltpu.CompilerParams(vmem_limit_bytes=TILES_VMEM_BYTES),
         cost_estimate=SMALL,
         name="tiles",
     )(place, present, *operands)

time: 117 us -> 116 us (level)
  local copies, waits for them, and re-layouts: 8.07 us -> 2.6 us
  Pallas kernels: 27.8 us -> 29.5 us
  other arithmetic: 0.37 us -> 1.54 us
    unnamed x24 -> x22, local copies, waits for them, and re-layouts: 8.07 us -> 2.6 us
    pallas_call x2, Pallas kernels: 12.4 us -> 14 us  [make_tiles(): pl.pallas_call(functools.partial(tiles_kernel, sources=count, window=wind...]
  transfers between devices with their start and end apart: 22 -> 22, of which waited for: 11 -> 11; matrix products, arithmetic and copies ran while one was open for 0% -> 1% of each run, Pallas kernels for 14% -> 15%
where the time goes in v20:
time: 116 us; the launch traced here: 115 us
  waiting for transfers between devices  56.9 us (49%)
  Pallas kernels  29.5 us (25%)
  starting transfers between devices  24.4 us (21%)
  local copies, waits for them, and re-layouts  2.6 us (2%)
  other arithmetic  1.54 us (1%)
    pallas_call x2, Pallas kernels, make_tiles(): pl.pallas_call(functools.partial(tiles_kernel, sources=count, window=wind...  14 us
    ppermute x1, waiting for transfers between devices, on_device(): facing_0 = lax.ppermute(near_0, 'row', in_pair)  13.5 us
    pallas_call x4, Pallas kernels, call_on_rows(): pl.pallas_call(kernel, grid=(1,), in_specs=[whole(value) for value in ope...  12.4 us
    ppermute x1, waiting for transfers between devices, on_device(): pair_1 = lax.ppermute(own_1, 'row', in_pair)  11.2 us
    ppermute x1, waiting for transfers between devices, on_device(): pair_0 = lax.ppermute(after(own_0, halo_1), 'row', in_pair)  6.38 us
    ppermute x1, waiting for transfers between devices, on_device(): rest_0 = lax.ppermute(ahead_0, 'row', in_pair)  5.45 us
    ppermute x1, waiting for transfers between devices, on_device(): behind_1 = lax.ppermute(after(own_1, ahead_1), 'row', behind)  4.59 us
    ppermute x1, starting transfers between devices, on_device(): ahead_0 = lax.ppermute(own_0, 'row', ahead)  4.56 us
  transfers between devices with their start and end apart: 22, of which 11 were waited for; matrix products, arithmetic and copies ran while one was open for 1% of the time, Pallas kernels for 15%

profile of v20, /device:TPU:0, one launch (start us, length us, event | category | flops | bytes accessed | tf_op | source)
XLA Modules:
  0.0 115.3 jit_solution(640848558197590245)
XLA Ops:
  0.0 1.6 %copy-done = bf16[2,256,2,8,128]{4,3,2,1,0:T(8,128)(2,1)S(1)} copy-done((bf16[2,256,2,8,128]{4,3,2,1,0:T(8,128)(2,1)S(1)}, bf16[2,256,2,8,128]{4,3,2,1,0:T(8,128)(2,1)}, u32[]{:S(2)}) %copy-start) | copy-done | bytes 2097176
  2.3 3.0 %faces.1 = (bf16[2064,128]{1,0:T(8,128)(2,1)S(1)}, bf16[8,256,128]{2,1,0:T(8,128)(2,1)}, bf16[2,256,128]{2,1,0:T(8,128)(2,1)}, bf16[8,256,128]{2,1,0:T(8,128)(2,...) custom-call(bf16[2,256,2,8,128]{4,3,2,1,0:T(8,128)(2,1)S(1)} %copy-done, s32[8,128]{1,0:T(8,128)S(1)} %bitcast.15), custom_call_target="tpu_custom_call" | custom-call | flops 1 | bytes 1 | tf_op jit(solution)/shard_map/faces/pallas_call | solution.py:79
  5.3 3.0 %collective-permute-start.3 = (bf16[2064,128]{1,0:T(8,128)(2,1)S(1)}, bf16[2064,128]{1,0:T(8,128)(2,1)S(1)}, u32[]{:S(2)}, u32[]{:S(2)}) collective-permute-start(bf16[2064,128]{1,0:T(8,128)(2,1)S(1)} %get-tuple-element.31.near_ref), channel_id=1, source_target_pairs={{0,2},{2,0},{4,6},{6,4},{8,10},{10,8},{12,14},{14,12},{1,3},{3,1},... | collective-permute-start | bytes 1585160 | tf_op jit(solution)/shard_map/ppermute | solution.py:397
  9.0 1.5 %collective-permute-start.2 = (bf16[8,256,128]{2,1,0:T(8,128)(2,1)S(1)}, bf16[8,256,128]{2,1,0:T(8,128)(2,1)S(1)}, u32[]{:S(2)}, u32[]{:S(2)}) collective-permute-start(bf16[8,256,128]{2,1,0:T(8,128)(2,1)S(1)} %get-tuple-element.27.outer_ref), channel_id=1, source_target_pairs={{2,6},{4,0},{6,10},{8,4},{10,14},{12,8},{3,7},{5,1},{7,11},{9,5},{... | collective-permute-start | bytes 1572872 | tf_op jit(solution)/shard_map/ppermute | solution.py:399
  12.1 5.2 %inner_blur.1.inner_ref = f32[256,1024]{1,0:T(8,128)S(1)} custom-call(bf16[8,256,128]{2,1,0:T(8,128)(2,1)S(1)} %get-tuple-element.26.near_ref, bf16[8,256,128]{2,1,0:T(8,128)(2,1)S(1)} %get-tuple-element.27.outer_ref, bf16[2,256,128]{2,1,0:T(8,128)(2,1)S(1)} %collective-permute-done.edge_ref, s32[8,128]{1,0:T(8,128)S(1)} %bitcast.16), custom_call_target="tpu_custom_call" | custom-call | flops 1 | bytes 1 | tf_op jit(solution)/shard_map/inner_blur/pallas_call | solution.py:223
  17.3 13.5 %collective-permute-done.3.facing_ref = bf16[2064,128]{1,0:T(8,128)(2,1)S(1)} collective-permute-done((bf16[2064,128]{1,0:T(8,128)(2,1)S(1)}, bf16[2064,128]{1,0:T(8,128)(2,1)S(1)}, u32[]{:S(2)}, u32[]{:S(2)}) %collective-permute-start.3) | collective-permute-done | bytes 528416 | tf_op jit(solution)/shard_map/ppermute | solution.py:397
  30.8 4.1 %collective-permute-done.2.beyond_ref = bf16[8,256,128]{2,1,0:T(8,128)(2,1)S(1)} collective-permute-done((bf16[8,256,128]{2,1,0:T(8,128)(2,1)S(1)}, bf16[8,256,128]{2,1,0:T(8,128)(2,1)S(1)}, u32[]{:S(2)}, u32[]{:S(2)}) %collective-permute-start.2) | collective-permute-done | bytes 524320 | tf_op jit(solution)/shard_map/ppermute | solution.py:399
  35.1 1.4 %collective-permute-done.5.corner_ref = bf16[3,256,128]{2,1,0:T(8,128)(2,1)S(1)} collective-permute-done((bf16[3,256,128]{2,1,0:T(8,128)(2,1)S(1)}, bf16[3,256,128]{2,1,0:T(8,128)(2,1)S(1)}, u32[]{:S(2)}, u32[]{:S(2)}) %collective-permute-start.5) | collective-permute-done | bytes 196640 | tf_op jit(solution)/shard_map/ppermute | solution.py:352
  36.5 2.4 %halo_blur.1 = bf16[256,1024]{1,0:T(8,128)(2,1)S(1)} custom-call(bf16[8,256,128]{2,1,0:T(8,128)(2,1)S(1)} %get-tuple-element.26.near_ref, bf16[8,256,128]{2,1,0:T(8,128)(2,1)S(1)} %collective-permute-done.2.beyond_ref, bf16[2,256,128]{2,1,0:T(8,128)(2,1)S(1)} %collective-permute-done.edge_ref, bf16[3,256,128]{2,1,0:T(8,128)(2,1)S(1)} %collective-permute-done.5.corner_ref, ...), custom_call_target="tpu_custom_call" | custom-call | flops 1 | bytes 1 | tf_op jit(solution)/shard_map/halo_blur/pallas_call | solution.py:223
  39.6 4.4 %blur_score_pick.1 = bf16[256,1024]{1,0:T(8,128)(2,1)S(1)} custom-call(bf16[2064,128]{1,0:T(8,128)(2,1)S(1)} %get-tuple-element.31.near_ref, bf16[8,256,128]{2,1,0:T(8,128)(2,1)} %get-tuple-element.33.outer_ref, bf16[2064,128]{1,0:T(8,128)(2,1)S(1)} %collective-permute-done.3.facing_ref, bf16[8,256,128]{2,1,0:T(8,128)(2,1)S(1)} %collective-permute-done.4.across_ref, ...), custom_call_target="tpu_custom_call" | custom-call | flops 1 | bytes 1 | tf_op jit(solution)/shard_map/blur_score_pick/pallas_call | solution.py:223
  44.0 4.6 %collective-permute-start.10 = (bf16[256,1024]{1,0:T(8,128)(2,1)S(1)}, bf16[256,1024]{1,0:T(8,128)(2,1)S(1)}, u32[]{:S(2)}, u32[]{:S(2)}) collective-permute-start(bf16[256,1024]{1,0:T(8,128)(2,1)S(1)} %blur_score_pick.1), channel_id=1, source_target_pairs={{4,0},{14,2},{8,4},{2,6},{12,8},{6,10},{0,12},{10,14},{5,1},{15,3}... | collective-permute-start | bytes 1572872 | tf_op jit(solution)/shard_map/ppermute | solution.py:410
  48.6 4.3 %collective-permute-done.6.halo_ref = bf16[256,1024]{1,0:T(8,128)(2,1)S(1)} collective-permute-done((bf16[256,1024]{1,0:T(8,128)(2,1)S(1)}, bf16[256,1024]{1,0:T(8,128)(2,1)S(1)}, u32[]{:S(2)}, u32[]{:S(2)}) %collective-permute-start.6) | collective-permute-done | bytes 524320 | tf_op jit(solution)/shard_map/ppermute | solution.py:407
  54.1 1.4 %collective-permute-start.8 = (bf16[256,1024]{1,0:T(8,128)(2,1)S(1)}, bf16[256,1024]{1,0:T(8,128)(2,1)S(1)}, u32[]{:S(2)}, u32[]{:S(2)}) collective-permute-start(bf16[256,1024]{1,0:T(8,128)(2,1)S(1)} %join_score.1), channel_id=1, source_target_pairs={{0,2},{2,0},{4,6},{6,4},{8,10},{10,8},{12,14},{14,12},{1,3},{3,1},... | collective-permute-start | bytes 1572872 | tf_op jit(solution)/shard_map/ppermute | solution.py:414
  55.5 3.5 %collective-permute-start.7 = (bf16[256,1024]{1,0:T(8,128)(2,1)S(1)}, bf16[256,1024]{1,0:T(8,128)(2,1)S(1)}, u32[]{:S(2)}, u32[]{:S(2)}) collective-permute-start(bf16[256,1024]{1,0:T(8,128)(2,1)S(1)} %join_score.1), channel_id=1, source_target_pairs={{4,0},{14,2},{8,4},{2,6},{12,8},{6,10},{0,12},{10,14},{5,1},{15,3}... | collective-permute-start | bytes 1572872 | tf_op jit(solution)/shard_map/ppermute | solution.py:415
  59.0 1.9 %collective-permute-done.10 = bf16[256,1024]{1,0:T(8,128)(2,1)S(1)} collective-permute-done((bf16[256,1024]{1,0:T(8,128)(2,1)S(1)}, bf16[256,1024]{1,0:T(8,128)(2,1)S(1)}, u32[]{:S(2)}, u32[]{:S(2)}) %collective-permute-start.10) | collective-permute-done | bytes 524320 | tf_op jit(solution)/shard_map/ppermute | solution.py:410
  61.4 6.4 %collective-permute-done.9 = bf16[256,1024]{1,0:T(8,128)(2,1)S(1)} collective-permute-done((bf16[256,1024]{1,0:T(8,128)(2,1)S(1)}, bf16[256,1024]{1,0:T(8,128)(2,1)S(1)}, u32[]{:S(2)}, u32[]{:S(2)}) %collective-permute-start.9) | collective-permute-done | bytes 524320 | tf_op jit(solution)/shard_map/ppermute | solution.py:413
  67.8 11.2 %collective-permute-done.8 = bf16[256,1024]{1,0:T(8,128)(2,1)S(1)} collective-permute-done((bf16[256,1024]{1,0:T(8,128)(2,1)S(1)}, bf16[256,1024]{1,0:T(8,128)(2,1)S(1)}, u32[]{:S(2)}, u32[]{:S(2)}) %collective-permute-start.8) | collective-permute-done | bytes 524320 | tf_op jit(solution)/shard_map/ppermute | solution.py:414
  79.3 1.9 %collective-permute-start.15 = (bf16[256,1024]{1,0:T(8,128)(2,1)S(1)}, bf16[256,1024]{1,0:T(8,128)(2,1)}, u32[]{:S(2)}, u32[]{:S(2)}) collective-permute-start(bf16[256,1024]{1,0:T(8,128)(2,1)S(1)} %join_score.1), channel_id=1, source_target_pairs={{0,4},{2,14},{4,8},{6,2},{8,12},{10,6},{12,0},{14,10},{1,5},{3,15}... | collective-permute-start | bytes 1572872 | tf_op jit(solution)/shard_map/ppermute | solution.py:425
  81.2 3.6 %collective-permute-start.13 = (bf16[256,1024]{1,0:T(8,128)(2,1)S(1)}, bf16[256,1024]{1,0:T(8,128)(2,1)}, u32[]{:S(2)}, u32[]{:S(2)}) collective-permute-start(bf16[256,1024]{1,0:T(8,128)(2,1)S(1)} %collective-permute-done.7), channel_id=1, source_target_pairs={{0,2},{2,0},{4,6},{6,4},{8,10},{10,8},{12,14},{14,12},{1,3},{3,1},... | collective-permute-start | bytes 1572872 | tf_op jit(solution)/shard_map/ppermute | solution.py:424
  84.8 5.5 %collective-permute-done.19 = bf16[256,1024]{1,0:T(8,128)(2,1)S(1)} collective-permute-done((bf16[256,1024]{1,0:T(8,128)(2,1)S(1)}, bf16[256,1024]{1,0:T(8,128)(2,1)S(1)}, u32[]{:S(2)}, u32[]{:S(2)}) %collective-permute-start.19) | collective-permute-done | bytes 524320 | tf_op jit(solution)/shard_map/ppermute | solution.py:418
  90.9 4.6 %collective-permute-done.15 = bf16[256,1024]{1,0:T(8,128)(2,1)} collective-permute-done((bf16[256,1024]{1,0:T(8,128)(2,1)S(1)}, bf16[256,1024]{1,0:T(8,128)(2,1)}, u32[]{:S(2)}, u32[]{:S(2)}) %collective-permute-start.15) | collective-permute-done | bytes 524320 | tf_op jit(solution)/shard_map/ppermute | solution.py:425
  96.9 2.9 %collective-permute-done.13 = bf16[256,1024]{1,0:T(8,128)(2,1)} collective-permute-done((bf16[256,1024]{1,0:T(8,128)(2,1)S(1)}, bf16[256,1024]{1,0:T(8,128)(2,1)}, u32[]{:S(2)}, u32[]{:S(2)}) %collective-permute-start.13) | collective-permute-done | bytes 524320 | tf_op jit(solution)/shard_map/ppermute | solution.py:424
  101.1 7.0 %tiles.2.refs_8_ = bf16[8,16,2,128,128]{4,3,2,1,0:T(8,128)(2,1)} custom-call(s32[8,16]{1,0:T(8,128)} %get-tuple-element.47.place_ref, s32[8,16]{1,0:T(8,128)} %fusion.17.present_ref, bf16[3,256,1024]{2,1,0:T(8,128)(2,1)} %copy-done.3, bf16[3,256,1024]{2,1,0:T(8,128)(2,1)} %collective-permute-done.17.refs_1_, bf16[1,256,1024]{2,1,0:T(8,128)(2,1)} %bitcast.23, ...), custom_call_target="tpu_custom_call" | custom-call | flops 1 | bytes 1 | tf_op jit(solution)/shard_map/tiles/pallas_call | solution.py:318
  108.1 7.0 %tiles.3 = bf16[8,16,2,128,128]{4,3,2,1,0:T(8,128)(2,1)} custom-call(s32[8,16]{1,0:T(8,128)} %get-tuple-element.48.place_ref, s32[8,16]{1,0:T(8,128)} %fusion.17.present_ref, bf16[2,256,1024]{2,1,0:T(8,128)(2,1)} %copy-done.4, bf16[2,256,1024]{2,1,0:T(8,128)(2,1)} %collective-permute-done.11.refs_1_, ...), custom_call_target="tpu_custom_call", output_to_operand_aliasing={{}: (10, {})} | custom-call | flops 1 | bytes 1 | tf_op jit(solution)/shard_map/tiles/pallas_call | solution.py:318
  (57 shorter events, 9.1 us)
Async XLA Ops:
  5.3 25.5 %collective-permute-start.3 = (bf16[2064,128]{1,0:T(8,128)(2,1)S(1)}, bf16[2064,128]{1,0:T(8,128)(2,1)S(1)}, u32[]{:S(2)}, u32[]{:S(2)}) collective-permute-start(bf16[2064,128]{1,0:T(8,128)(2,1)S(1)} %get-tuple-element.31.near_ref), channel_id=1, source_target_pairs={{0,2},{2,0},{4,6},{6,4},{8,10},{10,8},{12,14},{14,12},{1,3},{3,1},... | collective-permute-start | bytes 1585160 | tf_op jit(solution)/shard_map/ppermute | solution.py:397
  8.3 9.0 %collective-permute-start.4 = (bf16[8,256,128]{2,1,0:T(8,128)(2,1)}, bf16[8,256,128]{2,1,0:T(8,128)(2,1)S(1)}, u32[]{:S(2)}, u32[]{:S(2)}) collective-permute-start(bf16[8,256,128]{2,1,0:T(8,128)(2,1)} %get-tuple-element.33.outer_ref), channel_id=1, source_target_pairs={{2,4},{4,2},{6,8},{8,6},{10,12},{12,10},{3,5},{5,3},{7,9},{9,7},{1... | collective-permute-start | bytes 1572872 | tf_op jit(solution)/shard_map/ppermute | solution.py:398
  9.0 25.9 %collective-permute-start.2 = (bf16[8,256,128]{2,1,0:T(8,128)(2,1)S(1)}, bf16[8,256,128]{2,1,0:T(8,128)(2,1)S(1)}, u32[]{:S(2)}, u32[]{:S(2)}) collective-permute-start(bf16[8,256,128]{2,1,0:T(8,128)(2,1)S(1)} %get-tuple-element.27.outer_ref), channel_id=1, source_target_pairs={{2,6},{4,0},{6,10},{8,4},{10,14},{12,8},{3,7},{5,1},{7,11},{9,5},{... | collective-permute-start | bytes 1572872 | tf_op jit(solution)/shard_map/ppermute | solution.py:399
  10.5 1.6 %collective-permute-start.1 = (bf16[2,256,128]{2,1,0:T(8,128)(2,1)}, bf16[2,256,128]{2,1,0:T(8,128)(2,1)S(1)}, u32[]{:S(2)}, u32[]{:S(2)}) collective-permute-start(bf16[2,256,128]{2,1,0:T(8,128)(2,1)} %get-tuple-element.29), channel_id=1, source_target_pairs={{0,1},{1,0},{2,3},{3,2},{4,5},{5,4},{6,7},{7,6},{8,9},{9,8},{10,11... | collective-permute-start | bytes 393224 | tf_op jit(solution)/shard_map/ppermute | solution.py:352
  10.6 1.5 %collective-permute-start = (bf16[2,256,128]{2,1,0:T(8,128)(2,1)S(1)}, bf16[2,256,128]{2,1,0:T(8,128)(2,1)S(1)}, u32[]{:S(2)}, u32[]{:S(2)}) collective-permute-start(bf16[2,256,128]{2,1,0:T(8,128)(2,1)S(1)} %get-tuple-element.28), channel_id=1, source_target_pairs={{0,1},{1,0},{2,3},{3,2},{4,5},{5,4},{6,7},{7,6},{8,9},{9,8},{10,11... | collective-permute-start | bytes 393224 | tf_op jit(solution)/shard_map/ppermute | solution.py:352
  35.0 1.5 %collective-permute-start.5 = (bf16[3,256,128]{2,1,0:T(8,128)(2,1)S(1)}, bf16[3,256,128]{2,1,0:T(8,128)(2,1)S(1)}, u32[]{:S(2)}, u32[]{:S(2)}) collective-permute-start(bf16[3,256,128]{2,1,0:T(8,128)(2,1)S(1)} %pad_maximum_fusion.2), channel_id=1, source_target_pairs={{0,1},{1,0},{2,3},{3,2},{4,5},{5,4},{6,7},{7,6},{8,9},{9,8},{10,11... | collective-permute-start | bytes 589832 | tf_op jit(solution)/shard_map/ppermute | solution.py:352
  38.9 14.0 %collective-permute-start.6 = (bf16[256,1024]{1,0:T(8,128)(2,1)S(1)}, bf16[256,1024]{1,0:T(8,128)(2,1)S(1)}, u32[]{:S(2)}, u32[]{:S(2)}) collective-permute-start(bf16[256,1024]{1,0:T(8,128)(2,1)S(1)} %halo_blur.1), channel_id=1, source_target_pairs={{0,2},{2,0},{4,6},{6,4},{8,10},{10,8},{12,14},{14,12},{1,3},{3,1},... | collective-permute-start | bytes 1572872 | tf_op jit(solution)/shard_map/ppermute | solution.py:407
  44.0 16.9 %collective-permute-start.10 = (bf16[256,1024]{1,0:T(8,128)(2,1)S(1)}, bf16[256,1024]{1,0:T(8,128)(2,1)S(1)}, u32[]{:S(2)}, u32[]{:S(2)}) collective-permute-start(bf16[256,1024]{1,0:T(8,128)(2,1)S(1)} %blur_score_pick.1), channel_id=1, source_target_pairs={{4,0},{14,2},{8,4},{2,6},{12,8},{6,10},{0,12},{10,14},{5,1},{15,3}... | collective-permute-start | bytes 1572872 | tf_op jit(solution)/shard_map/ppermute | solution.py:410
  52.9 14.9 %collective-permute-start.9 = (bf16[256,1024]{1,0:T(8,128)(2,1)S(1)}, bf16[256,1024]{1,0:T(8,128)(2,1)S(1)}, u32[]{:S(2)}, u32[]{:S(2)}) collective-permute-start(bf16[256,1024]{1,0:T(8,128)(2,1)S(1)} %blur_score_pick.1), channel_id=1, source_target_pairs={{0,2},{2,0},{4,6},{6,4},{8,10},{10,8},{12,14},{14,12},{1,3},{3,1},... | collective-permute-start | bytes 1572872 | tf_op jit(solution)/shard_map/ppermute | solution.py:413
  54.1 24.9 %collective-permute-start.8 = (bf16[256,1024]{1,0:T(8,128)(2,1)S(1)}, bf16[256,1024]{1,0:T(8,128)(2,1)S(1)}, u32[]{:S(2)}, u32[]{:S(2)}) collective-permute-start(bf16[256,1024]{1,0:T(8,128)(2,1)S(1)} %join_score.1), channel_id=1, source_target_pairs={{0,2},{2,0},{4,6},{6,4},{8,10},{10,8},{12,14},{14,12},{1,3},{3,1},... | collective-permute-start | bytes 1572872 | tf_op jit(solution)/shard_map/ppermute | solution.py:414
  55.5 23.5 %collective-permute-start.7 = (bf16[256,1024]{1,0:T(8,128)(2,1)S(1)}, bf16[256,1024]{1,0:T(8,128)(2,1)S(1)}, u32[]{:S(2)}, u32[]{:S(2)}) collective-permute-start(bf16[256,1024]{1,0:T(8,128)(2,1)S(1)} %join_score.1), channel_id=1, source_target_pairs={{4,0},{14,2},{8,4},{2,6},{12,8},{6,10},{0,12},{10,14},{5,1},{15,3}... | collective-permute-start | bytes 1572872 | tf_op jit(solution)/shard_map/ppermute | solution.py:415
  60.9 29.3 %collective-permute-start.19 = (bf16[256,1024]{1,0:T(8,128)(2,1)S(1)}, bf16[256,1024]{1,0:T(8,128)(2,1)S(1)}, u32[]{:S(2)}, u32[]{:S(2)}) collective-permute-start(bf16[256,1024]{1,0:T(8,128)(2,1)S(1)} %collective-permute-done.10), channel_id=1, source_target_pairs={{0,2},{2,0},{4,6},{6,4},{8,10},{10,8},{12,14},{14,12},{1,3},{3,1},... | collective-permute-start | bytes 1572872 | tf_op jit(solution)/shard_map/ppermute | solution.py:418
  61.4 28.9 %collective-permute-start.18 = (bf16[256,1024]{1,0:T(8,128)(2,1)S(1)}, bf16[256,1024]{1,0:T(8,128)(2,1)S(1)}, u32[]{:S(2)}, u32[]{:S(2)}) collective-permute-start(bf16[256,1024]{1,0:T(8,128)(2,1)S(1)} %blur_score_pick.1), channel_id=1, source_target_pairs={{0,4},{2,14},{4,8},{6,2},{8,12},{10,6},{12,0},{14,10},{1,5},{3,15}... | collective-permute-start | bytes 1572872 | tf_op jit(solution)/shard_map/ppermute | solution.py:417
  79.2 21.9 %copy-start.3 = (bf16[3,256,1024]{2,1,0:T(8,128)(2,1)}, bf16[3,256,1024]{2,1,0:T(8,128)(2,1)S(1)}, u32[]{:S(2)}) copy-start(bf16[3,256,1024]{2,1,0:T(8,128)(2,1)S(1)} %pad_maximum_fusion.refs_0_) | copy-start | bytes 4718596
  79.2 20.7 %copy-start.10 = (s32[8,16]{1,0:T(8,128)S(1)}, s32[8,16]{1,0:T(8,128)}, u32[]{:S(2)}) copy-start(s32[8,16]{1,0:T(8,128)} %param.5) | copy-start | bytes 1540
  79.2 21.9 %collective-permute-start.17 = (bf16[3,256,1024]{2,1,0:T(8,128)(2,1)S(1)}, bf16[3,256,1024]{2,1,0:T(8,128)(2,1)}, u32[]{:S(2)}, u32[]{:S(2)}) collective-permute-start(bf16[3,256,1024]{2,1,0:T(8,128)(2,1)S(1)} %pad_maximum_fusion.refs_0_), channel_id=1, source_target_pairs={{0,1},{1,0},{2,3},{3,2},{4,5},{5,4},{6,7},{7,6},{8,9},{9,8},{10,11... | collective-permute-start | bytes 4718600 | tf_op jit(solution)/shard_map/ppermute | solution.py:352
  79.3 16.2 %collective-permute-start.15 = (bf16[256,1024]{1,0:T(8,128)(2,1)S(1)}, bf16[256,1024]{1,0:T(8,128)(2,1)}, u32[]{:S(2)}, u32[]{:S(2)}) collective-permute-start(bf16[256,1024]{1,0:T(8,128)(2,1)S(1)} %join_score.1), channel_id=1, source_target_pairs={{0,4},{2,14},{4,8},{6,2},{8,12},{10,6},{12,0},{14,10},{1,5},{3,15}... | collective-permute-start | bytes 1572872 | tf_op jit(solution)/shard_map/ppermute | solution.py:425
  81.2 18.6 %collective-permute-start.13 = (bf16[256,1024]{1,0:T(8,128)(2,1)S(1)}, bf16[256,1024]{1,0:T(8,128)(2,1)}, u32[]{:S(2)}, u32[]{:S(2)}) collective-permute-start(bf16[256,1024]{1,0:T(8,128)(2,1)S(1)} %collective-permute-done.7), channel_id=1, source_target_pairs={{0,2},{2,0},{4,6},{6,4},{8,10},{10,8},{12,14},{14,12},{1,3},{3,1},... | collective-permute-start | bytes 1572872 | tf_op jit(solution)/shard_map/ppermute | solution.py:424
  90.2 5.3 %collective-permute-start.20 = (bf16[1,256,1024]{2,1,0:T(8,128)(2,1)S(1)}, bf16[1,256,1024]{2,1,0:T(8,128)(2,1)S(1)}, u32[]{:S(2)}, u32[]{:S(2)}) collective-permute-start(bf16[1,256,1024]{2,1,0:T(8,128)(2,1)S(1)} %bitcast.22), channel_id=1, source_target_pairs={{0,1},{1,0},{2,3},{3,2},{4,5},{5,4},{6,7},{7,6},{8,9},{9,8},{10,11... | collective-permute-start | bytes 1572872 | tf_op jit(solution)/shard_map/ppermute | solution.py:352
  90.3 5.8 %collective-permute-start.21 = (bf16[1,256,1024]{2,1,0:T(8,128)(2,1)S(1)}, bf16[1,256,1024]{2,1,0:T(8,128)(2,1)S(1)}, u32[]{:S(2)}, u32[]{:S(2)}) collective-permute-start(bf16[1,256,1024]{2,1,0:T(8,128)(2,1)S(1)} %bitcast.20), channel_id=1, source_target_pairs={{0,1},{1,0},{2,3},{3,2},{4,5},{5,4},{6,7},{7,6},{8,9},{9,8},{10,11... | collective-permute-start | bytes 1572872 | tf_op jit(solution)/shard_map/ppermute | solution.py:352
  95.5 12.6 %collective-permute-start.11 = (bf16[2,256,1024]{2,1,0:T(8,128)(2,1)S(1)}, bf16[2,256,1024]{2,1,0:T(8,128)(2,1)}, u32[]{:S(2)}, u32[]{:S(2)}) collective-permute-start(bf16[2,256,1024]{2,1,0:T(8,128)(2,1)S(1)} %pad_maximum_fusion.1.refs_0_), channel_id=1, source_target_pairs={{0,1},{1,0},{2,3},{3,2},{4,5},{5,4},{6,7},{7,6},{8,9},{9,8},{10,11... | collective-permute-start | bytes 3145736 | tf_op jit(solution)/shard_map/ppermute | solution.py:352
  95.5 12.6 %collective-permute-start.12 = (bf16[1,256,1024]{2,1,0:T(8,128)(2,1)S(1)}, bf16[1,256,1024]{2,1,0:T(8,128)(2,1)}, u32[]{:S(2)}, u32[]{:S(2)}) collective-permute-start(bf16[1,256,1024]{2,1,0:T(8,128)(2,1)S(1)} %bitcast.18), channel_id=1, source_target_pairs={{0,1},{1,0},{2,3},{3,2},{4,5},{5,4},{6,7},{7,6},{8,9},{9,8},{10,11... | collective-permute-start | bytes 1572872 | tf_op jit(solution)/shard_map/ppermute | solution.py:352
  96.3 11.8 %collective-permute-start.16 = (bf16[1,256,1024]{2,1,0:T(8,128)(2,1)}, bf16[1,256,1024]{2,1,0:T(8,128)(2,1)}, u32[]{:S(2)}, u32[]{:S(2)}) collective-permute-start(bf16[1,256,1024]{2,1,0:T(8,128)(2,1)} %bitcast.6.refs_6_), channel_id=1, source_target_pairs={{0,1},{1,0},{2,3},{3,2},{4,5},{5,4},{6,7},{7,6},{8,9},{9,8},{10,11... | collective-permute-start | bytes 1572872 | tf_op jit(solution)/shard_map/ppermute | solution.py:352
  99.8 8.3 %collective-permute-start.14 = (bf16[1,256,1024]{2,1,0:T(8,128)(2,1)}, bf16[1,256,1024]{2,1,0:T(8,128)(2,1)}, u32[]{:S(2)}, u32[]{:S(2)}) collective-permute-start(bf16[1,256,1024]{2,1,0:T(8,128)(2,1)} %bitcast.5.refs_4_), channel_id=1, source_target_pairs={{0,1},{1,0},{2,3},{3,2},{4,5},{5,4},{6,7},{7,6},{8,9},{9,8},{10,11... | collective-permute-start | bytes 1572872 | tf_op jit(solution)/shard_map/ppermute | solution.py:352
  (9 other events, 59.1 us)

commit v21 on v14

--- a/solution.py
+++ b/solution.py
@@ -392,7 +392,7 @@
     rest_0 = after(rest_0, ahead_1)
     behind_0 = after(behind_0, rest_0)
     rest_1 = lax.ppermute(after(ahead_1, rest_0), "row", in_pair)
-    behind_1 = lax.ppermute(after(own_1, rest_0), "row", behind)
+    behind_1 = lax.ppermute(after(own_1, ahead_1), "row", behind)
     sources_0 = both(own_0, ahead_0) + both(behind_0, pair_0) + both(rest_0)
     out = make_tiles(0, windows, place_0, present, sources_0, None)
     rest_1, behind_1 = after(rest_1, out), after(behind_1, out)

time: 114 us -> 114 us (level)
    ppermute x1, starting transfers between devices: 0.51 us -> 2.22 us  [on_device(): rest_1 = lax.ppermute(after(ahead_1, rest_0), 'row', in_pair)]
where the time goes in v21:
time: 114 us; the launch traced here: 113 us
  waiting for transfers between devices  46.6 us (41%)
  Pallas kernels  29.9 us (26%)
  starting transfers between devices  29.9 us (26%)
  local copies, waits for them, and re-layouts  5.16 us (5%)
  other arithmetic  1.58 us (1%)
    pallas_call x4, Pallas kernels, call_on_rows(): pl.pallas_call(kernel, grid=(1,), in_specs=[whole(value) for value in ope...  14.4 us
    pallas_call x2, Pallas kernels, make_tiles(): pl.pallas_call(functools.partial(tiles_kernel, sources=count, window=wind...  12.2 us
    ppermute x1, waiting for transfers between devices, on_device(): pair_1 = lax.ppermute(own_1, 'row', in_pair)  11.2 us
    ppermute x1, waiting for transfers between devices, on_device(): facing_0 = lax.ppermute(after(near_0, gm_pair), 'row', in_pair)  9.42 us
    ppermute x1, waiting for transfers between devices, on_device(): rest_0 = lax.ppermute(ahead_0, 'row', in_pair)  9.21 us
    ppermute x11, waiting for transfers between devices, other_col(): return lax.ppermute(value, 'col', [(0, 1), (1, 0)])  5.66 us
    ppermute x1, starting transfers between devices, on_device(): gm_pair = lax.ppermute(gm, 'row', in_pair)  5.28 us
    unnamed x16, local copies, waits for them, and re-layouts  5.16 us
  transfers between devices with their start and end apart: 24, of which 14 were waited for; matrix products, arithmetic and copies ran while one was open for 1% of the time, Pallas kernels for 18%

profile of v21, /device:TPU:0, one launch (start us, length us, event | category | flops | bytes accessed | tf_op | source)
XLA Modules:
  0.0 113.5 jit_solution(7276284297010310977)
XLA Ops:
  0.0 1.6 %copy-done = bf16[2,256,2,8,128]{4,3,2,1,0:T(8,128)(2,1)S(1)} copy-done((bf16[2,256,2,8,128]{4,3,2,1,0:T(8,128)(2,1)S(1)}, bf16[2,256,2,8,128]{4,3,2,1,0:T(8,128)(2,1)}, u32[]{:S(2)}) %copy-start) | copy-done | bytes 2097176
  1.6 3.4 %faces.1 = (bf16[8,256,128]{2,1,0:T(8,128)(2,1)}, bf16[8,256,128]{2,1,0:T(8,128)(2,1)}, bf16[2,256,128]{2,1,0:T(8,128)(2,1)S(1)}, bf16[8,256,128]{2,1,0:T(8,128)...) custom-call(bf16[2,256,2,8,128]{4,3,2,1,0:T(8,128)(2,1)S(1)} %copy-done), custom_call_target="tpu_custom_call" | custom-call | flops 1 | bytes 1 | tf_op jit(solution)/shard_map/faces/pallas_call | solution.py:59
  5.0 1.4 %collective-permute-start.2 = (bf16[8,256,128]{2,1,0:T(8,128)(2,1)}, bf16[8,256,128]{2,1,0:T(8,128)(2,1)S(1)}, u32[]{:S(2)}, u32[]{:S(2)}) collective-permute-start(bf16[8,256,128]{2,1,0:T(8,128)(2,1)} %get-tuple-element.32.outer_ref), channel_id=1, source_target_pairs={{2,6},{4,0},{6,10},{8,4},{10,14},{12,8},{3,7},{5,1},{7,11},{9,5},{... | collective-permute-start | bytes 1572872 | tf_op jit(solution)/shard_map/ppermute | solution.py:369
  6.4 5.3 %collective-permute-start.4 = (s32[1,1024]{1,0:T(1,128)}, s32[1,1024]{1,0:T(1,128)S(1)}, u32[]{:S(2)}, u32[]{:S(2)}) collective-permute-start(s32[1,1024]{1,0:T(1,128)} %bitcast.16), channel_id=1, source_target_pairs={{0,2},{2,0},{4,6},{6,4},{8,10},{10,8},{12,14},{14,12},{1,3},{3,1},... | collective-permute-start | bytes 12296 | tf_op jit(solution)/shard_map/ppermute | solution.py:363
  11.7 1.8 %collective-permute-done.4.gm_ref = s32[1,1024]{1,0:T(1,128)S(1)} collective-permute-done((s32[1,1024]{1,0:T(1,128)}, s32[1,1024]{1,0:T(1,128)S(1)}, u32[]{:S(2)}, u32[]{:S(2)}) %collective-permute-start.4) | collective-permute-done | bytes 4128 | tf_op jit(solution)/shard_map/ppermute | solution.py:363
  14.3 4.3 %collective-permute-start.5 = (bf16[8,256,128]{2,1,0:T(8,128)(2,1)}, bf16[8,256,128]{2,1,0:T(8,128)(2,1)S(1)}, u32[]{:S(2)}, u32[]{:S(2)}) collective-permute-start(bf16[8,256,128]{2,1,0:T(8,128)(2,1)} %get-tuple-element.38.near_ref), channel_id=1, source_target_pairs={{0,2},{2,0},{4,6},{6,4},{8,10},{10,8},{12,14},{14,12},{1,3},{3,1},... | collective-permute-start | bytes 1572872 | tf_op jit(solution)/shard_map/ppermute | solution.py:370
  20.8 6.2 %inner_blur.1.inner_ref = f32[256,1024]{1,0:T(8,128)S(1)} custom-call(bf16[8,256,128]{2,1,0:T(8,128)(2,1)S(1)} %get-tuple-element.31.near_ref, bf16[8,256,128]{2,1,0:T(8,128)(2,1)} %get-tuple-element.32.outer_ref, bf16[2,256,128]{2,1,0:T(8,128)(2,1)S(1)} %collective-permute-done.edge_ref, s32[1,1024]{1,0:T(1,128)S(1)} %bitcast.17), custom_call_target="tpu_custom_call" | custom-call | flops 1 | bytes 1 | tf_op jit(solution)/shard_map/inner_blur/pallas_call | solution.py:200
  28.4 2.4 %halo_blur.1 = bf16[256,1024]{1,0:T(8,128)(2,1)S(1)} custom-call(bf16[8,256,128]{2,1,0:T(8,128)(2,1)S(1)} %get-tuple-element.31.near_ref, bf16[8,256,128]{2,1,0:T(8,128)(2,1)S(1)} %collective-permute-done.2.beyond_ref, bf16[2,256,128]{2,1,0:T(8,128)(2,1)S(1)} %collective-permute-done.edge_ref, bf16[256,128]{1,0:T(8,128)(2,1)S(1)} %bitcast.15, ...), custom_call_target="tpu_custom_call" | custom-call | flops 1 | bytes 1 | tf_op jit(solution)/shard_map/halo_blur/pallas_call | solution.py:200
  30.8 9.4 %collective-permute-done.5.facing_ref = bf16[8,256,128]{2,1,0:T(8,128)(2,1)S(1)} collective-permute-done((bf16[8,256,128]{2,1,0:T(8,128)(2,1)}, bf16[8,256,128]{2,1,0:T(8,128)(2,1)S(1)}, u32[]{:S(2)}, u32[]{:S(2)}) %collective-permute-start.5) | collective-permute-done | bytes 524320 | tf_op jit(solution)/shard_map/ppermute | solution.py:370
  40.2 2.4 %collective-permute-start.7 = (bf16[256,1024]{1,0:T(8,128)(2,1)S(1)}, bf16[256,1024]{1,0:T(8,128)(2,1)S(1)}, u32[]{:S(2)}, u32[]{:S(2)}) collective-permute-start(bf16[256,1024]{1,0:T(8,128)(2,1)S(1)} %halo_blur.1), channel_id=1, source_target_pairs={{0,2},{2,0},{4,6},{6,4},{8,10},{10,8},{12,14},{14,12},{1,3},{3,1},... | collective-permute-start | bytes 1572872 | tf_op jit(solution)/shard_map/ppermute | solution.py:377
  42.7 1.3 %collective-permute-done.8.corner_ref = bf16[2,256,128]{2,1,0:T(8,128)(2,1)S(1)} collective-permute-done((bf16[2,256,128]{2,1,0:T(8,128)(2,1)S(1)}, bf16[2,256,128]{2,1,0:T(8,128)(2,1)S(1)}, u32[]{:S(2)}, u32[]{:S(2)}) %collective-permute-start.8) | collective-permute-done | bytes 131104 | tf_op jit(solution)/shard_map/ppermute | solution.py:329
  44.7 4.5 %blur_score_pick.1 = bf16[256,1024]{1,0:T(8,128)(2,1)S(1)} custom-call(bf16[8,256,128]{2,1,0:T(8,128)(2,1)} %get-tuple-element.38.near_ref, bf16[8,256,128]{2,1,0:T(8,128)(2,1)} %get-tuple-element.41.outer_ref, bf16[8,256,128]{2,1,0:T(8,128)(2,1)S(1)} %collective-permute-done.5.facing_ref, bf16[8,256,128]{2,1,0:T(8,128)(2,1)S(1)} %collective-permute-done.6.across_ref, ...), custom_call_target="tpu_custom_call" | custom-call | flops 1 | bytes 1 | tf_op jit(solution)/shard_map/blur_score_pick/pallas_call | solution.py:200
  49.2 2.2 %collective-permute-start.12 = (bf16[256,1024]{1,0:T(8,128)(2,1)S(1)}, bf16[256,1024]{1,0:T(8,128)(2,1)S(1)}, u32[]{:S(2)}, u32[]{:S(2)}) collective-permute-start(bf16[256,1024]{1,0:T(8,128)(2,1)S(1)} %blur_score_pick.1), channel_id=1, source_target_pairs={{4,0},{14,2},{8,4},{2,6},{12,8},{6,10},{0,12},{10,14},{5,1},{15,3}... | collective-permute-start | bytes 1572872 | tf_op jit(solution)/shard_map/ppermute | solution.py:380
  52.5 1.7 %collective-permute-start.11 = (bf16[256,1024]{1,0:T(8,128)(2,1)S(1)}, bf16[256,1024]{1,0:T(8,128)(2,1)S(1)}, u32[]{:S(2)}, u32[]{:S(2)}) collective-permute-start(bf16[256,1024]{1,0:T(8,128)(2,1)S(1)} %blur_score_pick.1), channel_id=1, source_target_pairs={{0,2},{2,0},{4,6},{6,4},{8,10},{10,8},{12,14},{14,12},{1,3},{3,1},... | collective-permute-start | bytes 1572872 | tf_op jit(solution)/shard_map/ppermute | solution.py:383
  55.8 4.4 %collective-permute-start.9 = (bf16[256,1024]{1,0:T(8,128)(2,1)}, bf16[256,1024]{1,0:T(8,128)(2,1)}, u32[]{:S(2)}, u32[]{:S(2)}) collective-permute-start(bf16[256,1024]{1,0:T(8,128)(2,1)} %join_score.1), channel_id=1, source_target_pairs={{4,0},{14,2},{8,4},{2,6},{12,8},{6,10},{0,12},{10,14},{5,1},{15,3}... | collective-permute-start | bytes 1572872 | tf_op jit(solution)/shard_map/ppermute | solution.py:385
  60.2 3.9 %collective-permute-done.12 = bf16[256,1024]{1,0:T(8,128)(2,1)S(1)} collective-permute-done((bf16[256,1024]{1,0:T(8,128)(2,1)S(1)}, bf16[256,1024]{1,0:T(8,128)(2,1)S(1)}, u32[]{:S(2)}, u32[]{:S(2)}) %collective-permute-start.12) | collective-permute-done | bytes 524320 | tf_op jit(solution)/shard_map/ppermute | solution.py:380
  64.1 2.2 %collective-permute-start.15 = (bf16[256,1024]{1,0:T(8,128)(2,1)S(1)}, bf16[256,1024]{1,0:T(8,128)(2,1)}, u32[]{:S(2)}, u32[]{:S(2)}) collective-permute-start(bf16[256,1024]{1,0:T(8,128)(2,1)S(1)} %collective-permute-done.12), channel_id=1, source_target_pairs={{0,2},{2,0},{4,6},{6,4},{8,10},{10,8},{12,14},{14,12},{1,3},{3,1},... | collective-permute-start | bytes 1572872 | tf_op jit(solution)/shard_map/ppermute | solution.py:388
  67.3 11.2 %collective-permute-done.10 = bf16[256,1024]{1,0:T(8,128)(2,1)S(1)} collective-permute-done((bf16[256,1024]{1,0:T(8,128)(2,1)}, bf16[256,1024]{1,0:T(8,128)(2,1)S(1)}, u32[]{:S(2)}, u32[]{:S(2)}) %collective-permute-start.10) | collective-permute-done | bytes 524320 | tf_op jit(solution)/shard_map/ppermute | solution.py:384
  78.6 9.2 %collective-permute-done.15 = bf16[256,1024]{1,0:T(8,128)(2,1)} collective-permute-done((bf16[256,1024]{1,0:T(8,128)(2,1)S(1)}, bf16[256,1024]{1,0:T(8,128)(2,1)}, u32[]{:S(2)}, u32[]{:S(2)}) %collective-permute-start.15) | collective-permute-done | bytes 524320 | tf_op jit(solution)/shard_map/ppermute | solution.py:388
  88.4 2.2 %collective-permute-start.16 = (bf16[256,1024]{1,0:T(8,128)(2,1)}, bf16[256,1024]{1,0:T(8,128)(2,1)}, u32[]{:S(2)}, u32[]{:S(2)}) collective-permute-start(bf16[256,1024]{1,0:T(8,128)(2,1)} %collective-permute-done.9), channel_id=1, source_target_pairs={{0,2},{2,0},{4,6},{6,4},{8,10},{10,8},{12,14},{14,12},{1,3},{3,1},... | collective-permute-start | bytes 1572872 | tf_op jit(solution)/shard_map/ppermute | solution.py:394
  94.8 6.1 %tiles.2.refs_8_ = bf16[8,16,2,128,128]{4,3,2,1,0:T(8,128)(2,1)} custom-call(s32[8,16]{1,0:T(8,128)S(1)} %get-tuple-element.57.place_ref, s32[8,16]{1,0:T(8,128)S(1)} %fusion.21.present_ref, bf16[2,256,1024]{2,1,0:T(8,128)(2,1)S(1)} %pad_maximum_fusion.1.refs_0_, bf16[2,256,1024]{2,1,0:T(8,128)(2,1)S(1)} %copy-done.2, ...), custom_call_target="tpu_custom_call" | custom-call | flops 1 | bytes 1 | tf_op jit(solution)/shard_map/tiles/pallas_call | solution.py:295
  101.0 3.4 %collective-permute-done.22 = bf16[256,1024]{1,0:T(8,128)(2,1)} collective-permute-done((bf16[256,1024]{1,0:T(8,128)(2,1)}, bf16[256,1024]{1,0:T(8,128)(2,1)}, u32[]{:S(2)}, u32[]{:S(2)}) %collective-permute-start.22) | collective-permute-done | bytes 524320 | tf_op jit(solution)/shard_map/ppermute | solution.py:395
  104.9 1.6 %collective-permute-done.21.refs_5_ = bf16[1,256,1024]{2,1,0:T(8,128)(2,1)S(1)} collective-permute-done((bf16[1,256,1024]{2,1,0:T(8,128)(2,1)}, bf16[1,256,1024]{2,1,0:T(8,128)(2,1)S(1)}, u32[]{:S(2)}, u32[]{:S(2)}) %collective-permute-start.21) | collective-permute-done | bytes 524320 | tf_op jit(solution)/shard_map/ppermute | solution.py:329
  107.3 6.0 %tiles.3 = bf16[8,16,2,128,128]{4,3,2,1,0:T(8,128)(2,1)} custom-call(s32[8,16]{1,0:T(8,128)S(1)} %get-tuple-element.58.place_ref, s32[8,16]{1,0:T(8,128)S(1)} %fusion.21.present_ref, bf16[2,256,1024]{2,1,0:T(8,128)(2,1)S(1)} %pad_maximum_fusion.refs_0_, bf16[2,256,1024]{2,1,0:T(8,128)(2,1)} %collective-permute-done.13.refs_1_, ...), custom_call_target="tpu_custom_call", output_to_operand_aliasing={{}: (10, {})} | custom-call | flops 1 | bytes 1 | tf_op jit(solution)/shard_map/tiles/pallas_call | solution.py:295
  (55 shorter events, 14.9 us)
Async XLA Ops:
  5.0 22.1 %collective-permute-start.2 = (bf16[8,256,128]{2,1,0:T(8,128)(2,1)}, bf16[8,256,128]{2,1,0:T(8,128)(2,1)S(1)}, u32[]{:S(2)}, u32[]{:S(2)}) collective-permute-start(bf16[8,256,128]{2,1,0:T(8,128)(2,1)} %get-tuple-element.32.outer_ref), channel_id=1, source_target_pairs={{2,6},{4,0},{6,10},{8,4},{10,14},{12,8},{3,7},{5,1},{7,11},{9,5},{... | collective-permute-start | bytes 1572872 | tf_op jit(solution)/shard_map/ppermute | solution.py:369
  6.4 7.1 %collective-permute-start.4 = (s32[1,1024]{1,0:T(1,128)}, s32[1,1024]{1,0:T(1,128)S(1)}, u32[]{:S(2)}, u32[]{:S(2)}) collective-permute-start(s32[1,1024]{1,0:T(1,128)} %bitcast.16), channel_id=1, source_target_pairs={{0,2},{2,0},{4,6},{6,4},{8,10},{10,8},{12,14},{14,12},{1,3},{3,1},... | collective-permute-start | bytes 12296 | tf_op jit(solution)/shard_map/ppermute | solution.py:363
  13.5 17.3 %collective-permute-start.6 = (bf16[8,256,128]{2,1,0:T(8,128)(2,1)}, bf16[8,256,128]{2,1,0:T(8,128)(2,1)S(1)}, u32[]{:S(2)}, u32[]{:S(2)}) collective-permute-start(bf16[8,256,128]{2,1,0:T(8,128)(2,1)} %get-tuple-element.41.outer_ref), channel_id=1, source_target_pairs={{2,4},{4,2},{6,8},{8,6},{10,12},{12,10},{3,5},{5,3},{7,9},{9,7},{1... | collective-permute-start | bytes 1572872 | tf_op jit(solution)/shard_map/ppermute | solution.py:371
  14.3 25.9 %collective-permute-start.5 = (bf16[8,256,128]{2,1,0:T(8,128)(2,1)}, bf16[8,256,128]{2,1,0:T(8,128)(2,1)S(1)}, u32[]{:S(2)}, u32[]{:S(2)}) collective-permute-start(bf16[8,256,128]{2,1,0:T(8,128)(2,1)} %get-tuple-element.38.near_ref), channel_id=1, source_target_pairs={{0,2},{2,0},{4,6},{6,4},{8,10},{10,8},{12,14},{14,12},{1,3},{3,1},... | collective-permute-start | bytes 1572872 | tf_op jit(solution)/shard_map/ppermute | solution.py:370
  18.6 1.3 %collective-permute-start.1 = (bf16[2,256,128]{2,1,0:T(8,128)(2,1)S(1)}, bf16[2,256,128]{2,1,0:T(8,128)(2,1)S(1)}, u32[]{:S(2)}, u32[]{:S(2)}) collective-permute-start(bf16[2,256,128]{2,1,0:T(8,128)(2,1)S(1)} %get-tuple-element.34), channel_id=1, source_target_pairs={{0,1},{1,0},{2,3},{3,2},{4,5},{5,4},{6,7},{7,6},{8,9},{9,8},{10,11... | collective-permute-start | bytes 393224 | tf_op jit(solution)/shard_map/ppermute | solution.py:329
  18.6 1.5 %collective-permute-start = (bf16[2,256,128]{2,1,0:T(8,128)(2,1)S(1)}, bf16[2,256,128]{2,1,0:T(8,128)(2,1)S(1)}, u32[]{:S(2)}, u32[]{:S(2)}) collective-permute-start(bf16[2,256,128]{2,1,0:T(8,128)(2,1)S(1)} %get-tuple-element.33), channel_id=1, source_target_pairs={{0,1},{1,0},{2,3},{3,2},{4,5},{5,4},{6,7},{7,6},{8,9},{9,8},{10,11... | collective-permute-start | bytes 393224 | tf_op jit(solution)/shard_map/ppermute | solution.py:329
  27.1 1.3 %collective-permute-start.3 = (bf16[1,256,128]{2,1,0:T(8,128)(2,1)S(1)}, bf16[1,256,128]{2,1,0:T(8,128)(2,1)S(1)}, u32[]{:S(2)}, u32[]{:S(2)}) collective-permute-start(bf16[1,256,128]{2,1,0:T(8,128)(2,1)S(1)} %slice_select_fusion.2), channel_id=1, source_target_pairs={{0,1},{1,0},{2,3},{3,2},{4,5},{5,4},{6,7},{7,6},{8,9},{9,8},{10,11... | collective-permute-start | bytes 196616 | tf_op jit(solution)/shard_map/ppermute | solution.py:329
  40.2 12.2 %collective-permute-start.7 = (bf16[256,1024]{1,0:T(8,128)(2,1)S(1)}, bf16[256,1024]{1,0:T(8,128)(2,1)S(1)}, u32[]{:S(2)}, u32[]{:S(2)}) collective-permute-start(bf16[256,1024]{1,0:T(8,128)(2,1)S(1)} %halo_blur.1), channel_id=1, source_target_pairs={{0,2},{2,0},{4,6},{6,4},{8,10},{10,8},{12,14},{14,12},{1,3},{3,1},... | collective-permute-start | bytes 1572872 | tf_op jit(solution)/shard_map/ppermute | solution.py:377
  42.6 1.4 %collective-permute-start.8 = (bf16[2,256,128]{2,1,0:T(8,128)(2,1)S(1)}, bf16[2,256,128]{2,1,0:T(8,128)(2,1)S(1)}, u32[]{:S(2)}, u32[]{:S(2)}) collective-permute-start(bf16[2,256,128]{2,1,0:T(8,128)(2,1)S(1)} %pad_maximum_fusion.3), channel_id=1, source_target_pairs={{0,1},{1,0},{2,3},{3,2},{4,5},{5,4},{6,7},{7,6},{8,9},{9,8},{10,11... | collective-permute-start | bytes 393224 | tf_op jit(solution)/shard_map/ppermute | solution.py:329
  49.2 14.8 %collective-permute-start.12 = (bf16[256,1024]{1,0:T(8,128)(2,1)S(1)}, bf16[256,1024]{1,0:T(8,128)(2,1)S(1)}, u32[]{:S(2)}, u32[]{:S(2)}) collective-permute-start(bf16[256,1024]{1,0:T(8,128)(2,1)S(1)} %blur_score_pick.1), channel_id=1, source_target_pairs={{4,0},{14,2},{8,4},{2,6},{12,8},{6,10},{0,12},{10,14},{5,1},{15,3}... | collective-permute-start | bytes 1572872 | tf_op jit(solution)/shard_map/ppermute | solution.py:380
  52.5 14.9 %collective-permute-start.11 = (bf16[256,1024]{1,0:T(8,128)(2,1)S(1)}, bf16[256,1024]{1,0:T(8,128)(2,1)S(1)}, u32[]{:S(2)}, u32[]{:S(2)}) collective-permute-start(bf16[256,1024]{1,0:T(8,128)(2,1)S(1)} %blur_score_pick.1), channel_id=1, source_target_pairs={{0,2},{2,0},{4,6},{6,4},{8,10},{10,8},{12,14},{14,12},{1,3},{3,1},... | collective-permute-start | bytes 1572872 | tf_op jit(solution)/shard_map/ppermute | solution.py:383
  55.5 23.1 %collective-permute-start.10 = (bf16[256,1024]{1,0:T(8,128)(2,1)}, bf16[256,1024]{1,0:T(8,128)(2,1)S(1)}, u32[]{:S(2)}, u32[]{:S(2)}) collective-permute-start(bf16[256,1024]{1,0:T(8,128)(2,1)} %join_score.1), channel_id=1, source_target_pairs={{0,2},{2,0},{4,6},{6,4},{8,10},{10,8},{12,14},{14,12},{1,3},{3,1},... | collective-permute-start | bytes 1572872 | tf_op jit(solution)/shard_map/ppermute | solution.py:384
  55.8 22.8 %collective-permute-start.9 = (bf16[256,1024]{1,0:T(8,128)(2,1)}, bf16[256,1024]{1,0:T(8,128)(2,1)}, u32[]{:S(2)}, u32[]{:S(2)}) collective-permute-start(bf16[256,1024]{1,0:T(8,128)(2,1)} %join_score.1), channel_id=1, source_target_pairs={{4,0},{14,2},{8,4},{2,6},{12,8},{6,10},{0,12},{10,14},{5,1},{15,3}... | collective-permute-start | bytes 1572872 | tf_op jit(solution)/shard_map/ppermute | solution.py:385
  64.1 23.7 %collective-permute-start.15 = (bf16[256,1024]{1,0:T(8,128)(2,1)S(1)}, bf16[256,1024]{1,0:T(8,128)(2,1)}, u32[]{:S(2)}, u32[]{:S(2)}) collective-permute-start(bf16[256,1024]{1,0:T(8,128)(2,1)S(1)} %collective-permute-done.12), channel_id=1, source_target_pairs={{0,2},{2,0},{4,6},{6,4},{8,10},{10,8},{12,14},{14,12},{1,3},{3,1},... | collective-permute-start | bytes 1572872 | tf_op jit(solution)/shard_map/ppermute | solution.py:388
  66.2 21.5 %collective-permute-start.18 = (bf16[256,1024]{1,0:T(8,128)(2,1)S(1)}, bf16[256,1024]{1,0:T(8,128)(2,1)S(1)}, u32[]{:S(2)}, u32[]{:S(2)}) collective-permute-start(bf16[256,1024]{1,0:T(8,128)(2,1)S(1)} %blur_score_pick.1), channel_id=1, source_target_pairs={{0,4},{2,14},{4,8},{6,2},{8,12},{10,6},{12,0},{14,10},{1,5},{3,15}... | collective-permute-start | bytes 1572872 | tf_op jit(solution)/shard_map/ppermute | solution.py:387
  67.3 24.6 %collective-permute-start.17 = (bf16[2,256,1024]{2,1,0:T(8,128)(2,1)S(1)}, bf16[2,256,1024]{2,1,0:T(8,128)(2,1)S(1)}, u32[]{:S(2)}, u32[]{:S(2)}) collective-permute-start(bf16[2,256,1024]{2,1,0:T(8,128)(2,1)S(1)} %pad_maximum_fusion.1.refs_0_), channel_id=1, source_target_pairs={{0,1},{1,0},{2,3},{3,2},{4,5},{5,4},{6,7},{7,6},{8,9},{9,8},{10,11... | collective-permute-start | bytes 3145736 | tf_op jit(solution)/shard_map/ppermute | solution.py:329
  87.9 5.7 %collective-permute-start.19 = (bf16[2,256,1024]{2,1,0:T(8,128)(2,1)S(1)}, bf16[2,256,1024]{2,1,0:T(8,128)(2,1)}, u32[]{:S(2)}, u32[]{:S(2)}) collective-permute-start(bf16[2,256,1024]{2,1,0:T(8,128)(2,1)S(1)} %pad_maximum_fusion.2.refs_2_), channel_id=1, source_target_pairs={{0,1},{1,0},{2,3},{3,2},{4,5},{5,4},{6,7},{7,6},{8,9},{9,8},{10,11... | collective-permute-start | bytes 3145736 | tf_op jit(solution)/shard_map/ppermute | solution.py:329
  88.0 16.4 %collective-permute-start.22 = (bf16[256,1024]{1,0:T(8,128)(2,1)}, bf16[256,1024]{1,0:T(8,128)(2,1)}, u32[]{:S(2)}, u32[]{:S(2)}) collective-permute-start(bf16[256,1024]{1,0:T(8,128)(2,1)} %join_score.1), channel_id=1, source_target_pairs={{0,4},{2,14},{4,8},{6,2},{8,12},{10,6},{12,0},{14,10},{1,5},{3,15}... | collective-permute-start | bytes 1572872 | tf_op jit(solution)/shard_map/ppermute | solution.py:395
  88.4 16.0 %collective-permute-start.16 = (bf16[256,1024]{1,0:T(8,128)(2,1)}, bf16[256,1024]{1,0:T(8,128)(2,1)}, u32[]{:S(2)}, u32[]{:S(2)}) collective-permute-start(bf16[256,1024]{1,0:T(8,128)(2,1)} %collective-permute-done.9), channel_id=1, source_target_pairs={{0,2},{2,0},{4,6},{6,4},{8,10},{10,8},{12,14},{14,12},{1,3},{3,1},... | collective-permute-start | bytes 1572872 | tf_op jit(solution)/shard_map/ppermute | solution.py:394
  90.7 2.9 %collective-permute-start.20 = (bf16[1,256,1024]{2,1,0:T(8,128)(2,1)}, bf16[1,256,1024]{2,1,0:T(8,128)(2,1)}, u32[]{:S(2)}, u32[]{:S(2)}) collective-permute-start(bf16[1,256,1024]{2,1,0:T(8,128)(2,1)} %bitcast.9.refs_4_), channel_id=1, source_target_pairs={{0,1},{1,0},{2,3},{3,2},{4,5},{5,4},{6,7},{7,6},{8,9},{9,8},{10,11... | collective-permute-start | bytes 1572872 | tf_op jit(solution)/shard_map/ppermute | solution.py:329
  92.9 12.0 %collective-permute-start.13 = (bf16[2,256,1024]{2,1,0:T(8,128)(2,1)S(1)}, bf16[2,256,1024]{2,1,0:T(8,128)(2,1)}, u32[]{:S(2)}, u32[]{:S(2)}) collective-permute-start(bf16[2,256,1024]{2,1,0:T(8,128)(2,1)S(1)} %pad_maximum_fusion.refs_0_), channel_id=1, source_target_pairs={{0,1},{1,0},{2,3},{3,2},{4,5},{5,4},{6,7},{7,6},{8,9},{9,8},{10,11... | collective-permute-start | bytes 3145736 | tf_op jit(solution)/shard_map/ppermute | solution.py:329
  93.5 11.4 %collective-permute-start.14 = (bf16[1,256,1024]{2,1,0:T(8,128)(2,1)}, bf16[1,256,1024]{2,1,0:T(8,128)(2,1)S(1)}, u32[]{:S(2)}, u32[]{:S(2)}) collective-permute-start(bf16[1,256,1024]{2,1,0:T(8,128)(2,1)} %bitcast.13), channel_id=1, source_target_pairs={{0,1},{1,0},{2,3},{3,2},{4,5},{5,4},{6,7},{7,6},{8,9},{9,8},{10,11... | collective-permute-start | bytes 1572872 | tf_op jit(solution)/shard_map/ppermute | solution.py:329
  104.4 2.1 %collective-permute-start.21 = (bf16[1,256,1024]{2,1,0:T(8,128)(2,1)}, bf16[1,256,1024]{2,1,0:T(8,128)(2,1)S(1)}, u32[]{:S(2)}, u32[]{:S(2)}) collective-permute-start(bf16[1,256,1024]{2,1,0:T(8,128)(2,1)} %bitcast.10.refs_4_), channel_id=1, source_target_pairs={{0,1},{1,0},{2,3},{3,2},{4,5},{5,4},{6,7},{7,6},{8,9},{9,8},{10,11... | collective-permute-start | bytes 1572872 | tf_op jit(solution)/shard_map/ppermute | solution.py:329
  104.4 2.9 %collective-permute-start.23 = (bf16[1,256,1024]{2,1,0:T(8,128)(2,1)}, bf16[1,256,1024]{2,1,0:T(8,128)(2,1)S(1)}, u32[]{:S(2)}, u32[]{:S(2)}) collective-permute-start(bf16[1,256,1024]{2,1,0:T(8,128)(2,1)} %bitcast.11.refs_6_), channel_id=1, source_target_pairs={{0,1},{1,0},{2,3},{3,2},{4,5},{5,4},{6,7},{7,6},{8,9},{9,8},{10,11... | collective-permute-start | bytes 1572872 | tf_op jit(solution)/shard_map/ppermute | solution.py:329
  (8 other events, 118.2 us)

commit v22 on v21

--- a/solution.py
+++ b/solution.py
@@ -392,7 +392,7 @@
     rest_0 = after(rest_0, ahead_1)
     behind_0 = after(behind_0, rest_0)
     rest_1 = lax.ppermute(after(ahead_1, rest_0), "row", in_pair)
-    behind_1 = lax.ppermute(after(own_1, ahead_1), "row", behind)
+    behind_1 = lax.ppermute(own_1, "row", behind)
     sources_0 = both(own_0, ahead_0) + both(behind_0, pair_0) + both(rest_0)
     out = make_tiles(0, windows, place_0, present, sources_0, None)
     rest_1, behind_1 = after(rest_1, out), after(behind_1, out)

time: 114 us -> 114 us (level)
  no operation moved by 1% of the time
where the time goes in v22:
time: 114 us; the launch traced here: 113 us
  waiting for transfers between devices  46.6 us (41%)
  Pallas kernels  29.9 us (26%)
  starting transfers between devices  29.9 us (26%)
  local copies, waits for them, and re-layouts  5.16 us (5%)
  other arithmetic  1.58 us (1%)
    pallas_call x4, Pallas kernels, call_on_rows(): pl.pallas_call(kernel, grid=(1,), in_specs=[whole(value) for value in ope...  14.4 us
    pallas_call x2, Pallas kernels, make_tiles(): pl.pallas_call(functools.partial(tiles_kernel, sources=count, window=wind...  12.2 us
    ppermute x1, waiting for transfers between devices, on_device(): pair_1 = lax.ppermute(own_1, 'row', in_pair)  11.2 us
    ppermute x1, waiting for transfers between devices, on_device(): facing_0 = lax.ppermute(after(near_0, gm_pair), 'row', in_pair)  9.42 us
    ppermute x1, waiting for transfers between devices, on_device(): rest_0 = lax.ppermute(ahead_0, 'row', in_pair)  9.21 us
    ppermute x11, waiting for transfers between devices, other_col(): return lax.ppermute(value, 'col', [(0, 1), (1, 0)])  5.66 us
    ppermute x1, starting transfers between devices, on_device(): gm_pair = lax.ppermute(gm, 'row', in_pair)  5.28 us
    unnamed x16, local copies, waits for them, and re-layouts  5.16 us
  transfers between devices with their start and end apart: 24, of which 14 were waited for; matrix products, arithmetic and copies ran while one was open for 1% of the time, Pallas kernels for 18%

profile of v22, /device:TPU:0, one launch (start us, length us, event | category | flops | bytes accessed | tf_op | source)
XLA Modules:
  0.0 113.5 jit_solution(7276284297010310977)
XLA Ops:
  0.0 1.6 %copy-done = bf16[2,256,2,8,128]{4,3,2,1,0:T(8,128)(2,1)S(1)} copy-done((bf16[2,256,2,8,128]{4,3,2,1,0:T(8,128)(2,1)S(1)}, bf16[2,256,2,8,128]{4,3,2,1,0:T(8,128)(2,1)}, u32[]{:S(2)}) %copy-start) | copy-done | bytes 2097176
  1.6 3.4 %faces.1 = (bf16[8,256,128]{2,1,0:T(8,128)(2,1)}, bf16[8,256,128]{2,1,0:T(8,128)(2,1)}, bf16[2,256,128]{2,1,0:T(8,128)(2,1)S(1)}, bf16[8,256,128]{2,1,0:T(8,128)...) custom-call(bf16[2,256,2,8,128]{4,3,2,1,0:T(8,128)(2,1)S(1)} %copy-done), custom_call_target="tpu_custom_call" | custom-call | flops 1 | bytes 1 | tf_op jit(solution)/shard_map/faces/pallas_call | solution.py:59
  5.0 1.4 %collective-permute-start.2 = (bf16[8,256,128]{2,1,0:T(8,128)(2,1)}, bf16[8,256,128]{2,1,0:T(8,128)(2,1)S(1)}, u32[]{:S(2)}, u32[]{:S(2)}) collective-permute-start(bf16[8,256,128]{2,1,0:T(8,128)(2,1)} %get-tuple-element.31.outer_ref), channel_id=1, source_target_pairs={{2,6},{4,0},{6,10},{8,4},{10,14},{12,8},{3,7},{5,1},{7,11},{9,5},{... | collective-permute-start | bytes 1572872 | tf_op jit(solution)/shard_map/ppermute | solution.py:369
  6.4 5.3 %collective-permute-start.4 = (s32[1,1024]{1,0:T(1,128)}, s32[1,1024]{1,0:T(1,128)S(1)}, u32[]{:S(2)}, u32[]{:S(2)}) collective-permute-start(s32[1,1024]{1,0:T(1,128)} %bitcast.16), channel_id=1, source_target_pairs={{0,2},{2,0},{4,6},{6,4},{8,10},{10,8},{12,14},{14,12},{1,3},{3,1},... | collective-permute-start | bytes 12296 | tf_op jit(solution)/shard_map/ppermute | solution.py:363
  11.7 1.8 %collective-permute-done.4.gm_ref = s32[1,1024]{1,0:T(1,128)S(1)} collective-permute-done((s32[1,1024]{1,0:T(1,128)}, s32[1,1024]{1,0:T(1,128)S(1)}, u32[]{:S(2)}, u32[]{:S(2)}) %collective-permute-start.4) | collective-permute-done | bytes 4128 | tf_op jit(solution)/shard_map/ppermute | solution.py:363
  14.3 4.3 %collective-permute-start.5 = (bf16[8,256,128]{2,1,0:T(8,128)(2,1)}, bf16[8,256,128]{2,1,0:T(8,128)(2,1)S(1)}, u32[]{:S(2)}, u32[]{:S(2)}) collective-permute-start(bf16[8,256,128]{2,1,0:T(8,128)(2,1)} %get-tuple-element.37.near_ref), channel_id=1, source_target_pairs={{0,2},{2,0},{4,6},{6,4},{8,10},{10,8},{12,14},{14,12},{1,3},{3,1},... | collective-permute-start | bytes 1572872 | tf_op jit(solution)/shard_map/ppermute | solution.py:370
  20.8 6.2 %inner_blur.1.inner_ref = f32[256,1024]{1,0:T(8,128)S(1)} custom-call(bf16[8,256,128]{2,1,0:T(8,128)(2,1)S(1)} %get-tuple-element.30.near_ref, bf16[8,256,128]{2,1,0:T(8,128)(2,1)} %get-tuple-element.31.outer_ref, bf16[2,256,128]{2,1,0:T(8,128)(2,1)S(1)} %collective-permute-done.edge_ref, s32[1,1024]{1,0:T(1,128)S(1)} %bitcast.17), custom_call_target="tpu_custom_call" | custom-call | flops 1 | bytes 1 | tf_op jit(solution)/shard_map/inner_blur/pallas_call | solution.py:200
  28.4 2.4 %halo_blur.1 = bf16[256,1024]{1,0:T(8,128)(2,1)S(1)} custom-call(bf16[8,256,128]{2,1,0:T(8,128)(2,1)S(1)} %get-tuple-element.30.near_ref, bf16[8,256,128]{2,1,0:T(8,128)(2,1)S(1)} %collective-permute-done.2.beyond_ref, bf16[2,256,128]{2,1,0:T(8,128)(2,1)S(1)} %collective-permute-done.edge_ref, bf16[256,128]{1,0:T(8,128)(2,1)S(1)} %bitcast.15, ...), custom_call_target="tpu_custom_call" | custom-call | flops 1 | bytes 1 | tf_op jit(solution)/shard_map/halo_blur/pallas_call | solution.py:200
  30.8 9.4 %collective-permute-done.5.facing_ref = bf16[8,256,128]{2,1,0:T(8,128)(2,1)S(1)} collective-permute-done((bf16[8,256,128]{2,1,0:T(8,128)(2,1)}, bf16[8,256,128]{2,1,0:T(8,128)(2,1)S(1)}, u32[]{:S(2)}, u32[]{:S(2)}) %collective-permute-start.5) | collective-permute-done | bytes 524320 | tf_op jit(solution)/shard_map/ppermute | solution.py:370
  40.2 2.4 %collective-permute-start.7 = (bf16[256,1024]{1,0:T(8,128)(2,1)S(1)}, bf16[256,1024]{1,0:T(8,128)(2,1)S(1)}, u32[]{:S(2)}, u32[]{:S(2)}) collective-permute-start(bf16[256,1024]{1,0:T(8,128)(2,1)S(1)} %halo_blur.1), channel_id=1, source_target_pairs={{0,2},{2,0},{4,6},{6,4},{8,10},{10,8},{12,14},{14,12},{1,3},{3,1},... | collective-permute-start | bytes 1572872 | tf_op jit(solution)/shard_map/ppermute | solution.py:377
  42.7 1.3 %collective-permute-done.8.corner_ref = bf16[2,256,128]{2,1,0:T(8,128)(2,1)S(1)} collective-permute-done((bf16[2,256,128]{2,1,0:T(8,128)(2,1)S(1)}, bf16[2,256,128]{2,1,0:T(8,128)(2,1)S(1)}, u32[]{:S(2)}, u32[]{:S(2)}) %collective-permute-start.8) | collective-permute-done | bytes 131104 | tf_op jit(solution)/shard_map/ppermute | solution.py:329
  44.7 4.5 %blur_score_pick.1 = bf16[256,1024]{1,0:T(8,128)(2,1)S(1)} custom-call(bf16[8,256,128]{2,1,0:T(8,128)(2,1)} %get-tuple-element.37.near_ref, bf16[8,256,128]{2,1,0:T(8,128)(2,1)} %get-tuple-element.40.outer_ref, bf16[8,256,128]{2,1,0:T(8,128)(2,1)S(1)} %collective-permute-done.5.facing_ref, bf16[8,256,128]{2,1,0:T(8,128)(2,1)S(1)} %collective-permute-done.6.across_ref, ...), custom_call_target="tpu_custom_call" | custom-call | flops 1 | bytes 1 | tf_op jit(solution)/shard_map/blur_score_pick/pallas_call | solution.py:200
  49.2 2.2 %collective-permute-start.12 = (bf16[256,1024]{1,0:T(8,128)(2,1)S(1)}, bf16[256,1024]{1,0:T(8,128)(2,1)S(1)}, u32[]{:S(2)}, u32[]{:S(2)}) collective-permute-start(bf16[256,1024]{1,0:T(8,128)(2,1)S(1)} %blur_score_pick.1), channel_id=1, source_target_pairs={{4,0},{14,2},{8,4},{2,6},{12,8},{6,10},{0,12},{10,14},{5,1},{15,3}... | collective-permute-start | bytes 1572872 | tf_op jit(solution)/shard_map/ppermute | solution.py:380
  52.5 1.7 %collective-permute-start.11 = (bf16[256,1024]{1,0:T(8,128)(2,1)S(1)}, bf16[256,1024]{1,0:T(8,128)(2,1)S(1)}, u32[]{:S(2)}, u32[]{:S(2)}) collective-permute-start(bf16[256,1024]{1,0:T(8,128)(2,1)S(1)} %blur_score_pick.1), channel_id=1, source_target_pairs={{0,2},{2,0},{4,6},{6,4},{8,10},{10,8},{12,14},{14,12},{1,3},{3,1},... | collective-permute-start | bytes 1572872 | tf_op jit(solution)/shard_map/ppermute | solution.py:383
  55.8 4.4 %collective-permute-start.9 = (bf16[256,1024]{1,0:T(8,128)(2,1)}, bf16[256,1024]{1,0:T(8,128)(2,1)}, u32[]{:S(2)}, u32[]{:S(2)}) collective-permute-start(bf16[256,1024]{1,0:T(8,128)(2,1)} %join_score.1), channel_id=1, source_target_pairs={{4,0},{14,2},{8,4},{2,6},{12,8},{6,10},{0,12},{10,14},{5,1},{15,3}... | collective-permute-start | bytes 1572872 | tf_op jit(solution)/shard_map/ppermute | solution.py:385
  60.2 3.9 %collective-permute-done.12 = bf16[256,1024]{1,0:T(8,128)(2,1)S(1)} collective-permute-done((bf16[256,1024]{1,0:T(8,128)(2,1)S(1)}, bf16[256,1024]{1,0:T(8,128)(2,1)S(1)}, u32[]{:S(2)}, u32[]{:S(2)}) %collective-permute-start.12) | collective-permute-done | bytes 524320 | tf_op jit(solution)/shard_map/ppermute | solution.py:380
  64.1 2.2 %collective-permute-start.15 = (bf16[256,1024]{1,0:T(8,128)(2,1)S(1)}, bf16[256,1024]{1,0:T(8,128)(2,1)}, u32[]{:S(2)}, u32[]{:S(2)}) collective-permute-start(bf16[256,1024]{1,0:T(8,128)(2,1)S(1)} %collective-permute-done.12), channel_id=1, source_target_pairs={{0,2},{2,0},{4,6},{6,4},{8,10},{10,8},{12,14},{14,12},{1,3},{3,1},... | collective-permute-start | bytes 1572872 | tf_op jit(solution)/shard_map/ppermute | solution.py:388
  67.3 11.2 %collective-permute-done.10 = bf16[256,1024]{1,0:T(8,128)(2,1)S(1)} collective-permute-done((bf16[256,1024]{1,0:T(8,128)(2,1)}, bf16[256,1024]{1,0:T(8,128)(2,1)S(1)}, u32[]{:S(2)}, u32[]{:S(2)}) %collective-permute-start.10) | collective-permute-done | bytes 524320 | tf_op jit(solution)/shard_map/ppermute | solution.py:384
  78.6 9.2 %collective-permute-done.15 = bf16[256,1024]{1,0:T(8,128)(2,1)} collective-permute-done((bf16[256,1024]{1,0:T(8,128)(2,1)S(1)}, bf16[256,1024]{1,0:T(8,128)(2,1)}, u32[]{:S(2)}, u32[]{:S(2)}) %collective-permute-start.15) | collective-permute-done | bytes 524320 | tf_op jit(solution)/shard_map/ppermute | solution.py:388
  88.4 2.2 %collective-permute-start.16 = (bf16[256,1024]{1,0:T(8,128)(2,1)}, bf16[256,1024]{1,0:T(8,128)(2,1)}, u32[]{:S(2)}, u32[]{:S(2)}) collective-permute-start(bf16[256,1024]{1,0:T(8,128)(2,1)} %collective-permute-done.9), channel_id=1, source_target_pairs={{0,2},{2,0},{4,6},{6,4},{8,10},{10,8},{12,14},{14,12},{1,3},{3,1},... | collective-permute-start | bytes 1572872 | tf_op jit(solution)/shard_map/ppermute | solution.py:394
  94.8 6.1 %tiles.2.refs_8_ = bf16[8,16,2,128,128]{4,3,2,1,0:T(8,128)(2,1)} custom-call(s32[8,16]{1,0:T(8,128)S(1)} %get-tuple-element.55.place_ref, s32[8,16]{1,0:T(8,128)S(1)} %fusion.21.present_ref, bf16[2,256,1024]{2,1,0:T(8,128)(2,1)S(1)} %pad_maximum_fusion.1.refs_0_, bf16[2,256,1024]{2,1,0:T(8,128)(2,1)S(1)} %copy-done.2, ...), custom_call_target="tpu_custom_call" | custom-call | flops 1 | bytes 1 | tf_op jit(solution)/shard_map/tiles/pallas_call | solution.py:295
  101.0 3.4 %collective-permute-done.22 = bf16[256,1024]{1,0:T(8,128)(2,1)} collective-permute-done((bf16[256,1024]{1,0:T(8,128)(2,1)}, bf16[256,1024]{1,0:T(8,128)(2,1)}, u32[]{:S(2)}, u32[]{:S(2)}) %collective-permute-start.22) | collective-permute-done | bytes 524320 | tf_op jit(solution)/shard_map/ppermute | solution.py:395
  104.9 1.6 %collective-permute-done.21.refs_5_ = bf16[1,256,1024]{2,1,0:T(8,128)(2,1)S(1)} collective-permute-done((bf16[1,256,1024]{2,1,0:T(8,128)(2,1)}, bf16[1,256,1024]{2,1,0:T(8,128)(2,1)S(1)}, u32[]{:S(2)}, u32[]{:S(2)}) %collective-permute-start.21) | collective-permute-done | bytes 524320 | tf_op jit(solution)/shard_map/ppermute | solution.py:329
  107.3 6.0 %tiles.3 = bf16[8,16,2,128,128]{4,3,2,1,0:T(8,128)(2,1)} custom-call(s32[8,16]{1,0:T(8,128)S(1)} %get-tuple-element.56.place_ref, s32[8,16]{1,0:T(8,128)S(1)} %fusion.21.present_ref, bf16[2,256,1024]{2,1,0:T(8,128)(2,1)S(1)} %pad_maximum_fusion.refs_0_, bf16[2,256,1024]{2,1,0:T(8,128)(2,1)} %collective-permute-done.13.refs_1_, ...), custom_call_target="tpu_custom_call", output_to_operand_aliasing={{}: (10, {})} | custom-call | flops 1 | bytes 1 | tf_op jit(solution)/shard_map/tiles/pallas_call | solution.py:295
  (55 shorter events, 14.9 us)
Async XLA Ops:
  5.0 22.1 %collective-permute-start.2 = (bf16[8,256,128]{2,1,0:T(8,128)(2,1)}, bf16[8,256,128]{2,1,0:T(8,128)(2,1)S(1)}, u32[]{:S(2)}, u32[]{:S(2)}) collective-permute-start(bf16[8,256,128]{2,1,0:T(8,128)(2,1)} %get-tuple-element.31.outer_ref), channel_id=1, source_target_pairs={{2,6},{4,0},{6,10},{8,4},{10,14},{12,8},{3,7},{5,1},{7,11},{9,5},{... | collective-permute-start | bytes 1572872 | tf_op jit(solution)/shard_map/ppermute | solution.py:369
  6.4 7.1 %collective-permute-start.4 = (s32[1,1024]{1,0:T(1,128)}, s32[1,1024]{1,0:T(1,128)S(1)}, u32[]{:S(2)}, u32[]{:S(2)}) collective-permute-start(s32[1,1024]{1,0:T(1,128)} %bitcast.16), channel_id=1, source_target_pairs={{0,2},{2,0},{4,6},{6,4},{8,10},{10,8},{12,14},{14,12},{1,3},{3,1},... | collective-permute-start | bytes 12296 | tf_op jit(solution)/shard_map/ppermute | solution.py:363
  13.5 17.3 %collective-permute-start.6 = (bf16[8,256,128]{2,1,0:T(8,128)(2,1)}, bf16[8,256,128]{2,1,0:T(8,128)(2,1)S(1)}, u32[]{:S(2)}, u32[]{:S(2)}) collective-permute-start(bf16[8,256,128]{2,1,0:T(8,128)(2,1)} %get-tuple-element.40.outer_ref), channel_id=1, source_target_pairs={{2,4},{4,2},{6,8},{8,6},{10,12},{12,10},{3,5},{5,3},{7,9},{9,7},{1... | collective-permute-start | bytes 1572872 | tf_op jit(solution)/shard_map/ppermute | solution.py:371
  14.3 25.9 %collective-permute-start.5 = (bf16[8,256,128]{2,1,0:T(8,128)(2,1)}, bf16[8,256,128]{2,1,0:T(8,128)(2,1)S(1)}, u32[]{:S(2)}, u32[]{:S(2)}) collective-permute-start(bf16[8,256,128]{2,1,0:T(8,128)(2,1)} %get-tuple-element.37.near_ref), channel_id=1, source_target_pairs={{0,2},{2,0},{4,6},{6,4},{8,10},{10,8},{12,14},{14,12},{1,3},{3,1},... | collective-permute-start | bytes 1572872 | tf_op jit(solution)/shard_map/ppermute | solution.py:370
  18.6 1.3 %collective-permute-start.1 = (bf16[2,256,128]{2,1,0:T(8,128)(2,1)S(1)}, bf16[2,256,128]{2,1,0:T(8,128)(2,1)S(1)}, u32[]{:S(2)}, u32[]{:S(2)}) collective-permute-start(bf16[2,256,128]{2,1,0:T(8,128)(2,1)S(1)} %get-tuple-element.33), channel_id=1, source_target_pairs={{0,1},{1,0},{2,3},{3,2},{4,5},{5,4},{6,7},{7,6},{8,9},{9,8},{10,11... | collective-permute-start | bytes 393224 | tf_op jit(solution)/shard_map/ppermute | solution.py:329
  18.6 1.5 %collective-permute-start = (bf16[2,256,128]{2,1,0:T(8,128)(2,1)S(1)}, bf16[2,256,128]{2,1,0:T(8,128)(2,1)S(1)}, u32[]{:S(2)}, u32[]{:S(2)}) collective-permute-start(bf16[2,256,128]{2,1,0:T(8,128)(2,1)S(1)} %get-tuple-element.32), channel_id=1, source_target_pairs={{0,1},{1,0},{2,3},{3,2},{4,5},{5,4},{6,7},{7,6},{8,9},{9,8},{10,11... | collective-permute-start | bytes 393224 | tf_op jit(solution)/shard_map/ppermute | solution.py:329
  27.1 1.3 %collective-permute-start.3 = (bf16[1,256,128]{2,1,0:T(8,128)(2,1)S(1)}, bf16[1,256,128]{2,1,0:T(8,128)(2,1)S(1)}, u32[]{:S(2)}, u32[]{:S(2)}) collective-permute-start(bf16[1,256,128]{2,1,0:T(8,128)(2,1)S(1)} %slice_select_fusion.2), channel_id=1, source_target_pairs={{0,1},{1,0},{2,3},{3,2},{4,5},{5,4},{6,7},{7,6},{8,9},{9,8},{10,11... | collective-permute-start | bytes 196616 | tf_op jit(solution)/shard_map/ppermute | solution.py:329
  40.2 12.2 %collective-permute-start.7 = (bf16[256,1024]{1,0:T(8,128)(2,1)S(1)}, bf16[256,1024]{1,0:T(8,128)(2,1)S(1)}, u32[]{:S(2)}, u32[]{:S(2)}) collective-permute-start(bf16[256,1024]{1,0:T(8,128)(2,1)S(1)} %halo_blur.1), channel_id=1, source_target_pairs={{0,2},{2,0},{4,6},{6,4},{8,10},{10,8},{12,14},{14,12},{1,3},{3,1},... | collective-permute-start | bytes 1572872 | tf_op jit(solution)/shard_map/ppermute | solution.py:377
  42.6 1.4 %collective-permute-start.8 = (bf16[2,256,128]{2,1,0:T(8,128)(2,1)S(1)}, bf16[2,256,128]{2,1,0:T(8,128)(2,1)S(1)}, u32[]{:S(2)}, u32[]{:S(2)}) collective-permute-start(bf16[2,256,128]{2,1,0:T(8,128)(2,1)S(1)} %pad_maximum_fusion.3), channel_id=1, source_target_pairs={{0,1},{1,0},{2,3},{3,2},{4,5},{5,4},{6,7},{7,6},{8,9},{9,8},{10,11... | collective-permute-start | bytes 393224 | tf_op jit(solution)/shard_map/ppermute | solution.py:329
  49.2 14.8 %collective-permute-start.12 = (bf16[256,1024]{1,0:T(8,128)(2,1)S(1)}, bf16[256,1024]{1,0:T(8,128)(2,1)S(1)}, u32[]{:S(2)}, u32[]{:S(2)}) collective-permute-start(bf16[256,1024]{1,0:T(8,128)(2,1)S(1)} %blur_score_pick.1), channel_id=1, source_target_pairs={{4,0},{14,2},{8,4},{2,6},{12,8},{6,10},{0,12},{10,14},{5,1},{15,3}... | collective-permute-start | bytes 1572872 | tf_op jit(solution)/shard_map/ppermute | solution.py:380
  52.5 14.9 %collective-permute-start.11 = (bf16[256,1024]{1,0:T(8,128)(2,1)S(1)}, bf16[256,1024]{1,0:T(8,128)(2,1)S(1)}, u32[]{:S(2)}, u32[]{:S(2)}) collective-permute-start(bf16[256,1024]{1,0:T(8,128)(2,1)S(1)} %blur_score_pick.1), channel_id=1, source_target_pairs={{0,2},{2,0},{4,6},{6,4},{8,10},{10,8},{12,14},{14,12},{1,3},{3,1},... | collective-permute-start | bytes 1572872 | tf_op jit(solution)/shard_map/ppermute | solution.py:383
  55.5 23.1 %collective-permute-start.10 = (bf16[256,1024]{1,0:T(8,128)(2,1)}, bf16[256,1024]{1,0:T(8,128)(2,1)S(1)}, u32[]{:S(2)}, u32[]{:S(2)}) collective-permute-start(bf16[256,1024]{1,0:T(8,128)(2,1)} %join_score.1), channel_id=1, source_target_pairs={{0,2},{2,0},{4,6},{6,4},{8,10},{10,8},{12,14},{14,12},{1,3},{3,1},... | collective-permute-start | bytes 1572872 | tf_op jit(solution)/shard_map/ppermute | solution.py:384
  55.8 22.8 %collective-permute-start.9 = (bf16[256,1024]{1,0:T(8,128)(2,1)}, bf16[256,1024]{1,0:T(8,128)(2,1)}, u32[]{:S(2)}, u32[]{:S(2)}) collective-permute-start(bf16[256,1024]{1,0:T(8,128)(2,1)} %join_score.1), channel_id=1, source_target_pairs={{4,0},{14,2},{8,4},{2,6},{12,8},{6,10},{0,12},{10,14},{5,1},{15,3}... | collective-permute-start | bytes 1572872 | tf_op jit(solution)/shard_map/ppermute | solution.py:385
  64.1 23.7 %collective-permute-start.15 = (bf16[256,1024]{1,0:T(8,128)(2,1)S(1)}, bf16[256,1024]{1,0:T(8,128)(2,1)}, u32[]{:S(2)}, u32[]{:S(2)}) collective-permute-start(bf16[256,1024]{1,0:T(8,128)(2,1)S(1)} %collective-permute-done.12), channel_id=1, source_target_pairs={{0,2},{2,0},{4,6},{6,4},{8,10},{10,8},{12,14},{14,12},{1,3},{3,1},... | collective-permute-start | bytes 1572872 | tf_op jit(solution)/shard_map/ppermute | solution.py:388
  66.2 21.5 %collective-permute-start.18 = (bf16[256,1024]{1,0:T(8,128)(2,1)S(1)}, bf16[256,1024]{1,0:T(8,128)(2,1)S(1)}, u32[]{:S(2)}, u32[]{:S(2)}) collective-permute-start(bf16[256,1024]{1,0:T(8,128)(2,1)S(1)} %blur_score_pick.1), channel_id=1, source_target_pairs={{0,4},{2,14},{4,8},{6,2},{8,12},{10,6},{12,0},{14,10},{1,5},{3,15}... | collective-permute-start | bytes 1572872 | tf_op jit(solution)/shard_map/ppermute | solution.py:387
  67.3 24.6 %collective-permute-start.17 = (bf16[2,256,1024]{2,1,0:T(8,128)(2,1)S(1)}, bf16[2,256,1024]{2,1,0:T(8,128)(2,1)S(1)}, u32[]{:S(2)}, u32[]{:S(2)}) collective-permute-start(bf16[2,256,1024]{2,1,0:T(8,128)(2,1)S(1)} %pad_maximum_fusion.1.refs_0_), channel_id=1, source_target_pairs={{0,1},{1,0},{2,3},{3,2},{4,5},{5,4},{6,7},{7,6},{8,9},{9,8},{10,11... | collective-permute-start | bytes 3145736 | tf_op jit(solution)/shard_map/ppermute | solution.py:329
  87.9 5.7 %collective-permute-start.19 = (bf16[2,256,1024]{2,1,0:T(8,128)(2,1)S(1)}, bf16[2,256,1024]{2,1,0:T(8,128)(2,1)}, u32[]{:S(2)}, u32[]{:S(2)}) collective-permute-start(bf16[2,256,1024]{2,1,0:T(8,128)(2,1)S(1)} %pad_maximum_fusion.2.refs_2_), channel_id=1, source_target_pairs={{0,1},{1,0},{2,3},{3,2},{4,5},{5,4},{6,7},{7,6},{8,9},{9,8},{10,11... | collective-permute-start | bytes 3145736 | tf_op jit(solution)/shard_map/ppermute | solution.py:329
  88.0 16.4 %collective-permute-start.22 = (bf16[256,1024]{1,0:T(8,128)(2,1)}, bf16[256,1024]{1,0:T(8,128)(2,1)}, u32[]{:S(2)}, u32[]{:S(2)}) collective-permute-start(bf16[256,1024]{1,0:T(8,128)(2,1)} %join_score.1), channel_id=1, source_target_pairs={{0,4},{2,14},{4,8},{6,2},{8,12},{10,6},{12,0},{14,10},{1,5},{3,15}... | collective-permute-start | bytes 1572872 | tf_op jit(solution)/shard_map/ppermute | solution.py:395
  88.4 16.0 %collective-permute-start.16 = (bf16[256,1024]{1,0:T(8,128)(2,1)}, bf16[256,1024]{1,0:T(8,128)(2,1)}, u32[]{:S(2)}, u32[]{:S(2)}) collective-permute-start(bf16[256,1024]{1,0:T(8,128)(2,1)} %collective-permute-done.9), channel_id=1, source_target_pairs={{0,2},{2,0},{4,6},{6,4},{8,10},{10,8},{12,14},{14,12},{1,3},{3,1},... | collective-permute-start | bytes 1572872 | tf_op jit(solution)/shard_map/ppermute | solution.py:394
  90.7 2.9 %collective-permute-start.20 = (bf16[1,256,1024]{2,1,0:T(8,128)(2,1)}, bf16[1,256,1024]{2,1,0:T(8,128)(2,1)}, u32[]{:S(2)}, u32[]{:S(2)}) collective-permute-start(bf16[1,256,1024]{2,1,0:T(8,128)(2,1)} %bitcast.9.refs_4_), channel_id=1, source_target_pairs={{0,1},{1,0},{2,3},{3,2},{4,5},{5,4},{6,7},{7,6},{8,9},{9,8},{10,11... | collective-permute-start | bytes 1572872 | tf_op jit(solution)/shard_map/ppermute | solution.py:329
  92.9 12.0 %collective-permute-start.13 = (bf16[2,256,1024]{2,1,0:T(8,128)(2,1)S(1)}, bf16[2,256,1024]{2,1,0:T(8,128)(2,1)}, u32[]{:S(2)}, u32[]{:S(2)}) collective-permute-start(bf16[2,256,1024]{2,1,0:T(8,128)(2,1)S(1)} %pad_maximum_fusion.refs_0_), channel_id=1, source_target_pairs={{0,1},{1,0},{2,3},{3,2},{4,5},{5,4},{6,7},{7,6},{8,9},{9,8},{10,11... | collective-permute-start | bytes 3145736 | tf_op jit(solution)/shard_map/ppermute | solution.py:329
  93.5 11.4 %collective-permute-start.14 = (bf16[1,256,1024]{2,1,0:T(8,128)(2,1)}, bf16[1,256,1024]{2,1,0:T(8,128)(2,1)S(1)}, u32[]{:S(2)}, u32[]{:S(2)}) collective-permute-start(bf16[1,256,1024]{2,1,0:T(8,128)(2,1)} %bitcast.13), channel_id=1, source_target_pairs={{0,1},{1,0},{2,3},{3,2},{4,5},{5,4},{6,7},{7,6},{8,9},{9,8},{10,11... | collective-permute-start | bytes 1572872 | tf_op jit(solution)/shard_map/ppermute | solution.py:329
  104.4 2.1 %collective-permute-start.21 = (bf16[1,256,1024]{2,1,0:T(8,128)(2,1)}, bf16[1,256,1024]{2,1,0:T(8,128)(2,1)S(1)}, u32[]{:S(2)}, u32[]{:S(2)}) collective-permute-start(bf16[1,256,1024]{2,1,0:T(8,128)(2,1)} %bitcast.10.refs_4_), channel_id=1, source_target_pairs={{0,1},{1,0},{2,3},{3,2},{4,5},{5,4},{6,7},{7,6},{8,9},{9,8},{10,11... | collective-permute-start | bytes 1572872 | tf_op jit(solution)/shard_map/ppermute | solution.py:329
  104.4 2.9 %collective-permute-start.23 = (bf16[1,256,1024]{2,1,0:T(8,128)(2,1)}, bf16[1,256,1024]{2,1,0:T(8,128)(2,1)S(1)}, u32[]{:S(2)}, u32[]{:S(2)}) collective-permute-start(bf16[1,256,1024]{2,1,0:T(8,128)(2,1)} %bitcast.11.refs_6_), channel_id=1, source_target_pairs={{0,1},{1,0},{2,3},{3,2},{4,5},{5,4},{6,7},{7,6},{8,9},{9,8},{10,11... | collective-permute-start | bytes 1572872 | tf_op jit(solution)/shard_map/ppermute | solution.py:329
  (8 other events, 118.2 us)
